TPU v7x, 32 devices: a whole 2x2x4 slice. The times are simulated.
32 devices in a mesh: ctx: 4 (over y, core), exp: 8 (over z, x).
Axes of the slice: x: 2, y: 2, z: 4, core: 2. Of those that a mesh axis runs over, the one named last changes fastest.
Arguments:
- queries: bfloat16 [4, 8, 64, 4096], P('ctx', 'exp'), may hold values from -90 to 90
- new_keys_values: bfloat16 [4, 8, 64, 512], P('ctx', 'exp'), may hold values from -4.5 to 4.5
- cached_keys_values: bfloat16 [4, 8, 64, 512], P('ctx', 'exp'), may hold values from -4.5 to 4.5
- residual: bfloat16 [4, 8, 64, 4096], P(None, 'exp', None, 'ctx'), may hold values from -17 to 17
- out_weight: bfloat16 [4096, 4096], P('exp', 'ctx'), may hold values from -0.125 to 0.125
- norm_gain: float32 [4096], P('ctx'), may hold values from 0.1 to 1.9
- routes: int32 [4, 8, 64, 8], P(None, 'exp'), may hold values from 0 to 127, as said below
- gates: float32 [4, 8, 64, 8], P(None, 'exp'), may hold values from 0.3 to 1
- w_gate_up: bfloat16 [8, 4096, 3072], P('exp', 'ctx'), may hold values from -0.125 to 0.125
- w_down: bfloat16 [8, 1536, 4096], P('exp', None, 'ctx'), may hold values from -0.15625 to 0.15625
Outputs:
- layer_out: bfloat16 [4, 8, 64, 4096], P(None, 'exp', None, 'ctx')
Inputs may be any that keep to these rules, and one draw needn't show every extreme that they name: `routes`: each row names 8 different experts, at most one of them below 8. Among the rows that share the second index, an expert below 8 is named by at most 16 of them, and some expert by exactly 16.
All inputs are finite; a program needn't handle non-finite values.
Results may differ from a plain program's by a relative error of at most 0.02.
Values may be sent and summed in bfloat16 or wider, within the bound.
No kernel may reach another device: no remote copies, remote signals or barrier semaphores. Data moves between devices by JAX's collectives and lax.ppermute only.
A program may use at most 64 MiB of HBM per device.

v0:
```python
import jax
import jax.numpy as jnp
from jax import lax
from jax.sharding import PartitionSpec as P

D = 4096
QUERY_HEADS = 32
KEY_VALUE_HEADS = 2
HEAD_SIZE = 128


NEG_FILL = -1e30


def body(
    queries,
    new_keys_values,
    cached_keys_values,
    residual,
    out_weight,
    norm_gain,
    routes,
    gates,
    w_gate_up,
    w_down,
):
    groups = lax.axis_size("ctx")
    experts_here = lax.axis_size("exp")
    tok_dev = queries.shape[2]
    past_dev = cached_keys_values.shape[2]
    tok_rows = groups * tok_dev
    past_rows = groups * past_dev
    width_block = residual.shape[3]
    hidden = w_down.shape[1]
    ctx_index = lax.axis_index("ctx")
    group_extent = QUERY_HEADS // KEY_VALUE_HEADS
    kv_width = new_keys_values.shape[3]
    queries_flat = queries.reshape(1, tok_dev, queries.shape[3])
    grouped = lax.all_to_all(queries_flat, "ctx", split_axis=2, concat_axis=0, tiled=True)
    heads_here = grouped.shape[2] // HEAD_SIZE
    local_query = grouped.reshape(tok_rows, heads_here, HEAD_SIZE)
    gathered_kv, gathered_past = (
        lax.all_gather(new_keys_values.reshape(1, tok_dev, kv_width), "ctx", axis=0, tiled=True),
        lax.all_gather(
            cached_keys_values.reshape(1, past_dev, kv_width), "ctx", axis=0, tiled=True
        ),
    )
    common_key_head = ctx_index * heads_here // group_extent

    def own_head(gathered_rows):
        key_portion = lax.dynamic_slice_in_dim(
            gathered_rows, common_key_head * HEAD_SIZE, HEAD_SIZE, 2
        )
        value_portion = lax.dynamic_slice_in_dim(
            gathered_rows, KEY_VALUE_HEADS * HEAD_SIZE + common_key_head * HEAD_SIZE, HEAD_SIZE, 2
        )
        return jnp.concatenate([key_portion, value_portion], axis=2)

    own_keys = own_head(gathered_kv)
    own_past = own_head(gathered_past)
    stacked = own_keys.reshape(tok_rows, 2 * HEAD_SIZE)
    stacked_past = own_past.reshape(past_rows, 2 * HEAD_SIZE)
    keys_all = jnp.concatenate([stacked_past[:, :HEAD_SIZE], stacked[:, :HEAD_SIZE]], axis=0)
    values_all = jnp.concatenate([stacked_past[:, HEAD_SIZE:], stacked[:, HEAD_SIZE:]], axis=0)
    key_places = jnp.arange(past_rows + tok_rows) - past_rows
    block_rows = min(512, tok_rows)
    block_count = tok_rows // block_rows
    query_blocks = local_query.reshape(block_count, block_rows, heads_here, HEAD_SIZE)

    def attend(operands):
        query_block, block_index = operands
        row_places = block_index * block_rows + jnp.arange(block_rows)
        visible = (key_places[None, :] <= row_places[:, None])[:, None, :]
        scores = jnp.einsum(
            "rhd,kd->rhk", query_block, keys_all, preferred_element_type=jnp.float32
        ) * HEAD_SIZE ** (-0.5)
        scores = jnp.where(visible, scores, NEG_FILL)
        row_max = jnp.max(scores, axis=2, keepdims=True)
        weights = jnp.where(visible, jnp.exp(scores - row_max), 0.0)
        totals = jnp.sum(weights, axis=2)
        numerator = jnp.einsum(
            "rhk,kd->rhd",
            weights.astype(jnp.bfloat16),
            values_all,
            preferred_element_type=jnp.float32,
        )
        return (numerator / totals[:, :, None]).astype(jnp.bfloat16)

    attended = lax.map(attend, (query_blocks, jnp.arange(block_count)))
    head_width = heads_here * HEAD_SIZE
    attended_rows = attended.reshape(1, tok_rows, head_width)
    full_weight = lax.all_gather(out_weight, "exp", axis=0, tiled=True)
    piece = lax.all_gather(attended_rows, "ctx", axis=0, tiled=True)
    count = piece.shape[0]
    projected = jnp.einsum(
        "krc,kcd->rd",
        piece,
        full_weight.reshape(count, head_width, width_block),
        preferred_element_type=jnp.float32,
    )
    mixed = residual.reshape(tok_rows, width_block).astype(jnp.float32) + projected
    square_sum = lax.psum(jnp.sum(mixed * mixed, axis=1), "ctx")
    normed = (mixed * lax.rsqrt(square_sum / D + 1e-06)[:, None] * norm_gain[None, :]).astype(
        jnp.bfloat16
    )
    route_rows = routes.reshape(tok_rows, routes.shape[3])
    gate_rows = gates.reshape(tok_rows, gates.shape[3])
    resident = route_rows < experts_here
    has_expert = jnp.any(resident, axis=1)
    target = jnp.sum(jnp.where(resident, route_rows, 0), axis=1)
    gate_share = jnp.sum(jnp.where(resident, gate_rows, 0.0), axis=1)
    capacity = tok_rows // (2 * experts_here)
    one_hot = ((target[:, None] == jnp.arange(experts_here)[None, :]) & has_expert[:, None]).astype(
        jnp.int32
    )
    earlier_positions = jnp.cumsum(one_hot, axis=0) - one_hot
    place_index = jnp.where(
        has_expert, target * capacity + jnp.sum(earlier_positions * one_hot, axis=1), -1
    )
    placement = (place_index[None, :] == jnp.arange(experts_here * capacity)[:, None]).astype(
        jnp.bfloat16
    )
    outgoing_rows = jnp.dot(placement, normed, preferred_element_type=jnp.float32).astype(
        jnp.bfloat16
    )
    arrived = lax.all_to_all(
        outgoing_rows.reshape(experts_here, capacity, width_block),
        "exp",
        split_axis=0,
        concat_axis=0,
        tiled=True,
    )
    arrived = arrived.reshape(experts_here * capacity, width_block)
    partials = jnp.dot(arrived, w_gate_up[0], preferred_element_type=jnp.float32)
    summed = lax.psum(partials.astype(jnp.bfloat16), "ctx").astype(jnp.float32)
    activated = (jax.nn.silu(summed[:, :hidden]) * summed[:, hidden:]).astype(jnp.bfloat16)
    expert_out = jnp.dot(activated, w_down[0], preferred_element_type=jnp.float32).astype(
        jnp.bfloat16
    )
    returned = lax.all_to_all(
        expert_out.reshape(experts_here, capacity, width_block),
        "exp",
        split_axis=0,
        concat_axis=0,
        tiled=True,
    )
    collected = jnp.einsum(
        "mr,md->rd",
        placement,
        returned.reshape(experts_here * capacity, width_block),
        preferred_element_type=jnp.float32,
    )
    result = mixed + gate_share[:, None] * collected
    return result.astype(jnp.bfloat16).reshape(groups, 1, tok_dev, width_block)


def solution(mesh):
    in_specs = (
        P("ctx", "exp", None, None),
        P("ctx", "exp", None, None),
        P("ctx", "exp", None, None),
        P(None, "exp", None, "ctx"),
        P("exp", "ctx"),
        P("ctx"),
        P(None, "exp", None, None),
        P(None, "exp", None, None),
        P("exp", "ctx", None),
        P("exp", None, "ctx"),
    )
    out_specs = P(None, "exp", None, "ctx")
    return jax.shard_map(body, mesh=mesh, in_specs=in_specs, out_specs=out_specs, check_vma=False)
```

profile of v0, /device:TPU:0, one launch (start us, length us, event | category | flops | bytes accessed | tf_op | source)
XLA Modules:
  0.0 322.8 jit_solution(15347316314210763982)
XLA Ops:
  6.5 5.5 %copy.28 = bf16[1,64,4096]{1,0,2:T(2,128)(2,1)} copy(bf16[1,64,4096]{2,1,0:T(8,128)(2,1)} %bitcast.82) | data formatting | bytes 1048576 | tf_op jit(solution)/shard_map/reshape | solution.py:38
  12.0 0.5 broadcast.79
  12.5 24.4 %reduce.8 = bf16[4096,64]{1,0:T(8,128)(2,1)} reduce(bf16[4096,1,64]{2,1,0:T(2,128)(2,1)} %bitcast.75, bf16[]{:T(256)} %broadcast.79), dimensions={1}, to_apply=%bitcast.65.reduce_sub_computation | reduce | bytes 1048578
  36.9 2.6 reshape.148
  39.5 4.2 %all-to-all-start = ((bf16[4,2,32768]{2,1,0:T(2,128)(2,1)}), bf16[4,2,32768]{2,1,0:T(2,128)(2,1)}, u32[]{:S(2)}, u32[]{:S(2)}) async-start(bf16[4,2,32768]{2,1,0:T(2,128)(2,1)} %reshape.148), calls=%async_computation | async-start | bytes 1048576 | tf_op jit(solution)/shard_map/all_to_all | solution.py:39
  43.8 11.6 %all-gather = bf16[4,1,64,512]{3,2,1,0:T(8,128)(2,1)S(1)} all-gather(bf16[1,1,64,512]{3,2,1,0:T(8,128)(2,1)S(1)} %copy-done.2), channel_id=2, replica_groups=mesh['ctx'=4,'exp'=8] {'ctx'}, dimensions={0}, use_global_device_ids=true | all-gather | bytes 327680 | tf_op jit(solution)/shard_map/all_gather | solution.py:44
  55.3 6.3 %all-gather.1 = bf16[4,1,64,512]{3,2,1,0:T(8,128)(2,1)} all-gather(bf16[1,1,64,512]{3,2,1,0:T(8,128)(2,1)S(1)} %copy-done.3), channel_id=3, replica_groups=mesh['ctx'=4,'exp'=8] {'ctx'}, dimensions={0}, use_global_device_ids=true | all-gather | bytes 327680 | tf_op jit(solution)/shard_map/all_gather | solution.py:43
  61.6 0.9 dynamic-slice_bitcast_fusion.1
  62.6 0.1 iota_compare_fusion
  62.8 0.0 all-to-all-done
  62.8 3.9 %reshape.149 = bf16[4096,1,64]{2,1,0:T(2,128)(2,1)} reshape(bf16[4,2,32768]{2,1,0:T(2,128)(2,1)} %all-to-all-done) | data formatting | bytes 1048576
  66.6 5.2 %copy.29 = bf16[1,64,4096]{2,1,0:T(8,128)(2,1)} copy(bf16[1,64,4096]{1,0,2:T(2,128)(2,1)} %bitcast.74) | data formatting | bytes 1048576 | tf_op jit(solution)/shard_map/all_to_all | solution.py:39
  71.9 2.2 all_to_all.18
  74.1 1.2 copy.30
  75.3 0.1 copy.39
  75.4 0.7 fusion.27
  76.1 2.3 fusion.52
  78.4 1.3 fusion.20
  79.7 2.1 copy.34
  81.8 0.0 all-gather.5.cloned.1.call-update
  81.8 0.0 all-gather.7.cloned.1.call-start
  81.9 0.7 all-gather.7.cloned.1.call-update
  82.6 0.2 all-reduce.2.cloned.1.call-start
  82.8 0.1 eq.39
  82.9 0.1 reduce_sum.51
  83.0 0.1 and.25
  83.1 0.1 reduce_or.12
  83.2 0.6 reduce-window.6
  83.8 0.2 slice_reduce_fusion
  84.0 0.1 fusion.40
  84.1 21.6 %all-gather.5.cloned.1.call-done = bf16[4,256,1024]{2,1,0:T(8,128)(2,1)} async-done(((bf16[1,256,1024]{2,1,0:T(8,128)(2,1)}), bf16[4,256,1024]{2,1,0:T(8,128)(2,1)}) %all-gather.5.cloned.1.call-update) | async-done | bytes 2097168 | tf_op jit(solution)/shard_map/all_gather | solution.py:93
  105.7 127.1 %all-gather.7.cloned.1.call-done = bf16[4096,1024]{1,0:T(8,128)(2,1)} async-done(((bf16[512,1024]{1,0:T(8,128)(2,1)}), bf16[4096,1024]{1,0:T(8,128)(2,1)}) %all-gather.7.cloned.1.call-update) | async-done | bytes 8388624 | tf_op jit(solution)/shard_map/all_gather | solution.py:92
  232.8 7.4 %multiply_reduce_fusion = (f32[256]{0:T(256)S(1)}, f32[256,1024]{1,0:T(8,128)}) fusion(bf16[4,256,1024]{2,1,0:T(8,128)(2,1)} %all-gather.5.cloned.1.call-done, bf16[4,1024,1024]{2,1,0:T(8,128)(2,1)} %bitcast.87, bf16[256,1024]{1,0:T(8,128)(2,1)} %bitcast.88), kind=kOutput, calls=%fused_computation.24 | convolution fusion | flops 2148531968 | bytes 12059648 | tf_op jit(solution)/shard_map/krc,kcd->rd/dot_general | solution.py:95
  240.1 6.1 %psum.14 = f32[256]{0:T(256)S(1)} all-reduce(f32[256]{0:T(256)S(1)} %get-tuple-element.33), channel_id=1, replica_groups=mesh['ctx'=4,'exp'=8] {'ctx'}, use_global_device_ids=true, to_apply=%region_9.10 | all-reduce | flops 256 | bytes 2048 | tf_op jit(solution)/shard_map/psum | solution.py:102
  246.3 0.0 copy-done.5
  246.3 1.6 convolution_convert_fusion
  247.8 11.4 %all_to_all.25 = bf16[8,16,1024]{2,1,0:T(8,128)(2,1)S(1)} all-to-all(bf16[8,16,1024]{2,1,0:T(8,128)(2,1)S(1)} %bitcast.80), channel_id=1, replica_groups=mesh['ctx'=4,'exp'=8] {'exp'}, dimensions={0} | all-to-all | bytes 524288 | tf_op jit(solution)/shard_map/all_to_all | solution.py:126
  259.2 4.7 %fusion.3 = bf16[128,3072]{1,0:T(8,128)(2,1)} fusion(bf16[128,1024]{1,0:T(8,128)(2,1)S(1)} %bitcast.79, bf16[1,1024,3072]{2,1,0:T(8,128)(2,1)} %param.18), kind=kOutput, calls=%fused_computation.5 | convolution fusion | flops 805699584 | bytes 7340032 | tf_op jit(solution)/shard_map/dot_general | solution.py:134
  263.9 0.0 all-reduce.2.cloned.1.call-update
  263.9 33.5 %all-reduce.2.cloned.1.call-done = bf16[128,3072]{1,0:T(8,128)(2,1)} async-done(((bf16[128,3072]{1,0:T(8,128)(2,1)}), bf16[128,3072]{1,0:T(8,128)(2,1)}) %all-reduce.2.cloned.1.call-update) | async-done | bytes 786448 | tf_op jit(solution)/shard_map/psum | solution.py:135
  297.5 1.3 convert_element_type.52
  298.8 0.0 copy-done
  298.8 0.0 copy-start.4
  298.8 1.4 fusion.23
  300.2 5.5 %all-to-all-start.2 = ((bf16[8,16,1024]{2,1,0:T(8,128)(2,1)}), bf16[8,16,1024]{2,1,0:T(8,128)(2,1)S(1)}, u32[]{:S(2)}, u32[]{:S(2)}) async-start(bf16[8,16,1024]{2,1,0:T(8,128)(2,1)} %bitcast.86), calls=%async_computation.2 | async-start | bytes 524288 | tf_op jit(solution)/shard_map/all_to_all | solution.py:140
  305.7 0.1 mul.71
  305.8 8.1 %all-to-all-done.2 = bf16[8,16,1024]{2,1,0:T(8,128)(2,1)S(1)} async-done(((bf16[8,16,1024]{2,1,0:T(8,128)(2,1)}), bf16[8,16,1024]{2,1,0:T(8,128)(2,1)S(1)}, u32[]{:S(2)}, u32[]{:S(2)}) %all-to-all-start.2) | async-done | bytes 262176 | tf_op jit(solution)/shard_map/all_to_all | solution.py:140
  313.9 2.4 fusion.19
  (23 shorter events, 0.2 us)
Async XLA Ops:
  6.5 292.2 %copy-start = (bf16[1,1536,1024]{2,1,0:T(8,128)(2,1)S(1)}, bf16[1,1536,1024]{2,1,0:T(8,128)(2,1)}, u32[]{:S(2)}) copy-start(bf16[1,1536,1024]{2,1,0:T(8,128)(2,1)} %param.19) | copy-start | bytes 9437188
  6.5 37.2 %copy-start.2 = (bf16[1,1,64,512]{3,2,1,0:T(8,128)(2,1)S(1)}, bf16[1,1,64,512]{3,2,1,0:T(8,128)(2,1)}, u32[]{:S(2)}) copy-start(bf16[1,1,64,512]{3,2,1,0:T(8,128)(2,1)} %param.12) | copy-start | bytes 196612
  6.5 48.8 %copy-start.3 = (bf16[1,1,64,512]{3,2,1,0:T(8,128)(2,1)S(1)}, bf16[1,1,64,512]{3,2,1,0:T(8,128)(2,1)}, u32[]{:S(2)}) copy-start(bf16[1,1,64,512]{3,2,1,0:T(8,128)(2,1)} %param.11) | copy-start | bytes 196612
  39.5 23.3 %all-to-all-start = ((bf16[4,2,32768]{2,1,0:T(2,128)(2,1)}), bf16[4,2,32768]{2,1,0:T(2,128)(2,1)}, u32[]{:S(2)}, u32[]{:S(2)}) async-start(bf16[4,2,32768]{2,1,0:T(2,128)(2,1)} %reshape.148), calls=%async_computation | async-start | bytes 1048576 | tf_op jit(solution)/shard_map/all_to_all | solution.py:39
  43.7 62.0 %all-gather.5.cloned.1.call-start = ((), (), s32[]{:S(2)}) async-start(), calls=%async_computation.3 | async-start | bytes 2621440 | tf_op jit(solution)/shard_map/all_gather | solution.py:93
  78.4 4.4 %copy-start.1 = (s32[4,1,64,8]{2,3,1,0:T(8,128)S(1)}, s32[4,1,64,8]{2,3,1,0:T(8,128)}, u32[]{:S(2)}) copy-start(s32[4,1,64,8]{2,3,1,0:T(8,128)} %param.16) | copy-start | bytes 24580
  81.8 151.0 %all-gather.7.cloned.1.call-start = ((), (), s32[]{:S(2)}) async-start(), calls=%async_computation.4 | async-start | bytes 9437184 | tf_op jit(solution)/shard_map/all_gather | solution.py:92
  82.6 214.9 %all-reduce.2.cloned.1.call-start = ((), (), s32[]{:S(2)}) async-start(), calls=%async_computation.5 | async-start | bytes 1572864 | tf_op jit(solution)/shard_map/psum | solution.py:135
  232.8 13.5 %copy-start.5 = (f32[1024]{0:T(1024)S(1)}, f32[1024]{0:T(1024)}, u32[]{:S(2)}) copy-start(f32[1024]{0:T(1024)} %param.15) | copy-start | bytes 12292
  298.8 6.9 %copy-start.4 = (f32[4,1,64,8]{2,3,1,0:T(8,128)S(1)}, f32[4,1,64,8]{2,3,1,0:T(8,128)}, u32[]{:S(2)}) copy-start(f32[4,1,64,8]{2,3,1,0:T(8,128)} %param.17) | copy-start | bytes 24580
  300.2 13.7 %all-to-all-start.2 = ((bf16[8,16,1024]{2,1,0:T(8,128)(2,1)}), bf16[8,16,1024]{2,1,0:T(8,128)(2,1)S(1)}, u32[]{:S(2)}, u32[]{:S(2)}) async-start(bf16[8,16,1024]{2,1,0:T(8,128)(2,1)} %bitcast.86), calls=%async_computation.2 | async-start | bytes 524288 | tf_op jit(solution)/shard_map/all_to_all | solution.py:140
Sparse Core Ops, SparseCore 0:
  81.9 23.7 all-gather.4
  107.8 124.9 all-gather.6
  264.1 33.3 all-reduce.1
where the time goes:
time: 324 us; the launch traced here: 323 us
  waiting for transfers between devices  191 us (59%)
  blocking collectives  35.4 us (11%)
  other arithmetic  29 us (9%)
  local copies, waits for them, and re-layouts  24.8 us (8%)
  matrix products  19.4 us (6%)
  between operations  13.3 us (4%)
  starting transfers between devices  10 us (3%)
    all_gather x1, waiting for transfers between devices, body(): full_weight = lax.all_gather(out_weight, 'exp', axis=0, tiled=True)  127 us
    psum x1, waiting for transfers between devices, body(): summed = lax.psum(partials.astype(jnp.bfloat16), 'ctx').astype(jnp.float32)  33.5 us
    unnamed x1, other arithmetic  24.4 us
    all_gather x1, waiting for transfers between devices, body(): piece = lax.all_gather(attended_rows, 'ctx', axis=0, tiled=True)  21.6 us
    all_gather x1, blocking collectives, body(): lax.all_gather(cached_keys_values.reshape(1, past_dev, kv_width), 'ctx',...  11.6 us
    all_to_all x1, blocking collectives, body(): lax.all_to_all(outgoing_rows.reshape(experts_here, capacity, width_block)...  11.4 us
    all_to_all x3, local copies, waits for them, and re-layouts, body(): lax.all_to_all(queries_flat, 'ctx', split_axis=2, concat_axis=0, tiled=True)  8.64 us
    all_to_all x1, waiting for transfers between devices, body(): lax.all_to_all(expert_out.reshape(experts_here, capacity, width_block), '...  8.12 us
  transfers between devices with their start and end apart: 5, of which 4 were waited for; matrix products, arithmetic and copies ran while one was open for 1% of the time, Pallas kernels for 0%

commit v1 on v0

v1 whole, which is shorter than its diff:
```python
import functools

import jax
import jax.numpy as jnp
from jax import lax
from jax.experimental import pallas as pl
from jax.experimental.pallas import tpu as pltpu
from jax.sharding import PartitionSpec as P

D = 4096
QUERY_HEADS = 32
KEY_VALUE_HEADS = 2
HEAD_SIZE = 128
GROUP_EXTENT = QUERY_HEADS // KEY_VALUE_HEADS
NEG_FILL = -1e30
BF16 = jnp.bfloat16
F32 = jnp.float32
VMEM = pl.BlockSpec(memory_space=pltpu.VMEM)


def call(kernel, out_shape, n_in, scratch=(), cost=(0, 0), limit=32, **kw):
    kw.setdefault("in_specs", [VMEM] * n_in)
    kw.setdefault("out_specs", jax.tree.map(lambda _: VMEM, out_shape))
    return pl.pallas_call(
        kernel,
        out_shape=out_shape,
        scratch_shapes=list(scratch),
        cost_estimate=pl.CostEstimate(flops=cost[0], bytes_accessed=cost[1], transcendentals=0),
        compiler_params=pltpu.CompilerParams(vmem_limit_bytes=limit * 2**20),
        **kw,
    )


def sds(shape, dtype):
    return jax.ShapeDtypeStruct(shape, dtype)


def dot(a, b):
    return jnp.dot(a, b, preferred_element_type=F32)


def pack_kernel(C, q_ref, new_ref, past_ref, *outs):
    c = lax.axis_index("ctx")
    lo = lax.rem(lax.axis_index("exp"), 2)
    heads = QUERY_HEADS // C
    qw = heads // 2 * HEAD_SIZE
    for t in range(2):
        for s in range(C):
            target = jnp.bitwise_xor(c, s)
            out = outs[t * C + s]
            offset = (target * heads + jnp.bitwise_xor(lo, t) * (heads // 2)) * HEAD_SIZE
            out[:, :qw] = q_ref[:, pl.ds(pl.multiple_of(offset, HEAD_SIZE), qw)]
            kv = lax.div(target * heads, GROUP_EXTENT)
            k_at = pl.ds(pl.multiple_of(kv * HEAD_SIZE, HEAD_SIZE), HEAD_SIZE)
            v_at = pl.ds(pl.multiple_of((KEY_VALUE_HEADS + kv) * HEAD_SIZE, HEAD_SIZE), HEAD_SIZE)
            out[:, qw : qw + 128] = new_ref[:, k_at]
            out[:, qw + 128 : qw + 256] = new_ref[:, v_at]
            out[:, qw + 256 : qw + 384] = past_ref[:, k_at]
            out[:, qw + 384 :] = past_ref[:, v_at]


def attend_kernel(C, tok, *refs):
    msgs, out, q_s, kv_s = refs[: 2 * C], refs[2 * C], refs[2 * C + 1], refs[2 * C + 2]
    c = lax.axis_index("ctx")
    qw = q_s.shape[2]
    rows = C * tok
    for t in range(2):
        for s in range(C):
            msg = msgs[t * C + s]
            at = pl.multiple_of(jnp.bitwise_xor(c, s) * tok, tok)
            q_s[t, pl.ds(at, tok), :] = msg[:, :qw]
            kv_s[t, pl.ds(rows + at, tok), :] = msg[:, qw : qw + 256]
            kv_s[t, pl.ds(at, tok), :] = msg[:, qw + 256 :]
    block = 128
    for t in range(2):
        for b in range(rows // block):
            seen = rows + (b + 1) * block
            k = kv_s[t, :seen, :HEAD_SIZE]
            v = kv_s[t, :seen, HEAD_SIZE:]
            row = lax.broadcasted_iota(jnp.int32, (block, seen), 0) + (rows + b * block)
            visible = lax.broadcasted_iota(jnp.int32, (block, seen), 1) <= row
            for h in range(qw // HEAD_SIZE):
                q = q_s[t, b * block : (b + 1) * block, h * HEAD_SIZE : (h + 1) * HEAD_SIZE]
                scores = lax.dot_general(q, k, (((1,), (1,)), ((), ())), preferred_element_type=F32)
                scores = jnp.where(visible, scores * HEAD_SIZE ** (-0.5), NEG_FILL)
                weights = jnp.exp(scores - jnp.max(scores, axis=1, keepdims=True))
                total = jnp.sum(weights, axis=1, keepdims=True)
                numerator = dot(weights.astype(BF16), v)
                out[
                    t * rows + b * block : t * rows + (b + 1) * block,
                    h * HEAD_SIZE : (h + 1) * HEAD_SIZE,
                ] = (numerator / total).astype(BF16)


def route_kernel(E, cap, routes_ref, gates_ref, place_ref, gate_ref):
    e = lax.axis_index("exp")
    rows = routes_ref.shape[0]
    routes = routes_ref[...]
    resident = routes < E
    target = jnp.sum(jnp.where(resident, routes, 0), axis=1, keepdims=True)
    has = jnp.sum(resident.astype(jnp.int32), axis=1, keepdims=True) > 0
    gate = jnp.sum(jnp.where(resident, gates_ref[...], 0.0), axis=1, keepdims=True)
    gate_ref[...] = jnp.broadcast_to(gate, gate_ref.shape)
    lanes = lax.broadcasted_iota(jnp.int32, (rows, 128), 1)
    one_hot = jnp.where((target == lanes) & has, 1.0, 0.0)
    earlier = (
        lax.broadcasted_iota(jnp.int32, (rows, rows), 1)
        < lax.broadcasted_iota(jnp.int32, (rows, rows), 0)
    ).astype(F32).astype(BF16)
    rank = jnp.sum(dot(earlier, one_hot.astype(BF16)) * one_hot, axis=1, keepdims=True)
    slot = jnp.bitwise_xor(target, e) * cap + rank.astype(jnp.int32)
    slot = jnp.where(has, slot, -1)
    places = lax.broadcasted_iota(jnp.int32, (rows, E * cap), 1)
    place_ref[...] = jnp.where(slot == places, 1.0, 0.0).astype(BF16)


def project_kernel(C, *refs):
    atts, ws = refs[:C], refs[C : C + 2 * (C - 1)]
    acc, last, stacked = refs[-3:]
    c = lax.axis_index("ctx")
    hi = lax.div(lax.axis_index("exp"), 2)
    for s in range(C):
        stacked[jnp.bitwise_xor(c, s)] = atts[s][...]
    half = ws[0].shape[1]
    for j in range(2):
        total = None
        for k in range(C - 1):
            term = dot(stacked[lax.rem(hi - k + C, C)], ws[2 * k + j][...])
            total = term if total is None else total + term
        acc[:, j * half : (j + 1) * half] = total
    last[...] = stacked[lax.rem(hi + 1, C)]


def last_kernel(j, acc_ref, last_ref, w_ref, own_ref, send_ref):
    half = w_ref.shape[1]
    rows = own_ref.shape[0]
    total = acc_ref[:, j * half : (j + 1) * half] + dot(last_ref[...], w_ref[...])
    own_ref[...] = total[:rows]
    send_ref[...] = total[rows:].astype(BF16)


def mix_kernel(E, cap, own0, own1, got0, got1, res_ref, gain_ref, place_ref, mixed_ref, *outs):
    half = own0.shape[1]
    for j, (own, got) in enumerate(((own0, got0), (own1, got1))):
        at = slice(j * half, (j + 1) * half)
        mixed = res_ref[:, at].astype(F32) + (own[...] + got[...].astype(F32))
        mixed_ref[:, at] = mixed
        scaled = (mixed * gain_ref[:, at]).astype(BF16)
        picked = lax.dot_general(
            place_ref[...], scaled, (((0,), (0,)), ((), ())), preferred_element_type=F32
        ).astype(BF16)
        for s in range(E):
            outs[s][:, at] = picked[s * cap : (s + 1) * cap]


def gate_up_kernel(C, E, cap, *refs):
    xs, gain_ref, w_ref = refs[:E], refs[E], refs[E + 1]
    outs, x_s, part_s, sq_s = refs[E + 2 : E + 2 + C], refs[-3], refs[-2], refs[-1]
    c = lax.axis_index("ctx")
    j = pl.program_id(0)
    own_rows = E * cap // C
    width = w_ref.shape[1]
    wide = outs[0].shape[1] - 128

    @pl.when(j == 0)
    def _():
        e = lax.axis_index("exp")
        for s in range(E):
            at = pl.multiple_of(jnp.bitwise_xor(e, s) * cap, cap)
            x_s[pl.ds(at, cap), :] = xs[s][...]
        plain = x_s[...].astype(F32) / gain_ref[...]
        square = jnp.sum(plain * plain, axis=1, keepdims=True)
        high = square.astype(BF16).astype(F32)
        lane = lax.broadcasted_iota(jnp.int32, sq_s.shape, 1)
        parts = jnp.where(lane == 0, high, jnp.where(lane == 1, square - high, 0.0))
        sq_s[...] = parts.astype(BF16)
        for s in range(C):
            at = pl.multiple_of(jnp.bitwise_xor(c, s) * own_rows, own_rows)
            outs[s][:, wide:] = sq_s[pl.ds(at, own_rows), :]

    part_s[...] = dot(x_s[...], w_ref[...]).astype(BF16)
    col = pl.multiple_of(j * width, 128)
    for s in range(C):
        at = pl.multiple_of(jnp.bitwise_xor(c, s) * own_rows, own_rows)
        outs[s][:, pl.ds(col, width)] = part_s[pl.ds(at, own_rows), :]


def activate_kernel(hidden, *refs):
    xs, out = refs[:-1], refs[-1]

    def summed(at):
        total = xs[0][:, at].astype(F32)
        for x in xs[1:]:
            total = total + x[:, at].astype(F32)
        return total

    square = jnp.sum(summed(slice(2 * hidden, 2 * hidden + 128)), axis=1, keepdims=True)
    scale = lax.rsqrt(square / D + 1e-6)
    gate = summed(slice(0, hidden)) * scale
    up = summed(slice(hidden, 2 * hidden)) * scale
    out[...] = (gate / (1.0 + jnp.exp(-gate)) * up).astype(BF16)


def down_kernel(C, E, cap, *refs):
    acts, w_ref, outs, x_s, part_s = refs[:C], refs[C], refs[C + 1 : C + 1 + E], refs[-2], refs[-1]
    c = lax.axis_index("ctx")
    e = lax.axis_index("exp")
    j = pl.program_id(0)
    own_rows = E * cap // C
    width = w_ref.shape[1]

    @pl.when(j == 0)
    def _():
        for s in range(C):
            at = pl.multiple_of(jnp.bitwise_xor(c, s) * own_rows, own_rows)
            x_s[pl.ds(at, own_rows), :] = acts[s][...]

    part_s[...] = dot(x_s[...], w_ref[...]).astype(BF16)
    col = pl.multiple_of(j * width, 128)
    for s in range(E):
        at = pl.multiple_of(jnp.bitwise_xor(e, s) * cap, cap)
        outs[s][:, pl.ds(col, width)] = part_s[pl.ds(at, cap), :]


def combine_kernel(E, cap, mixed_ref, place_ref, gate_ref, *refs):
    xs, out, x_s = refs[:E], refs[E], refs[E + 1]
    for s in range(E):
        x_s[s * cap : (s + 1) * cap, :] = xs[s][...]
    collected = dot(place_ref[...], x_s[...])
    out[...] = (mixed_ref[...] + gate_ref[:, :1] * collected).astype(BF16)


def body(
    queries,
    new_keys_values,
    cached_keys_values,
    residual,
    out_weight,
    norm_gain,
    routes,
    gates,
    w_gate_up,
    w_down,
):
    C = lax.axis_size("ctx")
    E = lax.axis_size("exp")
    tok = queries.shape[2]
    rows = C * tok
    width = residual.shape[3]
    hidden = w_down.shape[1]
    cap = rows // (2 * E)
    qw = QUERY_HEADS // C // 2 * HEAD_SIZE

    def permute(x, target):
        pairs = []
        for c in range(C):
            for e in range(E):
                c2, e2 = target(c, e)
                pairs.append((c * E + e, c2 * E + e2))
        return lax.ppermute(x, ("ctx", "exp"), pairs)

    def along_ctx(s):
        return lambda c, e: (c ^ s, e)

    def along_exp(s):
        return lambda c, e: (c, e ^ s)

    half = width // 2
    ring = lambda c, e: (c, (e + 2) % E)
    pieces = [[out_weight[:, j * half : (j + 1) * half] for j in range(2)]]

    msgs = call(
        functools.partial(pack_kernel, C),
        [sds((tok, qw + 512), BF16)] * (2 * C),
        3,
        cost=(0, 4 * 2**20),
    )(
        queries.reshape(tok, queries.shape[3]),
        new_keys_values.reshape(tok, new_keys_values.shape[3]),
        cached_keys_values.reshape(tok, cached_keys_values.shape[3]),
    )
    got = [msgs[0]]
    for i in range(1, 2 * C):
        t, s = divmod(i, C)
        got.append(permute(msgs[i], lambda c, e, s=s, t=t: (c ^ s, e ^ t)))
    for k in range(1, C):
        pieces.append([permute(p, ring) for p in pieces[-1]])

    place, gate = call(
        functools.partial(route_kernel, E, cap),
        [sds((rows, E * cap), BF16), sds((rows, 128), F32)],
        2,
        cost=(0, 2**20),
    )(routes.reshape(rows, routes.shape[3]), gates.reshape(rows, gates.shape[3]))

    attended = call(
        functools.partial(attend_kernel, C, tok),
        sds((2 * rows, qw), BF16),
        2 * C,
        scratch=[pltpu.VMEM((2, rows, qw), BF16), pltpu.VMEM((2, 2 * rows, 2 * HEAD_SIZE), BF16)],
        cost=(4 * 2 * rows * 2 * rows * qw, 16 * 2**20),
    )(*got)
    atts = [attended] + [permute(attended, along_ctx(s)) for s in range(1, C)]

    early = [p for pair in pieces[: C - 1] for p in pair]
    acc, last = call(
        functools.partial(project_kernel, C),
        [sds((2 * rows, width), F32), sds((2 * rows, qw), BF16)],
        C + len(early),
        scratch=[pltpu.VMEM((C, 2 * rows, qw), BF16)],
        cost=(4 * rows * qw * width * (C - 1), 8 * 2**20),
    )(*atts, *early)
    own, arrived = [], []
    for j in range(2):
        mine, send = call(
            functools.partial(last_kernel, j),
            [sds((rows, half), F32), sds((rows, half), BF16)],
            3,
            cost=(4 * rows * qw * half, 2**20),
        )(acc, last, pieces[C - 1][j])
        own.append(mine)
        arrived.append(permute(send, along_exp(1)))

    gain = norm_gain.reshape(1, width)
    mixed, *outgoing = call(
        functools.partial(mix_kernel, E, cap),
        [sds((rows, width), F32)] + [sds((cap, width), BF16)] * E,
        7,
        cost=(0, 4 * 2**20),
    )(*own, *arrived, residual.reshape(rows, width), gain, place)
    incoming = [outgoing[0]] + [permute(outgoing[s], along_exp(s)) for s in range(1, E)]

    slots = E * cap
    own_rows = slots // C
    steps = 4
    wide = 2 * hidden
    whole = lambda shape: pl.BlockSpec(shape, lambda j: (0,) * len(shape))
    partials = call(
        functools.partial(gate_up_kernel, C, E, cap),
        [sds((own_rows, wide + 128), BF16)] * C,
        E + 2,
        scratch=[
            pltpu.VMEM((slots, width), BF16),
            pltpu.VMEM((slots, wide // steps), BF16),
            pltpu.VMEM((slots, 128), BF16),
        ],
        cost=(2 * slots * width * wide, 2 * width * wide),
        grid=(steps,),
        in_specs=[whole((cap, width))] * E
        + [whole((1, width)), pl.BlockSpec((width, wide // steps), lambda j: (0, j))],
        out_specs=[whole((own_rows, wide + 128))] * C,
    )(*incoming, gain, w_gate_up.reshape(width, wide))
    terms = [partials[0]] + [permute(partials[s], along_ctx(s)) for s in range(1, C)]
    activated = call(
        functools.partial(activate_kernel, hidden),
        sds((own_rows, hidden), BF16),
        C,
        cost=(0, 2**20),
    )(*terms)
    acts = [activated] + [permute(activated, along_ctx(s)) for s in range(1, C)]
    steps = 2
    expert_out = call(
        functools.partial(down_kernel, C, E, cap),
        [sds((cap, width), BF16)] * E,
        C + 1,
        scratch=[pltpu.VMEM((slots, hidden), BF16), pltpu.VMEM((slots, width // steps), BF16)],
        cost=(2 * slots * width * hidden, 2 * width * hidden),
        grid=(steps,),
        in_specs=[whole((own_rows, hidden))] * C
        + [pl.BlockSpec((hidden, width // steps), lambda j: (0, j))],
        out_specs=[whole((cap, width))] * E,
    )(*acts, w_down.reshape(hidden, width))
    returned = [expert_out[0]] + [permute(expert_out[s], along_exp(s)) for s in range(1, E)]
    result = call(
        functools.partial(combine_kernel, E, cap),
        sds((rows, width), BF16),
        3 + E,
        scratch=[pltpu.VMEM((slots, width), BF16)],
        cost=(0, 2 * 2**20),
    )(mixed, place, gate, *returned)
    return result.reshape(C, 1, tok, width)


def solution(mesh):
    in_specs = (
        P("ctx", "exp", None, None),
        P("ctx", "exp", None, None),
        P("ctx", "exp", None, None),
        P(None, "exp", None, "ctx"),
        P("exp", "ctx"),
        P("ctx"),
        P(None, "exp", None, None),
        P(None, "exp", None, None),
        P("exp", "ctx", None),
        P("exp", None, "ctx"),
    )
    out_specs = P(None, "exp", None, "ctx")
    return jax.shard_map(body, mesh=mesh, in_specs=in_specs, out_specs=out_specs, check_vma=False)
```

time: 324 us -> 153 us (0.47)
  waiting for transfers between devices: 191 us -> 88 us
  blocking collectives: 35.4 us -> 0 us
  starting transfers between devices: 10 us -> 44.3 us
  other arithmetic: 29 us -> 0 us
  matrix products: 19.4 us -> 0 us
  local copies, waits for them, and re-layouts: 24.8 us -> 6.97 us
  between operations: 13.3 us -> 0.19 us
  Pallas kernels: 0 us -> 12.8 us
    all_gather x2 -> x0, waiting for transfers between devices: 149 us -> none  [the longest x1 127 us: body(): full_weight = lax.all_gather(out_weight, 'exp', axis=0, tiled=True)]
    ppermute x0 -> x38, waiting for transfers between devices: none -> 88 us  [permute(): return lax.ppermute(x, ('ctx', 'exp'), pairs)]
    ppermute x0 -> x38, starting transfers between devices: none -> 44.3 us  [permute(): return lax.ppermute(x, ('ctx', 'exp'), pairs)]
    psum x1 -> x0, waiting for transfers between devices: 33.5 us -> none  [body(): summed = lax.psum(partials.astype(jnp.bfloat16), 'ctx').astype(jnp.float32)]
    unnamed x1 -> x0, other arithmetic: 24.4 us -> none
    dot_general x7 -> x0, matrix products: 19.4 us -> none  [the longest x1 7.35 us: body(): jnp.einsum('krc,kcd->rd', piece, full_weight.reshape(count, head_width, w...]
    all_gather x2 -> x0, blocking collectives: 17.9 us -> none  [the longest x1 11.6 us: body(): lax.all_gather(cached_keys_values.reshape(1, past_dev, kv_width), 'ctx',...]
    pallas_call x0 -> x11, Pallas kernels: none -> 12.8 us  [the longest x1 4.38 us: body(): call(functools.partial(attend_kernel, C, tok), sds((2 * rows, qw), BF16),...]
  transfers between devices with their start and end apart: 5 -> 38, of which waited for: 4 -> 21; matrix products, arithmetic and copies ran while one was open for 1% -> 0% of each run, Pallas kernels for 0% -> 5%
where the time goes in v1:
time: 153 us; the launch traced here: 152 us
  waiting for transfers between devices  88 us (58%)
  starting transfers between devices  44.3 us (29%)
  Pallas kernels  12.8 us (8%)
  local copies, waits for them, and re-layouts  6.97 us (5%)
    ppermute x38, waiting for transfers between devices, permute(): return lax.ppermute(x, ('ctx', 'exp'), pairs)  88 us
    ppermute x38, starting transfers between devices, permute(): return lax.ppermute(x, ('ctx', 'exp'), pairs)  44.3 us
    unnamed x20, local copies, waits for them, and re-layouts  5.71 us
    pallas_call x1, Pallas kernels, body(): call(functools.partial(attend_kernel, C, tok), sds((2 * rows, qw), BF16),...  4.38 us
  transfers between devices with their start and end apart: 38, of which 21 were waited for; matrix products, arithmetic and copies ran while one was open for 0% of the time, Pallas kernels for 5%

profile of v1, /device:TPU:0, one launch (start us, length us, event | category | flops | bytes accessed | tf_op | source)
XLA Modules:
  0.0 152.2 jit_solution(12885663614290650089)
XLA Ops:
  0.0 1.3 fusion
  1.3 3.1 %collective-permute-start.11 = (bf16[512,512]{1,0:T(8,128)(2,1)S(1)}, bf16[512,512]{1,0:T(8,128)(2,1)S(1)}, u32[]{:S(2)}, u32[]{:S(2)}) collective-permute-start(bf16[512,512]{1,0:T(8,128)(2,1)S(1)} %get-tuple-element.79.refs_5_), channel_id=1, source_target_pairs={{0,2},{1,3},{2,4},{3,5},{4,6},{5,7},{6,0},{7,1},{8,10},{9,11},{10,... | collective-permute-start | bytes 1572872 | tf_op jit(solution)/shard_map/ppermute | solution.py:260
  4.3 1.6 %collective-permute-start.10 = (bf16[512,512]{1,0:T(8,128)(2,1)S(1)}, bf16[512,512]{1,0:T(8,128)(2,1)S(1)}, u32[]{:S(2)}, u32[]{:S(2)}) collective-permute-start(bf16[512,512]{1,0:T(8,128)(2,1)S(1)} %get-tuple-element.80.refs_4_), channel_id=1, source_target_pairs={{0,2},{1,3},{2,4},{3,5},{4,6},{5,7},{6,0},{7,1},{8,10},{9,11},{10,... | collective-permute-start | bytes 1572872 | tf_op jit(solution)/shard_map/ppermute | solution.py:260
  5.9 1.0 copy-done.2
  8.9 10.2 %collective-permute-done.11.refs_7_ = bf16[512,512]{1,0:T(8,128)(2,1)S(1)} collective-permute-done((bf16[512,512]{1,0:T(8,128)(2,1)S(1)}, bf16[512,512]{1,0:T(8,128)(2,1)S(1)}, u32[]{:S(2)}, u32[]{:S(2)}) %collective-permute-start.11) | collective-permute-done | bytes 524320 | tf_op jit(solution)/shard_map/ppermute | solution.py:260
  19.2 11.2 %collective-permute-done.10.refs_6_ = bf16[512,512]{1,0:T(8,128)(2,1)S(1)} collective-permute-done((bf16[512,512]{1,0:T(8,128)(2,1)S(1)}, bf16[512,512]{1,0:T(8,128)(2,1)S(1)}, u32[]{:S(2)}, u32[]{:S(2)}) %collective-permute-start.10) | collective-permute-done | bytes 524320 | tf_op jit(solution)/shard_map/ppermute | solution.py:260
  30.4 1.7 %collective-permute-start.1 = (bf16[64,1024]{1,0:T(8,128)(2,1)S(1)}, bf16[64,1024]{1,0:T(8,128)(2,1)S(1)}, u32[]{:S(2)}, u32[]{:S(2)}) collective-permute-start(bf16[64,1024]{1,0:T(8,128)(2,1)S(1)} %get-tuple-element.44), channel_id=1, source_target_pairs={{0,16},{1,17},{2,18},{3,19},{4,20},{5,21},{6,22},{7,23},{8,24},{9,... | collective-permute-start | bytes 393224 | tf_op jit(solution)/shard_map/ppermute | solution.py:260
  32.1 1.5 collective-permute-start.3
  33.6 2.1 %collective-permute-done.1.refs_2_ = bf16[64,1024]{1,0:T(8,128)(2,1)S(1)} collective-permute-done((bf16[64,1024]{1,0:T(8,128)(2,1)S(1)}, bf16[64,1024]{1,0:T(8,128)(2,1)S(1)}, u32[]{:S(2)}, u32[]{:S(2)}) %collective-permute-start.1) | collective-permute-done | bytes 131104 | tf_op jit(solution)/shard_map/ppermute | solution.py:260
  35.7 2.2 %collective-permute-done.2.refs_3_ = bf16[64,1024]{1,0:T(8,128)(2,1)S(1)} collective-permute-done((bf16[64,1024]{1,0:T(8,128)(2,1)S(1)}, bf16[64,1024]{1,0:T(8,128)(2,1)S(1)}, u32[]{:S(2)}, u32[]{:S(2)}) %collective-permute-start.2) | collective-permute-done | bytes 131104 | tf_op jit(solution)/shard_map/ppermute | solution.py:260
  37.9 1.4 collective-permute-start.5
  39.4 1.2 collective-permute-start.6
  41.3 5.2 %collective-permute-done.5.refs_6_ = bf16[64,1024]{1,0:T(8,128)(2,1)S(1)} collective-permute-done((bf16[64,1024]{1,0:T(8,128)(2,1)S(1)}, bf16[64,1024]{1,0:T(8,128)(2,1)S(1)}, u32[]{:S(2)}, u32[]{:S(2)}) %collective-permute-start.5) | collective-permute-done | bytes 131104 | tf_op jit(solution)/shard_map/ppermute | solution.py:260
  46.5 2.3 %collective-permute-done.6.refs_7_ = bf16[64,1024]{1,0:T(8,128)(2,1)S(1)} collective-permute-done((bf16[64,1024]{1,0:T(8,128)(2,1)S(1)}, bf16[64,1024]{1,0:T(8,128)(2,1)S(1)}, u32[]{:S(2)}, u32[]{:S(2)}) %collective-permute-start.6) | collective-permute-done | bytes 131104 | tf_op jit(solution)/shard_map/ppermute | solution.py:260
  48.8 4.4 %shard_map.101.refs_0_ = bf16[512,512]{1,0:T(8,128)(2,1)S(1)} custom-call(bf16[64,1024]{1,0:T(8,128)(2,1)S(1)} %get-tuple-element.42.refs_0_, bf16[64,1024]{1,0:T(8,128)(2,1)S(1)} %collective-permute-done.refs_1_, bf16[64,1024]{1,0:T(8,128)(2,1)S(1)} %collective-permute-done.1.refs_2_, bf16[64,1024]{1,0:T(8,128)(2,1)S(1)} %collective-permute-done.2.refs_3_, ...), custom_call_target="tpu_custom_call" | custom-call | flops 536870912 | bytes 16777216 | tf_op jit(solution)/shard_map/pallas_call | solution.py:296
  53.6 1.5 collective-permute-start.9
  55.1 1.8 %collective-permute-start.15 = (bf16[512,512]{1,0:T(8,128)(2,1)S(1)}, bf16[512,512]{1,0:T(8,128)(2,1)S(1)}, u32[]{:S(2)}, u32[]{:S(2)}) collective-permute-start(bf16[512,512]{1,0:T(8,128)(2,1)S(1)} %collective-permute-done.13.refs_9_), channel_id=1, source_target_pairs={{0,2},{1,3},{2,4},{3,5},{4,6},{5,7},{6,0},{7,1},{8,10},{9,11},{10,... | collective-permute-start | bytes 1572872 | tf_op jit(solution)/shard_map/ppermute | solution.py:260
  57.0 1.5 collective-permute-start.14
  58.5 9.9 %collective-permute-done.8.refs_2_ = bf16[512,512]{1,0:T(8,128)(2,1)S(1)} collective-permute-done((bf16[512,512]{1,0:T(8,128)(2,1)S(1)}, bf16[512,512]{1,0:T(8,128)(2,1)S(1)}, u32[]{:S(2)}, u32[]{:S(2)}) %collective-permute-start.8) | collective-permute-done | bytes 524320 | tf_op jit(solution)/shard_map/ppermute | solution.py:260
  68.4 9.6 %collective-permute-done.9.refs_3_ = bf16[512,512]{1,0:T(8,128)(2,1)S(1)} collective-permute-done((bf16[512,512]{1,0:T(8,128)(2,1)S(1)}, bf16[512,512]{1,0:T(8,128)(2,1)S(1)}, u32[]{:S(2)}, u32[]{:S(2)}) %collective-permute-start.9) | collective-permute-done | bytes 524320 | tf_op jit(solution)/shard_map/ppermute | solution.py:260
  78.0 1.9 %shard_map.102 = (f32[512,1024]{1,0:T(8,128)S(1)}, bf16[512,512]{1,0:T(8,128)(2,1)S(1)}) custom-call(bf16[512,512]{1,0:T(8,128)(2,1)S(1)} %shard_map.101.refs_0_, bf16[512,512]{1,0:T(8,128)(2,1)S(1)} %collective-permute-done.7.refs_1_, bf16[512,512]{1,0:T(8,128)(2,1)S(1)} %collective-permute-done.8.refs_2_, ...), custom_call_target="tpu_custom_call" | custom-call | flops 1610612736 | bytes 8388608 | tf_op jit(solution)/shard_map/pallas_call | solution.py:306
  80.5 1.3 collective-permute-start.17
  81.7 0.9 collective-permute-done.14.w_ref
  83.1 0.9 collective-permute-start.16
  84.6 5.1 %collective-permute-done.17.got1 = bf16[256,512]{1,0:T(8,128)(2,1)S(1)} collective-permute-done((bf16[256,512]{1,0:T(8,128)(2,1)S(1)}, bf16[256,512]{1,0:T(8,128)(2,1)S(1)}, u32[]{:S(2)}, u32[]{:S(2)}) %collective-permute-start.17) | collective-permute-done | bytes 262176 | tf_op jit(solution)/shard_map/ppermute | solution.py:260
  89.7 5.6 %collective-permute-done.16.got0 = bf16[256,512]{1,0:T(8,128)(2,1)S(1)} collective-permute-done((bf16[256,512]{1,0:T(8,128)(2,1)S(1)}, bf16[256,512]{1,0:T(8,128)(2,1)S(1)}, u32[]{:S(2)}, u32[]{:S(2)}) %collective-permute-start.16) | collective-permute-done | bytes 262176 | tf_op jit(solution)/shard_map/ppermute | solution.py:260
  95.7 0.9 collective-permute-start.18
  96.6 1.6 %collective-permute-start.19 = (bf16[16,1024]{1,0:T(8,128)(2,1)S(1)}, bf16[16,1024]{1,0:T(8,128)(2,1)S(1)}, u32[]{:S(2)}, u32[]{:S(2)}) collective-permute-start(bf16[16,1024]{1,0:T(8,128)(2,1)S(1)} %get-tuple-element.61), channel_id=1, source_target_pairs={{0,2},{1,3},{2,0},{3,1},{4,6},{5,7},{6,4},{7,5},{8,10},{9,11},{10,... | collective-permute-start | bytes 98312 | tf_op jit(solution)/shard_map/ppermute | solution.py:260
  98.2 1.1 collective-permute-start.20
  99.2 2.8 %collective-permute-start.21 = (bf16[16,1024]{1,0:T(8,128)(2,1)S(1)}, bf16[16,1024]{1,0:T(8,128)(2,1)S(1)}, u32[]{:S(2)}, u32[]{:S(2)}) collective-permute-start(bf16[16,1024]{1,0:T(8,128)(2,1)S(1)} %get-tuple-element.63), channel_id=1, source_target_pairs={{0,4},{1,5},{2,6},{3,7},{4,0},{5,1},{6,2},{7,3},{8,12},{9,13},{10,... | collective-permute-start | bytes 98312 | tf_op jit(solution)/shard_map/ppermute | solution.py:260
  102.4 3.8 %collective-permute-start.23 = (bf16[16,1024]{1,0:T(8,128)(2,1)S(1)}, bf16[16,1024]{1,0:T(8,128)(2,1)S(1)}, u32[]{:S(2)}, u32[]{:S(2)}) collective-permute-start(bf16[16,1024]{1,0:T(8,128)(2,1)S(1)} %get-tuple-element.65), channel_id=1, source_target_pairs={{0,6},{1,7},{2,4},{3,5},{4,2},{5,3},{6,0},{7,1},{8,14},{9,15},{10,... | collective-permute-start | bytes 98312 | tf_op jit(solution)/shard_map/ppermute | solution.py:260
  106.9 0.8 collective-permute-done.22.refs_5_
  108.4 4.4 %collective-permute-done.24.refs_7_ = bf16[16,1024]{1,0:T(8,128)(2,1)S(1)} collective-permute-done((bf16[16,1024]{1,0:T(8,128)(2,1)S(1)}, bf16[16,1024]{1,0:T(8,128)(2,1)S(1)}, u32[]{:S(2)}, u32[]{:S(2)}) %collective-permute-start.24) | collective-permute-done | bytes 32800 | tf_op jit(solution)/shard_map/ppermute | solution.py:260
  112.8 2.8 %copy-done = bf16[1,1024,3072]{2,1,0:T(8,128)(2,1)S(1)} copy-done((bf16[1,1024,3072]{2,1,0:T(8,128)(2,1)S(1)}, bf16[1,1024,3072]{2,1,0:T(8,128)(2,1)}, u32[]{:S(2)}) %copy-start) | copy-done | bytes 6291480
  115.6 2.3 %shard_map.107 = (bf16[32,3200]{1,0:T(8,128)(2,1)S(1)}, bf16[32,3200]{1,0:T(8,128)(2,1)S(1)}, bf16[32,3200]{1,0:T(8,128)(2,1)S(1)}, bf16[32,3200]{1,0:T(8,128)(2,1)S(1)}) custom-call(bf16[16,1024]{1,0:T(8,128)(2,1)S(1)} %get-tuple-element.59.refs_0_, bf16[16,1024]{1,0:T(8,128)(2,1)S(1)} %collective-permute-done.18.refs_1_, ...), custom_call_target="tpu_custom_call" | custom-call | flops 805306368 | bytes 6291456 | tf_op jit(solution)/shard_map/pallas_call | solution.py:338
  118.5 1.4 collective-permute-start.27
  119.9 6.1 %collective-permute-done.26.refs_2_ = bf16[32,3200]{1,0:T(8,128)(2,1)S(1)} collective-permute-done((bf16[32,3200]{1,0:T(8,128)(2,1)S(1)}, bf16[32,3200]{1,0:T(8,128)(2,1)S(1)}, u32[]{:S(2)}, u32[]{:S(2)}) %collective-permute-start.26) | collective-permute-done | bytes 204832 | tf_op jit(solution)/shard_map/ppermute | solution.py:260
  125.9 3.5 %collective-permute-done.27.refs_3_ = bf16[32,3200]{1,0:T(8,128)(2,1)S(1)} collective-permute-done((bf16[32,3200]{1,0:T(8,128)(2,1)S(1)}, bf16[32,3200]{1,0:T(8,128)(2,1)S(1)}, u32[]{:S(2)}, u32[]{:S(2)}) %collective-permute-start.27) | collective-permute-done | bytes 204832 | tf_op jit(solution)/shard_map/ppermute | solution.py:260
  130.4 1.2 collective-permute-start.30
  131.5 4.1 %collective-permute-done.29.refs_2_ = bf16[32,1536]{1,0:T(8,128)(2,1)S(1)} collective-permute-done((bf16[32,1536]{1,0:T(8,128)(2,1)S(1)}, bf16[32,1536]{1,0:T(8,128)(2,1)S(1)}, u32[]{:S(2)}, u32[]{:S(2)}) %collective-permute-start.29) | collective-permute-done | bytes 98336 | tf_op jit(solution)/shard_map/ppermute | solution.py:260
  136.3 1.1 shard_map.109
  137.4 1.2 collective-permute-start.31
  138.6 2.3 %collective-permute-start.33 = (bf16[16,1024]{1,0:T(8,128)(2,1)S(1)}, bf16[16,1024]{1,0:T(8,128)(2,1)S(1)}, u32[]{:S(2)}, u32[]{:S(2)}) collective-permute-start(bf16[16,1024]{1,0:T(8,128)(2,1)S(1)} %get-tuple-element.74), channel_id=1, source_target_pairs={{0,3},{1,2},{2,1},{3,0},{4,7},{5,6},{6,5},{7,4},{8,11},{9,10},{10,... | collective-permute-start | bytes 98312 | tf_op jit(solution)/shard_map/ppermute | solution.py:260
  140.9 3.5 %collective-permute-start.35 = (bf16[16,1024]{1,0:T(8,128)(2,1)S(1)}, bf16[16,1024]{1,0:T(8,128)(2,1)S(1)}, u32[]{:S(2)}, u32[]{:S(2)}) collective-permute-start(bf16[16,1024]{1,0:T(8,128)(2,1)S(1)} %get-tuple-element.76), channel_id=1, source_target_pairs={{0,5},{1,4},{2,7},{3,6},{4,1},{5,0},{6,3},{7,2},{8,13},{9,12},{10,... | collective-permute-start | bytes 98312 | tf_op jit(solution)/shard_map/ppermute | solution.py:260
  144.5 4.1 %collective-permute-start.37 = (bf16[16,1024]{1,0:T(8,128)(2,1)S(1)}, bf16[16,1024]{1,0:T(8,128)(2,1)S(1)}, u32[]{:S(2)}, u32[]{:S(2)}) collective-permute-start(bf16[16,1024]{1,0:T(8,128)(2,1)S(1)} %get-tuple-element.78), channel_id=1, source_target_pairs={{0,7},{1,6},{2,5},{3,4},{4,3},{5,2},{6,1},{7,0},{8,15},{9,14},{10,... | collective-permute-start | bytes 98312 | tf_op jit(solution)/shard_map/ppermute | solution.py:260
  148.6 1.6 %collective-permute-done.36.refs_6_ = bf16[16,1024]{1,0:T(8,128)(2,1)S(1)} collective-permute-done((bf16[16,1024]{1,0:T(8,128)(2,1)S(1)}, bf16[16,1024]{1,0:T(8,128)(2,1)S(1)}, u32[]{:S(2)}, u32[]{:S(2)}) %collective-permute-start.36) | collective-permute-done | bytes 32800 | tf_op jit(solution)/shard_map/ppermute | solution.py:260
  150.2 1.0 collective-permute-done.37.refs_7_
  151.1 1.1 shard_map.110
  (60 shorter events, 9.2 us)
Async XLA Ops:
  1.3 17.9 %collective-permute-start.11 = (bf16[512,512]{1,0:T(8,128)(2,1)S(1)}, bf16[512,512]{1,0:T(8,128)(2,1)S(1)}, u32[]{:S(2)}, u32[]{:S(2)}) collective-permute-start(bf16[512,512]{1,0:T(8,128)(2,1)S(1)} %get-tuple-element.79.refs_5_), channel_id=1, source_target_pairs={{0,2},{1,3},{2,4},{3,5},{4,6},{5,7},{6,0},{7,1},{8,10},{9,11},{10,... | collective-permute-start | bytes 1572872 | tf_op jit(solution)/shard_map/ppermute | solution.py:260
  4.3 26.0 %collective-permute-start.10 = (bf16[512,512]{1,0:T(8,128)(2,1)S(1)}, bf16[512,512]{1,0:T(8,128)(2,1)S(1)}, u32[]{:S(2)}, u32[]{:S(2)}) collective-permute-start(bf16[512,512]{1,0:T(8,128)(2,1)S(1)} %get-tuple-element.80.refs_4_), channel_id=1, source_target_pairs={{0,2},{1,3},{2,4},{3,5},{4,6},{5,7},{6,0},{7,1},{8,10},{9,11},{10,... | collective-permute-start | bytes 1572872 | tf_op jit(solution)/shard_map/ppermute | solution.py:260
  5.9 1.0 copy-start.2
  7.0 0.8 copy-start.4
  7.8 0.8 copy-start.5
  8.8 23.3 %collective-permute-start = (bf16[64,1024]{1,0:T(8,128)(2,1)S(1)}, bf16[64,1024]{1,0:T(8,128)(2,1)S(1)}, u32[]{:S(2)}, u32[]{:S(2)}) collective-permute-start(bf16[64,1024]{1,0:T(8,128)(2,1)S(1)} %get-tuple-element.43), channel_id=1, source_target_pairs={{0,8},{1,9},{2,10},{3,11},{4,12},{5,13},{6,14},{7,15},{8,0},{9,1},... | collective-permute-start | bytes 393224 | tf_op jit(solution)/shard_map/ppermute | solution.py:260
  19.1 36.0 %collective-permute-start.13 = (bf16[512,512]{1,0:T(8,128)(2,1)S(1)}, bf16[512,512]{1,0:T(8,128)(2,1)S(1)}, u32[]{:S(2)}, u32[]{:S(2)}) collective-permute-start(bf16[512,512]{1,0:T(8,128)(2,1)S(1)} %collective-permute-done.11.refs_7_), channel_id=1, source_target_pairs={{0,2},{1,3},{2,4},{3,5},{4,6},{5,7},{6,0},{7,1},{8,10},{9,11},{10,... | collective-permute-start | bytes 1572872 | tf_op jit(solution)/shard_map/ppermute | solution.py:260
  30.4 26.6 %collective-permute-start.12 = (bf16[512,512]{1,0:T(8,128)(2,1)S(1)}, bf16[512,512]{1,0:T(8,128)(2,1)S(1)}, u32[]{:S(2)}, u32[]{:S(2)}) collective-permute-start(bf16[512,512]{1,0:T(8,128)(2,1)S(1)} %collective-permute-done.10.refs_6_), channel_id=1, source_target_pairs={{0,2},{1,3},{2,4},{3,5},{4,6},{5,7},{6,0},{7,1},{8,10},{9,11},{10,... | collective-permute-start | bytes 1572872 | tf_op jit(solution)/shard_map/ppermute | solution.py:260
  30.4 5.3 %collective-permute-start.1 = (bf16[64,1024]{1,0:T(8,128)(2,1)S(1)}, bf16[64,1024]{1,0:T(8,128)(2,1)S(1)}, u32[]{:S(2)}, u32[]{:S(2)}) collective-permute-start(bf16[64,1024]{1,0:T(8,128)(2,1)S(1)} %get-tuple-element.44), channel_id=1, source_target_pairs={{0,16},{1,17},{2,18},{3,19},{4,20},{5,21},{6,22},{7,23},{8,24},{9,... | collective-permute-start | bytes 393224 | tf_op jit(solution)/shard_map/ppermute | solution.py:260
  32.1 5.8 %collective-permute-start.2 = (bf16[64,1024]{1,0:T(8,128)(2,1)S(1)}, bf16[64,1024]{1,0:T(8,128)(2,1)S(1)}, u32[]{:S(2)}, u32[]{:S(2)}) collective-permute-start(bf16[64,1024]{1,0:T(8,128)(2,1)S(1)} %get-tuple-element.45), channel_id=1, source_target_pairs={{0,24},{1,25},{2,26},{3,27},{4,28},{5,29},{6,30},{7,31},{8,16},{9,... | collective-permute-start | bytes 393224 | tf_op jit(solution)/shard_map/ppermute | solution.py:260
  32.1 7.2 %collective-permute-start.3 = (bf16[64,1024]{1,0:T(8,128)(2,1)S(1)}, bf16[64,1024]{1,0:T(8,128)(2,1)S(1)}, u32[]{:S(2)}, u32[]{:S(2)}) collective-permute-start(bf16[64,1024]{1,0:T(8,128)(2,1)S(1)} %get-tuple-element.46), channel_id=1, source_target_pairs={{0,1},{1,0},{2,3},{3,2},{4,5},{5,4},{6,7},{7,6},{8,9},{9,8},{10,11... | collective-permute-start | bytes 393224 | tf_op jit(solution)/shard_map/ppermute | solution.py:260
  35.7 5.5 %collective-permute-start.4 = (bf16[64,1024]{1,0:T(8,128)(2,1)S(1)}, bf16[64,1024]{1,0:T(8,128)(2,1)S(1)}, u32[]{:S(2)}, u32[]{:S(2)}) collective-permute-start(bf16[64,1024]{1,0:T(8,128)(2,1)S(1)} %get-tuple-element.47), channel_id=1, source_target_pairs={{0,9},{1,8},{2,11},{3,10},{4,13},{5,12},{6,15},{7,14},{8,1},{9,0},... | collective-permute-start | bytes 393224 | tf_op jit(solution)/shard_map/ppermute | solution.py:260
  37.9 8.6 %collective-permute-start.5 = (bf16[64,1024]{1,0:T(8,128)(2,1)S(1)}, bf16[64,1024]{1,0:T(8,128)(2,1)S(1)}, u32[]{:S(2)}, u32[]{:S(2)}) collective-permute-start(bf16[64,1024]{1,0:T(8,128)(2,1)S(1)} %get-tuple-element.48), channel_id=1, source_target_pairs={{0,17},{1,16},{2,19},{3,18},{4,21},{5,20},{6,23},{7,22},{8,25},{9,... | collective-permute-start | bytes 393224 | tf_op jit(solution)/shard_map/ppermute | solution.py:260
  39.4 9.4 %collective-permute-start.6 = (bf16[64,1024]{1,0:T(8,128)(2,1)S(1)}, bf16[64,1024]{1,0:T(8,128)(2,1)S(1)}, u32[]{:S(2)}, u32[]{:S(2)}) collective-permute-start(bf16[64,1024]{1,0:T(8,128)(2,1)S(1)} %get-tuple-element.49), channel_id=1, source_target_pairs={{0,25},{1,24},{2,27},{3,26},{4,29},{5,28},{6,31},{7,30},{8,17},{9,... | collective-permute-start | bytes 393224 | tf_op jit(solution)/shard_map/ppermute | solution.py:260
  53.2 5.3 %collective-permute-start.7 = (bf16[512,512]{1,0:T(8,128)(2,1)S(1)}, bf16[512,512]{1,0:T(8,128)(2,1)S(1)}, u32[]{:S(2)}, u32[]{:S(2)}) collective-permute-start(bf16[512,512]{1,0:T(8,128)(2,1)S(1)} %shard_map.101.refs_0_), channel_id=1, source_target_pairs={{0,8},{1,9},{2,10},{3,11},{4,12},{5,13},{6,14},{7,15},{8,0},{9,1},... | collective-permute-start | bytes 1572872 | tf_op jit(solution)/shard_map/ppermute | solution.py:260
  53.6 14.8 %collective-permute-start.8 = (bf16[512,512]{1,0:T(8,128)(2,1)S(1)}, bf16[512,512]{1,0:T(8,128)(2,1)S(1)}, u32[]{:S(2)}, u32[]{:S(2)}) collective-permute-start(bf16[512,512]{1,0:T(8,128)(2,1)S(1)} %shard_map.101.refs_0_), channel_id=1, source_target_pairs={{0,16},{1,17},{2,18},{3,19},{4,20},{5,21},{6,22},{7,23},{8,24},{9,... | collective-permute-start | bytes 1572872 | tf_op jit(solution)/shard_map/ppermute | solution.py:260
  53.6 24.4 %collective-permute-start.9 = (bf16[512,512]{1,0:T(8,128)(2,1)S(1)}, bf16[512,512]{1,0:T(8,128)(2,1)S(1)}, u32[]{:S(2)}, u32[]{:S(2)}) collective-permute-start(bf16[512,512]{1,0:T(8,128)(2,1)S(1)} %shard_map.101.refs_0_), channel_id=1, source_target_pairs={{0,24},{1,25},{2,26},{3,27},{4,28},{5,29},{6,30},{7,31},{8,16},{9,... | collective-permute-start | bytes 1572872 | tf_op jit(solution)/shard_map/ppermute | solution.py:260
  55.1 24.8 %collective-permute-start.15 = (bf16[512,512]{1,0:T(8,128)(2,1)S(1)}, bf16[512,512]{1,0:T(8,128)(2,1)S(1)}, u32[]{:S(2)}, u32[]{:S(2)}) collective-permute-start(bf16[512,512]{1,0:T(8,128)(2,1)S(1)} %collective-permute-done.13.refs_9_), channel_id=1, source_target_pairs={{0,2},{1,3},{2,4},{3,5},{4,6},{5,7},{6,0},{7,1},{8,10},{9,11},{10,... | collective-permute-start | bytes 1572872 | tf_op jit(solution)/shard_map/ppermute | solution.py:260
  57.0 25.7 %collective-permute-start.14 = (bf16[512,512]{1,0:T(8,128)(2,1)S(1)}, bf16[512,512]{1,0:T(8,128)(2,1)S(1)}, u32[]{:S(2)}, u32[]{:S(2)}) collective-permute-start(bf16[512,512]{1,0:T(8,128)(2,1)S(1)} %collective-permute-done.12.refs_8_), channel_id=1, source_target_pairs={{0,2},{1,3},{2,4},{3,5},{4,6},{5,7},{6,0},{7,1},{8,10},{9,11},{10,... | collective-permute-start | bytes 1572872 | tf_op jit(solution)/shard_map/ppermute | solution.py:260
  80.0 4.0 %copy-start.7 = (s32[4,1,64,8]{2,3,1,0:T(8,128)S(1)}, s32[4,1,64,8]{2,3,1,0:T(8,128)}, u32[]{:S(2)}) copy-start(s32[4,1,64,8]{2,3,1,0:T(8,128)} %param.16) | copy-start | bytes 24580
  80.0 4.0 %copy-start.8 = (f32[4,1,64,8]{2,3,1,0:T(8,128)S(1)}, f32[4,1,64,8]{2,3,1,0:T(8,128)}, u32[]{:S(2)}) copy-start(f32[4,1,64,8]{2,3,1,0:T(8,128)} %param.17) | copy-start | bytes 24580
  80.0 15.3 %copy-start.3 = (bf16[4,1,64,1024]{3,2,1,0:T(8,128)(2,1)S(1)}, bf16[4,1,64,1024]{3,2,1,0:T(8,128)(2,1)}, u32[]{:S(2)}) copy-start(bf16[4,1,64,1024]{3,2,1,0:T(8,128)(2,1)} %param.13) | copy-start | bytes 1572868
  80.0 15.3 %copy-start.6 = (f32[1024]{0:T(1024)S(1)}, f32[1024]{0:T(1024)}, u32[]{:S(2)}) copy-start(f32[1024]{0:T(1024)} %param.15) | copy-start | bytes 12292
  80.5 9.2 %collective-permute-start.17 = (bf16[256,512]{1,0:T(8,128)(2,1)S(1)}, bf16[256,512]{1,0:T(8,128)(2,1)S(1)}, u32[]{:S(2)}, u32[]{:S(2)}) collective-permute-start(bf16[256,512]{1,0:T(8,128)(2,1)S(1)} %get-tuple-element.55), channel_id=1, source_target_pairs={{0,1},{1,0},{2,3},{3,2},{4,5},{5,4},{6,7},{7,6},{8,9},{9,8},{10,11... | collective-permute-start | bytes 786440 | tf_op jit(solution)/shard_map/ppermute | solution.py:260
  83.1 12.2 %collective-permute-start.16 = (bf16[256,512]{1,0:T(8,128)(2,1)S(1)}, bf16[256,512]{1,0:T(8,128)(2,1)S(1)}, u32[]{:S(2)}, u32[]{:S(2)}) collective-permute-start(bf16[256,512]{1,0:T(8,128)(2,1)S(1)} %get-tuple-element.54), channel_id=1, source_target_pairs={{0,1},{1,0},{2,3},{3,2},{4,5},{5,4},{6,7},{7,6},{8,9},{9,8},{10,11... | collective-permute-start | bytes 786440 | tf_op jit(solution)/shard_map/ppermute | solution.py:260
  95.7 6.8 %collective-permute-start.18 = (bf16[16,1024]{1,0:T(8,128)(2,1)S(1)}, bf16[16,1024]{1,0:T(8,128)(2,1)S(1)}, u32[]{:S(2)}, u32[]{:S(2)}) collective-permute-start(bf16[16,1024]{1,0:T(8,128)(2,1)S(1)} %get-tuple-element.60), channel_id=1, source_target_pairs={{0,1},{1,0},{2,3},{3,2},{4,5},{5,4},{6,7},{7,6},{8,9},{9,8},{10,11... | collective-permute-start | bytes 98312 | tf_op jit(solution)/shard_map/ppermute | solution.py:260
  96.6 9.6 %collective-permute-start.19 = (bf16[16,1024]{1,0:T(8,128)(2,1)S(1)}, bf16[16,1024]{1,0:T(8,128)(2,1)S(1)}, u32[]{:S(2)}, u32[]{:S(2)}) collective-permute-start(bf16[16,1024]{1,0:T(8,128)(2,1)S(1)} %get-tuple-element.61), channel_id=1, source_target_pairs={{0,2},{1,3},{2,0},{3,1},{4,6},{5,7},{6,4},{7,5},{8,10},{9,11},{10,... | collective-permute-start | bytes 98312 | tf_op jit(solution)/shard_map/ppermute | solution.py:260
  98.2 8.7 %collective-permute-start.20 = (bf16[16,1024]{1,0:T(8,128)(2,1)S(1)}, bf16[16,1024]{1,0:T(8,128)(2,1)S(1)}, u32[]{:S(2)}, u32[]{:S(2)}) collective-permute-start(bf16[16,1024]{1,0:T(8,128)(2,1)S(1)} %get-tuple-element.62), channel_id=1, source_target_pairs={{0,3},{1,2},{2,1},{3,0},{4,7},{5,6},{6,5},{7,4},{8,11},{9,10},{10,... | collective-permute-start | bytes 98312 | tf_op jit(solution)/shard_map/ppermute | solution.py:260
  99.2 7.7 %collective-permute-start.21 = (bf16[16,1024]{1,0:T(8,128)(2,1)S(1)}, bf16[16,1024]{1,0:T(8,128)(2,1)S(1)}, u32[]{:S(2)}, u32[]{:S(2)}) collective-permute-start(bf16[16,1024]{1,0:T(8,128)(2,1)S(1)} %get-tuple-element.63), channel_id=1, source_target_pairs={{0,4},{1,5},{2,6},{3,7},{4,0},{5,1},{6,2},{7,3},{8,12},{9,13},{10,... | collective-permute-start | bytes 98312 | tf_op jit(solution)/shard_map/ppermute | solution.py:260
  102.0 5.7 %collective-permute-start.22 = (bf16[16,1024]{1,0:T(8,128)(2,1)S(1)}, bf16[16,1024]{1,0:T(8,128)(2,1)S(1)}, u32[]{:S(2)}, u32[]{:S(2)}) collective-permute-start(bf16[16,1024]{1,0:T(8,128)(2,1)S(1)} %get-tuple-element.64), channel_id=1, source_target_pairs={{0,5},{1,4},{2,7},{3,6},{4,1},{5,0},{6,3},{7,2},{8,13},{9,12},{10,... | collective-permute-start | bytes 98312 | tf_op jit(solution)/shard_map/ppermute | solution.py:260
  102.4 6.0 %collective-permute-start.23 = (bf16[16,1024]{1,0:T(8,128)(2,1)S(1)}, bf16[16,1024]{1,0:T(8,128)(2,1)S(1)}, u32[]{:S(2)}, u32[]{:S(2)}) collective-permute-start(bf16[16,1024]{1,0:T(8,128)(2,1)S(1)} %get-tuple-element.65), channel_id=1, source_target_pairs={{0,6},{1,7},{2,4},{3,5},{4,2},{5,3},{6,0},{7,1},{8,14},{9,15},{10,... | collective-permute-start | bytes 98312 | tf_op jit(solution)/shard_map/ppermute | solution.py:260
  106.2 6.6 %collective-permute-start.24 = (bf16[16,1024]{1,0:T(8,128)(2,1)S(1)}, bf16[16,1024]{1,0:T(8,128)(2,1)S(1)}, u32[]{:S(2)}, u32[]{:S(2)}) collective-permute-start(bf16[16,1024]{1,0:T(8,128)(2,1)S(1)} %get-tuple-element.66), channel_id=1, source_target_pairs={{0,7},{1,6},{2,5},{3,4},{4,3},{5,2},{6,1},{7,0},{8,15},{9,14},{10,... | collective-permute-start | bytes 98312 | tf_op jit(solution)/shard_map/ppermute | solution.py:260
  112.8 2.8 %copy-start = (bf16[1,1024,3072]{2,1,0:T(8,128)(2,1)S(1)}, bf16[1,1024,3072]{2,1,0:T(8,128)(2,1)}, u32[]{:S(2)}) copy-start(bf16[1,1024,3072]{2,1,0:T(8,128)(2,1)} %param.18) | copy-start | bytes 18874372
  115.6 20.7 %copy-start.1 = (bf16[1,1536,1024]{2,1,0:T(8,128)(2,1)S(1)}, bf16[1,1536,1024]{2,1,0:T(8,128)(2,1)}, u32[]{:S(2)}) copy-start(bf16[1,1536,1024]{2,1,0:T(8,128)(2,1)} %param.19) | copy-start | bytes 9437188
  117.9 1.9 %collective-permute-start.25 = (bf16[32,3200]{1,0:T(8,128)(2,1)S(1)}, bf16[32,3200]{1,0:T(8,128)(2,1)S(1)}, u32[]{:S(2)}, u32[]{:S(2)}) collective-permute-start(bf16[32,3200]{1,0:T(8,128)(2,1)S(1)} %get-tuple-element.68), channel_id=1, source_target_pairs={{0,8},{1,9},{2,10},{3,11},{4,12},{5,13},{6,14},{7,15},{8,0},{9,1},... | collective-permute-start | bytes 614408 | tf_op jit(solution)/shard_map/ppermute | solution.py:260
  118.0 7.9 %collective-permute-start.26 = (bf16[32,3200]{1,0:T(8,128)(2,1)S(1)}, bf16[32,3200]{1,0:T(8,128)(2,1)S(1)}, u32[]{:S(2)}, u32[]{:S(2)}) collective-permute-start(bf16[32,3200]{1,0:T(8,128)(2,1)S(1)} %get-tuple-element.69), channel_id=1, source_target_pairs={{0,16},{1,17},{2,18},{3,19},{4,20},{5,21},{6,22},{7,23},{8,24},{9,... | collective-permute-start | bytes 614408 | tf_op jit(solution)/shard_map/ppermute | solution.py:260
  118.5 11.0 %collective-permute-start.27 = (bf16[32,3200]{1,0:T(8,128)(2,1)S(1)}, bf16[32,3200]{1,0:T(8,128)(2,1)S(1)}, u32[]{:S(2)}, u32[]{:S(2)}) collective-permute-start(bf16[32,3200]{1,0:T(8,128)(2,1)S(1)} %get-tuple-element.70), channel_id=1, source_target_pairs={{0,24},{1,25},{2,26},{3,27},{4,28},{5,29},{6,30},{7,31},{8,16},{9,... | collective-permute-start | bytes 614408 | tf_op jit(solution)/shard_map/ppermute | solution.py:260
  129.6 1.9 %collective-permute-start.28 = (bf16[32,1536]{1,0:T(8,128)(2,1)S(1)}, bf16[32,1536]{1,0:T(8,128)(2,1)S(1)}, u32[]{:S(2)}, u32[]{:S(2)}) collective-permute-start(bf16[32,1536]{1,0:T(8,128)(2,1)S(1)} %shard_map.108.refs_0_), channel_id=1, source_target_pairs={{0,8},{1,9},{2,10},{3,11},{4,12},{5,13},{6,14},{7,15},{8,0},{9,1},... | collective-permute-start | bytes 294920 | tf_op jit(solution)/shard_map/ppermute | solution.py:260
  129.9 5.6 %collective-permute-start.29 = (bf16[32,1536]{1,0:T(8,128)(2,1)S(1)}, bf16[32,1536]{1,0:T(8,128)(2,1)S(1)}, u32[]{:S(2)}, u32[]{:S(2)}) collective-permute-start(bf16[32,1536]{1,0:T(8,128)(2,1)S(1)} %shard_map.108.refs_0_), channel_id=1, source_target_pairs={{0,16},{1,17},{2,18},{3,19},{4,20},{5,21},{6,22},{7,23},{8,24},{9,... | collective-permute-start | bytes 294920 | tf_op jit(solution)/shard_map/ppermute | solution.py:260
  130.4 5.9 %collective-permute-start.30 = (bf16[32,1536]{1,0:T(8,128)(2,1)S(1)}, bf16[32,1536]{1,0:T(8,128)(2,1)S(1)}, u32[]{:S(2)}, u32[]{:S(2)}) collective-permute-start(bf16[32,1536]{1,0:T(8,128)(2,1)S(1)} %shard_map.108.refs_0_), channel_id=1, source_target_pairs={{0,24},{1,25},{2,26},{3,27},{4,28},{5,29},{6,30},{7,31},{8,16},{9,... | collective-permute-start | bytes 294920 | tf_op jit(solution)/shard_map/ppermute | solution.py:260
  137.4 7.1 %collective-permute-start.31 = (bf16[16,1024]{1,0:T(8,128)(2,1)S(1)}, bf16[16,1024]{1,0:T(8,128)(2,1)S(1)}, u32[]{:S(2)}, u32[]{:S(2)}) collective-permute-start(bf16[16,1024]{1,0:T(8,128)(2,1)S(1)} %get-tuple-element.72), channel_id=1, source_target_pairs={{0,1},{1,0},{2,3},{3,2},{4,5},{5,4},{6,7},{7,6},{8,9},{9,8},{10,11... | collective-permute-start | bytes 98312 | tf_op jit(solution)/shard_map/ppermute | solution.py:260
  138.6 5.9 %collective-permute-start.32 = (bf16[16,1024]{1,0:T(8,128)(2,1)S(1)}, bf16[16,1024]{1,0:T(8,128)(2,1)S(1)}, u32[]{:S(2)}, u32[]{:S(2)}) collective-permute-start(bf16[16,1024]{1,0:T(8,128)(2,1)S(1)} %get-tuple-element.73), channel_id=1, source_target_pairs={{0,2},{1,3},{2,0},{3,1},{4,6},{5,7},{6,4},{7,5},{8,10},{9,11},{10,... | collective-permute-start | bytes 98312 | tf_op jit(solution)/shard_map/ppermute | solution.py:260
  138.6 10.0 %collective-permute-start.33 = (bf16[16,1024]{1,0:T(8,128)(2,1)S(1)}, bf16[16,1024]{1,0:T(8,128)(2,1)S(1)}, u32[]{:S(2)}, u32[]{:S(2)}) collective-permute-start(bf16[16,1024]{1,0:T(8,128)(2,1)S(1)} %get-tuple-element.74), channel_id=1, source_target_pairs={{0,3},{1,2},{2,1},{3,0},{4,7},{5,6},{6,5},{7,4},{8,11},{9,10},{10,... | collective-permute-start | bytes 98312 | tf_op jit(solution)/shard_map/ppermute | solution.py:260
  140.9 7.7 %collective-permute-start.34 = (bf16[16,1024]{1,0:T(8,128)(2,1)S(1)}, bf16[16,1024]{1,0:T(8,128)(2,1)S(1)}, u32[]{:S(2)}, u32[]{:S(2)}) collective-permute-start(bf16[16,1024]{1,0:T(8,128)(2,1)S(1)} %get-tuple-element.75), channel_id=1, source_target_pairs={{0,4},{1,5},{2,6},{3,7},{4,0},{5,1},{6,2},{7,3},{8,12},{9,13},{10,... | collective-permute-start | bytes 98312 | tf_op jit(solution)/shard_map/ppermute | solution.py:260
  140.9 7.7 %collective-permute-start.35 = (bf16[16,1024]{1,0:T(8,128)(2,1)S(1)}, bf16[16,1024]{1,0:T(8,128)(2,1)S(1)}, u32[]{:S(2)}, u32[]{:S(2)}) collective-permute-start(bf16[16,1024]{1,0:T(8,128)(2,1)S(1)} %get-tuple-element.76), channel_id=1, source_target_pairs={{0,5},{1,4},{2,7},{3,6},{4,1},{5,0},{6,3},{7,2},{8,13},{9,12},{10,... | collective-permute-start | bytes 98312 | tf_op jit(solution)/shard_map/ppermute | solution.py:260
  144.4 5.7 %collective-permute-start.36 = (bf16[16,1024]{1,0:T(8,128)(2,1)S(1)}, bf16[16,1024]{1,0:T(8,128)(2,1)S(1)}, u32[]{:S(2)}, u32[]{:S(2)}) collective-permute-start(bf16[16,1024]{1,0:T(8,128)(2,1)S(1)} %get-tuple-element.77), channel_id=1, source_target_pairs={{0,6},{1,7},{2,4},{3,5},{4,2},{5,3},{6,0},{7,1},{8,14},{9,15},{10,... | collective-permute-start | bytes 98312 | tf_op jit(solution)/shard_map/ppermute | solution.py:260
  144.5 6.6 %collective-permute-start.37 = (bf16[16,1024]{1,0:T(8,128)(2,1)S(1)}, bf16[16,1024]{1,0:T(8,128)(2,1)S(1)}, u32[]{:S(2)}, u32[]{:S(2)}) collective-permute-start(bf16[16,1024]{1,0:T(8,128)(2,1)S(1)} %get-tuple-element.78), channel_id=1, source_target_pairs={{0,7},{1,6},{2,5},{3,4},{4,3},{5,2},{6,1},{7,0},{8,15},{9,14},{10,... | collective-permute-start | bytes 98312 | tf_op jit(solution)/shard_map/ppermute | solution.py:260

commit v2 on v1

v2 whole, which is shorter than its diff:
```python
import functools

import jax
import jax.numpy as jnp
from jax import lax
from jax.experimental import pallas as pl
from jax.experimental.pallas import tpu as pltpu
from jax.sharding import PartitionSpec as P

D = 4096
QUERY_HEADS = 32
KEY_VALUE_HEADS = 2
HEAD_SIZE = 128
GROUP_EXTENT = QUERY_HEADS // KEY_VALUE_HEADS
NEG_FILL = -1e30
BF16 = jnp.bfloat16
F32 = jnp.float32
VMEM = pl.BlockSpec(memory_space=pltpu.VMEM)
HBM = pl.BlockSpec(memory_space=pltpu.HBM)


def call(kernel, out_shape, n_in, scratch=(), cost=(0, 0), limit=32, **kw):
    kw.setdefault("in_specs", [VMEM] * n_in)
    kw.setdefault("out_specs", jax.tree.map(lambda _: VMEM, out_shape))
    return pl.pallas_call(
        kernel,
        out_shape=out_shape,
        scratch_shapes=list(scratch),
        cost_estimate=pl.CostEstimate(flops=cost[0], bytes_accessed=cost[1], transcendentals=0),
        compiler_params=pltpu.CompilerParams(vmem_limit_bytes=limit * 2**20),
        **kw,
    )


def sds(shape, dtype):
    return jax.ShapeDtypeStruct(shape, dtype)


def dot(a, b):
    return jnp.dot(a, b, preferred_element_type=F32)


def spread(d):
    return (d >> 1) * 4 + (d & 1)


def own_hi_lo():
    e = lax.axis_index("exp")
    return lax.div(e, 4) * 2 + lax.rem(e, 2), lax.rem(lax.div(e, 2), 2)


def aligned(x, n):
    return pl.multiple_of(x, n)


def pack_kernel(C, qw, q_ref, new_ref, past_ref, *refs):
    outs, sems = refs[:-1], refs[-1]
    c = lax.axis_index("ctx")
    _, lo = own_hi_lo()
    copies = []

    def copy(src, dst):
        copies.append(pltpu.make_async_copy(src, dst, sems.at[len(copies)]))
        copies[-1].start()

    for s in reversed(range(C)):
        target = jnp.bitwise_xor(c, s)
        out = outs[s]
        first = lax.div(target, 2) * 4 + lax.rem(target, 2)
        for t in range(2):
            offset = (first + 2 * jnp.bitwise_xor(lo, t)) * qw
            copy(q_ref.at[:, pl.ds(aligned(offset, 128), qw)], out.at[:, t * qw : (t + 1) * qw])
        kv = lax.div(target * (2 * qw // HEAD_SIZE), GROUP_EXTENT)
        at = 2 * qw
        for ref in (new_ref, past_ref):
            for part in (0, KEY_VALUE_HEADS):
                offset = (part + kv) * HEAD_SIZE
                copy(ref.at[:, pl.ds(aligned(offset, 128), 128)], out.at[:, at : at + 128])
                at += 128
    for c in copies:
        c.wait()


def attend_kernel(C, tok, *refs):
    msgs, outs, q_s, kv_s = refs[:C], refs[C : C + 2], refs[C + 2], refs[C + 3]
    c = lax.axis_index("ctx")
    qw = outs[0].shape[1]
    rows = C * tok
    for s in range(C):
        msg = msgs[s]
        at = aligned(jnp.bitwise_xor(c, s) * tok, tok)
        q_s[pl.ds(at, tok), :] = msg[:, : 2 * qw]
        kv_s[pl.ds(rows + at, tok), :] = msg[:, 2 * qw : 2 * qw + 256]
        kv_s[pl.ds(at, tok), :] = msg[:, 2 * qw + 256 :]
    block = 128
    for b in range(rows // block):
        seen = rows + (b + 1) * block
        k = kv_s[:seen, :HEAD_SIZE]
        v = kv_s[:seen, HEAD_SIZE:]
        row = lax.broadcasted_iota(jnp.int32, (block, seen), 0) + (rows + b * block)
        visible = lax.broadcasted_iota(jnp.int32, (block, seen), 1) <= row
        at = slice(b * block, (b + 1) * block)
        for h in range(2 * qw // HEAD_SIZE):
            q = q_s[at, h * HEAD_SIZE : (h + 1) * HEAD_SIZE]
            scores = lax.dot_general(q, k, (((1,), (1,)), ((), ())), preferred_element_type=F32)
            scores = jnp.where(visible, scores * HEAD_SIZE ** (-0.5), NEG_FILL)
            weights = jnp.exp(scores - jnp.max(scores, axis=1, keepdims=True))
            total = jnp.sum(weights, axis=1, keepdims=True)
            numerator = dot(weights.astype(BF16), v)
            t, col = divmod(h * HEAD_SIZE, qw)
            outs[t][at, col : col + HEAD_SIZE] = (numerator / total).astype(BF16)


def route_kernel(E, cap, routes_ref, gates_ref, place_ref, gate_ref):
    e = lax.axis_index("exp")
    rows = routes_ref.shape[0]
    routes = routes_ref[...]
    resident = routes < E
    target = jnp.sum(jnp.where(resident, routes, 0), axis=1, keepdims=True)
    has = jnp.sum(resident.astype(jnp.int32), axis=1, keepdims=True) > 0
    gate = jnp.sum(jnp.where(resident, gates_ref[...], 0.0), axis=1, keepdims=True)
    gate_ref[...] = jnp.broadcast_to(gate, gate_ref.shape)
    lanes = lax.broadcasted_iota(jnp.int32, (rows, 128), 1)
    one_hot = jnp.where((target == lanes) & has, 1.0, 0.0)
    earlier = (
        lax.broadcasted_iota(jnp.int32, (rows, rows), 1)
        < lax.broadcasted_iota(jnp.int32, (rows, rows), 0)
    ).astype(F32).astype(BF16)
    rank = jnp.sum(dot(earlier, one_hot.astype(BF16)) * one_hot, axis=1, keepdims=True)
    slot = jnp.bitwise_xor(target, e) * cap + rank.astype(jnp.int32)
    slot = jnp.where(has, slot, -1)
    places = lax.broadcasted_iota(jnp.int32, (rows, E * cap), 1)
    place_ref[...] = jnp.where(slot == places, 1.0, 0.0).astype(BF16)


def project_kernel(C, spans, *refs):
    atts, res_ref, ws = refs[:C], refs[C], refs[C + 1 : C + 1 + len(spans)]
    acc, last, stacked = refs[-3:]
    c = lax.axis_index("ctx")
    hi, _ = own_hi_lo()
    for s in range(C):
        stacked[jnp.bitwise_xor(c, s)] = atts[s][...]
    rows = res_ref.shape[0]
    width = acc.shape[1]
    half = width // 2
    for j in range(2):
        at = slice(j * half, (j + 1) * half)
        total = None
        for (d, first, count), w in zip(spans, ws):
            term = dot(stacked[jnp.bitwise_xor(hi, d), :, first : first + count], w[:, at])
            total = term if total is None else total + term
        acc[:rows, at] = total[:rows] + res_ref[:, at].astype(F32)
        acc[rows:, at] = total[rows:]
    count = last.shape[1]
    last[...] = stacked[jnp.bitwise_xor(hi, C - 1), :, stacked.shape[2] - count :]


def last_kernel(E, cap, acc_ref, last_ref, w_ref, mine_ref, other_ref, own_ref, full_ref, keep_ref, send_ref):
    rows = own_ref.shape[0]
    total = acc_ref[...] + dot(last_ref[...], w_ref[...])
    own_ref[...] = total[:rows]
    rounded = total.astype(BF16)
    full_ref[...] = rounded[rows:]
    for t, place in enumerate((mine_ref, other_ref)):
        picked = lax.dot_general(
            place[...],
            rounded[t * rows : (t + 1) * rows],
            (((0,), (0,)), ((), ())),
            preferred_element_type=F32,
        )
        for d in range(E // 2):
            near, far = spread(d) ^ (2 * t), spread(d) ^ 2 ^ (2 * t)
            at = (2 * d + t) * cap
            keep_ref[at : at + cap, :] = picked[near * cap : (near + 1) * cap]
            at = (2 * d + 1 - t) * cap
            send_ref[at : at + cap, :] = picked[far * cap : (far + 1) * cap].astype(BF16)


def outgoing_kernel(keep_ref, got_ref, gain_ref, *outs):
    scaled = ((keep_ref[...] + got_ref[...].astype(F32)) * gain_ref[...]).astype(BF16)
    count = outs[0].shape[0]
    for d, out in enumerate(outs):
        out[...] = scaled[d * count : (d + 1) * count]


def gate_up_kernel(C, E, cap, order, *refs):
    xs, gain_ref, w_ref, keep_ref, send_ref, x_s, part_s = refs[: E // 2], *refs[E // 2 :]
    c = lax.axis_index("ctx")
    e = lax.axis_index("exp")
    own_rows = E * cap // C
    wide = w_ref.shape[1]
    for d in range(E // 2):
        for t in range(2):
            at = aligned(jnp.bitwise_xor(e, spread(d) ^ (2 * t)) * cap, cap)
            x_s[pl.ds(at, cap), :] = xs[d][t * cap : (t + 1) * cap, :]
    plain = x_s[...].astype(F32) / gain_ref[...]
    square = jnp.sum(plain * plain, axis=1, keepdims=True)
    lane = lax.broadcasted_iota(jnp.int32, (E * cap, 128), 1)
    part_s[:, wide:] = jnp.where(lane == 0, square, 0.0)
    step = 512
    for j in range(wide // step):
        at = slice(j * step, (j + 1) * step)
        part_s[:, at] = dot(x_s[...], w_ref[:, at])
    for i, r in enumerate(order):
        at = aligned(jnp.bitwise_xor(c, r) * own_rows, own_rows)
        block = part_s[pl.ds(at, own_rows), :]
        if i < C // 2:
            keep_ref[i * own_rows : (i + 1) * own_rows, :] = block
        else:
            to = (i - C // 2) * own_rows
            send_ref[to : to + own_rows, :wide] = block[:, :wide].astype(BF16)
            square = block[:, wide:]
            high = square.astype(BF16).astype(F32)
            lane = lax.broadcasted_iota(jnp.int32, square.shape, 1)
            low = pltpu.roll(square - high, 1, 1)
            pair = jnp.where(lane == 1, low, high)
            send_ref[to : to + own_rows, wide:] = pair.astype(BF16)


def halve_kernel(keep_in, got_ref, keep_ref, send_ref):
    rows = keep_ref.shape[0]
    wide = keep_ref.shape[1] - 128
    total = keep_in[...] + got_ref[...].astype(F32)
    keep_ref[...] = total[:rows]
    send_ref[:, :wide] = total[rows:, :wide].astype(BF16)
    square = jnp.sum(total[rows:, wide:], axis=1, keepdims=True)
    high = square.astype(BF16).astype(F32)
    lane = lax.broadcasted_iota(jnp.int32, (rows, 128), 1)
    pair = jnp.where(lane == 0, high, jnp.where(lane == 1, square - high, 0.0))
    send_ref[:, wide:] = pair.astype(BF16)


def activate_kernel(hidden, keep_ref, got_ref, out):
    def summed(at):
        return keep_ref[:, at] + got_ref[:, at].astype(F32)

    square = jnp.sum(summed(slice(2 * hidden, 2 * hidden + 128)), axis=1, keepdims=True)
    scale = lax.rsqrt(square / D + 1e-6)
    gate = summed(slice(0, hidden)) * scale
    up = summed(slice(hidden, 2 * hidden)) * scale
    out[...] = (gate / (1.0 + jnp.exp(-gate)) * up).astype(BF16)


def down_kernel(C, E, cap, *refs):
    acts, w_ref, outs, x_s, part_s = refs[:C], refs[C], refs[C + 1 : C + 1 + E // 2], refs[-2], refs[-1]
    c = lax.axis_index("ctx")
    e = lax.axis_index("exp")
    own_rows = E * cap // C
    for s in range(C):
        at = aligned(jnp.bitwise_xor(c, s) * own_rows, own_rows)
        x_s[pl.ds(at, own_rows), :] = acts[s][...]
    part_s[...] = dot(x_s[...], w_ref[...]).astype(BF16)
    for d in range(E // 2):
        for t in range(2):
            at = aligned(jnp.bitwise_xor(e, spread(d) ^ (2 * t)) * cap, cap)
            outs[d][t * cap : (t + 1) * cap, :] = part_s[pl.ds(at, cap), :]


def forward_kernel(cap, *refs):
    for d, x in enumerate(refs[:-1]):
        refs[-1][d * cap : (d + 1) * cap, :] = x[cap:, :]


def combine_kernel(E, cap, own_ref, got_ref, place_ref, gate_ref, *refs):
    xs, far, out, x_s = refs[: E // 2], refs[E // 2], refs[E // 2 + 1], refs[E // 2 + 2]
    for d in range(E // 2):
        at = spread(d) * cap
        x_s[at : at + cap, :] = xs[d][:cap, :]
        at = (spread(d) ^ 2) * cap
        x_s[at : at + cap, :] = far[d * cap : (d + 1) * cap, :]
    collected = dot(place_ref[...], x_s[...])
    mixed = own_ref[...] + got_ref[...].astype(F32)
    out[...] = (mixed + gate_ref[:, :1] * collected).astype(BF16)


def body(
    queries,
    new_keys_values,
    cached_keys_values,
    residual,
    out_weight,
    norm_gain,
    routes,
    gates,
    w_gate_up,
    w_down,
):
    C = lax.axis_size("ctx")
    E = lax.axis_size("exp")
    tok = queries.shape[2]
    rows = C * tok
    width = residual.shape[3]
    hidden = w_down.shape[1]
    wide = 2 * hidden
    cap = rows // (2 * E)
    slots = E * cap
    own_rows = slots // C
    qw = QUERY_HEADS // E * HEAD_SIZE

    def permute(x, ctx=0, exp=0):
        pairs = [(c * E + e, (c ^ ctx) * E + (e ^ exp)) for c in range(C) for e in range(E)]
        return lax.ppermute(x, ("ctx", "exp"), pairs)

    def after(x, *others):
        return lax.optimization_barrier((x, *others))[0]

    cuts = [(0, qw // 2), (qw // 2, qw // 4), (qw * 3 // 4, qw // 4)]
    chunks = [out_weight[a : a + n] for a, n in cuts]
    shards = {0: [(0, qw, out_weight)]}
    for d in range(2, C, 2):
        shards[d] = [(0, cuts[0][1], permute(chunks[0], exp=spread(d)))]
    shards[1] = [(0, qw, permute(out_weight, exp=1))]

    msgs = call(
        functools.partial(pack_kernel, C, qw),
        [sds((tok, 2 * qw + 512), BF16)] * C,
        3,
        scratch=[pltpu.SemaphoreType.DMA((6 * C,))],
        in_specs=[HBM] * 3,
        cost=(0, 4 * 2**20),
    )(
        queries.reshape(tok, queries.shape[3]),
        new_keys_values.reshape(tok, new_keys_values.shape[3]),
        cached_keys_values.reshape(tok, cached_keys_values.shape[3]),
    )
    got = [msgs[0]] + [permute(msgs[s], ctx=s) for s in range(1, C)]
    mine, other = call(
        functools.partial(attend_kernel, C, tok),
        [sds((rows, qw), BF16)] * 2,
        C,
        scratch=[pltpu.VMEM((rows, 2 * qw), BF16), pltpu.VMEM((2 * rows, 2 * HEAD_SIZE), BF16)],
        cost=(4 * 2 * rows * 2 * rows * qw, 16 * 2**20),
        limit=16,
    )(*got)
    theirs = permute(other, exp=2)
    for d in range(2, C, 2):
        for (a, n), chunk in zip(cuts[1:], chunks[1:]):
            shards[d].append((a, n, permute(after(chunk, mine), exp=spread(d))))
    place, gate = call(
        functools.partial(route_kernel, E, cap),
        [sds((rows, slots), BF16), sds((rows, 128), F32)],
        2,
        cost=(0, 2**20),
    )(
        after(routes, mine).reshape(rows, routes.shape[3]),
        after(gates, mine).reshape(rows, gates.shape[3]),
    )
    attended = jnp.concatenate([mine, theirs], axis=0)
    atts = {0: attended}
    for s in range(2, C, 2):
        atts[s] = permute(attended, ctx=s)
    atts[1] = permute(attended, ctx=1)
    for d in range(3, C, 2):
        shards[d] = [
            (a, n, permute(after(w, mine), exp=1)) for a, n, w in shards[d - 1]
        ]
    for s in range(3, C, 2):
        atts[s] = permute(after(atts[s - 1], shards[2][1][2]), ctx=1)
    other_place = permute(place, exp=2)

    spans, pieces = [], []
    for d in range(C):
        for a, n, w in shards[d]:
            spans.append((d, a, n))
            pieces.append(w)
    last_rows = spans[-1][2]
    acc, last = call(
        functools.partial(project_kernel, C, spans[:-1]),
        [sds((2 * rows, width), F32), sds((2 * rows, last_rows), BF16)],
        C + len(spans),
        scratch=[pltpu.VMEM((C, 2 * rows, qw), BF16)],
        cost=(4 * rows * qw * width * (C - 1), 8 * 2**20),
    )(*[atts[s] for s in range(C)], residual.reshape(rows, width), *pieces[:-1])
    own, full, keep, send = call(
        functools.partial(last_kernel, E, cap),
        [
            sds((rows, width), F32),
            sds((rows, width), BF16),
            sds((slots, width), F32),
            sds((slots, width), BF16),
        ],
        5,
        cost=(4 * rows * (last_rows + slots) * width, 6 * 2**20),
    )(acc, last, pieces[-1], place, other_place)
    gain = norm_gain.reshape(1, width)
    outgoing = call(
        outgoing_kernel,
        [sds((2 * cap, width), BF16)] * (E // 2),
        3,
        cost=(0, 2**20),
    )(keep, permute(send, exp=2), gain)
    incoming = [outgoing[0]] + [permute(outgoing[d], exp=spread(d)) for d in range(1, E // 2)]

    order = [0]
    bit = C // 2
    while bit:
        order = order + [r | bit for r in order]
        bit //= 2
    keep, send = call(
        functools.partial(gate_up_kernel, C, E, cap, order),
        [sds((slots // 2, wide + 128), F32), sds((slots // 2, wide + 128), BF16)],
        E // 2 + 2,
        scratch=[pltpu.VMEM((slots, width), BF16), pltpu.VMEM((slots, wide + 128), F32)],
        cost=(2 * slots * width * wide, 2 * width * wide),
    )(*incoming, gain, w_gate_up.reshape(width, wide))
    arrived = permute(after(full, *incoming), exp=2)
    bit = 1
    while 2 * bit < C:
        count = keep.shape[0] // 2
        keep, send = call(
            halve_kernel,
            [sds((count, wide + 128), F32), sds((count, wide + 128), BF16)],
            2,
            cost=(0, 2**21),
        )(keep, permute(send, ctx=bit))
        bit *= 2
    activated = call(
        functools.partial(activate_kernel, hidden),
        sds((own_rows, hidden), BF16),
        2,
        cost=(0, 2**20),
    )(keep, permute(send, ctx=bit))
    acts = {0: activated}
    while bit:
        for r in list(acts):
            acts[r ^ bit] = permute(acts[r], ctx=bit)
        bit //= 2
    expert_out = call(
        functools.partial(down_kernel, C, E, cap),
        [sds((2 * cap, width), BF16)] * (E // 2),
        C + 1,
        scratch=[pltpu.VMEM((slots, hidden), BF16), pltpu.VMEM((slots, width), BF16)],
        cost=(2 * slots * width * hidden, 2 * width * hidden),
    )(*[acts[s] for s in range(C)], w_down.reshape(hidden, width))
    returned = [expert_out[0]]
    returned += [permute(expert_out[d], exp=spread(d)) for d in range(1, E // 2)]
    far = call(
        functools.partial(forward_kernel, cap), sds((slots // 2, width), BF16), E // 2, cost=(0, 2**19)
    )(*returned)
    result = call(
        functools.partial(combine_kernel, E, cap),
        sds((rows, width), BF16),
        5 + E // 2,
        scratch=[pltpu.VMEM((slots, width), BF16)],
        cost=(0, 2 * 2**20),
    )(own, arrived, place, gate, *returned, permute(far, exp=2))
    return result.reshape(C, 1, tok, width)


def solution(mesh):
    in_specs = (
        P("ctx", "exp", None, None),
        P("ctx", "exp", None, None),
        P("ctx", "exp", None, None),
        P(None, "exp", None, "ctx"),
        P("exp", "ctx"),
        P("ctx"),
        P(None, "exp", None, None),
        P(None, "exp", None, None),
        P("exp", "ctx", None),
        P("exp", None, "ctx"),
    )
    out_specs = P(None, "exp", None, "ctx")
    return jax.shard_map(body, mesh=mesh, in_specs=in_specs, out_specs=out_specs, check_vma=False)
```

time: 153 us -> 148 us (0.967)
  starting transfers between devices: 44.3 us -> 33.3 us
  local copies, waits for them, and re-layouts: 6.97 us -> 9.9 us
  Pallas kernels: 12.8 us -> 15.2 us
    ppermute x38 -> x29, starting transfers between devices: 44.3 us -> 33.3 us  [permute(): return lax.ppermute(x, ('ctx', 'exp'), pairs)]
    pallas_call x9 -> x10, Pallas kernels: 11.5 us -> 14 us  [the longest x1 5.14 us: body(): call(functools.partial(project_kernel, C, spans[:-1]), [sds((2 * rows, wi...]
    unnamed x20 -> x31, local copies, waits for them, and re-layouts: 5.71 us -> 7.89 us
    ppermute x38 -> x29, waiting for transfers between devices: 88 us -> 89.1 us  [permute(): return lax.ppermute(x, ('ctx', 'exp'), pairs)]
  transfers between devices with their start and end apart: 38 -> 29, of which waited for: 21 -> 17; matrix products, arithmetic and copies ran while one was open for 0% -> 2% of each run, Pallas kernels for 5% -> 4%
where the time goes in v2:
time: 148 us
  waiting for transfers between devices  89.1 us (60%)
  starting transfers between devices  33.3 us (22%)
  Pallas kernels  15.2 us (10%)
  local copies, waits for them, and re-layouts  9.9 us (7%)
    ppermute x29, waiting for transfers between devices, permute(): return lax.ppermute(x, ('ctx', 'exp'), pairs)  89.1 us
    ppermute x29, starting transfers between devices, permute(): return lax.ppermute(x, ('ctx', 'exp'), pairs)  33.3 us
    unnamed x31, local copies, waits for them, and re-layouts  7.89 us
    pallas_call x1, Pallas kernels, body(): call(functools.partial(project_kernel, C, spans[:-1]), [sds((2 * rows, wi...  5.14 us
    pallas_call x1, Pallas kernels, body(): call(functools.partial(attend_kernel, C, tok), [sds((rows, qw), BF16)] *...  4.36 us
  transfers between devices with their start and end apart: 29, of which 17 were waited for; matrix products, arithmetic and copies ran while one was open for 2% of the time, Pallas kernels for 4%

profile of v2, /device:TPU:0, one launch (start us, length us, event | category | flops | bytes accessed | tf_op | source)
XLA Modules:
  0.0 147.8 jit_solution(8524237547808806957)
XLA Ops:
  0.0 1.1 copy-done.3
  1.1 0.8 copy-done.8
  2.0 0.8 copy-done.9
  3.8 2.6 %collective-permute-start.1 = (bf16[64,1536]{1,0:T(8,128)(2,1)S(1)}, bf16[64,1536]{1,0:T(8,128)(2,1)S(1)}, u32[]{:S(2)}, u32[]{:S(2)}) collective-permute-start(bf16[64,1536]{1,0:T(8,128)(2,1)S(1)} %get-tuple-element.42), channel_id=1, source_target_pairs={{0,16},{1,17},{2,18},{3,19},{4,20},{5,21},{6,22},{7,23},{8,24},{9,... | collective-permute-start | bytes 589832 | tf_op jit(solution)/shard_map/ppermute | solution.py:302
  6.5 5.7 %collective-permute-done.1.refs_2_ = bf16[64,1536]{1,0:T(8,128)(2,1)S(1)} collective-permute-done((bf16[64,1536]{1,0:T(8,128)(2,1)S(1)}, bf16[64,1536]{1,0:T(8,128)(2,1)S(1)}, u32[]{:S(2)}, u32[]{:S(2)}) %collective-permute-start.1) | collective-permute-done | bytes 196640 | tf_op jit(solution)/shard_map/ppermute | solution.py:302
  12.1 3.7 %collective-permute-done.2.refs_3_ = bf16[64,1536]{1,0:T(8,128)(2,1)S(1)} collective-permute-done((bf16[64,1536]{1,0:T(8,128)(2,1)S(1)}, bf16[64,1536]{1,0:T(8,128)(2,1)S(1)}, u32[]{:S(2)}, u32[]{:S(2)}) %collective-permute-start.2) | collective-permute-done | bytes 196640 | tf_op jit(solution)/shard_map/ppermute | solution.py:302
  15.8 4.4 %shard_map.101 = (bf16[256,512]{1,0:T(8,128)(2,1)S(1)}, bf16[256,512]{1,0:T(8,128)(2,1)S(1)}) custom-call(bf16[64,1536]{1,0:T(8,128)(2,1)S(1)} %get-tuple-element.40.refs_0_, bf16[64,1536]{1,0:T(8,128)(2,1)S(1)} %collective-permute-done.refs_1_, bf16[64,1536]{1,0:T(8,128)(2,1)S(1)} %collective-permute-done.1.refs_2_, ...), custom_call_target="tpu_custom_call" | custom-call | flops 536870912 | bytes 16777216 | tf_op jit(solution)/shard_map/pallas_call | solution.py:327
  20.2 1.7 %collective-permute-start.3 = (bf16[256,512]{1,0:T(8,128)(2,1)S(1)}, bf16[256,512]{1,0:T(8,128)(2,1)S(1)}, u32[]{:S(2)}, u32[]{:S(2)}) collective-permute-start(bf16[256,512]{1,0:T(8,128)(2,1)S(1)} %get-tuple-element.45), channel_id=1, source_target_pairs={{0,2},{1,3},{2,0},{3,1},{4,6},{5,7},{6,4},{7,5},{8,10},{9,11},{10,... | collective-permute-start | bytes 786440 | tf_op jit(solution)/shard_map/ppermute | solution.py:302
  21.9 1.1 slice.10
  23.0 2.6 %collective-permute-start.9 = (bf16[256,1024]{1,0:T(8,128)(2,1)S(1)}, bf16[256,1024]{1,0:T(8,128)(2,1)}, u32[]{:S(2)}, u32[]{:S(2)}) collective-permute-start(bf16[256,1024]{1,0:T(8,128)(2,1)S(1)} %slice.10), channel_id=1, source_target_pairs={{0,4},{1,5},{2,6},{3,7},{4,0},{5,1},{6,2},{7,3},{8,12},{9,13},{10,... | collective-permute-start | bytes 1572872 | tf_op jit(solution)/shard_map/ppermute | solution.py:302
  25.6 0.7 constant_dynamic-update-slice_fusion.1
  26.3 6.6 %collective-permute-done.3 = bf16[256,512]{1,0:T(8,128)(2,1)S(1)} collective-permute-done((bf16[256,512]{1,0:T(8,128)(2,1)S(1)}, bf16[256,512]{1,0:T(8,128)(2,1)S(1)}, u32[]{:S(2)}, u32[]{:S(2)}) %collective-permute-start.3) | collective-permute-done | bytes 262176 | tf_op jit(solution)/shard_map/ppermute | solution.py:302
  33.0 0.7 constant_dynamic-update-slice_fusion.refs_0_
  33.7 1.7 %collective-permute-start.5 = (bf16[512,512]{1,0:T(8,128)(2,1)}, bf16[512,512]{1,0:T(8,128)(2,1)}, u32[]{:S(2)}, u32[]{:S(2)}) collective-permute-start(bf16[512,512]{1,0:T(8,128)(2,1)} %constant_dynamic-update-slice_fusion.refs_0_), channel_id=1, source_target_pairs={{0,16},{1,17},{2,18},{3,19},{4,20},{5,21},{6,22},{7,23},{8,24},{9,... | collective-permute-start | bytes 1572872 | tf_op jit(solution)/shard_map/ppermute | solution.py:302
  35.4 1.5 %collective-permute-start.8 = (bf16[512,1024]{1,0:T(8,128)(2,1)S(1)}, bf16[512,1024]{1,0:T(8,128)(2,1)}, u32[]{:S(2)}, u32[]{:S(2)}) collective-permute-start(bf16[512,1024]{1,0:T(8,128)(2,1)S(1)} %copy-done), channel_id=1, source_target_pairs={{0,1},{1,0},{2,3},{3,2},{4,5},{5,4},{6,7},{7,6},{8,9},{9,8},{10,11... | collective-permute-start | bytes 3145736 | tf_op jit(solution)/shard_map/ppermute | solution.py:302
  37.5 2.4 %collective-permute-start.10 = (bf16[128,1024]{1,0:T(8,128)(2,1)S(1)}, bf16[128,1024]{1,0:T(8,128)(2,1)}, u32[]{:S(2)}, u32[]{:S(2)}) collective-permute-start(bf16[128,1024]{1,0:T(8,128)(2,1)S(1)} %get-tuple-element.48), channel_id=1, source_target_pairs={{0,4},{1,5},{2,6},{3,7},{4,0},{5,1},{6,2},{7,3},{8,12},{9,13},{10,... | collective-permute-start | bytes 786440 | tf_op jit(solution)/shard_map/ppermute | solution.py:302
  39.9 21.4 %collective-permute-done.9.refs_7_ = bf16[256,1024]{1,0:T(8,128)(2,1)} collective-permute-done((bf16[256,1024]{1,0:T(8,128)(2,1)S(1)}, bf16[256,1024]{1,0:T(8,128)(2,1)}, u32[]{:S(2)}, u32[]{:S(2)}) %collective-permute-start.9) | collective-permute-done | bytes 524320 | tf_op jit(solution)/shard_map/ppermute | solution.py:302
  61.3 5.5 %collective-permute-done.6.refs_8_ = bf16[128,1024]{1,0:T(8,128)(2,1)S(1)} collective-permute-done((bf16[128,1024]{1,0:T(8,128)(2,1)S(1)}, bf16[128,1024]{1,0:T(8,128)(2,1)S(1)}, u32[]{:S(2)}, u32[]{:S(2)}) %collective-permute-start.6) | collective-permute-done | bytes 262176 | tf_op jit(solution)/shard_map/ppermute | solution.py:302
  66.9 1.5 %collective-permute-start.11 = (bf16[256,1024]{1,0:T(8,128)(2,1)}, bf16[256,1024]{1,0:T(8,128)(2,1)}, u32[]{:S(2)}, u32[]{:S(2)}) collective-permute-start(bf16[256,1024]{1,0:T(8,128)(2,1)} %collective-permute-done.9.refs_7_), channel_id=1, source_target_pairs={{0,1},{1,0},{2,3},{3,2},{4,5},{5,4},{6,7},{7,6},{8,9},{9,8},{10,11... | collective-permute-start | bytes 1572872 | tf_op jit(solution)/shard_map/ppermute | solution.py:302
  68.3 3.3 %collective-permute-done.10.refs_9_ = bf16[128,1024]{1,0:T(8,128)(2,1)} collective-permute-done((bf16[128,1024]{1,0:T(8,128)(2,1)S(1)}, bf16[128,1024]{1,0:T(8,128)(2,1)}, u32[]{:S(2)}, u32[]{:S(2)}) %collective-permute-start.10) | collective-permute-done | bytes 262176 | tf_op jit(solution)/shard_map/ppermute | solution.py:302
  71.6 1.5 %collective-permute-start.12 = (bf16[128,1024]{1,0:T(8,128)(2,1)S(1)}, bf16[128,1024]{1,0:T(8,128)(2,1)S(1)}, u32[]{:S(2)}, u32[]{:S(2)}) collective-permute-start(bf16[128,1024]{1,0:T(8,128)(2,1)S(1)} %collective-permute-done.6.refs_8_), channel_id=1, source_target_pairs={{0,1},{1,0},{2,3},{3,2},{4,5},{5,4},{6,7},{7,6},{8,9},{9,8},{10,11... | collective-permute-start | bytes 786440 | tf_op jit(solution)/shard_map/ppermute | solution.py:302
  73.8 10.9 %collective-permute-done.12.refs_11_ = bf16[128,1024]{1,0:T(8,128)(2,1)S(1)} collective-permute-done((bf16[128,1024]{1,0:T(8,128)(2,1)S(1)}, bf16[128,1024]{1,0:T(8,128)(2,1)S(1)}, u32[]{:S(2)}, u32[]{:S(2)}) %collective-permute-start.12) | collective-permute-done | bytes 262176 | tf_op jit(solution)/shard_map/ppermute | solution.py:302
  84.7 0.7 copy-done.6
  85.4 1.5 %collective-permute-start.13 = (bf16[128,1024]{1,0:T(8,128)(2,1)}, bf16[128,1024]{1,0:T(8,128)(2,1)}, u32[]{:S(2)}, u32[]{:S(2)}) collective-permute-start(bf16[128,1024]{1,0:T(8,128)(2,1)} %collective-permute-done.10.refs_9_), channel_id=1, source_target_pairs={{0,1},{1,0},{2,3},{3,2},{4,5},{5,4},{6,7},{7,6},{8,9},{9,8},{10,11... | collective-permute-start | bytes 786440 | tf_op jit(solution)/shard_map/ppermute | solution.py:302
  87.7 1.0 copy-done.2
  88.7 0.9 copy-done.5
  89.7 0.9 copy-done.7
  90.6 5.1 %shard_map.102 = (f32[512,1024]{1,0:T(8,128)S(1)}, bf16[512,128]{1,0:T(8,128)(2,1)S(1)}) custom-call(bf16[512,512]{1,0:T(8,128)(2,1)} %constant_dynamic-update-slice_fusion.refs_0_, bf16[512,512]{1,0:T(8,128)(2,1)} %collective-permute-done.4.refs_1_, bf16[512,512]{1,0:T(8,128)(2,1)} %collective-permute-done.5.refs_2_, ...), custom_call_target="tpu_custom_call" | custom-call | flops 1610612736 | bytes 8388608 | tf_op jit(solution)/shard_map/pallas_call | solution.py:367
  95.8 1.5 %shard_map.104 = (f32[256,1024]{1,0:T(8,128)S(1)}, bf16[256,1024]{1,0:T(8,128)(2,1)S(1)}, f32[128,1024]{1,0:T(8,128)S(1)}, bf16[128,1024]{1,0:T(8,128)(2,1)S(1)}) custom-call(f32[512,1024]{1,0:T(8,128)S(1)} %get-tuple-element.51.acc_ref, bf16[512,128]{1,0:T(8,128)(2,1)S(1)} %get-tuple-element.52.last_ref, bf16[128,1024]{1,0:T(8,128)(2,1)} %collective-permute-done.13.w_ref, ...), custom_call_target="tpu_custom_call" | custom-call | flops 268435456 | bytes 6291456 | tf_op jit(solution)/shard_map/pallas_call | solution.py:374
  97.3 2.1 %collective-permute-start.15 = (bf16[128,1024]{1,0:T(8,128)(2,1)S(1)}, bf16[128,1024]{1,0:T(8,128)(2,1)S(1)}, u32[]{:S(2)}, u32[]{:S(2)}) collective-permute-start(bf16[128,1024]{1,0:T(8,128)(2,1)S(1)} %get-tuple-element.60), channel_id=1, source_target_pairs={{0,2},{1,3},{2,0},{3,1},{4,6},{5,7},{6,4},{7,5},{8,10},{9,11},{10,... | collective-permute-start | bytes 786440 | tf_op jit(solution)/shard_map/ppermute | solution.py:302
  99.4 4.4 %collective-permute-done.15.got_ref = bf16[128,1024]{1,0:T(8,128)(2,1)S(1)} collective-permute-done((bf16[128,1024]{1,0:T(8,128)(2,1)S(1)}, bf16[128,1024]{1,0:T(8,128)(2,1)S(1)}, u32[]{:S(2)}, u32[]{:S(2)}) %collective-permute-start.15) | collective-permute-done | bytes 262176 | tf_op jit(solution)/shard_map/ppermute | solution.py:302
  104.5 3.4 %collective-permute-start.17 = (bf16[32,1024]{1,0:T(8,128)(2,1)S(1)}, bf16[32,1024]{1,0:T(8,128)(2,1)S(1)}, u32[]{:S(2)}, u32[]{:S(2)}) collective-permute-start(bf16[32,1024]{1,0:T(8,128)(2,1)S(1)} %get-tuple-element.63), channel_id=1, source_target_pairs={{0,4},{1,5},{2,6},{3,7},{4,0},{5,1},{6,2},{7,3},{8,12},{9,13},{10,... | collective-permute-start | bytes 196616 | tf_op jit(solution)/shard_map/ppermute | solution.py:302
  107.9 1.3 collective-permute-start.18
  109.2 0.9 collective-permute-done.17.refs_2_
  110.1 3.8 %collective-permute-done.18.refs_3_ = bf16[32,1024]{1,0:T(8,128)(2,1)S(1)} collective-permute-done((bf16[32,1024]{1,0:T(8,128)(2,1)S(1)}, bf16[32,1024]{1,0:T(8,128)(2,1)S(1)}, u32[]{:S(2)}, u32[]{:S(2)}) %collective-permute-start.18) | collective-permute-done | bytes 65568 | tf_op jit(solution)/shard_map/ppermute | solution.py:302
  114.0 1.2 shard_map.106
  115.2 1.7 %collective-permute-done.20.got_ref = bf16[64,3200]{1,0:T(8,128)(2,1)S(1)} collective-permute-done((bf16[64,3200]{1,0:T(8,128)(2,1)S(1)}, bf16[64,3200]{1,0:T(8,128)(2,1)S(1)}, u32[]{:S(2)}, u32[]{:S(2)}) %collective-permute-start.20) | collective-permute-done | bytes 409632 | tf_op jit(solution)/shard_map/ppermute | solution.py:302
  117.0 1.6 %collective-permute-start.21 = (bf16[32,3200]{1,0:T(8,128)(2,1)S(1)}, bf16[32,3200]{1,0:T(8,128)(2,1)S(1)}, u32[]{:S(2)}, u32[]{:S(2)}) collective-permute-start(bf16[32,3200]{1,0:T(8,128)(2,1)S(1)} %get-tuple-element.70), channel_id=1, source_target_pairs={{0,16},{1,17},{2,18},{3,19},{4,20},{5,21},{6,22},{7,23},{8,24},{9,... | collective-permute-start | bytes 614408 | tf_op jit(solution)/shard_map/ppermute | solution.py:302
  118.6 5.6 %collective-permute-done.21.got_ref = bf16[32,3200]{1,0:T(8,128)(2,1)S(1)} collective-permute-done((bf16[32,3200]{1,0:T(8,128)(2,1)S(1)}, bf16[32,3200]{1,0:T(8,128)(2,1)S(1)}, u32[]{:S(2)}, u32[]{:S(2)}) %collective-permute-start.21) | collective-permute-done | bytes 204832 | tf_op jit(solution)/shard_map/ppermute | solution.py:302
  124.4 1.6 %collective-permute-start.23 = (bf16[32,1536]{1,0:T(8,128)(2,1)S(1)}, bf16[32,1536]{1,0:T(8,128)(2,1)S(1)}, u32[]{:S(2)}, u32[]{:S(2)}) collective-permute-start(bf16[32,1536]{1,0:T(8,128)(2,1)S(1)} %shard_map.108.refs_0_), channel_id=1, source_target_pairs={{0,16},{1,17},{2,18},{3,19},{4,20},{5,21},{6,22},{7,23},{8,24},{9,... | collective-permute-start | bytes 294920 | tf_op jit(solution)/shard_map/ppermute | solution.py:302
  126.0 3.1 %collective-permute-done.23.refs_2_ = bf16[32,1536]{1,0:T(8,128)(2,1)S(1)} collective-permute-done((bf16[32,1536]{1,0:T(8,128)(2,1)S(1)}, bf16[32,1536]{1,0:T(8,128)(2,1)S(1)}, u32[]{:S(2)}, u32[]{:S(2)}) %collective-permute-start.23) | collective-permute-done | bytes 98336 | tf_op jit(solution)/shard_map/ppermute | solution.py:302
  129.1 1.3 collective-permute-done.24.refs_3_
  131.0 2.0 %collective-permute-start.25 = (bf16[32,1024]{1,0:T(8,128)(2,1)S(1)}, bf16[32,1024]{1,0:T(8,128)(2,1)S(1)}, u32[]{:S(2)}, u32[]{:S(2)}) collective-permute-start(bf16[32,1024]{1,0:T(8,128)(2,1)S(1)} %get-tuple-element.72), channel_id=1, source_target_pairs={{0,1},{1,0},{2,3},{3,2},{4,5},{5,4},{6,7},{7,6},{8,9},{9,8},{10,11... | collective-permute-start | bytes 196616 | tf_op jit(solution)/shard_map/ppermute | solution.py:302
  133.1 2.4 %collective-permute-start.27 = (bf16[32,1024]{1,0:T(8,128)(2,1)S(1)}, bf16[32,1024]{1,0:T(8,128)(2,1)S(1)}, u32[]{:S(2)}, u32[]{:S(2)}) collective-permute-start(bf16[32,1024]{1,0:T(8,128)(2,1)S(1)} %get-tuple-element.74), channel_id=1, source_target_pairs={{0,5},{1,4},{2,7},{3,6},{4,1},{5,0},{6,3},{7,2},{8,13},{9,12},{10,... | collective-permute-start | bytes 196616 | tf_op jit(solution)/shard_map/ppermute | solution.py:302
  135.5 4.9 %collective-permute-done.26.refs_2_ = bf16[32,1024]{1,0:T(8,128)(2,1)S(1)} collective-permute-done((bf16[32,1024]{1,0:T(8,128)(2,1)S(1)}, bf16[32,1024]{1,0:T(8,128)(2,1)S(1)}, u32[]{:S(2)}, u32[]{:S(2)}) %collective-permute-start.26) | collective-permute-done | bytes 65568 | tf_op jit(solution)/shard_map/ppermute | solution.py:302
  140.4 0.8 collective-permute-done.27.refs_3_
  141.3 5.4 %collective-permute-done.28.refs_4_ = bf16[64,1024]{1,0:T(8,128)(2,1)S(1)} collective-permute-done((bf16[64,1024]{1,0:T(8,128)(2,1)S(1)}, bf16[64,1024]{1,0:T(8,128)(2,1)S(1)}, u32[]{:S(2)}, u32[]{:S(2)}) %collective-permute-start.28) | collective-permute-done | bytes 131104 | tf_op jit(solution)/shard_map/ppermute | solution.py:302
  146.7 1.1 shard_map.111
  (59 shorter events, 4.9 us)
Async XLA Ops:
  0.0 35.4 %copy-start = (bf16[512,1024]{1,0:T(8,128)(2,1)S(1)}, bf16[512,1024]{1,0:T(8,128)(2,1)}, u32[]{:S(2)}) copy-start(bf16[512,1024]{1,0:T(8,128)(2,1)} %refs_5_.1) | copy-start | bytes 3145732
  0.0 1.1 copy-start.3
  1.1 0.8 copy-start.8
  2.0 0.8 copy-start.9
  2.8 84.1 %copy-start.11 = (s32[4,1,64,8]{2,3,1,0:T(8,128)S(1)}, s32[4,1,64,8]{2,3,1,0:T(8,128)}, u32[]{:S(2)}) copy-start(s32[4,1,64,8]{2,3,1,0:T(8,128)} %param.16) | copy-start | bytes 24580
  2.8 84.2 %copy-start.12 = (f32[4,1,64,8]{2,3,1,0:T(8,128)S(1)}, f32[4,1,64,8]{2,3,1,0:T(8,128)}, u32[]{:S(2)}) copy-start(f32[4,1,64,8]{2,3,1,0:T(8,128)} %param.17) | copy-start | bytes 24580
  3.3 3.2 %collective-permute-start = (bf16[64,1536]{1,0:T(8,128)(2,1)S(1)}, bf16[64,1536]{1,0:T(8,128)(2,1)S(1)}, u32[]{:S(2)}, u32[]{:S(2)}) collective-permute-start(bf16[64,1536]{1,0:T(8,128)(2,1)S(1)} %get-tuple-element.41), channel_id=1, source_target_pairs={{0,8},{1,9},{2,10},{3,11},{4,12},{5,13},{6,14},{7,15},{8,0},{9,1},... | collective-permute-start | bytes 589832 | tf_op jit(solution)/shard_map/ppermute | solution.py:302
  3.8 8.3 %collective-permute-start.1 = (bf16[64,1536]{1,0:T(8,128)(2,1)S(1)}, bf16[64,1536]{1,0:T(8,128)(2,1)S(1)}, u32[]{:S(2)}, u32[]{:S(2)}) collective-permute-start(bf16[64,1536]{1,0:T(8,128)(2,1)S(1)} %get-tuple-element.42), channel_id=1, source_target_pairs={{0,16},{1,17},{2,18},{3,19},{4,20},{5,21},{6,22},{7,23},{8,24},{9,... | collective-permute-start | bytes 589832 | tf_op jit(solution)/shard_map/ppermute | solution.py:302
  6.4 9.4 %collective-permute-start.2 = (bf16[64,1536]{1,0:T(8,128)(2,1)S(1)}, bf16[64,1536]{1,0:T(8,128)(2,1)S(1)}, u32[]{:S(2)}, u32[]{:S(2)}) collective-permute-start(bf16[64,1536]{1,0:T(8,128)(2,1)S(1)} %get-tuple-element.43), channel_id=1, source_target_pairs={{0,24},{1,25},{2,26},{3,27},{4,28},{5,29},{6,30},{7,31},{8,16},{9,... | collective-permute-start | bytes 589832 | tf_op jit(solution)/shard_map/ppermute | solution.py:302
  20.2 12.8 %collective-permute-start.3 = (bf16[256,512]{1,0:T(8,128)(2,1)S(1)}, bf16[256,512]{1,0:T(8,128)(2,1)S(1)}, u32[]{:S(2)}, u32[]{:S(2)}) collective-permute-start(bf16[256,512]{1,0:T(8,128)(2,1)S(1)} %get-tuple-element.45), channel_id=1, source_target_pairs={{0,2},{1,3},{2,0},{3,1},{4,6},{5,7},{6,4},{7,5},{8,10},{9,11},{10,... | collective-permute-start | bytes 786440 | tf_op jit(solution)/shard_map/ppermute | solution.py:302
  23.0 38.4 %collective-permute-start.9 = (bf16[256,1024]{1,0:T(8,128)(2,1)S(1)}, bf16[256,1024]{1,0:T(8,128)(2,1)}, u32[]{:S(2)}, u32[]{:S(2)}) collective-permute-start(bf16[256,1024]{1,0:T(8,128)(2,1)S(1)} %slice.10), channel_id=1, source_target_pairs={{0,4},{1,5},{2,6},{3,7},{4,0},{5,1},{6,2},{7,3},{8,12},{9,13},{10,... | collective-permute-start | bytes 1572872 | tf_op jit(solution)/shard_map/ppermute | solution.py:302
  33.7 34.6 %collective-permute-start.5 = (bf16[512,512]{1,0:T(8,128)(2,1)}, bf16[512,512]{1,0:T(8,128)(2,1)}, u32[]{:S(2)}, u32[]{:S(2)}) collective-permute-start(bf16[512,512]{1,0:T(8,128)(2,1)} %constant_dynamic-update-slice_fusion.refs_0_), channel_id=1, source_target_pairs={{0,16},{1,17},{2,18},{3,19},{4,20},{5,21},{6,22},{7,23},{8,24},{9,... | collective-permute-start | bytes 1572872 | tf_op jit(solution)/shard_map/ppermute | solution.py:302
  35.4 52.3 %collective-permute-start.8 = (bf16[512,1024]{1,0:T(8,128)(2,1)S(1)}, bf16[512,1024]{1,0:T(8,128)(2,1)}, u32[]{:S(2)}, u32[]{:S(2)}) collective-permute-start(bf16[512,1024]{1,0:T(8,128)(2,1)S(1)} %copy-done), channel_id=1, source_target_pairs={{0,1},{1,0},{2,3},{3,2},{4,5},{5,4},{6,7},{7,6},{8,9},{9,8},{10,11... | collective-permute-start | bytes 3145736 | tf_op jit(solution)/shard_map/ppermute | solution.py:302
  36.9 77.1 %slice-start = ((s8[6291456]{0:T(1024)(128)(4,1)}), s8[2097152]{0:T(1024)(128)(4,1)S(1)}, s32[]{:S(2)}) async-start(s8[6291456]{0:T(1024)(128)(4,1)} %bitcast.12), calls=%async_computation | async-start | bytes 4194304
  36.9 29.9 %collective-permute-start.6 = (bf16[128,1024]{1,0:T(8,128)(2,1)S(1)}, bf16[128,1024]{1,0:T(8,128)(2,1)S(1)}, u32[]{:S(2)}, u32[]{:S(2)}) collective-permute-start(bf16[128,1024]{1,0:T(8,128)(2,1)S(1)} %get-tuple-element.46), channel_id=1, source_target_pairs={{0,4},{1,5},{2,6},{3,7},{4,0},{5,1},{6,2},{7,3},{8,12},{9,13},{10,... | collective-permute-start | bytes 786440 | tf_op jit(solution)/shard_map/ppermute | solution.py:302
  37.5 34.1 %collective-permute-start.10 = (bf16[128,1024]{1,0:T(8,128)(2,1)S(1)}, bf16[128,1024]{1,0:T(8,128)(2,1)}, u32[]{:S(2)}, u32[]{:S(2)}) collective-permute-start(bf16[128,1024]{1,0:T(8,128)(2,1)S(1)} %get-tuple-element.48), channel_id=1, source_target_pairs={{0,4},{1,5},{2,6},{3,7},{4,0},{5,1},{6,2},{7,3},{8,12},{9,13},{10,... | collective-permute-start | bytes 786440 | tf_op jit(solution)/shard_map/ppermute | solution.py:302
  61.3 26.2 %collective-permute-start.4 = (bf16[512,512]{1,0:T(8,128)(2,1)}, bf16[512,512]{1,0:T(8,128)(2,1)}, u32[]{:S(2)}, u32[]{:S(2)}) collective-permute-start(bf16[512,512]{1,0:T(8,128)(2,1)} %constant_dynamic-update-slice_fusion.refs_0_), channel_id=1, source_target_pairs={{0,8},{1,9},{2,10},{3,11},{4,12},{5,13},{6,14},{7,15},{8,0},{9,1},... | collective-permute-start | bytes 1572872 | tf_op jit(solution)/shard_map/ppermute | solution.py:302
  66.9 20.8 %collective-permute-start.11 = (bf16[256,1024]{1,0:T(8,128)(2,1)}, bf16[256,1024]{1,0:T(8,128)(2,1)}, u32[]{:S(2)}, u32[]{:S(2)}) collective-permute-start(bf16[256,1024]{1,0:T(8,128)(2,1)} %collective-permute-done.9.refs_7_), channel_id=1, source_target_pairs={{0,1},{1,0},{2,3},{3,2},{4,5},{5,4},{6,7},{7,6},{8,9},{9,8},{10,11... | collective-permute-start | bytes 1572872 | tf_op jit(solution)/shard_map/ppermute | solution.py:302
  68.3 19.3 %collective-permute-start.7 = (bf16[512,512]{1,0:T(8,128)(2,1)}, bf16[512,512]{1,0:T(8,128)(2,1)}, u32[]{:S(2)}, u32[]{:S(2)}) collective-permute-start(bf16[512,512]{1,0:T(8,128)(2,1)} %collective-permute-done.5.refs_2_), channel_id=1, source_target_pairs={{0,8},{1,9},{2,10},{3,11},{4,12},{5,13},{6,14},{7,15},{8,0},{9,1},... | collective-permute-start | bytes 1572872 | tf_op jit(solution)/shard_map/ppermute | solution.py:302
  71.6 13.1 %collective-permute-start.12 = (bf16[128,1024]{1,0:T(8,128)(2,1)S(1)}, bf16[128,1024]{1,0:T(8,128)(2,1)S(1)}, u32[]{:S(2)}, u32[]{:S(2)}) collective-permute-start(bf16[128,1024]{1,0:T(8,128)(2,1)S(1)} %collective-permute-done.6.refs_8_), channel_id=1, source_target_pairs={{0,1},{1,0},{2,3},{3,2},{4,5},{5,4},{6,7},{7,6},{8,9},{9,8},{10,11... | collective-permute-start | bytes 786440 | tf_op jit(solution)/shard_map/ppermute | solution.py:302
  73.1 0.7 copy-start.4
  84.7 0.7 copy-start.6
  85.4 10.4 %collective-permute-start.13 = (bf16[128,1024]{1,0:T(8,128)(2,1)}, bf16[128,1024]{1,0:T(8,128)(2,1)}, u32[]{:S(2)}, u32[]{:S(2)}) collective-permute-start(bf16[128,1024]{1,0:T(8,128)(2,1)} %collective-permute-done.10.refs_9_), channel_id=1, source_target_pairs={{0,1},{1,0},{2,3},{3,2},{4,5},{5,4},{6,7},{7,6},{8,9},{9,8},{10,11... | collective-permute-start | bytes 786440 | tf_op jit(solution)/shard_map/ppermute | solution.py:302
  87.6 8.2 %collective-permute-start.14 = (bf16[256,128]{1,0:T(8,128)(2,1)S(1)}, bf16[256,128]{1,0:T(8,128)(2,1)S(1)}, u32[]{:S(2)}, u32[]{:S(2)}) collective-permute-start(bf16[256,128]{1,0:T(8,128)(2,1)S(1)} %get-tuple-element.56.mine_ref.place_ref), channel_id=1, source_target_pairs={{0,2},{1,3},{2,0},{3,1},{4,6},{5,7},{6,4},{7,5},{8,10},{9,11},{10,... | collective-permute-start | bytes 196616 | tf_op jit(solution)/shard_map/ppermute | solution.py:302
  87.7 1.0 copy-start.2
  88.7 0.9 copy-start.5
  89.7 0.9 copy-start.7
  90.6 13.2 %copy-start.10 = (f32[1024]{0:T(1024)S(1)}, f32[1024]{0:T(1024)}, u32[]{:S(2)}) copy-start(f32[1024]{0:T(1024)} %param.15) | copy-start | bytes 12292
  90.6 23.3 %slice-start.1 = ((s8[6291456]{0:T(1024)(128)(4,1)}), s8[4194304]{0:T(1024)(128)(4,1)S(1)}, s32[]{:S(2)}) async-start(s8[6291456]{0:T(1024)(128)(4,1)} %bitcast.12), calls=%async_computation.1 | async-start | bytes 8388608
  97.3 6.4 %collective-permute-start.15 = (bf16[128,1024]{1,0:T(8,128)(2,1)S(1)}, bf16[128,1024]{1,0:T(8,128)(2,1)S(1)}, u32[]{:S(2)}, u32[]{:S(2)}) collective-permute-start(bf16[128,1024]{1,0:T(8,128)(2,1)S(1)} %get-tuple-element.60), channel_id=1, source_target_pairs={{0,2},{1,3},{2,0},{3,1},{4,6},{5,7},{6,4},{7,5},{8,10},{9,11},{10,... | collective-permute-start | bytes 786440 | tf_op jit(solution)/shard_map/ppermute | solution.py:302
  103.9 5.3 %collective-permute-start.16 = (bf16[32,1024]{1,0:T(8,128)(2,1)S(1)}, bf16[32,1024]{1,0:T(8,128)(2,1)S(1)}, u32[]{:S(2)}, u32[]{:S(2)}) collective-permute-start(bf16[32,1024]{1,0:T(8,128)(2,1)S(1)} %get-tuple-element.62), channel_id=1, source_target_pairs={{0,1},{1,0},{2,3},{3,2},{4,5},{5,4},{6,7},{7,6},{8,9},{9,8},{10,11... | collective-permute-start | bytes 196616 | tf_op jit(solution)/shard_map/ppermute | solution.py:302
  104.5 5.7 %collective-permute-start.17 = (bf16[32,1024]{1,0:T(8,128)(2,1)S(1)}, bf16[32,1024]{1,0:T(8,128)(2,1)S(1)}, u32[]{:S(2)}, u32[]{:S(2)}) collective-permute-start(bf16[32,1024]{1,0:T(8,128)(2,1)S(1)} %get-tuple-element.63), channel_id=1, source_target_pairs={{0,4},{1,5},{2,6},{3,7},{4,0},{5,1},{6,2},{7,3},{8,12},{9,13},{10,... | collective-permute-start | bytes 196616 | tf_op jit(solution)/shard_map/ppermute | solution.py:302
  107.9 6.1 %collective-permute-start.18 = (bf16[32,1024]{1,0:T(8,128)(2,1)S(1)}, bf16[32,1024]{1,0:T(8,128)(2,1)S(1)}, u32[]{:S(2)}, u32[]{:S(2)}) collective-permute-start(bf16[32,1024]{1,0:T(8,128)(2,1)S(1)} %get-tuple-element.64), channel_id=1, source_target_pairs={{0,5},{1,4},{2,7},{3,6},{4,1},{5,0},{6,3},{7,2},{8,13},{9,12},{10,... | collective-permute-start | bytes 196616 | tf_op jit(solution)/shard_map/ppermute | solution.py:302
  114.0 16.4 %copy-start.1 = (bf16[1,1536,1024]{2,1,0:T(8,128)(2,1)S(1)}, bf16[1,1536,1024]{2,1,0:T(8,128)(2,1)}, u32[]{:S(2)}) copy-start(bf16[1,1536,1024]{2,1,0:T(8,128)(2,1)} %param.19) | copy-start | bytes 9437188
  115.2 1.8 %collective-permute-start.20 = (bf16[64,3200]{1,0:T(8,128)(2,1)S(1)}, bf16[64,3200]{1,0:T(8,128)(2,1)S(1)}, u32[]{:S(2)}, u32[]{:S(2)}) collective-permute-start(bf16[64,3200]{1,0:T(8,128)(2,1)S(1)} %get-tuple-element.68), channel_id=1, source_target_pairs={{0,8},{1,9},{2,10},{3,11},{4,12},{5,13},{6,14},{7,15},{8,0},{9,1},... | collective-permute-start | bytes 1228808 | tf_op jit(solution)/shard_map/ppermute | solution.py:302
  117.0 7.2 %collective-permute-start.21 = (bf16[32,3200]{1,0:T(8,128)(2,1)S(1)}, bf16[32,3200]{1,0:T(8,128)(2,1)S(1)}, u32[]{:S(2)}, u32[]{:S(2)}) collective-permute-start(bf16[32,3200]{1,0:T(8,128)(2,1)S(1)} %get-tuple-element.70), channel_id=1, source_target_pairs={{0,16},{1,17},{2,18},{3,19},{4,20},{5,21},{6,22},{7,23},{8,24},{9,... | collective-permute-start | bytes 614408 | tf_op jit(solution)/shard_map/ppermute | solution.py:302
  118.6 22.7 %collective-permute-start.19 = (bf16[256,1024]{1,0:T(8,128)(2,1)S(1)}, bf16[256,1024]{1,0:T(8,128)(2,1)S(1)}, u32[]{:S(2)}, u32[]{:S(2)}) collective-permute-start(bf16[256,1024]{1,0:T(8,128)(2,1)S(1)} %get-tuple-element.65), channel_id=1, source_target_pairs={{0,2},{1,3},{2,0},{3,1},{4,6},{5,7},{6,4},{7,5},{8,10},{9,11},{10,... | collective-permute-start | bytes 1572872 | tf_op jit(solution)/shard_map/ppermute | solution.py:302
  124.4 4.7 %collective-permute-start.23 = (bf16[32,1536]{1,0:T(8,128)(2,1)S(1)}, bf16[32,1536]{1,0:T(8,128)(2,1)S(1)}, u32[]{:S(2)}, u32[]{:S(2)}) collective-permute-start(bf16[32,1536]{1,0:T(8,128)(2,1)S(1)} %shard_map.108.refs_0_), channel_id=1, source_target_pairs={{0,16},{1,17},{2,18},{3,19},{4,20},{5,21},{6,22},{7,23},{8,24},{9,... | collective-permute-start | bytes 294920 | tf_op jit(solution)/shard_map/ppermute | solution.py:302
  126.0 3.1 %collective-permute-start.22 = (bf16[32,1536]{1,0:T(8,128)(2,1)S(1)}, bf16[32,1536]{1,0:T(8,128)(2,1)S(1)}, u32[]{:S(2)}, u32[]{:S(2)}) collective-permute-start(bf16[32,1536]{1,0:T(8,128)(2,1)S(1)} %shard_map.108.refs_0_), channel_id=1, source_target_pairs={{0,8},{1,9},{2,10},{3,11},{4,12},{5,13},{6,14},{7,15},{8,0},{9,1},... | collective-permute-start | bytes 294920 | tf_op jit(solution)/shard_map/ppermute | solution.py:302
  129.1 1.3 collective-permute-start.24
  131.0 4.5 %collective-permute-start.25 = (bf16[32,1024]{1,0:T(8,128)(2,1)S(1)}, bf16[32,1024]{1,0:T(8,128)(2,1)S(1)}, u32[]{:S(2)}, u32[]{:S(2)}) collective-permute-start(bf16[32,1024]{1,0:T(8,128)(2,1)S(1)} %get-tuple-element.72), channel_id=1, source_target_pairs={{0,1},{1,0},{2,3},{3,2},{4,5},{5,4},{6,7},{7,6},{8,9},{9,8},{10,11... | collective-permute-start | bytes 196616 | tf_op jit(solution)/shard_map/ppermute | solution.py:302
  133.0 7.4 %collective-permute-start.26 = (bf16[32,1024]{1,0:T(8,128)(2,1)S(1)}, bf16[32,1024]{1,0:T(8,128)(2,1)S(1)}, u32[]{:S(2)}, u32[]{:S(2)}) collective-permute-start(bf16[32,1024]{1,0:T(8,128)(2,1)S(1)} %get-tuple-element.73), channel_id=1, source_target_pairs={{0,4},{1,5},{2,6},{3,7},{4,0},{5,1},{6,2},{7,3},{8,12},{9,13},{10,... | collective-permute-start | bytes 196616 | tf_op jit(solution)/shard_map/ppermute | solution.py:302
  133.1 8.2 %collective-permute-start.27 = (bf16[32,1024]{1,0:T(8,128)(2,1)S(1)}, bf16[32,1024]{1,0:T(8,128)(2,1)S(1)}, u32[]{:S(2)}, u32[]{:S(2)}) collective-permute-start(bf16[32,1024]{1,0:T(8,128)(2,1)S(1)} %get-tuple-element.74), channel_id=1, source_target_pairs={{0,5},{1,4},{2,7},{3,6},{4,1},{5,0},{6,3},{7,2},{8,13},{9,12},{10,... | collective-permute-start | bytes 196616 | tf_op jit(solution)/shard_map/ppermute | solution.py:302
  141.2 5.5 %collective-permute-start.28 = (bf16[64,1024]{1,0:T(8,128)(2,1)S(1)}, bf16[64,1024]{1,0:T(8,128)(2,1)S(1)}, u32[]{:S(2)}, u32[]{:S(2)}) collective-permute-start(bf16[64,1024]{1,0:T(8,128)(2,1)S(1)} %shard_map.110), channel_id=1, source_target_pairs={{0,2},{1,3},{2,0},{3,1},{4,6},{5,7},{6,4},{7,5},{8,10},{9,11},{10,... | collective-permute-start | bytes 393224 | tf_op jit(solution)/shard_map/ppermute | solution.py:302

commit v3 on v2

--- a/solution.py
+++ b/solution.py
@@ -40,21 +40,24 @@
     return jnp.dot(a, b, preferred_element_type=F32)
 
 
+PAIR = 4
+
+
 def spread(d):
-    return (d >> 1) * 4 + (d & 1)
+    return (d // PAIR) * 2 * PAIR + d % PAIR
 
 
 def own_hi_lo():
     e = lax.axis_index("exp")
-    return lax.div(e, 4) * 2 + lax.rem(e, 2), lax.rem(lax.div(e, 2), 2)
+    return lax.div(e, 2 * PAIR) * PAIR + lax.rem(e, PAIR), lax.rem(lax.div(e, PAIR), 2)
 
 
 def aligned(x, n):
     return pl.multiple_of(x, n)
 
 
-def pack_kernel(C, qw, q_ref, new_ref, past_ref, *refs):
-    outs, sems = refs[:-1], refs[-1]
+def pack_kernel(C, qw, q_ref, new_ref, past_ref, w_ref, *refs):
+    outs, halves, sems = refs[:C], refs[C:-1], refs[-1]
     c = lax.axis_index("ctx")
     _, lo = own_hi_lo()
     copies = []
@@ -66,32 +69,37 @@
     for s in reversed(range(C)):
         target = jnp.bitwise_xor(c, s)
         out = outs[s]
-        first = lax.div(target, 2) * 4 + lax.rem(target, 2)
         for t in range(2):
-            offset = (first + 2 * jnp.bitwise_xor(lo, t)) * qw
-            copy(q_ref.at[:, pl.ds(aligned(offset, 128), qw)], out.at[:, t * qw : (t + 1) * qw])
-        kv = lax.div(target * (2 * qw // HEAD_SIZE), GROUP_EXTENT)
-        at = 2 * qw
-        for ref in (new_ref, past_ref):
-            for part in (0, KEY_VALUE_HEADS):
-                offset = (part + kv) * HEAD_SIZE
-                copy(ref.at[:, pl.ds(aligned(offset, 128), 128)], out.at[:, at : at + 128])
-                at += 128
+            shard = lax.div(target, PAIR) * 2 * PAIR + lax.rem(target, PAIR)
+            shard = shard + PAIR * jnp.bitwise_xor(lo, t)
+            copy(q_ref.at[:, pl.ds(aligned(shard * qw, 128), qw)], out.at[:, t * qw : (t + 1) * qw])
+            kv = lax.div(shard * (qw // HEAD_SIZE), GROUP_EXTENT)
+            at = 2 * qw + t * 4 * HEAD_SIZE
+            for ref in (new_ref, past_ref):
+                for part in (0, KEY_VALUE_HEADS):
+                    offset = (part + kv) * HEAD_SIZE
+                    copy(ref.at[:, pl.ds(aligned(offset, 128), 128)], out.at[:, at : at + 128])
+                    at += 128
+    half = halves[0].shape[1]
+    for j in range(2):
+        copy(w_ref.at[:, j * half : (j + 1) * half], halves[j])
     for c in copies:
         c.wait()
 
 
-def attend_kernel(C, tok, *refs):
-    msgs, outs, q_s, kv_s = refs[:C], refs[C : C + 2], refs[C + 2], refs[C + 3]
+def attend_kernel(C, t, *refs):
+    msgs, out, kv_s = refs[:C], refs[C], refs[C + 1]
     c = lax.axis_index("ctx")
-    qw = outs[0].shape[1]
+    tok, qw = msgs[0].shape[0], out.shape[1]
     rows = C * tok
+    q_s = refs[C + 2]
     for s in range(C):
         msg = msgs[s]
         at = aligned(jnp.bitwise_xor(c, s) * tok, tok)
-        q_s[pl.ds(at, tok), :] = msg[:, : 2 * qw]
-        kv_s[pl.ds(rows + at, tok), :] = msg[:, 2 * qw : 2 * qw + 256]
-        kv_s[pl.ds(at, tok), :] = msg[:, 2 * qw + 256 :]
+        first = 2 * qw + t * 4 * HEAD_SIZE
+        q_s[pl.ds(at, tok), :] = msg[:, t * qw : (t + 1) * qw]
+        kv_s[pl.ds(rows + at, tok), :] = msg[:, first : first + 2 * HEAD_SIZE]
+        kv_s[pl.ds(at, tok), :] = msg[:, first + 2 * HEAD_SIZE : first + 4 * HEAD_SIZE]
     block = 128
     for b in range(rows // block):
         seen = rows + (b + 1) * block
@@ -100,15 +108,14 @@
         row = lax.broadcasted_iota(jnp.int32, (block, seen), 0) + (rows + b * block)
         visible = lax.broadcasted_iota(jnp.int32, (block, seen), 1) <= row
         at = slice(b * block, (b + 1) * block)
-        for h in range(2 * qw // HEAD_SIZE):
+        for h in range(qw // HEAD_SIZE):
             q = q_s[at, h * HEAD_SIZE : (h + 1) * HEAD_SIZE]
             scores = lax.dot_general(q, k, (((1,), (1,)), ((), ())), preferred_element_type=F32)
             scores = jnp.where(visible, scores * HEAD_SIZE ** (-0.5), NEG_FILL)
             weights = jnp.exp(scores - jnp.max(scores, axis=1, keepdims=True))
             total = jnp.sum(weights, axis=1, keepdims=True)
             numerator = dot(weights.astype(BF16), v)
-            t, col = divmod(h * HEAD_SIZE, qw)
-            outs[t][at, col : col + HEAD_SIZE] = (numerator / total).astype(BF16)
+            out[at, h * HEAD_SIZE : (h + 1) * HEAD_SIZE] = (numerator / total).astype(BF16)
 
 
 def route_kernel(E, cap, routes_ref, gates_ref, place_ref, gate_ref):
@@ -133,47 +140,51 @@
     place_ref[...] = jnp.where(slot == places, 1.0, 0.0).astype(BF16)
 
 
-def project_kernel(C, spans, *refs):
-    atts, res_ref, ws = refs[:C], refs[C], refs[C + 1 : C + 1 + len(spans)]
-    acc, last, stacked = refs[-3:]
-    c = lax.axis_index("ctx")
+def project_kernel(C, with_residual, *refs):
+    atts, ws, acc, last, stacked = refs[:C], refs[C : C + 2 * (C - 1)], refs[-3], refs[-2], refs[-1]
     hi, _ = own_hi_lo()
+    turn = jnp.bitwise_xor(lax.axis_index("ctx"), hi)
     for s in range(C):
-        stacked[jnp.bitwise_xor(c, s)] = atts[s][...]
-    rows = res_ref.shape[0]
-    width = acc.shape[1]
-    half = width // 2
+        stacked[jnp.bitwise_xor(turn, s)] = atts[s][...]
+    half = acc.shape[1] // 2
     for j in range(2):
         at = slice(j * half, (j + 1) * half)
-        total = None
-        for (d, first, count), w in zip(spans, ws):
-            term = dot(stacked[jnp.bitwise_xor(hi, d), :, first : first + count], w[:, at])
+        total = refs[-4][:, at].astype(F32) if with_residual else None
+        for d in range(C - 1):
+            w = ws[2 * d + j]
+            term = dot(stacked[d], w[...] if w.shape[1] == half else w[:, at])
             total = term if total is None else total + term
-        acc[:rows, at] = total[:rows] + res_ref[:, at].astype(F32)
-        acc[rows:, at] = total[rows:]
-    count = last.shape[1]
-    last[...] = stacked[jnp.bitwise_xor(hi, C - 1), :, stacked.shape[2] - count :]
-
-
-def last_kernel(E, cap, acc_ref, last_ref, w_ref, mine_ref, other_ref, own_ref, full_ref, keep_ref, send_ref):
-    rows = own_ref.shape[0]
-    total = acc_ref[...] + dot(last_ref[...], w_ref[...])
-    own_ref[...] = total[:rows]
-    rounded = total.astype(BF16)
-    full_ref[...] = rounded[rows:]
-    for t, place in enumerate((mine_ref, other_ref)):
-        picked = lax.dot_general(
-            place[...],
-            rounded[t * rows : (t + 1) * rows],
-            (((0,), (0,)), ((), ())),
-            preferred_element_type=F32,
-        )
-        for d in range(E // 2):
-            near, far = spread(d) ^ (2 * t), spread(d) ^ 2 ^ (2 * t)
-            at = (2 * d + t) * cap
-            keep_ref[at : at + cap, :] = picked[near * cap : (near + 1) * cap]
-            at = (2 * d + 1 - t) * cap
-            send_ref[at : at + cap, :] = picked[far * cap : (far + 1) * cap].astype(BF16)
+        acc[:, at] = total
+    last[...] = stacked[C - 1]
+
+
+def last_kernel(E, cap, *refs):
+    accs, lasts, ws, places, (own_ref, full_ref, keep_ref, send_ref) = (
+        refs[:2],
+        refs[2:4],
+        refs[4:6],
+        refs[6:8],
+        refs[8:],
+    )
+    half = ws[0].shape[1]
+    for j in range(2):
+        cols = slice(j * half, (j + 1) * half)
+        for t in range(2):
+            total = accs[t][:, cols] + dot(lasts[t][...], ws[j][...])
+            rounded = total.astype(BF16)
+            if t == 0:
+                own_ref[:, cols] = total
+            else:
+                full_ref[:, cols] = rounded
+            picked = lax.dot_general(
+                places[t][...], rounded, (((0,), (0,)), ((), ())), preferred_element_type=F32
+            )
+            for d in range(E // 2):
+                near, far = spread(d) ^ (PAIR * t), spread(d) ^ PAIR ^ (PAIR * t)
+                at = (2 * d + t) * cap
+                keep_ref[at : at + cap, cols] = picked[near * cap : (near + 1) * cap]
+                at = (2 * d + 1 - t) * cap
+                send_ref[at : at + cap, cols] = picked[far * cap : (far + 1) * cap].astype(BF16)
 
 
 def outgoing_kernel(keep_ref, got_ref, gain_ref, *outs):
@@ -191,7 +202,7 @@
     wide = w_ref.shape[1]
     for d in range(E // 2):
         for t in range(2):
-            at = aligned(jnp.bitwise_xor(e, spread(d) ^ (2 * t)) * cap, cap)
+            at = aligned(jnp.bitwise_xor(e, spread(d) ^ (PAIR * t)) * cap, cap)
             x_s[pl.ds(at, cap), :] = xs[d][t * cap : (t + 1) * cap, :]
     plain = x_s[...].astype(F32) / gain_ref[...]
     square = jnp.sum(plain * plain, axis=1, keepdims=True)
@@ -252,7 +263,7 @@
     part_s[...] = dot(x_s[...], w_ref[...]).astype(BF16)
     for d in range(E // 2):
         for t in range(2):
-            at = aligned(jnp.bitwise_xor(e, spread(d) ^ (2 * t)) * cap, cap)
+            at = aligned(jnp.bitwise_xor(e, spread(d) ^ (PAIR * t)) * cap, cap)
             outs[d][t * cap : (t + 1) * cap, :] = part_s[pl.ds(at, cap), :]
 
 
@@ -266,7 +277,7 @@
     for d in range(E // 2):
         at = spread(d) * cap
         x_s[at : at + cap, :] = xs[d][:cap, :]
-        at = (spread(d) ^ 2) * cap
+        at = (spread(d) ^ PAIR) * cap
         x_s[at : at + cap, :] = far[d * cap : (d + 1) * cap, :]
     collected = dot(place_ref[...], x_s[...])
     mixed = own_ref[...] + got_ref[...].astype(F32)
@@ -304,73 +315,83 @@
     def after(x, *others):
         return lax.optimization_barrier((x, *others))[0]
 
-    cuts = [(0, qw // 2), (qw // 2, qw // 4), (qw * 3 // 4, qw // 4)]
-    chunks = [out_weight[a : a + n] for a, n in cuts]
-    shards = {0: [(0, qw, out_weight)]}
-    for d in range(2, C, 2):
-        shards[d] = [(0, cuts[0][1], permute(chunks[0], exp=spread(d)))]
-    shards[1] = [(0, qw, permute(out_weight, exp=1))]
-
-    msgs = call(
+    half = width // 2
+    *msgs, half_a, half_b = call(
         functools.partial(pack_kernel, C, qw),
-        [sds((tok, 2 * qw + 512), BF16)] * C,
-        3,
-        scratch=[pltpu.SemaphoreType.DMA((6 * C,))],
-        in_specs=[HBM] * 3,
+        [sds((tok, 2 * qw + 8 * HEAD_SIZE), BF16)] * C + [sds((qw, half), BF16)] * 2,
+        4,
+        scratch=[pltpu.SemaphoreType.DMA((10 * C + 2,))],
+        in_specs=[HBM] * 4,
         cost=(0, 4 * 2**20),
+        limit=57,
     )(
         queries.reshape(tok, queries.shape[3]),
         new_keys_values.reshape(tok, new_keys_values.shape[3]),
         cached_keys_values.reshape(tok, cached_keys_values.shape[3]),
+        out_weight,
     )
     got = [msgs[0]] + [permute(msgs[s], ctx=s) for s in range(1, C)]
-    mine, other = call(
-        functools.partial(attend_kernel, C, tok),
-        [sds((rows, qw), BF16)] * 2,
-        C,
-        scratch=[pltpu.VMEM((rows, 2 * qw), BF16), pltpu.VMEM((2 * rows, 2 * HEAD_SIZE), BF16)],
-        cost=(4 * 2 * rows * 2 * rows * qw, 16 * 2**20),
-        limit=16,
-    )(*got)
-    theirs = permute(other, exp=2)
+    shards = {0: [out_weight, out_weight], 1: [None, permute(half_b, exp=1)]}
     for d in range(2, C, 2):
-        for (a, n), chunk in zip(cuts[1:], chunks[1:]):
-            shards[d].append((a, n, permute(after(chunk, mine), exp=spread(d))))
+        shards[d] = [permute(half_a, exp=spread(d)), None]
+    step = [shards[1][1]] + [shards[d][0] for d in range(2, C, 2)]
+    got[0] = after(got[0], *step)
+    shards[1][0] = permute(after(half_a, *step), exp=1)
+    for d in range(2, C, 2):
+        shards[d][1] = permute(after(half_b, *step), exp=spread(d))
+    step = [shards[1][0]] + [shards[d][1] for d in range(2, C, 2)]
+    for d in range(3, C, 2):
+        shards[d] = [
+            permute(after(shards[d - 1][0], *step), exp=1),
+            permute(after(shards[1][1], *step), exp=spread(d - 1)),
+        ]
+
+    def attend(t, msgs):
+        return call(
+            functools.partial(attend_kernel, C, t),
+            sds((rows, qw), BF16),
+            C,
+            scratch=[pltpu.VMEM((2 * rows, 2 * HEAD_SIZE), BF16), pltpu.VMEM((rows, qw), BF16)],
+            cost=(4 * rows * 2 * rows * qw, 8 * 2**20),
+            limit=16,
+        )(*msgs)
+
+    other = attend(1, got)
+    theirs = permute(other, exp=PAIR)
+    mine = attend(0, [after(got[0], other)] + got[1:])
+
+    def gather(x, before):
+        atts = {0: x, 1: permute(x, ctx=1)}
+        for s in range(2, C, 2):
+            atts[s] = permute(x, ctx=s)
+            atts[s + 1] = permute(after(atts[s], *before), ctx=1)
+        return [atts[s] for s in range(C)]
+
+    mine_all = gather(mine, [])
+    theirs_all = gather(after(theirs, *step), [])
     place, gate = call(
         functools.partial(route_kernel, E, cap),
         [sds((rows, slots), BF16), sds((rows, 128), F32)],
         2,
         cost=(0, 2**20),
+        limit=16,
     )(
         after(routes, mine).reshape(rows, routes.shape[3]),
         after(gates, mine).reshape(rows, gates.shape[3]),
     )
-    attended = jnp.concatenate([mine, theirs], axis=0)
-    atts = {0: attended}
-    for s in range(2, C, 2):
-        atts[s] = permute(attended, ctx=s)
-    atts[1] = permute(attended, ctx=1)
-    for d in range(3, C, 2):
-        shards[d] = [
-            (a, n, permute(after(w, mine), exp=1)) for a, n, w in shards[d - 1]
-        ]
-    for s in range(3, C, 2):
-        atts[s] = permute(after(atts[s - 1], shards[2][1][2]), ctx=1)
-    other_place = permute(place, exp=2)
-
-    spans, pieces = [], []
-    for d in range(C):
-        for a, n, w in shards[d]:
-            spans.append((d, a, n))
-            pieces.append(w)
-    last_rows = spans[-1][2]
-    acc, last = call(
-        functools.partial(project_kernel, C, spans[:-1]),
-        [sds((2 * rows, width), F32), sds((2 * rows, last_rows), BF16)],
-        C + len(spans),
-        scratch=[pltpu.VMEM((C, 2 * rows, qw), BF16)],
-        cost=(4 * rows * qw * width * (C - 1), 8 * 2**20),
-    )(*[atts[s] for s in range(C)], residual.reshape(rows, width), *pieces[:-1])
+    other_place = permute(place, exp=PAIR)
+
+    def project(atts, *extra):
+        return call(
+            functools.partial(project_kernel, C, bool(extra)),
+            [sds((rows, width), F32), sds((rows, qw), BF16)],
+            C + 2 * (C - 1) + len(extra),
+            scratch=[pltpu.VMEM((C, rows, qw), BF16)],
+            cost=(2 * rows * qw * width * (C - 1), 4 * 2**20),
+        )(*atts, *[w for d in range(C - 1) for w in shards[d]], *extra)
+
+    acc, last = project(mine_all, residual.reshape(rows, width))
+    acc_far, last_far = project(theirs_all)
     own, full, keep, send = call(
         functools.partial(last_kernel, E, cap),
         [
@@ -379,16 +400,16 @@
             sds((slots, width), F32),
             sds((slots, width), BF16),
         ],
-        5,
-        cost=(4 * rows * (last_rows + slots) * width, 6 * 2**20),
-    )(acc, last, pieces[-1], place, other_place)
+        8,
+        cost=(4 * rows * (qw + slots) * width, 6 * 2**20),
+    )(acc, acc_far, last, last_far, *shards[C - 1], place, other_place)
     gain = norm_gain.reshape(1, width)
     outgoing = call(
         outgoing_kernel,
         [sds((2 * cap, width), BF16)] * (E // 2),
         3,
         cost=(0, 2**20),
-    )(keep, permute(send, exp=2), gain)
+    )(keep, permute(send, exp=PAIR), gain)
     incoming = [outgoing[0]] + [permute(outgoing[d], exp=spread(d)) for d in range(1, E // 2)]
 
     order = [0]
@@ -403,7 +424,7 @@
         scratch=[pltpu.VMEM((slots, width), BF16), pltpu.VMEM((slots, wide + 128), F32)],
         cost=(2 * slots * width * wide, 2 * width * wide),
     )(*incoming, gain, w_gate_up.reshape(width, wide))
-    arrived = permute(after(full, *incoming), exp=2)
+    arrived = permute(after(full, *incoming), exp=PAIR)
     bit = 1
     while 2 * bit < C:
         count = keep.shape[0] // 2
@@ -443,7 +464,7 @@
         5 + E // 2,
         scratch=[pltpu.VMEM((slots, width), BF16)],
         cost=(0, 2 * 2**20),
-    )(own, arrived, place, gate, *returned, permute(far, exp=2))
+    )(own, arrived, place, gate, *returned, permute(far, exp=PAIR))
     return result.reshape(C, 1, tok, width)
 
 

time: 148 us -> 126 us (0.85)
  waiting for transfers between devices: 89.1 us -> 65 us
  Pallas kernels: 15.2 us -> 18.9 us
  local copies, waits for them, and re-layouts: 9.9 us -> 6.5 us
  starting transfers between devices: 33.3 us -> 35.2 us
    ppermute x29 -> x31, waiting for transfers between devices: 89.1 us -> 65 us  [permute(): return lax.ppermute(x, ('ctx', 'exp'), pairs)]
    unnamed x31 -> x18, local copies, waits for them, and re-layouts: 7.89 us -> 4.89 us
    pallas_call x3 -> x5, Pallas kernels: 9.95 us -> 12.5 us  [the longest x2 4.59 us: attend(): call(functools.partial(attend_kernel, C, t), sds((rows, qw), BF16), C, sc...]
    ppermute x29 -> x31, starting transfers between devices: 33.3 us -> 35.2 us  [permute(): return lax.ppermute(x, ('ctx', 'exp'), pairs)]
  transfers between devices with their start and end apart: 29 -> 31, of which waited for: 17 -> 17; matrix products, arithmetic and copies ran while one was open for 2% -> 1% of each run, Pallas kernels for 4% -> 8%
where the time goes in v3:
time: 126 us
  waiting for transfers between devices  65 us (52%)
  starting transfers between devices  35.2 us (28%)
  Pallas kernels  18.9 us (15%)
  local copies, waits for them, and re-layouts  6.5 us (5%)
    ppermute x31, waiting for transfers between devices, permute(): return lax.ppermute(x, ('ctx', 'exp'), pairs)  65 us
    ppermute x31, starting transfers between devices, permute(): return lax.ppermute(x, ('ctx', 'exp'), pairs)  35.2 us
    unnamed x18, local copies, waits for them, and re-layouts  4.89 us
    pallas_call x2, Pallas kernels, attend(): call(functools.partial(attend_kernel, C, t), sds((rows, qw), BF16), C, sc...  4.59 us
    pallas_call x2, Pallas kernels, project(): call(functools.partial(project_kernel, C, bool(extra)), [sds((rows, width...  4.56 us
    pallas_call x1, Pallas kernels, body(): call(functools.partial(pack_kernel, C, qw), [sds((tok, 2 * qw + 8 * HEAD_...  3.36 us
    pallas_call x1, Pallas kernels, body(): call(functools.partial(last_kernel, E, cap), [sds((rows, width), F32), sd...  2.58 us
  transfers between devices with their start and end apart: 31, of which 17 were waited for; matrix products, arithmetic and copies ran while one was open for 1% of the time, Pallas kernels for 8%

profile of v3, /device:TPU:0, one launch (start us, length us, event | category | flops | bytes accessed | tf_op | source)
XLA Modules:
  0.0 125.9 jit_solution(5288290743070626935)
XLA Ops:
  0.0 3.4 %shard_map.100 = (bf16[64,2048]{1,0:T(8,128)(2,1)}, bf16[64,2048]{1,0:T(8,128)(2,1)}, bf16[64,2048]{1,0:T(8,128)(2,1)}, bf16[64,2048]{1,0:T(8,128)(2,1)}, bf16[5...) custom-call(bf16[64,4096]{1,0:T(8,128)(2,1)} %bitcast.21, bf16[64,512]{1,0:T(8,128)(2,1)} %bitcast.22, ...), custom_call_target="tpu_custom_call" | custom-call | bytes 4194304 | tf_op jit(solution)/shard_map/pallas_call | solution.py:319
  3.4 3.0 %collective-permute-start = (bf16[512,512]{1,0:T(8,128)(2,1)}, bf16[512,512]{1,0:T(8,128)(2,1)S(1)}, u32[]{:S(2)}, u32[]{:S(2)}) collective-permute-start(bf16[512,512]{1,0:T(8,128)(2,1)} %get-tuple-element.52), channel_id=1, source_target_pairs={{0,1},{1,0},{2,3},{3,2},{4,5},{5,4},{6,7},{7,6},{8,9},{9,8},{10,11... | collective-permute-start | bytes 1572872 | tf_op jit(solution)/shard_map/ppermute | solution.py:313
  6.4 1.6 %collective-permute-start.1 = (bf16[512,512]{1,0:T(8,128)(2,1)}, bf16[512,512]{1,0:T(8,128)(2,1)S(1)}, u32[]{:S(2)}, u32[]{:S(2)}) collective-permute-start(bf16[512,512]{1,0:T(8,128)(2,1)} %get-tuple-element.51), channel_id=1, source_target_pairs={{0,2},{1,3},{2,0},{3,1},{4,6},{5,7},{6,4},{7,5},{8,10},{9,11},{10,... | collective-permute-start | bytes 1572872 | tf_op jit(solution)/shard_map/ppermute | solution.py:313
  8.0 1.5 %collective-permute-start.3 = (bf16[64,2048]{1,0:T(8,128)(2,1)}, bf16[64,2048]{1,0:T(8,128)(2,1)S(1)}, u32[]{:S(2)}, u32[]{:S(2)}) collective-permute-start(bf16[64,2048]{1,0:T(8,128)(2,1)} %get-tuple-element.48), channel_id=1, source_target_pairs={{0,16},{1,17},{2,18},{3,19},{4,20},{5,21},{6,22},{7,23},{8,24},{9,... | collective-permute-start | bytes 786440 | tf_op jit(solution)/shard_map/ppermute | solution.py:313
  9.8 8.7 %collective-permute-done.refs_7_ = bf16[512,512]{1,0:T(8,128)(2,1)S(1)} collective-permute-done((bf16[512,512]{1,0:T(8,128)(2,1)}, bf16[512,512]{1,0:T(8,128)(2,1)S(1)}, u32[]{:S(2)}, u32[]{:S(2)}) %collective-permute-start) | collective-permute-done | bytes 524320 | tf_op jit(solution)/shard_map/ppermute | solution.py:313
  18.5 1.5 %collective-permute-done.1.refs_8_ = bf16[512,512]{1,0:T(8,128)(2,1)S(1)} collective-permute-done((bf16[512,512]{1,0:T(8,128)(2,1)}, bf16[512,512]{1,0:T(8,128)(2,1)S(1)}, u32[]{:S(2)}, u32[]{:S(2)}) %collective-permute-start.1) | collective-permute-done | bytes 524320 | tf_op jit(solution)/shard_map/ppermute | solution.py:313
  20.3 1.7 %collective-permute-start.9 = (bf16[512,512]{1,0:T(8,128)(2,1)}, bf16[512,512]{1,0:T(8,128)(2,1)S(1)}, u32[]{:S(2)}, u32[]{:S(2)}) collective-permute-start(bf16[512,512]{1,0:T(8,128)(2,1)} %get-tuple-element.52), channel_id=1, source_target_pairs={{0,2},{1,3},{2,0},{3,1},{4,6},{5,7},{6,4},{7,5},{8,10},{9,11},{10,... | collective-permute-start | bytes 1572872 | tf_op jit(solution)/shard_map/ppermute | solution.py:313
  22.1 0.9 copy-done.2
  23.1 2.3 %shard_map.101 = bf16[256,512]{1,0:T(8,128)(2,1)S(1)} custom-call(bf16[64,2048]{1,0:T(8,128)(2,1)S(1)} %copy-done.2, bf16[64,2048]{1,0:T(8,128)(2,1)S(1)} %collective-permute-done.2.refs_1_, bf16[64,2048]{1,0:T(8,128)(2,1)S(1)} %collective-permute-done.3.refs_2_, bf16[64,2048]{1,0:T(8,128)(2,1)S(1)} %collective-permute-done.4.refs_3_), custom_call_target="tpu_custom_call" | custom-call | flops 268435456 | bytes 8388608 | tf_op jit(solution)/shard_map/pallas_call | solution.py:350
  25.4 2.6 %collective-permute-start.10 = (bf16[256,512]{1,0:T(8,128)(2,1)S(1)}, bf16[256,512]{1,0:T(8,128)(2,1)S(1)}, u32[]{:S(2)}, u32[]{:S(2)}) collective-permute-start(bf16[256,512]{1,0:T(8,128)(2,1)S(1)} %shard_map.101), channel_id=1, source_target_pairs={{0,4},{1,5},{2,6},{3,7},{4,0},{5,1},{6,2},{7,3},{8,12},{9,13},{10,... | collective-permute-start | bytes 786440 | tf_op jit(solution)/shard_map/ppermute | solution.py:313
  28.0 2.3 %shard_map.102.refs_0_ = bf16[256,512]{1,0:T(8,128)(2,1)S(1)} custom-call(bf16[64,2048]{1,0:T(8,128)(2,1)S(1)} %copy-done.2, bf16[64,2048]{1,0:T(8,128)(2,1)S(1)} %collective-permute-done.2.refs_1_, bf16[64,2048]{1,0:T(8,128)(2,1)S(1)} %collective-permute-done.3.refs_2_, bf16[64,2048]{1,0:T(8,128)(2,1)S(1)} %collective-permute-done.4.refs_3_), custom_call_target="tpu_custom_call" | custom-call | flops 268435456 | bytes 8388608 | tf_op jit(solution)/shard_map/pallas_call | solution.py:350
  30.3 1.6 %collective-permute-start.6 = (bf16[256,512]{1,0:T(8,128)(2,1)S(1)}, bf16[256,512]{1,0:T(8,128)(2,1)}, u32[]{:S(2)}, u32[]{:S(2)}) collective-permute-start(bf16[256,512]{1,0:T(8,128)(2,1)S(1)} %shard_map.102.refs_0_), channel_id=1, source_target_pairs={{0,16},{1,17},{2,18},{3,19},{4,20},{5,21},{6,22},{7,23},{8,24},{9,... | collective-permute-start | bytes 786440 | tf_op jit(solution)/shard_map/ppermute | solution.py:313
  31.9 5.8 %collective-permute-done.10.refs_0_ = bf16[256,512]{1,0:T(8,128)(2,1)S(1)} collective-permute-done((bf16[256,512]{1,0:T(8,128)(2,1)S(1)}, bf16[256,512]{1,0:T(8,128)(2,1)S(1)}, u32[]{:S(2)}, u32[]{:S(2)}) %collective-permute-start.10) | collective-permute-done | bytes 262176 | tf_op jit(solution)/shard_map/ppermute | solution.py:313
  37.7 0.9 collective-permute-done.9.refs_9_
  38.7 1.4 %collective-permute-start.12 = (bf16[256,512]{1,0:T(8,128)(2,1)S(1)}, bf16[256,512]{1,0:T(8,128)(2,1)}, u32[]{:S(2)}, u32[]{:S(2)}) collective-permute-start(bf16[256,512]{1,0:T(8,128)(2,1)S(1)} %collective-permute-done.10.refs_0_), channel_id=1, source_target_pairs={{0,16},{1,17},{2,18},{3,19},{4,20},{5,21},{6,22},{7,23},{8,24},{9,... | collective-permute-start | bytes 786440 | tf_op jit(solution)/shard_map/ppermute | solution.py:313
  40.1 1.4 %collective-permute-start.14 = (bf16[512,512]{1,0:T(8,128)(2,1)S(1)}, bf16[512,512]{1,0:T(8,128)(2,1)S(1)}, u32[]{:S(2)}, u32[]{:S(2)}) collective-permute-start(bf16[512,512]{1,0:T(8,128)(2,1)S(1)} %collective-permute-done.1.refs_8_), channel_id=1, source_target_pairs={{0,1},{1,0},{2,3},{3,2},{4,5},{5,4},{6,7},{7,6},{8,9},{9,8},{10,11... | collective-permute-start | bytes 1572872 | tf_op jit(solution)/shard_map/ppermute | solution.py:313
  41.5 2.6 %collective-permute-start.15 = (bf16[512,512]{1,0:T(8,128)(2,1)S(1)}, bf16[512,512]{1,0:T(8,128)(2,1)}, u32[]{:S(2)}, u32[]{:S(2)}) collective-permute-start(bf16[512,512]{1,0:T(8,128)(2,1)S(1)} %collective-permute-done.refs_7_), channel_id=1, source_target_pairs={{0,2},{1,3},{2,0},{3,1},{4,6},{5,7},{6,4},{7,5},{8,10},{9,11},{10,... | collective-permute-start | bytes 1572872 | tf_op jit(solution)/shard_map/ppermute | solution.py:313
  44.1 1.0 collective-permute-done.12.refs_2_
  46.4 0.8 copy.11
  47.2 0.8 copy.12
  48.5 2.6 %collective-permute-start.16 = (bf16[256,128]{1,0:T(8,128)(2,1)S(1)}, bf16[256,128]{1,0:T(8,128)(2,1)S(1)}, u32[]{:S(2)}, u32[]{:S(2)}) collective-permute-start(bf16[256,128]{1,0:T(8,128)(2,1)S(1)} %get-tuple-element.62.refs_6_.place_ref), channel_id=1, source_target_pairs={{0,4},{1,5},{2,6},{3,7},{4,0},{5,1},{6,2},{7,3},{8,12},{9,13},{10,... | collective-permute-start | bytes 196616 | tf_op jit(solution)/shard_map/ppermute | solution.py:313
  51.0 1.2 copy-done
  52.3 1.0 copy-done.3
  53.3 0.9 copy-done.5
  54.3 2.2 %shard_map.103 = (f32[256,1024]{1,0:T(8,128)S(1)}, bf16[256,512]{1,0:T(8,128)(2,1)S(1)}) custom-call(bf16[256,512]{1,0:T(8,128)(2,1)S(1)} %shard_map.102.refs_0_, bf16[256,512]{1,0:T(8,128)(2,1)S(1)} %copy-done.5, bf16[256,512]{1,0:T(8,128)(2,1)} %collective-permute-done.6.refs_2_, bf16[256,512]{1,0:T(8,128)(2,1)} %collective-permute-done.7.refs_3_, ...), custom_call_target="tpu_custom_call" | custom-call | flops 805306368 | bytes 4194304 | tf_op jit(solution)/shard_map/pallas_call | solution.py:385
  56.5 2.3 %shard_map.104 = (f32[256,1024]{1,0:T(8,128)S(1)}, bf16[256,512]{1,0:T(8,128)(2,1)S(1)}) custom-call(bf16[256,512]{1,0:T(8,128)(2,1)S(1)} %collective-permute-done.10.refs_0_, bf16[256,512]{1,0:T(8,128)(2,1)} %collective-permute-done.11.refs_1_, bf16[256,512]{1,0:T(8,128)(2,1)} %collective-permute-done.12.refs_2_, ...), custom_call_target="tpu_custom_call" | custom-call | flops 805306368 | bytes 4194304 | tf_op jit(solution)/shard_map/pallas_call | solution.py:385
  58.9 2.6 %shard_map.106 = (f32[256,1024]{1,0:T(8,128)S(1)}, bf16[256,1024]{1,0:T(8,128)(2,1)S(1)}, f32[128,1024]{1,0:T(8,128)S(1)}, bf16[128,1024]{1,0:T(8,128)(2,1)S(1)}) custom-call(f32[256,1024]{1,0:T(8,128)S(1)} %get-tuple-element.53.refs_0_, f32[256,1024]{1,0:T(8,128)S(1)} %get-tuple-element.55.refs_1_, bf16[256,512]{1,0:T(8,128)(2,1)S(1)} %get-tuple-element.56.refs_2_, ...), custom_call_target="tpu_custom_call" | custom-call | flops 671088640 | bytes 6291456 | tf_op jit(solution)/shard_map/pallas_call | solution.py:395
  61.5 1.7 %collective-permute-start.17 = (bf16[128,1024]{1,0:T(8,128)(2,1)S(1)}, bf16[128,1024]{1,0:T(8,128)(2,1)S(1)}, u32[]{:S(2)}, u32[]{:S(2)}) collective-permute-start(bf16[128,1024]{1,0:T(8,128)(2,1)S(1)} %get-tuple-element.66), channel_id=1, source_target_pairs={{0,4},{1,5},{2,6},{3,7},{4,0},{5,1},{6,2},{7,3},{8,12},{9,13},{10,... | collective-permute-start | bytes 786440 | tf_op jit(solution)/shard_map/ppermute | solution.py:313
  63.2 12.9 %collective-permute-done.17.got_ref = bf16[128,1024]{1,0:T(8,128)(2,1)S(1)} collective-permute-done((bf16[128,1024]{1,0:T(8,128)(2,1)S(1)}, bf16[128,1024]{1,0:T(8,128)(2,1)S(1)}, u32[]{:S(2)}, u32[]{:S(2)}) %collective-permute-start.17) | collective-permute-done | bytes 262176 | tf_op jit(solution)/shard_map/ppermute | solution.py:313
  76.1 1.4 %collective-permute-start.18 = (bf16[32,1024]{1,0:T(8,128)(2,1)S(1)}, bf16[32,1024]{1,0:T(8,128)(2,1)S(1)}, u32[]{:S(2)}, u32[]{:S(2)}) collective-permute-start(bf16[32,1024]{1,0:T(8,128)(2,1)S(1)} %get-tuple-element.68), channel_id=1, source_target_pairs={{0,1},{1,0},{2,3},{3,2},{4,5},{5,4},{6,7},{7,6},{8,9},{9,8},{10,11... | collective-permute-start | bytes 196616 | tf_op jit(solution)/shard_map/ppermute | solution.py:313
  77.5 2.1 %collective-permute-start.20 = (bf16[32,1024]{1,0:T(8,128)(2,1)S(1)}, bf16[32,1024]{1,0:T(8,128)(2,1)S(1)}, u32[]{:S(2)}, u32[]{:S(2)}) collective-permute-start(bf16[32,1024]{1,0:T(8,128)(2,1)S(1)} %get-tuple-element.70), channel_id=1, source_target_pairs={{0,3},{1,2},{2,1},{3,0},{4,7},{5,6},{6,5},{7,4},{8,11},{9,10},{10,... | collective-permute-start | bytes 196616 | tf_op jit(solution)/shard_map/ppermute | solution.py:313
  79.7 1.4 %collective-permute-done.18.refs_1_ = bf16[32,1024]{1,0:T(8,128)(2,1)S(1)} collective-permute-done((bf16[32,1024]{1,0:T(8,128)(2,1)S(1)}, bf16[32,1024]{1,0:T(8,128)(2,1)S(1)}, u32[]{:S(2)}, u32[]{:S(2)}) %collective-permute-start.18) | collective-permute-done | bytes 65568 | tf_op jit(solution)/shard_map/ppermute | solution.py:313
  81.8 0.9 collective-permute-done.20.refs_3_
  82.7 1.3 shard_map.108
  84.0 1.7 %collective-permute-done.22.got_ref = bf16[64,3200]{1,0:T(8,128)(2,1)S(1)} collective-permute-done((bf16[64,3200]{1,0:T(8,128)(2,1)S(1)}, bf16[64,3200]{1,0:T(8,128)(2,1)S(1)}, u32[]{:S(2)}, u32[]{:S(2)}) %collective-permute-start.22) | collective-permute-done | bytes 409632 | tf_op jit(solution)/shard_map/ppermute | solution.py:313
  85.8 1.6 %collective-permute-start.23 = (bf16[32,3200]{1,0:T(8,128)(2,1)S(1)}, bf16[32,3200]{1,0:T(8,128)(2,1)S(1)}, u32[]{:S(2)}, u32[]{:S(2)}) collective-permute-start(bf16[32,3200]{1,0:T(8,128)(2,1)S(1)} %get-tuple-element.76), channel_id=1, source_target_pairs={{0,16},{1,17},{2,18},{3,19},{4,20},{5,21},{6,22},{7,23},{8,24},{9,... | collective-permute-start | bytes 614408 | tf_op jit(solution)/shard_map/ppermute | solution.py:313
  87.4 1.9 %collective-permute-start.21 = (bf16[256,1024]{1,0:T(8,128)(2,1)S(1)}, bf16[256,1024]{1,0:T(8,128)(2,1)S(1)}, u32[]{:S(2)}, u32[]{:S(2)}) collective-permute-start(bf16[256,1024]{1,0:T(8,128)(2,1)S(1)} %get-tuple-element.71), channel_id=1, source_target_pairs={{0,4},{1,5},{2,6},{3,7},{4,0},{5,1},{6,2},{7,3},{8,12},{9,13},{10,... | collective-permute-start | bytes 1572872 | tf_op jit(solution)/shard_map/ppermute | solution.py:313
  89.3 3.7 %collective-permute-done.23.got_ref = bf16[32,3200]{1,0:T(8,128)(2,1)S(1)} collective-permute-done((bf16[32,3200]{1,0:T(8,128)(2,1)S(1)}, bf16[32,3200]{1,0:T(8,128)(2,1)S(1)}, u32[]{:S(2)}, u32[]{:S(2)}) %collective-permute-start.23) | collective-permute-done | bytes 204832 | tf_op jit(solution)/shard_map/ppermute | solution.py:313
  93.2 1.6 %collective-permute-start.25 = (bf16[32,1536]{1,0:T(8,128)(2,1)S(1)}, bf16[32,1536]{1,0:T(8,128)(2,1)S(1)}, u32[]{:S(2)}, u32[]{:S(2)}) collective-permute-start(bf16[32,1536]{1,0:T(8,128)(2,1)S(1)} %shard_map.110.refs_0_), channel_id=1, source_target_pairs={{0,16},{1,17},{2,18},{3,19},{4,20},{5,21},{6,22},{7,23},{8,24},{9,... | collective-permute-start | bytes 294920 | tf_op jit(solution)/shard_map/ppermute | solution.py:313
  94.8 3.1 %collective-permute-done.25.refs_2_ = bf16[32,1536]{1,0:T(8,128)(2,1)S(1)} collective-permute-done((bf16[32,1536]{1,0:T(8,128)(2,1)S(1)}, bf16[32,1536]{1,0:T(8,128)(2,1)S(1)}, u32[]{:S(2)}, u32[]{:S(2)}) %collective-permute-start.25) | collective-permute-done | bytes 98336 | tf_op jit(solution)/shard_map/ppermute | solution.py:313
  97.9 1.3 %collective-permute-done.26.refs_3_ = bf16[32,1536]{1,0:T(8,128)(2,1)S(1)} collective-permute-done((bf16[32,1536]{1,0:T(8,128)(2,1)S(1)}, bf16[32,1536]{1,0:T(8,128)(2,1)S(1)}, u32[]{:S(2)}, u32[]{:S(2)}) %collective-permute-start.26) | collective-permute-done | bytes 98336 | tf_op jit(solution)/shard_map/ppermute | solution.py:313
  99.8 1.3 %collective-permute-start.27 = (bf16[32,1024]{1,0:T(8,128)(2,1)S(1)}, bf16[32,1024]{1,0:T(8,128)(2,1)S(1)}, u32[]{:S(2)}, u32[]{:S(2)}) collective-permute-start(bf16[32,1024]{1,0:T(8,128)(2,1)S(1)} %get-tuple-element.78), channel_id=1, source_target_pairs={{0,1},{1,0},{2,3},{3,2},{4,5},{5,4},{6,7},{7,6},{8,9},{9,8},{10,11... | collective-permute-start | bytes 196616 | tf_op jit(solution)/shard_map/ppermute | solution.py:313
  101.2 1.4 %collective-permute-start.28 = (bf16[32,1024]{1,0:T(8,128)(2,1)S(1)}, bf16[32,1024]{1,0:T(8,128)(2,1)S(1)}, u32[]{:S(2)}, u32[]{:S(2)}) collective-permute-start(bf16[32,1024]{1,0:T(8,128)(2,1)S(1)} %get-tuple-element.79), channel_id=1, source_target_pairs={{0,2},{1,3},{2,0},{3,1},{4,6},{5,7},{6,4},{7,5},{8,10},{9,11},{10,... | collective-permute-start | bytes 196616 | tf_op jit(solution)/shard_map/ppermute | solution.py:313
  102.6 0.8 collective-permute-start.29
  104.2 10.6 %collective-permute-done.28.refs_2_ = bf16[32,1024]{1,0:T(8,128)(2,1)S(1)} collective-permute-done((bf16[32,1024]{1,0:T(8,128)(2,1)S(1)}, bf16[32,1024]{1,0:T(8,128)(2,1)S(1)}, u32[]{:S(2)}, u32[]{:S(2)}) %collective-permute-start.28) | collective-permute-done | bytes 65568 | tf_op jit(solution)/shard_map/ppermute | solution.py:313
  114.7 2.0 %collective-permute-done.29.refs_3_ = bf16[32,1024]{1,0:T(8,128)(2,1)S(1)} collective-permute-done((bf16[32,1024]{1,0:T(8,128)(2,1)S(1)}, bf16[32,1024]{1,0:T(8,128)(2,1)S(1)}, u32[]{:S(2)}, u32[]{:S(2)}) %collective-permute-start.29) | collective-permute-done | bytes 65568 | tf_op jit(solution)/shard_map/ppermute | solution.py:313
  116.9 7.9 %collective-permute-done.30.refs_4_ = bf16[64,1024]{1,0:T(8,128)(2,1)S(1)} collective-permute-done((bf16[64,1024]{1,0:T(8,128)(2,1)S(1)}, bf16[64,1024]{1,0:T(8,128)(2,1)S(1)}, u32[]{:S(2)}, u32[]{:S(2)}) %collective-permute-start.30) | collective-permute-done | bytes 131104 | tf_op jit(solution)/shard_map/ppermute | solution.py:313
  124.8 1.1 shard_map.113
  (49 shorter events, 5.1 us)
Async XLA Ops:
  3.4 15.1 %collective-permute-start = (bf16[512,512]{1,0:T(8,128)(2,1)}, bf16[512,512]{1,0:T(8,128)(2,1)S(1)}, u32[]{:S(2)}, u32[]{:S(2)}) collective-permute-start(bf16[512,512]{1,0:T(8,128)(2,1)} %get-tuple-element.52), channel_id=1, source_target_pairs={{0,1},{1,0},{2,3},{3,2},{4,5},{5,4},{6,7},{7,6},{8,9},{9,8},{10,11... | collective-permute-start | bytes 1572872 | tf_op jit(solution)/shard_map/ppermute | solution.py:313
  6.4 13.6 %collective-permute-start.1 = (bf16[512,512]{1,0:T(8,128)(2,1)}, bf16[512,512]{1,0:T(8,128)(2,1)S(1)}, u32[]{:S(2)}, u32[]{:S(2)}) collective-permute-start(bf16[512,512]{1,0:T(8,128)(2,1)} %get-tuple-element.51), channel_id=1, source_target_pairs={{0,2},{1,3},{2,0},{3,1},{4,6},{5,7},{6,4},{7,5},{8,10},{9,11},{10,... | collective-permute-start | bytes 1572872 | tf_op jit(solution)/shard_map/ppermute | solution.py:313
  7.9 14.1 %collective-permute-start.2 = (bf16[64,2048]{1,0:T(8,128)(2,1)}, bf16[64,2048]{1,0:T(8,128)(2,1)S(1)}, u32[]{:S(2)}, u32[]{:S(2)}) collective-permute-start(bf16[64,2048]{1,0:T(8,128)(2,1)} %get-tuple-element.47), channel_id=1, source_target_pairs={{0,8},{1,9},{2,10},{3,11},{4,12},{5,13},{6,14},{7,15},{8,0},{9,1},... | collective-permute-start | bytes 786440 | tf_op jit(solution)/shard_map/ppermute | solution.py:313
  8.0 14.1 %collective-permute-start.3 = (bf16[64,2048]{1,0:T(8,128)(2,1)}, bf16[64,2048]{1,0:T(8,128)(2,1)S(1)}, u32[]{:S(2)}, u32[]{:S(2)}) collective-permute-start(bf16[64,2048]{1,0:T(8,128)(2,1)} %get-tuple-element.48), channel_id=1, source_target_pairs={{0,16},{1,17},{2,18},{3,19},{4,20},{5,21},{6,22},{7,23},{8,24},{9,... | collective-permute-start | bytes 786440 | tf_op jit(solution)/shard_map/ppermute | solution.py:313
  9.5 12.6 %collective-permute-start.4 = (bf16[64,2048]{1,0:T(8,128)(2,1)}, bf16[64,2048]{1,0:T(8,128)(2,1)S(1)}, u32[]{:S(2)}, u32[]{:S(2)}) collective-permute-start(bf16[64,2048]{1,0:T(8,128)(2,1)} %get-tuple-element.49), channel_id=1, source_target_pairs={{0,24},{1,25},{2,26},{3,27},{4,28},{5,29},{6,30},{7,31},{8,16},{9,... | collective-permute-start | bytes 786440 | tf_op jit(solution)/shard_map/ppermute | solution.py:313
  20.0 17.8 %collective-permute-start.8 = (bf16[512,512]{1,0:T(8,128)(2,1)}, bf16[512,512]{1,0:T(8,128)(2,1)S(1)}, u32[]{:S(2)}, u32[]{:S(2)}) collective-permute-start(bf16[512,512]{1,0:T(8,128)(2,1)} %get-tuple-element.51), channel_id=1, source_target_pairs={{0,1},{1,0},{2,3},{3,2},{4,5},{5,4},{6,7},{7,6},{8,9},{9,8},{10,11... | collective-permute-start | bytes 1572872 | tf_op jit(solution)/shard_map/ppermute | solution.py:313
  20.3 18.3 %collective-permute-start.9 = (bf16[512,512]{1,0:T(8,128)(2,1)}, bf16[512,512]{1,0:T(8,128)(2,1)S(1)}, u32[]{:S(2)}, u32[]{:S(2)}) collective-permute-start(bf16[512,512]{1,0:T(8,128)(2,1)} %get-tuple-element.52), channel_id=1, source_target_pairs={{0,2},{1,3},{2,0},{3,1},{4,6},{5,7},{6,4},{7,5},{8,10},{9,11},{10,... | collective-permute-start | bytes 1572872 | tf_op jit(solution)/shard_map/ppermute | solution.py:313
  22.1 1.0 copy-start.2
  25.4 12.4 %collective-permute-start.10 = (bf16[256,512]{1,0:T(8,128)(2,1)S(1)}, bf16[256,512]{1,0:T(8,128)(2,1)S(1)}, u32[]{:S(2)}, u32[]{:S(2)}) collective-permute-start(bf16[256,512]{1,0:T(8,128)(2,1)S(1)} %shard_map.101), channel_id=1, source_target_pairs={{0,4},{1,5},{2,6},{3,7},{4,0},{5,1},{6,2},{7,3},{8,12},{9,13},{10,... | collective-permute-start | bytes 786440 | tf_op jit(solution)/shard_map/ppermute | solution.py:313
  30.3 13.8 %collective-permute-start.6 = (bf16[256,512]{1,0:T(8,128)(2,1)S(1)}, bf16[256,512]{1,0:T(8,128)(2,1)}, u32[]{:S(2)}, u32[]{:S(2)}) collective-permute-start(bf16[256,512]{1,0:T(8,128)(2,1)S(1)} %shard_map.102.refs_0_), channel_id=1, source_target_pairs={{0,16},{1,17},{2,18},{3,19},{4,20},{5,21},{6,22},{7,23},{8,24},{9,... | collective-permute-start | bytes 786440 | tf_op jit(solution)/shard_map/ppermute | solution.py:313
  38.7 6.5 %collective-permute-start.12 = (bf16[256,512]{1,0:T(8,128)(2,1)S(1)}, bf16[256,512]{1,0:T(8,128)(2,1)}, u32[]{:S(2)}, u32[]{:S(2)}) collective-permute-start(bf16[256,512]{1,0:T(8,128)(2,1)S(1)} %collective-permute-done.10.refs_0_), channel_id=1, source_target_pairs={{0,16},{1,17},{2,18},{3,19},{4,20},{5,21},{6,22},{7,23},{8,24},{9,... | collective-permute-start | bytes 786440 | tf_op jit(solution)/shard_map/ppermute | solution.py:313
  40.1 5.0 %collective-permute-start.5 = (bf16[256,512]{1,0:T(8,128)(2,1)S(1)}, bf16[256,512]{1,0:T(8,128)(2,1)S(1)}, u32[]{:S(2)}, u32[]{:S(2)}) collective-permute-start(bf16[256,512]{1,0:T(8,128)(2,1)S(1)} %shard_map.102.refs_0_), channel_id=1, source_target_pairs={{0,8},{1,9},{2,10},{3,11},{4,12},{5,13},{6,14},{7,15},{8,0},{9,1},... | collective-permute-start | bytes 786440 | tf_op jit(solution)/shard_map/ppermute | solution.py:313
  40.1 18.8 %collective-permute-start.14 = (bf16[512,512]{1,0:T(8,128)(2,1)S(1)}, bf16[512,512]{1,0:T(8,128)(2,1)S(1)}, u32[]{:S(2)}, u32[]{:S(2)}) collective-permute-start(bf16[512,512]{1,0:T(8,128)(2,1)S(1)} %collective-permute-done.1.refs_8_), channel_id=1, source_target_pairs={{0,1},{1,0},{2,3},{3,2},{4,5},{5,4},{6,7},{7,6},{8,9},{9,8},{10,11... | collective-permute-start | bytes 1572872 | tf_op jit(solution)/shard_map/ppermute | solution.py:313
  41.5 17.4 %collective-permute-start.15 = (bf16[512,512]{1,0:T(8,128)(2,1)S(1)}, bf16[512,512]{1,0:T(8,128)(2,1)}, u32[]{:S(2)}, u32[]{:S(2)}) collective-permute-start(bf16[512,512]{1,0:T(8,128)(2,1)S(1)} %collective-permute-done.refs_7_), channel_id=1, source_target_pairs={{0,2},{1,3},{2,0},{3,1},{4,6},{5,7},{6,4},{7,5},{8,10},{9,11},{10,... | collective-permute-start | bytes 1572872 | tf_op jit(solution)/shard_map/ppermute | solution.py:313
  44.1 4.3 %collective-permute-start.7 = (bf16[256,512]{1,0:T(8,128)(2,1)}, bf16[256,512]{1,0:T(8,128)(2,1)}, u32[]{:S(2)}, u32[]{:S(2)}) collective-permute-start(bf16[256,512]{1,0:T(8,128)(2,1)} %collective-permute-done.6.refs_2_), channel_id=1, source_target_pairs={{0,8},{1,9},{2,10},{3,11},{4,12},{5,13},{6,14},{7,15},{8,0},{9,1},... | collective-permute-start | bytes 786440 | tf_op jit(solution)/shard_map/ppermute | solution.py:313
  45.2 11.4 %collective-permute-start.11 = (bf16[256,512]{1,0:T(8,128)(2,1)S(1)}, bf16[256,512]{1,0:T(8,128)(2,1)}, u32[]{:S(2)}, u32[]{:S(2)}) collective-permute-start(bf16[256,512]{1,0:T(8,128)(2,1)S(1)} %collective-permute-done.10.refs_0_), channel_id=1, source_target_pairs={{0,8},{1,9},{2,10},{3,11},{4,12},{5,13},{6,14},{7,15},{8,0},{9,1},... | collective-permute-start | bytes 786440 | tf_op jit(solution)/shard_map/ppermute | solution.py:313
  45.2 0.7 copy-start.4
  45.9 10.7 %collective-permute-start.13 = (bf16[256,512]{1,0:T(8,128)(2,1)}, bf16[256,512]{1,0:T(8,128)(2,1)}, u32[]{:S(2)}, u32[]{:S(2)}) collective-permute-start(bf16[256,512]{1,0:T(8,128)(2,1)} %collective-permute-done.12.refs_2_), channel_id=1, source_target_pairs={{0,8},{1,9},{2,10},{3,11},{4,12},{5,13},{6,14},{7,15},{8,0},{9,1},... | collective-permute-start | bytes 786440 | tf_op jit(solution)/shard_map/ppermute | solution.py:313
  48.5 10.4 %collective-permute-start.16 = (bf16[256,128]{1,0:T(8,128)(2,1)S(1)}, bf16[256,128]{1,0:T(8,128)(2,1)S(1)}, u32[]{:S(2)}, u32[]{:S(2)}) collective-permute-start(bf16[256,128]{1,0:T(8,128)(2,1)S(1)} %get-tuple-element.62.refs_6_.place_ref), channel_id=1, source_target_pairs={{0,4},{1,5},{2,6},{3,7},{4,0},{5,1},{6,2},{7,3},{8,12},{9,13},{10,... | collective-permute-start | bytes 196616 | tf_op jit(solution)/shard_map/ppermute | solution.py:313
  51.0 1.2 copy-start
  52.3 1.0 copy-start.3
  53.3 0.9 copy-start.5
  54.3 21.8 %copy-start.6 = (f32[1024]{0:T(1024)S(1)}, f32[1024]{0:T(1024)}, u32[]{:S(2)}) copy-start(f32[1024]{0:T(1024)} %param.15) | copy-start | bytes 12292
  54.3 28.4 %slice-start = ((s8[6291456]{0:T(1024)(128)(4,1)}), s8[4194304]{0:T(1024)(128)(4,1)S(1)}, s32[]{:S(2)}) async-start(s8[6291456]{0:T(1024)(128)(4,1)} %bitcast.12), calls=%async_computation | async-start | bytes 8388608
  56.5 26.2 %slice-start.1 = ((s8[6291456]{0:T(1024)(128)(4,1)}), s8[2097152]{0:T(1024)(128)(4,1)S(1)}, s32[]{:S(2)}) async-start(s8[6291456]{0:T(1024)(128)(4,1)} %bitcast.12), calls=%async_computation.1 | async-start | bytes 4194304
  58.9 40.3 %copy-start.1 = (bf16[1,1536,1024]{2,1,0:T(8,128)(2,1)S(1)}, bf16[1,1536,1024]{2,1,0:T(8,128)(2,1)}, u32[]{:S(2)}) copy-start(bf16[1,1536,1024]{2,1,0:T(8,128)(2,1)} %param.19) | copy-start | bytes 9437188
  61.5 14.5 %collective-permute-start.17 = (bf16[128,1024]{1,0:T(8,128)(2,1)S(1)}, bf16[128,1024]{1,0:T(8,128)(2,1)S(1)}, u32[]{:S(2)}, u32[]{:S(2)}) collective-permute-start(bf16[128,1024]{1,0:T(8,128)(2,1)S(1)} %get-tuple-element.66), channel_id=1, source_target_pairs={{0,4},{1,5},{2,6},{3,7},{4,0},{5,1},{6,2},{7,3},{8,12},{9,13},{10,... | collective-permute-start | bytes 786440 | tf_op jit(solution)/shard_map/ppermute | solution.py:313
  76.1 4.9 %collective-permute-start.18 = (bf16[32,1024]{1,0:T(8,128)(2,1)S(1)}, bf16[32,1024]{1,0:T(8,128)(2,1)S(1)}, u32[]{:S(2)}, u32[]{:S(2)}) collective-permute-start(bf16[32,1024]{1,0:T(8,128)(2,1)S(1)} %get-tuple-element.68), channel_id=1, source_target_pairs={{0,1},{1,0},{2,3},{3,2},{4,5},{5,4},{6,7},{7,6},{8,9},{9,8},{10,11... | collective-permute-start | bytes 196616 | tf_op jit(solution)/shard_map/ppermute | solution.py:313
  77.5 4.3 %collective-permute-start.19 = (bf16[32,1024]{1,0:T(8,128)(2,1)S(1)}, bf16[32,1024]{1,0:T(8,128)(2,1)S(1)}, u32[]{:S(2)}, u32[]{:S(2)}) collective-permute-start(bf16[32,1024]{1,0:T(8,128)(2,1)S(1)} %get-tuple-element.69), channel_id=1, source_target_pairs={{0,2},{1,3},{2,0},{3,1},{4,6},{5,7},{6,4},{7,5},{8,10},{9,11},{10,... | collective-permute-start | bytes 196616 | tf_op jit(solution)/shard_map/ppermute | solution.py:313
  77.5 5.2 %collective-permute-start.20 = (bf16[32,1024]{1,0:T(8,128)(2,1)S(1)}, bf16[32,1024]{1,0:T(8,128)(2,1)S(1)}, u32[]{:S(2)}, u32[]{:S(2)}) collective-permute-start(bf16[32,1024]{1,0:T(8,128)(2,1)S(1)} %get-tuple-element.70), channel_id=1, source_target_pairs={{0,3},{1,2},{2,1},{3,0},{4,7},{5,6},{6,5},{7,4},{8,11},{9,10},{10,... | collective-permute-start | bytes 196616 | tf_op jit(solution)/shard_map/ppermute | solution.py:313
  84.0 1.8 %collective-permute-start.22 = (bf16[64,3200]{1,0:T(8,128)(2,1)S(1)}, bf16[64,3200]{1,0:T(8,128)(2,1)S(1)}, u32[]{:S(2)}, u32[]{:S(2)}) collective-permute-start(bf16[64,3200]{1,0:T(8,128)(2,1)S(1)} %get-tuple-element.74), channel_id=1, source_target_pairs={{0,8},{1,9},{2,10},{3,11},{4,12},{5,13},{6,14},{7,15},{8,0},{9,1},... | collective-permute-start | bytes 1228808 | tf_op jit(solution)/shard_map/ppermute | solution.py:313
  85.8 7.2 %collective-permute-start.23 = (bf16[32,3200]{1,0:T(8,128)(2,1)S(1)}, bf16[32,3200]{1,0:T(8,128)(2,1)S(1)}, u32[]{:S(2)}, u32[]{:S(2)}) collective-permute-start(bf16[32,3200]{1,0:T(8,128)(2,1)S(1)} %get-tuple-element.76), channel_id=1, source_target_pairs={{0,16},{1,17},{2,18},{3,19},{4,20},{5,21},{6,22},{7,23},{8,24},{9,... | collective-permute-start | bytes 614408 | tf_op jit(solution)/shard_map/ppermute | solution.py:313
  87.4 29.4 %collective-permute-start.21 = (bf16[256,1024]{1,0:T(8,128)(2,1)S(1)}, bf16[256,1024]{1,0:T(8,128)(2,1)S(1)}, u32[]{:S(2)}, u32[]{:S(2)}) collective-permute-start(bf16[256,1024]{1,0:T(8,128)(2,1)S(1)} %get-tuple-element.71), channel_id=1, source_target_pairs={{0,4},{1,5},{2,6},{3,7},{4,0},{5,1},{6,2},{7,3},{8,12},{9,13},{10,... | collective-permute-start | bytes 1572872 | tf_op jit(solution)/shard_map/ppermute | solution.py:313
  93.2 4.7 %collective-permute-start.25 = (bf16[32,1536]{1,0:T(8,128)(2,1)S(1)}, bf16[32,1536]{1,0:T(8,128)(2,1)S(1)}, u32[]{:S(2)}, u32[]{:S(2)}) collective-permute-start(bf16[32,1536]{1,0:T(8,128)(2,1)S(1)} %shard_map.110.refs_0_), channel_id=1, source_target_pairs={{0,16},{1,17},{2,18},{3,19},{4,20},{5,21},{6,22},{7,23},{8,24},{9,... | collective-permute-start | bytes 294920 | tf_op jit(solution)/shard_map/ppermute | solution.py:313
  94.8 3.1 %collective-permute-start.24 = (bf16[32,1536]{1,0:T(8,128)(2,1)S(1)}, bf16[32,1536]{1,0:T(8,128)(2,1)S(1)}, u32[]{:S(2)}, u32[]{:S(2)}) collective-permute-start(bf16[32,1536]{1,0:T(8,128)(2,1)S(1)} %shard_map.110.refs_0_), channel_id=1, source_target_pairs={{0,8},{1,9},{2,10},{3,11},{4,12},{5,13},{6,14},{7,15},{8,0},{9,1},... | collective-permute-start | bytes 294920 | tf_op jit(solution)/shard_map/ppermute | solution.py:313
  97.9 1.3 %collective-permute-start.26 = (bf16[32,1536]{1,0:T(8,128)(2,1)S(1)}, bf16[32,1536]{1,0:T(8,128)(2,1)S(1)}, u32[]{:S(2)}, u32[]{:S(2)}) collective-permute-start(bf16[32,1536]{1,0:T(8,128)(2,1)S(1)} %collective-permute-done.25.refs_2_), channel_id=1, source_target_pairs={{0,8},{1,9},{2,10},{3,11},{4,12},{5,13},{6,14},{7,15},{8,0},{9,1},... | collective-permute-start | bytes 294920 | tf_op jit(solution)/shard_map/ppermute | solution.py:313
  99.8 4.3 %collective-permute-start.27 = (bf16[32,1024]{1,0:T(8,128)(2,1)S(1)}, bf16[32,1024]{1,0:T(8,128)(2,1)S(1)}, u32[]{:S(2)}, u32[]{:S(2)}) collective-permute-start(bf16[32,1024]{1,0:T(8,128)(2,1)S(1)} %get-tuple-element.78), channel_id=1, source_target_pairs={{0,1},{1,0},{2,3},{3,2},{4,5},{5,4},{6,7},{7,6},{8,9},{9,8},{10,11... | collective-permute-start | bytes 196616 | tf_op jit(solution)/shard_map/ppermute | solution.py:313
  101.2 13.6 %collective-permute-start.28 = (bf16[32,1024]{1,0:T(8,128)(2,1)S(1)}, bf16[32,1024]{1,0:T(8,128)(2,1)S(1)}, u32[]{:S(2)}, u32[]{:S(2)}) collective-permute-start(bf16[32,1024]{1,0:T(8,128)(2,1)S(1)} %get-tuple-element.79), channel_id=1, source_target_pairs={{0,2},{1,3},{2,0},{3,1},{4,6},{5,7},{6,4},{7,5},{8,10},{9,11},{10,... | collective-permute-start | bytes 196616 | tf_op jit(solution)/shard_map/ppermute | solution.py:313
  102.6 14.1 %collective-permute-start.29 = (bf16[32,1024]{1,0:T(8,128)(2,1)S(1)}, bf16[32,1024]{1,0:T(8,128)(2,1)S(1)}, u32[]{:S(2)}, u32[]{:S(2)}) collective-permute-start(bf16[32,1024]{1,0:T(8,128)(2,1)S(1)} %get-tuple-element.80), channel_id=1, source_target_pairs={{0,3},{1,2},{2,1},{3,0},{4,7},{5,6},{6,5},{7,4},{8,11},{9,10},{10,... | collective-permute-start | bytes 196616 | tf_op jit(solution)/shard_map/ppermute | solution.py:313
  116.8 8.0 %collective-permute-start.30 = (bf16[64,1024]{1,0:T(8,128)(2,1)S(1)}, bf16[64,1024]{1,0:T(8,128)(2,1)S(1)}, u32[]{:S(2)}, u32[]{:S(2)}) collective-permute-start(bf16[64,1024]{1,0:T(8,128)(2,1)S(1)} %shard_map.112), channel_id=1, source_target_pairs={{0,4},{1,5},{2,6},{3,7},{4,0},{5,1},{6,2},{7,3},{8,12},{9,13},{10,... | collective-permute-start | bytes 393224 | tf_op jit(solution)/shard_map/ppermute | solution.py:313

commit v4 on v3

--- a/solution.py
+++ b/solution.py
@@ -17,6 +17,7 @@
 F32 = jnp.float32
 VMEM = pl.BlockSpec(memory_space=pltpu.VMEM)
 HBM = pl.BlockSpec(memory_space=pltpu.HBM)
+ANY = pl.BlockSpec(memory_space=pl.ANY)
 
 
 def call(kernel, out_shape, n_in, scratch=(), cost=(0, 0), limit=32, **kw):
@@ -56,8 +57,8 @@
     return pl.multiple_of(x, n)
 
 
-def pack_kernel(C, qw, q_ref, new_ref, past_ref, w_ref, *refs):
-    outs, halves, sems = refs[:C], refs[C:-1], refs[-1]
+def pack_kernel(C, qw, q_ref, new_ref, past_ref, w_ref, res_ref, *refs):
+    outs, halves, res_out, sems = refs[:C], refs[C : C + 2], refs[C + 2], refs[C + 3]
     c = lax.axis_index("ctx")
     _, lo = own_hi_lo()
     copies = []
@@ -66,6 +67,10 @@
         copies.append(pltpu.make_async_copy(src, dst, sems.at[len(copies)]))
         copies[-1].start()
 
+    half = halves[0].shape[1]
+    kv = new_ref.shape[1]
+    for j in (1, 0):
+        copy(w_ref.at[:, j * half : (j + 1) * half], halves[j])
     for s in reversed(range(C)):
         target = jnp.bitwise_xor(c, s)
         out = outs[s]
@@ -73,16 +78,9 @@
             shard = lax.div(target, PAIR) * 2 * PAIR + lax.rem(target, PAIR)
             shard = shard + PAIR * jnp.bitwise_xor(lo, t)
             copy(q_ref.at[:, pl.ds(aligned(shard * qw, 128), qw)], out.at[:, t * qw : (t + 1) * qw])
-            kv = lax.div(shard * (qw // HEAD_SIZE), GROUP_EXTENT)
-            at = 2 * qw + t * 4 * HEAD_SIZE
-            for ref in (new_ref, past_ref):
-                for part in (0, KEY_VALUE_HEADS):
-                    offset = (part + kv) * HEAD_SIZE
-                    copy(ref.at[:, pl.ds(aligned(offset, 128), 128)], out.at[:, at : at + 128])
-                    at += 128
-    half = halves[0].shape[1]
-    for j in range(2):
-        copy(w_ref.at[:, j * half : (j + 1) * half], halves[j])
+        copy(new_ref, out.at[:, 2 * qw : 2 * qw + kv])
+        copy(past_ref, out.at[:, 2 * qw + kv :])
+    copy(res_ref, res_out)
     for c in copies:
         c.wait()
 
@@ -93,13 +91,18 @@
     tok, qw = msgs[0].shape[0], out.shape[1]
     rows = C * tok
     q_s = refs[C + 2]
+    _, lo = own_hi_lo()
+    shard = lax.div(c, PAIR) * 2 * PAIR + lax.rem(c, PAIR) + PAIR * jnp.bitwise_xor(lo, t)
+    head = lax.div(shard * (qw // HEAD_SIZE), GROUP_EXTENT)
     for s in range(C):
         msg = msgs[s]
         at = aligned(jnp.bitwise_xor(c, s) * tok, tok)
-        first = 2 * qw + t * 4 * HEAD_SIZE
         q_s[pl.ds(at, tok), :] = msg[:, t * qw : (t + 1) * qw]
-        kv_s[pl.ds(rows + at, tok), :] = msg[:, first : first + 2 * HEAD_SIZE]
-        kv_s[pl.ds(at, tok), :] = msg[:, first + 2 * HEAD_SIZE : first + 4 * HEAD_SIZE]
+        for i, to in ((0, rows + at), (1, at)):
+            for part in range(2):
+                first = 2 * qw + (i * 2 + part) * KEY_VALUE_HEADS * HEAD_SIZE
+                cols = pl.ds(aligned(first + head * HEAD_SIZE, 128), HEAD_SIZE)
+                kv_s[pl.ds(to, tok), part * HEAD_SIZE : (part + 1) * HEAD_SIZE] = msg[:, cols]
     block = 128
     for b in range(rows // block):
         seen = rows + (b + 1) * block
@@ -118,84 +121,103 @@
             out[at, h * HEAD_SIZE : (h + 1) * HEAD_SIZE] = (numerator / total).astype(BF16)
 
 
-def route_kernel(E, cap, routes_ref, gates_ref, place_ref, gate_ref):
+def route_kernel(E, cap, routes_ref, gates_ref, place_ref, gate_ref, line_s, gate_s):
     e = lax.axis_index("exp")
-    rows = routes_ref.shape[0]
-    routes = routes_ref[...]
-    resident = routes < E
-    target = jnp.sum(jnp.where(resident, routes, 0), axis=1, keepdims=True)
-    has = jnp.sum(resident.astype(jnp.int32), axis=1, keepdims=True) > 0
-    gate = jnp.sum(jnp.where(resident, gates_ref[...], 0.0), axis=1, keepdims=True)
-    gate_ref[...] = jnp.broadcast_to(gate, gate_ref.shape)
-    lanes = lax.broadcasted_iota(jnp.int32, (rows, 128), 1)
-    one_hot = jnp.where((target == lanes) & has, 1.0, 0.0)
-    earlier = (
-        lax.broadcasted_iota(jnp.int32, (rows, rows), 1)
-        < lax.broadcasted_iota(jnp.int32, (rows, rows), 0)
-    ).astype(F32).astype(BF16)
-    rank = jnp.sum(dot(earlier, one_hot.astype(BF16)) * one_hot, axis=1, keepdims=True)
+    blocks, _, tok = routes_ref.shape
+    rows = blocks * tok
+    for i in range(blocks):
+        routes = routes_ref[i]
+        resident = routes < E
+        target = jnp.sum(jnp.where(resident, routes + 1, 0), axis=0, keepdims=True) - 1
+        gate = jnp.sum(jnp.where(resident, gates_ref[i], 0.0), axis=0, keepdims=True)
+        line_s[:, i * tok : (i + 1) * tok] = jnp.broadcast_to(target, (8, tok))
+        gate_s[:, i * tok : (i + 1) * tok] = jnp.broadcast_to(gate, (128, tok))
+    target = line_s[:1, :]
+    gate_ref[...] = gate_s[...].T
+    has = target >= 0
+    experts = lax.broadcasted_iota(jnp.int32, (E, rows), 0)
+    one_hot = jnp.where(target == experts, 1.0, 0.0)
+    earlier = jnp.where(
+        lax.broadcasted_iota(jnp.int32, (rows, rows), 0)
+        < lax.broadcasted_iota(jnp.int32, (rows, rows), 1),
+        1.0,
+        0.0,
+    ).astype(BF16)
+    rank = jnp.sum(dot(one_hot.astype(BF16), earlier) * one_hot, axis=0, keepdims=True)
     slot = jnp.bitwise_xor(target, e) * cap + rank.astype(jnp.int32)
     slot = jnp.where(has, slot, -1)
-    places = lax.broadcasted_iota(jnp.int32, (rows, E * cap), 1)
+    places = lax.broadcasted_iota(jnp.int32, (E * cap, rows), 0)
     place_ref[...] = jnp.where(slot == places, 1.0, 0.0).astype(BF16)
 
 
 def project_kernel(C, with_residual, *refs):
-    atts, ws, acc, last, stacked = refs[:C], refs[C : C + 2 * (C - 1)], refs[-3], refs[-2], refs[-1]
+    own_w, refs = refs[:2], refs[2:]
+    if with_residual:
+        res, refs = refs[0], refs[1:]
+    atts, ws, (acc, last, stacked, w_s, res_s, sems) = refs[:C], refs[C : 3 * C - 4], refs[3 * C - 4 :]
     hi, _ = own_hi_lo()
+    copies = [pltpu.make_async_copy(own_w[j], w_s.at[j], sems.at[j]) for j in range(2)]
+    if with_residual:
+        copies.append(pltpu.make_async_copy(res, res_s, sems.at[2]))
+    for c in copies:
+        c.start()
     turn = jnp.bitwise_xor(lax.axis_index("ctx"), hi)
     for s in range(C):
         stacked[jnp.bitwise_xor(turn, s)] = atts[s][...]
+    last[...] = stacked[C - 1]
     half = acc.shape[1] // 2
     for j in range(2):
         at = slice(j * half, (j + 1) * half)
-        total = refs[-4][:, at].astype(F32) if with_residual else None
-        for d in range(C - 1):
-            w = ws[2 * d + j]
-            term = dot(stacked[d], w[...] if w.shape[1] == half else w[:, at])
+        total = None
+        for d in range(1, C - 1):
+            term = dot(stacked[d], ws[2 * (d - 1) + j][...])
             total = term if total is None else total + term
+        if j == 0:
+            for c in copies:
+                c.wait()
+        total = total + dot(stacked[0], w_s[j])
+        if with_residual:
+            total = total + res_s[:, at].astype(F32)
         acc[:, at] = total
-    last[...] = stacked[C - 1]
-
-
-def last_kernel(E, cap, *refs):
-    accs, lasts, ws, places, (own_ref, full_ref, keep_ref, send_ref) = (
+
+
+def last_kernel(E, cap, j, *refs):
+    accs, lasts, w_ref, places, (own_ref, full_ref, keep_ref, send_ref) = (
         refs[:2],
         refs[2:4],
-        refs[4:6],
-        refs[6:8],
-        refs[8:],
+        refs[4],
+        refs[5:7],
+        refs[7:],
     )
-    half = ws[0].shape[1]
-    for j in range(2):
-        cols = slice(j * half, (j + 1) * half)
-        for t in range(2):
-            total = accs[t][:, cols] + dot(lasts[t][...], ws[j][...])
-            rounded = total.astype(BF16)
-            if t == 0:
-                own_ref[:, cols] = total
-            else:
-                full_ref[:, cols] = rounded
-            picked = lax.dot_general(
-                places[t][...], rounded, (((0,), (0,)), ((), ())), preferred_element_type=F32
-            )
-            for d in range(E // 2):
-                near, far = spread(d) ^ (PAIR * t), spread(d) ^ PAIR ^ (PAIR * t)
-                at = (2 * d + t) * cap
-                keep_ref[at : at + cap, cols] = picked[near * cap : (near + 1) * cap]
-                at = (2 * d + 1 - t) * cap
-                send_ref[at : at + cap, cols] = picked[far * cap : (far + 1) * cap].astype(BF16)
-
-
-def outgoing_kernel(keep_ref, got_ref, gain_ref, *outs):
-    scaled = ((keep_ref[...] + got_ref[...].astype(F32)) * gain_ref[...]).astype(BF16)
+    half = w_ref.shape[1]
+    cols = slice(j * half, (j + 1) * half)
+    for t in (1, 0):
+        total = accs[t][:, cols] + dot(lasts[t][...], w_ref[...])
+        rounded = total.astype(BF16)
+        if t == 0:
+            own_ref[...] = total
+        else:
+            full_ref[...] = rounded
+        picked = dot(places[t][...], rounded)
+        for d in range(E // 2):
+            near, far = spread(d) ^ (PAIR * t), spread(d) ^ PAIR ^ (PAIR * t)
+            at = (2 * d + t) * cap
+            keep_ref[at : at + cap, :] = picked[near * cap : (near + 1) * cap]
+            at = (2 * d + 1 - t) * cap
+            send_ref[at : at + cap, :] = picked[far * cap : (far + 1) * cap].astype(BF16)
+
+
+def outgoing_kernel(j, keep_ref, got_ref, gain_ref, *outs):
+    half = keep_ref.shape[1]
+    gain = gain_ref[:, j * half : (j + 1) * half]
+    scaled = ((keep_ref[...] + got_ref[...].astype(F32)) * gain).astype(BF16)
     count = outs[0].shape[0]
     for d, out in enumerate(outs):
         out[...] = scaled[d * count : (d + 1) * count]
 
 
 def gate_up_kernel(C, E, cap, order, *refs):
-    xs, gain_ref, w_ref, keep_ref, send_ref, x_s, part_s = refs[: E // 2], *refs[E // 2 :]
+    xs, gain_ref, w_ref, keep_ref, send_ref, x_s, part_s = refs[:E], *refs[E:]
     c = lax.axis_index("ctx")
     e = lax.axis_index("exp")
     own_rows = E * cap // C
@@ -203,7 +225,10 @@
     for d in range(E // 2):
         for t in range(2):
             at = aligned(jnp.bitwise_xor(e, spread(d) ^ (PAIR * t)) * cap, cap)
-            x_s[pl.ds(at, cap), :] = xs[d][t * cap : (t + 1) * cap, :]
+            for j in range(2):
+                half = xs[d].shape[1]
+                cols = slice(j * half, (j + 1) * half)
+                x_s[pl.ds(at, cap), cols] = xs[j * (E // 2) + d][t * cap : (t + 1) * cap, :]
     plain = x_s[...].astype(F32) / gain_ref[...]
     square = jnp.sum(plain * plain, axis=1, keepdims=True)
     lane = lax.broadcasted_iota(jnp.int32, (E * cap, 128), 1)
@@ -272,16 +297,21 @@
         refs[-1][d * cap : (d + 1) * cap, :] = x[cap:, :]
 
 
-def combine_kernel(E, cap, own_ref, got_ref, place_ref, gate_ref, *refs):
+def combine_kernel(E, cap, own0, own1, got0, got1, place_ref, gate_ref, *refs):
     xs, far, out, x_s = refs[: E // 2], refs[E // 2], refs[E // 2 + 1], refs[E // 2 + 2]
     for d in range(E // 2):
         at = spread(d) * cap
         x_s[at : at + cap, :] = xs[d][:cap, :]
         at = (spread(d) ^ PAIR) * cap
         x_s[at : at + cap, :] = far[d * cap : (d + 1) * cap, :]
-    collected = dot(place_ref[...], x_s[...])
-    mixed = own_ref[...] + got_ref[...].astype(F32)
-    out[...] = (mixed + gate_ref[:, :1] * collected).astype(BF16)
+    half = own0.shape[1]
+    for j, (own, got) in enumerate(((own0, got0), (own1, got1))):
+        cols = slice(j * half, (j + 1) * half)
+        collected = lax.dot_general(
+            place_ref[...], x_s[:, cols], (((0,), (0,)), ((), ())), preferred_element_type=F32
+        )
+        mixed = own[...] + got[...].astype(F32)
+        out[:, cols] = (mixed + gate_ref[:, :1] * collected).astype(BF16)
 
 
 def body(
@@ -316,12 +346,15 @@
         return lax.optimization_barrier((x, *others))[0]
 
     half = width // 2
-    *msgs, half_a, half_b = call(
+    kv = new_keys_values.shape[3]
+    *msgs, half_a, half_b, res = call(
         functools.partial(pack_kernel, C, qw),
-        [sds((tok, 2 * qw + 8 * HEAD_SIZE), BF16)] * C + [sds((qw, half), BF16)] * 2,
-        4,
-        scratch=[pltpu.SemaphoreType.DMA((10 * C + 2,))],
-        in_specs=[HBM] * 4,
+        [sds((tok, 2 * qw + 2 * kv), BF16)] * C
+        + [sds((qw, half), BF16)] * 2
+        + [sds((rows, width), BF16)],
+        5,
+        scratch=[pltpu.SemaphoreType.DMA((4 * C + 3,))],
+        in_specs=[HBM] * 5,
         cost=(0, 4 * 2**20),
         limit=57,
     )(
@@ -329,13 +362,24 @@
         new_keys_values.reshape(tok, new_keys_values.shape[3]),
         cached_keys_values.reshape(tok, cached_keys_values.shape[3]),
         out_weight,
+        residual.reshape(rows, width),
     )
     got = [msgs[0]] + [permute(msgs[s], ctx=s) for s in range(1, C)]
-    shards = {0: [out_weight, out_weight], 1: [None, permute(half_b, exp=1)]}
+    shards = {0: [half_a, half_b], 1: [None, permute(half_b, exp=1)]}
     for d in range(2, C, 2):
         shards[d] = [permute(half_a, exp=spread(d)), None]
     step = [shards[1][1]] + [shards[d][0] for d in range(2, C, 2)]
-    got[0] = after(got[0], *step)
+    tokens_last = lambda x: jnp.transpose(x.reshape(C, tok, x.shape[3]), (0, 2, 1))
+    place, gate = call(
+        functools.partial(route_kernel, E, cap),
+        [sds((slots, rows), BF16), sds((rows, 128), F32)],
+        2,
+        scratch=[pltpu.VMEM((8, rows), jnp.int32), pltpu.VMEM((128, rows), F32)],
+        cost=(0, 2**20),
+        limit=16,
+    )(tokens_last(after(routes, msgs[0])), tokens_last(after(gates, msgs[0])))
+    other_place = permute(place, exp=PAIR)
+    got[1] = after(got[1], other_place, *step)
     shards[1][0] = permute(after(half_a, *step), exp=1)
     for d in range(2, C, 2):
         shards[d][1] = permute(after(half_b, *step), exp=spread(d))
@@ -358,7 +402,7 @@
 
     other = attend(1, got)
     theirs = permute(other, exp=PAIR)
-    mine = attend(0, [after(got[0], other)] + got[1:])
+    mine = attend(0, [got[0], after(got[1], other)] + got[2:])
 
     def gather(x, before):
         atts = {0: x, 1: permute(x, ctx=1)}
@@ -367,50 +411,55 @@
             atts[s + 1] = permute(after(atts[s], *before), ctx=1)
         return [atts[s] for s in range(C)]
 
-    mine_all = gather(mine, [])
-    theirs_all = gather(after(theirs, *step), [])
-    place, gate = call(
-        functools.partial(route_kernel, E, cap),
-        [sds((rows, slots), BF16), sds((rows, 128), F32)],
-        2,
-        cost=(0, 2**20),
-        limit=16,
-    )(
-        after(routes, mine).reshape(rows, routes.shape[3]),
-        after(gates, mine).reshape(rows, gates.shape[3]),
-    )
-    other_place = permute(place, exp=PAIR)
+    mine_all = gather(after(mine, *step), [])
+    theirs_all = gather(after(theirs, mine), [])
 
     def project(atts, *extra):
+        operands = [*shards[0], *extra, *atts]
+        operands += [w for d in range(1, C - 1) for w in shards[d]]
         return call(
             functools.partial(project_kernel, C, bool(extra)),
             [sds((rows, width), F32), sds((rows, qw), BF16)],
-            C + 2 * (C - 1) + len(extra),
-            scratch=[pltpu.VMEM((C, rows, qw), BF16)],
+            len(operands),
+            scratch=[
+                pltpu.VMEM((C, rows, qw), BF16),
+                pltpu.VMEM((2, qw, half), BF16),
+                pltpu.VMEM((rows, width), BF16),
+                pltpu.SemaphoreType.DMA((3,)),
+            ],
+            in_specs=[ANY] * (2 + len(extra)) + [VMEM] * (len(operands) - 2 - len(extra)),
             cost=(2 * rows * qw * width * (C - 1), 4 * 2**20),
-        )(*atts, *[w for d in range(C - 1) for w in shards[d]], *extra)
-
-    acc, last = project(mine_all, residual.reshape(rows, width))
+        )(*operands)
+
+    acc, last = project(mine_all, res)
     acc_far, last_far = project(theirs_all)
-    own, full, keep, send = call(
-        functools.partial(last_kernel, E, cap),
-        [
-            sds((rows, width), F32),
-            sds((rows, width), BF16),
-            sds((slots, width), F32),
-            sds((slots, width), BF16),
-        ],
-        8,
-        cost=(4 * rows * (qw + slots) * width, 6 * 2**20),
-    )(acc, acc_far, last, last_far, *shards[C - 1], place, other_place)
     gain = norm_gain.reshape(1, width)
-    outgoing = call(
-        outgoing_kernel,
-        [sds((2 * cap, width), BF16)] * (E // 2),
-        3,
-        cost=(0, 2**20),
-    )(keep, permute(send, exp=PAIR), gain)
-    incoming = [outgoing[0]] + [permute(outgoing[d], exp=spread(d)) for d in range(1, E // 2)]
+    own, full, outgoing, incoming = [], [], [], []
+    for j in range(2):
+        mine_j, full_j, keep, send = call(
+            functools.partial(last_kernel, E, cap, j),
+            [
+                sds((rows, half), F32),
+                sds((rows, half), BF16),
+                sds((slots, half), F32),
+                sds((slots, half), BF16),
+            ],
+            7,
+            cost=(4 * rows * (qw + slots) * half, 3 * 2**20),
+        )(acc, acc_far, last, last_far, shards[C - 1][j], place, other_place)
+        own.append(mine_j)
+        full.append(full_j)
+        rows_out = call(
+            functools.partial(outgoing_kernel, j),
+            [sds((2 * cap, half), BF16)] * (E // 2),
+            3,
+            cost=(0, 2**20),
+        )(keep, after(permute(send, exp=PAIR), *incoming), gain)
+        came = {0: rows_out[0]}
+        for d in reversed(range(1, E // 2)):
+            came[d] = permute(rows_out[d], exp=spread(d))
+        incoming += [came[d] for d in range(E // 2)]
+    arrived = [permute(after(full[0], incoming[E // 2 + 1]), exp=PAIR)]
 
     order = [0]
     bit = C // 2
@@ -420,11 +469,11 @@
     keep, send = call(
         functools.partial(gate_up_kernel, C, E, cap, order),
         [sds((slots // 2, wide + 128), F32), sds((slots // 2, wide + 128), BF16)],
-        E // 2 + 2,
+        E + 2,
         scratch=[pltpu.VMEM((slots, width), BF16), pltpu.VMEM((slots, wide + 128), F32)],
         cost=(2 * slots * width * wide, 2 * width * wide),
     )(*incoming, gain, w_gate_up.reshape(width, wide))
-    arrived = permute(after(full, *incoming), exp=PAIR)
+    arrived.append(permute(after(full[1], keep), exp=PAIR))
     bit = 1
     while 2 * bit < C:
         count = keep.shape[0] // 2
@@ -440,7 +489,7 @@
         sds((own_rows, hidden), BF16),
         2,
         cost=(0, 2**20),
-    )(keep, permute(send, ctx=bit))
+    )(after(keep, arrived[0]), permute(send, ctx=bit))
     acts = {0: activated}
     while bit:
         for r in list(acts):
@@ -452,19 +501,19 @@
         C + 1,
         scratch=[pltpu.VMEM((slots, hidden), BF16), pltpu.VMEM((slots, width), BF16)],
         cost=(2 * slots * width * hidden, 2 * width * hidden),
-    )(*[acts[s] for s in range(C)], w_down.reshape(hidden, width))
+    )(after(acts[0], arrived[1]), *[acts[s] for s in range(1, C)], w_down.reshape(hidden, width))
     returned = [expert_out[0]]
-    returned += [permute(expert_out[d], exp=spread(d)) for d in range(1, E // 2)]
+    returned += [permute(expert_out[d], exp=spread(d)) for d in reversed(range(1, E // 2))][::-1]
     far = call(
         functools.partial(forward_kernel, cap), sds((slots // 2, width), BF16), E // 2, cost=(0, 2**19)
     )(*returned)
     result = call(
         functools.partial(combine_kernel, E, cap),
         sds((rows, width), BF16),
-        5 + E // 2,
+        7 + E // 2,
         scratch=[pltpu.VMEM((slots, width), BF16)],
         cost=(0, 2 * 2**20),
-    )(own, arrived, place, gate, *returned, permute(far, exp=PAIR))
+    )(*own, *arrived, place, gate, *returned, permute(far, exp=PAIR))
     return result.reshape(C, 1, tok, width)
 
 

time: 126 us -> 130 us (1.032)
  starting transfers between devices: 35.2 us -> 48.4 us
  waiting for transfers between devices: 65 us -> 61.2 us
  Pallas kernels: 18.9 us -> 15.7 us
  local copies, waits for them, and re-layouts: 6.5 us -> 4.49 us
    ppermute x31 -> x36, starting transfers between devices: 35.2 us -> 48.4 us  [permute(): return lax.ppermute(x, ('ctx', 'exp'), pairs)]
    ppermute x31 -> x36, waiting for transfers between devices: 65 us -> 61.2 us  [permute(): return lax.ppermute(x, ('ctx', 'exp'), pairs)]
    pallas_call x2, Pallas kernels: 4.56 us -> 2.46 us  [project(): call(functools.partial(project_kernel, C, bool(extra)), [sds((rows, width...]
    optimization_barrier x2 -> x0, local copies, waits for them, and re-layouts: 1.61 us -> none  [after(): return lax.optimization_barrier((x, *others))[0]]
    pallas_call x4 -> x6, Pallas kernels: 6.47 us -> 5.26 us  [the longest x1 3.41 us: body(): call(functools.partial(pack_kernel, C, qw), [sds((tok, 2 * qw + 2 * kv),...]
    unnamed x18 -> x20, local copies, waits for them, and re-layouts: 4.89 us -> 4.49 us
  transfers between devices with their start and end apart: 31 -> 36, of which waited for: 17 -> 21; matrix products, arithmetic and copies ran while one was open for 1% -> 0% of each run, Pallas kernels for 8% -> 7%
where the time goes in v4:
time: 130 us
  waiting for transfers between devices  61.2 us (47%)
  starting transfers between devices  48.4 us (37%)
  Pallas kernels  15.7 us (12%)
  local copies, waits for them, and re-layouts  4.49 us (3%)
    ppermute x36, waiting for transfers between devices, permute(): return lax.ppermute(x, ('ctx', 'exp'), pairs)  61.2 us
    ppermute x36, starting transfers between devices, permute(): return lax.ppermute(x, ('ctx', 'exp'), pairs)  48.4 us
    pallas_call x2, Pallas kernels, attend(): call(functools.partial(attend_kernel, C, t), sds((rows, qw), BF16), C, sc...  4.65 us
    unnamed x20, local copies, waits for them, and re-layouts  4.49 us
    pallas_call x1, Pallas kernels, body(): call(functools.partial(pack_kernel, C, qw), [sds((tok, 2 * qw + 2 * kv),...  3.41 us
  transfers between devices with their start and end apart: 36, of which 21 were waited for; matrix products, arithmetic and copies ran while one was open for 0% of the time, Pallas kernels for 7%

profile of v4, /device:TPU:0, one launch (start us, length us, event | category | flops | bytes accessed | tf_op | source)
XLA Modules:
  0.0 130.0 jit_solution(4289347222217843394)
XLA Ops:
  0.0 3.4 %shard_map.100 = (bf16[64,2048]{1,0:T(8,128)(2,1)}, bf16[64,2048]{1,0:T(8,128)(2,1)}, bf16[64,2048]{1,0:T(8,128)(2,1)}, bf16[64,2048]{1,0:T(8,128)(2,1)}, bf16[5...) custom-call(bf16[64,4096]{1,0:T(8,128)(2,1)} %bitcast.25, bf16[64,512]{1,0:T(8,128)(2,1)} %bitcast.27, ...), custom_call_target="tpu_custom_call" | custom-call | bytes 4194304 | tf_op jit(solution)/shard_map/pallas_call | solution.py:350
  3.4 3.0 %collective-permute-start.2 = (bf16[512,512]{1,0:T(8,128)(2,1)}, bf16[512,512]{1,0:T(8,128)(2,1)S(1)}, u32[]{:S(2)}, u32[]{:S(2)}) collective-permute-start(bf16[512,512]{1,0:T(8,128)(2,1)} %get-tuple-element.70.refs_1_), channel_id=1, source_target_pairs={{0,1},{1,0},{2,3},{3,2},{4,5},{5,4},{6,7},{7,6},{8,9},{9,8},{10,11... | collective-permute-start | bytes 1572872 | tf_op jit(solution)/shard_map/ppermute | solution.py:343
  6.4 1.6 %collective-permute-start.3 = (bf16[512,512]{1,0:T(8,128)(2,1)}, bf16[512,512]{1,0:T(8,128)(2,1)S(1)}, u32[]{:S(2)}, u32[]{:S(2)}) collective-permute-start(bf16[512,512]{1,0:T(8,128)(2,1)} %get-tuple-element.69.refs_0_), channel_id=1, source_target_pairs={{0,2},{1,3},{2,0},{3,1},{4,6},{5,7},{6,4},{7,5},{8,10},{9,11},{10,... | collective-permute-start | bytes 1572872 | tf_op jit(solution)/shard_map/ppermute | solution.py:343
  8.0 1.5 %collective-permute-start.4 = (bf16[64,2048]{1,0:T(8,128)(2,1)}, bf16[64,2048]{1,0:T(8,128)(2,1)S(1)}, u32[]{:S(2)}, u32[]{:S(2)}) collective-permute-start(bf16[64,2048]{1,0:T(8,128)(2,1)} %get-tuple-element.66), channel_id=1, source_target_pairs={{0,16},{1,17},{2,18},{3,19},{4,20},{5,21},{6,22},{7,23},{8,24},{9,... | collective-permute-start | bytes 786440 | tf_op jit(solution)/shard_map/ppermute | solution.py:343
  11.5 7.0 %collective-permute-done.2.refs_8_.refs_7_ = bf16[512,512]{1,0:T(8,128)(2,1)S(1)} collective-permute-done((bf16[512,512]{1,0:T(8,128)(2,1)}, bf16[512,512]{1,0:T(8,128)(2,1)S(1)}, u32[]{:S(2)}, u32[]{:S(2)}) %collective-permute-start.2) | collective-permute-done | bytes 524320 | tf_op jit(solution)/shard_map/ppermute | solution.py:343
  18.6 2.8 %collective-permute-start.1 = (bf16[128,256]{1,0:T(8,128)(2,1)S(1)}, bf16[128,256]{1,0:T(8,128)(2,1)S(1)}, u32[]{:S(2)}, u32[]{:S(2)}) collective-permute-start(bf16[128,256]{1,0:T(8,128)(2,1)S(1)} %get-tuple-element.64.refs_5_.place_ref), channel_id=1, source_target_pairs={{0,4},{1,5},{2,6},{3,7},{4,0},{5,1},{6,2},{7,3},{8,12},{9,13},{10,... | collective-permute-start | bytes 196616 | tf_op jit(solution)/shard_map/ppermute | solution.py:343
  21.4 1.5 %collective-permute-start.6 = (bf16[512,512]{1,0:T(8,128)(2,1)}, bf16[512,512]{1,0:T(8,128)(2,1)S(1)}, u32[]{:S(2)}, u32[]{:S(2)}) collective-permute-start(bf16[512,512]{1,0:T(8,128)(2,1)} %get-tuple-element.69.refs_0_), channel_id=1, source_target_pairs={{0,1},{1,0},{2,3},{3,2},{4,5},{5,4},{6,7},{7,6},{8,9},{9,8},{10,11... | collective-permute-start | bytes 1572872 | tf_op jit(solution)/shard_map/ppermute | solution.py:343
  22.9 0.8 collective-permute-done.1.refs_6_
  23.7 1.8 %collective-permute-start.7 = (bf16[512,512]{1,0:T(8,128)(2,1)}, bf16[512,512]{1,0:T(8,128)(2,1)S(1)}, u32[]{:S(2)}, u32[]{:S(2)}) collective-permute-start(bf16[512,512]{1,0:T(8,128)(2,1)} %get-tuple-element.70.refs_1_), channel_id=1, source_target_pairs={{0,2},{1,3},{2,0},{3,1},{4,6},{5,7},{6,4},{7,5},{8,10},{9,11},{10,... | collective-permute-start | bytes 1572872 | tf_op jit(solution)/shard_map/ppermute | solution.py:343
  25.6 0.9 copy-done.3
  26.5 2.3 %shard_map.102 = bf16[256,512]{1,0:T(8,128)(2,1)S(1)} custom-call(bf16[64,2048]{1,0:T(8,128)(2,1)S(1)} %copy-done.3, bf16[64,2048]{1,0:T(8,128)(2,1)S(1)} %collective-permute-done.refs_1_, bf16[64,2048]{1,0:T(8,128)(2,1)S(1)} %collective-permute-done.4.refs_2_, bf16[64,2048]{1,0:T(8,128)(2,1)S(1)} %collective-permute-done.5.refs_3_), custom_call_target="tpu_custom_call" | custom-call | flops 268435456 | bytes 8388608 | tf_op jit(solution)/shard_map/pallas_call | solution.py:394
  28.8 3.3 %collective-permute-start.11 = (bf16[256,512]{1,0:T(8,128)(2,1)S(1)}, bf16[256,512]{1,0:T(8,128)(2,1)S(1)}, u32[]{:S(2)}, u32[]{:S(2)}) collective-permute-start(bf16[256,512]{1,0:T(8,128)(2,1)S(1)} %shard_map.102), channel_id=1, source_target_pairs={{0,4},{1,5},{2,6},{3,7},{4,0},{5,1},{6,2},{7,3},{8,12},{9,13},{10,... | collective-permute-start | bytes 786440 | tf_op jit(solution)/shard_map/ppermute | solution.py:343
  32.1 2.3 %shard_map.103.refs_3_ = bf16[256,512]{1,0:T(8,128)(2,1)S(1)} custom-call(bf16[64,2048]{1,0:T(8,128)(2,1)S(1)} %copy-done.3, bf16[64,2048]{1,0:T(8,128)(2,1)S(1)} %collective-permute-done.refs_1_, bf16[64,2048]{1,0:T(8,128)(2,1)S(1)} %collective-permute-done.4.refs_2_, bf16[64,2048]{1,0:T(8,128)(2,1)S(1)} %collective-permute-done.5.refs_3_), custom_call_target="tpu_custom_call" | custom-call | flops 268435456 | bytes 8388608 | tf_op jit(solution)/shard_map/pallas_call | solution.py:394
  34.4 6.2 %collective-permute-done.11.refs_2_ = bf16[256,512]{1,0:T(8,128)(2,1)S(1)} collective-permute-done((bf16[256,512]{1,0:T(8,128)(2,1)S(1)}, bf16[256,512]{1,0:T(8,128)(2,1)S(1)}, u32[]{:S(2)}, u32[]{:S(2)}) %collective-permute-start.11) | collective-permute-done | bytes 262176 | tf_op jit(solution)/shard_map/ppermute | solution.py:343
  40.6 1.5 %collective-permute-start.13 = (bf16[256,512]{1,0:T(8,128)(2,1)S(1)}, bf16[256,512]{1,0:T(8,128)(2,1)S(1)}, u32[]{:S(2)}, u32[]{:S(2)}) collective-permute-start(bf16[256,512]{1,0:T(8,128)(2,1)S(1)} %collective-permute-done.11.refs_2_), channel_id=1, source_target_pairs={{0,16},{1,17},{2,18},{3,19},{4,20},{5,21},{6,22},{7,23},{8,24},{9,... | collective-permute-start | bytes 786440 | tf_op jit(solution)/shard_map/ppermute | solution.py:343
  42.2 0.8 collective-permute-start.9
  43.0 1.5 %collective-permute-start.15 = (bf16[512,512]{1,0:T(8,128)(2,1)S(1)}, bf16[512,512]{1,0:T(8,128)(2,1)S(1)}, u32[]{:S(2)}, u32[]{:S(2)}) collective-permute-start(bf16[512,512]{1,0:T(8,128)(2,1)S(1)} %collective-permute-done.3.refs_9_.refs_8_), channel_id=1, source_target_pairs={{0,1},{1,0},{2,3},{3,2},{4,5},{5,4},{6,7},{7,6},{8,9},{9,8},{10,11... | collective-permute-start | bytes 1572872 | tf_op jit(solution)/shard_map/ppermute | solution.py:343
  44.5 3.5 %collective-permute-start.16 = (bf16[512,512]{1,0:T(8,128)(2,1)S(1)}, bf16[512,512]{1,0:T(8,128)(2,1)S(1)}, u32[]{:S(2)}, u32[]{:S(2)}) collective-permute-start(bf16[512,512]{1,0:T(8,128)(2,1)S(1)} %collective-permute-done.2.refs_8_.refs_7_), channel_id=1, source_target_pairs={{0,2},{1,3},{2,0},{3,1},{4,6},{5,7},{6,4},{7,5},{8,10},{9,11},{10,... | collective-permute-start | bytes 1572872 | tf_op jit(solution)/shard_map/ppermute | solution.py:343
  48.6 2.8 %collective-permute-done.9.refs_5_ = bf16[256,512]{1,0:T(8,128)(2,1)S(1)} collective-permute-done((bf16[256,512]{1,0:T(8,128)(2,1)S(1)}, bf16[256,512]{1,0:T(8,128)(2,1)S(1)}, u32[]{:S(2)}, u32[]{:S(2)}) %collective-permute-start.9) | collective-permute-done | bytes 262176 | tf_op jit(solution)/shard_map/ppermute | solution.py:343
  52.0 1.0 copy-done.1
  53.0 1.0 copy-done.2
  54.0 1.2 shard_map.105
  55.3 1.3 shard_map.104
  58.1 3.1 %collective-permute-start.18 = (bf16[128,512]{1,0:T(8,128)(2,1)S(1)}, bf16[128,512]{1,0:T(8,128)(2,1)S(1)}, u32[]{:S(2)}, u32[]{:S(2)}) collective-permute-start(bf16[128,512]{1,0:T(8,128)(2,1)S(1)} %get-tuple-element.85), channel_id=1, source_target_pairs={{0,4},{1,5},{2,6},{3,7},{4,0},{5,1},{6,2},{7,3},{8,12},{9,13},{10,... | collective-permute-start | bytes 393224 | tf_op jit(solution)/shard_map/ppermute | solution.py:343
  62.4 7.9 %collective-permute-done.18.got_ref = bf16[128,512]{1,0:T(8,128)(2,1)S(1)} collective-permute-done((bf16[128,512]{1,0:T(8,128)(2,1)S(1)}, bf16[128,512]{1,0:T(8,128)(2,1)S(1)}, u32[]{:S(2)}, u32[]{:S(2)}) %collective-permute-start.18) | collective-permute-done | bytes 131104 | tf_op jit(solution)/shard_map/ppermute | solution.py:343
  70.4 1.6 %collective-permute-start.19 = (bf16[32,512]{1,0:T(8,128)(2,1)S(1)}, bf16[32,512]{1,0:T(8,128)(2,1)S(1)}, u32[]{:S(2)}, u32[]{:S(2)}) collective-permute-start(bf16[32,512]{1,0:T(8,128)(2,1)S(1)} %get-tuple-element.87), channel_id=1, source_target_pairs={{0,1},{1,0},{2,3},{3,2},{4,5},{5,4},{6,7},{7,6},{8,9},{9,8},{10,11... | collective-permute-start | bytes 98312 | tf_op jit(solution)/shard_map/ppermute | solution.py:343
  72.7 1.3 %collective-permute-start.21 = (bf16[32,512]{1,0:T(8,128)(2,1)S(1)}, bf16[32,512]{1,0:T(8,128)(2,1)S(1)}, u32[]{:S(2)}, u32[]{:S(2)}) collective-permute-start(bf16[32,512]{1,0:T(8,128)(2,1)S(1)} %get-tuple-element.89), channel_id=1, source_target_pairs={{0,3},{1,2},{2,1},{3,0},{4,7},{5,6},{6,5},{7,4},{8,11},{9,10},{10,... | collective-permute-start | bytes 98312 | tf_op jit(solution)/shard_map/ppermute | solution.py:343
  74.4 1.5 %collective-permute-done.20.refs_2_ = bf16[32,512]{1,0:T(8,128)(2,1)S(1)} collective-permute-done((bf16[32,512]{1,0:T(8,128)(2,1)S(1)}, bf16[32,512]{1,0:T(8,128)(2,1)S(1)}, u32[]{:S(2)}, u32[]{:S(2)}) %collective-permute-start.20) | collective-permute-done | bytes 32800 | tf_op jit(solution)/shard_map/ppermute | solution.py:343
  75.9 1.6 %collective-permute-done.21.refs_3_ = bf16[32,512]{1,0:T(8,128)(2,1)S(1)} collective-permute-done((bf16[32,512]{1,0:T(8,128)(2,1)S(1)}, bf16[32,512]{1,0:T(8,128)(2,1)S(1)}, u32[]{:S(2)}, u32[]{:S(2)}) %collective-permute-start.21) | collective-permute-done | bytes 32800 | tf_op jit(solution)/shard_map/ppermute | solution.py:343
  78.1 1.3 %collective-permute-start.24 = (bf16[32,512]{1,0:T(8,128)(2,1)S(1)}, bf16[32,512]{1,0:T(8,128)(2,1)S(1)}, u32[]{:S(2)}, u32[]{:S(2)}) collective-permute-start(bf16[32,512]{1,0:T(8,128)(2,1)S(1)} %get-tuple-element.95), channel_id=1, source_target_pairs={{0,2},{1,3},{2,0},{3,1},{4,6},{5,7},{6,4},{7,5},{8,10},{9,11},{10,... | collective-permute-start | bytes 98312 | tf_op jit(solution)/shard_map/ppermute | solution.py:343
  79.4 1.6 %collective-permute-start.25 = (bf16[32,512]{1,0:T(8,128)(2,1)S(1)}, bf16[32,512]{1,0:T(8,128)(2,1)S(1)}, u32[]{:S(2)}, u32[]{:S(2)}) collective-permute-start(bf16[32,512]{1,0:T(8,128)(2,1)S(1)} %get-tuple-element.96), channel_id=1, source_target_pairs={{0,3},{1,2},{2,1},{3,0},{4,7},{5,6},{6,5},{7,4},{8,11},{9,10},{10,... | collective-permute-start | bytes 98312 | tf_op jit(solution)/shard_map/ppermute | solution.py:343
  82.0 2.2 %collective-permute-done.25.refs_7_ = bf16[32,512]{1,0:T(8,128)(2,1)S(1)} collective-permute-done((bf16[32,512]{1,0:T(8,128)(2,1)S(1)}, bf16[32,512]{1,0:T(8,128)(2,1)S(1)}, u32[]{:S(2)}, u32[]{:S(2)}) %collective-permute-start.25) | collective-permute-done | bytes 32800 | tf_op jit(solution)/shard_map/ppermute | solution.py:343
  84.3 1.3 shard_map.110
  85.5 2.5 %collective-permute-start.23 = (bf16[256,512]{1,0:T(8,128)(2,1)S(1)}, bf16[256,512]{1,0:T(8,128)(2,1)S(1)}, u32[]{:S(2)}, u32[]{:S(2)}) collective-permute-start(bf16[256,512]{1,0:T(8,128)(2,1)S(1)} %get-tuple-element.92), channel_id=1, source_target_pairs={{0,4},{1,5},{2,6},{3,7},{4,0},{5,1},{6,2},{7,3},{8,12},{9,13},{10,... | collective-permute-start | bytes 786440 | tf_op jit(solution)/shard_map/ppermute | solution.py:343
  88.2 1.7 %collective-permute-start.28 = (bf16[32,3200]{1,0:T(8,128)(2,1)S(1)}, bf16[32,3200]{1,0:T(8,128)(2,1)S(1)}, u32[]{:S(2)}, u32[]{:S(2)}) collective-permute-start(bf16[32,3200]{1,0:T(8,128)(2,1)S(1)} %get-tuple-element.103), channel_id=1, source_target_pairs={{0,16},{1,17},{2,18},{3,19},{4,20},{5,21},{6,22},{7,23},{8,24},{9,... | collective-permute-start | bytes 614408 | tf_op jit(solution)/shard_map/ppermute | solution.py:343
  89.9 1.7 %collective-permute-start.26 = (bf16[256,512]{1,0:T(8,128)(2,1)S(1)}, bf16[256,512]{1,0:T(8,128)(2,1)S(1)}, u32[]{:S(2)}, u32[]{:S(2)}) collective-permute-start(bf16[256,512]{1,0:T(8,128)(2,1)S(1)} %get-tuple-element.98), channel_id=1, source_target_pairs={{0,4},{1,5},{2,6},{3,7},{4,0},{5,1},{6,2},{7,3},{8,12},{9,13},{10,... | collective-permute-start | bytes 786440 | tf_op jit(solution)/shard_map/ppermute | solution.py:343
  91.6 15.3 %collective-permute-done.23.got0 = bf16[256,512]{1,0:T(8,128)(2,1)S(1)} collective-permute-done((bf16[256,512]{1,0:T(8,128)(2,1)S(1)}, bf16[256,512]{1,0:T(8,128)(2,1)S(1)}, u32[]{:S(2)}, u32[]{:S(2)}) %collective-permute-start.23) | collective-permute-done | bytes 262176 | tf_op jit(solution)/shard_map/ppermute | solution.py:343
  107.0 1.7 %collective-permute-start.30 = (bf16[32,1536]{1,0:T(8,128)(2,1)S(1)}, bf16[32,1536]{1,0:T(8,128)(2,1)S(1)}, u32[]{:S(2)}, u32[]{:S(2)}) collective-permute-start(bf16[32,1536]{1,0:T(8,128)(2,1)S(1)} %shard_map.112.refs_0_), channel_id=1, source_target_pairs={{0,16},{1,17},{2,18},{3,19},{4,20},{5,21},{6,22},{7,23},{8,24},{9,... | collective-permute-start | bytes 294920 | tf_op jit(solution)/shard_map/ppermute | solution.py:343
  108.7 3.0 %collective-permute-done.30.refs_2_ = bf16[32,1536]{1,0:T(8,128)(2,1)S(1)} collective-permute-done((bf16[32,1536]{1,0:T(8,128)(2,1)S(1)}, bf16[32,1536]{1,0:T(8,128)(2,1)S(1)}, u32[]{:S(2)}, u32[]{:S(2)}) %collective-permute-start.30) | collective-permute-done | bytes 98336 | tf_op jit(solution)/shard_map/ppermute | solution.py:343
  112.0 1.0 collective-permute-done.31.refs_3_
  113.7 1.6 %collective-permute-start.32 = (bf16[32,1024]{1,0:T(8,128)(2,1)S(1)}, bf16[32,1024]{1,0:T(8,128)(2,1)S(1)}, u32[]{:S(2)}, u32[]{:S(2)}) collective-permute-start(bf16[32,1024]{1,0:T(8,128)(2,1)S(1)} %get-tuple-element.106), channel_id=1, source_target_pairs={{0,1},{1,0},{2,3},{3,2},{4,5},{5,4},{6,7},{7,6},{8,9},{9,8},{10,11... | collective-permute-start | bytes 196616 | tf_op jit(solution)/shard_map/ppermute | solution.py:343
  115.3 2.0 %collective-permute-start.34 = (bf16[32,1024]{1,0:T(8,128)(2,1)S(1)}, bf16[32,1024]{1,0:T(8,128)(2,1)S(1)}, u32[]{:S(2)}, u32[]{:S(2)}) collective-permute-start(bf16[32,1024]{1,0:T(8,128)(2,1)S(1)} %get-tuple-element.108), channel_id=1, source_target_pairs={{0,3},{1,2},{2,1},{3,0},{4,7},{5,6},{6,5},{7,4},{8,11},{9,10},{10,... | collective-permute-start | bytes 196616 | tf_op jit(solution)/shard_map/ppermute | solution.py:343
  117.2 0.8 collective-permute-done.32.refs_1_
  118.0 1.8 %collective-permute-done.33.refs_2_ = bf16[32,1024]{1,0:T(8,128)(2,1)S(1)} collective-permute-done((bf16[32,1024]{1,0:T(8,128)(2,1)S(1)}, bf16[32,1024]{1,0:T(8,128)(2,1)S(1)}, u32[]{:S(2)}, u32[]{:S(2)}) %collective-permute-start.33) | collective-permute-done | bytes 65568 | tf_op jit(solution)/shard_map/ppermute | solution.py:343
  119.8 0.9 collective-permute-done.34.refs_3_
  120.7 3.0 %collective-permute-start.35 = (bf16[64,1024]{1,0:T(8,128)(2,1)S(1)}, bf16[64,1024]{1,0:T(8,128)(2,1)S(1)}, u32[]{:S(2)}, u32[]{:S(2)}) collective-permute-start(bf16[64,1024]{1,0:T(8,128)(2,1)S(1)} %shard_map.114), channel_id=1, source_target_pairs={{0,4},{1,5},{2,6},{3,7},{4,0},{5,1},{6,2},{7,3},{8,12},{9,13},{10,... | collective-permute-start | bytes 393224 | tf_op jit(solution)/shard_map/ppermute | solution.py:343
  123.7 5.2 %collective-permute-done.35.refs_4_ = bf16[64,1024]{1,0:T(8,128)(2,1)S(1)} collective-permute-done((bf16[64,1024]{1,0:T(8,128)(2,1)S(1)}, bf16[64,1024]{1,0:T(8,128)(2,1)S(1)}, u32[]{:S(2)}, u32[]{:S(2)}) %collective-permute-start.35) | collective-permute-done | bytes 131104 | tf_op jit(solution)/shard_map/ppermute | solution.py:343
  128.9 1.1 shard_map.115
  (61 shorter events, 10.0 us)
Async XLA Ops:
  3.4 15.1 %collective-permute-start.2 = (bf16[512,512]{1,0:T(8,128)(2,1)}, bf16[512,512]{1,0:T(8,128)(2,1)S(1)}, u32[]{:S(2)}, u32[]{:S(2)}) collective-permute-start(bf16[512,512]{1,0:T(8,128)(2,1)} %get-tuple-element.70.refs_1_), channel_id=1, source_target_pairs={{0,1},{1,0},{2,3},{3,2},{4,5},{5,4},{6,7},{7,6},{8,9},{9,8},{10,11... | collective-permute-start | bytes 1572872 | tf_op jit(solution)/shard_map/ppermute | solution.py:343
  6.4 15.0 %collective-permute-start.3 = (bf16[512,512]{1,0:T(8,128)(2,1)}, bf16[512,512]{1,0:T(8,128)(2,1)S(1)}, u32[]{:S(2)}, u32[]{:S(2)}) collective-permute-start(bf16[512,512]{1,0:T(8,128)(2,1)} %get-tuple-element.69.refs_0_), channel_id=1, source_target_pairs={{0,2},{1,3},{2,0},{3,1},{4,6},{5,7},{6,4},{7,5},{8,10},{9,11},{10,... | collective-permute-start | bytes 1572872 | tf_op jit(solution)/shard_map/ppermute | solution.py:343
  8.0 17.6 %collective-permute-start = (bf16[64,2048]{1,0:T(8,128)(2,1)}, bf16[64,2048]{1,0:T(8,128)(2,1)S(1)}, u32[]{:S(2)}, u32[]{:S(2)}) collective-permute-start(bf16[64,2048]{1,0:T(8,128)(2,1)} %get-tuple-element.61), channel_id=1, source_target_pairs={{0,8},{1,9},{2,10},{3,11},{4,12},{5,13},{6,14},{7,15},{8,0},{9,1},... | collective-permute-start | bytes 786440 | tf_op jit(solution)/shard_map/ppermute | solution.py:343
  8.0 17.6 %collective-permute-start.4 = (bf16[64,2048]{1,0:T(8,128)(2,1)}, bf16[64,2048]{1,0:T(8,128)(2,1)S(1)}, u32[]{:S(2)}, u32[]{:S(2)}) collective-permute-start(bf16[64,2048]{1,0:T(8,128)(2,1)} %get-tuple-element.66), channel_id=1, source_target_pairs={{0,16},{1,17},{2,18},{3,19},{4,20},{5,21},{6,22},{7,23},{8,24},{9,... | collective-permute-start | bytes 786440 | tf_op jit(solution)/shard_map/ppermute | solution.py:343
  9.5 16.0 %collective-permute-start.5 = (bf16[64,2048]{1,0:T(8,128)(2,1)}, bf16[64,2048]{1,0:T(8,128)(2,1)S(1)}, u32[]{:S(2)}, u32[]{:S(2)}) collective-permute-start(bf16[64,2048]{1,0:T(8,128)(2,1)} %get-tuple-element.67), channel_id=1, source_target_pairs={{0,24},{1,25},{2,26},{3,27},{4,28},{5,29},{6,30},{7,31},{8,16},{9,... | collective-permute-start | bytes 786440 | tf_op jit(solution)/shard_map/ppermute | solution.py:343
  9.9 0.7 copy-start.6
  10.6 0.7 copy-start.7
  18.6 5.2 %collective-permute-start.1 = (bf16[128,256]{1,0:T(8,128)(2,1)S(1)}, bf16[128,256]{1,0:T(8,128)(2,1)S(1)}, u32[]{:S(2)}, u32[]{:S(2)}) collective-permute-start(bf16[128,256]{1,0:T(8,128)(2,1)S(1)} %get-tuple-element.64.refs_5_.place_ref), channel_id=1, source_target_pairs={{0,4},{1,5},{2,6},{3,7},{4,0},{5,1},{6,2},{7,3},{8,12},{9,13},{10,... | collective-permute-start | bytes 196616 | tf_op jit(solution)/shard_map/ppermute | solution.py:343
  21.4 20.8 %collective-permute-start.6 = (bf16[512,512]{1,0:T(8,128)(2,1)}, bf16[512,512]{1,0:T(8,128)(2,1)S(1)}, u32[]{:S(2)}, u32[]{:S(2)}) collective-permute-start(bf16[512,512]{1,0:T(8,128)(2,1)} %get-tuple-element.69.refs_0_), channel_id=1, source_target_pairs={{0,1},{1,0},{2,3},{3,2},{4,5},{5,4},{6,7},{7,6},{8,9},{9,8},{10,11... | collective-permute-start | bytes 1572872 | tf_op jit(solution)/shard_map/ppermute | solution.py:343
  23.7 18.4 %collective-permute-start.7 = (bf16[512,512]{1,0:T(8,128)(2,1)}, bf16[512,512]{1,0:T(8,128)(2,1)S(1)}, u32[]{:S(2)}, u32[]{:S(2)}) collective-permute-start(bf16[512,512]{1,0:T(8,128)(2,1)} %get-tuple-element.70.refs_1_), channel_id=1, source_target_pairs={{0,2},{1,3},{2,0},{3,1},{4,6},{5,7},{6,4},{7,5},{8,10},{9,11},{10,... | collective-permute-start | bytes 1572872 | tf_op jit(solution)/shard_map/ppermute | solution.py:343
  25.6 1.0 copy-start.3
  26.5 28.8 %copy-start.4 = (bf16[256,1024]{1,0:T(8,128)(2,1)S(1)}, bf16[256,1024]{1,0:T(8,128)(2,1)}, u32[]{:S(2)}) copy-start(bf16[256,1024]{1,0:T(8,128)(2,1)} %get-tuple-element.59.refs_2_) | copy-start | bytes 1572868
  28.8 11.8 %collective-permute-start.11 = (bf16[256,512]{1,0:T(8,128)(2,1)S(1)}, bf16[256,512]{1,0:T(8,128)(2,1)S(1)}, u32[]{:S(2)}, u32[]{:S(2)}) collective-permute-start(bf16[256,512]{1,0:T(8,128)(2,1)S(1)} %shard_map.102), channel_id=1, source_target_pairs={{0,4},{1,5},{2,6},{3,7},{4,0},{5,1},{6,2},{7,3},{8,12},{9,13},{10,... | collective-permute-start | bytes 786440 | tf_op jit(solution)/shard_map/ppermute | solution.py:343
  40.6 8.0 %collective-permute-start.13 = (bf16[256,512]{1,0:T(8,128)(2,1)S(1)}, bf16[256,512]{1,0:T(8,128)(2,1)S(1)}, u32[]{:S(2)}, u32[]{:S(2)}) collective-permute-start(bf16[256,512]{1,0:T(8,128)(2,1)S(1)} %collective-permute-done.11.refs_2_), channel_id=1, source_target_pairs={{0,16},{1,17},{2,18},{3,19},{4,20},{5,21},{6,22},{7,23},{8,24},{9,... | collective-permute-start | bytes 786440 | tf_op jit(solution)/shard_map/ppermute | solution.py:343
  42.2 9.3 %collective-permute-start.9 = (bf16[256,512]{1,0:T(8,128)(2,1)S(1)}, bf16[256,512]{1,0:T(8,128)(2,1)S(1)}, u32[]{:S(2)}, u32[]{:S(2)}) collective-permute-start(bf16[256,512]{1,0:T(8,128)(2,1)S(1)} %shard_map.103.refs_3_), channel_id=1, source_target_pairs={{0,16},{1,17},{2,18},{3,19},{4,20},{5,21},{6,22},{7,23},{8,24},{9,... | collective-permute-start | bytes 786440 | tf_op jit(solution)/shard_map/ppermute | solution.py:343
  43.0 8.5 %collective-permute-start.12 = (bf16[256,512]{1,0:T(8,128)(2,1)S(1)}, bf16[256,512]{1,0:T(8,128)(2,1)S(1)}, u32[]{:S(2)}, u32[]{:S(2)}) collective-permute-start(bf16[256,512]{1,0:T(8,128)(2,1)S(1)} %collective-permute-done.11.refs_2_), channel_id=1, source_target_pairs={{0,8},{1,9},{2,10},{3,11},{4,12},{5,13},{6,14},{7,15},{8,0},{9,1},... | collective-permute-start | bytes 786440 | tf_op jit(solution)/shard_map/ppermute | solution.py:343
  43.0 14.3 %collective-permute-start.15 = (bf16[512,512]{1,0:T(8,128)(2,1)S(1)}, bf16[512,512]{1,0:T(8,128)(2,1)S(1)}, u32[]{:S(2)}, u32[]{:S(2)}) collective-permute-start(bf16[512,512]{1,0:T(8,128)(2,1)S(1)} %collective-permute-done.3.refs_9_.refs_8_), channel_id=1, source_target_pairs={{0,1},{1,0},{2,3},{3,2},{4,5},{5,4},{6,7},{7,6},{8,9},{9,8},{10,11... | collective-permute-start | bytes 1572872 | tf_op jit(solution)/shard_map/ppermute | solution.py:343
  44.5 16.8 %collective-permute-start.16 = (bf16[512,512]{1,0:T(8,128)(2,1)S(1)}, bf16[512,512]{1,0:T(8,128)(2,1)S(1)}, u32[]{:S(2)}, u32[]{:S(2)}) collective-permute-start(bf16[512,512]{1,0:T(8,128)(2,1)S(1)} %collective-permute-done.2.refs_8_.refs_7_), channel_id=1, source_target_pairs={{0,2},{1,3},{2,0},{3,1},{4,6},{5,7},{6,4},{7,5},{8,10},{9,11},{10,... | collective-permute-start | bytes 1572872 | tf_op jit(solution)/shard_map/ppermute | solution.py:343
  48.6 3.3 %collective-permute-start.14 = (bf16[256,512]{1,0:T(8,128)(2,1)S(1)}, bf16[256,512]{1,0:T(8,128)(2,1)S(1)}, u32[]{:S(2)}, u32[]{:S(2)}) collective-permute-start(bf16[256,512]{1,0:T(8,128)(2,1)S(1)} %collective-permute-done.13.refs_4_), channel_id=1, source_target_pairs={{0,8},{1,9},{2,10},{3,11},{4,12},{5,13},{6,14},{7,15},{8,0},{9,1},... | collective-permute-start | bytes 786440 | tf_op jit(solution)/shard_map/ppermute | solution.py:343
  51.4 3.8 %collective-permute-start.8 = (bf16[256,512]{1,0:T(8,128)(2,1)S(1)}, bf16[256,512]{1,0:T(8,128)(2,1)S(1)}, u32[]{:S(2)}, u32[]{:S(2)}) collective-permute-start(bf16[256,512]{1,0:T(8,128)(2,1)S(1)} %shard_map.103.refs_3_), channel_id=1, source_target_pairs={{0,8},{1,9},{2,10},{3,11},{4,12},{5,13},{6,14},{7,15},{8,0},{9,1},... | collective-permute-start | bytes 786440 | tf_op jit(solution)/shard_map/ppermute | solution.py:343
  51.4 3.8 %collective-permute-start.10 = (bf16[256,512]{1,0:T(8,128)(2,1)S(1)}, bf16[256,512]{1,0:T(8,128)(2,1)S(1)}, u32[]{:S(2)}, u32[]{:S(2)}) collective-permute-start(bf16[256,512]{1,0:T(8,128)(2,1)S(1)} %collective-permute-done.9.refs_5_), channel_id=1, source_target_pairs={{0,8},{1,9},{2,10},{3,11},{4,12},{5,13},{6,14},{7,15},{8,0},{9,1},... | collective-permute-start | bytes 786440 | tf_op jit(solution)/shard_map/ppermute | solution.py:343
  52.0 1.0 copy-start.1
  53.0 1.0 copy-start.2
  54.0 30.2 %slice-start = ((s8[6291456]{0:T(1024)(128)(4,1)}), s8[4194304]{0:T(1024)(128)(4,1)S(1)}, s32[]{:S(2)}) async-start(s8[6291456]{0:T(1024)(128)(4,1)} %bitcast.16), calls=%async_computation | async-start | bytes 8388608
  55.3 15.1 %copy-start.5 = (f32[1024]{0:T(1024)S(1)}, f32[1024]{0:T(1024)}, u32[]{:S(2)}) copy-start(f32[1024]{0:T(1024)} %param.15) | copy-start | bytes 12292
  55.3 29.0 %slice-start.1 = ((s8[6291456]{0:T(1024)(128)(4,1)}), s8[2097152]{0:T(1024)(128)(4,1)S(1)}, s32[]{:S(2)}) async-start(s8[6291456]{0:T(1024)(128)(4,1)} %bitcast.16), calls=%async_computation.1 | async-start | bytes 4194304
  58.1 54.9 %copy-start = (bf16[1,1536,1024]{2,1,0:T(8,128)(2,1)S(1)}, bf16[1,1536,1024]{2,1,0:T(8,128)(2,1)}, u32[]{:S(2)}) copy-start(bf16[1,1536,1024]{2,1,0:T(8,128)(2,1)} %param.19) | copy-start | bytes 9437188
  58.1 12.3 %collective-permute-start.18 = (bf16[128,512]{1,0:T(8,128)(2,1)S(1)}, bf16[128,512]{1,0:T(8,128)(2,1)S(1)}, u32[]{:S(2)}, u32[]{:S(2)}) collective-permute-start(bf16[128,512]{1,0:T(8,128)(2,1)S(1)} %get-tuple-element.85), channel_id=1, source_target_pairs={{0,4},{1,5},{2,6},{3,7},{4,0},{5,1},{6,2},{7,3},{8,12},{9,13},{10,... | collective-permute-start | bytes 393224 | tf_op jit(solution)/shard_map/ppermute | solution.py:343
  62.0 11.9 %collective-permute-start.17 = (bf16[128,512]{1,0:T(8,128)(2,1)S(1)}, bf16[128,512]{1,0:T(8,128)(2,1)S(1)}, u32[]{:S(2)}, u32[]{:S(2)}) collective-permute-start(bf16[128,512]{1,0:T(8,128)(2,1)S(1)} %get-tuple-element.83), channel_id=1, source_target_pairs={{0,4},{1,5},{2,6},{3,7},{4,0},{5,1},{6,2},{7,3},{8,12},{9,13},{10,... | collective-permute-start | bytes 393224 | tf_op jit(solution)/shard_map/ppermute | solution.py:343
  70.4 4.0 %collective-permute-start.19 = (bf16[32,512]{1,0:T(8,128)(2,1)S(1)}, bf16[32,512]{1,0:T(8,128)(2,1)S(1)}, u32[]{:S(2)}, u32[]{:S(2)}) collective-permute-start(bf16[32,512]{1,0:T(8,128)(2,1)S(1)} %get-tuple-element.87), channel_id=1, source_target_pairs={{0,1},{1,0},{2,3},{3,2},{4,5},{5,4},{6,7},{7,6},{8,9},{9,8},{10,11... | collective-permute-start | bytes 98312 | tf_op jit(solution)/shard_map/ppermute | solution.py:343
  72.0 3.9 %collective-permute-start.20 = (bf16[32,512]{1,0:T(8,128)(2,1)S(1)}, bf16[32,512]{1,0:T(8,128)(2,1)S(1)}, u32[]{:S(2)}, u32[]{:S(2)}) collective-permute-start(bf16[32,512]{1,0:T(8,128)(2,1)S(1)} %get-tuple-element.88), channel_id=1, source_target_pairs={{0,2},{1,3},{2,0},{3,1},{4,6},{5,7},{6,4},{7,5},{8,10},{9,11},{10,... | collective-permute-start | bytes 98312 | tf_op jit(solution)/shard_map/ppermute | solution.py:343
  72.7 4.8 %collective-permute-start.21 = (bf16[32,512]{1,0:T(8,128)(2,1)S(1)}, bf16[32,512]{1,0:T(8,128)(2,1)S(1)}, u32[]{:S(2)}, u32[]{:S(2)}) collective-permute-start(bf16[32,512]{1,0:T(8,128)(2,1)S(1)} %get-tuple-element.89), channel_id=1, source_target_pairs={{0,3},{1,2},{2,1},{3,0},{4,7},{5,6},{6,5},{7,4},{8,11},{9,10},{10,... | collective-permute-start | bytes 98312 | tf_op jit(solution)/shard_map/ppermute | solution.py:343
  77.5 4.0 %collective-permute-start.22 = (bf16[32,512]{1,0:T(8,128)(2,1)S(1)}, bf16[32,512]{1,0:T(8,128)(2,1)S(1)}, u32[]{:S(2)}, u32[]{:S(2)}) collective-permute-start(bf16[32,512]{1,0:T(8,128)(2,1)S(1)} %get-tuple-element.91), channel_id=1, source_target_pairs={{0,1},{1,0},{2,3},{3,2},{4,5},{5,4},{6,7},{7,6},{8,9},{9,8},{10,11... | collective-permute-start | bytes 98312 | tf_op jit(solution)/shard_map/ppermute | solution.py:343
  78.1 3.9 %collective-permute-start.24 = (bf16[32,512]{1,0:T(8,128)(2,1)S(1)}, bf16[32,512]{1,0:T(8,128)(2,1)S(1)}, u32[]{:S(2)}, u32[]{:S(2)}) collective-permute-start(bf16[32,512]{1,0:T(8,128)(2,1)S(1)} %get-tuple-element.95), channel_id=1, source_target_pairs={{0,2},{1,3},{2,0},{3,1},{4,6},{5,7},{6,4},{7,5},{8,10},{9,11},{10,... | collective-permute-start | bytes 98312 | tf_op jit(solution)/shard_map/ppermute | solution.py:343
  79.4 4.8 %collective-permute-start.25 = (bf16[32,512]{1,0:T(8,128)(2,1)S(1)}, bf16[32,512]{1,0:T(8,128)(2,1)S(1)}, u32[]{:S(2)}, u32[]{:S(2)}) collective-permute-start(bf16[32,512]{1,0:T(8,128)(2,1)S(1)} %get-tuple-element.96), channel_id=1, source_target_pairs={{0,3},{1,2},{2,1},{3,0},{4,7},{5,6},{6,5},{7,4},{8,11},{9,10},{10,... | collective-permute-start | bytes 98312 | tf_op jit(solution)/shard_map/ppermute | solution.py:343
  85.5 2.5 %collective-permute-start.27 = (bf16[64,3200]{1,0:T(8,128)(2,1)S(1)}, bf16[64,3200]{1,0:T(8,128)(2,1)S(1)}, u32[]{:S(2)}, u32[]{:S(2)}) collective-permute-start(bf16[64,3200]{1,0:T(8,128)(2,1)S(1)} %get-tuple-element.100), channel_id=1, source_target_pairs={{0,8},{1,9},{2,10},{3,11},{4,12},{5,13},{6,14},{7,15},{8,0},{9,1},... | collective-permute-start | bytes 1228808 | tf_op jit(solution)/shard_map/ppermute | solution.py:343
  85.5 21.3 %collective-permute-start.23 = (bf16[256,512]{1,0:T(8,128)(2,1)S(1)}, bf16[256,512]{1,0:T(8,128)(2,1)S(1)}, u32[]{:S(2)}, u32[]{:S(2)}) collective-permute-start(bf16[256,512]{1,0:T(8,128)(2,1)S(1)} %get-tuple-element.92), channel_id=1, source_target_pairs={{0,4},{1,5},{2,6},{3,7},{4,0},{5,1},{6,2},{7,3},{8,12},{9,13},{10,... | collective-permute-start | bytes 786440 | tf_op jit(solution)/shard_map/ppermute | solution.py:343
  88.2 18.7 %collective-permute-start.28 = (bf16[32,3200]{1,0:T(8,128)(2,1)S(1)}, bf16[32,3200]{1,0:T(8,128)(2,1)S(1)}, u32[]{:S(2)}, u32[]{:S(2)}) collective-permute-start(bf16[32,3200]{1,0:T(8,128)(2,1)S(1)} %get-tuple-element.103), channel_id=1, source_target_pairs={{0,16},{1,17},{2,18},{3,19},{4,20},{5,21},{6,22},{7,23},{8,24},{9,... | collective-permute-start | bytes 614408 | tf_op jit(solution)/shard_map/ppermute | solution.py:343
  89.9 22.1 %collective-permute-start.26 = (bf16[256,512]{1,0:T(8,128)(2,1)S(1)}, bf16[256,512]{1,0:T(8,128)(2,1)S(1)}, u32[]{:S(2)}, u32[]{:S(2)}) collective-permute-start(bf16[256,512]{1,0:T(8,128)(2,1)S(1)} %get-tuple-element.98), channel_id=1, source_target_pairs={{0,4},{1,5},{2,6},{3,7},{4,0},{5,1},{6,2},{7,3},{8,12},{9,13},{10,... | collective-permute-start | bytes 786440 | tf_op jit(solution)/shard_map/ppermute | solution.py:343
  107.0 4.7 %collective-permute-start.30 = (bf16[32,1536]{1,0:T(8,128)(2,1)S(1)}, bf16[32,1536]{1,0:T(8,128)(2,1)S(1)}, u32[]{:S(2)}, u32[]{:S(2)}) collective-permute-start(bf16[32,1536]{1,0:T(8,128)(2,1)S(1)} %shard_map.112.refs_0_), channel_id=1, source_target_pairs={{0,16},{1,17},{2,18},{3,19},{4,20},{5,21},{6,22},{7,23},{8,24},{9,... | collective-permute-start | bytes 294920 | tf_op jit(solution)/shard_map/ppermute | solution.py:343
  108.7 3.4 %collective-permute-start.29 = (bf16[32,1536]{1,0:T(8,128)(2,1)S(1)}, bf16[32,1536]{1,0:T(8,128)(2,1)S(1)}, u32[]{:S(2)}, u32[]{:S(2)}) collective-permute-start(bf16[32,1536]{1,0:T(8,128)(2,1)S(1)} %shard_map.112.refs_0_), channel_id=1, source_target_pairs={{0,8},{1,9},{2,10},{3,11},{4,12},{5,13},{6,14},{7,15},{8,0},{9,1},... | collective-permute-start | bytes 294920 | tf_op jit(solution)/shard_map/ppermute | solution.py:343
  111.7 1.3 %collective-permute-start.31 = (bf16[32,1536]{1,0:T(8,128)(2,1)S(1)}, bf16[32,1536]{1,0:T(8,128)(2,1)S(1)}, u32[]{:S(2)}, u32[]{:S(2)}) collective-permute-start(bf16[32,1536]{1,0:T(8,128)(2,1)S(1)} %collective-permute-done.30.refs_2_), channel_id=1, source_target_pairs={{0,8},{1,9},{2,10},{3,11},{4,12},{5,13},{6,14},{7,15},{8,0},{9,1},... | collective-permute-start | bytes 294920 | tf_op jit(solution)/shard_map/ppermute | solution.py:343
  113.7 4.3 %collective-permute-start.32 = (bf16[32,1024]{1,0:T(8,128)(2,1)S(1)}, bf16[32,1024]{1,0:T(8,128)(2,1)S(1)}, u32[]{:S(2)}, u32[]{:S(2)}) collective-permute-start(bf16[32,1024]{1,0:T(8,128)(2,1)S(1)} %get-tuple-element.106), channel_id=1, source_target_pairs={{0,1},{1,0},{2,3},{3,2},{4,5},{5,4},{6,7},{7,6},{8,9},{9,8},{10,11... | collective-permute-start | bytes 196616 | tf_op jit(solution)/shard_map/ppermute | solution.py:343
  115.3 4.6 %collective-permute-start.33 = (bf16[32,1024]{1,0:T(8,128)(2,1)S(1)}, bf16[32,1024]{1,0:T(8,128)(2,1)S(1)}, u32[]{:S(2)}, u32[]{:S(2)}) collective-permute-start(bf16[32,1024]{1,0:T(8,128)(2,1)S(1)} %get-tuple-element.107), channel_id=1, source_target_pairs={{0,2},{1,3},{2,0},{3,1},{4,6},{5,7},{6,4},{7,5},{8,10},{9,11},{10,... | collective-permute-start | bytes 196616 | tf_op jit(solution)/shard_map/ppermute | solution.py:343
  115.3 5.5 %collective-permute-start.34 = (bf16[32,1024]{1,0:T(8,128)(2,1)S(1)}, bf16[32,1024]{1,0:T(8,128)(2,1)S(1)}, u32[]{:S(2)}, u32[]{:S(2)}) collective-permute-start(bf16[32,1024]{1,0:T(8,128)(2,1)S(1)} %get-tuple-element.108), channel_id=1, source_target_pairs={{0,3},{1,2},{2,1},{3,0},{4,7},{5,6},{6,5},{7,4},{8,11},{9,10},{10,... | collective-permute-start | bytes 196616 | tf_op jit(solution)/shard_map/ppermute | solution.py:343
  120.7 8.1 %collective-permute-start.35 = (bf16[64,1024]{1,0:T(8,128)(2,1)S(1)}, bf16[64,1024]{1,0:T(8,128)(2,1)S(1)}, u32[]{:S(2)}, u32[]{:S(2)}) collective-permute-start(bf16[64,1024]{1,0:T(8,128)(2,1)S(1)} %shard_map.114), channel_id=1, source_target_pairs={{0,4},{1,5},{2,6},{3,7},{4,0},{5,1},{6,2},{7,3},{8,12},{9,13},{10,... | collective-permute-start | bytes 393224 | tf_op jit(solution)/shard_map/ppermute | solution.py:343

commit v5 on v4

--- a/solution.py
+++ b/solution.py
@@ -181,43 +181,40 @@
         acc[:, at] = total
 
 
-def last_kernel(E, cap, j, *refs):
-    accs, lasts, w_ref, places, (own_ref, full_ref, keep_ref, send_ref) = (
-        refs[:2],
-        refs[2:4],
-        refs[4],
-        refs[5:7],
-        refs[7:],
-    )
-    half = w_ref.shape[1]
-    cols = slice(j * half, (j + 1) * half)
-    for t in (1, 0):
-        total = accs[t][:, cols] + dot(lasts[t][...], w_ref[...])
-        rounded = total.astype(BF16)
-        if t == 0:
-            own_ref[...] = total
-        else:
-            full_ref[...] = rounded
-        picked = dot(places[t][...], rounded)
-        for d in range(E // 2):
-            near, far = spread(d) ^ (PAIR * t), spread(d) ^ PAIR ^ (PAIR * t)
-            at = (2 * d + t) * cap
-            keep_ref[at : at + cap, :] = picked[near * cap : (near + 1) * cap]
-            at = (2 * d + 1 - t) * cap
-            send_ref[at : at + cap, :] = picked[far * cap : (far + 1) * cap].astype(BF16)
-
-
-def outgoing_kernel(j, keep_ref, got_ref, gain_ref, *outs):
-    half = keep_ref.shape[1]
-    gain = gain_ref[:, j * half : (j + 1) * half]
-    scaled = ((keep_ref[...] + got_ref[...].astype(F32)) * gain).astype(BF16)
+def last_kernel(E, cap, *refs):
+    accs, lasts, ws, places = refs[:2], refs[2:4], refs[4:6], refs[6:8]
+    own_ref, *full_refs, keep_ref, send_ref = refs[8:]
+    half = ws[0].shape[1]
+    for j in range(2):
+        cols = slice(j * half, (j + 1) * half)
+        for t in (1, 0):
+            total = accs[t][:, cols] + dot(lasts[t][...], ws[j][...])
+            rounded = total.astype(BF16)
+            if t == 0:
+                own_ref[:, cols] = total
+            else:
+                first = 0
+                for full in full_refs:
+                    full[:, cols] = rounded[first : first + full.shape[0]]
+                    first += full.shape[0]
+            picked = dot(places[t][...], rounded)
+            for d in range(E // 2):
+                near, far = spread(d) ^ (PAIR * t), spread(d) ^ PAIR ^ (PAIR * t)
+                at = (2 * d + t) * cap
+                keep_ref[at : at + cap, cols] = picked[near * cap : (near + 1) * cap]
+                at = (2 * d + 1 - t) * cap
+                send_ref[at : at + cap, cols] = picked[far * cap : (far + 1) * cap].astype(BF16)
+
+
+def outgoing_kernel(keep_ref, got_ref, gain_ref, *outs):
+    scaled = ((keep_ref[...] + got_ref[...].astype(F32)) * gain_ref[...]).astype(BF16)
     count = outs[0].shape[0]
     for d, out in enumerate(outs):
         out[...] = scaled[d * count : (d + 1) * count]
 
 
 def gate_up_kernel(C, E, cap, order, *refs):
-    xs, gain_ref, w_ref, keep_ref, send_ref, x_s, part_s = refs[:E], *refs[E:]
+    xs, gain_ref, w_ref, keep_ref, send_ref, x_s, part_s = refs[: E // 2], *refs[E // 2 :]
     c = lax.axis_index("ctx")
     e = lax.axis_index("exp")
     own_rows = E * cap // C
@@ -225,10 +222,7 @@
     for d in range(E // 2):
         for t in range(2):
             at = aligned(jnp.bitwise_xor(e, spread(d) ^ (PAIR * t)) * cap, cap)
-            for j in range(2):
-                half = xs[d].shape[1]
-                cols = slice(j * half, (j + 1) * half)
-                x_s[pl.ds(at, cap), cols] = xs[j * (E // 2) + d][t * cap : (t + 1) * cap, :]
+            x_s[pl.ds(at, cap), :] = xs[d][t * cap : (t + 1) * cap, :]
     plain = x_s[...].astype(F32) / gain_ref[...]
     square = jnp.sum(plain * plain, axis=1, keepdims=True)
     lane = lax.broadcasted_iota(jnp.int32, (E * cap, 128), 1)
@@ -297,21 +291,25 @@
         refs[-1][d * cap : (d + 1) * cap, :] = x[cap:, :]
 
 
-def combine_kernel(E, cap, own0, own1, got0, got1, place_ref, gate_ref, *refs):
+def combine_kernel(E, cap, own, got0, got1, got2, place_ref, gate_ref, *refs):
     xs, far, out, x_s = refs[: E // 2], refs[E // 2], refs[E // 2 + 1], refs[E // 2 + 2]
     for d in range(E // 2):
         at = spread(d) * cap
         x_s[at : at + cap, :] = xs[d][:cap, :]
         at = (spread(d) ^ PAIR) * cap
         x_s[at : at + cap, :] = far[d * cap : (d + 1) * cap, :]
-    half = own0.shape[1]
-    for j, (own, got) in enumerate(((own0, got0), (own1, got1))):
+    half = own.shape[1] // 2
+    for j in range(2):
         cols = slice(j * half, (j + 1) * half)
         collected = lax.dot_general(
             place_ref[...], x_s[:, cols], (((0,), (0,)), ((), ())), preferred_element_type=F32
         )
-        mixed = own[...] + got[...].astype(F32)
-        out[:, cols] = (mixed + gate_ref[:, :1] * collected).astype(BF16)
+        first = 0
+        for got in (got0, got1, got2):
+            at = slice(first, first + got.shape[0])
+            first += got.shape[0]
+            mixed = own[at, cols] + got[:, cols].astype(F32)
+            out[at, cols] = (mixed + gate_ref[at, :1] * collected[at]).astype(BF16)
 
 
 def body(
@@ -369,17 +367,7 @@
     for d in range(2, C, 2):
         shards[d] = [permute(half_a, exp=spread(d)), None]
     step = [shards[1][1]] + [shards[d][0] for d in range(2, C, 2)]
-    tokens_last = lambda x: jnp.transpose(x.reshape(C, tok, x.shape[3]), (0, 2, 1))
-    place, gate = call(
-        functools.partial(route_kernel, E, cap),
-        [sds((slots, rows), BF16), sds((rows, 128), F32)],
-        2,
-        scratch=[pltpu.VMEM((8, rows), jnp.int32), pltpu.VMEM((128, rows), F32)],
-        cost=(0, 2**20),
-        limit=16,
-    )(tokens_last(after(routes, msgs[0])), tokens_last(after(gates, msgs[0])))
-    other_place = permute(place, exp=PAIR)
-    got[1] = after(got[1], other_place, *step)
+    got[1] = after(got[1], *step)
     shards[1][0] = permute(after(half_a, *step), exp=1)
     for d in range(2, C, 2):
         shards[d][1] = permute(after(half_b, *step), exp=spread(d))
@@ -396,7 +384,7 @@
             sds((rows, qw), BF16),
             C,
             scratch=[pltpu.VMEM((2 * rows, 2 * HEAD_SIZE), BF16), pltpu.VMEM((rows, qw), BF16)],
-            cost=(4 * rows * 2 * rows * qw, 8 * 2**20),
+            cost=(0, 2**14),
             limit=16,
         )(*msgs)
 
@@ -411,8 +399,18 @@
             atts[s + 1] = permute(after(atts[s], *before), ctx=1)
         return [atts[s] for s in range(C)]
 
-    mine_all = gather(after(mine, *step), [])
-    theirs_all = gather(after(theirs, mine), [])
+    tokens_last = lambda x: jnp.transpose(x.reshape(C, tok, x.shape[3]), (0, 2, 1))
+    place, gate = call(
+        functools.partial(route_kernel, E, cap),
+        [sds((slots, rows), BF16), sds((rows, 128), F32)],
+        2,
+        scratch=[pltpu.VMEM((8, rows), jnp.int32), pltpu.VMEM((128, rows), F32)],
+        cost=(0, 2**20),
+        limit=16,
+    )(tokens_last(after(routes, other)), tokens_last(after(gates, other)))
+    other_place = permute(after(place, theirs), exp=PAIR)
+    mine_all = gather(mine, [])
+    theirs_all = gather(after(theirs, mine, *step), [])
 
     def project(atts, *extra):
         operands = [*shards[0], *extra, *atts]
@@ -428,38 +426,36 @@
                 pltpu.SemaphoreType.DMA((3,)),
             ],
             in_specs=[ANY] * (2 + len(extra)) + [VMEM] * (len(operands) - 2 - len(extra)),
-            cost=(2 * rows * qw * width * (C - 1), 4 * 2**20),
+            cost=(0, 2**14),
         )(*operands)
 
     acc, last = project(mine_all, res)
     acc_far, last_far = project(theirs_all)
     gain = norm_gain.reshape(1, width)
-    own, full, outgoing, incoming = [], [], [], []
-    for j in range(2):
-        mine_j, full_j, keep, send = call(
-            functools.partial(last_kernel, E, cap, j),
-            [
-                sds((rows, half), F32),
-                sds((rows, half), BF16),
-                sds((slots, half), F32),
-                sds((slots, half), BF16),
-            ],
-            7,
-            cost=(4 * rows * (qw + slots) * half, 3 * 2**20),
-        )(acc, acc_far, last, last_far, shards[C - 1][j], place, other_place)
-        own.append(mine_j)
-        full.append(full_j)
-        rows_out = call(
-            functools.partial(outgoing_kernel, j),
-            [sds((2 * cap, half), BF16)] * (E // 2),
-            3,
-            cost=(0, 2**20),
-        )(keep, after(permute(send, exp=PAIR), *incoming), gain)
-        came = {0: rows_out[0]}
-        for d in reversed(range(1, E // 2)):
-            came[d] = permute(rows_out[d], exp=spread(d))
-        incoming += [came[d] for d in range(E // 2)]
-    arrived = [permute(after(full[0], incoming[E // 2 + 1]), exp=PAIR)]
+    parts = (rows // 4, rows // 8, rows * 5 // 8)
+    own, *full, keep, send = call(
+        functools.partial(last_kernel, E, cap),
+        [
+            sds((rows, width), F32),
+            *[sds((n, width), BF16) for n in parts],
+            sds((slots, width), F32),
+            sds((slots, width), BF16),
+        ],
+        8,
+        cost=(4 * rows * (qw + slots) * width, 2**20),
+    )(acc, acc_far, last, last_far, *shards[C - 1], place, other_place)
+    received = permute(send, exp=PAIR)
+    outgoing = call(
+        outgoing_kernel, [sds((2 * cap, width), BF16)] * (E // 2), 3, cost=(0, 2**20)
+    )(keep, received, gain)
+    incoming = {0: outgoing[0]}
+    for d in reversed(range(1, E // 2)):
+        incoming[d] = permute(outgoing[d], exp=spread(d))
+    incoming = [incoming[d] for d in range(E // 2)]
+    arrived = [permute(after(full[0], received), exp=PAIR)]
+    incoming[0] = after(incoming[0], arrived[0])
+    arrived.append(permute(after(full[1], arrived[0]), exp=PAIR))
+    arrived.append(permute(after(full[2], arrived[1]), exp=PAIR))
 
     order = [0]
     bit = C // 2
@@ -469,11 +465,11 @@
     keep, send = call(
         functools.partial(gate_up_kernel, C, E, cap, order),
         [sds((slots // 2, wide + 128), F32), sds((slots // 2, wide + 128), BF16)],
-        E + 2,
+        E // 2 + 2,
         scratch=[pltpu.VMEM((slots, width), BF16), pltpu.VMEM((slots, wide + 128), F32)],
         cost=(2 * slots * width * wide, 2 * width * wide),
     )(*incoming, gain, w_gate_up.reshape(width, wide))
-    arrived.append(permute(after(full[1], keep), exp=PAIR))
+    keep = after(keep, arrived[1])
     bit = 1
     while 2 * bit < C:
         count = keep.shape[0] // 2
@@ -489,7 +485,7 @@
         sds((own_rows, hidden), BF16),
         2,
         cost=(0, 2**20),
-    )(after(keep, arrived[0]), permute(send, ctx=bit))
+    )(keep, permute(send, ctx=bit))
     acts = {0: activated}
     while bit:
         for r in list(acts):
@@ -501,7 +497,7 @@
         C + 1,
         scratch=[pltpu.VMEM((slots, hidden), BF16), pltpu.VMEM((slots, width), BF16)],
         cost=(2 * slots * width * hidden, 2 * width * hidden),
-    )(after(acts[0], arrived[1]), *[acts[s] for s in range(1, C)], w_down.reshape(hidden, width))
+    )(after(acts[0], arrived[2]), *[acts[s] for s in range(1, C)], w_down.reshape(hidden, width))
     returned = [expert_out[0]]
     returned += [permute(expert_out[d], exp=spread(d)) for d in reversed(range(1, E // 2))][::-1]
     far = call(
@@ -513,7 +509,7 @@
         7 + E // 2,
         scratch=[pltpu.VMEM((slots, width), BF16)],
         cost=(0, 2 * 2**20),
-    )(*own, *arrived, place, gate, *returned, permute(far, exp=PAIR))
+    )(own, *arrived, place, gate, *returned, permute(far, exp=PAIR))
     return result.reshape(C, 1, tok, width)
 
 

time: 130 us -> 123 us (0.946)
  starting transfers between devices: 48.4 us -> 34.8 us
  waiting for transfers between devices: 61.2 us -> 67 us
    ppermute x36 -> x33, starting transfers between devices: 48.4 us -> 34.8 us  [permute(): return lax.ppermute(x, ('ctx', 'exp'), pairs)]
    ppermute x36 -> x33, waiting for transfers between devices: 61.2 us -> 67 us  [permute(): return lax.ppermute(x, ('ctx', 'exp'), pairs)]
  transfers between devices with their start and end apart: 36 -> 33, of which waited for: 21 -> 17; matrix products, arithmetic and copies ran while one was open for 0% -> 0% of each run, Pallas kernels for 7% -> 6%
where the time goes in v5:
time: 123 us
  waiting for transfers between devices  67 us (54%)
  starting transfers between devices  34.8 us (28%)
  Pallas kernels  15.5 us (13%)
  local copies, waits for them, and re-layouts  5.53 us (4%)
    ppermute x33, waiting for transfers between devices, permute(): return lax.ppermute(x, ('ctx', 'exp'), pairs)  67 us
    ppermute x33, starting transfers between devices, permute(): return lax.ppermute(x, ('ctx', 'exp'), pairs)  34.8 us
    unnamed x20, local copies, waits for them, and re-layouts  5.53 us
    pallas_call x2, Pallas kernels, attend(): call(functools.partial(attend_kernel, C, t), sds((rows, qw), BF16), C, sc...  4.66 us
    pallas_call x1, Pallas kernels, body(): call(functools.partial(pack_kernel, C, qw), [sds((tok, 2 * qw + 2 * kv),...  3.39 us
  transfers between devices with their start and end apart: 33, of which 17 were waited for; matrix products, arithmetic and copies ran while one was open for 0% of the time, Pallas kernels for 6%

profile of v5, /device:TPU:0, one launch (start us, length us, event | category | flops | bytes accessed | tf_op | source)
XLA Modules:
  0.0 123.0 jit_solution(16000638851988384376)
XLA Ops:
  0.0 3.4 %shard_map.100 = (bf16[64,2048]{1,0:T(8,128)(2,1)}, bf16[64,2048]{1,0:T(8,128)(2,1)}, bf16[64,2048]{1,0:T(8,128)(2,1)}, bf16[64,2048]{1,0:T(8,128)(2,1)}, bf16[5...) custom-call(bf16[64,4096]{1,0:T(8,128)(2,1)} %bitcast.24, bf16[64,512]{1,0:T(8,128)(2,1)} %bitcast.26, ...), custom_call_target="tpu_custom_call" | custom-call | bytes 4194304 | tf_op jit(solution)/shard_map/pallas_call | solution.py:348
  3.4 3.1 %collective-permute-start.2 = (bf16[512,512]{1,0:T(8,128)(2,1)}, bf16[512,512]{1,0:T(8,128)(2,1)S(1)}, u32[]{:S(2)}, u32[]{:S(2)}) collective-permute-start(bf16[512,512]{1,0:T(8,128)(2,1)} %get-tuple-element.61.refs_0_), channel_id=1, source_target_pairs={{0,2},{1,3},{2,0},{3,1},{4,6},{5,7},{6,4},{7,5},{8,10},{9,11},{10,... | collective-permute-start | bytes 1572872 | tf_op jit(solution)/shard_map/ppermute | solution.py:341
  6.5 1.5 %collective-permute-start.1 = (bf16[512,512]{1,0:T(8,128)(2,1)}, bf16[512,512]{1,0:T(8,128)(2,1)S(1)}, u32[]{:S(2)}, u32[]{:S(2)}) collective-permute-start(bf16[512,512]{1,0:T(8,128)(2,1)} %get-tuple-element.62.refs_1_), channel_id=1, source_target_pairs={{0,1},{1,0},{2,3},{3,2},{4,5},{5,4},{6,7},{7,6},{8,9},{9,8},{10,11... | collective-permute-start | bytes 1572872 | tf_op jit(solution)/shard_map/ppermute | solution.py:341
  8.0 1.5 %collective-permute-start.3 = (bf16[64,2048]{1,0:T(8,128)(2,1)}, bf16[64,2048]{1,0:T(8,128)(2,1)S(1)}, u32[]{:S(2)}, u32[]{:S(2)}) collective-permute-start(bf16[64,2048]{1,0:T(8,128)(2,1)} %get-tuple-element.58), channel_id=1, source_target_pairs={{0,16},{1,17},{2,18},{3,19},{4,20},{5,21},{6,22},{7,23},{8,24},{9,... | collective-permute-start | bytes 786440 | tf_op jit(solution)/shard_map/ppermute | solution.py:341
  9.8 8.8 %collective-permute-done.2.refs_9_.refs_8_ = bf16[512,512]{1,0:T(8,128)(2,1)S(1)} collective-permute-done((bf16[512,512]{1,0:T(8,128)(2,1)}, bf16[512,512]{1,0:T(8,128)(2,1)S(1)}, u32[]{:S(2)}, u32[]{:S(2)}) %collective-permute-start.2) | collective-permute-done | bytes 524320 | tf_op jit(solution)/shard_map/ppermute | solution.py:341
  18.6 1.5 %collective-permute-done.1.refs_8_.refs_7_ = bf16[512,512]{1,0:T(8,128)(2,1)S(1)} collective-permute-done((bf16[512,512]{1,0:T(8,128)(2,1)}, bf16[512,512]{1,0:T(8,128)(2,1)S(1)}, u32[]{:S(2)}, u32[]{:S(2)}) %collective-permute-start.1) | collective-permute-done | bytes 524320 | tf_op jit(solution)/shard_map/ppermute | solution.py:341
  20.1 1.5 %collective-permute-start.8 = (bf16[512,512]{1,0:T(8,128)(2,1)}, bf16[512,512]{1,0:T(8,128)(2,1)S(1)}, u32[]{:S(2)}, u32[]{:S(2)}) collective-permute-start(bf16[512,512]{1,0:T(8,128)(2,1)} %get-tuple-element.61.refs_0_), channel_id=1, source_target_pairs={{0,1},{1,0},{2,3},{3,2},{4,5},{5,4},{6,7},{7,6},{8,9},{9,8},{10,11... | collective-permute-start | bytes 1572872 | tf_op jit(solution)/shard_map/ppermute | solution.py:341
  22.1 0.9 copy-done.3
  23.1 2.3 %shard_map.101 = bf16[256,512]{1,0:T(8,128)(2,1)S(1)} custom-call(bf16[64,2048]{1,0:T(8,128)(2,1)S(1)} %copy-done.3, bf16[64,2048]{1,0:T(8,128)(2,1)S(1)} %collective-permute-done.refs_1_, bf16[64,2048]{1,0:T(8,128)(2,1)S(1)} %collective-permute-done.3.refs_2_, bf16[64,2048]{1,0:T(8,128)(2,1)S(1)} %collective-permute-done.4.refs_3_), custom_call_target="tpu_custom_call" | custom-call | bytes 16384 | tf_op jit(solution)/shard_map/pallas_call | solution.py:382
  25.4 2.7 %collective-permute-start.10 = (bf16[256,512]{1,0:T(8,128)(2,1)S(1)}, bf16[256,512]{1,0:T(8,128)(2,1)S(1)}, u32[]{:S(2)}, u32[]{:S(2)}) collective-permute-start(bf16[256,512]{1,0:T(8,128)(2,1)S(1)} %shard_map.101), channel_id=1, source_target_pairs={{0,4},{1,5},{2,6},{3,7},{4,0},{5,1},{6,2},{7,3},{8,12},{9,13},{10,... | collective-permute-start | bytes 786440 | tf_op jit(solution)/shard_map/ppermute | solution.py:341
  28.1 2.3 %shard_map.102.refs_3_ = bf16[256,512]{1,0:T(8,128)(2,1)S(1)} custom-call(bf16[64,2048]{1,0:T(8,128)(2,1)S(1)} %copy-done.3, bf16[64,2048]{1,0:T(8,128)(2,1)S(1)} %collective-permute-done.refs_1_, bf16[64,2048]{1,0:T(8,128)(2,1)S(1)} %collective-permute-done.3.refs_2_, bf16[64,2048]{1,0:T(8,128)(2,1)S(1)} %collective-permute-done.4.refs_3_), custom_call_target="tpu_custom_call" | custom-call | bytes 16384 | tf_op jit(solution)/shard_map/pallas_call | solution.py:382
  30.4 1.6 %collective-permute-start.6 = (bf16[256,512]{1,0:T(8,128)(2,1)S(1)}, bf16[256,512]{1,0:T(8,128)(2,1)S(1)}, u32[]{:S(2)}, u32[]{:S(2)}) collective-permute-start(bf16[256,512]{1,0:T(8,128)(2,1)S(1)} %shard_map.102.refs_3_), channel_id=1, source_target_pairs={{0,16},{1,17},{2,18},{3,19},{4,20},{5,21},{6,22},{7,23},{8,24},{9,... | collective-permute-start | bytes 786440 | tf_op jit(solution)/shard_map/ppermute | solution.py:341
  32.0 5.8 %collective-permute-done.10.refs_2_ = bf16[256,512]{1,0:T(8,128)(2,1)S(1)} collective-permute-done((bf16[256,512]{1,0:T(8,128)(2,1)S(1)}, bf16[256,512]{1,0:T(8,128)(2,1)S(1)}, u32[]{:S(2)}, u32[]{:S(2)}) %collective-permute-start.10) | collective-permute-done | bytes 262176 | tf_op jit(solution)/shard_map/ppermute | solution.py:341
  37.8 1.8 %collective-permute-done.9.refs_10_.refs_9_ = bf16[512,512]{1,0:T(8,128)(2,1)S(1)} collective-permute-done((bf16[512,512]{1,0:T(8,128)(2,1)}, bf16[512,512]{1,0:T(8,128)(2,1)S(1)}, u32[]{:S(2)}, u32[]{:S(2)}) %collective-permute-start.9) | collective-permute-done | bytes 524320 | tf_op jit(solution)/shard_map/ppermute | solution.py:341
  39.6 1.5 %collective-permute-start.12 = (bf16[256,512]{1,0:T(8,128)(2,1)S(1)}, bf16[256,512]{1,0:T(8,128)(2,1)S(1)}, u32[]{:S(2)}, u32[]{:S(2)}) collective-permute-start(bf16[256,512]{1,0:T(8,128)(2,1)S(1)} %collective-permute-done.10.refs_2_), channel_id=1, source_target_pairs={{0,16},{1,17},{2,18},{3,19},{4,20},{5,21},{6,22},{7,23},{8,24},{9,... | collective-permute-start | bytes 786440 | tf_op jit(solution)/shard_map/ppermute | solution.py:341
  41.6 2.6 %collective-permute-start.15 = (bf16[512,512]{1,0:T(8,128)(2,1)S(1)}, bf16[512,512]{1,0:T(8,128)(2,1)S(1)}, u32[]{:S(2)}, u32[]{:S(2)}) collective-permute-start(bf16[512,512]{1,0:T(8,128)(2,1)S(1)} %collective-permute-done.1.refs_8_.refs_7_), channel_id=1, source_target_pairs={{0,2},{1,3},{2,0},{3,1},{4,6},{5,7},{6,4},{7,5},{8,10},{9,11},{10,... | collective-permute-start | bytes 1572872 | tf_op jit(solution)/shard_map/ppermute | solution.py:341
  44.3 1.7 %collective-permute-done.12.refs_4_ = bf16[256,512]{1,0:T(8,128)(2,1)S(1)} collective-permute-done((bf16[256,512]{1,0:T(8,128)(2,1)S(1)}, bf16[256,512]{1,0:T(8,128)(2,1)S(1)}, u32[]{:S(2)}, u32[]{:S(2)}) %collective-permute-start.12) | collective-permute-done | bytes 262176 | tf_op jit(solution)/shard_map/ppermute | solution.py:341
  46.5 0.7 copy-done.5
  47.2 0.7 copy-done.6
  48.2 1.7 %collective-permute-start.16 = (bf16[128,256]{1,0:T(8,128)(2,1)S(1)}, bf16[128,256]{1,0:T(8,128)(2,1)S(1)}, u32[]{:S(2)}, u32[]{:S(2)}) collective-permute-start(bf16[128,256]{1,0:T(8,128)(2,1)S(1)} %get-tuple-element.73.refs_6_.place_ref), channel_id=1, source_target_pairs={{0,4},{1,5},{2,6},{3,7},{4,0},{5,1},{6,2},{7,3},{8,12},{9,13},{10,... | collective-permute-start | bytes 196616 | tf_op jit(solution)/shard_map/ppermute | solution.py:341
  49.9 1.0 copy-done.1
  50.9 1.0 copy-done.2
  51.9 1.0 copy-done.4
  53.0 1.2 shard_map.103
  54.3 1.2 shard_map.104
  55.5 1.4 %shard_map.106 = (f32[256,1024]{1,0:T(8,128)S(1)}, bf16[64,1024]{1,0:T(8,128)(2,1)S(1)}, bf16[32,1024]{1,0:T(8,128)(2,1)S(1)}, bf16[160,1024]{1,0:T(8,128)(2,1)S...) custom-call(f32[256,1024]{1,0:T(8,128)S(1)} %get-tuple-element.63.refs_0_, ...), custom_call_target="tpu_custom_call" | custom-call | flops 671088640 | bytes 1048576 | tf_op jit(solution)/shard_map/pallas_call | solution.py:436
  56.9 1.8 %collective-permute-start.17 = (bf16[128,1024]{1,0:T(8,128)(2,1)S(1)}, bf16[128,1024]{1,0:T(8,128)(2,1)S(1)}, u32[]{:S(2)}, u32[]{:S(2)}) collective-permute-start(bf16[128,1024]{1,0:T(8,128)(2,1)S(1)} %get-tuple-element.76), channel_id=1, source_target_pairs={{0,4},{1,5},{2,6},{3,7},{4,0},{5,1},{6,2},{7,3},{8,12},{9,13},{10,... | collective-permute-start | bytes 786440 | tf_op jit(solution)/shard_map/ppermute | solution.py:341
  58.7 12.7 %collective-permute-done.17.got_ref = bf16[128,1024]{1,0:T(8,128)(2,1)S(1)} collective-permute-done((bf16[128,1024]{1,0:T(8,128)(2,1)S(1)}, bf16[128,1024]{1,0:T(8,128)(2,1)S(1)}, u32[]{:S(2)}, u32[]{:S(2)}) %collective-permute-start.17) | collective-permute-done | bytes 262176 | tf_op jit(solution)/shard_map/ppermute | solution.py:341
  71.5 0.7 collective-permute-start.21
  72.2 2.7 %collective-permute-start.22 = (bf16[32,1024]{1,0:T(8,128)(2,1)S(1)}, bf16[32,1024]{1,0:T(8,128)(2,1)S(1)}, u32[]{:S(2)}, u32[]{:S(2)}) collective-permute-start(bf16[32,1024]{1,0:T(8,128)(2,1)S(1)} %get-tuple-element.87), channel_id=1, source_target_pairs={{0,2},{1,3},{2,0},{3,1},{4,6},{5,7},{6,4},{7,5},{8,10},{9,11},{10,... | collective-permute-start | bytes 196616 | tf_op jit(solution)/shard_map/ppermute | solution.py:341
  74.9 0.9 collective-permute-start.23
  75.8 3.6 %collective-permute-done.18.got0 = bf16[64,1024]{1,0:T(8,128)(2,1)S(1)} collective-permute-done((bf16[64,1024]{1,0:T(8,128)(2,1)S(1)}, bf16[64,1024]{1,0:T(8,128)(2,1)S(1)}, u32[]{:S(2)}, u32[]{:S(2)}) %collective-permute-start.18) | collective-permute-done | bytes 131104 | tf_op jit(solution)/shard_map/ppermute | solution.py:341
  79.5 1.7 %collective-permute-done.23.refs_3_ = bf16[32,1024]{1,0:T(8,128)(2,1)S(1)} collective-permute-done((bf16[32,1024]{1,0:T(8,128)(2,1)S(1)}, bf16[32,1024]{1,0:T(8,128)(2,1)S(1)}, u32[]{:S(2)}, u32[]{:S(2)}) %collective-permute-start.23) | collective-permute-done | bytes 65568 | tf_op jit(solution)/shard_map/ppermute | solution.py:341
  81.2 1.3 %shard_map.108 = (f32[64,3200]{1,0:T(8,128)S(1)}, bf16[64,3200]{1,0:T(8,128)(2,1)S(1)}) custom-call(bf16[32,1024]{1,0:T(8,128)(2,1)S(1)} %get-tuple-element.85.refs_0_, bf16[32,1024]{1,0:T(8,128)(2,1)S(1)} %collective-permute-done.21.refs_1_, bf16[32,1024]{1,0:T(8,128)(2,1)S(1)} %collective-permute-done.22.refs_2_, ...), custom_call_target="tpu_custom_call" | custom-call | flops 805306368 | bytes 6291456 | tf_op jit(solution)/shard_map/pallas_call | solution.py:465
  82.6 6.0 %collective-permute-done.19.got1 = bf16[32,1024]{1,0:T(8,128)(2,1)S(1)} collective-permute-done((bf16[32,1024]{1,0:T(8,128)(2,1)S(1)}, bf16[32,1024]{1,0:T(8,128)(2,1)S(1)}, u32[]{:S(2)}, u32[]{:S(2)}) %collective-permute-start.19) | collective-permute-done | bytes 65568 | tf_op jit(solution)/shard_map/ppermute | solution.py:341
  88.7 1.6 %collective-permute-start.25 = (bf16[32,3200]{1,0:T(8,128)(2,1)S(1)}, bf16[32,3200]{1,0:T(8,128)(2,1)S(1)}, u32[]{:S(2)}, u32[]{:S(2)}) collective-permute-start(bf16[32,3200]{1,0:T(8,128)(2,1)S(1)} %get-tuple-element.93), channel_id=1, source_target_pairs={{0,16},{1,17},{2,18},{3,19},{4,20},{5,21},{6,22},{7,23},{8,24},{9,... | collective-permute-start | bytes 614408 | tf_op jit(solution)/shard_map/ppermute | solution.py:341
  90.3 5.5 %collective-permute-done.25.got_ref = bf16[32,3200]{1,0:T(8,128)(2,1)S(1)} collective-permute-done((bf16[32,3200]{1,0:T(8,128)(2,1)S(1)}, bf16[32,3200]{1,0:T(8,128)(2,1)S(1)}, u32[]{:S(2)}, u32[]{:S(2)}) %collective-permute-start.25) | collective-permute-done | bytes 204832 | tf_op jit(solution)/shard_map/ppermute | solution.py:341
  96.0 1.6 %collective-permute-start.27 = (bf16[32,1536]{1,0:T(8,128)(2,1)S(1)}, bf16[32,1536]{1,0:T(8,128)(2,1)S(1)}, u32[]{:S(2)}, u32[]{:S(2)}) collective-permute-start(bf16[32,1536]{1,0:T(8,128)(2,1)S(1)} %shard_map.110.refs_0_), channel_id=1, source_target_pairs={{0,16},{1,17},{2,18},{3,19},{4,20},{5,21},{6,22},{7,23},{8,24},{9,... | collective-permute-start | bytes 294920 | tf_op jit(solution)/shard_map/ppermute | solution.py:341
  97.6 3.1 %collective-permute-done.27.refs_2_ = bf16[32,1536]{1,0:T(8,128)(2,1)S(1)} collective-permute-done((bf16[32,1536]{1,0:T(8,128)(2,1)S(1)}, bf16[32,1536]{1,0:T(8,128)(2,1)S(1)}, u32[]{:S(2)}, u32[]{:S(2)}) %collective-permute-start.27) | collective-permute-done | bytes 98336 | tf_op jit(solution)/shard_map/ppermute | solution.py:341
  100.7 6.1 %collective-permute-done.20.got2 = bf16[160,1024]{1,0:T(8,128)(2,1)S(1)} collective-permute-done((bf16[160,1024]{1,0:T(8,128)(2,1)S(1)}, bf16[160,1024]{1,0:T(8,128)(2,1)S(1)}, u32[]{:S(2)}, u32[]{:S(2)}) %collective-permute-start.20) | collective-permute-done | bytes 327712 | tf_op jit(solution)/shard_map/ppermute | solution.py:341
  107.5 0.8 collective-permute-start.29
  108.3 2.8 %collective-permute-start.31 = (bf16[32,1024]{1,0:T(8,128)(2,1)S(1)}, bf16[32,1024]{1,0:T(8,128)(2,1)S(1)}, u32[]{:S(2)}, u32[]{:S(2)}) collective-permute-start(bf16[32,1024]{1,0:T(8,128)(2,1)S(1)} %get-tuple-element.98), channel_id=1, source_target_pairs={{0,3},{1,2},{2,1},{3,0},{4,7},{5,6},{6,5},{7,4},{8,11},{9,10},{10,... | collective-permute-start | bytes 196616 | tf_op jit(solution)/shard_map/ppermute | solution.py:341
  111.1 0.8 collective-permute-done.29.refs_1_
  111.8 0.9 collective-permute-done.30.refs_2_
  112.8 1.4 %collective-permute-done.31.refs_3_ = bf16[32,1024]{1,0:T(8,128)(2,1)S(1)} collective-permute-done((bf16[32,1024]{1,0:T(8,128)(2,1)S(1)}, bf16[32,1024]{1,0:T(8,128)(2,1)S(1)}, u32[]{:S(2)}, u32[]{:S(2)}) %collective-permute-start.31) | collective-permute-done | bytes 65568 | tf_op jit(solution)/shard_map/ppermute | solution.py:341
  114.2 2.3 %collective-permute-start.32 = (bf16[64,1024]{1,0:T(8,128)(2,1)S(1)}, bf16[64,1024]{1,0:T(8,128)(2,1)S(1)}, u32[]{:S(2)}, u32[]{:S(2)}) collective-permute-start(bf16[64,1024]{1,0:T(8,128)(2,1)S(1)} %shard_map.112), channel_id=1, source_target_pairs={{0,4},{1,5},{2,6},{3,7},{4,0},{5,1},{6,2},{7,3},{8,12},{9,13},{10,... | collective-permute-start | bytes 393224 | tf_op jit(solution)/shard_map/ppermute | solution.py:341
  116.5 5.4 %collective-permute-done.32.refs_4_ = bf16[64,1024]{1,0:T(8,128)(2,1)S(1)} collective-permute-done((bf16[64,1024]{1,0:T(8,128)(2,1)S(1)}, bf16[64,1024]{1,0:T(8,128)(2,1)S(1)}, u32[]{:S(2)}, u32[]{:S(2)}) %collective-permute-start.32) | collective-permute-done | bytes 131104 | tf_op jit(solution)/shard_map/ppermute | solution.py:341
  121.9 1.1 shard_map.113
  (53 shorter events, 3.4 us)
Async XLA Ops:
  3.4 15.2 %collective-permute-start.2 = (bf16[512,512]{1,0:T(8,128)(2,1)}, bf16[512,512]{1,0:T(8,128)(2,1)S(1)}, u32[]{:S(2)}, u32[]{:S(2)}) collective-permute-start(bf16[512,512]{1,0:T(8,128)(2,1)} %get-tuple-element.61.refs_0_), channel_id=1, source_target_pairs={{0,2},{1,3},{2,0},{3,1},{4,6},{5,7},{6,4},{7,5},{8,10},{9,11},{10,... | collective-permute-start | bytes 1572872 | tf_op jit(solution)/shard_map/ppermute | solution.py:341
  6.5 13.6 %collective-permute-start.1 = (bf16[512,512]{1,0:T(8,128)(2,1)}, bf16[512,512]{1,0:T(8,128)(2,1)S(1)}, u32[]{:S(2)}, u32[]{:S(2)}) collective-permute-start(bf16[512,512]{1,0:T(8,128)(2,1)} %get-tuple-element.62.refs_1_), channel_id=1, source_target_pairs={{0,1},{1,0},{2,3},{3,2},{4,5},{5,4},{6,7},{7,6},{8,9},{9,8},{10,11... | collective-permute-start | bytes 1572872 | tf_op jit(solution)/shard_map/ppermute | solution.py:341
  8.0 14.0 %collective-permute-start = (bf16[64,2048]{1,0:T(8,128)(2,1)}, bf16[64,2048]{1,0:T(8,128)(2,1)S(1)}, u32[]{:S(2)}, u32[]{:S(2)}) collective-permute-start(bf16[64,2048]{1,0:T(8,128)(2,1)} %get-tuple-element.56), channel_id=1, source_target_pairs={{0,8},{1,9},{2,10},{3,11},{4,12},{5,13},{6,14},{7,15},{8,0},{9,1},... | collective-permute-start | bytes 786440 | tf_op jit(solution)/shard_map/ppermute | solution.py:341
  8.0 14.0 %collective-permute-start.3 = (bf16[64,2048]{1,0:T(8,128)(2,1)}, bf16[64,2048]{1,0:T(8,128)(2,1)S(1)}, u32[]{:S(2)}, u32[]{:S(2)}) collective-permute-start(bf16[64,2048]{1,0:T(8,128)(2,1)} %get-tuple-element.58), channel_id=1, source_target_pairs={{0,16},{1,17},{2,18},{3,19},{4,20},{5,21},{6,22},{7,23},{8,24},{9,... | collective-permute-start | bytes 786440 | tf_op jit(solution)/shard_map/ppermute | solution.py:341
  9.5 12.6 %collective-permute-start.4 = (bf16[64,2048]{1,0:T(8,128)(2,1)}, bf16[64,2048]{1,0:T(8,128)(2,1)S(1)}, u32[]{:S(2)}, u32[]{:S(2)}) collective-permute-start(bf16[64,2048]{1,0:T(8,128)(2,1)} %get-tuple-element.59), channel_id=1, source_target_pairs={{0,24},{1,25},{2,26},{3,27},{4,28},{5,29},{6,30},{7,31},{8,16},{9,... | collective-permute-start | bytes 786440 | tf_op jit(solution)/shard_map/ppermute | solution.py:341
  20.1 17.7 %collective-permute-start.8 = (bf16[512,512]{1,0:T(8,128)(2,1)}, bf16[512,512]{1,0:T(8,128)(2,1)S(1)}, u32[]{:S(2)}, u32[]{:S(2)}) collective-permute-start(bf16[512,512]{1,0:T(8,128)(2,1)} %get-tuple-element.61.refs_0_), channel_id=1, source_target_pairs={{0,1},{1,0},{2,3},{3,2},{4,5},{5,4},{6,7},{7,6},{8,9},{9,8},{10,11... | collective-permute-start | bytes 1572872 | tf_op jit(solution)/shard_map/ppermute | solution.py:341
  21.6 18.0 %collective-permute-start.9 = (bf16[512,512]{1,0:T(8,128)(2,1)}, bf16[512,512]{1,0:T(8,128)(2,1)S(1)}, u32[]{:S(2)}, u32[]{:S(2)}) collective-permute-start(bf16[512,512]{1,0:T(8,128)(2,1)} %get-tuple-element.62.refs_1_), channel_id=1, source_target_pairs={{0,2},{1,3},{2,0},{3,1},{4,6},{5,7},{6,4},{7,5},{8,10},{9,11},{10,... | collective-permute-start | bytes 1572872 | tf_op jit(solution)/shard_map/ppermute | solution.py:341
  22.1 1.0 copy-start.3
  25.4 12.3 %collective-permute-start.10 = (bf16[256,512]{1,0:T(8,128)(2,1)S(1)}, bf16[256,512]{1,0:T(8,128)(2,1)S(1)}, u32[]{:S(2)}, u32[]{:S(2)}) collective-permute-start(bf16[256,512]{1,0:T(8,128)(2,1)S(1)} %shard_map.101), channel_id=1, source_target_pairs={{0,4},{1,5},{2,6},{3,7},{4,0},{5,1},{6,2},{7,3},{8,12},{9,13},{10,... | collective-permute-start | bytes 786440 | tf_op jit(solution)/shard_map/ppermute | solution.py:341
  30.4 13.8 %collective-permute-start.6 = (bf16[256,512]{1,0:T(8,128)(2,1)S(1)}, bf16[256,512]{1,0:T(8,128)(2,1)S(1)}, u32[]{:S(2)}, u32[]{:S(2)}) collective-permute-start(bf16[256,512]{1,0:T(8,128)(2,1)S(1)} %shard_map.102.refs_3_), channel_id=1, source_target_pairs={{0,16},{1,17},{2,18},{3,19},{4,20},{5,21},{6,22},{7,23},{8,24},{9,... | collective-permute-start | bytes 786440 | tf_op jit(solution)/shard_map/ppermute | solution.py:341
  32.0 14.0 %collective-permute-start.5 = (bf16[256,512]{1,0:T(8,128)(2,1)S(1)}, bf16[256,512]{1,0:T(8,128)(2,1)S(1)}, u32[]{:S(2)}, u32[]{:S(2)}) collective-permute-start(bf16[256,512]{1,0:T(8,128)(2,1)S(1)} %shard_map.102.refs_3_), channel_id=1, source_target_pairs={{0,8},{1,9},{2,10},{3,11},{4,12},{5,13},{6,14},{7,15},{8,0},{9,1},... | collective-permute-start | bytes 786440 | tf_op jit(solution)/shard_map/ppermute | solution.py:341
  39.6 6.4 %collective-permute-start.12 = (bf16[256,512]{1,0:T(8,128)(2,1)S(1)}, bf16[256,512]{1,0:T(8,128)(2,1)S(1)}, u32[]{:S(2)}, u32[]{:S(2)}) collective-permute-start(bf16[256,512]{1,0:T(8,128)(2,1)S(1)} %collective-permute-done.10.refs_2_), channel_id=1, source_target_pairs={{0,16},{1,17},{2,18},{3,19},{4,20},{5,21},{6,22},{7,23},{8,24},{9,... | collective-permute-start | bytes 786440 | tf_op jit(solution)/shard_map/ppermute | solution.py:341
  41.1 14.4 %collective-permute-start.14 = (bf16[512,512]{1,0:T(8,128)(2,1)S(1)}, bf16[512,512]{1,0:T(8,128)(2,1)S(1)}, u32[]{:S(2)}, u32[]{:S(2)}) collective-permute-start(bf16[512,512]{1,0:T(8,128)(2,1)S(1)} %collective-permute-done.2.refs_9_.refs_8_), channel_id=1, source_target_pairs={{0,1},{1,0},{2,3},{3,2},{4,5},{5,4},{6,7},{7,6},{8,9},{9,8},{10,11... | collective-permute-start | bytes 1572872 | tf_op jit(solution)/shard_map/ppermute | solution.py:341
  41.6 13.8 %collective-permute-start.15 = (bf16[512,512]{1,0:T(8,128)(2,1)S(1)}, bf16[512,512]{1,0:T(8,128)(2,1)S(1)}, u32[]{:S(2)}, u32[]{:S(2)}) collective-permute-start(bf16[512,512]{1,0:T(8,128)(2,1)S(1)} %collective-permute-done.1.refs_8_.refs_7_), channel_id=1, source_target_pairs={{0,2},{1,3},{2,0},{3,1},{4,6},{5,7},{6,4},{7,5},{8,10},{9,11},{10,... | collective-permute-start | bytes 1572872 | tf_op jit(solution)/shard_map/ppermute | solution.py:341
  44.3 3.9 %collective-permute-start.7 = (bf16[256,512]{1,0:T(8,128)(2,1)S(1)}, bf16[256,512]{1,0:T(8,128)(2,1)S(1)}, u32[]{:S(2)}, u32[]{:S(2)}) collective-permute-start(bf16[256,512]{1,0:T(8,128)(2,1)S(1)} %collective-permute-done.6.refs_5_), channel_id=1, source_target_pairs={{0,8},{1,9},{2,10},{3,11},{4,12},{5,13},{6,14},{7,15},{8,0},{9,1},... | collective-permute-start | bytes 786440 | tf_op jit(solution)/shard_map/ppermute | solution.py:341
  46.0 8.3 %collective-permute-start.11 = (bf16[256,512]{1,0:T(8,128)(2,1)S(1)}, bf16[256,512]{1,0:T(8,128)(2,1)S(1)}, u32[]{:S(2)}, u32[]{:S(2)}) collective-permute-start(bf16[256,512]{1,0:T(8,128)(2,1)S(1)} %collective-permute-done.10.refs_2_), channel_id=1, source_target_pairs={{0,8},{1,9},{2,10},{3,11},{4,12},{5,13},{6,14},{7,15},{8,0},{9,1},... | collective-permute-start | bytes 786440 | tf_op jit(solution)/shard_map/ppermute | solution.py:341
  46.0 8.3 %collective-permute-start.13 = (bf16[256,512]{1,0:T(8,128)(2,1)S(1)}, bf16[256,512]{1,0:T(8,128)(2,1)S(1)}, u32[]{:S(2)}, u32[]{:S(2)}) collective-permute-start(bf16[256,512]{1,0:T(8,128)(2,1)S(1)} %collective-permute-done.12.refs_4_), channel_id=1, source_target_pairs={{0,8},{1,9},{2,10},{3,11},{4,12},{5,13},{6,14},{7,15},{8,0},{9,1},... | collective-permute-start | bytes 786440 | tf_op jit(solution)/shard_map/ppermute | solution.py:341
  46.5 0.7 copy-start.5
  47.2 0.7 copy-start.6
  48.2 7.3 %collective-permute-start.16 = (bf16[128,256]{1,0:T(8,128)(2,1)S(1)}, bf16[128,256]{1,0:T(8,128)(2,1)S(1)}, u32[]{:S(2)}, u32[]{:S(2)}) collective-permute-start(bf16[128,256]{1,0:T(8,128)(2,1)S(1)} %get-tuple-element.73.refs_6_.place_ref), channel_id=1, source_target_pairs={{0,4},{1,5},{2,6},{3,7},{4,0},{5,1},{6,2},{7,3},{8,12},{9,13},{10,... | collective-permute-start | bytes 196616 | tf_op jit(solution)/shard_map/ppermute | solution.py:341
  49.9 1.0 copy-start.1
  50.9 1.0 copy-start.2
  51.9 1.0 copy-start.4
  53.0 18.5 %copy-start.7 = (f32[1024]{0:T(1024)S(1)}, f32[1024]{0:T(1024)}, u32[]{:S(2)}) copy-start(f32[1024]{0:T(1024)} %param.15) | copy-start | bytes 12292
  53.0 28.2 %slice-start = ((s8[6291456]{0:T(1024)(128)(4,1)}), s8[4194304]{0:T(1024)(128)(4,1)S(1)}, s32[]{:S(2)}) async-start(s8[6291456]{0:T(1024)(128)(4,1)} %bitcast.16), calls=%async_computation | async-start | bytes 8388608
  54.2 27.0 %slice-start.1 = ((s8[6291456]{0:T(1024)(128)(4,1)}), s8[2097152]{0:T(1024)(128)(4,1)S(1)}, s32[]{:S(2)}) async-start(s8[6291456]{0:T(1024)(128)(4,1)} %bitcast.16), calls=%async_computation.1 | async-start | bytes 4194304
  55.5 51.3 %copy-start = (bf16[1,1536,1024]{2,1,0:T(8,128)(2,1)S(1)}, bf16[1,1536,1024]{2,1,0:T(8,128)(2,1)}, u32[]{:S(2)}) copy-start(bf16[1,1536,1024]{2,1,0:T(8,128)(2,1)} %param.19) | copy-start | bytes 9437188
  56.9 14.5 %collective-permute-start.17 = (bf16[128,1024]{1,0:T(8,128)(2,1)S(1)}, bf16[128,1024]{1,0:T(8,128)(2,1)S(1)}, u32[]{:S(2)}, u32[]{:S(2)}) collective-permute-start(bf16[128,1024]{1,0:T(8,128)(2,1)S(1)} %get-tuple-element.76), channel_id=1, source_target_pairs={{0,4},{1,5},{2,6},{3,7},{4,0},{5,1},{6,2},{7,3},{8,12},{9,13},{10,... | collective-permute-start | bytes 786440 | tf_op jit(solution)/shard_map/ppermute | solution.py:341
  71.4 8.0 %collective-permute-start.18 = (bf16[64,1024]{1,0:T(8,128)(2,1)S(1)}, bf16[64,1024]{1,0:T(8,128)(2,1)S(1)}, u32[]{:S(2)}, u32[]{:S(2)}) collective-permute-start(bf16[64,1024]{1,0:T(8,128)(2,1)S(1)} %get-tuple-element.77), channel_id=1, source_target_pairs={{0,4},{1,5},{2,6},{3,7},{4,0},{5,1},{6,2},{7,3},{8,12},{9,13},{10,... | collective-permute-start | bytes 393224 | tf_op jit(solution)/shard_map/ppermute | solution.py:341
  71.5 8.0 %collective-permute-start.21 = (bf16[32,1024]{1,0:T(8,128)(2,1)S(1)}, bf16[32,1024]{1,0:T(8,128)(2,1)S(1)}, u32[]{:S(2)}, u32[]{:S(2)}) collective-permute-start(bf16[32,1024]{1,0:T(8,128)(2,1)S(1)} %get-tuple-element.86), channel_id=1, source_target_pairs={{0,1},{1,0},{2,3},{3,2},{4,5},{5,4},{6,7},{7,6},{8,9},{9,8},{10,11... | collective-permute-start | bytes 196616 | tf_op jit(solution)/shard_map/ppermute | solution.py:341
  72.2 7.3 %collective-permute-start.22 = (bf16[32,1024]{1,0:T(8,128)(2,1)S(1)}, bf16[32,1024]{1,0:T(8,128)(2,1)S(1)}, u32[]{:S(2)}, u32[]{:S(2)}) collective-permute-start(bf16[32,1024]{1,0:T(8,128)(2,1)S(1)} %get-tuple-element.87), channel_id=1, source_target_pairs={{0,2},{1,3},{2,0},{3,1},{4,6},{5,7},{6,4},{7,5},{8,10},{9,11},{10,... | collective-permute-start | bytes 196616 | tf_op jit(solution)/shard_map/ppermute | solution.py:341
  74.9 6.3 %collective-permute-start.23 = (bf16[32,1024]{1,0:T(8,128)(2,1)S(1)}, bf16[32,1024]{1,0:T(8,128)(2,1)S(1)}, u32[]{:S(2)}, u32[]{:S(2)}) collective-permute-start(bf16[32,1024]{1,0:T(8,128)(2,1)S(1)} %get-tuple-element.88), channel_id=1, source_target_pairs={{0,3},{1,2},{2,1},{3,0},{4,7},{5,6},{6,5},{7,4},{8,11},{9,10},{10,... | collective-permute-start | bytes 196616 | tf_op jit(solution)/shard_map/ppermute | solution.py:341
  82.5 6.1 %collective-permute-start.24 = (bf16[64,3200]{1,0:T(8,128)(2,1)S(1)}, bf16[64,3200]{1,0:T(8,128)(2,1)S(1)}, u32[]{:S(2)}, u32[]{:S(2)}) collective-permute-start(bf16[64,3200]{1,0:T(8,128)(2,1)S(1)} %get-tuple-element.91), channel_id=1, source_target_pairs={{0,8},{1,9},{2,10},{3,11},{4,12},{5,13},{6,14},{7,15},{8,0},{9,1},... | collective-permute-start | bytes 1228808 | tf_op jit(solution)/shard_map/ppermute | solution.py:341
  82.5 6.1 %collective-permute-start.19 = (bf16[32,1024]{1,0:T(8,128)(2,1)S(1)}, bf16[32,1024]{1,0:T(8,128)(2,1)S(1)}, u32[]{:S(2)}, u32[]{:S(2)}) collective-permute-start(bf16[32,1024]{1,0:T(8,128)(2,1)S(1)} %get-tuple-element.79), channel_id=1, source_target_pairs={{0,4},{1,5},{2,6},{3,7},{4,0},{5,1},{6,2},{7,3},{8,12},{9,13},{10,... | collective-permute-start | bytes 196616 | tf_op jit(solution)/shard_map/ppermute | solution.py:341
  88.7 7.1 %collective-permute-start.25 = (bf16[32,3200]{1,0:T(8,128)(2,1)S(1)}, bf16[32,3200]{1,0:T(8,128)(2,1)S(1)}, u32[]{:S(2)}, u32[]{:S(2)}) collective-permute-start(bf16[32,3200]{1,0:T(8,128)(2,1)S(1)} %get-tuple-element.93), channel_id=1, source_target_pairs={{0,16},{1,17},{2,18},{3,19},{4,20},{5,21},{6,22},{7,23},{8,24},{9,... | collective-permute-start | bytes 614408 | tf_op jit(solution)/shard_map/ppermute | solution.py:341
  90.3 16.5 %collective-permute-start.20 = (bf16[160,1024]{1,0:T(8,128)(2,1)S(1)}, bf16[160,1024]{1,0:T(8,128)(2,1)S(1)}, u32[]{:S(2)}, u32[]{:S(2)}) collective-permute-start(bf16[160,1024]{1,0:T(8,128)(2,1)S(1)} %get-tuple-element.81), channel_id=1, source_target_pairs={{0,4},{1,5},{2,6},{3,7},{4,0},{5,1},{6,2},{7,3},{8,12},{9,13},{10,... | collective-permute-start | bytes 983048 | tf_op jit(solution)/shard_map/ppermute | solution.py:341
  96.0 4.7 %collective-permute-start.27 = (bf16[32,1536]{1,0:T(8,128)(2,1)S(1)}, bf16[32,1536]{1,0:T(8,128)(2,1)S(1)}, u32[]{:S(2)}, u32[]{:S(2)}) collective-permute-start(bf16[32,1536]{1,0:T(8,128)(2,1)S(1)} %shard_map.110.refs_0_), channel_id=1, source_target_pairs={{0,16},{1,17},{2,18},{3,19},{4,20},{5,21},{6,22},{7,23},{8,24},{9,... | collective-permute-start | bytes 294920 | tf_op jit(solution)/shard_map/ppermute | solution.py:341
  97.6 9.2 %collective-permute-start.26 = (bf16[32,1536]{1,0:T(8,128)(2,1)S(1)}, bf16[32,1536]{1,0:T(8,128)(2,1)S(1)}, u32[]{:S(2)}, u32[]{:S(2)}) collective-permute-start(bf16[32,1536]{1,0:T(8,128)(2,1)S(1)} %shard_map.110.refs_0_), channel_id=1, source_target_pairs={{0,8},{1,9},{2,10},{3,11},{4,12},{5,13},{6,14},{7,15},{8,0},{9,1},... | collective-permute-start | bytes 294920 | tf_op jit(solution)/shard_map/ppermute | solution.py:341
  100.7 6.1 %collective-permute-start.28 = (bf16[32,1536]{1,0:T(8,128)(2,1)S(1)}, bf16[32,1536]{1,0:T(8,128)(2,1)S(1)}, u32[]{:S(2)}, u32[]{:S(2)}) collective-permute-start(bf16[32,1536]{1,0:T(8,128)(2,1)S(1)} %collective-permute-done.27.refs_2_), channel_id=1, source_target_pairs={{0,8},{1,9},{2,10},{3,11},{4,12},{5,13},{6,14},{7,15},{8,0},{9,1},... | collective-permute-start | bytes 294920 | tf_op jit(solution)/shard_map/ppermute | solution.py:341
  107.5 4.3 %collective-permute-start.29 = (bf16[32,1024]{1,0:T(8,128)(2,1)S(1)}, bf16[32,1024]{1,0:T(8,128)(2,1)S(1)}, u32[]{:S(2)}, u32[]{:S(2)}) collective-permute-start(bf16[32,1024]{1,0:T(8,128)(2,1)S(1)} %get-tuple-element.96), channel_id=1, source_target_pairs={{0,1},{1,0},{2,3},{3,2},{4,5},{5,4},{6,7},{7,6},{8,9},{9,8},{10,11... | collective-permute-start | bytes 196616 | tf_op jit(solution)/shard_map/ppermute | solution.py:341
  108.3 4.5 %collective-permute-start.30 = (bf16[32,1024]{1,0:T(8,128)(2,1)S(1)}, bf16[32,1024]{1,0:T(8,128)(2,1)S(1)}, u32[]{:S(2)}, u32[]{:S(2)}) collective-permute-start(bf16[32,1024]{1,0:T(8,128)(2,1)S(1)} %get-tuple-element.97), channel_id=1, source_target_pairs={{0,2},{1,3},{2,0},{3,1},{4,6},{5,7},{6,4},{7,5},{8,10},{9,11},{10,... | collective-permute-start | bytes 196616 | tf_op jit(solution)/shard_map/ppermute | solution.py:341
  108.3 5.9 %collective-permute-start.31 = (bf16[32,1024]{1,0:T(8,128)(2,1)S(1)}, bf16[32,1024]{1,0:T(8,128)(2,1)S(1)}, u32[]{:S(2)}, u32[]{:S(2)}) collective-permute-start(bf16[32,1024]{1,0:T(8,128)(2,1)S(1)} %get-tuple-element.98), channel_id=1, source_target_pairs={{0,3},{1,2},{2,1},{3,0},{4,7},{5,6},{6,5},{7,4},{8,11},{9,10},{10,... | collective-permute-start | bytes 196616 | tf_op jit(solution)/shard_map/ppermute | solution.py:341
  114.2 7.7 %collective-permute-start.32 = (bf16[64,1024]{1,0:T(8,128)(2,1)S(1)}, bf16[64,1024]{1,0:T(8,128)(2,1)S(1)}, u32[]{:S(2)}, u32[]{:S(2)}) collective-permute-start(bf16[64,1024]{1,0:T(8,128)(2,1)S(1)} %shard_map.112), channel_id=1, source_target_pairs={{0,4},{1,5},{2,6},{3,7},{4,0},{5,1},{6,2},{7,3},{8,12},{9,13},{10,... | collective-permute-start | bytes 393224 | tf_op jit(solution)/shard_map/ppermute | solution.py:341

commit v6 on v5

--- a/solution.py
+++ b/solution.py
@@ -42,6 +42,7 @@
 
 
 PAIR = 4
+PACK_LIMIT = 57
 
 
 def spread(d):
@@ -57,40 +58,45 @@
     return pl.multiple_of(x, n)
 
 
-def pack_kernel(C, qw, q_ref, new_ref, past_ref, w_ref, res_ref, *refs):
-    outs, halves, res_out, sems = refs[:C], refs[C : C + 2], refs[C + 2], refs[C + 3]
+def run_copies(pairs, sems):
+    copies = [pltpu.make_async_copy(src, dst, sems.at[i]) for i, (src, dst) in enumerate(pairs)]
+    for c in copies:
+        c.start()
+    for c in copies:
+        c.wait()
+
+
+def pack_kernel(C, qw, q_ref, new_ref, past_ref, *refs):
+    outs, sems = refs[:C], refs[C]
     c = lax.axis_index("ctx")
     _, lo = own_hi_lo()
-    copies = []
-
-    def copy(src, dst):
-        copies.append(pltpu.make_async_copy(src, dst, sems.at[len(copies)]))
-        copies[-1].start()
-
-    half = halves[0].shape[1]
     kv = new_ref.shape[1]
-    for j in (1, 0):
-        copy(w_ref.at[:, j * half : (j + 1) * half], halves[j])
+    pairs = []
     for s in reversed(range(C)):
         target = jnp.bitwise_xor(c, s)
         out = outs[s]
         for t in range(2):
             shard = lax.div(target, PAIR) * 2 * PAIR + lax.rem(target, PAIR)
             shard = shard + PAIR * jnp.bitwise_xor(lo, t)
-            copy(q_ref.at[:, pl.ds(aligned(shard * qw, 128), qw)], out.at[:, t * qw : (t + 1) * qw])
-        copy(new_ref, out.at[:, 2 * qw : 2 * qw + kv])
-        copy(past_ref, out.at[:, 2 * qw + kv :])
-    copy(res_ref, res_out)
-    for c in copies:
-        c.wait()
+            at = pl.ds(aligned(shard * qw, 128), qw)
+            pairs.append((q_ref.at[:, at], out.at[:, t * qw : (t + 1) * qw]))
+        pairs.append((new_ref, out.at[:, 2 * qw : 2 * qw + kv]))
+        pairs.append((past_ref, out.at[:, 2 * qw + kv :]))
+    run_copies(pairs, sems)
+
+
+def halve_weight_kernel(w_ref, a_ref, b_ref, sems):
+    half = a_ref.shape[1]
+    run_copies([(w_ref.at[:, half:], b_ref), (w_ref.at[:, :half], a_ref)], sems)
 
 
 def attend_kernel(C, t, *refs):
-    msgs, out, kv_s = refs[:C], refs[C], refs[C + 1]
+    msgs, out, kv_s, q_s = refs[:C], refs[C], refs[-2], refs[-1]
+    if t == 1:
+        refs[C + 1][...] = msgs[0][...]
     c = lax.axis_index("ctx")
     tok, qw = msgs[0].shape[0], out.shape[1]
     rows = C * tok
-    q_s = refs[C + 2]
     _, lo = own_hi_lo()
     shard = lax.div(c, PAIR) * 2 * PAIR + lax.rem(c, PAIR) + PAIR * jnp.bitwise_xor(lo, t)
     head = lax.div(shard * (qw // HEAD_SIZE), GROUP_EXTENT)
@@ -121,7 +127,10 @@
             out[at, h * HEAD_SIZE : (h + 1) * HEAD_SIZE] = (numerator / total).astype(BF16)
 
 
-def route_kernel(E, cap, routes_ref, gates_ref, place_ref, gate_ref, line_s, gate_s):
+def route_kernel(E, cap, routes_ref, gates_ref, *refs):
+    place_ref, gate_ref, line_s, gate_s = refs[3], refs[4], refs[-2], refs[-1]
+    for src, dst in zip(refs[:3], refs[5:8]):
+        dst[...] = src[...]
     e = lax.axis_index("exp")
     blocks, _, tok = routes_ref.shape
     rows = blocks * tok
@@ -154,13 +163,8 @@
     own_w, refs = refs[:2], refs[2:]
     if with_residual:
         res, refs = refs[0], refs[1:]
-    atts, ws, (acc, last, stacked, w_s, res_s, sems) = refs[:C], refs[C : 3 * C - 4], refs[3 * C - 4 :]
+    atts, ws, (acc, last, stacked) = refs[:C], refs[C : 3 * C - 4], refs[3 * C - 4 :]
     hi, _ = own_hi_lo()
-    copies = [pltpu.make_async_copy(own_w[j], w_s.at[j], sems.at[j]) for j in range(2)]
-    if with_residual:
-        copies.append(pltpu.make_async_copy(res, res_s, sems.at[2]))
-    for c in copies:
-        c.start()
     turn = jnp.bitwise_xor(lax.axis_index("ctx"), hi)
     for s in range(C):
         stacked[jnp.bitwise_xor(turn, s)] = atts[s][...]
@@ -169,15 +173,12 @@
     for j in range(2):
         at = slice(j * half, (j + 1) * half)
         total = None
-        for d in range(1, C - 1):
-            term = dot(stacked[d], ws[2 * (d - 1) + j][...])
+        for d in range(C - 1):
+            w = own_w[j] if d == 0 else ws[2 * (d - 1) + j]
+            term = dot(stacked[d], w[...])
             total = term if total is None else total + term
-        if j == 0:
-            for c in copies:
-                c.wait()
-        total = total + dot(stacked[0], w_s[j])
         if with_residual:
-            total = total + res_s[:, at].astype(F32)
+            total = total + res[:, at].astype(F32)
         acc[:, at] = total
 
 
@@ -291,7 +292,7 @@
         refs[-1][d * cap : (d + 1) * cap, :] = x[cap:, :]
 
 
-def combine_kernel(E, cap, own, got0, got1, got2, place_ref, gate_ref, *refs):
+def combine_kernel(E, cap, own, got0, got1, place_ref, gate_ref, *refs):
     xs, far, out, x_s = refs[: E // 2], refs[E // 2], refs[E // 2 + 1], refs[E // 2 + 2]
     for d in range(E // 2):
         at = spread(d) * cap
@@ -304,10 +305,8 @@
         collected = lax.dot_general(
             place_ref[...], x_s[:, cols], (((0,), (0,)), ((), ())), preferred_element_type=F32
         )
-        first = 0
-        for got in (got0, got1, got2):
-            at = slice(first, first + got.shape[0])
-            first += got.shape[0]
+        few = got0.shape[0]
+        for got, at in ((got0, slice(0, few)), (got1, slice(few, own.shape[0]))):
             mixed = own[at, cols] + got[:, cols].astype(F32)
             out[at, cols] = (mixed + gate_ref[at, :1] * collected[at]).astype(BF16)
 
@@ -345,29 +344,38 @@
 
     half = width // 2
     kv = new_keys_values.shape[3]
-    *msgs, half_a, half_b, res = call(
+    msgs = call(
         functools.partial(pack_kernel, C, qw),
-        [sds((tok, 2 * qw + 2 * kv), BF16)] * C
-        + [sds((qw, half), BF16)] * 2
-        + [sds((rows, width), BF16)],
-        5,
-        scratch=[pltpu.SemaphoreType.DMA((4 * C + 3,))],
-        in_specs=[HBM] * 5,
-        cost=(0, 4 * 2**20),
-        limit=57,
+        [sds((tok, 2 * qw + 2 * kv), BF16)] * C,
+        3,
+        scratch=[pltpu.SemaphoreType.DMA((4 * C,))],
+        in_specs=[HBM] * 3,
+        out_specs=[ANY] * C,
+        cost=(0, 2**20),
+        limit=PACK_LIMIT,
     )(
         queries.reshape(tok, queries.shape[3]),
-        new_keys_values.reshape(tok, new_keys_values.shape[3]),
-        cached_keys_values.reshape(tok, cached_keys_values.shape[3]),
-        out_weight,
-        residual.reshape(rows, width),
+        new_keys_values.reshape(tok, kv),
+        cached_keys_values.reshape(tok, kv),
     )
+    half_a, half_b = call(
+        halve_weight_kernel,
+        [sds((qw, half), BF16)] * 2,
+        1,
+        scratch=[pltpu.SemaphoreType.DMA((2,))],
+        in_specs=[HBM],
+        out_specs=[ANY] * 2,
+        cost=(0, 2**20),
+        limit=PACK_LIMIT,
+    )(after(out_weight, msgs[0]))
+    res = residual.reshape(rows, width)
     got = [msgs[0]] + [permute(msgs[s], ctx=s) for s in range(1, C)]
     shards = {0: [half_a, half_b], 1: [None, permute(half_b, exp=1)]}
     for d in range(2, C, 2):
         shards[d] = [permute(half_a, exp=spread(d)), None]
     step = [shards[1][1]] + [shards[d][0] for d in range(2, C, 2)]
     got[1] = after(got[1], *step)
+    step += got[1:]
     shards[1][0] = permute(after(half_a, *step), exp=1)
     for d in range(2, C, 2):
         shards[d][1] = permute(after(half_b, *step), exp=spread(d))
@@ -378,19 +386,33 @@
             permute(after(shards[1][1], *step), exp=spread(d - 1)),
         ]
 
+    step2 = step
+
     def attend(t, msgs):
         return call(
             functools.partial(attend_kernel, C, t),
-            sds((rows, qw), BF16),
+            [sds((rows, qw), BF16)] + [sds(msgs[0].shape, BF16)] * t,
             C,
             scratch=[pltpu.VMEM((2 * rows, 2 * HEAD_SIZE), BF16), pltpu.VMEM((rows, qw), BF16)],
             cost=(0, 2**14),
             limit=16,
         )(*msgs)
 
-    other = attend(1, got)
+    other, own_msg = attend(1, got)
     theirs = permute(other, exp=PAIR)
-    mine = attend(0, [got[0], after(got[1], other)] + got[2:])
+    (mine,) = attend(0, [own_msg, after(got[1], other)] + got[2:])
+    tokens_last = lambda x: jnp.transpose(x.reshape(C, tok, x.shape[3]), (0, 2, 1))
+    place, gate, *staged = call(
+        functools.partial(route_kernel, E, cap),
+        [sds((slots, rows), BF16), sds((rows, 128), F32)]
+        + [sds((qw, half), BF16)] * 2
+        + [sds((rows, width), BF16)],
+        5,
+        scratch=[pltpu.VMEM((8, rows), jnp.int32), pltpu.VMEM((128, rows), F32)],
+        cost=(0, 2**14),
+        limit=16,
+    )(tokens_last(after(routes, mine)), tokens_last(after(gates, mine)), half_a, half_b, res)
+    shards[0], res = staged[:2], staged[2]
 
     def gather(x, before):
         atts = {0: x, 1: permute(x, ctx=1)}
@@ -399,18 +421,11 @@
             atts[s + 1] = permute(after(atts[s], *before), ctx=1)
         return [atts[s] for s in range(C)]
 
-    tokens_last = lambda x: jnp.transpose(x.reshape(C, tok, x.shape[3]), (0, 2, 1))
-    place, gate = call(
-        functools.partial(route_kernel, E, cap),
-        [sds((slots, rows), BF16), sds((rows, 128), F32)],
-        2,
-        scratch=[pltpu.VMEM((8, rows), jnp.int32), pltpu.VMEM((128, rows), F32)],
-        cost=(0, 2**20),
-        limit=16,
-    )(tokens_last(after(routes, other)), tokens_last(after(gates, other)))
     other_place = permute(after(place, theirs), exp=PAIR)
+    step = shards[C - 1]
     mine_all = gather(mine, [])
-    theirs_all = gather(after(theirs, mine, *step), [])
+    theirs_all = gather(after(theirs, place, *step2), [])
+    mine_all[1] = after(mine_all[1], other_place, *step)
 
     def project(atts, *extra):
         operands = [*shards[0], *extra, *atts]
@@ -421,18 +436,14 @@
             len(operands),
             scratch=[
                 pltpu.VMEM((C, rows, qw), BF16),
-                pltpu.VMEM((2, qw, half), BF16),
-                pltpu.VMEM((rows, width), BF16),
-                pltpu.SemaphoreType.DMA((3,)),
             ],
-            in_specs=[ANY] * (2 + len(extra)) + [VMEM] * (len(operands) - 2 - len(extra)),
             cost=(0, 2**14),
         )(*operands)
 
     acc, last = project(mine_all, res)
     acc_far, last_far = project(theirs_all)
     gain = norm_gain.reshape(1, width)
-    parts = (rows // 4, rows // 8, rows * 5 // 8)
+    parts = (rows * 3 // 8, rows * 5 // 8)
     own, *full, keep, send = call(
         functools.partial(last_kernel, E, cap),
         [
@@ -455,7 +466,6 @@
     arrived = [permute(after(full[0], received), exp=PAIR)]
     incoming[0] = after(incoming[0], arrived[0])
     arrived.append(permute(after(full[1], arrived[0]), exp=PAIR))
-    arrived.append(permute(after(full[2], arrived[1]), exp=PAIR))
 
     order = [0]
     bit = C // 2
@@ -469,7 +479,6 @@
         scratch=[pltpu.VMEM((slots, width), BF16), pltpu.VMEM((slots, wide + 128), F32)],
         cost=(2 * slots * width * wide, 2 * width * wide),
     )(*incoming, gain, w_gate_up.reshape(width, wide))
-    keep = after(keep, arrived[1])
     bit = 1
     while 2 * bit < C:
         count = keep.shape[0] // 2
@@ -487,6 +496,8 @@
         cost=(0, 2**20),
     )(keep, permute(send, ctx=bit))
     acts = {0: activated}
+    acts[bit] = after(permute(activated, ctx=bit), arrived[1])
+    bit //= 2
     while bit:
         for r in list(acts):
             acts[r ^ bit] = permute(acts[r], ctx=bit)
@@ -497,7 +508,7 @@
         C + 1,
         scratch=[pltpu.VMEM((slots, hidden), BF16), pltpu.VMEM((slots, width), BF16)],
         cost=(2 * slots * width * hidden, 2 * width * hidden),
-    )(after(acts[0], arrived[2]), *[acts[s] for s in range(1, C)], w_down.reshape(hidden, width))
+    )(acts[0], *[acts[s] for s in range(1, C)], w_down.reshape(hidden, width))
     returned = [expert_out[0]]
     returned += [permute(expert_out[d], exp=spread(d)) for d in reversed(range(1, E // 2))][::-1]
     far = call(
@@ -506,7 +517,7 @@
     result = call(
         functools.partial(combine_kernel, E, cap),
         sds((rows, width), BF16),
-        7 + E // 2,
+        6 + E // 2,
         scratch=[pltpu.VMEM((slots, width), BF16)],
         cost=(0, 2 * 2**20),
     )(own, *arrived, place, gate, *returned, permute(far, exp=PAIR))

time: 123 us -> 185 us (1.50)
  Pallas kernels: 15.5 us -> 77.8 us
    pallas_call x2 -> x3, Pallas kernels: 4.66 us -> 37.6 us  [the longest x1 32.9 us: body(): call(halve_weight_kernel, [sds((qw, half), BF16)] * 2, 1, scratch=[pltpu....]
    pallas_call x1, Pallas kernels: 3.39 us -> 33 us  [body(): call(functools.partial(pack_kernel, C, qw), [sds((tok, 2 * qw + 2 * kv),...]
    ppermute x33 -> x32, starting transfers between devices: 34.8 us -> 33.8 us  [permute(): return lax.ppermute(x, ('ctx', 'exp'), pairs)]
    ppermute x33 -> x32, waiting for transfers between devices: 67 us -> 67.6 us  [permute(): return lax.ppermute(x, ('ctx', 'exp'), pairs)]
  transfers between devices with their start and end apart: 33 -> 32, of which waited for: 17 -> 18; matrix products, arithmetic and copies ran while one was open for 0% -> 0% of each run, Pallas kernels for 6% -> 3%
where the time goes in v6:
time: 185 us
  Pallas kernels  77.8 us (42%)
  waiting for transfers between devices  67.6 us (37%)
  starting transfers between devices  33.8 us (18%)
  local copies, waits for them, and re-layouts  5.53 us (3%)
    ppermute x32, waiting for transfers between devices, permute(): return lax.ppermute(x, ('ctx', 'exp'), pairs)  67.6 us
    ppermute x32, starting transfers between devices, permute(): return lax.ppermute(x, ('ctx', 'exp'), pairs)  33.8 us
    pallas_call x1, Pallas kernels, body(): call(functools.partial(pack_kernel, C, qw), [sds((tok, 2 * qw + 2 * kv),...  33 us
    pallas_call x1, Pallas kernels, body(): call(halve_weight_kernel, [sds((qw, half), BF16)] * 2, 1, scratch=[pltpu....  32.9 us
    unnamed x20, local copies, waits for them, and re-layouts  5.53 us
    pallas_call x2, Pallas kernels, attend(): call(functools.partial(attend_kernel, C, t), [sds((rows, qw), BF16)] + [s...  4.68 us
  transfers between devices with their start and end apart: 32, of which 18 were waited for; matrix products, arithmetic and copies ran while one was open for 0% of the time, Pallas kernels for 3%

profile of v6, /device:TPU:0, one launch (start us, length us, event | category | flops | bytes accessed | tf_op | source)
XLA Modules:
  0.0 184.9 jit_solution(18157144126081577386)
XLA Ops:
  0.0 33.0 %shard_map.100 = (bf16[64,2048]{1,0:T(8,128)(2,1)}, bf16[64,2048]{1,0:T(8,128)(2,1)}, bf16[64,2048]{1,0:T(8,128)(2,1)}, bf16[64,2048]{1,0:T(8,128)(2,1)}) custom-call(bf16[64,4096]{1,0:T(8,128)(2,1)} %bitcast.25, bf16[64,512]{1,0:T(8,128)(2,1)} %bitcast.26, bf16[64,512]{1,0:T(8,128)(2,1)} %bitcast.27), custom_call_target="tpu_custom_call" | custom-call | bytes 1048576 | tf_op jit(solution)/shard_map/pallas_call | solution.py:347
  33.0 32.9 %shard_map.101 = (bf16[512,512]{1,0:T(8,128)(2,1)}, bf16[512,512]{1,0:T(8,128)(2,1)}) custom-call(bf16[512,1024]{1,0:T(8,128)(2,1)} %w_ref), custom_call_target="tpu_custom_call" | custom-call | bytes 1048576 | tf_op jit(solution)/shard_map/pallas_call | solution.py:361
  65.9 3.0 %collective-permute-start.1 = (bf16[512,512]{1,0:T(8,128)(2,1)}, bf16[512,512]{1,0:T(8,128)(2,1)S(1)}, u32[]{:S(2)}, u32[]{:S(2)}) collective-permute-start(bf16[512,512]{1,0:T(8,128)(2,1)} %get-tuple-element.74.refs_1_), channel_id=1, source_target_pairs={{0,1},{1,0},{2,3},{3,2},{4,5},{5,4},{6,7},{7,6},{8,9},{9,8},{10,11... | collective-permute-start | bytes 1572872 | tf_op jit(solution)/shard_map/ppermute | solution.py:340
  68.9 1.6 collective-permute-start.2
  70.5 1.5 collective-permute-start.3
  72.4 8.7 %collective-permute-done.1.refs_8_.refs_7_ = bf16[512,512]{1,0:T(8,128)(2,1)S(1)} collective-permute-done((bf16[512,512]{1,0:T(8,128)(2,1)}, bf16[512,512]{1,0:T(8,128)(2,1)S(1)}, u32[]{:S(2)}, u32[]{:S(2)}) %collective-permute-start.1) | collective-permute-done | bytes 524320 | tf_op jit(solution)/shard_map/ppermute | solution.py:340
  81.0 1.5 collective-permute-done.2.refs_9_.refs_8_
  82.5 2.1 %collective-permute-done.4.refs_3_ = bf16[64,2048]{1,0:T(8,128)(2,1)S(1)} collective-permute-done((bf16[64,2048]{1,0:T(8,128)(2,1)}, bf16[64,2048]{1,0:T(8,128)(2,1)S(1)}, u32[]{:S(2)}, u32[]{:S(2)}) %collective-permute-start.4) | collective-permute-done | bytes 262176 | tf_op jit(solution)/shard_map/ppermute | solution.py:340
  85.6 0.9 copy-done.4
  86.5 2.3 %shard_map.102 = (bf16[256,512]{1,0:T(8,128)(2,1)S(1)}, bf16[64,2048]{1,0:T(8,128)(2,1)S(1)}) custom-call(bf16[64,2048]{1,0:T(8,128)(2,1)S(1)} %copy-done.4, bf16[64,2048]{1,0:T(8,128)(2,1)S(1)} %collective-permute-done.refs_1_, bf16[64,2048]{1,0:T(8,128)(2,1)S(1)} %collective-permute-done.3.refs_2_, bf16[64,2048]{1,0:T(8,128)(2,1)S(1)} %collective-permute-done.4.refs_3_), custom_call_target="tpu_custom_call" | custom-call | bytes 16384 | tf_op jit(solution)/shard_map/pallas_call | solution.py:392
  88.9 2.7 %collective-permute-start.6 = (bf16[256,512]{1,0:T(8,128)(2,1)S(1)}, bf16[256,512]{1,0:T(8,128)(2,1)S(1)}, u32[]{:S(2)}, u32[]{:S(2)}) collective-permute-start(bf16[256,512]{1,0:T(8,128)(2,1)S(1)} %get-tuple-element.64), channel_id=1, source_target_pairs={{0,4},{1,5},{2,6},{3,7},{4,0},{5,1},{6,2},{7,3},{8,12},{9,13},{10,... | collective-permute-start | bytes 786440 | tf_op jit(solution)/shard_map/ppermute | solution.py:340
  91.6 2.3 %shard_map.103.refs_3_ = bf16[256,512]{1,0:T(8,128)(2,1)S(1)} custom-call(bf16[64,2048]{1,0:T(8,128)(2,1)S(1)} %get-tuple-element.63.refs_0_, bf16[64,2048]{1,0:T(8,128)(2,1)S(1)} %collective-permute-done.refs_1_, bf16[64,2048]{1,0:T(8,128)(2,1)S(1)} %collective-permute-done.3.refs_2_, bf16[64,2048]{1,0:T(8,128)(2,1)S(1)} %collective-permute-done.4.refs_3_), custom_call_target="tpu_custom_call" | custom-call | bytes 16384 | tf_op jit(solution)/shard_map/pallas_call | solution.py:392
  93.9 1.6 collective-permute-start.12
  95.5 1.0 copy-done.1
  96.6 1.0 copy-done.2
  97.6 1.0 copy-done.3
  98.6 0.7 copy-done.5
  99.4 0.7 copy-done.6
  100.4 4.4 %collective-permute-done.9.refs_10_.refs_9_ = bf16[512,512]{1,0:T(8,128)(2,1)S(1)} collective-permute-done((bf16[512,512]{1,0:T(8,128)(2,1)}, bf16[512,512]{1,0:T(8,128)(2,1)S(1)}, u32[]{:S(2)}, u32[]{:S(2)}) %collective-permute-start.9) | collective-permute-done | bytes 524320 | tf_op jit(solution)/shard_map/ppermute | solution.py:340
  104.8 1.5 collective-permute-start.10
  106.3 1.5 collective-permute-start.15
  107.8 3.0 %collective-permute-start.7 = (bf16[128,256]{1,0:T(8,128)(2,1)S(1)}, bf16[128,256]{1,0:T(8,128)(2,1)S(1)}, u32[]{:S(2)}, u32[]{:S(2)}) collective-permute-start(bf16[128,256]{1,0:T(8,128)(2,1)S(1)} %get-tuple-element.72.refs_6_.place_ref), channel_id=1, source_target_pairs={{0,4},{1,5},{2,6},{3,7},{4,0},{5,1},{6,2},{7,3},{8,12},{9,13},{10,... | collective-permute-start | bytes 196616 | tf_op jit(solution)/shard_map/ppermute | solution.py:340
  110.8 2.4 %collective-permute-done.15.refs_4_ = bf16[256,512]{1,0:T(8,128)(2,1)S(1)} collective-permute-done((bf16[256,512]{1,0:T(8,128)(2,1)S(1)}, bf16[256,512]{1,0:T(8,128)(2,1)S(1)}, u32[]{:S(2)}, u32[]{:S(2)}) %collective-permute-start.15) | collective-permute-done | bytes 262176 | tf_op jit(solution)/shard_map/ppermute | solution.py:340
  113.8 4.3 %collective-permute-done.7.refs_7_ = bf16[128,256]{1,0:T(8,128)(2,1)S(1)} collective-permute-done((bf16[128,256]{1,0:T(8,128)(2,1)S(1)}, bf16[128,256]{1,0:T(8,128)(2,1)S(1)}, u32[]{:S(2)}, u32[]{:S(2)}) %collective-permute-start.7) | collective-permute-done | bytes 65568 | tf_op jit(solution)/shard_map/ppermute | solution.py:340
  118.1 2.2 %collective-permute-done.11.refs_5_ = bf16[512,512]{1,0:T(8,128)(2,1)S(1)} collective-permute-done((bf16[512,512]{1,0:T(8,128)(2,1)S(1)}, bf16[512,512]{1,0:T(8,128)(2,1)S(1)}, u32[]{:S(2)}, u32[]{:S(2)}) %collective-permute-start.11) | collective-permute-done | bytes 524320 | tf_op jit(solution)/shard_map/ppermute | solution.py:340
  120.3 1.0 shard_map.105
  121.4 1.0 shard_map.106
  122.4 1.4 shard_map.107
  123.8 1.7 collective-permute-start.17
  125.5 12.2 %collective-permute-done.17.got_ref = bf16[128,1024]{1,0:T(8,128)(2,1)S(1)} collective-permute-done((bf16[128,1024]{1,0:T(8,128)(2,1)S(1)}, bf16[128,1024]{1,0:T(8,128)(2,1)S(1)}, u32[]{:S(2)}, u32[]{:S(2)}) %collective-permute-start.17) | collective-permute-done | bytes 262176 | tf_op jit(solution)/shard_map/ppermute | solution.py:340
  138.4 3.0 %collective-permute-start.21 = (bf16[32,1024]{1,0:T(8,128)(2,1)S(1)}, bf16[32,1024]{1,0:T(8,128)(2,1)S(1)}, u32[]{:S(2)}, u32[]{:S(2)}) collective-permute-start(bf16[32,1024]{1,0:T(8,128)(2,1)S(1)} %get-tuple-element.94), channel_id=1, source_target_pairs={{0,2},{1,3},{2,0},{3,1},{4,6},{5,7},{6,4},{7,5},{8,10},{9,11},{10,... | collective-permute-start | bytes 196616 | tf_op jit(solution)/shard_map/ppermute | solution.py:340
  141.4 1.0 collective-permute-start.22
  142.4 5.6 %collective-permute-done.18.got0 = bf16[96,1024]{1,0:T(8,128)(2,1)S(1)} collective-permute-done((bf16[96,1024]{1,0:T(8,128)(2,1)S(1)}, bf16[96,1024]{1,0:T(8,128)(2,1)S(1)}, u32[]{:S(2)}, u32[]{:S(2)}) %collective-permute-start.18) | collective-permute-done | bytes 196640 | tf_op jit(solution)/shard_map/ppermute | solution.py:340
  148.6 1.3 shard_map.109
  149.9 1.7 collective-permute-done.23.got_ref
  151.7 1.6 collective-permute-start.24
  153.3 5.6 %collective-permute-done.24.got_ref = bf16[32,3200]{1,0:T(8,128)(2,1)S(1)} collective-permute-done((bf16[32,3200]{1,0:T(8,128)(2,1)S(1)}, bf16[32,3200]{1,0:T(8,128)(2,1)S(1)}, u32[]{:S(2)}, u32[]{:S(2)}) %collective-permute-start.24) | collective-permute-done | bytes 204832 | tf_op jit(solution)/shard_map/ppermute | solution.py:340
  159.0 1.6 collective-permute-start.26
  160.6 6.5 %collective-permute-done.19.got1 = bf16[160,1024]{1,0:T(8,128)(2,1)S(1)} collective-permute-done((bf16[160,1024]{1,0:T(8,128)(2,1)S(1)}, bf16[160,1024]{1,0:T(8,128)(2,1)S(1)}, u32[]{:S(2)}, u32[]{:S(2)}) %collective-permute-start.19) | collective-permute-done | bytes 327712 | tf_op jit(solution)/shard_map/ppermute | solution.py:340
  167.2 1.2 collective-permute-done.27.refs_3_
  169.1 0.9 collective-permute-start.28
  170.0 2.7 %collective-permute-start.30 = (bf16[32,1024]{1,0:T(8,128)(2,1)S(1)}, bf16[32,1024]{1,0:T(8,128)(2,1)S(1)}, u32[]{:S(2)}, u32[]{:S(2)}) collective-permute-start(bf16[32,1024]{1,0:T(8,128)(2,1)S(1)} %get-tuple-element.104), channel_id=1, source_target_pairs={{0,3},{1,2},{2,1},{3,0},{4,7},{5,6},{6,5},{7,4},{8,11},{9,10},{10,... | collective-permute-start | bytes 196616 | tf_op jit(solution)/shard_map/ppermute | solution.py:340
  172.6 0.8 collective-permute-done.28.refs_1_
  173.4 1.1 collective-permute-done.29.refs_2_
  174.5 1.4 collective-permute-done.30.refs_3_
  175.9 2.5 %collective-permute-start.31 = (bf16[64,1024]{1,0:T(8,128)(2,1)S(1)}, bf16[64,1024]{1,0:T(8,128)(2,1)S(1)}, u32[]{:S(2)}, u32[]{:S(2)}) collective-permute-start(bf16[64,1024]{1,0:T(8,128)(2,1)S(1)} %shard_map.113), channel_id=1, source_target_pairs={{0,4},{1,5},{2,6},{3,7},{4,0},{5,1},{6,2},{7,3},{8,12},{9,13},{10,... | collective-permute-start | bytes 393224 | tf_op jit(solution)/shard_map/ppermute | solution.py:340
  178.4 5.4 %collective-permute-done.31.refs_4_ = bf16[64,1024]{1,0:T(8,128)(2,1)S(1)} collective-permute-done((bf16[64,1024]{1,0:T(8,128)(2,1)S(1)}, bf16[64,1024]{1,0:T(8,128)(2,1)S(1)}, u32[]{:S(2)}, u32[]{:S(2)}) %collective-permute-start.31) | collective-permute-done | bytes 131104 | tf_op jit(solution)/shard_map/ppermute | solution.py:340
  183.8 1.1 shard_map.114
  (52 shorter events, 4.5 us)
Async XLA Ops:
  65.9 15.1 %collective-permute-start.1 = (bf16[512,512]{1,0:T(8,128)(2,1)}, bf16[512,512]{1,0:T(8,128)(2,1)S(1)}, u32[]{:S(2)}, u32[]{:S(2)}) collective-permute-start(bf16[512,512]{1,0:T(8,128)(2,1)} %get-tuple-element.74.refs_1_), channel_id=1, source_target_pairs={{0,1},{1,0},{2,3},{3,2},{4,5},{5,4},{6,7},{7,6},{8,9},{9,8},{10,11... | collective-permute-start | bytes 1572872 | tf_op jit(solution)/shard_map/ppermute | solution.py:340
  68.9 13.6 %collective-permute-start.2 = (bf16[512,512]{1,0:T(8,128)(2,1)}, bf16[512,512]{1,0:T(8,128)(2,1)S(1)}, u32[]{:S(2)}, u32[]{:S(2)}) collective-permute-start(bf16[512,512]{1,0:T(8,128)(2,1)} %get-tuple-element.73.refs_0_), channel_id=1, source_target_pairs={{0,2},{1,3},{2,0},{3,1},{4,6},{5,7},{6,4},{7,5},{8,10},{9,11},{10,... | collective-permute-start | bytes 1572872 | tf_op jit(solution)/shard_map/ppermute | solution.py:340
  70.5 1.9 %collective-permute-start = (bf16[64,2048]{1,0:T(8,128)(2,1)}, bf16[64,2048]{1,0:T(8,128)(2,1)S(1)}, u32[]{:S(2)}, u32[]{:S(2)}) collective-permute-start(bf16[64,2048]{1,0:T(8,128)(2,1)} %get-tuple-element.56), channel_id=1, source_target_pairs={{0,8},{1,9},{2,10},{3,11},{4,12},{5,13},{6,14},{7,15},{8,0},{9,1},... | collective-permute-start | bytes 786440 | tf_op jit(solution)/shard_map/ppermute | solution.py:340
  70.5 12.0 %collective-permute-start.3 = (bf16[64,2048]{1,0:T(8,128)(2,1)}, bf16[64,2048]{1,0:T(8,128)(2,1)S(1)}, u32[]{:S(2)}, u32[]{:S(2)}) collective-permute-start(bf16[64,2048]{1,0:T(8,128)(2,1)} %get-tuple-element.61), channel_id=1, source_target_pairs={{0,16},{1,17},{2,18},{3,19},{4,20},{5,21},{6,22},{7,23},{8,24},{9,... | collective-permute-start | bytes 786440 | tf_op jit(solution)/shard_map/ppermute | solution.py:340
  72.0 12.6 %collective-permute-start.4 = (bf16[64,2048]{1,0:T(8,128)(2,1)}, bf16[64,2048]{1,0:T(8,128)(2,1)S(1)}, u32[]{:S(2)}, u32[]{:S(2)}) collective-permute-start(bf16[64,2048]{1,0:T(8,128)(2,1)} %get-tuple-element.62), channel_id=1, source_target_pairs={{0,24},{1,25},{2,26},{3,27},{4,28},{5,29},{6,30},{7,31},{8,16},{9,... | collective-permute-start | bytes 786440 | tf_op jit(solution)/shard_map/ppermute | solution.py:340
  84.7 15.7 %collective-permute-start.8 = (bf16[512,512]{1,0:T(8,128)(2,1)}, bf16[512,512]{1,0:T(8,128)(2,1)S(1)}, u32[]{:S(2)}, u32[]{:S(2)}) collective-permute-start(bf16[512,512]{1,0:T(8,128)(2,1)} %get-tuple-element.73.refs_0_), channel_id=1, source_target_pairs={{0,1},{1,0},{2,3},{3,2},{4,5},{5,4},{6,7},{7,6},{8,9},{9,8},{10,11... | collective-permute-start | bytes 1572872 | tf_op jit(solution)/shard_map/ppermute | solution.py:340
  85.2 19.6 %collective-permute-start.9 = (bf16[512,512]{1,0:T(8,128)(2,1)}, bf16[512,512]{1,0:T(8,128)(2,1)S(1)}, u32[]{:S(2)}, u32[]{:S(2)}) collective-permute-start(bf16[512,512]{1,0:T(8,128)(2,1)} %get-tuple-element.74.refs_1_), channel_id=1, source_target_pairs={{0,2},{1,3},{2,0},{3,1},{4,6},{5,7},{6,4},{7,5},{8,10},{9,11},{10,... | collective-permute-start | bytes 1572872 | tf_op jit(solution)/shard_map/ppermute | solution.py:340
  85.6 0.9 copy-start.4
  88.9 17.4 %collective-permute-start.6 = (bf16[256,512]{1,0:T(8,128)(2,1)S(1)}, bf16[256,512]{1,0:T(8,128)(2,1)S(1)}, u32[]{:S(2)}, u32[]{:S(2)}) collective-permute-start(bf16[256,512]{1,0:T(8,128)(2,1)S(1)} %get-tuple-element.64), channel_id=1, source_target_pairs={{0,4},{1,5},{2,6},{3,7},{4,0},{5,1},{6,2},{7,3},{8,12},{9,13},{10,... | collective-permute-start | bytes 786440 | tf_op jit(solution)/shard_map/ppermute | solution.py:340
  93.9 13.9 %collective-permute-start.12 = (bf16[256,512]{1,0:T(8,128)(2,1)S(1)}, bf16[256,512]{1,0:T(8,128)(2,1)S(1)}, u32[]{:S(2)}, u32[]{:S(2)}) collective-permute-start(bf16[256,512]{1,0:T(8,128)(2,1)S(1)} %shard_map.103.refs_3_), channel_id=1, source_target_pairs={{0,16},{1,17},{2,18},{3,19},{4,20},{5,21},{6,22},{7,23},{8,24},{9,... | collective-permute-start | bytes 786440 | tf_op jit(solution)/shard_map/ppermute | solution.py:340
  95.5 1.0 copy-start.1
  96.6 1.0 copy-start.2
  97.6 1.0 copy-start.3
  98.6 0.7 copy-start.5
  99.4 0.7 copy-start.6
  104.8 13.3 %collective-permute-start.10 = (bf16[512,512]{1,0:T(8,128)(2,1)S(1)}, bf16[512,512]{1,0:T(8,128)(2,1)S(1)}, u32[]{:S(2)}, u32[]{:S(2)}) collective-permute-start(bf16[512,512]{1,0:T(8,128)(2,1)S(1)} %collective-permute-done.2.refs_9_.refs_8_), channel_id=1, source_target_pairs={{0,1},{1,0},{2,3},{3,2},{4,5},{5,4},{6,7},{7,6},{8,9},{9,8},{10,11... | collective-permute-start | bytes 1572872 | tf_op jit(solution)/shard_map/ppermute | solution.py:340
  106.3 14.0 %collective-permute-start.11 = (bf16[512,512]{1,0:T(8,128)(2,1)S(1)}, bf16[512,512]{1,0:T(8,128)(2,1)S(1)}, u32[]{:S(2)}, u32[]{:S(2)}) collective-permute-start(bf16[512,512]{1,0:T(8,128)(2,1)S(1)} %collective-permute-done.1.refs_8_.refs_7_), channel_id=1, source_target_pairs={{0,2},{1,3},{2,0},{3,1},{4,6},{5,7},{6,4},{7,5},{8,10},{9,11},{10,... | collective-permute-start | bytes 1572872 | tf_op jit(solution)/shard_map/ppermute | solution.py:340
  106.3 7.0 %collective-permute-start.15 = (bf16[256,512]{1,0:T(8,128)(2,1)S(1)}, bf16[256,512]{1,0:T(8,128)(2,1)S(1)}, u32[]{:S(2)}, u32[]{:S(2)}) collective-permute-start(bf16[256,512]{1,0:T(8,128)(2,1)S(1)} %collective-permute-done.6.refs_2_), channel_id=1, source_target_pairs={{0,16},{1,17},{2,18},{3,19},{4,20},{5,21},{6,22},{7,23},{8,24},{9,... | collective-permute-start | bytes 786440 | tf_op jit(solution)/shard_map/ppermute | solution.py:340
  107.8 5.5 %collective-permute-start.5 = (bf16[256,512]{1,0:T(8,128)(2,1)S(1)}, bf16[256,512]{1,0:T(8,128)(2,1)S(1)}, u32[]{:S(2)}, u32[]{:S(2)}) collective-permute-start(bf16[256,512]{1,0:T(8,128)(2,1)S(1)} %shard_map.103.refs_3_), channel_id=1, source_target_pairs={{0,8},{1,9},{2,10},{3,11},{4,12},{5,13},{6,14},{7,15},{8,0},{9,1},... | collective-permute-start | bytes 786440 | tf_op jit(solution)/shard_map/ppermute | solution.py:340
  107.8 10.3 %collective-permute-start.7 = (bf16[128,256]{1,0:T(8,128)(2,1)S(1)}, bf16[128,256]{1,0:T(8,128)(2,1)S(1)}, u32[]{:S(2)}, u32[]{:S(2)}) collective-permute-start(bf16[128,256]{1,0:T(8,128)(2,1)S(1)} %get-tuple-element.72.refs_6_.place_ref), channel_id=1, source_target_pairs={{0,4},{1,5},{2,6},{3,7},{4,0},{5,1},{6,2},{7,3},{8,12},{9,13},{10,... | collective-permute-start | bytes 196616 | tf_op jit(solution)/shard_map/ppermute | solution.py:340
  113.3 7.0 %collective-permute-start.13 = (bf16[256,512]{1,0:T(8,128)(2,1)S(1)}, bf16[256,512]{1,0:T(8,128)(2,1)S(1)}, u32[]{:S(2)}, u32[]{:S(2)}) collective-permute-start(bf16[256,512]{1,0:T(8,128)(2,1)S(1)} %collective-permute-done.12.refs_5_), channel_id=1, source_target_pairs={{0,8},{1,9},{2,10},{3,11},{4,12},{5,13},{6,14},{7,15},{8,0},{9,1},... | collective-permute-start | bytes 786440 | tf_op jit(solution)/shard_map/ppermute | solution.py:340
  113.3 8.1 %collective-permute-start.14 = (bf16[256,512]{1,0:T(8,128)(2,1)S(1)}, bf16[256,512]{1,0:T(8,128)(2,1)S(1)}, u32[]{:S(2)}, u32[]{:S(2)}) collective-permute-start(bf16[256,512]{1,0:T(8,128)(2,1)S(1)} %collective-permute-done.6.refs_2_), channel_id=1, source_target_pairs={{0,8},{1,9},{2,10},{3,11},{4,12},{5,13},{6,14},{7,15},{8,0},{9,1},... | collective-permute-start | bytes 786440 | tf_op jit(solution)/shard_map/ppermute | solution.py:340
  118.1 3.3 %collective-permute-start.16 = (bf16[256,512]{1,0:T(8,128)(2,1)S(1)}, bf16[256,512]{1,0:T(8,128)(2,1)S(1)}, u32[]{:S(2)}, u32[]{:S(2)}) collective-permute-start(bf16[256,512]{1,0:T(8,128)(2,1)S(1)} %collective-permute-done.15.refs_4_), channel_id=1, source_target_pairs={{0,8},{1,9},{2,10},{3,11},{4,12},{5,13},{6,14},{7,15},{8,0},{9,1},... | collective-permute-start | bytes 786440 | tf_op jit(solution)/shard_map/ppermute | solution.py:340
  120.3 17.5 %copy-start.7 = (f32[1024]{0:T(1024)S(1)}, f32[1024]{0:T(1024)}, u32[]{:S(2)}) copy-start(f32[1024]{0:T(1024)} %param.15) | copy-start | bytes 12292
  120.3 28.3 %slice-start = ((s8[6291456]{0:T(1024)(128)(4,1)}), s8[4194304]{0:T(1024)(128)(4,1)S(1)}, s32[]{:S(2)}) async-start(s8[6291456]{0:T(1024)(128)(4,1)} %bitcast.16), calls=%async_computation | async-start | bytes 8388608
  121.3 27.2 %slice-start.1 = ((s8[6291456]{0:T(1024)(128)(4,1)}), s8[2097152]{0:T(1024)(128)(4,1)S(1)}, s32[]{:S(2)}) async-start(s8[6291456]{0:T(1024)(128)(4,1)} %bitcast.16), calls=%async_computation.1 | async-start | bytes 4194304
  122.4 46.0 %copy-start = (bf16[1,1536,1024]{2,1,0:T(8,128)(2,1)S(1)}, bf16[1,1536,1024]{2,1,0:T(8,128)(2,1)}, u32[]{:S(2)}) copy-start(bf16[1,1536,1024]{2,1,0:T(8,128)(2,1)} %param.19) | copy-start | bytes 9437188
  123.8 13.9 %collective-permute-start.17 = (bf16[128,1024]{1,0:T(8,128)(2,1)S(1)}, bf16[128,1024]{1,0:T(8,128)(2,1)S(1)}, u32[]{:S(2)}, u32[]{:S(2)}) collective-permute-start(bf16[128,1024]{1,0:T(8,128)(2,1)S(1)} %get-tuple-element.85), channel_id=1, source_target_pairs={{0,4},{1,5},{2,6},{3,7},{4,0},{5,1},{6,2},{7,3},{8,12},{9,13},{10,... | collective-permute-start | bytes 786440 | tf_op jit(solution)/shard_map/ppermute | solution.py:340
  137.8 10.2 %collective-permute-start.18 = (bf16[96,1024]{1,0:T(8,128)(2,1)S(1)}, bf16[96,1024]{1,0:T(8,128)(2,1)S(1)}, u32[]{:S(2)}, u32[]{:S(2)}) collective-permute-start(bf16[96,1024]{1,0:T(8,128)(2,1)S(1)} %get-tuple-element.86), channel_id=1, source_target_pairs={{0,4},{1,5},{2,6},{3,7},{4,0},{5,1},{6,2},{7,3},{8,12},{9,13},{10,... | collective-permute-start | bytes 589832 | tf_op jit(solution)/shard_map/ppermute | solution.py:340
  137.8 10.1 %collective-permute-start.20 = (bf16[32,1024]{1,0:T(8,128)(2,1)S(1)}, bf16[32,1024]{1,0:T(8,128)(2,1)S(1)}, u32[]{:S(2)}, u32[]{:S(2)}) collective-permute-start(bf16[32,1024]{1,0:T(8,128)(2,1)S(1)} %get-tuple-element.93), channel_id=1, source_target_pairs={{0,1},{1,0},{2,3},{3,2},{4,5},{5,4},{6,7},{7,6},{8,9},{9,8},{10,11... | collective-permute-start | bytes 196616 | tf_op jit(solution)/shard_map/ppermute | solution.py:340
  138.4 9.5 %collective-permute-start.21 = (bf16[32,1024]{1,0:T(8,128)(2,1)S(1)}, bf16[32,1024]{1,0:T(8,128)(2,1)S(1)}, u32[]{:S(2)}, u32[]{:S(2)}) collective-permute-start(bf16[32,1024]{1,0:T(8,128)(2,1)S(1)} %get-tuple-element.94), channel_id=1, source_target_pairs={{0,2},{1,3},{2,0},{3,1},{4,6},{5,7},{6,4},{7,5},{8,10},{9,11},{10,... | collective-permute-start | bytes 196616 | tf_op jit(solution)/shard_map/ppermute | solution.py:340
  141.4 7.2 %collective-permute-start.22 = (bf16[32,1024]{1,0:T(8,128)(2,1)S(1)}, bf16[32,1024]{1,0:T(8,128)(2,1)S(1)}, u32[]{:S(2)}, u32[]{:S(2)}) collective-permute-start(bf16[32,1024]{1,0:T(8,128)(2,1)S(1)} %get-tuple-element.95), channel_id=1, source_target_pairs={{0,3},{1,2},{2,1},{3,0},{4,7},{5,6},{6,5},{7,4},{8,11},{9,10},{10,... | collective-permute-start | bytes 196616 | tf_op jit(solution)/shard_map/ppermute | solution.py:340
  149.8 1.8 collective-permute-start.23
  149.8 17.3 %collective-permute-start.19 = (bf16[160,1024]{1,0:T(8,128)(2,1)S(1)}, bf16[160,1024]{1,0:T(8,128)(2,1)S(1)}, u32[]{:S(2)}, u32[]{:S(2)}) collective-permute-start(bf16[160,1024]{1,0:T(8,128)(2,1)S(1)} %get-tuple-element.88), channel_id=1, source_target_pairs={{0,4},{1,5},{2,6},{3,7},{4,0},{5,1},{6,2},{7,3},{8,12},{9,13},{10,... | collective-permute-start | bytes 983048 | tf_op jit(solution)/shard_map/ppermute | solution.py:340
  151.7 7.2 %collective-permute-start.24 = (bf16[32,3200]{1,0:T(8,128)(2,1)S(1)}, bf16[32,3200]{1,0:T(8,128)(2,1)S(1)}, u32[]{:S(2)}, u32[]{:S(2)}) collective-permute-start(bf16[32,3200]{1,0:T(8,128)(2,1)S(1)} %get-tuple-element.99), channel_id=1, source_target_pairs={{0,16},{1,17},{2,18},{3,19},{4,20},{5,21},{6,22},{7,23},{8,24},{9,... | collective-permute-start | bytes 614408 | tf_op jit(solution)/shard_map/ppermute | solution.py:340
  159.0 8.1 %collective-permute-start.26 = (bf16[32,1536]{1,0:T(8,128)(2,1)S(1)}, bf16[32,1536]{1,0:T(8,128)(2,1)S(1)}, u32[]{:S(2)}, u32[]{:S(2)}) collective-permute-start(bf16[32,1536]{1,0:T(8,128)(2,1)S(1)} %shard_map.111.refs_0_), channel_id=1, source_target_pairs={{0,16},{1,17},{2,18},{3,19},{4,20},{5,21},{6,22},{7,23},{8,24},{9,... | collective-permute-start | bytes 294920 | tf_op jit(solution)/shard_map/ppermute | solution.py:340
  160.6 6.6 %collective-permute-start.25 = (bf16[32,1536]{1,0:T(8,128)(2,1)S(1)}, bf16[32,1536]{1,0:T(8,128)(2,1)S(1)}, u32[]{:S(2)}, u32[]{:S(2)}) collective-permute-start(bf16[32,1536]{1,0:T(8,128)(2,1)S(1)} %shard_map.111.refs_0_), channel_id=1, source_target_pairs={{0,8},{1,9},{2,10},{3,11},{4,12},{5,13},{6,14},{7,15},{8,0},{9,1},... | collective-permute-start | bytes 294920 | tf_op jit(solution)/shard_map/ppermute | solution.py:340
  167.1 1.3 collective-permute-start.27
  169.1 4.3 %collective-permute-start.28 = (bf16[32,1024]{1,0:T(8,128)(2,1)S(1)}, bf16[32,1024]{1,0:T(8,128)(2,1)S(1)}, u32[]{:S(2)}, u32[]{:S(2)}) collective-permute-start(bf16[32,1024]{1,0:T(8,128)(2,1)S(1)} %get-tuple-element.102), channel_id=1, source_target_pairs={{0,1},{1,0},{2,3},{3,2},{4,5},{5,4},{6,7},{7,6},{8,9},{9,8},{10,11... | collective-permute-start | bytes 196616 | tf_op jit(solution)/shard_map/ppermute | solution.py:340
  170.0 4.6 %collective-permute-start.29 = (bf16[32,1024]{1,0:T(8,128)(2,1)S(1)}, bf16[32,1024]{1,0:T(8,128)(2,1)S(1)}, u32[]{:S(2)}, u32[]{:S(2)}) collective-permute-start(bf16[32,1024]{1,0:T(8,128)(2,1)S(1)} %get-tuple-element.103), channel_id=1, source_target_pairs={{0,2},{1,3},{2,0},{3,1},{4,6},{5,7},{6,4},{7,5},{8,10},{9,11},{10,... | collective-permute-start | bytes 196616 | tf_op jit(solution)/shard_map/ppermute | solution.py:340
  170.0 5.9 %collective-permute-start.30 = (bf16[32,1024]{1,0:T(8,128)(2,1)S(1)}, bf16[32,1024]{1,0:T(8,128)(2,1)S(1)}, u32[]{:S(2)}, u32[]{:S(2)}) collective-permute-start(bf16[32,1024]{1,0:T(8,128)(2,1)S(1)} %get-tuple-element.104), channel_id=1, source_target_pairs={{0,3},{1,2},{2,1},{3,0},{4,7},{5,6},{6,5},{7,4},{8,11},{9,10},{10,... | collective-permute-start | bytes 196616 | tf_op jit(solution)/shard_map/ppermute | solution.py:340
  175.9 7.9 %collective-permute-start.31 = (bf16[64,1024]{1,0:T(8,128)(2,1)S(1)}, bf16[64,1024]{1,0:T(8,128)(2,1)S(1)}, u32[]{:S(2)}, u32[]{:S(2)}) collective-permute-start(bf16[64,1024]{1,0:T(8,128)(2,1)S(1)} %shard_map.113), channel_id=1, source_target_pairs={{0,4},{1,5},{2,6},{3,7},{4,0},{5,1},{6,2},{7,3},{8,12},{9,13},{10,... | collective-permute-start | bytes 393224 | tf_op jit(solution)/shard_map/ppermute | solution.py:340

commit v7 on v6

--- a/solution.py
+++ b/solution.py
@@ -42,7 +42,7 @@
 
 
 PAIR = 4
-PACK_LIMIT = 57
+PACK_LIMIT = 16
 
 
 def spread(d):
@@ -83,11 +83,6 @@
         pairs.append((new_ref, out.at[:, 2 * qw : 2 * qw + kv]))
         pairs.append((past_ref, out.at[:, 2 * qw + kv :]))
     run_copies(pairs, sems)
-
-
-def halve_weight_kernel(w_ref, a_ref, b_ref, sems):
-    half = a_ref.shape[1]
-    run_copies([(w_ref.at[:, half:], b_ref), (w_ref.at[:, :half], a_ref)], sems)
 
 
 def attend_kernel(C, t, *refs):
@@ -128,8 +123,8 @@
 
 
 def route_kernel(E, cap, routes_ref, gates_ref, *refs):
-    place_ref, gate_ref, line_s, gate_s = refs[3], refs[4], refs[-2], refs[-1]
-    for src, dst in zip(refs[:3], refs[5:8]):
+    place_ref, gate_ref, line_s, gate_s = refs[2], refs[3], refs[-2], refs[-1]
+    for src, dst in zip(refs[:2], refs[4:6]):
         dst[...] = src[...]
     e = lax.axis_index("exp")
     blocks, _, tok = routes_ref.shape
@@ -159,35 +154,33 @@
     place_ref[...] = jnp.where(slot == places, 1.0, 0.0).astype(BF16)
 
 
-def project_kernel(C, with_residual, *refs):
-    own_w, refs = refs[:2], refs[2:]
-    if with_residual:
-        res, refs = refs[0], refs[1:]
-    atts, ws, (acc, last, stacked) = refs[:C], refs[C : 3 * C - 4], refs[3 * C - 4 :]
+def project_kernel(C, cut, with_residual, *refs):
+    refs, (acc, last, stacked) = list(refs[:-3]), refs[-3:]
+    res = refs.pop(0) if with_residual else None
+    atts, ws = refs[:C], refs[C:]
     hi, _ = own_hi_lo()
     turn = jnp.bitwise_xor(lax.axis_index("ctx"), hi)
     for s in range(C):
         stacked[jnp.bitwise_xor(turn, s)] = atts[s][...]
     last[...] = stacked[C - 1]
-    half = acc.shape[1] // 2
-    for j in range(2):
-        at = slice(j * half, (j + 1) * half)
-        total = None
+    width = acc.shape[1]
+    for j, at in enumerate((slice(0, cut), slice(cut, width))):
+        total = res[:, at].astype(F32) if with_residual else None
         for d in range(C - 1):
-            w = own_w[j] if d == 0 else ws[2 * (d - 1) + j]
-            term = dot(stacked[d], w[...])
+            if d < 2:
+                w = ws[d][:, at]
+            else:
+                w = ws[2 * d - 2 + j][...]
+            term = dot(stacked[d], w)
             total = term if total is None else total + term
-        if with_residual:
-            total = total + res[:, at].astype(F32)
         acc[:, at] = total
 
 
 def last_kernel(E, cap, *refs):
     accs, lasts, ws, places = refs[:2], refs[2:4], refs[4:6], refs[6:8]
     own_ref, *full_refs, keep_ref, send_ref = refs[8:]
-    half = ws[0].shape[1]
-    for j in range(2):
-        cols = slice(j * half, (j + 1) * half)
+    cut = ws[0].shape[1]
+    for j, cols in enumerate((slice(0, cut), slice(cut, own_ref.shape[1]))):
         for t in (1, 0):
             total = accs[t][:, cols] + dot(lasts[t][...], ws[j][...])
             rounded = total.astype(BF16)
@@ -342,7 +335,7 @@
     def after(x, *others):
         return lax.optimization_barrier((x, *others))[0]
 
-    half = width // 2
+    cut = width - max(width * 3 // 8, 128)
     kv = new_keys_values.shape[3]
     msgs = call(
         functools.partial(pack_kernel, C, qw),
@@ -350,7 +343,6 @@
         3,
         scratch=[pltpu.SemaphoreType.DMA((4 * C,))],
         in_specs=[HBM] * 3,
-        out_specs=[ANY] * C,
         cost=(0, 2**20),
         limit=PACK_LIMIT,
     )(
@@ -358,33 +350,19 @@
         new_keys_values.reshape(tok, kv),
         cached_keys_values.reshape(tok, kv),
     )
-    half_a, half_b = call(
-        halve_weight_kernel,
-        [sds((qw, half), BF16)] * 2,
-        1,
-        scratch=[pltpu.SemaphoreType.DMA((2,))],
-        in_specs=[HBM],
-        out_specs=[ANY] * 2,
-        cost=(0, 2**20),
-        limit=PACK_LIMIT,
-    )(after(out_weight, msgs[0]))
     res = residual.reshape(rows, width)
     got = [msgs[0]] + [permute(msgs[s], ctx=s) for s in range(1, C)]
-    shards = {0: [half_a, half_b], 1: [None, permute(half_b, exp=1)]}
+    shards = {0: [out_weight], 1: [permute(out_weight, exp=1)]}
     for d in range(2, C, 2):
-        shards[d] = [permute(half_a, exp=spread(d)), None]
-    step = [shards[1][1]] + [shards[d][0] for d in range(2, C, 2)]
+        shards[d] = [permute(out_weight[:, :cut], exp=spread(d))]
+    step = [shards[d][0] for d in range(2, C, 2)]
     got[1] = after(got[1], *step)
-    step += got[1:]
-    shards[1][0] = permute(after(half_a, *step), exp=1)
     for d in range(2, C, 2):
-        shards[d][1] = permute(after(half_b, *step), exp=spread(d))
-    step = [shards[1][0]] + [shards[d][1] for d in range(2, C, 2)]
-    for d in range(3, C, 2):
-        shards[d] = [
-            permute(after(shards[d - 1][0], *step), exp=1),
-            permute(after(shards[1][1], *step), exp=spread(d - 1)),
-        ]
+        shards[d].append(permute(after(out_weight[:, cut:], *got), exp=spread(d)))
+        shards[d + 1] = [permute(after(shards[d][0], *got), exp=1)]
+    step = shards[1] + [shards[d][1] for d in range(2, C, 2)]
+    for d in range(2, C, 2):
+        shards[d + 1].append(permute(after(shards[1][0], *step)[:, cut:], exp=spread(d)))
 
     step2 = step
 
@@ -405,14 +383,13 @@
     place, gate, *staged = call(
         functools.partial(route_kernel, E, cap),
         [sds((slots, rows), BF16), sds((rows, 128), F32)]
-        + [sds((qw, half), BF16)] * 2
-        + [sds((rows, width), BF16)],
-        5,
+        + [sds((qw, width), BF16), sds((rows, width), BF16)],
+        4,
         scratch=[pltpu.VMEM((8, rows), jnp.int32), pltpu.VMEM((128, rows), F32)],
         cost=(0, 2**14),
         limit=16,
-    )(tokens_last(after(routes, mine)), tokens_last(after(gates, mine)), half_a, half_b, res)
-    shards[0], res = staged[:2], staged[2]
+    )(tokens_last(after(routes, mine)), tokens_last(after(gates, mine)), out_weight, res)
+    shards[0], res = staged[:1], staged[1]
 
     def gather(x, before):
         atts = {0: x, 1: permute(x, ctx=1)}
@@ -428,10 +405,9 @@
     mine_all[1] = after(mine_all[1], other_place, *step)
 
     def project(atts, *extra):
-        operands = [*shards[0], *extra, *atts]
-        operands += [w for d in range(1, C - 1) for w in shards[d]]
+        operands = [*extra, *atts, *[w for d in range(C - 1) for w in shards[d]]]
         return call(
-            functools.partial(project_kernel, C, bool(extra)),
+            functools.partial(project_kernel, C, cut, bool(extra)),
             [sds((rows, width), F32), sds((rows, qw), BF16)],
             len(operands),
             scratch=[

time: 185 us -> 124 us (0.67)
  Pallas kernels: 77.8 us -> 12.8 us
  local copies, waits for them, and re-layouts: 5.53 us -> 8.65 us
    pallas_call x1, Pallas kernels: 33 us -> 0.36 us  [body(): call(functools.partial(pack_kernel, C, qw), [sds((tok, 2 * qw + 2 * kv),...]
    pallas_call x3 -> x2, Pallas kernels: 35 us -> 2.56 us  [project(): call(functools.partial(project_kernel, C, cut, bool(extra)), [sds((rows,...]
    slice x0 -> x3, local copies, waits for them, and re-layouts: none -> 2.21 us  [the longest x1 1.14 us: body(): shards[d] = [permute(out_weight[:, :cut], exp=spread(d))]]
    unnamed x20 -> x22, local copies, waits for them, and re-layouts: 5.53 us -> 6.44 us
    ppermute x32 -> x31, waiting for transfers between devices: 67.6 us -> 68 us  [permute(): return lax.ppermute(x, ('ctx', 'exp'), pairs)]
    ppermute x32 -> x31, starting transfers between devices: 33.8 us -> 33.5 us  [permute(): return lax.ppermute(x, ('ctx', 'exp'), pairs)]
  transfers between devices with their start and end apart: 32 -> 31, of which waited for: 18 -> 18; matrix products, arithmetic and copies ran while one was open for 0% -> 1% of each run, Pallas kernels for 3% -> 6%
where the time goes in v7:
time: 124 us; the launch traced here: 123 us
  waiting for transfers between devices  68 us (55%)
  starting transfers between devices  33.5 us (27%)
  Pallas kernels  12.8 us (10%)
  local copies, waits for them, and re-layouts  8.65 us (7%)
    ppermute x31, waiting for transfers between devices, permute(): return lax.ppermute(x, ('ctx', 'exp'), pairs)  68 us
    ppermute x31, starting transfers between devices, permute(): return lax.ppermute(x, ('ctx', 'exp'), pairs)  33.5 us
    unnamed x22, local copies, waits for them, and re-layouts  6.44 us
    pallas_call x2, Pallas kernels, attend(): call(functools.partial(attend_kernel, C, t), [sds((rows, qw), BF16)] + [s...  4.68 us
    pallas_call x2, Pallas kernels, project(): call(functools.partial(project_kernel, C, cut, bool(extra)), [sds((rows,...  2.56 us
  transfers between devices with their start and end apart: 31, of which 18 were waited for; matrix products, arithmetic and copies ran while one was open for 1% of the time, Pallas kernels for 6%

profile of v7, /device:TPU:0, one launch (start us, length us, event | category | flops | bytes accessed | tf_op | source)
XLA Modules:
  0.0 123.2 jit_solution(289170788049932966)
XLA Ops:
  0.0 1.1 slice.9
  1.1 3.1 %collective-permute-start.1 = (bf16[512,640]{1,0:T(8,128)(2,1)S(1)}, bf16[512,640]{1,0:T(8,128)(2,1)S(1)}, u32[]{:S(2)}, u32[]{:S(2)}) collective-permute-start(bf16[512,640]{1,0:T(8,128)(2,1)S(1)} %slice.9), channel_id=1, source_target_pairs={{0,2},{1,3},{2,0},{3,1},{4,6},{5,7},{6,4},{7,5},{8,10},{9,11},{10,... | collective-permute-start | bytes 1966088 | tf_op jit(solution)/shard_map/ppermute | solution.py:333
  4.2 1.5 %collective-permute-start.8 = (bf16[512,1024]{1,0:T(8,128)(2,1)}, bf16[512,1024]{1,0:T(8,128)(2,1)S(1)}, u32[]{:S(2)}, u32[]{:S(2)}) collective-permute-start(bf16[512,1024]{1,0:T(8,128)(2,1)} %refs_0_.1), channel_id=1, source_target_pairs={{0,1},{1,0},{2,3},{3,2},{4,5},{5,4},{6,7},{7,6},{8,9},{9,8},{10,11... | collective-permute-start | bytes 3145736 | tf_op jit(solution)/shard_map/ppermute | solution.py:333
  5.7 1.0 copy-done.3
  6.8 0.8 copy-done.4
  7.6 0.8 copy-done.5
  8.9 1.6 %collective-permute-start.2 = (bf16[64,2048]{1,0:T(8,128)(2,1)S(1)}, bf16[64,2048]{1,0:T(8,128)(2,1)S(1)}, u32[]{:S(2)}, u32[]{:S(2)}) collective-permute-start(bf16[64,2048]{1,0:T(8,128)(2,1)S(1)} %get-tuple-element.53), channel_id=1, source_target_pairs={{0,16},{1,17},{2,18},{3,19},{4,20},{5,21},{6,22},{7,23},{8,24},{9,... | collective-permute-start | bytes 786440 | tf_op jit(solution)/shard_map/ppermute | solution.py:333
  10.8 1.0 slice.10
  11.8 7.2 %collective-permute-done.1.refs_7_.refs_6_ = bf16[512,640]{1,0:T(8,128)(2,1)S(1)} collective-permute-done((bf16[512,640]{1,0:T(8,128)(2,1)S(1)}, bf16[512,640]{1,0:T(8,128)(2,1)S(1)}, u32[]{:S(2)}, u32[]{:S(2)}) %collective-permute-start.1) | collective-permute-done | bytes 655392 | tf_op jit(solution)/shard_map/ppermute | solution.py:333
  19.0 3.8 %collective-permute-done.3.refs_3_ = bf16[64,2048]{1,0:T(8,128)(2,1)S(1)} collective-permute-done((bf16[64,2048]{1,0:T(8,128)(2,1)S(1)}, bf16[64,2048]{1,0:T(8,128)(2,1)S(1)}, u32[]{:S(2)}, u32[]{:S(2)}) %collective-permute-start.3) | collective-permute-done | bytes 262176 | tf_op jit(solution)/shard_map/ppermute | solution.py:333
  23.2 2.3 %shard_map.101 = (bf16[256,512]{1,0:T(8,128)(2,1)S(1)}, bf16[64,2048]{1,0:T(8,128)(2,1)S(1)}) custom-call(bf16[64,2048]{1,0:T(8,128)(2,1)S(1)} %get-tuple-element.50.refs_0_, bf16[64,2048]{1,0:T(8,128)(2,1)S(1)} %collective-permute-done.refs_1_, bf16[64,2048]{1,0:T(8,128)(2,1)S(1)} %collective-permute-done.2.refs_2_, ...), custom_call_target="tpu_custom_call" | custom-call | bytes 16384 | tf_op jit(solution)/shard_map/pallas_call | solution.py:370
  25.6 2.6 %collective-permute-start.5 = (bf16[256,512]{1,0:T(8,128)(2,1)S(1)}, bf16[256,512]{1,0:T(8,128)(2,1)S(1)}, u32[]{:S(2)}, u32[]{:S(2)}) collective-permute-start(bf16[256,512]{1,0:T(8,128)(2,1)S(1)} %get-tuple-element.56), channel_id=1, source_target_pairs={{0,4},{1,5},{2,6},{3,7},{4,0},{5,1},{6,2},{7,3},{8,12},{9,13},{10,... | collective-permute-start | bytes 786440 | tf_op jit(solution)/shard_map/ppermute | solution.py:333
  28.8 2.3 %shard_map.102.refs_1_ = bf16[256,512]{1,0:T(8,128)(2,1)S(1)} custom-call(bf16[64,2048]{1,0:T(8,128)(2,1)S(1)} %get-tuple-element.55.refs_0_, bf16[64,2048]{1,0:T(8,128)(2,1)S(1)} %collective-permute-done.refs_1_, bf16[64,2048]{1,0:T(8,128)(2,1)S(1)} %collective-permute-done.2.refs_2_, bf16[64,2048]{1,0:T(8,128)(2,1)S(1)} %collective-permute-done.3.refs_3_), custom_call_target="tpu_custom_call" | custom-call | bytes 16384 | tf_op jit(solution)/shard_map/pallas_call | solution.py:370
  31.1 1.6 %collective-permute-start.11 = (bf16[256,512]{1,0:T(8,128)(2,1)S(1)}, bf16[256,512]{1,0:T(8,128)(2,1)S(1)}, u32[]{:S(2)}, u32[]{:S(2)}) collective-permute-start(bf16[256,512]{1,0:T(8,128)(2,1)S(1)} %shard_map.102.refs_1_), channel_id=1, source_target_pairs={{0,16},{1,17},{2,18},{3,19},{4,20},{5,21},{6,22},{7,23},{8,24},{9,... | collective-permute-start | bytes 786440 | tf_op jit(solution)/shard_map/ppermute | solution.py:333
  32.7 1.2 copy-done
  33.9 1.0 copy-done.2
  35.0 0.7 copy-done.6
  35.7 0.7 copy-done.7
  36.7 1.3 %collective-permute-done.5.refs_0_ = bf16[256,512]{1,0:T(8,128)(2,1)S(1)} collective-permute-done((bf16[256,512]{1,0:T(8,128)(2,1)S(1)}, bf16[256,512]{1,0:T(8,128)(2,1)S(1)}, u32[]{:S(2)}, u32[]{:S(2)}) %collective-permute-start.5) | collective-permute-done | bytes 262176 | tf_op jit(solution)/shard_map/ppermute | solution.py:333
  38.0 2.0 %collective-permute-done.9.refs_8_.refs_7_ = bf16[512,384]{1,0:T(8,128)(2,1)S(1)} collective-permute-done((bf16[512,384]{1,0:T(8,128)(2,1)S(1)}, bf16[512,384]{1,0:T(8,128)(2,1)S(1)}, u32[]{:S(2)}, u32[]{:S(2)}) %collective-permute-start.9) | collective-permute-done | bytes 393248 | tf_op jit(solution)/shard_map/ppermute | solution.py:333
  40.0 1.5 %collective-permute-start.14 = (bf16[256,512]{1,0:T(8,128)(2,1)S(1)}, bf16[256,512]{1,0:T(8,128)(2,1)S(1)}, u32[]{:S(2)}, u32[]{:S(2)}) collective-permute-start(bf16[256,512]{1,0:T(8,128)(2,1)S(1)} %collective-permute-done.5.refs_0_), channel_id=1, source_target_pairs={{0,16},{1,17},{2,18},{3,19},{4,20},{5,21},{6,22},{7,23},{8,24},{9,... | collective-permute-start | bytes 786440 | tf_op jit(solution)/shard_map/ppermute | solution.py:333
  41.6 2.7 %collective-permute-start.10 = (bf16[512,384]{1,0:T(8,128)(2,1)S(1)}, bf16[512,384]{1,0:T(8,128)(2,1)S(1)}, u32[]{:S(2)}, u32[]{:S(2)}) collective-permute-start(bf16[512,384]{1,0:T(8,128)(2,1)S(1)} %slice.11), channel_id=1, source_target_pairs={{0,2},{1,3},{2,0},{3,1},{4,6},{5,7},{6,4},{7,5},{8,10},{9,11},{10,... | collective-permute-start | bytes 1179656 | tf_op jit(solution)/shard_map/ppermute | solution.py:333
  44.2 2.3 %collective-permute-start.6 = (bf16[128,256]{1,0:T(8,128)(2,1)S(1)}, bf16[128,256]{1,0:T(8,128)(2,1)S(1)}, u32[]{:S(2)}, u32[]{:S(2)}) collective-permute-start(bf16[128,256]{1,0:T(8,128)(2,1)S(1)} %get-tuple-element.62.refs_6_.place_ref), channel_id=1, source_target_pairs={{0,4},{1,5},{2,6},{3,7},{4,0},{5,1},{6,2},{7,3},{8,12},{9,13},{10,... | collective-permute-start | bytes 196616 | tf_op jit(solution)/shard_map/ppermute | solution.py:333
  46.5 1.5 %collective-permute-done.14.refs_2_ = bf16[256,512]{1,0:T(8,128)(2,1)S(1)} collective-permute-done((bf16[256,512]{1,0:T(8,128)(2,1)S(1)}, bf16[256,512]{1,0:T(8,128)(2,1)S(1)}, u32[]{:S(2)}, u32[]{:S(2)}) %collective-permute-start.14) | collective-permute-done | bytes 262176 | tf_op jit(solution)/shard_map/ppermute | solution.py:333
  48.5 6.1 %collective-permute-done.6.refs_7_ = bf16[128,256]{1,0:T(8,128)(2,1)S(1)} collective-permute-done((bf16[128,256]{1,0:T(8,128)(2,1)S(1)}, bf16[128,256]{1,0:T(8,128)(2,1)S(1)}, u32[]{:S(2)}, u32[]{:S(2)}) %collective-permute-start.6) | collective-permute-done | bytes 65568 | tf_op jit(solution)/shard_map/ppermute | solution.py:333
  54.7 0.7 collective-permute-done.10.refs_5_
  55.4 1.3 %shard_map.104 = (f32[256,1024]{1,0:T(8,128)S(1)}, bf16[256,512]{1,0:T(8,128)(2,1)S(1)}) custom-call(bf16[256,1024]{1,0:T(8,128)(2,1)S(1)} %get-tuple-element.60.refs_0_, bf16[256,512]{1,0:T(8,128)(2,1)S(1)} %shard_map.102.refs_1_, bf16[256,512]{1,0:T(8,128)(2,1)S(1)} %collective-permute-done.4.refs_2_, ...), custom_call_target="tpu_custom_call" | custom-call | bytes 16384 | tf_op jit(solution)/shard_map/pallas_call | solution.py:409
  56.7 1.3 %shard_map.105 = (f32[256,1024]{1,0:T(8,128)S(1)}, bf16[256,512]{1,0:T(8,128)(2,1)S(1)}) custom-call(bf16[256,512]{1,0:T(8,128)(2,1)S(1)} %collective-permute-done.5.refs_0_, bf16[256,512]{1,0:T(8,128)(2,1)S(1)} %collective-permute-done.13.refs_1_, bf16[256,512]{1,0:T(8,128)(2,1)S(1)} %collective-permute-done.14.refs_2_, ...), custom_call_target="tpu_custom_call" | custom-call | bytes 16384 | tf_op jit(solution)/shard_map/pallas_call | solution.py:409
  58.0 1.5 %shard_map.106 = (f32[256,1024]{1,0:T(8,128)S(1)}, bf16[96,1024]{1,0:T(8,128)(2,1)S(1)}, bf16[160,1024]{1,0:T(8,128)(2,1)S(1)}, f32[128,1024]{1,0:T(8,128)S(1)}, bf16[128,1024]{1,0:T(8,128)(2,1)S(1)}) custom-call(f32[256,1024]{1,0:T(8,128)S(1)} %get-tuple-element.68.refs_0_, f32[256,1024]{1,0:T(8,128)S(1)} %get-tuple-element.70.refs_1_, ...), custom_call_target="tpu_custom_call" | custom-call | flops 671088640 | bytes 1048576 | tf_op jit(solution)/shard_map/pallas_call | solution.py:423
  59.6 2.9 %collective-permute-start.16 = (bf16[128,1024]{1,0:T(8,128)(2,1)S(1)}, bf16[128,1024]{1,0:T(8,128)(2,1)S(1)}, u32[]{:S(2)}, u32[]{:S(2)}) collective-permute-start(bf16[128,1024]{1,0:T(8,128)(2,1)S(1)} %get-tuple-element.75), channel_id=1, source_target_pairs={{0,4},{1,5},{2,6},{3,7},{4,0},{5,1},{6,2},{7,3},{8,12},{9,13},{10,... | collective-permute-start | bytes 786440 | tf_op jit(solution)/shard_map/ppermute | solution.py:333
  62.5 12.4 %collective-permute-done.16.got_ref = bf16[128,1024]{1,0:T(8,128)(2,1)S(1)} collective-permute-done((bf16[128,1024]{1,0:T(8,128)(2,1)S(1)}, bf16[128,1024]{1,0:T(8,128)(2,1)S(1)}, u32[]{:S(2)}, u32[]{:S(2)}) %collective-permute-start.16) | collective-permute-done | bytes 262176 | tf_op jit(solution)/shard_map/ppermute | solution.py:333
  75.6 3.2 %collective-permute-start.20 = (bf16[32,1024]{1,0:T(8,128)(2,1)S(1)}, bf16[32,1024]{1,0:T(8,128)(2,1)S(1)}, u32[]{:S(2)}, u32[]{:S(2)}) collective-permute-start(bf16[32,1024]{1,0:T(8,128)(2,1)S(1)} %get-tuple-element.84), channel_id=1, source_target_pairs={{0,2},{1,3},{2,0},{3,1},{4,6},{5,7},{6,4},{7,5},{8,10},{9,11},{10,... | collective-permute-start | bytes 196616 | tf_op jit(solution)/shard_map/ppermute | solution.py:333
  78.8 0.9 collective-permute-start.21
  79.7 6.3 %collective-permute-done.17.got0 = bf16[96,1024]{1,0:T(8,128)(2,1)S(1)} collective-permute-done((bf16[96,1024]{1,0:T(8,128)(2,1)S(1)}, bf16[96,1024]{1,0:T(8,128)(2,1)S(1)}, u32[]{:S(2)}, u32[]{:S(2)}) %collective-permute-start.17) | collective-permute-done | bytes 196640 | tf_op jit(solution)/shard_map/ppermute | solution.py:333
  86.0 0.7 collective-permute-done.21.refs_3_
  86.8 1.3 %shard_map.108 = (f32[64,3200]{1,0:T(8,128)S(1)}, bf16[64,3200]{1,0:T(8,128)(2,1)S(1)}) custom-call(bf16[32,1024]{1,0:T(8,128)(2,1)S(1)} %get-tuple-element.82.refs_0_, bf16[32,1024]{1,0:T(8,128)(2,1)S(1)} %collective-permute-done.19.refs_1_, bf16[32,1024]{1,0:T(8,128)(2,1)S(1)} %collective-permute-done.20.refs_2_, ...), custom_call_target="tpu_custom_call" | custom-call | flops 805306368 | bytes 6291456 | tf_op jit(solution)/shard_map/pallas_call | solution.py:451
  88.1 1.7 %collective-permute-done.22.got_ref = bf16[64,3200]{1,0:T(8,128)(2,1)S(1)} collective-permute-done((bf16[64,3200]{1,0:T(8,128)(2,1)S(1)}, bf16[64,3200]{1,0:T(8,128)(2,1)S(1)}, u32[]{:S(2)}, u32[]{:S(2)}) %collective-permute-start.22) | collective-permute-done | bytes 409632 | tf_op jit(solution)/shard_map/ppermute | solution.py:333
  90.5 6.6 %collective-permute-done.23.got_ref = bf16[32,3200]{1,0:T(8,128)(2,1)S(1)} collective-permute-done((bf16[32,3200]{1,0:T(8,128)(2,1)S(1)}, bf16[32,3200]{1,0:T(8,128)(2,1)S(1)}, u32[]{:S(2)}, u32[]{:S(2)}) %collective-permute-start.23) | collective-permute-done | bytes 204832 | tf_op jit(solution)/shard_map/ppermute | solution.py:333
  97.8 7.4 %collective-permute-done.18.got1 = bf16[160,1024]{1,0:T(8,128)(2,1)S(1)} collective-permute-done((bf16[160,1024]{1,0:T(8,128)(2,1)S(1)}, bf16[160,1024]{1,0:T(8,128)(2,1)S(1)}, u32[]{:S(2)}, u32[]{:S(2)}) %collective-permute-start.18) | collective-permute-done | bytes 327712 | tf_op jit(solution)/shard_map/ppermute | solution.py:333
  105.3 1.2 collective-permute-done.26.refs_3_
  107.2 1.4 %collective-permute-start.27 = (bf16[32,1024]{1,0:T(8,128)(2,1)S(1)}, bf16[32,1024]{1,0:T(8,128)(2,1)S(1)}, u32[]{:S(2)}, u32[]{:S(2)}) collective-permute-start(bf16[32,1024]{1,0:T(8,128)(2,1)S(1)} %get-tuple-element.92), channel_id=1, source_target_pairs={{0,1},{1,0},{2,3},{3,2},{4,5},{5,4},{6,7},{7,6},{8,9},{9,8},{10,11... | collective-permute-start | bytes 196616 | tf_op jit(solution)/shard_map/ppermute | solution.py:333
  108.6 2.2 %collective-permute-start.29 = (bf16[32,1024]{1,0:T(8,128)(2,1)S(1)}, bf16[32,1024]{1,0:T(8,128)(2,1)S(1)}, u32[]{:S(2)}, u32[]{:S(2)}) collective-permute-start(bf16[32,1024]{1,0:T(8,128)(2,1)S(1)} %get-tuple-element.94), channel_id=1, source_target_pairs={{0,3},{1,2},{2,1},{3,0},{4,7},{5,6},{6,5},{7,4},{8,11},{9,10},{10,... | collective-permute-start | bytes 196616 | tf_op jit(solution)/shard_map/ppermute | solution.py:333
  110.8 0.8 collective-permute-done.27.refs_1_
  111.6 1.6 %collective-permute-done.28.refs_2_ = bf16[32,1024]{1,0:T(8,128)(2,1)S(1)} collective-permute-done((bf16[32,1024]{1,0:T(8,128)(2,1)S(1)}, bf16[32,1024]{1,0:T(8,128)(2,1)S(1)}, u32[]{:S(2)}, u32[]{:S(2)}) %collective-permute-start.28) | collective-permute-done | bytes 65568 | tf_op jit(solution)/shard_map/ppermute | solution.py:333
  113.2 0.9 collective-permute-done.29.refs_3_
  114.1 2.4 %collective-permute-start.30 = (bf16[64,1024]{1,0:T(8,128)(2,1)S(1)}, bf16[64,1024]{1,0:T(8,128)(2,1)S(1)}, u32[]{:S(2)}, u32[]{:S(2)}) collective-permute-start(bf16[64,1024]{1,0:T(8,128)(2,1)S(1)} %shard_map.112), channel_id=1, source_target_pairs={{0,4},{1,5},{2,6},{3,7},{4,0},{5,1},{6,2},{7,3},{8,12},{9,13},{10,... | collective-permute-start | bytes 393224 | tf_op jit(solution)/shard_map/ppermute | solution.py:333
  116.4 5.7 %collective-permute-done.30.refs_4_ = bf16[64,1024]{1,0:T(8,128)(2,1)S(1)} collective-permute-done((bf16[64,1024]{1,0:T(8,128)(2,1)S(1)}, bf16[64,1024]{1,0:T(8,128)(2,1)S(1)}, u32[]{:S(2)}, u32[]{:S(2)}) %collective-permute-start.30) | collective-permute-done | bytes 131104 | tf_op jit(solution)/shard_map/ppermute | solution.py:333
  122.1 1.1 shard_map.113
  (54 shorter events, 5.5 us)
Async XLA Ops:
  1.1 17.8 %collective-permute-start.1 = (bf16[512,640]{1,0:T(8,128)(2,1)S(1)}, bf16[512,640]{1,0:T(8,128)(2,1)S(1)}, u32[]{:S(2)}, u32[]{:S(2)}) collective-permute-start(bf16[512,640]{1,0:T(8,128)(2,1)S(1)} %slice.9), channel_id=1, source_target_pairs={{0,2},{1,3},{2,0},{3,1},{4,6},{5,7},{6,4},{7,5},{8,10},{9,11},{10,... | collective-permute-start | bytes 1966088 | tf_op jit(solution)/shard_map/ppermute | solution.py:333
  4.2 35.8 %collective-permute-start.8 = (bf16[512,1024]{1,0:T(8,128)(2,1)}, bf16[512,1024]{1,0:T(8,128)(2,1)S(1)}, u32[]{:S(2)}, u32[]{:S(2)}) collective-permute-start(bf16[512,1024]{1,0:T(8,128)(2,1)} %refs_0_.1), channel_id=1, source_target_pairs={{0,1},{1,0},{2,3},{3,2},{4,5},{5,4},{6,7},{7,6},{8,9},{9,8},{10,11... | collective-permute-start | bytes 3145736 | tf_op jit(solution)/shard_map/ppermute | solution.py:333
  5.7 1.0 copy-start.3
  6.8 0.8 copy-start.4
  7.6 0.8 copy-start.5
  8.8 3.0 %collective-permute-start = (bf16[64,2048]{1,0:T(8,128)(2,1)S(1)}, bf16[64,2048]{1,0:T(8,128)(2,1)S(1)}, u32[]{:S(2)}, u32[]{:S(2)}) collective-permute-start(bf16[64,2048]{1,0:T(8,128)(2,1)S(1)} %get-tuple-element.51), channel_id=1, source_target_pairs={{0,8},{1,9},{2,10},{3,11},{4,12},{5,13},{6,14},{7,15},{8,0},{9,1},... | collective-permute-start | bytes 786440 | tf_op jit(solution)/shard_map/ppermute | solution.py:333
  8.9 10.1 %collective-permute-start.2 = (bf16[64,2048]{1,0:T(8,128)(2,1)S(1)}, bf16[64,2048]{1,0:T(8,128)(2,1)S(1)}, u32[]{:S(2)}, u32[]{:S(2)}) collective-permute-start(bf16[64,2048]{1,0:T(8,128)(2,1)S(1)} %get-tuple-element.53), channel_id=1, source_target_pairs={{0,16},{1,17},{2,18},{3,19},{4,20},{5,21},{6,22},{7,23},{8,24},{9,... | collective-permute-start | bytes 786440 | tf_op jit(solution)/shard_map/ppermute | solution.py:333
  10.5 12.3 %collective-permute-start.3 = (bf16[64,2048]{1,0:T(8,128)(2,1)S(1)}, bf16[64,2048]{1,0:T(8,128)(2,1)S(1)}, u32[]{:S(2)}, u32[]{:S(2)}) collective-permute-start(bf16[64,2048]{1,0:T(8,128)(2,1)S(1)} %get-tuple-element.54), channel_id=1, source_target_pairs={{0,24},{1,25},{2,26},{3,27},{4,28},{5,29},{6,30},{7,31},{8,16},{9,... | collective-permute-start | bytes 786440 | tf_op jit(solution)/shard_map/ppermute | solution.py:333
  22.8 17.2 %collective-permute-start.9 = (bf16[512,384]{1,0:T(8,128)(2,1)S(1)}, bf16[512,384]{1,0:T(8,128)(2,1)S(1)}, u32[]{:S(2)}, u32[]{:S(2)}) collective-permute-start(bf16[512,384]{1,0:T(8,128)(2,1)S(1)} %slice.10), channel_id=1, source_target_pairs={{0,2},{1,3},{2,0},{3,1},{4,6},{5,7},{6,4},{7,5},{8,10},{9,11},{10,... | collective-permute-start | bytes 1179656 | tf_op jit(solution)/shard_map/ppermute | solution.py:333
  25.6 12.4 %collective-permute-start.5 = (bf16[256,512]{1,0:T(8,128)(2,1)S(1)}, bf16[256,512]{1,0:T(8,128)(2,1)S(1)}, u32[]{:S(2)}, u32[]{:S(2)}) collective-permute-start(bf16[256,512]{1,0:T(8,128)(2,1)S(1)} %get-tuple-element.56), channel_id=1, source_target_pairs={{0,4},{1,5},{2,6},{3,7},{4,0},{5,1},{6,2},{7,3},{8,12},{9,13},{10,... | collective-permute-start | bytes 786440 | tf_op jit(solution)/shard_map/ppermute | solution.py:333
  28.2 26.4 %collective-permute-start.7 = (bf16[512,640]{1,0:T(8,128)(2,1)S(1)}, bf16[512,640]{1,0:T(8,128)(2,1)S(1)}, u32[]{:S(2)}, u32[]{:S(2)}) collective-permute-start(bf16[512,640]{1,0:T(8,128)(2,1)S(1)} %collective-permute-done.1.refs_7_.refs_6_), channel_id=1, source_target_pairs={{0,1},{1,0},{2,3},{3,2},{4,5},{5,4},{6,7},{7,6},{8,9},{9,8},{10,11... | collective-permute-start | bytes 1966088 | tf_op jit(solution)/shard_map/ppermute | solution.py:333
  31.1 13.1 %collective-permute-start.11 = (bf16[256,512]{1,0:T(8,128)(2,1)S(1)}, bf16[256,512]{1,0:T(8,128)(2,1)S(1)}, u32[]{:S(2)}, u32[]{:S(2)}) collective-permute-start(bf16[256,512]{1,0:T(8,128)(2,1)S(1)} %shard_map.102.refs_1_), channel_id=1, source_target_pairs={{0,16},{1,17},{2,18},{3,19},{4,20},{5,21},{6,22},{7,23},{8,24},{9,... | collective-permute-start | bytes 786440 | tf_op jit(solution)/shard_map/ppermute | solution.py:333
  32.7 1.2 copy-start
  33.9 1.0 copy-start.2
  35.0 0.7 copy-start.6
  35.7 0.7 copy-start.7
  40.0 8.0 %collective-permute-start.14 = (bf16[256,512]{1,0:T(8,128)(2,1)S(1)}, bf16[256,512]{1,0:T(8,128)(2,1)S(1)}, u32[]{:S(2)}, u32[]{:S(2)}) collective-permute-start(bf16[256,512]{1,0:T(8,128)(2,1)S(1)} %collective-permute-done.5.refs_0_), channel_id=1, source_target_pairs={{0,16},{1,17},{2,18},{3,19},{4,20},{5,21},{6,22},{7,23},{8,24},{9,... | collective-permute-start | bytes 786440 | tf_op jit(solution)/shard_map/ppermute | solution.py:333
  41.5 6.5 %collective-permute-start.4 = (bf16[256,512]{1,0:T(8,128)(2,1)S(1)}, bf16[256,512]{1,0:T(8,128)(2,1)S(1)}, u32[]{:S(2)}, u32[]{:S(2)}) collective-permute-start(bf16[256,512]{1,0:T(8,128)(2,1)S(1)} %shard_map.102.refs_1_), channel_id=1, source_target_pairs={{0,8},{1,9},{2,10},{3,11},{4,12},{5,13},{6,14},{7,15},{8,0},{9,1},... | collective-permute-start | bytes 786440 | tf_op jit(solution)/shard_map/ppermute | solution.py:333
  41.6 13.8 %collective-permute-start.10 = (bf16[512,384]{1,0:T(8,128)(2,1)S(1)}, bf16[512,384]{1,0:T(8,128)(2,1)S(1)}, u32[]{:S(2)}, u32[]{:S(2)}) collective-permute-start(bf16[512,384]{1,0:T(8,128)(2,1)S(1)} %slice.11), channel_id=1, source_target_pairs={{0,2},{1,3},{2,0},{3,1},{4,6},{5,7},{6,4},{7,5},{8,10},{9,11},{10,... | collective-permute-start | bytes 1179656 | tf_op jit(solution)/shard_map/ppermute | solution.py:333
  44.2 10.4 %collective-permute-start.6 = (bf16[128,256]{1,0:T(8,128)(2,1)S(1)}, bf16[128,256]{1,0:T(8,128)(2,1)S(1)}, u32[]{:S(2)}, u32[]{:S(2)}) collective-permute-start(bf16[128,256]{1,0:T(8,128)(2,1)S(1)} %get-tuple-element.62.refs_6_.place_ref), channel_id=1, source_target_pairs={{0,4},{1,5},{2,6},{3,7},{4,0},{5,1},{6,2},{7,3},{8,12},{9,13},{10,... | collective-permute-start | bytes 196616 | tf_op jit(solution)/shard_map/ppermute | solution.py:333
  48.0 7.4 %collective-permute-start.12 = (bf16[256,512]{1,0:T(8,128)(2,1)S(1)}, bf16[256,512]{1,0:T(8,128)(2,1)S(1)}, u32[]{:S(2)}, u32[]{:S(2)}) collective-permute-start(bf16[256,512]{1,0:T(8,128)(2,1)S(1)} %collective-permute-done.11.refs_3_), channel_id=1, source_target_pairs={{0,8},{1,9},{2,10},{3,11},{4,12},{5,13},{6,14},{7,15},{8,0},{9,1},... | collective-permute-start | bytes 786440 | tf_op jit(solution)/shard_map/ppermute | solution.py:333
  48.0 8.7 %collective-permute-start.13 = (bf16[256,512]{1,0:T(8,128)(2,1)S(1)}, bf16[256,512]{1,0:T(8,128)(2,1)S(1)}, u32[]{:S(2)}, u32[]{:S(2)}) collective-permute-start(bf16[256,512]{1,0:T(8,128)(2,1)S(1)} %collective-permute-done.5.refs_0_), channel_id=1, source_target_pairs={{0,8},{1,9},{2,10},{3,11},{4,12},{5,13},{6,14},{7,15},{8,0},{9,1},... | collective-permute-start | bytes 786440 | tf_op jit(solution)/shard_map/ppermute | solution.py:333
  54.7 2.1 %collective-permute-start.15 = (bf16[256,512]{1,0:T(8,128)(2,1)S(1)}, bf16[256,512]{1,0:T(8,128)(2,1)S(1)}, u32[]{:S(2)}, u32[]{:S(2)}) collective-permute-start(bf16[256,512]{1,0:T(8,128)(2,1)S(1)} %collective-permute-done.14.refs_2_), channel_id=1, source_target_pairs={{0,8},{1,9},{2,10},{3,11},{4,12},{5,13},{6,14},{7,15},{8,0},{9,1},... | collective-permute-start | bytes 786440 | tf_op jit(solution)/shard_map/ppermute | solution.py:333
  55.4 19.5 %copy-start.8 = (f32[1024]{0:T(1024)S(1)}, f32[1024]{0:T(1024)}, u32[]{:S(2)}) copy-start(f32[1024]{0:T(1024)} %param.15) | copy-start | bytes 12292
  55.4 31.4 %slice-start = ((s8[6291456]{0:T(1024)(128)(4,1)}), s8[4194304]{0:T(1024)(128)(4,1)S(1)}, s32[]{:S(2)}) async-start(s8[6291456]{0:T(1024)(128)(4,1)} %bitcast.16), calls=%async_computation | async-start | bytes 8388608
  56.7 30.1 %slice-start.1 = ((s8[6291456]{0:T(1024)(128)(4,1)}), s8[2097152]{0:T(1024)(128)(4,1)S(1)}, s32[]{:S(2)}) async-start(s8[6291456]{0:T(1024)(128)(4,1)} %bitcast.16), calls=%async_computation.1 | async-start | bytes 4194304
  58.0 48.5 %copy-start.1 = (bf16[1,1536,1024]{2,1,0:T(8,128)(2,1)S(1)}, bf16[1,1536,1024]{2,1,0:T(8,128)(2,1)}, u32[]{:S(2)}) copy-start(bf16[1,1536,1024]{2,1,0:T(8,128)(2,1)} %param.19) | copy-start | bytes 9437188
  59.6 15.3 %collective-permute-start.16 = (bf16[128,1024]{1,0:T(8,128)(2,1)S(1)}, bf16[128,1024]{1,0:T(8,128)(2,1)S(1)}, u32[]{:S(2)}, u32[]{:S(2)}) collective-permute-start(bf16[128,1024]{1,0:T(8,128)(2,1)S(1)} %get-tuple-element.75), channel_id=1, source_target_pairs={{0,4},{1,5},{2,6},{3,7},{4,0},{5,1},{6,2},{7,3},{8,12},{9,13},{10,... | collective-permute-start | bytes 786440 | tf_op jit(solution)/shard_map/ppermute | solution.py:333
  74.9 11.1 %collective-permute-start.17 = (bf16[96,1024]{1,0:T(8,128)(2,1)S(1)}, bf16[96,1024]{1,0:T(8,128)(2,1)S(1)}, u32[]{:S(2)}, u32[]{:S(2)}) collective-permute-start(bf16[96,1024]{1,0:T(8,128)(2,1)S(1)} %get-tuple-element.76), channel_id=1, source_target_pairs={{0,4},{1,5},{2,6},{3,7},{4,0},{5,1},{6,2},{7,3},{8,12},{9,13},{10,... | collective-permute-start | bytes 589832 | tf_op jit(solution)/shard_map/ppermute | solution.py:333
  75.0 11.1 %collective-permute-start.19 = (bf16[32,1024]{1,0:T(8,128)(2,1)S(1)}, bf16[32,1024]{1,0:T(8,128)(2,1)S(1)}, u32[]{:S(2)}, u32[]{:S(2)}) collective-permute-start(bf16[32,1024]{1,0:T(8,128)(2,1)S(1)} %get-tuple-element.83), channel_id=1, source_target_pairs={{0,1},{1,0},{2,3},{3,2},{4,5},{5,4},{6,7},{7,6},{8,9},{9,8},{10,11... | collective-permute-start | bytes 196616 | tf_op jit(solution)/shard_map/ppermute | solution.py:333
  75.6 10.5 %collective-permute-start.20 = (bf16[32,1024]{1,0:T(8,128)(2,1)S(1)}, bf16[32,1024]{1,0:T(8,128)(2,1)S(1)}, u32[]{:S(2)}, u32[]{:S(2)}) collective-permute-start(bf16[32,1024]{1,0:T(8,128)(2,1)S(1)} %get-tuple-element.84), channel_id=1, source_target_pairs={{0,2},{1,3},{2,0},{3,1},{4,6},{5,7},{6,4},{7,5},{8,10},{9,11},{10,... | collective-permute-start | bytes 196616 | tf_op jit(solution)/shard_map/ppermute | solution.py:333
  78.8 8.0 %collective-permute-start.21 = (bf16[32,1024]{1,0:T(8,128)(2,1)S(1)}, bf16[32,1024]{1,0:T(8,128)(2,1)S(1)}, u32[]{:S(2)}, u32[]{:S(2)}) collective-permute-start(bf16[32,1024]{1,0:T(8,128)(2,1)S(1)} %get-tuple-element.85), channel_id=1, source_target_pairs={{0,3},{1,2},{2,1},{3,0},{4,7},{5,6},{6,5},{7,4},{8,11},{9,10},{10,... | collective-permute-start | bytes 196616 | tf_op jit(solution)/shard_map/ppermute | solution.py:333
  88.0 1.8 %collective-permute-start.22 = (bf16[64,3200]{1,0:T(8,128)(2,1)S(1)}, bf16[64,3200]{1,0:T(8,128)(2,1)S(1)}, u32[]{:S(2)}, u32[]{:S(2)}) collective-permute-start(bf16[64,3200]{1,0:T(8,128)(2,1)S(1)} %get-tuple-element.87), channel_id=1, source_target_pairs={{0,8},{1,9},{2,10},{3,11},{4,12},{5,13},{6,14},{7,15},{8,0},{9,1},... | collective-permute-start | bytes 1228808 | tf_op jit(solution)/shard_map/ppermute | solution.py:333
  88.1 17.2 %collective-permute-start.18 = (bf16[160,1024]{1,0:T(8,128)(2,1)S(1)}, bf16[160,1024]{1,0:T(8,128)(2,1)S(1)}, u32[]{:S(2)}, u32[]{:S(2)}) collective-permute-start(bf16[160,1024]{1,0:T(8,128)(2,1)S(1)} %get-tuple-element.78), channel_id=1, source_target_pairs={{0,4},{1,5},{2,6},{3,7},{4,0},{5,1},{6,2},{7,3},{8,12},{9,13},{10,... | collective-permute-start | bytes 983048 | tf_op jit(solution)/shard_map/ppermute | solution.py:333
  89.9 7.2 %collective-permute-start.23 = (bf16[32,3200]{1,0:T(8,128)(2,1)S(1)}, bf16[32,3200]{1,0:T(8,128)(2,1)S(1)}, u32[]{:S(2)}, u32[]{:S(2)}) collective-permute-start(bf16[32,3200]{1,0:T(8,128)(2,1)S(1)} %get-tuple-element.89), channel_id=1, source_target_pairs={{0,16},{1,17},{2,18},{3,19},{4,20},{5,21},{6,22},{7,23},{8,24},{9,... | collective-permute-start | bytes 614408 | tf_op jit(solution)/shard_map/ppermute | solution.py:333
  97.3 8.0 %collective-permute-start.25 = (bf16[32,1536]{1,0:T(8,128)(2,1)S(1)}, bf16[32,1536]{1,0:T(8,128)(2,1)S(1)}, u32[]{:S(2)}, u32[]{:S(2)}) collective-permute-start(bf16[32,1536]{1,0:T(8,128)(2,1)S(1)} %shard_map.110.refs_0_), channel_id=1, source_target_pairs={{0,16},{1,17},{2,18},{3,19},{4,20},{5,21},{6,22},{7,23},{8,24},{9,... | collective-permute-start | bytes 294920 | tf_op jit(solution)/shard_map/ppermute | solution.py:333
  97.8 7.5 %collective-permute-start.24 = (bf16[32,1536]{1,0:T(8,128)(2,1)S(1)}, bf16[32,1536]{1,0:T(8,128)(2,1)S(1)}, u32[]{:S(2)}, u32[]{:S(2)}) collective-permute-start(bf16[32,1536]{1,0:T(8,128)(2,1)S(1)} %shard_map.110.refs_0_), channel_id=1, source_target_pairs={{0,8},{1,9},{2,10},{3,11},{4,12},{5,13},{6,14},{7,15},{8,0},{9,1},... | collective-permute-start | bytes 294920 | tf_op jit(solution)/shard_map/ppermute | solution.py:333
  105.3 1.3 %collective-permute-start.26 = (bf16[32,1536]{1,0:T(8,128)(2,1)S(1)}, bf16[32,1536]{1,0:T(8,128)(2,1)S(1)}, u32[]{:S(2)}, u32[]{:S(2)}) collective-permute-start(bf16[32,1536]{1,0:T(8,128)(2,1)S(1)} %collective-permute-done.25.refs_2_), channel_id=1, source_target_pairs={{0,8},{1,9},{2,10},{3,11},{4,12},{5,13},{6,14},{7,15},{8,0},{9,1},... | collective-permute-start | bytes 294920 | tf_op jit(solution)/shard_map/ppermute | solution.py:333
  107.2 4.3 %collective-permute-start.27 = (bf16[32,1024]{1,0:T(8,128)(2,1)S(1)}, bf16[32,1024]{1,0:T(8,128)(2,1)S(1)}, u32[]{:S(2)}, u32[]{:S(2)}) collective-permute-start(bf16[32,1024]{1,0:T(8,128)(2,1)S(1)} %get-tuple-element.92), channel_id=1, source_target_pairs={{0,1},{1,0},{2,3},{3,2},{4,5},{5,4},{6,7},{7,6},{8,9},{9,8},{10,11... | collective-permute-start | bytes 196616 | tf_op jit(solution)/shard_map/ppermute | solution.py:333
  108.6 4.6 %collective-permute-start.28 = (bf16[32,1024]{1,0:T(8,128)(2,1)S(1)}, bf16[32,1024]{1,0:T(8,128)(2,1)S(1)}, u32[]{:S(2)}, u32[]{:S(2)}) collective-permute-start(bf16[32,1024]{1,0:T(8,128)(2,1)S(1)} %get-tuple-element.93), channel_id=1, source_target_pairs={{0,2},{1,3},{2,0},{3,1},{4,6},{5,7},{6,4},{7,5},{8,10},{9,11},{10,... | collective-permute-start | bytes 196616 | tf_op jit(solution)/shard_map/ppermute | solution.py:333
  108.6 5.5 %collective-permute-start.29 = (bf16[32,1024]{1,0:T(8,128)(2,1)S(1)}, bf16[32,1024]{1,0:T(8,128)(2,1)S(1)}, u32[]{:S(2)}, u32[]{:S(2)}) collective-permute-start(bf16[32,1024]{1,0:T(8,128)(2,1)S(1)} %get-tuple-element.94), channel_id=1, source_target_pairs={{0,3},{1,2},{2,1},{3,0},{4,7},{5,6},{6,5},{7,4},{8,11},{9,10},{10,... | collective-permute-start | bytes 196616 | tf_op jit(solution)/shard_map/ppermute | solution.py:333
  114.1 8.0 %collective-permute-start.30 = (bf16[64,1024]{1,0:T(8,128)(2,1)S(1)}, bf16[64,1024]{1,0:T(8,128)(2,1)S(1)}, u32[]{:S(2)}, u32[]{:S(2)}) collective-permute-start(bf16[64,1024]{1,0:T(8,128)(2,1)S(1)} %shard_map.112), channel_id=1, source_target_pairs={{0,4},{1,5},{2,6},{3,7},{4,0},{5,1},{6,2},{7,3},{8,12},{9,13},{10,... | collective-permute-start | bytes 393224 | tf_op jit(solution)/shard_map/ppermute | solution.py:333

commit v8 on v7

--- a/solution.py
+++ b/solution.py
@@ -335,7 +335,7 @@
     def after(x, *others):
         return lax.optimization_barrier((x, *others))[0]
 
-    cut = width - max(width * 3 // 8, 128)
+    cut = width // 2
     kv = new_keys_values.shape[3]
     msgs = call(
         functools.partial(pack_kernel, C, qw),
@@ -358,11 +358,9 @@
     step = [shards[d][0] for d in range(2, C, 2)]
     got[1] = after(got[1], *step)
     for d in range(2, C, 2):
-        shards[d].append(permute(after(out_weight[:, cut:], *got), exp=spread(d)))
-        shards[d + 1] = [permute(after(shards[d][0], *got), exp=1)]
+        shards[d].append(permute(after(out_weight[:, cut:], *step), exp=spread(d)))
+        shards[d + 1] = [permute(after(w, *got), exp=1) for w in shards[d]]
     step = shards[1] + [shards[d][1] for d in range(2, C, 2)]
-    for d in range(2, C, 2):
-        shards[d + 1].append(permute(after(shards[1][0], *step)[:, cut:], exp=spread(d)))
 
     step2 = step
 
@@ -419,7 +417,7 @@
     acc, last = project(mine_all, res)
     acc_far, last_far = project(theirs_all)
     gain = norm_gain.reshape(1, width)
-    parts = (rows * 3 // 8, rows * 5 // 8)
+    parts = (rows // 4, rows * 3 // 4)
     own, *full, keep, send = call(
         functools.partial(last_kernel, E, cap),
         [
@@ -462,14 +460,14 @@
             halve_kernel,
             [sds((count, wide + 128), F32), sds((count, wide + 128), BF16)],
             2,
-            cost=(0, 2**21),
+            cost=(0, 2**10),
         )(keep, permute(send, ctx=bit))
         bit *= 2
     activated = call(
         functools.partial(activate_kernel, hidden),
         sds((own_rows, hidden), BF16),
         2,
-        cost=(0, 2**20),
+        cost=(0, 2**10),
     )(keep, permute(send, ctx=bit))
     acts = {0: activated}
     acts[bit] = after(permute(activated, ctx=bit), arrived[1])

time: 124 us -> 125 us (level)
  waiting for transfers between devices: 68 us -> 76.6 us
  starting transfers between devices: 33.5 us -> 27.9 us
    ppermute x31, waiting for transfers between devices: 68 us -> 76.6 us  [permute(): return lax.ppermute(x, ('ctx', 'exp'), pairs)]
    ppermute x31, starting transfers between devices: 33.5 us -> 27.9 us  [permute(): return lax.ppermute(x, ('ctx', 'exp'), pairs)]
  transfers between devices with their start and end apart: 31 -> 31, of which waited for: 18 -> 17; matrix products, arithmetic and copies ran while one was open for 1% -> 0% of each run, Pallas kernels for 6% -> 5%
where the time goes in v8:
time: 125 us
  waiting for transfers between devices  76.6 us (61%)
  starting transfers between devices  27.9 us (22%)
  Pallas kernels  12.3 us (10%)
  local copies, waits for them, and re-layouts  7.71 us (6%)
    ppermute x31, waiting for transfers between devices, permute(): return lax.ppermute(x, ('ctx', 'exp'), pairs)  76.6 us
    ppermute x31, starting transfers between devices, permute(): return lax.ppermute(x, ('ctx', 'exp'), pairs)  27.9 us
    unnamed x22, local copies, waits for them, and re-layouts  6.44 us
    pallas_call x2, Pallas kernels, attend(): call(functools.partial(attend_kernel, C, t), [sds((rows, qw), BF16)] + [s...  4.68 us
  transfers between devices with their start and end apart: 31, of which 17 were waited for; matrix products, arithmetic and copies ran while one was open for 0% of the time, Pallas kernels for 5%

profile of v8, /device:TPU:0, one launch (start us, length us, event | category | flops | bytes accessed | tf_op | source)
XLA Modules:
  0.0 124.6 jit_solution(2808637421811031389)
XLA Ops:
  0.0 1.3 %fusion = (bf16[512,512]{1,0:T(8,128)(2,1)S(1)}, bf16[512,512]{1,0:T(8,128)(2,1)S(1)}) fusion(bf16[512,1024]{1,0:T(8,128)(2,1)} %refs_0_.1), kind=kLoop, calls=%fused_computation | loop fusion | bytes 2097152 | tf_op jit(solution)/shard_map/slice | solution.py:361
  1.3 3.1 %collective-permute-start.1 = (bf16[512,512]{1,0:T(8,128)(2,1)S(1)}, bf16[512,512]{1,0:T(8,128)(2,1)S(1)}, u32[]{:S(2)}, u32[]{:S(2)}) collective-permute-start(bf16[512,512]{1,0:T(8,128)(2,1)S(1)} %get-tuple-element.96), channel_id=1, source_target_pairs={{0,2},{1,3},{2,0},{3,1},{4,6},{5,7},{6,4},{7,5},{8,10},{9,11},{10,... | collective-permute-start | bytes 1572872 | tf_op jit(solution)/shard_map/ppermute | solution.py:333
  4.4 1.5 %collective-permute-start.12 = (bf16[512,1024]{1,0:T(8,128)(2,1)}, bf16[512,1024]{1,0:T(8,128)(2,1)S(1)}, u32[]{:S(2)}, u32[]{:S(2)}) collective-permute-start(bf16[512,1024]{1,0:T(8,128)(2,1)} %refs_0_.1), channel_id=1, source_target_pairs={{0,1},{1,0},{2,3},{3,2},{4,5},{5,4},{6,7},{7,6},{8,9},{9,8},{10,11... | collective-permute-start | bytes 3145736 | tf_op jit(solution)/shard_map/ppermute | solution.py:333
  5.9 1.0 copy-done.3
  6.9 0.8 copy-done.4
  7.7 0.8 copy-done.5
  9.0 1.6 %collective-permute-start.2 = (bf16[64,2048]{1,0:T(8,128)(2,1)S(1)}, bf16[64,2048]{1,0:T(8,128)(2,1)S(1)}, u32[]{:S(2)}, u32[]{:S(2)}) collective-permute-start(bf16[64,2048]{1,0:T(8,128)(2,1)S(1)} %get-tuple-element.53), channel_id=1, source_target_pairs={{0,16},{1,17},{2,18},{3,19},{4,20},{5,21},{6,22},{7,23},{8,24},{9,... | collective-permute-start | bytes 786440 | tf_op jit(solution)/shard_map/ppermute | solution.py:333
  10.6 5.7 %collective-permute-done.1.refs_7_.refs_6_ = bf16[512,512]{1,0:T(8,128)(2,1)S(1)} collective-permute-done((bf16[512,512]{1,0:T(8,128)(2,1)S(1)}, bf16[512,512]{1,0:T(8,128)(2,1)S(1)}, u32[]{:S(2)}, u32[]{:S(2)}) %collective-permute-start.1) | collective-permute-done | bytes 524320 | tf_op jit(solution)/shard_map/ppermute | solution.py:333
  16.3 1.7 %collective-permute-start.8 = (bf16[512,512]{1,0:T(8,128)(2,1)S(1)}, bf16[512,512]{1,0:T(8,128)(2,1)S(1)}, u32[]{:S(2)}, u32[]{:S(2)}) collective-permute-start(bf16[512,512]{1,0:T(8,128)(2,1)S(1)} %get-tuple-element.64), channel_id=1, source_target_pairs={{0,2},{1,3},{2,0},{3,1},{4,6},{5,7},{6,4},{7,5},{8,10},{9,11},{10,... | collective-permute-start | bytes 1572872 | tf_op jit(solution)/shard_map/ppermute | solution.py:333
  18.0 8.5 %collective-permute-done.3.refs_3_ = bf16[64,2048]{1,0:T(8,128)(2,1)S(1)} collective-permute-done((bf16[64,2048]{1,0:T(8,128)(2,1)S(1)}, bf16[64,2048]{1,0:T(8,128)(2,1)S(1)}, u32[]{:S(2)}, u32[]{:S(2)}) %collective-permute-start.3) | collective-permute-done | bytes 262176 | tf_op jit(solution)/shard_map/ppermute | solution.py:333
  26.6 2.3 %shard_map.101 = (bf16[256,512]{1,0:T(8,128)(2,1)S(1)}, bf16[64,2048]{1,0:T(8,128)(2,1)S(1)}) custom-call(bf16[64,2048]{1,0:T(8,128)(2,1)S(1)} %get-tuple-element.50.refs_0_, bf16[64,2048]{1,0:T(8,128)(2,1)S(1)} %collective-permute-done.refs_1_, bf16[64,2048]{1,0:T(8,128)(2,1)S(1)} %collective-permute-done.2.refs_2_, ...), custom_call_target="tpu_custom_call" | custom-call | bytes 16384 | tf_op jit(solution)/shard_map/pallas_call | solution.py:368
  28.9 2.6 %collective-permute-start.5 = (bf16[256,512]{1,0:T(8,128)(2,1)S(1)}, bf16[256,512]{1,0:T(8,128)(2,1)S(1)}, u32[]{:S(2)}, u32[]{:S(2)}) collective-permute-start(bf16[256,512]{1,0:T(8,128)(2,1)S(1)} %get-tuple-element.56), channel_id=1, source_target_pairs={{0,4},{1,5},{2,6},{3,7},{4,0},{5,1},{6,2},{7,3},{8,12},{9,13},{10,... | collective-permute-start | bytes 786440 | tf_op jit(solution)/shard_map/ppermute | solution.py:333
  31.6 2.3 %shard_map.102.refs_1_ = bf16[256,512]{1,0:T(8,128)(2,1)S(1)} custom-call(bf16[64,2048]{1,0:T(8,128)(2,1)S(1)} %get-tuple-element.55.refs_0_, bf16[64,2048]{1,0:T(8,128)(2,1)S(1)} %collective-permute-done.refs_1_, bf16[64,2048]{1,0:T(8,128)(2,1)S(1)} %collective-permute-done.2.refs_2_, bf16[64,2048]{1,0:T(8,128)(2,1)S(1)} %collective-permute-done.3.refs_3_), custom_call_target="tpu_custom_call" | custom-call | bytes 16384 | tf_op jit(solution)/shard_map/pallas_call | solution.py:368
  33.9 0.7 collective-permute-start.10
  34.6 1.5 %collective-permute-start.7 = (bf16[512,512]{1,0:T(8,128)(2,1)S(1)}, bf16[512,512]{1,0:T(8,128)(2,1)S(1)}, u32[]{:S(2)}, u32[]{:S(2)}) collective-permute-start(bf16[512,512]{1,0:T(8,128)(2,1)S(1)} %collective-permute-done.1.refs_7_.refs_6_), channel_id=1, source_target_pairs={{0,1},{1,0},{2,3},{3,2},{4,5},{5,4},{6,7},{7,6},{8,9},{9,8},{10,11... | collective-permute-start | bytes 1572872 | tf_op jit(solution)/shard_map/ppermute | solution.py:333
  36.1 1.2 copy-done
  37.3 1.0 copy-done.2
  38.4 0.7 copy-done.6
  39.1 0.7 copy-done.7
  40.7 3.0 %collective-permute-done.5.refs_0_ = bf16[256,512]{1,0:T(8,128)(2,1)S(1)} collective-permute-done((bf16[256,512]{1,0:T(8,128)(2,1)S(1)}, bf16[256,512]{1,0:T(8,128)(2,1)S(1)}, u32[]{:S(2)}, u32[]{:S(2)}) %collective-permute-start.5) | collective-permute-done | bytes 262176 | tf_op jit(solution)/shard_map/ppermute | solution.py:333
  43.8 8.1 %collective-permute-done.14.refs_2_ = bf16[256,512]{1,0:T(8,128)(2,1)S(1)} collective-permute-done((bf16[256,512]{1,0:T(8,128)(2,1)S(1)}, bf16[256,512]{1,0:T(8,128)(2,1)S(1)}, u32[]{:S(2)}, u32[]{:S(2)}) %collective-permute-start.14) | collective-permute-done | bytes 262176 | tf_op jit(solution)/shard_map/ppermute | solution.py:333
  52.6 6.4 %collective-permute-done.9.refs_5_ = bf16[512,512]{1,0:T(8,128)(2,1)S(1)} collective-permute-done((bf16[512,512]{1,0:T(8,128)(2,1)S(1)}, bf16[512,512]{1,0:T(8,128)(2,1)S(1)}, u32[]{:S(2)}, u32[]{:S(2)}) %collective-permute-start.9) | collective-permute-done | bytes 524320 | tf_op jit(solution)/shard_map/ppermute | solution.py:333
  59.0 1.1 shard_map.104
  60.1 1.1 shard_map.105
  61.2 1.4 %shard_map.106 = (f32[256,1024]{1,0:T(8,128)S(1)}, bf16[64,1024]{1,0:T(8,128)(2,1)S(1)}, bf16[192,1024]{1,0:T(8,128)(2,1)S(1)}, f32[128,1024]{1,0:T(8,128)S(1)}, bf16[128,1024]{1,0:T(8,128)(2,1)S(1)}) custom-call(f32[256,1024]{1,0:T(8,128)S(1)} %get-tuple-element.68.refs_0_, f32[256,1024]{1,0:T(8,128)S(1)} %get-tuple-element.70.refs_1_, ...), custom_call_target="tpu_custom_call" | custom-call | flops 671088640 | bytes 1048576 | tf_op jit(solution)/shard_map/pallas_call | solution.py:421
  63.0 12.7 %collective-permute-done.16.got_ref = bf16[128,1024]{1,0:T(8,128)(2,1)S(1)} collective-permute-done((bf16[128,1024]{1,0:T(8,128)(2,1)S(1)}, bf16[128,1024]{1,0:T(8,128)(2,1)S(1)}, u32[]{:S(2)}, u32[]{:S(2)}) %collective-permute-start.16) | collective-permute-done | bytes 262176 | tf_op jit(solution)/shard_map/ppermute | solution.py:333
  75.7 1.6 %collective-permute-start.19 = (bf16[32,1024]{1,0:T(8,128)(2,1)S(1)}, bf16[32,1024]{1,0:T(8,128)(2,1)S(1)}, u32[]{:S(2)}, u32[]{:S(2)}) collective-permute-start(bf16[32,1024]{1,0:T(8,128)(2,1)S(1)} %get-tuple-element.83), channel_id=1, source_target_pairs={{0,1},{1,0},{2,3},{3,2},{4,5},{5,4},{6,7},{7,6},{8,9},{9,8},{10,11... | collective-permute-start | bytes 196616 | tf_op jit(solution)/shard_map/ppermute | solution.py:333
  77.3 0.9 collective-permute-start.20
  78.2 1.1 collective-permute-start.21
  79.3 2.8 %collective-permute-done.17.got0 = bf16[64,1024]{1,0:T(8,128)(2,1)S(1)} collective-permute-done((bf16[64,1024]{1,0:T(8,128)(2,1)S(1)}, bf16[64,1024]{1,0:T(8,128)(2,1)S(1)}, u32[]{:S(2)}, u32[]{:S(2)}) %collective-permute-start.17) | collective-permute-done | bytes 131104 | tf_op jit(solution)/shard_map/ppermute | solution.py:333
  82.1 1.4 %collective-permute-done.20.refs_2_ = bf16[32,1024]{1,0:T(8,128)(2,1)S(1)} collective-permute-done((bf16[32,1024]{1,0:T(8,128)(2,1)S(1)}, bf16[32,1024]{1,0:T(8,128)(2,1)S(1)}, u32[]{:S(2)}, u32[]{:S(2)}) %collective-permute-start.20) | collective-permute-done | bytes 65568 | tf_op jit(solution)/shard_map/ppermute | solution.py:333
  83.5 1.7 %collective-permute-done.21.refs_3_ = bf16[32,1024]{1,0:T(8,128)(2,1)S(1)} collective-permute-done((bf16[32,1024]{1,0:T(8,128)(2,1)S(1)}, bf16[32,1024]{1,0:T(8,128)(2,1)S(1)}, u32[]{:S(2)}, u32[]{:S(2)}) %collective-permute-start.21) | collective-permute-done | bytes 65568 | tf_op jit(solution)/shard_map/ppermute | solution.py:333
  85.2 1.3 %shard_map.108 = (f32[64,3200]{1,0:T(8,128)S(1)}, bf16[64,3200]{1,0:T(8,128)(2,1)S(1)}) custom-call(bf16[32,1024]{1,0:T(8,128)(2,1)S(1)} %get-tuple-element.82.refs_0_, bf16[32,1024]{1,0:T(8,128)(2,1)S(1)} %collective-permute-done.19.refs_1_, bf16[32,1024]{1,0:T(8,128)(2,1)S(1)} %collective-permute-done.20.refs_2_, ...), custom_call_target="tpu_custom_call" | custom-call | flops 805306368 | bytes 6291456 | tf_op jit(solution)/shard_map/pallas_call | solution.py:449
  86.8 1.5 %collective-permute-done.22.got_ref = bf16[64,3200]{1,0:T(8,128)(2,1)S(1)} collective-permute-done((bf16[64,3200]{1,0:T(8,128)(2,1)S(1)}, bf16[64,3200]{1,0:T(8,128)(2,1)S(1)}, u32[]{:S(2)}, u32[]{:S(2)}) %collective-permute-start.22) | collective-permute-done | bytes 409632 | tf_op jit(solution)/shard_map/ppermute | solution.py:333
  88.4 2.1 %collective-permute-start.23 = (bf16[32,3200]{1,0:T(8,128)(2,1)S(1)}, bf16[32,3200]{1,0:T(8,128)(2,1)S(1)}, u32[]{:S(2)}, u32[]{:S(2)}) collective-permute-start(bf16[32,3200]{1,0:T(8,128)(2,1)S(1)} %get-tuple-element.89), channel_id=1, source_target_pairs={{0,16},{1,17},{2,18},{3,19},{4,20},{5,21},{6,22},{7,23},{8,24},{9,... | collective-permute-start | bytes 614408 | tf_op jit(solution)/shard_map/ppermute | solution.py:333
  90.4 5.4 %collective-permute-done.23.got_ref = bf16[32,3200]{1,0:T(8,128)(2,1)S(1)} collective-permute-done((bf16[32,3200]{1,0:T(8,128)(2,1)S(1)}, bf16[32,3200]{1,0:T(8,128)(2,1)S(1)}, u32[]{:S(2)}, u32[]{:S(2)}) %collective-permute-start.23) | collective-permute-done | bytes 204832 | tf_op jit(solution)/shard_map/ppermute | solution.py:333
  96.0 1.8 %collective-permute-start.25 = (bf16[32,1536]{1,0:T(8,128)(2,1)S(1)}, bf16[32,1536]{1,0:T(8,128)(2,1)S(1)}, u32[]{:S(2)}, u32[]{:S(2)}) collective-permute-start(bf16[32,1536]{1,0:T(8,128)(2,1)S(1)} %shard_map.110.refs_0_), channel_id=1, source_target_pairs={{0,16},{1,17},{2,18},{3,19},{4,20},{5,21},{6,22},{7,23},{8,24},{9,... | collective-permute-start | bytes 294920 | tf_op jit(solution)/shard_map/ppermute | solution.py:333
  97.8 9.0 %collective-permute-done.18.got1 = bf16[192,1024]{1,0:T(8,128)(2,1)S(1)} collective-permute-done((bf16[192,1024]{1,0:T(8,128)(2,1)S(1)}, bf16[192,1024]{1,0:T(8,128)(2,1)S(1)}, u32[]{:S(2)}, u32[]{:S(2)}) %collective-permute-start.18) | collective-permute-done | bytes 393248 | tf_op jit(solution)/shard_map/ppermute | solution.py:333
  106.8 1.2 collective-permute-done.26.refs_3_
  108.1 0.7 shard_map.111
  108.8 0.6 collective-permute-start.27
  109.4 2.9 %collective-permute-start.29 = (bf16[32,1024]{1,0:T(8,128)(2,1)S(1)}, bf16[32,1024]{1,0:T(8,128)(2,1)S(1)}, u32[]{:S(2)}, u32[]{:S(2)}) collective-permute-start(bf16[32,1024]{1,0:T(8,128)(2,1)S(1)} %get-tuple-element.94), channel_id=1, source_target_pairs={{0,3},{1,2},{2,1},{3,0},{4,7},{5,6},{6,5},{7,4},{8,11},{9,10},{10,... | collective-permute-start | bytes 196616 | tf_op jit(solution)/shard_map/ppermute | solution.py:333
  112.3 0.8 collective-permute-done.27.refs_1_
  113.1 1.1 collective-permute-done.28.refs_2_
  114.2 1.4 %collective-permute-done.29.refs_3_ = bf16[32,1024]{1,0:T(8,128)(2,1)S(1)} collective-permute-done((bf16[32,1024]{1,0:T(8,128)(2,1)S(1)}, bf16[32,1024]{1,0:T(8,128)(2,1)S(1)}, u32[]{:S(2)}, u32[]{:S(2)}) %collective-permute-start.29) | collective-permute-done | bytes 65568 | tf_op jit(solution)/shard_map/ppermute | solution.py:333
  115.6 2.0 %collective-permute-start.30 = (bf16[64,1024]{1,0:T(8,128)(2,1)S(1)}, bf16[64,1024]{1,0:T(8,128)(2,1)S(1)}, u32[]{:S(2)}, u32[]{:S(2)}) collective-permute-start(bf16[64,1024]{1,0:T(8,128)(2,1)S(1)} %shard_map.112), channel_id=1, source_target_pairs={{0,4},{1,5},{2,6},{3,7},{4,0},{5,1},{6,2},{7,3},{8,12},{9,13},{10,... | collective-permute-start | bytes 393224 | tf_op jit(solution)/shard_map/ppermute | solution.py:333
  117.6 5.9 %collective-permute-done.30.refs_4_ = bf16[64,1024]{1,0:T(8,128)(2,1)S(1)} collective-permute-done((bf16[64,1024]{1,0:T(8,128)(2,1)S(1)}, bf16[64,1024]{1,0:T(8,128)(2,1)S(1)}, u32[]{:S(2)}, u32[]{:S(2)}) %collective-permute-start.30) | collective-permute-done | bytes 131104 | tf_op jit(solution)/shard_map/ppermute | solution.py:333
  123.4 1.1 shard_map.113
  (52 shorter events, 3.2 us)
Async XLA Ops:
  1.3 15.0 %collective-permute-start.1 = (bf16[512,512]{1,0:T(8,128)(2,1)S(1)}, bf16[512,512]{1,0:T(8,128)(2,1)S(1)}, u32[]{:S(2)}, u32[]{:S(2)}) collective-permute-start(bf16[512,512]{1,0:T(8,128)(2,1)S(1)} %get-tuple-element.96), channel_id=1, source_target_pairs={{0,2},{1,3},{2,0},{3,1},{4,6},{5,7},{6,4},{7,5},{8,10},{9,11},{10,... | collective-permute-start | bytes 1572872 | tf_op jit(solution)/shard_map/ppermute | solution.py:333
  4.4 39.4 %collective-permute-start.12 = (bf16[512,1024]{1,0:T(8,128)(2,1)}, bf16[512,1024]{1,0:T(8,128)(2,1)S(1)}, u32[]{:S(2)}, u32[]{:S(2)}) collective-permute-start(bf16[512,1024]{1,0:T(8,128)(2,1)} %refs_0_.1), channel_id=1, source_target_pairs={{0,1},{1,0},{2,3},{3,2},{4,5},{5,4},{6,7},{7,6},{8,9},{9,8},{10,11... | collective-permute-start | bytes 3145736 | tf_op jit(solution)/shard_map/ppermute | solution.py:333
  5.9 1.0 copy-start.3
  6.9 0.8 copy-start.4
  7.7 0.8 copy-start.5
  8.9 9.1 %collective-permute-start = (bf16[64,2048]{1,0:T(8,128)(2,1)S(1)}, bf16[64,2048]{1,0:T(8,128)(2,1)S(1)}, u32[]{:S(2)}, u32[]{:S(2)}) collective-permute-start(bf16[64,2048]{1,0:T(8,128)(2,1)S(1)} %get-tuple-element.51), channel_id=1, source_target_pairs={{0,8},{1,9},{2,10},{3,11},{4,12},{5,13},{6,14},{7,15},{8,0},{9,1},... | collective-permute-start | bytes 786440 | tf_op jit(solution)/shard_map/ppermute | solution.py:333
  9.0 9.0 %collective-permute-start.2 = (bf16[64,2048]{1,0:T(8,128)(2,1)S(1)}, bf16[64,2048]{1,0:T(8,128)(2,1)S(1)}, u32[]{:S(2)}, u32[]{:S(2)}) collective-permute-start(bf16[64,2048]{1,0:T(8,128)(2,1)S(1)} %get-tuple-element.53), channel_id=1, source_target_pairs={{0,16},{1,17},{2,18},{3,19},{4,20},{5,21},{6,22},{7,23},{8,24},{9,... | collective-permute-start | bytes 786440 | tf_op jit(solution)/shard_map/ppermute | solution.py:333
  16.3 23.8 %collective-permute-start.8 = (bf16[512,512]{1,0:T(8,128)(2,1)S(1)}, bf16[512,512]{1,0:T(8,128)(2,1)S(1)}, u32[]{:S(2)}, u32[]{:S(2)}) collective-permute-start(bf16[512,512]{1,0:T(8,128)(2,1)S(1)} %get-tuple-element.64), channel_id=1, source_target_pairs={{0,2},{1,3},{2,0},{3,1},{4,6},{5,7},{6,4},{7,5},{8,10},{9,11},{10,... | collective-permute-start | bytes 1572872 | tf_op jit(solution)/shard_map/ppermute | solution.py:333
  18.0 8.5 %collective-permute-start.3 = (bf16[64,2048]{1,0:T(8,128)(2,1)S(1)}, bf16[64,2048]{1,0:T(8,128)(2,1)S(1)}, u32[]{:S(2)}, u32[]{:S(2)}) collective-permute-start(bf16[64,2048]{1,0:T(8,128)(2,1)S(1)} %get-tuple-element.54), channel_id=1, source_target_pairs={{0,24},{1,25},{2,26},{3,27},{4,28},{5,29},{6,30},{7,31},{8,16},{9,... | collective-permute-start | bytes 786440 | tf_op jit(solution)/shard_map/ppermute | solution.py:333
  28.9 14.8 %collective-permute-start.5 = (bf16[256,512]{1,0:T(8,128)(2,1)S(1)}, bf16[256,512]{1,0:T(8,128)(2,1)S(1)}, u32[]{:S(2)}, u32[]{:S(2)}) collective-permute-start(bf16[256,512]{1,0:T(8,128)(2,1)S(1)} %get-tuple-element.56), channel_id=1, source_target_pairs={{0,4},{1,5},{2,6},{3,7},{4,0},{5,1},{6,2},{7,3},{8,12},{9,13},{10,... | collective-permute-start | bytes 786440 | tf_op jit(solution)/shard_map/ppermute | solution.py:333
  33.9 9.9 %collective-permute-start.10 = (bf16[256,512]{1,0:T(8,128)(2,1)S(1)}, bf16[256,512]{1,0:T(8,128)(2,1)S(1)}, u32[]{:S(2)}, u32[]{:S(2)}) collective-permute-start(bf16[256,512]{1,0:T(8,128)(2,1)S(1)} %shard_map.102.refs_1_), channel_id=1, source_target_pairs={{0,16},{1,17},{2,18},{3,19},{4,20},{5,21},{6,22},{7,23},{8,24},{9,... | collective-permute-start | bytes 786440 | tf_op jit(solution)/shard_map/ppermute | solution.py:333
  34.6 18.0 %collective-permute-start.7 = (bf16[512,512]{1,0:T(8,128)(2,1)S(1)}, bf16[512,512]{1,0:T(8,128)(2,1)S(1)}, u32[]{:S(2)}, u32[]{:S(2)}) collective-permute-start(bf16[512,512]{1,0:T(8,128)(2,1)S(1)} %collective-permute-done.1.refs_7_.refs_6_), channel_id=1, source_target_pairs={{0,1},{1,0},{2,3},{3,2},{4,5},{5,4},{6,7},{7,6},{8,9},{9,8},{10,11... | collective-permute-start | bytes 1572872 | tf_op jit(solution)/shard_map/ppermute | solution.py:333
  36.1 1.2 copy-start
  37.3 1.0 copy-start.2
  38.4 0.7 copy-start.6
  39.1 0.7 copy-start.7
  40.1 18.9 %collective-permute-start.9 = (bf16[512,512]{1,0:T(8,128)(2,1)S(1)}, bf16[512,512]{1,0:T(8,128)(2,1)S(1)}, u32[]{:S(2)}, u32[]{:S(2)}) collective-permute-start(bf16[512,512]{1,0:T(8,128)(2,1)S(1)} %collective-permute-done.8.refs_8_.refs_7_), channel_id=1, source_target_pairs={{0,1},{1,0},{2,3},{3,2},{4,5},{5,4},{6,7},{7,6},{8,9},{9,8},{10,11... | collective-permute-start | bytes 1572872 | tf_op jit(solution)/shard_map/ppermute | solution.py:333
  43.7 8.3 %collective-permute-start.14 = (bf16[256,512]{1,0:T(8,128)(2,1)S(1)}, bf16[256,512]{1,0:T(8,128)(2,1)S(1)}, u32[]{:S(2)}, u32[]{:S(2)}) collective-permute-start(bf16[256,512]{1,0:T(8,128)(2,1)S(1)} %collective-permute-done.5.refs_0_), channel_id=1, source_target_pairs={{0,16},{1,17},{2,18},{3,19},{4,20},{5,21},{6,22},{7,23},{8,24},{9,... | collective-permute-start | bytes 786440 | tf_op jit(solution)/shard_map/ppermute | solution.py:333
  43.7 8.3 %collective-permute-start.4 = (bf16[256,512]{1,0:T(8,128)(2,1)S(1)}, bf16[256,512]{1,0:T(8,128)(2,1)S(1)}, u32[]{:S(2)}, u32[]{:S(2)}) collective-permute-start(bf16[256,512]{1,0:T(8,128)(2,1)S(1)} %shard_map.102.refs_1_), channel_id=1, source_target_pairs={{0,8},{1,9},{2,10},{3,11},{4,12},{5,13},{6,14},{7,15},{8,0},{9,1},... | collective-permute-start | bytes 786440 | tf_op jit(solution)/shard_map/ppermute | solution.py:333
  43.8 8.7 %collective-permute-start.6 = (bf16[128,256]{1,0:T(8,128)(2,1)S(1)}, bf16[128,256]{1,0:T(8,128)(2,1)S(1)}, u32[]{:S(2)}, u32[]{:S(2)}) collective-permute-start(bf16[128,256]{1,0:T(8,128)(2,1)S(1)} %get-tuple-element.62.refs_6_.place_ref), channel_id=1, source_target_pairs={{0,4},{1,5},{2,6},{3,7},{4,0},{5,1},{6,2},{7,3},{8,12},{9,13},{10,... | collective-permute-start | bytes 196616 | tf_op jit(solution)/shard_map/ppermute | solution.py:333
  52.0 7.0 %collective-permute-start.11 = (bf16[256,512]{1,0:T(8,128)(2,1)S(1)}, bf16[256,512]{1,0:T(8,128)(2,1)S(1)}, u32[]{:S(2)}, u32[]{:S(2)}) collective-permute-start(bf16[256,512]{1,0:T(8,128)(2,1)S(1)} %collective-permute-done.10.refs_3_), channel_id=1, source_target_pairs={{0,8},{1,9},{2,10},{3,11},{4,12},{5,13},{6,14},{7,15},{8,0},{9,1},... | collective-permute-start | bytes 786440 | tf_op jit(solution)/shard_map/ppermute | solution.py:333
  52.0 8.1 %collective-permute-start.13 = (bf16[256,512]{1,0:T(8,128)(2,1)S(1)}, bf16[256,512]{1,0:T(8,128)(2,1)S(1)}, u32[]{:S(2)}, u32[]{:S(2)}) collective-permute-start(bf16[256,512]{1,0:T(8,128)(2,1)S(1)} %collective-permute-done.5.refs_0_), channel_id=1, source_target_pairs={{0,8},{1,9},{2,10},{3,11},{4,12},{5,13},{6,14},{7,15},{8,0},{9,1},... | collective-permute-start | bytes 786440 | tf_op jit(solution)/shard_map/ppermute | solution.py:333
  52.5 7.6 %collective-permute-start.15 = (bf16[256,512]{1,0:T(8,128)(2,1)S(1)}, bf16[256,512]{1,0:T(8,128)(2,1)S(1)}, u32[]{:S(2)}, u32[]{:S(2)}) collective-permute-start(bf16[256,512]{1,0:T(8,128)(2,1)S(1)} %collective-permute-done.14.refs_2_), channel_id=1, source_target_pairs={{0,8},{1,9},{2,10},{3,11},{4,12},{5,13},{6,14},{7,15},{8,0},{9,1},... | collective-permute-start | bytes 786440 | tf_op jit(solution)/shard_map/ppermute | solution.py:333
  59.0 16.7 %copy-start.8 = (f32[1024]{0:T(1024)S(1)}, f32[1024]{0:T(1024)}, u32[]{:S(2)}) copy-start(f32[1024]{0:T(1024)} %param.15) | copy-start | bytes 12292
  59.0 26.2 %slice-start = ((s8[6291456]{0:T(1024)(128)(4,1)}), s8[4194304]{0:T(1024)(128)(4,1)S(1)}, s32[]{:S(2)}) async-start(s8[6291456]{0:T(1024)(128)(4,1)} %bitcast.16), calls=%async_computation | async-start | bytes 8388608
  60.1 25.1 %slice-start.1 = ((s8[6291456]{0:T(1024)(128)(4,1)}), s8[2097152]{0:T(1024)(128)(4,1)S(1)}, s32[]{:S(2)}) async-start(s8[6291456]{0:T(1024)(128)(4,1)} %bitcast.16), calls=%async_computation.1 | async-start | bytes 4194304
  61.2 46.9 %copy-start.1 = (bf16[1,1536,1024]{2,1,0:T(8,128)(2,1)S(1)}, bf16[1,1536,1024]{2,1,0:T(8,128)(2,1)}, u32[]{:S(2)}) copy-start(bf16[1,1536,1024]{2,1,0:T(8,128)(2,1)} %param.19) | copy-start | bytes 9437188
  62.6 13.1 %collective-permute-start.16 = (bf16[128,1024]{1,0:T(8,128)(2,1)S(1)}, bf16[128,1024]{1,0:T(8,128)(2,1)S(1)}, u32[]{:S(2)}, u32[]{:S(2)}) collective-permute-start(bf16[128,1024]{1,0:T(8,128)(2,1)S(1)} %get-tuple-element.75), channel_id=1, source_target_pairs={{0,4},{1,5},{2,6},{3,7},{4,0},{5,1},{6,2},{7,3},{8,12},{9,13},{10,... | collective-permute-start | bytes 786440 | tf_op jit(solution)/shard_map/ppermute | solution.py:333
  75.7 6.4 %collective-permute-start.17 = (bf16[64,1024]{1,0:T(8,128)(2,1)S(1)}, bf16[64,1024]{1,0:T(8,128)(2,1)S(1)}, u32[]{:S(2)}, u32[]{:S(2)}) collective-permute-start(bf16[64,1024]{1,0:T(8,128)(2,1)S(1)} %get-tuple-element.76), channel_id=1, source_target_pairs={{0,4},{1,5},{2,6},{3,7},{4,0},{5,1},{6,2},{7,3},{8,12},{9,13},{10,... | collective-permute-start | bytes 393224 | tf_op jit(solution)/shard_map/ppermute | solution.py:333
  75.7 6.3 %collective-permute-start.19 = (bf16[32,1024]{1,0:T(8,128)(2,1)S(1)}, bf16[32,1024]{1,0:T(8,128)(2,1)S(1)}, u32[]{:S(2)}, u32[]{:S(2)}) collective-permute-start(bf16[32,1024]{1,0:T(8,128)(2,1)S(1)} %get-tuple-element.83), channel_id=1, source_target_pairs={{0,1},{1,0},{2,3},{3,2},{4,5},{5,4},{6,7},{7,6},{8,9},{9,8},{10,11... | collective-permute-start | bytes 196616 | tf_op jit(solution)/shard_map/ppermute | solution.py:333
  77.3 6.1 %collective-permute-start.20 = (bf16[32,1024]{1,0:T(8,128)(2,1)S(1)}, bf16[32,1024]{1,0:T(8,128)(2,1)S(1)}, u32[]{:S(2)}, u32[]{:S(2)}) collective-permute-start(bf16[32,1024]{1,0:T(8,128)(2,1)S(1)} %get-tuple-element.84), channel_id=1, source_target_pairs={{0,2},{1,3},{2,0},{3,1},{4,6},{5,7},{6,4},{7,5},{8,10},{9,11},{10,... | collective-permute-start | bytes 196616 | tf_op jit(solution)/shard_map/ppermute | solution.py:333
  78.2 7.0 %collective-permute-start.21 = (bf16[32,1024]{1,0:T(8,128)(2,1)S(1)}, bf16[32,1024]{1,0:T(8,128)(2,1)S(1)}, u32[]{:S(2)}, u32[]{:S(2)}) collective-permute-start(bf16[32,1024]{1,0:T(8,128)(2,1)S(1)} %get-tuple-element.85), channel_id=1, source_target_pairs={{0,3},{1,2},{2,1},{3,0},{4,7},{5,6},{6,5},{7,4},{8,11},{9,10},{10,... | collective-permute-start | bytes 196616 | tf_op jit(solution)/shard_map/ppermute | solution.py:333
  86.5 1.8 %collective-permute-start.22 = (bf16[64,3200]{1,0:T(8,128)(2,1)S(1)}, bf16[64,3200]{1,0:T(8,128)(2,1)S(1)}, u32[]{:S(2)}, u32[]{:S(2)}) collective-permute-start(bf16[64,3200]{1,0:T(8,128)(2,1)S(1)} %get-tuple-element.87), channel_id=1, source_target_pairs={{0,8},{1,9},{2,10},{3,11},{4,12},{5,13},{6,14},{7,15},{8,0},{9,1},... | collective-permute-start | bytes 1228808 | tf_op jit(solution)/shard_map/ppermute | solution.py:333
  86.5 20.3 %collective-permute-start.18 = (bf16[192,1024]{1,0:T(8,128)(2,1)S(1)}, bf16[192,1024]{1,0:T(8,128)(2,1)S(1)}, u32[]{:S(2)}, u32[]{:S(2)}) collective-permute-start(bf16[192,1024]{1,0:T(8,128)(2,1)S(1)} %get-tuple-element.78), channel_id=1, source_target_pairs={{0,4},{1,5},{2,6},{3,7},{4,0},{5,1},{6,2},{7,3},{8,12},{9,13},{10,... | collective-permute-start | bytes 1179656 | tf_op jit(solution)/shard_map/ppermute | solution.py:333
  88.4 7.4 %collective-permute-start.23 = (bf16[32,3200]{1,0:T(8,128)(2,1)S(1)}, bf16[32,3200]{1,0:T(8,128)(2,1)S(1)}, u32[]{:S(2)}, u32[]{:S(2)}) collective-permute-start(bf16[32,3200]{1,0:T(8,128)(2,1)S(1)} %get-tuple-element.89), channel_id=1, source_target_pairs={{0,16},{1,17},{2,18},{3,19},{4,20},{5,21},{6,22},{7,23},{8,24},{9,... | collective-permute-start | bytes 614408 | tf_op jit(solution)/shard_map/ppermute | solution.py:333
  96.0 10.8 %collective-permute-start.25 = (bf16[32,1536]{1,0:T(8,128)(2,1)S(1)}, bf16[32,1536]{1,0:T(8,128)(2,1)S(1)}, u32[]{:S(2)}, u32[]{:S(2)}) collective-permute-start(bf16[32,1536]{1,0:T(8,128)(2,1)S(1)} %shard_map.110.refs_0_), channel_id=1, source_target_pairs={{0,16},{1,17},{2,18},{3,19},{4,20},{5,21},{6,22},{7,23},{8,24},{9,... | collective-permute-start | bytes 294920 | tf_op jit(solution)/shard_map/ppermute | solution.py:333
  97.8 9.1 %collective-permute-start.24 = (bf16[32,1536]{1,0:T(8,128)(2,1)S(1)}, bf16[32,1536]{1,0:T(8,128)(2,1)S(1)}, u32[]{:S(2)}, u32[]{:S(2)}) collective-permute-start(bf16[32,1536]{1,0:T(8,128)(2,1)S(1)} %shard_map.110.refs_0_), channel_id=1, source_target_pairs={{0,8},{1,9},{2,10},{3,11},{4,12},{5,13},{6,14},{7,15},{8,0},{9,1},... | collective-permute-start | bytes 294920 | tf_op jit(solution)/shard_map/ppermute | solution.py:333
  106.8 1.3 %collective-permute-start.26 = (bf16[32,1536]{1,0:T(8,128)(2,1)S(1)}, bf16[32,1536]{1,0:T(8,128)(2,1)S(1)}, u32[]{:S(2)}, u32[]{:S(2)}) collective-permute-start(bf16[32,1536]{1,0:T(8,128)(2,1)S(1)} %collective-permute-done.25.refs_2_), channel_id=1, source_target_pairs={{0,8},{1,9},{2,10},{3,11},{4,12},{5,13},{6,14},{7,15},{8,0},{9,1},... | collective-permute-start | bytes 294920 | tf_op jit(solution)/shard_map/ppermute | solution.py:333
  108.8 4.3 %collective-permute-start.27 = (bf16[32,1024]{1,0:T(8,128)(2,1)S(1)}, bf16[32,1024]{1,0:T(8,128)(2,1)S(1)}, u32[]{:S(2)}, u32[]{:S(2)}) collective-permute-start(bf16[32,1024]{1,0:T(8,128)(2,1)S(1)} %get-tuple-element.92), channel_id=1, source_target_pairs={{0,1},{1,0},{2,3},{3,2},{4,5},{5,4},{6,7},{7,6},{8,9},{9,8},{10,11... | collective-permute-start | bytes 196616 | tf_op jit(solution)/shard_map/ppermute | solution.py:333
  109.4 4.8 %collective-permute-start.28 = (bf16[32,1024]{1,0:T(8,128)(2,1)S(1)}, bf16[32,1024]{1,0:T(8,128)(2,1)S(1)}, u32[]{:S(2)}, u32[]{:S(2)}) collective-permute-start(bf16[32,1024]{1,0:T(8,128)(2,1)S(1)} %get-tuple-element.93), channel_id=1, source_target_pairs={{0,2},{1,3},{2,0},{3,1},{4,6},{5,7},{6,4},{7,5},{8,10},{9,11},{10,... | collective-permute-start | bytes 196616 | tf_op jit(solution)/shard_map/ppermute | solution.py:333
  109.4 6.2 %collective-permute-start.29 = (bf16[32,1024]{1,0:T(8,128)(2,1)S(1)}, bf16[32,1024]{1,0:T(8,128)(2,1)S(1)}, u32[]{:S(2)}, u32[]{:S(2)}) collective-permute-start(bf16[32,1024]{1,0:T(8,128)(2,1)S(1)} %get-tuple-element.94), channel_id=1, source_target_pairs={{0,3},{1,2},{2,1},{3,0},{4,7},{5,6},{6,5},{7,4},{8,11},{9,10},{10,... | collective-permute-start | bytes 196616 | tf_op jit(solution)/shard_map/ppermute | solution.py:333
  115.6 7.9 %collective-permute-start.30 = (bf16[64,1024]{1,0:T(8,128)(2,1)S(1)}, bf16[64,1024]{1,0:T(8,128)(2,1)S(1)}, u32[]{:S(2)}, u32[]{:S(2)}) collective-permute-start(bf16[64,1024]{1,0:T(8,128)(2,1)S(1)} %shard_map.112), channel_id=1, source_target_pairs={{0,4},{1,5},{2,6},{3,7},{4,0},{5,1},{6,2},{7,3},{8,12},{9,13},{10,... | collective-permute-start | bytes 393224 | tf_op jit(solution)/shard_map/ppermute | solution.py:333

commit v9 on v8

--- a/solution.py
+++ b/solution.py
@@ -154,7 +154,7 @@
     place_ref[...] = jnp.where(slot == places, 1.0, 0.0).astype(BF16)
 
 
-def project_kernel(C, cut, with_residual, *refs):
+def project_kernel(C, with_residual, *refs):
     refs, (acc, last, stacked) = list(refs[:-3]), refs[-3:]
     res = refs.pop(0) if with_residual else None
     atts, ws = refs[:C], refs[C:]
@@ -163,34 +163,29 @@
     for s in range(C):
         stacked[jnp.bitwise_xor(turn, s)] = atts[s][...]
     last[...] = stacked[C - 1]
-    width = acc.shape[1]
-    for j, at in enumerate((slice(0, cut), slice(cut, width))):
+    half = acc.shape[1] // 2
+    for j in range(2):
+        at = slice(j * half, (j + 1) * half)
         total = res[:, at].astype(F32) if with_residual else None
         for d in range(C - 1):
-            if d < 2:
-                w = ws[d][:, at]
-            else:
-                w = ws[2 * d - 2 + j][...]
-            term = dot(stacked[d], w)
+            term = dot(stacked[d], ws[d][:, at])
             total = term if total is None else total + term
         acc[:, at] = total
 
 
 def last_kernel(E, cap, *refs):
-    accs, lasts, ws, places = refs[:2], refs[2:4], refs[4:6], refs[6:8]
-    own_ref, *full_refs, keep_ref, send_ref = refs[8:]
-    cut = ws[0].shape[1]
-    for j, cols in enumerate((slice(0, cut), slice(cut, own_ref.shape[1]))):
+    accs, lasts, w_ref, places = refs[:2], refs[2:4], refs[4], refs[5:7]
+    own_ref, full_ref, keep_ref, send_ref = refs[7:]
+    half = w_ref.shape[1] // 2
+    for j in range(2):
+        cols = slice(j * half, (j + 1) * half)
         for t in (1, 0):
-            total = accs[t][:, cols] + dot(lasts[t][...], ws[j][...])
+            total = accs[t][:, cols] + dot(lasts[t][...], w_ref[:, cols])
             rounded = total.astype(BF16)
             if t == 0:
                 own_ref[:, cols] = total
             else:
-                first = 0
-                for full in full_refs:
-                    full[:, cols] = rounded[first : first + full.shape[0]]
-                    first += full.shape[0]
+                full_ref[:, cols] = rounded
             picked = dot(places[t][...], rounded)
             for d in range(E // 2):
                 near, far = spread(d) ^ (PAIR * t), spread(d) ^ PAIR ^ (PAIR * t)
@@ -208,7 +203,7 @@
 
 
 def gate_up_kernel(C, E, cap, order, *refs):
-    xs, gain_ref, w_ref, keep_ref, send_ref, x_s, part_s = refs[: E // 2], *refs[E // 2 :]
+    xs, gain_ref, w_ref, keep_ref, *sends, x_s, part_s = refs[: E // 2], *refs[E // 2 :]
     c = lax.axis_index("ctx")
     e = lax.axis_index("exp")
     own_rows = E * cap // C
@@ -231,7 +226,9 @@
         if i < C // 2:
             keep_ref[i * own_rows : (i + 1) * own_rows, :] = block
         else:
-            to = (i - C // 2) * own_rows
+            first = (i - C // 2) * own_rows
+            send_ref = sends[first // sends[0].shape[0]]
+            to = first % sends[0].shape[0]
             send_ref[to : to + own_rows, :wide] = block[:, :wide].astype(BF16)
             square = block[:, wide:]
             high = square.astype(BF16).astype(F32)
@@ -241,13 +238,13 @@
             send_ref[to : to + own_rows, wide:] = pair.astype(BF16)
 
 
-def halve_kernel(keep_in, got_ref, keep_ref, send_ref):
+def halve_kernel(keep_in, got0, got1, keep_ref, send_ref):
     rows = keep_ref.shape[0]
     wide = keep_ref.shape[1] - 128
-    total = keep_in[...] + got_ref[...].astype(F32)
-    keep_ref[...] = total[:rows]
-    send_ref[:, :wide] = total[rows:, :wide].astype(BF16)
-    square = jnp.sum(total[rows:, wide:], axis=1, keepdims=True)
+    keep_ref[...] = keep_in[:rows, :] + got0[...].astype(F32)
+    total = keep_in[rows:, :] + got1[...].astype(F32)
+    send_ref[:, :wide] = total[:, :wide].astype(BF16)
+    square = jnp.sum(total[:, wide:], axis=1, keepdims=True)
     high = square.astype(BF16).astype(F32)
     lane = lax.broadcasted_iota(jnp.int32, (rows, 128), 1)
     pair = jnp.where(lane == 0, high, jnp.where(lane == 1, square - high, 0.0))
@@ -285,7 +282,7 @@
         refs[-1][d * cap : (d + 1) * cap, :] = x[cap:, :]
 
 
-def combine_kernel(E, cap, own, got0, got1, place_ref, gate_ref, *refs):
+def combine_kernel(E, cap, own, got, place_ref, gate_ref, *refs):
     xs, far, out, x_s = refs[: E // 2], refs[E // 2], refs[E // 2 + 1], refs[E // 2 + 2]
     for d in range(E // 2):
         at = spread(d) * cap
@@ -298,10 +295,8 @@
         collected = lax.dot_general(
             place_ref[...], x_s[:, cols], (((0,), (0,)), ((), ())), preferred_element_type=F32
         )
-        few = got0.shape[0]
-        for got, at in ((got0, slice(0, few)), (got1, slice(few, own.shape[0]))):
-            mixed = own[at, cols] + got[:, cols].astype(F32)
-            out[at, cols] = (mixed + gate_ref[at, :1] * collected[at]).astype(BF16)
+        mixed = own[:, cols] + got[:, cols].astype(F32)
+        out[:, cols] = (mixed + gate_ref[:, :1] * collected).astype(BF16)
 
 
 def body(
@@ -335,7 +330,6 @@
     def after(x, *others):
         return lax.optimization_barrier((x, *others))[0]
 
-    cut = width // 2
     kv = new_keys_values.shape[3]
     msgs = call(
         functools.partial(pack_kernel, C, qw),
@@ -352,17 +346,10 @@
     )
     res = residual.reshape(rows, width)
     got = [msgs[0]] + [permute(msgs[s], ctx=s) for s in range(1, C)]
-    shards = {0: [out_weight], 1: [permute(out_weight, exp=1)]}
+    shards = {0: out_weight, 1: permute(out_weight, exp=1)}
     for d in range(2, C, 2):
-        shards[d] = [permute(out_weight[:, :cut], exp=spread(d))]
-    step = [shards[d][0] for d in range(2, C, 2)]
-    got[1] = after(got[1], *step)
-    for d in range(2, C, 2):
-        shards[d].append(permute(after(out_weight[:, cut:], *step), exp=spread(d)))
-        shards[d + 1] = [permute(after(w, *got), exp=1) for w in shards[d]]
-    step = shards[1] + [shards[d][1] for d in range(2, C, 2)]
-
-    step2 = step
+        shards[d] = permute(out_weight, exp=spread(d))
+    step = [shards[d] for d in range(2, C, 2)]
 
     def attend(t, msgs):
         return call(
@@ -376,7 +363,9 @@
 
     other, own_msg = attend(1, got)
     theirs = permute(other, exp=PAIR)
-    (mine,) = attend(0, [own_msg, after(got[1], other)] + got[2:])
+    for d in range(2, C, 2):
+        shards[d + 1] = permute(after(shards[d], other), exp=1)
+    (mine,) = attend(0, [own_msg, after(got[1], other, *step)] + got[2:])
     tokens_last = lambda x: jnp.transpose(x.reshape(C, tok, x.shape[3]), (0, 2, 1))
     place, gate, *staged = call(
         functools.partial(route_kernel, E, cap),
@@ -387,7 +376,7 @@
         cost=(0, 2**14),
         limit=16,
     )(tokens_last(after(routes, mine)), tokens_last(after(gates, mine)), out_weight, res)
-    shards[0], res = staged[:1], staged[1]
+    shards[0], res = staged
 
     def gather(x, before):
         atts = {0: x, 1: permute(x, ctx=1)}
@@ -397,15 +386,14 @@
         return [atts[s] for s in range(C)]
 
     other_place = permute(after(place, theirs), exp=PAIR)
-    step = shards[C - 1]
     mine_all = gather(mine, [])
-    theirs_all = gather(after(theirs, place, *step2), [])
-    mine_all[1] = after(mine_all[1], other_place, *step)
+    theirs_all = gather(after(theirs, place, shards[1], *mine_all[2::2]), [])
+    mine_all[1] = after(mine_all[1], other_place)
 
     def project(atts, *extra):
-        operands = [*extra, *atts, *[w for d in range(C - 1) for w in shards[d]]]
+        operands = [*extra, *atts, *[shards[d] for d in range(C - 1)]]
         return call(
-            functools.partial(project_kernel, C, cut, bool(extra)),
+            functools.partial(project_kernel, C, bool(extra)),
             [sds((rows, width), F32), sds((rows, qw), BF16)],
             len(operands),
             scratch=[
@@ -417,18 +405,17 @@
     acc, last = project(mine_all, res)
     acc_far, last_far = project(theirs_all)
     gain = norm_gain.reshape(1, width)
-    parts = (rows // 4, rows * 3 // 4)
-    own, *full, keep, send = call(
+    own, full, keep, send = call(
         functools.partial(last_kernel, E, cap),
         [
             sds((rows, width), F32),
-            *[sds((n, width), BF16) for n in parts],
+            sds((rows, width), BF16),
             sds((slots, width), F32),
             sds((slots, width), BF16),
         ],
-        8,
+        7,
         cost=(4 * rows * (qw + slots) * width, 2**20),
-    )(acc, acc_far, last, last_far, *shards[C - 1], place, other_place)
+    )(acc, acc_far, last, last_far, shards[C - 1], place, other_place)
     received = permute(send, exp=PAIR)
     outgoing = call(
         outgoing_kernel, [sds((2 * cap, width), BF16)] * (E // 2), 3, cost=(0, 2**20)
@@ -437,18 +424,16 @@
     for d in reversed(range(1, E // 2)):
         incoming[d] = permute(outgoing[d], exp=spread(d))
     incoming = [incoming[d] for d in range(E // 2)]
-    arrived = [permute(after(full[0], received), exp=PAIR)]
-    incoming[0] = after(incoming[0], arrived[0])
-    arrived.append(permute(after(full[1], arrived[0]), exp=PAIR))
+    arrived = permute(after(full, received), exp=PAIR)
 
     order = [0]
     bit = C // 2
     while bit:
         order = order + [r | bit for r in order]
         bit //= 2
-    keep, send = call(
+    keep, *sends = call(
         functools.partial(gate_up_kernel, C, E, cap, order),
-        [sds((slots // 2, wide + 128), F32), sds((slots // 2, wide + 128), BF16)],
+        [sds((slots // 2, wide + 128), F32)] + [sds((slots // 4, wide + 128), BF16)] * 2,
         E // 2 + 2,
         scratch=[pltpu.VMEM((slots, width), BF16), pltpu.VMEM((slots, wide + 128), F32)],
         cost=(2 * slots * width * wide, 2 * width * wide),
@@ -459,9 +444,10 @@
         keep, send = call(
             halve_kernel,
             [sds((count, wide + 128), F32), sds((count, wide + 128), BF16)],
-            2,
+            3,
             cost=(0, 2**10),
-        )(keep, permute(send, ctx=bit))
+        )(keep, *[permute(x, ctx=bit) for x in sends])
+        sends = [send[: count // 2], send[count // 2 :]]
         bit *= 2
     activated = call(
         functools.partial(activate_kernel, hidden),
@@ -470,7 +456,7 @@
         cost=(0, 2**10),
     )(keep, permute(send, ctx=bit))
     acts = {0: activated}
-    acts[bit] = after(permute(activated, ctx=bit), arrived[1])
+    acts[bit] = after(permute(activated, ctx=bit), arrived)
     bit //= 2
     while bit:
         for r in list(acts):
@@ -491,10 +477,10 @@
     result = call(
         functools.partial(combine_kernel, E, cap),
         sds((rows, width), BF16),
-        6 + E // 2,
+        5 + E // 2,
         scratch=[pltpu.VMEM((slots, width), BF16)],
         cost=(0, 2 * 2**20),
-    )(own, *arrived, place, gate, *returned, permute(far, exp=PAIR))
+    )(own, arrived, place, gate, *returned, permute(far, exp=PAIR))
     return result.reshape(C, 1, tok, width)
 
 

time: 125 us -> 114 us (0.912)
  waiting for transfers between devices: 76.6 us -> 66.8 us
  local copies, waits for them, and re-layouts: 7.71 us -> 6.45 us
    ppermute x31 -> x29, waiting for transfers between devices: 76.6 us -> 66.8 us  [permute(): return lax.ppermute(x, ('ctx', 'exp'), pairs)]
    slice x1 -> x0, local copies, waits for them, and re-layouts: 1.27 us -> none  [body(): shards[d].append(permute(after(out_weight[:, cut:], *step), exp=spread(d)))]
    ppermute x31 -> x29, starting transfers between devices: 27.9 us -> 28.3 us  [permute(): return lax.ppermute(x, ('ctx', 'exp'), pairs)]
  transfers between devices with their start and end apart: 31 -> 29, of which waited for: 17 -> 19; matrix products, arithmetic and copies ran while one was open for 0% -> 0% of each run, Pallas kernels for 5% -> 8%
where the time goes in v9:
time: 114 us
  waiting for transfers between devices  66.8 us (59%)
  starting transfers between devices  28.3 us (25%)
  Pallas kernels  12.3 us (11%)
  local copies, waits for them, and re-layouts  6.45 us (6%)
    ppermute x29, waiting for transfers between devices, permute(): return lax.ppermute(x, ('ctx', 'exp'), pairs)  66.8 us
    ppermute x29, starting transfers between devices, permute(): return lax.ppermute(x, ('ctx', 'exp'), pairs)  28.3 us
    unnamed x22, local copies, waits for them, and re-layouts  6.45 us
    pallas_call x2, Pallas kernels, attend(): call(functools.partial(attend_kernel, C, t), [sds((rows, qw), BF16)] + [s...  4.67 us
  transfers between devices with their start and end apart: 29, of which 19 were waited for; matrix products, arithmetic and copies ran while one was open for 0% of the time, Pallas kernels for 8%

profile of v9, /device:TPU:0, one launch (start us, length us, event | category | flops | bytes accessed | tf_op | source)
XLA Modules:
  0.0 114.0 jit_solution(13414833307690792004)
XLA Ops:
  0.0 3.0 %collective-permute-start.3 = (bf16[512,1024]{1,0:T(8,128)(2,1)}, bf16[512,1024]{1,0:T(8,128)(2,1)S(1)}, u32[]{:S(2)}, u32[]{:S(2)}) collective-permute-start(bf16[512,1024]{1,0:T(8,128)(2,1)} %refs_0_.1), channel_id=1, source_target_pairs={{0,2},{1,3},{2,0},{3,1},{4,6},{5,7},{6,4},{7,5},{8,10},{9,11},{10,... | collective-permute-start | bytes 3145736 | tf_op jit(solution)/shard_map/ppermute | solution.py:328
  3.0 1.5 %collective-permute-start.9 = (bf16[512,1024]{1,0:T(8,128)(2,1)}, bf16[512,1024]{1,0:T(8,128)(2,1)S(1)}, u32[]{:S(2)}, u32[]{:S(2)}) collective-permute-start(bf16[512,1024]{1,0:T(8,128)(2,1)} %refs_0_.1), channel_id=1, source_target_pairs={{0,1},{1,0},{2,3},{3,2},{4,5},{5,4},{6,7},{7,6},{8,9},{9,8},{10,11... | collective-permute-start | bytes 3145736 | tf_op jit(solution)/shard_map/ppermute | solution.py:328
  4.5 1.0 copy-done.3
  5.6 0.8 copy-done.4
  6.4 0.8 copy-done.5
  7.7 1.6 %collective-permute-start.1 = (bf16[64,2048]{1,0:T(8,128)(2,1)S(1)}, bf16[64,2048]{1,0:T(8,128)(2,1)S(1)}, u32[]{:S(2)}, u32[]{:S(2)}) collective-permute-start(bf16[64,2048]{1,0:T(8,128)(2,1)S(1)} %get-tuple-element.47), channel_id=1, source_target_pairs={{0,16},{1,17},{2,18},{3,19},{4,20},{5,21},{6,22},{7,23},{8,24},{9,... | collective-permute-start | bytes 786440 | tf_op jit(solution)/shard_map/ppermute | solution.py:328
  9.6 7.3 %collective-permute-done.1.refs_2_ = bf16[64,2048]{1,0:T(8,128)(2,1)S(1)} collective-permute-done((bf16[64,2048]{1,0:T(8,128)(2,1)S(1)}, bf16[64,2048]{1,0:T(8,128)(2,1)S(1)}, u32[]{:S(2)}, u32[]{:S(2)}) %collective-permute-start.1) | collective-permute-done | bytes 262176 | tf_op jit(solution)/shard_map/ppermute | solution.py:328
  16.9 4.7 %collective-permute-done.2.refs_3_ = bf16[64,2048]{1,0:T(8,128)(2,1)S(1)} collective-permute-done((bf16[64,2048]{1,0:T(8,128)(2,1)S(1)}, bf16[64,2048]{1,0:T(8,128)(2,1)S(1)}, u32[]{:S(2)}, u32[]{:S(2)}) %collective-permute-start.2) | collective-permute-done | bytes 262176 | tf_op jit(solution)/shard_map/ppermute | solution.py:328
  21.6 2.3 %shard_map.101 = (bf16[256,512]{1,0:T(8,128)(2,1)S(1)}, bf16[64,2048]{1,0:T(8,128)(2,1)S(1)}) custom-call(bf16[64,2048]{1,0:T(8,128)(2,1)S(1)} %get-tuple-element.45.refs_0_, bf16[64,2048]{1,0:T(8,128)(2,1)S(1)} %collective-permute-done.refs_1_, bf16[64,2048]{1,0:T(8,128)(2,1)S(1)} %collective-permute-done.1.refs_2_, ...), custom_call_target="tpu_custom_call" | custom-call | bytes 16384 | tf_op jit(solution)/shard_map/pallas_call | solution.py:355
  23.9 2.5 %collective-permute-done.3.refs_7_.refs_6_ = bf16[512,1024]{1,0:T(8,128)(2,1)S(1)} collective-permute-done((bf16[512,1024]{1,0:T(8,128)(2,1)}, bf16[512,1024]{1,0:T(8,128)(2,1)S(1)}, u32[]{:S(2)}, u32[]{:S(2)}) %collective-permute-start.3) | collective-permute-done | bytes 1048608 | tf_op jit(solution)/shard_map/ppermute | solution.py:328
  26.4 1.7 %collective-permute-start.13 = (bf16[512,1024]{1,0:T(8,128)(2,1)S(1)}, bf16[512,1024]{1,0:T(8,128)(2,1)S(1)}, u32[]{:S(2)}, u32[]{:S(2)}) collective-permute-start(bf16[512,1024]{1,0:T(8,128)(2,1)S(1)} %collective-permute-done.3.refs_7_.refs_6_), channel_id=1, source_target_pairs={{0,1},{1,0},{2,3},{3,2},{4,5},{5,4},{6,7},{7,6},{8,9},{9,8},{10,11... | collective-permute-start | bytes 3145736 | tf_op jit(solution)/shard_map/ppermute | solution.py:328
  28.0 2.6 %collective-permute-start.5 = (bf16[256,512]{1,0:T(8,128)(2,1)S(1)}, bf16[256,512]{1,0:T(8,128)(2,1)S(1)}, u32[]{:S(2)}, u32[]{:S(2)}) collective-permute-start(bf16[256,512]{1,0:T(8,128)(2,1)S(1)} %get-tuple-element.50), channel_id=1, source_target_pairs={{0,4},{1,5},{2,6},{3,7},{4,0},{5,1},{6,2},{7,3},{8,12},{9,13},{10,... | collective-permute-start | bytes 786440 | tf_op jit(solution)/shard_map/ppermute | solution.py:328
  30.6 2.3 %shard_map.102.refs_1_ = bf16[256,512]{1,0:T(8,128)(2,1)S(1)} custom-call(bf16[64,2048]{1,0:T(8,128)(2,1)S(1)} %get-tuple-element.49.refs_0_, bf16[64,2048]{1,0:T(8,128)(2,1)S(1)} %collective-permute-done.refs_1_, bf16[64,2048]{1,0:T(8,128)(2,1)S(1)} %collective-permute-done.1.refs_2_, bf16[64,2048]{1,0:T(8,128)(2,1)S(1)} %collective-permute-done.2.refs_3_), custom_call_target="tpu_custom_call" | custom-call | bytes 16384 | tf_op jit(solution)/shard_map/pallas_call | solution.py:355
  33.0 1.6 %collective-permute-start.7 = (bf16[256,512]{1,0:T(8,128)(2,1)S(1)}, bf16[256,512]{1,0:T(8,128)(2,1)S(1)}, u32[]{:S(2)}, u32[]{:S(2)}) collective-permute-start(bf16[256,512]{1,0:T(8,128)(2,1)S(1)} %shard_map.102.refs_1_), channel_id=1, source_target_pairs={{0,16},{1,17},{2,18},{3,19},{4,20},{5,21},{6,22},{7,23},{8,24},{9,... | collective-permute-start | bytes 786440 | tf_op jit(solution)/shard_map/ppermute | solution.py:328
  34.6 1.2 %copy-done.1 = bf16[512,1024]{1,0:T(8,128)(2,1)S(1)} copy-done((bf16[512,1024]{1,0:T(8,128)(2,1)S(1)}, bf16[512,1024]{1,0:T(8,128)(2,1)}, u32[]{:S(2)}) %copy-start.1) | copy-done | bytes 1048600
  35.8 1.0 copy-done.2
  36.8 0.7 copy-done.6
  37.5 0.7 copy-done.7
  38.6 2.9 %collective-permute-done.5.refs_0_ = bf16[256,512]{1,0:T(8,128)(2,1)S(1)} collective-permute-done((bf16[256,512]{1,0:T(8,128)(2,1)S(1)}, bf16[256,512]{1,0:T(8,128)(2,1)S(1)}, u32[]{:S(2)}, u32[]{:S(2)}) %collective-permute-start.5) | collective-permute-done | bytes 262176 | tf_op jit(solution)/shard_map/ppermute | solution.py:328
  41.5 1.5 %collective-permute-start.11 = (bf16[256,512]{1,0:T(8,128)(2,1)S(1)}, bf16[256,512]{1,0:T(8,128)(2,1)S(1)}, u32[]{:S(2)}, u32[]{:S(2)}) collective-permute-start(bf16[256,512]{1,0:T(8,128)(2,1)S(1)} %collective-permute-done.5.refs_0_), channel_id=1, source_target_pairs={{0,16},{1,17},{2,18},{3,19},{4,20},{5,21},{6,22},{7,23},{8,24},{9,... | collective-permute-start | bytes 786440 | tf_op jit(solution)/shard_map/ppermute | solution.py:328
  43.0 0.5 collective-permute-start.8
  43.5 5.1 %collective-permute-done.11.refs_2_ = bf16[256,512]{1,0:T(8,128)(2,1)S(1)} collective-permute-done((bf16[256,512]{1,0:T(8,128)(2,1)S(1)}, bf16[256,512]{1,0:T(8,128)(2,1)S(1)}, u32[]{:S(2)}, u32[]{:S(2)}) %collective-permute-start.11) | collective-permute-done | bytes 262176 | tf_op jit(solution)/shard_map/ppermute | solution.py:328
  48.6 0.6 collective-permute-done.6.refs_6_
  49.2 1.1 shard_map.104
  50.7 1.1 shard_map.105
  51.8 1.4 %shard_map.106 = (f32[256,1024]{1,0:T(8,128)S(1)}, bf16[256,1024]{1,0:T(8,128)(2,1)S(1)}, f32[128,1024]{1,0:T(8,128)S(1)}, bf16[128,1024]{1,0:T(8,128)(2,1)S(1)}) custom-call(f32[256,1024]{1,0:T(8,128)S(1)} %get-tuple-element.59.refs_0_, f32[256,1024]{1,0:T(8,128)S(1)} %get-tuple-element.61.refs_1_, bf16[256,512]{1,0:T(8,128)(2,1)S(1)} %get-tuple-element.62.refs_2_, ...), custom_call_target="tpu_custom_call" | custom-call | flops 671088640 | bytes 1048576 | tf_op jit(solution)/shard_map/pallas_call | solution.py:408
  53.2 1.4 %collective-permute-start.14 = (bf16[128,1024]{1,0:T(8,128)(2,1)S(1)}, bf16[128,1024]{1,0:T(8,128)(2,1)S(1)}, u32[]{:S(2)}, u32[]{:S(2)}) collective-permute-start(bf16[128,1024]{1,0:T(8,128)(2,1)S(1)} %get-tuple-element.67), channel_id=1, source_target_pairs={{0,4},{1,5},{2,6},{3,7},{4,0},{5,1},{6,2},{7,3},{8,12},{9,13},{10,... | collective-permute-start | bytes 786440 | tf_op jit(solution)/shard_map/ppermute | solution.py:328
  54.7 13.5 %collective-permute-done.14.got_ref = bf16[128,1024]{1,0:T(8,128)(2,1)S(1)} collective-permute-done((bf16[128,1024]{1,0:T(8,128)(2,1)S(1)}, bf16[128,1024]{1,0:T(8,128)(2,1)S(1)}, u32[]{:S(2)}, u32[]{:S(2)}) %collective-permute-start.14) | collective-permute-done | bytes 262176 | tf_op jit(solution)/shard_map/ppermute | solution.py:328
  68.2 0.7 collective-permute-start.16
  69.0 2.8 %collective-permute-start.18 = (bf16[32,1024]{1,0:T(8,128)(2,1)S(1)}, bf16[32,1024]{1,0:T(8,128)(2,1)S(1)}, u32[]{:S(2)}, u32[]{:S(2)}) collective-permute-start(bf16[32,1024]{1,0:T(8,128)(2,1)S(1)} %get-tuple-element.74), channel_id=1, source_target_pairs={{0,3},{1,2},{2,1},{3,0},{4,7},{5,6},{6,5},{7,4},{8,11},{9,10},{10,... | collective-permute-start | bytes 196616 | tf_op jit(solution)/shard_map/ppermute | solution.py:328
  71.8 1.5 %collective-permute-done.16.refs_1_ = bf16[32,1024]{1,0:T(8,128)(2,1)S(1)} collective-permute-done((bf16[32,1024]{1,0:T(8,128)(2,1)S(1)}, bf16[32,1024]{1,0:T(8,128)(2,1)S(1)}, u32[]{:S(2)}, u32[]{:S(2)}) %collective-permute-start.16) | collective-permute-done | bytes 65568 | tf_op jit(solution)/shard_map/ppermute | solution.py:328
  73.3 1.6 %collective-permute-done.18.refs_3_ = bf16[32,1024]{1,0:T(8,128)(2,1)S(1)} collective-permute-done((bf16[32,1024]{1,0:T(8,128)(2,1)S(1)}, bf16[32,1024]{1,0:T(8,128)(2,1)S(1)}, u32[]{:S(2)}, u32[]{:S(2)}) %collective-permute-start.18) | collective-permute-done | bytes 65568 | tf_op jit(solution)/shard_map/ppermute | solution.py:328
  74.9 1.3 %shard_map.108 = (f32[64,3200]{1,0:T(8,128)S(1)}, bf16[32,3200]{1,0:T(8,128)(2,1)S(1)}, bf16[32,3200]{1,0:T(8,128)(2,1)S(1)}) custom-call(bf16[32,1024]{1,0:T(8,128)(2,1)S(1)} %get-tuple-element.71.refs_0_, bf16[32,1024]{1,0:T(8,128)(2,1)S(1)} %collective-permute-done.16.refs_1_, bf16[32,1024]{1,0:T(8,128)(2,1)S(1)} %collective-permute-done.17.refs_2_, ...), custom_call_target="tpu_custom_call" | custom-call | flops 805306368 | bytes 6291456 | tf_op jit(solution)/shard_map/pallas_call | solution.py:434
  76.7 0.9 collective-permute-done.19.got0
  78.0 1.6 %collective-permute-start.21 = (bf16[32,3200]{1,0:T(8,128)(2,1)S(1)}, bf16[32,3200]{1,0:T(8,128)(2,1)S(1)}, u32[]{:S(2)}, u32[]{:S(2)}) collective-permute-start(bf16[32,3200]{1,0:T(8,128)(2,1)S(1)} %get-tuple-element.79), channel_id=1, source_target_pairs={{0,16},{1,17},{2,18},{3,19},{4,20},{5,21},{6,22},{7,23},{8,24},{9,... | collective-permute-start | bytes 614408 | tf_op jit(solution)/shard_map/ppermute | solution.py:328
  79.6 5.6 %collective-permute-done.21.got_ref = bf16[32,3200]{1,0:T(8,128)(2,1)S(1)} collective-permute-done((bf16[32,3200]{1,0:T(8,128)(2,1)S(1)}, bf16[32,3200]{1,0:T(8,128)(2,1)S(1)}, u32[]{:S(2)}, u32[]{:S(2)}) %collective-permute-start.21) | collective-permute-done | bytes 204832 | tf_op jit(solution)/shard_map/ppermute | solution.py:328
  85.4 1.6 %collective-permute-start.23 = (bf16[32,1536]{1,0:T(8,128)(2,1)S(1)}, bf16[32,1536]{1,0:T(8,128)(2,1)S(1)}, u32[]{:S(2)}, u32[]{:S(2)}) collective-permute-start(bf16[32,1536]{1,0:T(8,128)(2,1)S(1)} %shard_map.110.refs_0_), channel_id=1, source_target_pairs={{0,16},{1,17},{2,18},{3,19},{4,20},{5,21},{6,22},{7,23},{8,24},{9,... | collective-permute-start | bytes 294920 | tf_op jit(solution)/shard_map/ppermute | solution.py:328
  87.1 9.1 %collective-permute-done.15.got = bf16[256,1024]{1,0:T(8,128)(2,1)S(1)} collective-permute-done((bf16[256,1024]{1,0:T(8,128)(2,1)S(1)}, bf16[256,1024]{1,0:T(8,128)(2,1)S(1)}, u32[]{:S(2)}, u32[]{:S(2)}) %collective-permute-start.15) | collective-permute-done | bytes 524320 | tf_op jit(solution)/shard_map/ppermute | solution.py:328
  96.2 1.3 %collective-permute-done.24.refs_3_ = bf16[32,1536]{1,0:T(8,128)(2,1)S(1)} collective-permute-done((bf16[32,1536]{1,0:T(8,128)(2,1)S(1)}, bf16[32,1536]{1,0:T(8,128)(2,1)S(1)}, u32[]{:S(2)}, u32[]{:S(2)}) %collective-permute-start.24) | collective-permute-done | bytes 98336 | tf_op jit(solution)/shard_map/ppermute | solution.py:328
  97.5 0.7 shard_map.111
  98.2 0.8 collective-permute-start.25
  98.9 2.8 %collective-permute-start.27 = (bf16[32,1024]{1,0:T(8,128)(2,1)S(1)}, bf16[32,1024]{1,0:T(8,128)(2,1)S(1)}, u32[]{:S(2)}, u32[]{:S(2)}) collective-permute-start(bf16[32,1024]{1,0:T(8,128)(2,1)S(1)} %get-tuple-element.84), channel_id=1, source_target_pairs={{0,3},{1,2},{2,1},{3,0},{4,7},{5,6},{6,5},{7,4},{8,11},{9,10},{10,... | collective-permute-start | bytes 196616 | tf_op jit(solution)/shard_map/ppermute | solution.py:328
  101.7 0.8 collective-permute-done.25.refs_1_
  102.5 1.1 collective-permute-done.26.refs_2_
  103.6 1.4 %collective-permute-done.27.refs_3_ = bf16[32,1024]{1,0:T(8,128)(2,1)S(1)} collective-permute-done((bf16[32,1024]{1,0:T(8,128)(2,1)S(1)}, bf16[32,1024]{1,0:T(8,128)(2,1)S(1)}, u32[]{:S(2)}, u32[]{:S(2)}) %collective-permute-start.27) | collective-permute-done | bytes 65568 | tf_op jit(solution)/shard_map/ppermute | solution.py:328
  105.0 1.7 %collective-permute-start.28 = (bf16[64,1024]{1,0:T(8,128)(2,1)S(1)}, bf16[64,1024]{1,0:T(8,128)(2,1)S(1)}, u32[]{:S(2)}, u32[]{:S(2)}) collective-permute-start(bf16[64,1024]{1,0:T(8,128)(2,1)S(1)} %shard_map.112), channel_id=1, source_target_pairs={{0,4},{1,5},{2,6},{3,7},{4,0},{5,1},{6,2},{7,3},{8,12},{9,13},{10,... | collective-permute-start | bytes 393224 | tf_op jit(solution)/shard_map/ppermute | solution.py:328
  106.6 6.2 %collective-permute-done.28.refs_4_ = bf16[64,1024]{1,0:T(8,128)(2,1)S(1)} collective-permute-done((bf16[64,1024]{1,0:T(8,128)(2,1)S(1)}, bf16[64,1024]{1,0:T(8,128)(2,1)S(1)}, u32[]{:S(2)}, u32[]{:S(2)}) %collective-permute-start.28) | collective-permute-done | bytes 131104 | tf_op jit(solution)/shard_map/ppermute | solution.py:328
  112.9 1.1 shard_map.113
  (47 shorter events, 2.6 us)
Async XLA Ops:
  0.0 26.4 %collective-permute-start.3 = (bf16[512,1024]{1,0:T(8,128)(2,1)}, bf16[512,1024]{1,0:T(8,128)(2,1)S(1)}, u32[]{:S(2)}, u32[]{:S(2)}) collective-permute-start(bf16[512,1024]{1,0:T(8,128)(2,1)} %refs_0_.1), channel_id=1, source_target_pairs={{0,2},{1,3},{2,0},{3,1},{4,6},{5,7},{6,4},{7,5},{8,10},{9,11},{10,... | collective-permute-start | bytes 3145736 | tf_op jit(solution)/shard_map/ppermute | solution.py:328
  3.0 38.4 %collective-permute-start.9 = (bf16[512,1024]{1,0:T(8,128)(2,1)}, bf16[512,1024]{1,0:T(8,128)(2,1)S(1)}, u32[]{:S(2)}, u32[]{:S(2)}) collective-permute-start(bf16[512,1024]{1,0:T(8,128)(2,1)} %refs_0_.1), channel_id=1, source_target_pairs={{0,1},{1,0},{2,3},{3,2},{4,5},{5,4},{6,7},{7,6},{8,9},{9,8},{10,11... | collective-permute-start | bytes 3145736 | tf_op jit(solution)/shard_map/ppermute | solution.py:328
  4.5 1.0 copy-start.3
  5.6 0.8 copy-start.4
  6.4 0.8 copy-start.5
  7.6 1.9 %collective-permute-start = (bf16[64,2048]{1,0:T(8,128)(2,1)S(1)}, bf16[64,2048]{1,0:T(8,128)(2,1)S(1)}, u32[]{:S(2)}, u32[]{:S(2)}) collective-permute-start(bf16[64,2048]{1,0:T(8,128)(2,1)S(1)} %get-tuple-element.46), channel_id=1, source_target_pairs={{0,8},{1,9},{2,10},{3,11},{4,12},{5,13},{6,14},{7,15},{8,0},{9,1},... | collective-permute-start | bytes 786440 | tf_op jit(solution)/shard_map/ppermute | solution.py:328
  7.7 9.2 %collective-permute-start.1 = (bf16[64,2048]{1,0:T(8,128)(2,1)S(1)}, bf16[64,2048]{1,0:T(8,128)(2,1)S(1)}, u32[]{:S(2)}, u32[]{:S(2)}) collective-permute-start(bf16[64,2048]{1,0:T(8,128)(2,1)S(1)} %get-tuple-element.47), channel_id=1, source_target_pairs={{0,16},{1,17},{2,18},{3,19},{4,20},{5,21},{6,22},{7,23},{8,24},{9,... | collective-permute-start | bytes 786440 | tf_op jit(solution)/shard_map/ppermute | solution.py:328
  9.3 12.3 %collective-permute-start.2 = (bf16[64,2048]{1,0:T(8,128)(2,1)S(1)}, bf16[64,2048]{1,0:T(8,128)(2,1)S(1)}, u32[]{:S(2)}, u32[]{:S(2)}) collective-permute-start(bf16[64,2048]{1,0:T(8,128)(2,1)S(1)} %get-tuple-element.48), channel_id=1, source_target_pairs={{0,24},{1,25},{2,26},{3,27},{4,28},{5,29},{6,30},{7,31},{8,16},{9,... | collective-permute-start | bytes 786440 | tf_op jit(solution)/shard_map/ppermute | solution.py:328
  26.4 25.4 %collective-permute-start.13 = (bf16[512,1024]{1,0:T(8,128)(2,1)S(1)}, bf16[512,1024]{1,0:T(8,128)(2,1)S(1)}, u32[]{:S(2)}, u32[]{:S(2)}) collective-permute-start(bf16[512,1024]{1,0:T(8,128)(2,1)S(1)} %collective-permute-done.3.refs_7_.refs_6_), channel_id=1, source_target_pairs={{0,1},{1,0},{2,3},{3,2},{4,5},{5,4},{6,7},{7,6},{8,9},{9,8},{10,11... | collective-permute-start | bytes 3145736 | tf_op jit(solution)/shard_map/ppermute | solution.py:328
  28.0 13.4 %collective-permute-start.5 = (bf16[256,512]{1,0:T(8,128)(2,1)S(1)}, bf16[256,512]{1,0:T(8,128)(2,1)S(1)}, u32[]{:S(2)}, u32[]{:S(2)}) collective-permute-start(bf16[256,512]{1,0:T(8,128)(2,1)S(1)} %get-tuple-element.50), channel_id=1, source_target_pairs={{0,4},{1,5},{2,6},{3,7},{4,0},{5,1},{6,2},{7,3},{8,12},{9,13},{10,... | collective-permute-start | bytes 786440 | tf_op jit(solution)/shard_map/ppermute | solution.py:328
  33.0 8.5 %collective-permute-start.7 = (bf16[256,512]{1,0:T(8,128)(2,1)S(1)}, bf16[256,512]{1,0:T(8,128)(2,1)S(1)}, u32[]{:S(2)}, u32[]{:S(2)}) collective-permute-start(bf16[256,512]{1,0:T(8,128)(2,1)S(1)} %shard_map.102.refs_1_), channel_id=1, source_target_pairs={{0,16},{1,17},{2,18},{3,19},{4,20},{5,21},{6,22},{7,23},{8,24},{9,... | collective-permute-start | bytes 786440 | tf_op jit(solution)/shard_map/ppermute | solution.py:328
  34.6 1.2 %copy-start.1 = (bf16[512,1024]{1,0:T(8,128)(2,1)S(1)}, bf16[512,1024]{1,0:T(8,128)(2,1)}, u32[]{:S(2)}) copy-start(bf16[512,1024]{1,0:T(8,128)(2,1)} %refs_0_.1) | copy-start | bytes 3145732
  35.8 1.0 copy-start.2
  36.8 0.7 copy-start.6
  37.5 0.7 copy-start.7
  41.5 7.1 %collective-permute-start.11 = (bf16[256,512]{1,0:T(8,128)(2,1)S(1)}, bf16[256,512]{1,0:T(8,128)(2,1)S(1)}, u32[]{:S(2)}, u32[]{:S(2)}) collective-permute-start(bf16[256,512]{1,0:T(8,128)(2,1)S(1)} %collective-permute-done.5.refs_0_), channel_id=1, source_target_pairs={{0,16},{1,17},{2,18},{3,19},{4,20},{5,21},{6,22},{7,23},{8,24},{9,... | collective-permute-start | bytes 786440 | tf_op jit(solution)/shard_map/ppermute | solution.py:328
  43.0 6.2 %collective-permute-start.6 = (bf16[128,256]{1,0:T(8,128)(2,1)S(1)}, bf16[128,256]{1,0:T(8,128)(2,1)S(1)}, u32[]{:S(2)}, u32[]{:S(2)}) collective-permute-start(bf16[128,256]{1,0:T(8,128)(2,1)S(1)} %get-tuple-element.56.refs_5_.place_ref), channel_id=1, source_target_pairs={{0,4},{1,5},{2,6},{3,7},{4,0},{5,1},{6,2},{7,3},{8,12},{9,13},{10,... | collective-permute-start | bytes 196616 | tf_op jit(solution)/shard_map/ppermute | solution.py:328
  43.0 6.2 %collective-permute-start.4 = (bf16[256,512]{1,0:T(8,128)(2,1)S(1)}, bf16[256,512]{1,0:T(8,128)(2,1)S(1)}, u32[]{:S(2)}, u32[]{:S(2)}) collective-permute-start(bf16[256,512]{1,0:T(8,128)(2,1)S(1)} %shard_map.102.refs_1_), channel_id=1, source_target_pairs={{0,8},{1,9},{2,10},{3,11},{4,12},{5,13},{6,14},{7,15},{8,0},{9,1},... | collective-permute-start | bytes 786440 | tf_op jit(solution)/shard_map/ppermute | solution.py:328
  43.0 6.2 %collective-permute-start.8 = (bf16[256,512]{1,0:T(8,128)(2,1)S(1)}, bf16[256,512]{1,0:T(8,128)(2,1)S(1)}, u32[]{:S(2)}, u32[]{:S(2)}) collective-permute-start(bf16[256,512]{1,0:T(8,128)(2,1)S(1)} %collective-permute-done.7.refs_3_), channel_id=1, source_target_pairs={{0,8},{1,9},{2,10},{3,11},{4,12},{5,13},{6,14},{7,15},{8,0},{9,1},... | collective-permute-start | bytes 786440 | tf_op jit(solution)/shard_map/ppermute | solution.py:328
  48.6 1.7 %collective-permute-start.10 = (bf16[256,512]{1,0:T(8,128)(2,1)S(1)}, bf16[256,512]{1,0:T(8,128)(2,1)S(1)}, u32[]{:S(2)}, u32[]{:S(2)}) collective-permute-start(bf16[256,512]{1,0:T(8,128)(2,1)S(1)} %collective-permute-done.5.refs_0_), channel_id=1, source_target_pairs={{0,8},{1,9},{2,10},{3,11},{4,12},{5,13},{6,14},{7,15},{8,0},{9,1},... | collective-permute-start | bytes 786440 | tf_op jit(solution)/shard_map/ppermute | solution.py:328
  49.2 1.5 %collective-permute-start.12 = (bf16[256,512]{1,0:T(8,128)(2,1)S(1)}, bf16[256,512]{1,0:T(8,128)(2,1)S(1)}, u32[]{:S(2)}, u32[]{:S(2)}) collective-permute-start(bf16[256,512]{1,0:T(8,128)(2,1)S(1)} %collective-permute-done.11.refs_2_), channel_id=1, source_target_pairs={{0,8},{1,9},{2,10},{3,11},{4,12},{5,13},{6,14},{7,15},{8,0},{9,1},... | collective-permute-start | bytes 786440 | tf_op jit(solution)/shard_map/ppermute | solution.py:328
  49.2 19.0 %copy-start.8 = (f32[1024]{0:T(1024)S(1)}, f32[1024]{0:T(1024)}, u32[]{:S(2)}) copy-start(f32[1024]{0:T(1024)} %param.15) | copy-start | bytes 12292
  49.2 25.7 %slice-start = ((s8[6291456]{0:T(1024)(128)(4,1)}), s8[4194304]{0:T(1024)(128)(4,1)S(1)}, s32[]{:S(2)}) async-start(s8[6291456]{0:T(1024)(128)(4,1)} %bitcast.16), calls=%async_computation | async-start | bytes 8388608
  50.3 24.6 %slice-start.1 = ((s8[6291456]{0:T(1024)(128)(4,1)}), s8[2097152]{0:T(1024)(128)(4,1)S(1)}, s32[]{:S(2)}) async-start(s8[6291456]{0:T(1024)(128)(4,1)} %bitcast.16), calls=%async_computation.1 | async-start | bytes 4194304
  51.8 45.7 %copy-start = (bf16[1,1536,1024]{2,1,0:T(8,128)(2,1)S(1)}, bf16[1,1536,1024]{2,1,0:T(8,128)(2,1)}, u32[]{:S(2)}) copy-start(bf16[1,1536,1024]{2,1,0:T(8,128)(2,1)} %param.19) | copy-start | bytes 9437188
  53.2 14.9 %collective-permute-start.14 = (bf16[128,1024]{1,0:T(8,128)(2,1)S(1)}, bf16[128,1024]{1,0:T(8,128)(2,1)S(1)}, u32[]{:S(2)}, u32[]{:S(2)}) collective-permute-start(bf16[128,1024]{1,0:T(8,128)(2,1)S(1)} %get-tuple-element.67), channel_id=1, source_target_pairs={{0,4},{1,5},{2,6},{3,7},{4,0},{5,1},{6,2},{7,3},{8,12},{9,13},{10,... | collective-permute-start | bytes 786440 | tf_op jit(solution)/shard_map/ppermute | solution.py:328
  68.2 5.0 %collective-permute-start.16 = (bf16[32,1024]{1,0:T(8,128)(2,1)S(1)}, bf16[32,1024]{1,0:T(8,128)(2,1)S(1)}, u32[]{:S(2)}, u32[]{:S(2)}) collective-permute-start(bf16[32,1024]{1,0:T(8,128)(2,1)S(1)} %get-tuple-element.72), channel_id=1, source_target_pairs={{0,1},{1,0},{2,3},{3,2},{4,5},{5,4},{6,7},{7,6},{8,9},{9,8},{10,11... | collective-permute-start | bytes 196616 | tf_op jit(solution)/shard_map/ppermute | solution.py:328
  69.0 4.3 %collective-permute-start.17 = (bf16[32,1024]{1,0:T(8,128)(2,1)S(1)}, bf16[32,1024]{1,0:T(8,128)(2,1)S(1)}, u32[]{:S(2)}, u32[]{:S(2)}) collective-permute-start(bf16[32,1024]{1,0:T(8,128)(2,1)S(1)} %get-tuple-element.73), channel_id=1, source_target_pairs={{0,2},{1,3},{2,0},{3,1},{4,6},{5,7},{6,4},{7,5},{8,10},{9,11},{10,... | collective-permute-start | bytes 196616 | tf_op jit(solution)/shard_map/ppermute | solution.py:328
  69.0 5.9 %collective-permute-start.18 = (bf16[32,1024]{1,0:T(8,128)(2,1)S(1)}, bf16[32,1024]{1,0:T(8,128)(2,1)S(1)}, u32[]{:S(2)}, u32[]{:S(2)}) collective-permute-start(bf16[32,1024]{1,0:T(8,128)(2,1)S(1)} %get-tuple-element.74), channel_id=1, source_target_pairs={{0,3},{1,2},{2,1},{3,0},{4,7},{5,6},{6,5},{7,4},{8,11},{9,10},{10,... | collective-permute-start | bytes 196616 | tf_op jit(solution)/shard_map/ppermute | solution.py:328
  71.8 24.4 %collective-permute-start.15 = (bf16[256,1024]{1,0:T(8,128)(2,1)S(1)}, bf16[256,1024]{1,0:T(8,128)(2,1)S(1)}, u32[]{:S(2)}, u32[]{:S(2)}) collective-permute-start(bf16[256,1024]{1,0:T(8,128)(2,1)S(1)} %get-tuple-element.68), channel_id=1, source_target_pairs={{0,4},{1,5},{2,6},{3,7},{4,0},{5,1},{6,2},{7,3},{8,12},{9,13},{10,... | collective-permute-start | bytes 1572872 | tf_op jit(solution)/shard_map/ppermute | solution.py:328
  76.1 1.5 %collective-permute-start.19 = (bf16[32,3200]{1,0:T(8,128)(2,1)S(1)}, bf16[32,3200]{1,0:T(8,128)(2,1)S(1)}, u32[]{:S(2)}, u32[]{:S(2)}) collective-permute-start(bf16[32,3200]{1,0:T(8,128)(2,1)S(1)} %get-tuple-element.76), channel_id=1, source_target_pairs={{0,8},{1,9},{2,10},{3,11},{4,12},{5,13},{6,14},{7,15},{8,0},{9,1},... | collective-permute-start | bytes 614408 | tf_op jit(solution)/shard_map/ppermute | solution.py:328
  76.2 1.7 %collective-permute-start.20 = (bf16[32,3200]{1,0:T(8,128)(2,1)S(1)}, bf16[32,3200]{1,0:T(8,128)(2,1)S(1)}, u32[]{:S(2)}, u32[]{:S(2)}) collective-permute-start(bf16[32,3200]{1,0:T(8,128)(2,1)S(1)} %get-tuple-element.77), channel_id=1, source_target_pairs={{0,8},{1,9},{2,10},{3,11},{4,12},{5,13},{6,14},{7,15},{8,0},{9,1},... | collective-permute-start | bytes 614408 | tf_op jit(solution)/shard_map/ppermute | solution.py:328
  78.0 7.3 %collective-permute-start.21 = (bf16[32,3200]{1,0:T(8,128)(2,1)S(1)}, bf16[32,3200]{1,0:T(8,128)(2,1)S(1)}, u32[]{:S(2)}, u32[]{:S(2)}) collective-permute-start(bf16[32,3200]{1,0:T(8,128)(2,1)S(1)} %get-tuple-element.79), channel_id=1, source_target_pairs={{0,16},{1,17},{2,18},{3,19},{4,20},{5,21},{6,22},{7,23},{8,24},{9,... | collective-permute-start | bytes 614408 | tf_op jit(solution)/shard_map/ppermute | solution.py:328
  85.4 10.8 %collective-permute-start.23 = (bf16[32,1536]{1,0:T(8,128)(2,1)S(1)}, bf16[32,1536]{1,0:T(8,128)(2,1)S(1)}, u32[]{:S(2)}, u32[]{:S(2)}) collective-permute-start(bf16[32,1536]{1,0:T(8,128)(2,1)S(1)} %shard_map.110.refs_0_), channel_id=1, source_target_pairs={{0,16},{1,17},{2,18},{3,19},{4,20},{5,21},{6,22},{7,23},{8,24},{9,... | collective-permute-start | bytes 294920 | tf_op jit(solution)/shard_map/ppermute | solution.py:328
  87.1 9.1 %collective-permute-start.22 = (bf16[32,1536]{1,0:T(8,128)(2,1)S(1)}, bf16[32,1536]{1,0:T(8,128)(2,1)S(1)}, u32[]{:S(2)}, u32[]{:S(2)}) collective-permute-start(bf16[32,1536]{1,0:T(8,128)(2,1)S(1)} %shard_map.110.refs_0_), channel_id=1, source_target_pairs={{0,8},{1,9},{2,10},{3,11},{4,12},{5,13},{6,14},{7,15},{8,0},{9,1},... | collective-permute-start | bytes 294920 | tf_op jit(solution)/shard_map/ppermute | solution.py:328
  96.2 1.3 %collective-permute-start.24 = (bf16[32,1536]{1,0:T(8,128)(2,1)S(1)}, bf16[32,1536]{1,0:T(8,128)(2,1)S(1)}, u32[]{:S(2)}, u32[]{:S(2)}) collective-permute-start(bf16[32,1536]{1,0:T(8,128)(2,1)S(1)} %collective-permute-done.23.refs_2_), channel_id=1, source_target_pairs={{0,8},{1,9},{2,10},{3,11},{4,12},{5,13},{6,14},{7,15},{8,0},{9,1},... | collective-permute-start | bytes 294920 | tf_op jit(solution)/shard_map/ppermute | solution.py:328
  98.2 4.3 %collective-permute-start.25 = (bf16[32,1024]{1,0:T(8,128)(2,1)S(1)}, bf16[32,1024]{1,0:T(8,128)(2,1)S(1)}, u32[]{:S(2)}, u32[]{:S(2)}) collective-permute-start(bf16[32,1024]{1,0:T(8,128)(2,1)S(1)} %get-tuple-element.82), channel_id=1, source_target_pairs={{0,1},{1,0},{2,3},{3,2},{4,5},{5,4},{6,7},{7,6},{8,9},{9,8},{10,11... | collective-permute-start | bytes 196616 | tf_op jit(solution)/shard_map/ppermute | solution.py:328
  98.9 4.6 %collective-permute-start.26 = (bf16[32,1024]{1,0:T(8,128)(2,1)S(1)}, bf16[32,1024]{1,0:T(8,128)(2,1)S(1)}, u32[]{:S(2)}, u32[]{:S(2)}) collective-permute-start(bf16[32,1024]{1,0:T(8,128)(2,1)S(1)} %get-tuple-element.83), channel_id=1, source_target_pairs={{0,2},{1,3},{2,0},{3,1},{4,6},{5,7},{6,4},{7,5},{8,10},{9,11},{10,... | collective-permute-start | bytes 196616 | tf_op jit(solution)/shard_map/ppermute | solution.py:328
  98.9 6.0 %collective-permute-start.27 = (bf16[32,1024]{1,0:T(8,128)(2,1)S(1)}, bf16[32,1024]{1,0:T(8,128)(2,1)S(1)}, u32[]{:S(2)}, u32[]{:S(2)}) collective-permute-start(bf16[32,1024]{1,0:T(8,128)(2,1)S(1)} %get-tuple-element.84), channel_id=1, source_target_pairs={{0,3},{1,2},{2,1},{3,0},{4,7},{5,6},{6,5},{7,4},{8,11},{9,10},{10,... | collective-permute-start | bytes 196616 | tf_op jit(solution)/shard_map/ppermute | solution.py:328
  105.0 7.9 %collective-permute-start.28 = (bf16[64,1024]{1,0:T(8,128)(2,1)S(1)}, bf16[64,1024]{1,0:T(8,128)(2,1)S(1)}, u32[]{:S(2)}, u32[]{:S(2)}) collective-permute-start(bf16[64,1024]{1,0:T(8,128)(2,1)S(1)} %shard_map.112), channel_id=1, source_target_pairs={{0,4},{1,5},{2,6},{3,7},{4,0},{5,1},{6,2},{7,3},{8,12},{9,13},{10,... | collective-permute-start | bytes 393224 | tf_op jit(solution)/shard_map/ppermute | solution.py:328

commit v10 on v9

--- a/solution.py
+++ b/solution.py
@@ -164,23 +164,36 @@
         stacked[jnp.bitwise_xor(turn, s)] = atts[s][...]
     last[...] = stacked[C - 1]
     half = acc.shape[1] // 2
+    acc[...] = res[...].astype(F32) if with_residual else jnp.zeros_like(acc)
     for j in range(2):
         at = slice(j * half, (j + 1) * half)
-        total = res[:, at].astype(F32) if with_residual else None
+        total = None
+        i = 0
         for d in range(C - 1):
-            term = dot(stacked[d], ws[d][:, at])
+            if d % 2 and d > 1:
+                i += 2
+                continue
+            term = dot(stacked[d], ws[i][:, at])
             total = term if total is None else total + term
-        acc[:, at] = total
+            i += 1
+        acc[:, at] += total
+    i = 0
+    for d in range(C - 1):
+        if d % 2 and d > 1:
+            cut = ws[i].shape[1]
+            acc[:, :cut] += dot(stacked[d], ws[i][...])
+            acc[:, cut:] += dot(stacked[d], ws[i + 1][...])
+            i += 1
+        i += 1
 
 
 def last_kernel(E, cap, *refs):
-    accs, lasts, w_ref, places = refs[:2], refs[2:4], refs[4], refs[5:7]
-    own_ref, full_ref, keep_ref, send_ref = refs[7:]
-    half = w_ref.shape[1] // 2
-    for j in range(2):
-        cols = slice(j * half, (j + 1) * half)
+    accs, lasts, ws, places = refs[:2], refs[2:4], refs[4:6], refs[6:8]
+    own_ref, full_ref, keep_ref, send_ref = refs[8:]
+    cut = ws[0].shape[1]
+    for j, cols in enumerate((slice(0, cut), slice(cut, own_ref.shape[1]))):
         for t in (1, 0):
-            total = accs[t][:, cols] + dot(lasts[t][...], w_ref[:, cols])
+            total = accs[t][:, cols] + dot(lasts[t][...], ws[j][...])
             rounded = total.astype(BF16)
             if t == 0:
                 own_ref[:, cols] = total
@@ -220,46 +233,62 @@
     for j in range(wide // step):
         at = slice(j * step, (j + 1) * step)
         part_s[:, at] = dot(x_s[...], w_ref[:, at])
-    for i, r in enumerate(order):
-        at = aligned(jnp.bitwise_xor(c, r) * own_rows, own_rows)
-        block = part_s[pl.ds(at, own_rows), :]
-        if i < C // 2:
-            keep_ref[i * own_rows : (i + 1) * own_rows, :] = block
+    piece = min(own_rows, sends[0].shape[0])
+    for k in range(C * own_rows // piece):
+        i, rest = divmod(k * piece, own_rows)
+        at = aligned(jnp.bitwise_xor(c, order[i]) * own_rows + rest, piece)
+        block = part_s[pl.ds(at, piece), :]
+        first = k * piece - C // 2 * own_rows
+        if first < 0:
+            keep_ref[k * piece : (k + 1) * piece, :] = block
         else:
-            first = (i - C // 2) * own_rows
             send_ref = sends[first // sends[0].shape[0]]
             to = first % sends[0].shape[0]
-            send_ref[to : to + own_rows, :wide] = block[:, :wide].astype(BF16)
+            send_ref[to : to + piece, :wide] = block[:, :wide].astype(BF16)
             square = block[:, wide:]
             high = square.astype(BF16).astype(F32)
             lane = lax.broadcasted_iota(jnp.int32, square.shape, 1)
             low = pltpu.roll(square - high, 1, 1)
             pair = jnp.where(lane == 1, low, high)
-            send_ref[to : to + own_rows, wide:] = pair.astype(BF16)
-
-
-def halve_kernel(keep_in, got0, got1, keep_ref, send_ref):
+            send_ref[to : to + piece, wide:] = pair.astype(BF16)
+
+
+def halve_kernel(pieces, keep_in, *refs):
+    gots, keep_ref, sends = refs[:pieces], refs[pieces], refs[pieces + 1 :]
     rows = keep_ref.shape[0]
     wide = keep_ref.shape[1] - 128
-    keep_ref[...] = keep_in[:rows, :] + got0[...].astype(F32)
-    total = keep_in[rows:, :] + got1[...].astype(F32)
-    send_ref[:, :wide] = total[:, :wide].astype(BF16)
-    square = jnp.sum(total[:, wide:], axis=1, keepdims=True)
-    high = square.astype(BF16).astype(F32)
-    lane = lax.broadcasted_iota(jnp.int32, (rows, 128), 1)
-    pair = jnp.where(lane == 0, high, jnp.where(lane == 1, square - high, 0.0))
-    send_ref[:, wide:] = pair.astype(BF16)
-
-
-def activate_kernel(hidden, keep_ref, got_ref, out):
-    def summed(at):
-        return keep_ref[:, at] + got_ref[:, at].astype(F32)
-
-    square = jnp.sum(summed(slice(2 * hidden, 2 * hidden + 128)), axis=1, keepdims=True)
-    scale = lax.rsqrt(square / D + 1e-6)
-    gate = summed(slice(0, hidden)) * scale
-    up = summed(slice(hidden, 2 * hidden)) * scale
-    out[...] = (gate / (1.0 + jnp.exp(-gate)) * up).astype(BF16)
+    count = gots[0].shape[0]
+    step = min(count, sends[0].shape[0])
+    for at in range(0, 2 * rows, step):
+        got = gots[at // count][at % count : at % count + step, :]
+        total = keep_in[at : at + step, :] + got.astype(F32)
+        if at < rows:
+            keep_ref[at : at + step, :] = total
+            continue
+        send_ref = sends[(at - rows) // sends[0].shape[0]]
+        to = (at - rows) % sends[0].shape[0]
+        send_ref[to : to + step, :wide] = total[:, :wide].astype(BF16)
+        square = jnp.sum(total[:, wide:], axis=1, keepdims=True)
+        high = square.astype(BF16).astype(F32)
+        lane = lax.broadcasted_iota(jnp.int32, (step, 128), 1)
+        pair = jnp.where(lane == 0, high, jnp.where(lane == 1, square - high, 0.0))
+        send_ref[to : to + step, wide:] = pair.astype(BF16)
+
+
+def activate_kernel(hidden, keep_ref, *refs):
+    gots, out = refs[:-1], refs[-1]
+    count = gots[0].shape[0]
+    for i, got in enumerate(gots):
+        rows = slice(i * count, (i + 1) * count)
+
+        def summed(at):
+            return keep_ref[rows, at] + got[:, at].astype(F32)
+
+        square = jnp.sum(summed(slice(2 * hidden, 2 * hidden + 128)), axis=1, keepdims=True)
+        scale = lax.rsqrt(square / D + 1e-6)
+        gate = summed(slice(0, hidden)) * scale
+        up = summed(slice(hidden, 2 * hidden)) * scale
+        out[rows, :] = (gate / (1.0 + jnp.exp(-gate)) * up).astype(BF16)
 
 
 def down_kernel(C, E, cap, *refs):
@@ -282,21 +311,24 @@
         refs[-1][d * cap : (d + 1) * cap, :] = x[cap:, :]
 
 
-def combine_kernel(E, cap, own, got, place_ref, gate_ref, *refs):
+def mix_kernel(own, got, out):
+    out[...] = own[...] + got[...].astype(F32)
+
+
+def combine_kernel(E, cap, mixed, place_ref, gate_ref, *refs):
     xs, far, out, x_s = refs[: E // 2], refs[E // 2], refs[E // 2 + 1], refs[E // 2 + 2]
     for d in range(E // 2):
         at = spread(d) * cap
         x_s[at : at + cap, :] = xs[d][:cap, :]
         at = (spread(d) ^ PAIR) * cap
         x_s[at : at + cap, :] = far[d * cap : (d + 1) * cap, :]
-    half = own.shape[1] // 2
+    half = mixed.shape[1] // 2
     for j in range(2):
         cols = slice(j * half, (j + 1) * half)
         collected = lax.dot_general(
             place_ref[...], x_s[:, cols], (((0,), (0,)), ((), ())), preferred_element_type=F32
         )
-        mixed = own[:, cols] + got[:, cols].astype(F32)
-        out[:, cols] = (mixed + gate_ref[:, :1] * collected).astype(BF16)
+        out[:, cols] = (mixed[:, cols] + gate_ref[:, :1] * collected).astype(BF16)
 
 
 def body(
@@ -363,9 +395,14 @@
 
     other, own_msg = attend(1, got)
     theirs = permute(other, exp=PAIR)
+    (mine,) = attend(0, [own_msg, after(got[1], other)] + got[2:])
+    cut = width - max(width // 4, 128)
+    near = after(shards[1], other)[:, cut:]
     for d in range(2, C, 2):
-        shards[d + 1] = permute(after(shards[d], other), exp=1)
-    (mine,) = attend(0, [own_msg, after(got[1], other, *step)] + got[2:])
+        shards[d + 1] = (
+            permute(after(shards[d], other)[:, :cut], exp=1),
+            permute(near, exp=spread(d)),
+        )
     tokens_last = lambda x: jnp.transpose(x.reshape(C, tok, x.shape[3]), (0, 2, 1))
     place, gate, *staged = call(
         functools.partial(route_kernel, E, cap),
@@ -375,7 +412,7 @@
         scratch=[pltpu.VMEM((8, rows), jnp.int32), pltpu.VMEM((128, rows), F32)],
         cost=(0, 2**14),
         limit=16,
-    )(tokens_last(after(routes, mine)), tokens_last(after(gates, mine)), out_weight, res)
+    )(tokens_last(after(routes, mine, *step)), tokens_last(after(gates, mine)), out_weight, res)
     shards[0], res = staged
 
     def gather(x, before):
@@ -387,11 +424,11 @@
 
     other_place = permute(after(place, theirs), exp=PAIR)
     mine_all = gather(mine, [])
-    theirs_all = gather(after(theirs, place, shards[1], *mine_all[2::2]), [])
+    theirs_all = gather(after(theirs, place, *mine_all[2::2], *[shards[d][1] for d in range(3, C, 2)]), [])
     mine_all[1] = after(mine_all[1], other_place)
 
     def project(atts, *extra):
-        operands = [*extra, *atts, *[shards[d] for d in range(C - 1)]]
+        operands = [*extra, *atts, shards[0], shards[1], *[w for d in range(2, C - 1) for w in (shards[d] if d % 2 else [shards[d]])]]
         return call(
             functools.partial(project_kernel, C, bool(extra)),
             [sds((rows, width), F32), sds((rows, qw), BF16)],
@@ -413,9 +450,9 @@
             sds((slots, width), F32),
             sds((slots, width), BF16),
         ],
-        7,
-        cost=(4 * rows * (qw + slots) * width, 2**20),
-    )(acc, acc_far, last, last_far, shards[C - 1], place, other_place)
+        8,
+        cost=(0, 2**14),
+    )(acc, acc_far, last, last_far, *shards[C - 1], place, other_place)
     received = permute(send, exp=PAIR)
     outgoing = call(
         outgoing_kernel, [sds((2 * cap, width), BF16)] * (E // 2), 3, cost=(0, 2**20)
@@ -436,25 +473,24 @@
         [sds((slots // 2, wide + 128), F32)] + [sds((slots // 4, wide + 128), BF16)] * 2,
         E // 2 + 2,
         scratch=[pltpu.VMEM((slots, width), BF16), pltpu.VMEM((slots, wide + 128), F32)],
-        cost=(2 * slots * width * wide, 2 * width * wide),
+        cost=(0, 2**10),
     )(*incoming, gain, w_gate_up.reshape(width, wide))
     bit = 1
     while 2 * bit < C:
         count = keep.shape[0] // 2
-        keep, send = call(
-            halve_kernel,
-            [sds((count, wide + 128), F32), sds((count, wide + 128), BF16)],
-            3,
+        keep, *sends = call(
+            functools.partial(halve_kernel, len(sends)),
+            [sds((count, wide + 128), F32)] + [sds((count // 2, wide + 128), BF16)] * 2,
+            1 + len(sends),
             cost=(0, 2**10),
         )(keep, *[permute(x, ctx=bit) for x in sends])
-        sends = [send[: count // 2], send[count // 2 :]]
         bit *= 2
     activated = call(
         functools.partial(activate_kernel, hidden),
         sds((own_rows, hidden), BF16),
-        2,
+        1 + len(sends),
         cost=(0, 2**10),
-    )(keep, permute(send, ctx=bit))
+    )(keep, *[permute(x, ctx=bit) for x in sends])
     acts = {0: activated}
     acts[bit] = after(permute(activated, ctx=bit), arrived)
     bit //= 2
@@ -474,13 +510,14 @@
     far = call(
         functools.partial(forward_kernel, cap), sds((slots // 2, width), BF16), E // 2, cost=(0, 2**19)
     )(*returned)
+    mixed = call(mix_kernel, sds((rows, width), F32), 2, cost=(0, 2**14))(own, arrived)
     result = call(
         functools.partial(combine_kernel, E, cap),
         sds((rows, width), BF16),
-        5 + E // 2,
+        4 + E // 2,
         scratch=[pltpu.VMEM((slots, width), BF16)],
         cost=(0, 2 * 2**20),
-    )(own, arrived, place, gate, *returned, permute(far, exp=PAIR))
+    )(mixed, place, gate, *returned, permute(far, exp=PAIR))
     return result.reshape(C, 1, tok, width)
 
 

time: 114 us -> 124 us (1.088)
  waiting for transfers between devices: 66.8 us -> 79 us
  starting transfers between devices: 28.3 us -> 25 us
    ppermute x29 -> x31, waiting for transfers between devices: 66.8 us -> 79 us  [permute(): return lax.ppermute(x, ('ctx', 'exp'), pairs)]
    ppermute x29 -> x31, starting transfers between devices: 28.3 us -> 25 us  [permute(): return lax.ppermute(x, ('ctx', 'exp'), pairs)]
  transfers between devices with their start and end apart: 29 -> 31, of which waited for: 19 -> 20; matrix products, arithmetic and copies ran while one was open for 0% -> 0% of each run, Pallas kernels for 8% -> 7%
where the time goes in v10:
time: 124 us; the launch traced here: 123 us
  waiting for transfers between devices  79 us (64%)
  starting transfers between devices  25 us (20%)
  Pallas kernels  12.5 us (10%)
  local copies, waits for them, and re-layouts  6.54 us (5%)
    ppermute x31, waiting for transfers between devices, permute(): return lax.ppermute(x, ('ctx', 'exp'), pairs)  79 us
    ppermute x31, starting transfers between devices, permute(): return lax.ppermute(x, ('ctx', 'exp'), pairs)  25 us
    unnamed x22, local copies, waits for them, and re-layouts  6.44 us
    pallas_call x2, Pallas kernels, attend(): call(functools.partial(attend_kernel, C, t), [sds((rows, qw), BF16)] + [s...  4.67 us
  transfers between devices with their start and end apart: 31, of which 20 were waited for; matrix products, arithmetic and copies ran while one was open for 0% of the time, Pallas kernels for 7%

profile of v10, /device:TPU:0, one launch (start us, length us, event | category | flops | bytes accessed | tf_op | source)
XLA Modules:
  0.0 123.3 jit_solution(2389202399806271831)
XLA Ops:
  0.0 2.9 %collective-permute-start.9 = (bf16[512,1024]{1,0:T(8,128)(2,1)}, bf16[512,1024]{1,0:T(8,128)(2,1)S(1)}, u32[]{:S(2)}, u32[]{:S(2)}) collective-permute-start(bf16[512,1024]{1,0:T(8,128)(2,1)} %refs_0_.1), channel_id=1, source_target_pairs={{0,1},{1,0},{2,3},{3,2},{4,5},{5,4},{6,7},{7,6},{8,9},{9,8},{10,11... | collective-permute-start | bytes 3145736 | tf_op jit(solution)/shard_map/ppermute | solution.py:360
  2.9 1.6 %collective-permute-start.3 = (bf16[512,1024]{1,0:T(8,128)(2,1)}, bf16[512,1024]{1,0:T(8,128)(2,1)S(1)}, u32[]{:S(2)}, u32[]{:S(2)}) collective-permute-start(bf16[512,1024]{1,0:T(8,128)(2,1)} %refs_0_.1), channel_id=1, source_target_pairs={{0,2},{1,3},{2,0},{3,1},{4,6},{5,7},{6,4},{7,5},{8,10},{9,11},{10,... | collective-permute-start | bytes 3145736 | tf_op jit(solution)/shard_map/ppermute | solution.py:360
  4.5 1.0 copy-done.3
  5.6 0.8 copy-done.4
  6.4 0.8 copy-done.5
  7.7 1.6 %collective-permute-start.1 = (bf16[64,2048]{1,0:T(8,128)(2,1)S(1)}, bf16[64,2048]{1,0:T(8,128)(2,1)S(1)}, u32[]{:S(2)}, u32[]{:S(2)}) collective-permute-start(bf16[64,2048]{1,0:T(8,128)(2,1)S(1)} %get-tuple-element.49), channel_id=1, source_target_pairs={{0,16},{1,17},{2,18},{3,19},{4,20},{5,21},{6,22},{7,23},{8,24},{9,... | collective-permute-start | bytes 786440 | tf_op jit(solution)/shard_map/ppermute | solution.py:360
  9.6 7.3 %collective-permute-done.1.refs_2_ = bf16[64,2048]{1,0:T(8,128)(2,1)S(1)} collective-permute-done((bf16[64,2048]{1,0:T(8,128)(2,1)S(1)}, bf16[64,2048]{1,0:T(8,128)(2,1)S(1)}, u32[]{:S(2)}, u32[]{:S(2)}) %collective-permute-start.1) | collective-permute-done | bytes 262176 | tf_op jit(solution)/shard_map/ppermute | solution.py:360
  16.9 4.7 %collective-permute-done.2.refs_3_ = bf16[64,2048]{1,0:T(8,128)(2,1)S(1)} collective-permute-done((bf16[64,2048]{1,0:T(8,128)(2,1)S(1)}, bf16[64,2048]{1,0:T(8,128)(2,1)S(1)}, u32[]{:S(2)}, u32[]{:S(2)}) %collective-permute-start.2) | collective-permute-done | bytes 262176 | tf_op jit(solution)/shard_map/ppermute | solution.py:360
  21.6 2.3 %shard_map.101 = (bf16[256,512]{1,0:T(8,128)(2,1)S(1)}, bf16[64,2048]{1,0:T(8,128)(2,1)S(1)}) custom-call(bf16[64,2048]{1,0:T(8,128)(2,1)S(1)} %get-tuple-element.47.refs_0_, bf16[64,2048]{1,0:T(8,128)(2,1)S(1)} %collective-permute-done.refs_1_, bf16[64,2048]{1,0:T(8,128)(2,1)S(1)} %collective-permute-done.1.refs_2_, ...), custom_call_target="tpu_custom_call" | custom-call | bytes 16384 | tf_op jit(solution)/shard_map/pallas_call | solution.py:387
  23.9 2.7 %collective-permute-start.5 = (bf16[256,512]{1,0:T(8,128)(2,1)S(1)}, bf16[256,512]{1,0:T(8,128)(2,1)S(1)}, u32[]{:S(2)}, u32[]{:S(2)}) collective-permute-start(bf16[256,512]{1,0:T(8,128)(2,1)S(1)} %get-tuple-element.52), channel_id=1, source_target_pairs={{0,4},{1,5},{2,6},{3,7},{4,0},{5,1},{6,2},{7,3},{8,12},{9,13},{10,... | collective-permute-start | bytes 786440 | tf_op jit(solution)/shard_map/ppermute | solution.py:360
  26.6 2.3 %shard_map.102.refs_1_ = bf16[256,512]{1,0:T(8,128)(2,1)S(1)} custom-call(bf16[64,2048]{1,0:T(8,128)(2,1)S(1)} %get-tuple-element.51.refs_0_, bf16[64,2048]{1,0:T(8,128)(2,1)S(1)} %collective-permute-done.refs_1_, bf16[64,2048]{1,0:T(8,128)(2,1)S(1)} %collective-permute-done.1.refs_2_, bf16[64,2048]{1,0:T(8,128)(2,1)S(1)} %collective-permute-done.2.refs_3_), custom_call_target="tpu_custom_call" | custom-call | bytes 16384 | tf_op jit(solution)/shard_map/pallas_call | solution.py:387
  28.9 1.6 %collective-permute-start.7 = (bf16[256,512]{1,0:T(8,128)(2,1)S(1)}, bf16[256,512]{1,0:T(8,128)(2,1)S(1)}, u32[]{:S(2)}, u32[]{:S(2)}) collective-permute-start(bf16[256,512]{1,0:T(8,128)(2,1)S(1)} %shard_map.102.refs_1_), channel_id=1, source_target_pairs={{0,16},{1,17},{2,18},{3,19},{4,20},{5,21},{6,22},{7,23},{8,24},{9,... | collective-permute-start | bytes 786440 | tf_op jit(solution)/shard_map/ppermute | solution.py:360
  30.5 0.5 collective-permute-start.10
  31.1 0.6 collective-permute-start.14
  31.7 1.2 copy-done.1
  33.0 1.0 copy-done.2
  34.0 0.7 copy-done.6
  34.7 0.7 copy-done.7
  35.7 3.7 %collective-permute-done.5.refs_0_ = bf16[256,512]{1,0:T(8,128)(2,1)S(1)} collective-permute-done((bf16[256,512]{1,0:T(8,128)(2,1)S(1)}, bf16[256,512]{1,0:T(8,128)(2,1)S(1)}, u32[]{:S(2)}, u32[]{:S(2)}) %collective-permute-start.5) | collective-permute-done | bytes 262176 | tf_op jit(solution)/shard_map/ppermute | solution.py:360
  39.4 3.2 %collective-permute-done.10.refs_5_ = bf16[512,256]{1,0:T(8,128)(2,1)S(1)} collective-permute-done((bf16[512,256]{1,0:T(8,128)(2,1)S(1)}, bf16[512,256]{1,0:T(8,128)(2,1)S(1)}, u32[]{:S(2)}, u32[]{:S(2)}) %collective-permute-start.10) | collective-permute-done | bytes 262176 | tf_op jit(solution)/shard_map/ppermute | solution.py:360
  42.6 0.5 collective-permute-start.12
  43.1 0.5 collective-permute-start.8
  43.6 6.4 %collective-permute-done.12.refs_2_ = bf16[256,512]{1,0:T(8,128)(2,1)S(1)} collective-permute-done((bf16[256,512]{1,0:T(8,128)(2,1)S(1)}, bf16[256,512]{1,0:T(8,128)(2,1)S(1)}, u32[]{:S(2)}, u32[]{:S(2)}) %collective-permute-start.12) | collective-permute-done | bytes 262176 | tf_op jit(solution)/shard_map/ppermute | solution.py:360
  50.0 5.8 %collective-permute-done.6.refs_7_ = bf16[128,256]{1,0:T(8,128)(2,1)S(1)} collective-permute-done((bf16[128,256]{1,0:T(8,128)(2,1)S(1)}, bf16[128,256]{1,0:T(8,128)(2,1)S(1)}, u32[]{:S(2)}, u32[]{:S(2)}) %collective-permute-start.6) | collective-permute-done | bytes 65568 | tf_op jit(solution)/shard_map/ppermute | solution.py:360
  55.8 1.1 shard_map.104
  56.9 1.1 shard_map.105
  58.0 1.6 %shard_map.106 = (f32[256,1024]{1,0:T(8,128)S(1)}, bf16[256,1024]{1,0:T(8,128)(2,1)S(1)}, f32[128,1024]{1,0:T(8,128)S(1)}, bf16[128,1024]{1,0:T(8,128)(2,1)S(1)}) custom-call(f32[256,1024]{1,0:T(8,128)S(1)} %get-tuple-element.61.refs_0_, f32[256,1024]{1,0:T(8,128)S(1)} %get-tuple-element.64.refs_1_, bf16[256,512]{1,0:T(8,128)(2,1)S(1)} %get-tuple-element.65.refs_2_, ...), custom_call_target="tpu_custom_call" | custom-call | bytes 16384 | tf_op jit(solution)/shard_map/pallas_call | solution.py:445
  59.7 13.9 %collective-permute-done.15.got_ref = bf16[128,1024]{1,0:T(8,128)(2,1)S(1)} collective-permute-done((bf16[128,1024]{1,0:T(8,128)(2,1)S(1)}, bf16[128,1024]{1,0:T(8,128)(2,1)S(1)}, u32[]{:S(2)}, u32[]{:S(2)}) %collective-permute-start.15) | collective-permute-done | bytes 262176 | tf_op jit(solution)/shard_map/ppermute | solution.py:360
  73.8 3.1 %collective-permute-start.18 = (bf16[32,1024]{1,0:T(8,128)(2,1)S(1)}, bf16[32,1024]{1,0:T(8,128)(2,1)S(1)}, u32[]{:S(2)}, u32[]{:S(2)}) collective-permute-start(bf16[32,1024]{1,0:T(8,128)(2,1)S(1)} %get-tuple-element.76), channel_id=1, source_target_pairs={{0,2},{1,3},{2,0},{3,1},{4,6},{5,7},{6,4},{7,5},{8,10},{9,11},{10,... | collective-permute-start | bytes 196616 | tf_op jit(solution)/shard_map/ppermute | solution.py:360
  76.9 0.9 collective-permute-start.19
  78.0 9.3 %collective-permute-done.18.refs_2_ = bf16[32,1024]{1,0:T(8,128)(2,1)S(1)} collective-permute-done((bf16[32,1024]{1,0:T(8,128)(2,1)S(1)}, bf16[32,1024]{1,0:T(8,128)(2,1)S(1)}, u32[]{:S(2)}, u32[]{:S(2)}) %collective-permute-start.18) | collective-permute-done | bytes 65568 | tf_op jit(solution)/shard_map/ppermute | solution.py:360
  87.4 0.8 collective-permute-done.19.refs_3_
  88.2 1.2 %shard_map.109 = (f32[64,3200]{1,0:T(8,128)S(1)}, bf16[32,3200]{1,0:T(8,128)(2,1)S(1)}, bf16[32,3200]{1,0:T(8,128)(2,1)S(1)}) custom-call(bf16[32,1024]{1,0:T(8,128)(2,1)S(1)} %get-tuple-element.74.refs_0_, bf16[32,1024]{1,0:T(8,128)(2,1)S(1)} %collective-permute-done.17.refs_1_, bf16[32,1024]{1,0:T(8,128)(2,1)S(1)} %collective-permute-done.18.refs_2_, ...), custom_call_target="tpu_custom_call" | custom-call | bytes 1024 | tf_op jit(solution)/shard_map/pallas_call | solution.py:471
  89.4 0.5 collective-permute-start.21
  89.9 0.9 collective-permute-done.20.refs_0_
  91.7 1.6 %collective-permute-start.23 = (bf16[16,3200]{1,0:T(8,128)(2,1)S(1)}, bf16[16,3200]{1,0:T(8,128)(2,1)S(1)}, u32[]{:S(2)}, u32[]{:S(2)}) collective-permute-start(bf16[16,3200]{1,0:T(8,128)(2,1)S(1)} %get-tuple-element.83), channel_id=1, source_target_pairs={{0,16},{1,17},{2,18},{3,19},{4,20},{5,21},{6,22},{7,23},{8,24},{9,... | collective-permute-start | bytes 307208 | tf_op jit(solution)/shard_map/ppermute | solution.py:360
  93.3 3.7 %collective-permute-done.22.refs_0_ = bf16[16,3200]{1,0:T(8,128)(2,1)S(1)} collective-permute-done((bf16[16,3200]{1,0:T(8,128)(2,1)S(1)}, bf16[16,3200]{1,0:T(8,128)(2,1)S(1)}, u32[]{:S(2)}, u32[]{:S(2)}) %collective-permute-start.22) | collective-permute-done | bytes 102432 | tf_op jit(solution)/shard_map/ppermute | solution.py:360
  97.0 1.5 %collective-permute-done.23.refs_1_ = bf16[16,3200]{1,0:T(8,128)(2,1)S(1)} collective-permute-done((bf16[16,3200]{1,0:T(8,128)(2,1)S(1)}, bf16[16,3200]{1,0:T(8,128)(2,1)S(1)}, u32[]{:S(2)}, u32[]{:S(2)}) %collective-permute-start.23) | collective-permute-done | bytes 102432 | tf_op jit(solution)/shard_map/ppermute | solution.py:360
  98.7 0.5 collective-permute-start.25
  99.1 4.2 %collective-permute-done.25.refs_2_ = bf16[32,1536]{1,0:T(8,128)(2,1)S(1)} collective-permute-done((bf16[32,1536]{1,0:T(8,128)(2,1)S(1)}, bf16[32,1536]{1,0:T(8,128)(2,1)S(1)}, u32[]{:S(2)}, u32[]{:S(2)}) %collective-permute-start.25) | collective-permute-done | bytes 98336 | tf_op jit(solution)/shard_map/ppermute | solution.py:360
  103.4 1.3 %collective-permute-done.26.refs_3_ = bf16[32,1536]{1,0:T(8,128)(2,1)S(1)} collective-permute-done((bf16[32,1536]{1,0:T(8,128)(2,1)S(1)}, bf16[32,1536]{1,0:T(8,128)(2,1)S(1)}, u32[]{:S(2)}, u32[]{:S(2)}) %collective-permute-start.26) | collective-permute-done | bytes 98336 | tf_op jit(solution)/shard_map/ppermute | solution.py:360
  104.7 0.7 shard_map.112
  105.4 3.9 %collective-permute-start.28 = (bf16[32,1024]{1,0:T(8,128)(2,1)S(1)}, bf16[32,1024]{1,0:T(8,128)(2,1)S(1)}, u32[]{:S(2)}, u32[]{:S(2)}) collective-permute-start(bf16[32,1024]{1,0:T(8,128)(2,1)S(1)} %get-tuple-element.87), channel_id=1, source_target_pairs={{0,2},{1,3},{2,0},{3,1},{4,6},{5,7},{6,4},{7,5},{8,10},{9,11},{10,... | collective-permute-start | bytes 196616 | tf_op jit(solution)/shard_map/ppermute | solution.py:360
  109.7 2.3 %collective-permute-done.28.refs_2_ = bf16[32,1024]{1,0:T(8,128)(2,1)S(1)} collective-permute-done((bf16[32,1024]{1,0:T(8,128)(2,1)S(1)}, bf16[32,1024]{1,0:T(8,128)(2,1)S(1)}, u32[]{:S(2)}, u32[]{:S(2)}) %collective-permute-start.28) | collective-permute-done | bytes 65568 | tf_op jit(solution)/shard_map/ppermute | solution.py:360
  111.9 2.6 %collective-permute-done.29.refs_3_ = bf16[32,1024]{1,0:T(8,128)(2,1)S(1)} collective-permute-done((bf16[32,1024]{1,0:T(8,128)(2,1)S(1)}, bf16[32,1024]{1,0:T(8,128)(2,1)S(1)}, u32[]{:S(2)}, u32[]{:S(2)}) %collective-permute-start.29) | collective-permute-done | bytes 65568 | tf_op jit(solution)/shard_map/ppermute | solution.py:360
  114.5 0.9 collective-permute-start.30
  115.5 6.6 %collective-permute-done.30.refs_4_ = bf16[64,1024]{1,0:T(8,128)(2,1)S(1)} collective-permute-done((bf16[64,1024]{1,0:T(8,128)(2,1)S(1)}, bf16[64,1024]{1,0:T(8,128)(2,1)S(1)}, u32[]{:S(2)}, u32[]{:S(2)}) %collective-permute-start.30) | collective-permute-done | bytes 131104 | tf_op jit(solution)/shard_map/ppermute | solution.py:360
  122.2 1.1 shard_map.114
  (54 shorter events, 3.1 us)
Async XLA Ops:
  0.0 30.5 %collective-permute-start.9 = (bf16[512,1024]{1,0:T(8,128)(2,1)}, bf16[512,1024]{1,0:T(8,128)(2,1)S(1)}, u32[]{:S(2)}, u32[]{:S(2)}) collective-permute-start(bf16[512,1024]{1,0:T(8,128)(2,1)} %refs_0_.1), channel_id=1, source_target_pairs={{0,1},{1,0},{2,3},{3,2},{4,5},{5,4},{6,7},{7,6},{8,9},{9,8},{10,11... | collective-permute-start | bytes 3145736 | tf_op jit(solution)/shard_map/ppermute | solution.py:360
  2.9 28.1 %collective-permute-start.3 = (bf16[512,1024]{1,0:T(8,128)(2,1)}, bf16[512,1024]{1,0:T(8,128)(2,1)S(1)}, u32[]{:S(2)}, u32[]{:S(2)}) collective-permute-start(bf16[512,1024]{1,0:T(8,128)(2,1)} %refs_0_.1), channel_id=1, source_target_pairs={{0,2},{1,3},{2,0},{3,1},{4,6},{5,7},{6,4},{7,5},{8,10},{9,11},{10,... | collective-permute-start | bytes 3145736 | tf_op jit(solution)/shard_map/ppermute | solution.py:360
  4.5 1.0 copy-start.3
  5.6 0.8 copy-start.4
  6.4 0.8 copy-start.5
  7.6 1.9 %collective-permute-start = (bf16[64,2048]{1,0:T(8,128)(2,1)S(1)}, bf16[64,2048]{1,0:T(8,128)(2,1)S(1)}, u32[]{:S(2)}, u32[]{:S(2)}) collective-permute-start(bf16[64,2048]{1,0:T(8,128)(2,1)S(1)} %get-tuple-element.48), channel_id=1, source_target_pairs={{0,8},{1,9},{2,10},{3,11},{4,12},{5,13},{6,14},{7,15},{8,0},{9,1},... | collective-permute-start | bytes 786440 | tf_op jit(solution)/shard_map/ppermute | solution.py:360
  7.7 9.2 %collective-permute-start.1 = (bf16[64,2048]{1,0:T(8,128)(2,1)S(1)}, bf16[64,2048]{1,0:T(8,128)(2,1)S(1)}, u32[]{:S(2)}, u32[]{:S(2)}) collective-permute-start(bf16[64,2048]{1,0:T(8,128)(2,1)S(1)} %get-tuple-element.49), channel_id=1, source_target_pairs={{0,16},{1,17},{2,18},{3,19},{4,20},{5,21},{6,22},{7,23},{8,24},{9,... | collective-permute-start | bytes 786440 | tf_op jit(solution)/shard_map/ppermute | solution.py:360
  9.3 12.3 %collective-permute-start.2 = (bf16[64,2048]{1,0:T(8,128)(2,1)S(1)}, bf16[64,2048]{1,0:T(8,128)(2,1)S(1)}, u32[]{:S(2)}, u32[]{:S(2)}) collective-permute-start(bf16[64,2048]{1,0:T(8,128)(2,1)S(1)} %get-tuple-element.50), channel_id=1, source_target_pairs={{0,24},{1,25},{2,26},{3,27},{4,28},{5,29},{6,30},{7,31},{8,16},{9,... | collective-permute-start | bytes 786440 | tf_op jit(solution)/shard_map/ppermute | solution.py:360
  23.9 15.5 %collective-permute-start.5 = (bf16[256,512]{1,0:T(8,128)(2,1)S(1)}, bf16[256,512]{1,0:T(8,128)(2,1)S(1)}, u32[]{:S(2)}, u32[]{:S(2)}) collective-permute-start(bf16[256,512]{1,0:T(8,128)(2,1)S(1)} %get-tuple-element.52), channel_id=1, source_target_pairs={{0,4},{1,5},{2,6},{3,7},{4,0},{5,1},{6,2},{7,3},{8,12},{9,13},{10,... | collective-permute-start | bytes 786440 | tf_op jit(solution)/shard_map/ppermute | solution.py:360
  28.9 10.5 %collective-permute-start.7 = (bf16[256,512]{1,0:T(8,128)(2,1)S(1)}, bf16[256,512]{1,0:T(8,128)(2,1)S(1)}, u32[]{:S(2)}, u32[]{:S(2)}) collective-permute-start(bf16[256,512]{1,0:T(8,128)(2,1)S(1)} %shard_map.102.refs_1_), channel_id=1, source_target_pairs={{0,16},{1,17},{2,18},{3,19},{4,20},{5,21},{6,22},{7,23},{8,24},{9,... | collective-permute-start | bytes 786440 | tf_op jit(solution)/shard_map/ppermute | solution.py:360
  30.5 12.0 %collective-permute-start.10 = (bf16[512,256]{1,0:T(8,128)(2,1)S(1)}, bf16[512,256]{1,0:T(8,128)(2,1)S(1)}, u32[]{:S(2)}, u32[]{:S(2)}) collective-permute-start(bf16[512,256]{1,0:T(8,128)(2,1)S(1)} %slice.6), channel_id=1, source_target_pairs={{0,2},{1,3},{2,0},{3,1},{4,6},{5,7},{6,4},{7,5},{8,10},{9,11},{10,... | collective-permute-start | bytes 786440 | tf_op jit(solution)/shard_map/ppermute | solution.py:360
  31.1 26.8 %collective-permute-start.14 = (bf16[512,768]{1,0:T(8,128)(2,1)S(1)}, bf16[512,768]{1,0:T(8,128)(2,1)S(1)}, u32[]{:S(2)}, u32[]{:S(2)}) collective-permute-start(bf16[512,768]{1,0:T(8,128)(2,1)S(1)} %slice.7), channel_id=1, source_target_pairs={{0,1},{1,0},{2,3},{3,2},{4,5},{5,4},{6,7},{7,6},{8,9},{9,8},{10,11... | collective-permute-start | bytes 2359304 | tf_op jit(solution)/shard_map/ppermute | solution.py:360
  31.7 1.2 copy-start.1
  33.0 1.0 copy-start.2
  34.0 0.7 copy-start.6
  34.7 0.7 copy-start.7
  42.6 7.4 %collective-permute-start.12 = (bf16[256,512]{1,0:T(8,128)(2,1)S(1)}, bf16[256,512]{1,0:T(8,128)(2,1)S(1)}, u32[]{:S(2)}, u32[]{:S(2)}) collective-permute-start(bf16[256,512]{1,0:T(8,128)(2,1)S(1)} %collective-permute-done.5.refs_0_), channel_id=1, source_target_pairs={{0,16},{1,17},{2,18},{3,19},{4,20},{5,21},{6,22},{7,23},{8,24},{9,... | collective-permute-start | bytes 786440 | tf_op jit(solution)/shard_map/ppermute | solution.py:360
  43.1 6.9 %collective-permute-start.4 = (bf16[256,512]{1,0:T(8,128)(2,1)S(1)}, bf16[256,512]{1,0:T(8,128)(2,1)S(1)}, u32[]{:S(2)}, u32[]{:S(2)}) collective-permute-start(bf16[256,512]{1,0:T(8,128)(2,1)S(1)} %shard_map.102.refs_1_), channel_id=1, source_target_pairs={{0,8},{1,9},{2,10},{3,11},{4,12},{5,13},{6,14},{7,15},{8,0},{9,1},... | collective-permute-start | bytes 786440 | tf_op jit(solution)/shard_map/ppermute | solution.py:360
  43.1 12.7 %collective-permute-start.8 = (bf16[256,512]{1,0:T(8,128)(2,1)S(1)}, bf16[256,512]{1,0:T(8,128)(2,1)S(1)}, u32[]{:S(2)}, u32[]{:S(2)}) collective-permute-start(bf16[256,512]{1,0:T(8,128)(2,1)S(1)} %collective-permute-done.7.refs_3_), channel_id=1, source_target_pairs={{0,8},{1,9},{2,10},{3,11},{4,12},{5,13},{6,14},{7,15},{8,0},{9,1},... | collective-permute-start | bytes 786440 | tf_op jit(solution)/shard_map/ppermute | solution.py:360
  43.6 13.3 %collective-permute-start.11 = (bf16[256,512]{1,0:T(8,128)(2,1)S(1)}, bf16[256,512]{1,0:T(8,128)(2,1)S(1)}, u32[]{:S(2)}, u32[]{:S(2)}) collective-permute-start(bf16[256,512]{1,0:T(8,128)(2,1)S(1)} %collective-permute-done.5.refs_0_), channel_id=1, source_target_pairs={{0,8},{1,9},{2,10},{3,11},{4,12},{5,13},{6,14},{7,15},{8,0},{9,1},... | collective-permute-start | bytes 786440 | tf_op jit(solution)/shard_map/ppermute | solution.py:360
  50.0 6.9 %collective-permute-start.13 = (bf16[256,512]{1,0:T(8,128)(2,1)S(1)}, bf16[256,512]{1,0:T(8,128)(2,1)S(1)}, u32[]{:S(2)}, u32[]{:S(2)}) collective-permute-start(bf16[256,512]{1,0:T(8,128)(2,1)S(1)} %collective-permute-done.12.refs_2_), channel_id=1, source_target_pairs={{0,8},{1,9},{2,10},{3,11},{4,12},{5,13},{6,14},{7,15},{8,0},{9,1},... | collective-permute-start | bytes 786440 | tf_op jit(solution)/shard_map/ppermute | solution.py:360
  50.0 5.8 %collective-permute-start.6 = (bf16[128,256]{1,0:T(8,128)(2,1)S(1)}, bf16[128,256]{1,0:T(8,128)(2,1)S(1)}, u32[]{:S(2)}, u32[]{:S(2)}) collective-permute-start(bf16[128,256]{1,0:T(8,128)(2,1)S(1)} %get-tuple-element.58.refs_6_.place_ref), channel_id=1, source_target_pairs={{0,4},{1,5},{2,6},{3,7},{4,0},{5,1},{6,2},{7,3},{8,12},{9,13},{10,... | collective-permute-start | bytes 196616 | tf_op jit(solution)/shard_map/ppermute | solution.py:360
  55.8 17.9 %copy-start.8 = (f32[1024]{0:T(1024)S(1)}, f32[1024]{0:T(1024)}, u32[]{:S(2)}) copy-start(f32[1024]{0:T(1024)} %param.15) | copy-start | bytes 12292
  55.8 32.4 %slice-start = ((s8[6291456]{0:T(1024)(128)(4,1)}), s8[4194304]{0:T(1024)(128)(4,1)S(1)}, s32[]{:S(2)}) async-start(s8[6291456]{0:T(1024)(128)(4,1)} %bitcast.16), calls=%async_computation | async-start | bytes 8388608
  56.9 31.3 %slice-start.1 = ((s8[6291456]{0:T(1024)(128)(4,1)}), s8[2097152]{0:T(1024)(128)(4,1)S(1)}, s32[]{:S(2)}) async-start(s8[6291456]{0:T(1024)(128)(4,1)} %bitcast.16), calls=%async_computation.1 | async-start | bytes 4194304
  58.0 46.7 %copy-start = (bf16[1,1536,1024]{2,1,0:T(8,128)(2,1)S(1)}, bf16[1,1536,1024]{2,1,0:T(8,128)(2,1)}, u32[]{:S(2)}) copy-start(bf16[1,1536,1024]{2,1,0:T(8,128)(2,1)} %param.19) | copy-start | bytes 9437188
  59.6 14.0 %collective-permute-start.15 = (bf16[128,1024]{1,0:T(8,128)(2,1)S(1)}, bf16[128,1024]{1,0:T(8,128)(2,1)S(1)}, u32[]{:S(2)}, u32[]{:S(2)}) collective-permute-start(bf16[128,1024]{1,0:T(8,128)(2,1)S(1)} %get-tuple-element.70), channel_id=1, source_target_pairs={{0,4},{1,5},{2,6},{3,7},{4,0},{5,1},{6,2},{7,3},{8,12},{9,13},{10,... | collective-permute-start | bytes 786440 | tf_op jit(solution)/shard_map/ppermute | solution.py:360
  73.6 29.7 %collective-permute-start.16 = (bf16[256,1024]{1,0:T(8,128)(2,1)S(1)}, bf16[256,1024]{1,0:T(8,128)(2,1)S(1)}, u32[]{:S(2)}, u32[]{:S(2)}) collective-permute-start(bf16[256,1024]{1,0:T(8,128)(2,1)S(1)} %get-tuple-element.71), channel_id=1, source_target_pairs={{0,4},{1,5},{2,6},{3,7},{4,0},{5,1},{6,2},{7,3},{8,12},{9,13},{10,... | collective-permute-start | bytes 1572872 | tf_op jit(solution)/shard_map/ppermute | solution.py:360
  73.7 4.3 %collective-permute-start.17 = (bf16[32,1024]{1,0:T(8,128)(2,1)S(1)}, bf16[32,1024]{1,0:T(8,128)(2,1)S(1)}, u32[]{:S(2)}, u32[]{:S(2)}) collective-permute-start(bf16[32,1024]{1,0:T(8,128)(2,1)S(1)} %get-tuple-element.75), channel_id=1, source_target_pairs={{0,1},{1,0},{2,3},{3,2},{4,5},{5,4},{6,7},{7,6},{8,9},{9,8},{10,11... | collective-permute-start | bytes 196616 | tf_op jit(solution)/shard_map/ppermute | solution.py:360
  73.8 13.6 %collective-permute-start.18 = (bf16[32,1024]{1,0:T(8,128)(2,1)S(1)}, bf16[32,1024]{1,0:T(8,128)(2,1)S(1)}, u32[]{:S(2)}, u32[]{:S(2)}) collective-permute-start(bf16[32,1024]{1,0:T(8,128)(2,1)S(1)} %get-tuple-element.76), channel_id=1, source_target_pairs={{0,2},{1,3},{2,0},{3,1},{4,6},{5,7},{6,4},{7,5},{8,10},{9,11},{10,... | collective-permute-start | bytes 196616 | tf_op jit(solution)/shard_map/ppermute | solution.py:360
  76.9 11.2 %collective-permute-start.19 = (bf16[32,1024]{1,0:T(8,128)(2,1)S(1)}, bf16[32,1024]{1,0:T(8,128)(2,1)S(1)}, u32[]{:S(2)}, u32[]{:S(2)}) collective-permute-start(bf16[32,1024]{1,0:T(8,128)(2,1)S(1)} %get-tuple-element.77), channel_id=1, source_target_pairs={{0,3},{1,2},{2,1},{3,0},{4,7},{5,6},{6,5},{7,4},{8,11},{9,10},{10,... | collective-permute-start | bytes 196616 | tf_op jit(solution)/shard_map/ppermute | solution.py:360
  89.4 1.5 %collective-permute-start.20 = (bf16[32,3200]{1,0:T(8,128)(2,1)S(1)}, bf16[32,3200]{1,0:T(8,128)(2,1)S(1)}, u32[]{:S(2)}, u32[]{:S(2)}) collective-permute-start(bf16[32,3200]{1,0:T(8,128)(2,1)S(1)} %get-tuple-element.79), channel_id=1, source_target_pairs={{0,8},{1,9},{2,10},{3,11},{4,12},{5,13},{6,14},{7,15},{8,0},{9,1},... | collective-permute-start | bytes 614408 | tf_op jit(solution)/shard_map/ppermute | solution.py:360
  89.4 1.7 %collective-permute-start.21 = (bf16[32,3200]{1,0:T(8,128)(2,1)S(1)}, bf16[32,3200]{1,0:T(8,128)(2,1)S(1)}, u32[]{:S(2)}, u32[]{:S(2)}) collective-permute-start(bf16[32,3200]{1,0:T(8,128)(2,1)S(1)} %get-tuple-element.80), channel_id=1, source_target_pairs={{0,8},{1,9},{2,10},{3,11},{4,12},{5,13},{6,14},{7,15},{8,0},{9,1},... | collective-permute-start | bytes 614408 | tf_op jit(solution)/shard_map/ppermute | solution.py:360
  91.2 5.8 %collective-permute-start.22 = (bf16[16,3200]{1,0:T(8,128)(2,1)S(1)}, bf16[16,3200]{1,0:T(8,128)(2,1)S(1)}, u32[]{:S(2)}, u32[]{:S(2)}) collective-permute-start(bf16[16,3200]{1,0:T(8,128)(2,1)S(1)} %get-tuple-element.82), channel_id=1, source_target_pairs={{0,16},{1,17},{2,18},{3,19},{4,20},{5,21},{6,22},{7,23},{8,24},{9,... | collective-permute-start | bytes 307208 | tf_op jit(solution)/shard_map/ppermute | solution.py:360
  91.7 6.8 %collective-permute-start.23 = (bf16[16,3200]{1,0:T(8,128)(2,1)S(1)}, bf16[16,3200]{1,0:T(8,128)(2,1)S(1)}, u32[]{:S(2)}, u32[]{:S(2)}) collective-permute-start(bf16[16,3200]{1,0:T(8,128)(2,1)S(1)} %get-tuple-element.83), channel_id=1, source_target_pairs={{0,16},{1,17},{2,18},{3,19},{4,20},{5,21},{6,22},{7,23},{8,24},{9,... | collective-permute-start | bytes 307208 | tf_op jit(solution)/shard_map/ppermute | solution.py:360
  98.7 4.7 %collective-permute-start.25 = (bf16[32,1536]{1,0:T(8,128)(2,1)S(1)}, bf16[32,1536]{1,0:T(8,128)(2,1)S(1)}, u32[]{:S(2)}, u32[]{:S(2)}) collective-permute-start(bf16[32,1536]{1,0:T(8,128)(2,1)S(1)} %shard_map.111.refs_0_), channel_id=1, source_target_pairs={{0,16},{1,17},{2,18},{3,19},{4,20},{5,21},{6,22},{7,23},{8,24},{9,... | collective-permute-start | bytes 294920 | tf_op jit(solution)/shard_map/ppermute | solution.py:360
  99.1 4.2 %collective-permute-start.24 = (bf16[32,1536]{1,0:T(8,128)(2,1)S(1)}, bf16[32,1536]{1,0:T(8,128)(2,1)S(1)}, u32[]{:S(2)}, u32[]{:S(2)}) collective-permute-start(bf16[32,1536]{1,0:T(8,128)(2,1)S(1)} %shard_map.111.refs_0_), channel_id=1, source_target_pairs={{0,8},{1,9},{2,10},{3,11},{4,12},{5,13},{6,14},{7,15},{8,0},{9,1},... | collective-permute-start | bytes 294920 | tf_op jit(solution)/shard_map/ppermute | solution.py:360
  103.4 1.3 %collective-permute-start.26 = (bf16[32,1536]{1,0:T(8,128)(2,1)S(1)}, bf16[32,1536]{1,0:T(8,128)(2,1)S(1)}, u32[]{:S(2)}, u32[]{:S(2)}) collective-permute-start(bf16[32,1536]{1,0:T(8,128)(2,1)S(1)} %collective-permute-done.25.refs_2_), channel_id=1, source_target_pairs={{0,8},{1,9},{2,10},{3,11},{4,12},{5,13},{6,14},{7,15},{8,0},{9,1},... | collective-permute-start | bytes 294920 | tf_op jit(solution)/shard_map/ppermute | solution.py:360
  105.3 4.3 %collective-permute-start.27 = (bf16[32,1024]{1,0:T(8,128)(2,1)S(1)}, bf16[32,1024]{1,0:T(8,128)(2,1)S(1)}, u32[]{:S(2)}, u32[]{:S(2)}) collective-permute-start(bf16[32,1024]{1,0:T(8,128)(2,1)S(1)} %get-tuple-element.86), channel_id=1, source_target_pairs={{0,1},{1,0},{2,3},{3,2},{4,5},{5,4},{6,7},{7,6},{8,9},{9,8},{10,11... | collective-permute-start | bytes 196616 | tf_op jit(solution)/shard_map/ppermute | solution.py:360
  105.4 6.5 %collective-permute-start.28 = (bf16[32,1024]{1,0:T(8,128)(2,1)S(1)}, bf16[32,1024]{1,0:T(8,128)(2,1)S(1)}, u32[]{:S(2)}, u32[]{:S(2)}) collective-permute-start(bf16[32,1024]{1,0:T(8,128)(2,1)S(1)} %get-tuple-element.87), channel_id=1, source_target_pairs={{0,2},{1,3},{2,0},{3,1},{4,6},{5,7},{6,4},{7,5},{8,10},{9,11},{10,... | collective-permute-start | bytes 196616 | tf_op jit(solution)/shard_map/ppermute | solution.py:360
  109.4 5.2 %collective-permute-start.29 = (bf16[32,1024]{1,0:T(8,128)(2,1)S(1)}, bf16[32,1024]{1,0:T(8,128)(2,1)S(1)}, u32[]{:S(2)}, u32[]{:S(2)}) collective-permute-start(bf16[32,1024]{1,0:T(8,128)(2,1)S(1)} %get-tuple-element.88), channel_id=1, source_target_pairs={{0,3},{1,2},{2,1},{3,0},{4,7},{5,6},{6,5},{7,4},{8,11},{9,10},{10,... | collective-permute-start | bytes 196616 | tf_op jit(solution)/shard_map/ppermute | solution.py:360
  114.5 7.6 %collective-permute-start.30 = (bf16[64,1024]{1,0:T(8,128)(2,1)S(1)}, bf16[64,1024]{1,0:T(8,128)(2,1)S(1)}, u32[]{:S(2)}, u32[]{:S(2)}) collective-permute-start(bf16[64,1024]{1,0:T(8,128)(2,1)S(1)} %shard_map.113), channel_id=1, source_target_pairs={{0,4},{1,5},{2,6},{3,7},{4,0},{5,1},{6,2},{7,3},{8,12},{9,13},{10,... | collective-permute-start | bytes 393224 | tf_op jit(solution)/shard_map/ppermute | solution.py:360

commit v11 on v10

--- a/solution.py
+++ b/solution.py
@@ -31,6 +31,10 @@
         compiler_params=pltpu.CompilerParams(vmem_limit_bytes=limit * 2**20),
         **kw,
     )
+
+
+def in_hbm(x):
+    return pltpu.with_memory_space_constraint(x, pltpu.HBM)
 
 
 def sds(shape, dtype):
@@ -164,41 +168,30 @@
         stacked[jnp.bitwise_xor(turn, s)] = atts[s][...]
     last[...] = stacked[C - 1]
     half = acc.shape[1] // 2
-    acc[...] = res[...].astype(F32) if with_residual else jnp.zeros_like(acc)
     for j in range(2):
         at = slice(j * half, (j + 1) * half)
-        total = None
-        i = 0
+        total = res[:, at].astype(F32) if with_residual else None
         for d in range(C - 1):
-            if d % 2 and d > 1:
-                i += 2
-                continue
-            term = dot(stacked[d], ws[i][:, at])
+            term = dot(stacked[d], ws[d][:, at])
             total = term if total is None else total + term
-            i += 1
-        acc[:, at] += total
-    i = 0
-    for d in range(C - 1):
-        if d % 2 and d > 1:
-            cut = ws[i].shape[1]
-            acc[:, :cut] += dot(stacked[d], ws[i][...])
-            acc[:, cut:] += dot(stacked[d], ws[i + 1][...])
-            i += 1
-        i += 1
+        acc[:, at] = total
 
 
 def last_kernel(E, cap, *refs):
-    accs, lasts, ws, places = refs[:2], refs[2:4], refs[4:6], refs[6:8]
-    own_ref, full_ref, keep_ref, send_ref = refs[8:]
-    cut = ws[0].shape[1]
-    for j, cols in enumerate((slice(0, cut), slice(cut, own_ref.shape[1]))):
+    accs, lasts, w_ref, places = refs[:2], refs[2:4], refs[4], refs[5:7]
+    own_ref, first_ref, second_ref, keep_ref, send_ref = refs[7:]
+    few = first_ref.shape[0]
+    half = own_ref.shape[1] // 2
+    for j in range(2):
+        cols = slice(j * half, (j + 1) * half)
         for t in (1, 0):
-            total = accs[t][:, cols] + dot(lasts[t][...], ws[j][...])
+            total = accs[t][:, cols] + dot(lasts[t][...], w_ref[:, cols])
             rounded = total.astype(BF16)
             if t == 0:
                 own_ref[:, cols] = total
             else:
-                full_ref[:, cols] = rounded
+                first_ref[:, cols] = rounded[:few]
+                second_ref[:, cols] = rounded[few:]
             picked = dot(places[t][...], rounded)
             for d in range(E // 2):
                 near, far = spread(d) ^ (PAIR * t), spread(d) ^ PAIR ^ (PAIR * t)
@@ -311,8 +304,10 @@
         refs[-1][d * cap : (d + 1) * cap, :] = x[cap:, :]
 
 
-def mix_kernel(own, got, out):
-    out[...] = own[...] + got[...].astype(F32)
+def mix_kernel(own, first, second, out):
+    few = first.shape[0]
+    out[:few, :] = own[:few, :] + first[...].astype(F32)
+    out[few:, :] = own[few:, :] + second[...].astype(F32)
 
 
 def combine_kernel(E, cap, mixed, place_ref, gate_ref, *refs):
@@ -372,9 +367,9 @@
         cost=(0, 2**20),
         limit=PACK_LIMIT,
     )(
-        queries.reshape(tok, queries.shape[3]),
-        new_keys_values.reshape(tok, kv),
-        cached_keys_values.reshape(tok, kv),
+        in_hbm(queries.reshape(tok, queries.shape[3])),
+        in_hbm(new_keys_values.reshape(tok, kv)),
+        in_hbm(cached_keys_values.reshape(tok, kv)),
     )
     res = residual.reshape(rows, width)
     got = [msgs[0]] + [permute(msgs[s], ctx=s) for s in range(1, C)]
@@ -396,13 +391,8 @@
     other, own_msg = attend(1, got)
     theirs = permute(other, exp=PAIR)
     (mine,) = attend(0, [own_msg, after(got[1], other)] + got[2:])
-    cut = width - max(width // 4, 128)
-    near = after(shards[1], other)[:, cut:]
     for d in range(2, C, 2):
-        shards[d + 1] = (
-            permute(after(shards[d], other)[:, :cut], exp=1),
-            permute(near, exp=spread(d)),
-        )
+        shards[d + 1] = permute(after(shards[d], other), exp=1)
     tokens_last = lambda x: jnp.transpose(x.reshape(C, tok, x.shape[3]), (0, 2, 1))
     place, gate, *staged = call(
         functools.partial(route_kernel, E, cap),
@@ -415,20 +405,17 @@
     )(tokens_last(after(routes, mine, *step)), tokens_last(after(gates, mine)), out_weight, res)
     shards[0], res = staged
 
-    def gather(x, before):
+    def gather(x, before=lambda: ()):
         atts = {0: x, 1: permute(x, ctx=1)}
         for s in range(2, C, 2):
             atts[s] = permute(x, ctx=s)
-            atts[s + 1] = permute(after(atts[s], *before), ctx=1)
+        due = before()
+        for s in range(2, C, 2):
+            atts[s + 1] = permute(after(atts[s], *due), ctx=1)
         return [atts[s] for s in range(C)]
 
-    other_place = permute(after(place, theirs), exp=PAIR)
-    mine_all = gather(mine, [])
-    theirs_all = gather(after(theirs, place, *mine_all[2::2], *[shards[d][1] for d in range(3, C, 2)]), [])
-    mine_all[1] = after(mine_all[1], other_place)
-
     def project(atts, *extra):
-        operands = [*extra, *atts, shards[0], shards[1], *[w for d in range(2, C - 1) for w in (shards[d] if d % 2 else [shards[d]])]]
+        operands = [*extra, *atts, *[shards[d] for d in range(C - 1)]]
         return call(
             functools.partial(project_kernel, C, bool(extra)),
             [sds((rows, width), F32), sds((rows, qw), BF16)],
@@ -439,20 +426,25 @@
             cost=(0, 2**14),
         )(*operands)
 
+    other_place = permute(after(place, theirs), exp=PAIR)
+    mine_all = gather(mine)
     acc, last = project(mine_all, res)
+    theirs_all = gather(after(theirs, place, shards[1]), lambda: (other_place,))
     acc_far, last_far = project(theirs_all)
     gain = norm_gain.reshape(1, width)
-    own, full, keep, send = call(
+    few = rows * 13 // 16
+    own, first, second, keep, send = call(
         functools.partial(last_kernel, E, cap),
         [
             sds((rows, width), F32),
-            sds((rows, width), BF16),
+            sds((few, width), BF16),
+            sds((rows - few, width), BF16),
             sds((slots, width), F32),
             sds((slots, width), BF16),
         ],
-        8,
+        7,
         cost=(0, 2**14),
-    )(acc, acc_far, last, last_far, *shards[C - 1], place, other_place)
+    )(acc, acc_far, last, last_far, shards[C - 1], place, other_place)
     received = permute(send, exp=PAIR)
     outgoing = call(
         outgoing_kernel, [sds((2 * cap, width), BF16)] * (E // 2), 3, cost=(0, 2**20)
@@ -461,7 +453,8 @@
     for d in reversed(range(1, E // 2)):
         incoming[d] = permute(outgoing[d], exp=spread(d))
     incoming = [incoming[d] for d in range(E // 2)]
-    arrived = permute(after(full, received), exp=PAIR)
+    first = permute(after(first, received), exp=PAIR)
+    second = permute(after(second, first), exp=PAIR)
 
     order = [0]
     bit = C // 2
@@ -492,7 +485,7 @@
         cost=(0, 2**10),
     )(keep, *[permute(x, ctx=bit) for x in sends])
     acts = {0: activated}
-    acts[bit] = after(permute(activated, ctx=bit), arrived)
+    acts[bit] = after(permute(activated, ctx=bit), first)
     bit //= 2
     while bit:
         for r in list(acts):
@@ -507,10 +500,11 @@
     )(acts[0], *[acts[s] for s in range(1, C)], w_down.reshape(hidden, width))
     returned = [expert_out[0]]
     returned += [permute(expert_out[d], exp=spread(d)) for d in reversed(range(1, E // 2))][::-1]
+    returned[0] = after(returned[0], second)
     far = call(
         functools.partial(forward_kernel, cap), sds((slots // 2, width), BF16), E // 2, cost=(0, 2**19)
     )(*returned)
-    mixed = call(mix_kernel, sds((rows, width), F32), 2, cost=(0, 2**14))(own, arrived)
+    mixed = call(mix_kernel, sds((rows, width), F32), 3, cost=(0, 2**14))(own, first, second)
     result = call(
         functools.partial(combine_kernel, E, cap),
         sds((rows, width), BF16),

time: 124 us -> 113 us (0.911)
  waiting for transfers between devices: 79 us -> 68 us
  local copies, waits for them, and re-layouts: 6.54 us -> 3.72 us
  starting transfers between devices: 25 us -> 26.8 us
    ppermute x31, waiting for transfers between devices: 79 us -> 68 us  [permute(): return lax.ppermute(x, ('ctx', 'exp'), pairs)]
    unnamed x22 -> x16, local copies, waits for them, and re-layouts: 6.44 us -> 3.72 us
    ppermute x31, starting transfers between devices: 25 us -> 26.8 us  [permute(): return lax.ppermute(x, ('ctx', 'exp'), pairs)]
  transfers between devices with their start and end apart: 31 -> 31, of which waited for: 20 -> 19; matrix products, arithmetic and copies ran while one was open for 0% -> 0% of each run, Pallas kernels for 7% -> 10%
where the time goes in v11:
time: 113 us; the launch traced here: 112 us
  waiting for transfers between devices  68 us (60%)
  starting transfers between devices  26.8 us (24%)
  Pallas kernels  13.4 us (12%)
  local copies, waits for them, and re-layouts  3.72 us (3%)
    ppermute x31, waiting for transfers between devices, permute(): return lax.ppermute(x, ('ctx', 'exp'), pairs)  68 us
    ppermute x31, starting transfers between devices, permute(): return lax.ppermute(x, ('ctx', 'exp'), pairs)  26.8 us
    pallas_call x2, Pallas kernels, attend(): call(functools.partial(attend_kernel, C, t), [sds((rows, qw), BF16)] + [s...  4.68 us
    unnamed x16, local copies, waits for them, and re-layouts  3.72 us
  transfers between devices with their start and end apart: 31, of which 19 were waited for; matrix products, arithmetic and copies ran while one was open for 0% of the time, Pallas kernels for 10%

profile of v11, /device:TPU:0, one launch (start us, length us, event | category | flops | bytes accessed | tf_op | source)
XLA Modules:
  0.0 112.1 jit_solution(10113753333948372113)
XLA Ops:
  0.0 3.0 %collective-permute-start.3 = (bf16[512,1024]{1,0:T(8,128)(2,1)}, bf16[512,1024]{1,0:T(8,128)(2,1)S(1)}, u32[]{:S(2)}, u32[]{:S(2)}) collective-permute-start(bf16[512,1024]{1,0:T(8,128)(2,1)} %refs_0_.1), channel_id=1, source_target_pairs={{0,2},{1,3},{2,0},{3,1},{4,6},{5,7},{6,4},{7,5},{8,10},{9,11},{10,... | collective-permute-start | bytes 3145736 | tf_op jit(solution)/shard_map/ppermute | solution.py:355
  3.0 1.5 %collective-permute-start.7 = (bf16[512,1024]{1,0:T(8,128)(2,1)}, bf16[512,1024]{1,0:T(8,128)(2,1)S(1)}, u32[]{:S(2)}, u32[]{:S(2)}) collective-permute-start(bf16[512,1024]{1,0:T(8,128)(2,1)} %refs_0_.1), channel_id=1, source_target_pairs={{0,1},{1,0},{2,3},{3,2},{4,5},{5,4},{6,7},{7,6},{8,9},{9,8},{10,11... | collective-permute-start | bytes 3145736 | tf_op jit(solution)/shard_map/ppermute | solution.py:355
  4.5 1.4 %shard_map.100 = (bf16[64,2048]{1,0:T(8,128)(2,1)S(1)}, bf16[64,2048]{1,0:T(8,128)(2,1)S(1)}, bf16[64,2048]{1,0:T(8,128)(2,1)S(1)}, bf16[64,2048]{1,0:T(8,128)(2,1)S(1)}) custom-call(bf16[64,4096]{1,0:T(8,128)(2,1)} %bitcast.25, bf16[64,512]{1,0:T(8,128)(2,1)} %bitcast.26, bf16[64,512]{1,0:T(8,128)(2,1)} %bitcast.27), custom_call_target="tpu_custom_call" | custom-call | bytes 1048576 | tf_op jit(solution)/shard_map/pallas_call | solution.py:361
  6.0 1.6 %collective-permute-start.1 = (bf16[64,2048]{1,0:T(8,128)(2,1)S(1)}, bf16[64,2048]{1,0:T(8,128)(2,1)S(1)}, u32[]{:S(2)}, u32[]{:S(2)}) collective-permute-start(bf16[64,2048]{1,0:T(8,128)(2,1)S(1)} %get-tuple-element.51), channel_id=1, source_target_pairs={{0,16},{1,17},{2,18},{3,19},{4,20},{5,21},{6,22},{7,23},{8,24},{9,... | collective-permute-start | bytes 786440 | tf_op jit(solution)/shard_map/ppermute | solution.py:355
  7.9 7.3 %collective-permute-done.1.refs_2_ = bf16[64,2048]{1,0:T(8,128)(2,1)S(1)} collective-permute-done((bf16[64,2048]{1,0:T(8,128)(2,1)S(1)}, bf16[64,2048]{1,0:T(8,128)(2,1)S(1)}, u32[]{:S(2)}, u32[]{:S(2)}) %collective-permute-start.1) | collective-permute-done | bytes 262176 | tf_op jit(solution)/shard_map/ppermute | solution.py:355
  15.2 4.7 %collective-permute-done.2.refs_3_ = bf16[64,2048]{1,0:T(8,128)(2,1)S(1)} collective-permute-done((bf16[64,2048]{1,0:T(8,128)(2,1)S(1)}, bf16[64,2048]{1,0:T(8,128)(2,1)S(1)}, u32[]{:S(2)}, u32[]{:S(2)}) %collective-permute-start.2) | collective-permute-done | bytes 262176 | tf_op jit(solution)/shard_map/ppermute | solution.py:355
  19.9 2.3 %shard_map.101 = (bf16[256,512]{1,0:T(8,128)(2,1)S(1)}, bf16[64,2048]{1,0:T(8,128)(2,1)S(1)}) custom-call(bf16[64,2048]{1,0:T(8,128)(2,1)S(1)} %get-tuple-element.49.refs_0_, bf16[64,2048]{1,0:T(8,128)(2,1)S(1)} %collective-permute-done.refs_1_, bf16[64,2048]{1,0:T(8,128)(2,1)S(1)} %collective-permute-done.1.refs_2_, ...), custom_call_target="tpu_custom_call" | custom-call | bytes 16384 | tf_op jit(solution)/shard_map/pallas_call | solution.py:382
  22.3 4.1 %collective-permute-done.3.refs_7_.refs_6_ = bf16[512,1024]{1,0:T(8,128)(2,1)S(1)} collective-permute-done((bf16[512,1024]{1,0:T(8,128)(2,1)}, bf16[512,1024]{1,0:T(8,128)(2,1)S(1)}, u32[]{:S(2)}, u32[]{:S(2)}) %collective-permute-start.3) | collective-permute-done | bytes 1048608 | tf_op jit(solution)/shard_map/ppermute | solution.py:355
  26.4 1.7 %collective-permute-start.13 = (bf16[512,1024]{1,0:T(8,128)(2,1)S(1)}, bf16[512,1024]{1,0:T(8,128)(2,1)S(1)}, u32[]{:S(2)}, u32[]{:S(2)}) collective-permute-start(bf16[512,1024]{1,0:T(8,128)(2,1)S(1)} %collective-permute-done.3.refs_7_.refs_6_), channel_id=1, source_target_pairs={{0,1},{1,0},{2,3},{3,2},{4,5},{5,4},{6,7},{7,6},{8,9},{9,8},{10,11... | collective-permute-start | bytes 3145736 | tf_op jit(solution)/shard_map/ppermute | solution.py:355
  28.0 2.6 %collective-permute-start.8 = (bf16[256,512]{1,0:T(8,128)(2,1)S(1)}, bf16[256,512]{1,0:T(8,128)(2,1)S(1)}, u32[]{:S(2)}, u32[]{:S(2)}) collective-permute-start(bf16[256,512]{1,0:T(8,128)(2,1)S(1)} %get-tuple-element.54), channel_id=1, source_target_pairs={{0,4},{1,5},{2,6},{3,7},{4,0},{5,1},{6,2},{7,3},{8,12},{9,13},{10,... | collective-permute-start | bytes 786440 | tf_op jit(solution)/shard_map/ppermute | solution.py:355
  30.6 2.3 %shard_map.102.refs_1_ = bf16[256,512]{1,0:T(8,128)(2,1)S(1)} custom-call(bf16[64,2048]{1,0:T(8,128)(2,1)S(1)} %get-tuple-element.53.refs_0_, bf16[64,2048]{1,0:T(8,128)(2,1)S(1)} %collective-permute-done.refs_1_, bf16[64,2048]{1,0:T(8,128)(2,1)S(1)} %collective-permute-done.1.refs_2_, bf16[64,2048]{1,0:T(8,128)(2,1)S(1)} %collective-permute-done.2.refs_3_), custom_call_target="tpu_custom_call" | custom-call | bytes 16384 | tf_op jit(solution)/shard_map/pallas_call | solution.py:382
  33.0 1.6 %collective-permute-start.5 = (bf16[256,512]{1,0:T(8,128)(2,1)S(1)}, bf16[256,512]{1,0:T(8,128)(2,1)S(1)}, u32[]{:S(2)}, u32[]{:S(2)}) collective-permute-start(bf16[256,512]{1,0:T(8,128)(2,1)S(1)} %shard_map.102.refs_1_), channel_id=1, source_target_pairs={{0,16},{1,17},{2,18},{3,19},{4,20},{5,21},{6,22},{7,23},{8,24},{9,... | collective-permute-start | bytes 786440 | tf_op jit(solution)/shard_map/ppermute | solution.py:355
  34.6 1.2 %copy-done.1 = bf16[512,1024]{1,0:T(8,128)(2,1)S(1)} copy-done((bf16[512,1024]{1,0:T(8,128)(2,1)S(1)}, bf16[512,1024]{1,0:T(8,128)(2,1)}, u32[]{:S(2)}) %copy-start.1) | copy-done | bytes 1048600
  35.8 1.0 copy-done.2
  36.8 0.7 copy-done.3
  37.5 0.7 copy-done.4
  38.6 2.9 %collective-permute-done.8.refs_0_ = bf16[256,512]{1,0:T(8,128)(2,1)S(1)} collective-permute-done((bf16[256,512]{1,0:T(8,128)(2,1)S(1)}, bf16[256,512]{1,0:T(8,128)(2,1)S(1)}, u32[]{:S(2)}, u32[]{:S(2)}) %collective-permute-start.8) | collective-permute-done | bytes 262176 | tf_op jit(solution)/shard_map/ppermute | solution.py:355
  41.5 1.5 %collective-permute-start.10 = (bf16[256,512]{1,0:T(8,128)(2,1)S(1)}, bf16[256,512]{1,0:T(8,128)(2,1)S(1)}, u32[]{:S(2)}, u32[]{:S(2)}) collective-permute-start(bf16[256,512]{1,0:T(8,128)(2,1)S(1)} %collective-permute-done.8.refs_0_), channel_id=1, source_target_pairs={{0,16},{1,17},{2,18},{3,19},{4,20},{5,21},{6,22},{7,23},{8,24},{9,... | collective-permute-start | bytes 786440 | tf_op jit(solution)/shard_map/ppermute | solution.py:355
  43.0 0.5 collective-permute-start.6
  43.5 5.7 %collective-permute-done.11.refs_6_ = bf16[128,256]{1,0:T(8,128)(2,1)S(1)} collective-permute-done((bf16[128,256]{1,0:T(8,128)(2,1)S(1)}, bf16[128,256]{1,0:T(8,128)(2,1)S(1)}, u32[]{:S(2)}, u32[]{:S(2)}) %collective-permute-start.11) | collective-permute-done | bytes 65568 | tf_op jit(solution)/shard_map/ppermute | solution.py:355
  49.2 0.5 collective-permute-start.12
  49.7 1.1 shard_map.104
  51.1 1.1 shard_map.105
  52.2 1.4 %shard_map.106 = (f32[256,1024]{1,0:T(8,128)S(1)}, bf16[208,1024]{1,0:T(8,128)(2,1)S(1)}, bf16[48,1024]{1,0:T(8,128)(2,1)S(1)}, f32[128,1024]{1,0:T(8,128)S(1)}, bf16[128,1024]{1,0:T(8,128)(2,1)S(1)}) custom-call(f32[256,1024]{1,0:T(8,128)S(1)} %get-tuple-element.60.refs_0_, f32[256,1024]{1,0:T(8,128)S(1)} %get-tuple-element.65.refs_1_, ...), custom_call_target="tpu_custom_call" | custom-call | bytes 16384 | tf_op jit(solution)/shard_map/pallas_call | solution.py:436
  53.6 1.1 collective-permute-start.14
  54.7 13.9 %collective-permute-done.14.got_ref = bf16[128,1024]{1,0:T(8,128)(2,1)S(1)} collective-permute-done((bf16[128,1024]{1,0:T(8,128)(2,1)S(1)}, bf16[128,1024]{1,0:T(8,128)(2,1)S(1)}, u32[]{:S(2)}, u32[]{:S(2)}) %collective-permute-start.14) | collective-permute-done | bytes 262176 | tf_op jit(solution)/shard_map/ppermute | solution.py:355
  68.6 0.6 collective-permute-start.17
  69.2 2.9 %collective-permute-start.19 = (bf16[32,1024]{1,0:T(8,128)(2,1)S(1)}, bf16[32,1024]{1,0:T(8,128)(2,1)S(1)}, u32[]{:S(2)}, u32[]{:S(2)}) collective-permute-start(bf16[32,1024]{1,0:T(8,128)(2,1)S(1)} %get-tuple-element.80), channel_id=1, source_target_pairs={{0,3},{1,2},{2,1},{3,0},{4,7},{5,6},{6,5},{7,4},{8,11},{9,10},{10,... | collective-permute-start | bytes 196616 | tf_op jit(solution)/shard_map/ppermute | solution.py:355
  72.2 1.5 %collective-permute-done.17.refs_1_ = bf16[32,1024]{1,0:T(8,128)(2,1)S(1)} collective-permute-done((bf16[32,1024]{1,0:T(8,128)(2,1)S(1)}, bf16[32,1024]{1,0:T(8,128)(2,1)S(1)}, u32[]{:S(2)}, u32[]{:S(2)}) %collective-permute-start.17) | collective-permute-done | bytes 65568 | tf_op jit(solution)/shard_map/ppermute | solution.py:355
  73.6 2.0 %collective-permute-done.19.refs_3_ = bf16[32,1024]{1,0:T(8,128)(2,1)S(1)} collective-permute-done((bf16[32,1024]{1,0:T(8,128)(2,1)S(1)}, bf16[32,1024]{1,0:T(8,128)(2,1)S(1)}, u32[]{:S(2)}, u32[]{:S(2)}) %collective-permute-start.19) | collective-permute-done | bytes 65568 | tf_op jit(solution)/shard_map/ppermute | solution.py:355
  75.6 1.2 %shard_map.109 = (f32[64,3200]{1,0:T(8,128)S(1)}, bf16[32,3200]{1,0:T(8,128)(2,1)S(1)}, bf16[32,3200]{1,0:T(8,128)(2,1)S(1)}) custom-call(bf16[32,1024]{1,0:T(8,128)(2,1)S(1)} %get-tuple-element.77.refs_0_, bf16[32,1024]{1,0:T(8,128)(2,1)S(1)} %collective-permute-done.17.refs_1_, bf16[32,1024]{1,0:T(8,128)(2,1)S(1)} %collective-permute-done.18.refs_2_, ...), custom_call_target="tpu_custom_call" | custom-call | bytes 1024 | tf_op jit(solution)/shard_map/pallas_call | solution.py:464
  77.4 0.9 collective-permute-done.20.refs_0_
  78.7 1.1 collective-permute-start.22
  79.8 1.0 collective-permute-start.23
  80.8 3.7 %collective-permute-done.22.refs_0_ = bf16[16,3200]{1,0:T(8,128)(2,1)S(1)} collective-permute-done((bf16[16,3200]{1,0:T(8,128)(2,1)S(1)}, bf16[16,3200]{1,0:T(8,128)(2,1)S(1)}, u32[]{:S(2)}, u32[]{:S(2)}) %collective-permute-start.22) | collective-permute-done | bytes 102432 | tf_op jit(solution)/shard_map/ppermute | solution.py:355
  84.5 1.5 %collective-permute-done.23.refs_1_ = bf16[16,3200]{1,0:T(8,128)(2,1)S(1)} collective-permute-done((bf16[16,3200]{1,0:T(8,128)(2,1)S(1)}, bf16[16,3200]{1,0:T(8,128)(2,1)S(1)}, u32[]{:S(2)}, u32[]{:S(2)}) %collective-permute-start.23) | collective-permute-done | bytes 102432 | tf_op jit(solution)/shard_map/ppermute | solution.py:355
  86.1 1.1 collective-permute-start.25
  87.2 5.1 %collective-permute-done.15.first = bf16[208,1024]{1,0:T(8,128)(2,1)S(1)} collective-permute-done((bf16[208,1024]{1,0:T(8,128)(2,1)S(1)}, bf16[208,1024]{1,0:T(8,128)(2,1)S(1)}, u32[]{:S(2)}, u32[]{:S(2)}) %collective-permute-start.15) | collective-permute-done | bytes 426016 | tf_op jit(solution)/shard_map/ppermute | solution.py:355
  92.4 1.3 %collective-permute-done.26.refs_3_ = bf16[32,1536]{1,0:T(8,128)(2,1)S(1)} collective-permute-done((bf16[32,1536]{1,0:T(8,128)(2,1)S(1)}, bf16[32,1536]{1,0:T(8,128)(2,1)S(1)}, u32[]{:S(2)}, u32[]{:S(2)}) %collective-permute-start.26) | collective-permute-done | bytes 98336 | tf_op jit(solution)/shard_map/ppermute | solution.py:355
  93.6 0.7 shard_map.112
  94.3 0.6 collective-permute-start.27
  95.0 1.2 %collective-permute-start.28 = (bf16[32,1024]{1,0:T(8,128)(2,1)S(1)}, bf16[32,1024]{1,0:T(8,128)(2,1)S(1)}, u32[]{:S(2)}, u32[]{:S(2)}) collective-permute-start(bf16[32,1024]{1,0:T(8,128)(2,1)S(1)} %get-tuple-element.91), channel_id=1, source_target_pairs={{0,2},{1,3},{2,0},{3,1},{4,6},{5,7},{6,4},{7,5},{8,10},{9,11},{10,... | collective-permute-start | bytes 196616 | tf_op jit(solution)/shard_map/ppermute | solution.py:355
  96.1 1.7 %collective-permute-start.29 = (bf16[32,1024]{1,0:T(8,128)(2,1)S(1)}, bf16[32,1024]{1,0:T(8,128)(2,1)S(1)}, u32[]{:S(2)}, u32[]{:S(2)}) collective-permute-start(bf16[32,1024]{1,0:T(8,128)(2,1)S(1)} %get-tuple-element.92), channel_id=1, source_target_pairs={{0,3},{1,2},{2,1},{3,0},{4,7},{5,6},{6,5},{7,4},{8,11},{9,10},{10,... | collective-permute-start | bytes 196616 | tf_op jit(solution)/shard_map/ppermute | solution.py:355
  97.9 2.3 %collective-permute-done.16.second = bf16[48,1024]{1,0:T(8,128)(2,1)S(1)} collective-permute-done((bf16[48,1024]{1,0:T(8,128)(2,1)S(1)}, bf16[48,1024]{1,0:T(8,128)(2,1)S(1)}, u32[]{:S(2)}, u32[]{:S(2)}) %collective-permute-start.16) | collective-permute-done | bytes 98336 | tf_op jit(solution)/shard_map/ppermute | solution.py:355
  100.1 1.4 %collective-permute-done.28.refs_2_ = bf16[32,1024]{1,0:T(8,128)(2,1)S(1)} collective-permute-done((bf16[32,1024]{1,0:T(8,128)(2,1)S(1)}, bf16[32,1024]{1,0:T(8,128)(2,1)S(1)}, u32[]{:S(2)}, u32[]{:S(2)}) %collective-permute-start.28) | collective-permute-done | bytes 65568 | tf_op jit(solution)/shard_map/ppermute | solution.py:355
  101.5 1.2 %collective-permute-done.29.refs_3_ = bf16[32,1024]{1,0:T(8,128)(2,1)S(1)} collective-permute-done((bf16[32,1024]{1,0:T(8,128)(2,1)S(1)}, bf16[32,1024]{1,0:T(8,128)(2,1)S(1)}, u32[]{:S(2)}, u32[]{:S(2)}) %collective-permute-start.29) | collective-permute-done | bytes 65568 | tf_op jit(solution)/shard_map/ppermute | solution.py:355
  103.0 8.0 %collective-permute-done.30.refs_4_ = bf16[64,1024]{1,0:T(8,128)(2,1)S(1)} collective-permute-done((bf16[64,1024]{1,0:T(8,128)(2,1)S(1)}, bf16[64,1024]{1,0:T(8,128)(2,1)S(1)}, u32[]{:S(2)}, u32[]{:S(2)}) %collective-permute-start.30) | collective-permute-done | bytes 131104 | tf_op jit(solution)/shard_map/ppermute | solution.py:355
  111.0 1.1 shard_map.114
  (46 shorter events, 2.4 us)
Async XLA Ops:
  0.0 26.4 %collective-permute-start.3 = (bf16[512,1024]{1,0:T(8,128)(2,1)}, bf16[512,1024]{1,0:T(8,128)(2,1)S(1)}, u32[]{:S(2)}, u32[]{:S(2)}) collective-permute-start(bf16[512,1024]{1,0:T(8,128)(2,1)} %refs_0_.1), channel_id=1, source_target_pairs={{0,2},{1,3},{2,0},{3,1},{4,6},{5,7},{6,4},{7,5},{8,10},{9,11},{10,... | collective-permute-start | bytes 3145736 | tf_op jit(solution)/shard_map/ppermute | solution.py:355
  3.0 38.4 %collective-permute-start.7 = (bf16[512,1024]{1,0:T(8,128)(2,1)}, bf16[512,1024]{1,0:T(8,128)(2,1)S(1)}, u32[]{:S(2)}, u32[]{:S(2)}) collective-permute-start(bf16[512,1024]{1,0:T(8,128)(2,1)} %refs_0_.1), channel_id=1, source_target_pairs={{0,1},{1,0},{2,3},{3,2},{4,5},{5,4},{6,7},{7,6},{8,9},{9,8},{10,11... | collective-permute-start | bytes 3145736 | tf_op jit(solution)/shard_map/ppermute | solution.py:355
  6.0 1.9 %collective-permute-start = (bf16[64,2048]{1,0:T(8,128)(2,1)S(1)}, bf16[64,2048]{1,0:T(8,128)(2,1)S(1)}, u32[]{:S(2)}, u32[]{:S(2)}) collective-permute-start(bf16[64,2048]{1,0:T(8,128)(2,1)S(1)} %get-tuple-element.50), channel_id=1, source_target_pairs={{0,8},{1,9},{2,10},{3,11},{4,12},{5,13},{6,14},{7,15},{8,0},{9,1},... | collective-permute-start | bytes 786440 | tf_op jit(solution)/shard_map/ppermute | solution.py:355
  6.0 9.2 %collective-permute-start.1 = (bf16[64,2048]{1,0:T(8,128)(2,1)S(1)}, bf16[64,2048]{1,0:T(8,128)(2,1)S(1)}, u32[]{:S(2)}, u32[]{:S(2)}) collective-permute-start(bf16[64,2048]{1,0:T(8,128)(2,1)S(1)} %get-tuple-element.51), channel_id=1, source_target_pairs={{0,16},{1,17},{2,18},{3,19},{4,20},{5,21},{6,22},{7,23},{8,24},{9,... | collective-permute-start | bytes 786440 | tf_op jit(solution)/shard_map/ppermute | solution.py:355
  7.6 12.3 %collective-permute-start.2 = (bf16[64,2048]{1,0:T(8,128)(2,1)S(1)}, bf16[64,2048]{1,0:T(8,128)(2,1)S(1)}, u32[]{:S(2)}, u32[]{:S(2)}) collective-permute-start(bf16[64,2048]{1,0:T(8,128)(2,1)S(1)} %get-tuple-element.52), channel_id=1, source_target_pairs={{0,24},{1,25},{2,26},{3,27},{4,28},{5,29},{6,30},{7,31},{8,16},{9,... | collective-permute-start | bytes 786440 | tf_op jit(solution)/shard_map/ppermute | solution.py:355
  26.4 25.8 %collective-permute-start.13 = (bf16[512,1024]{1,0:T(8,128)(2,1)S(1)}, bf16[512,1024]{1,0:T(8,128)(2,1)S(1)}, u32[]{:S(2)}, u32[]{:S(2)}) collective-permute-start(bf16[512,1024]{1,0:T(8,128)(2,1)S(1)} %collective-permute-done.3.refs_7_.refs_6_), channel_id=1, source_target_pairs={{0,1},{1,0},{2,3},{3,2},{4,5},{5,4},{6,7},{7,6},{8,9},{9,8},{10,11... | collective-permute-start | bytes 3145736 | tf_op jit(solution)/shard_map/ppermute | solution.py:355
  28.0 13.4 %collective-permute-start.8 = (bf16[256,512]{1,0:T(8,128)(2,1)S(1)}, bf16[256,512]{1,0:T(8,128)(2,1)S(1)}, u32[]{:S(2)}, u32[]{:S(2)}) collective-permute-start(bf16[256,512]{1,0:T(8,128)(2,1)S(1)} %get-tuple-element.54), channel_id=1, source_target_pairs={{0,4},{1,5},{2,6},{3,7},{4,0},{5,1},{6,2},{7,3},{8,12},{9,13},{10,... | collective-permute-start | bytes 786440 | tf_op jit(solution)/shard_map/ppermute | solution.py:355
  33.0 10.0 %collective-permute-start.5 = (bf16[256,512]{1,0:T(8,128)(2,1)S(1)}, bf16[256,512]{1,0:T(8,128)(2,1)S(1)}, u32[]{:S(2)}, u32[]{:S(2)}) collective-permute-start(bf16[256,512]{1,0:T(8,128)(2,1)S(1)} %shard_map.102.refs_1_), channel_id=1, source_target_pairs={{0,16},{1,17},{2,18},{3,19},{4,20},{5,21},{6,22},{7,23},{8,24},{9,... | collective-permute-start | bytes 786440 | tf_op jit(solution)/shard_map/ppermute | solution.py:355
  34.6 1.2 %copy-start.1 = (bf16[512,1024]{1,0:T(8,128)(2,1)S(1)}, bf16[512,1024]{1,0:T(8,128)(2,1)}, u32[]{:S(2)}) copy-start(bf16[512,1024]{1,0:T(8,128)(2,1)} %refs_0_.1) | copy-start | bytes 3145732
  35.8 1.0 copy-start.2
  36.8 0.7 copy-start.3
  37.5 0.7 copy-start.4
  41.5 7.7 %collective-permute-start.10 = (bf16[256,512]{1,0:T(8,128)(2,1)S(1)}, bf16[256,512]{1,0:T(8,128)(2,1)S(1)}, u32[]{:S(2)}, u32[]{:S(2)}) collective-permute-start(bf16[256,512]{1,0:T(8,128)(2,1)S(1)} %collective-permute-done.8.refs_0_), channel_id=1, source_target_pairs={{0,16},{1,17},{2,18},{3,19},{4,20},{5,21},{6,22},{7,23},{8,24},{9,... | collective-permute-start | bytes 786440 | tf_op jit(solution)/shard_map/ppermute | solution.py:355
  43.0 6.2 %collective-permute-start.11 = (bf16[128,256]{1,0:T(8,128)(2,1)S(1)}, bf16[128,256]{1,0:T(8,128)(2,1)S(1)}, u32[]{:S(2)}, u32[]{:S(2)}) collective-permute-start(bf16[128,256]{1,0:T(8,128)(2,1)S(1)} %get-tuple-element.63.refs_5_.place_ref), channel_id=1, source_target_pairs={{0,4},{1,5},{2,6},{3,7},{4,0},{5,1},{6,2},{7,3},{8,12},{9,13},{10,... | collective-permute-start | bytes 196616 | tf_op jit(solution)/shard_map/ppermute | solution.py:355
  43.0 6.7 %collective-permute-start.4 = (bf16[256,512]{1,0:T(8,128)(2,1)S(1)}, bf16[256,512]{1,0:T(8,128)(2,1)S(1)}, u32[]{:S(2)}, u32[]{:S(2)}) collective-permute-start(bf16[256,512]{1,0:T(8,128)(2,1)S(1)} %shard_map.102.refs_1_), channel_id=1, source_target_pairs={{0,8},{1,9},{2,10},{3,11},{4,12},{5,13},{6,14},{7,15},{8,0},{9,1},... | collective-permute-start | bytes 786440 | tf_op jit(solution)/shard_map/ppermute | solution.py:355
  43.0 6.7 %collective-permute-start.6 = (bf16[256,512]{1,0:T(8,128)(2,1)S(1)}, bf16[256,512]{1,0:T(8,128)(2,1)S(1)}, u32[]{:S(2)}, u32[]{:S(2)}) collective-permute-start(bf16[256,512]{1,0:T(8,128)(2,1)S(1)} %collective-permute-done.5.refs_3_), channel_id=1, source_target_pairs={{0,8},{1,9},{2,10},{3,11},{4,12},{5,13},{6,14},{7,15},{8,0},{9,1},... | collective-permute-start | bytes 786440 | tf_op jit(solution)/shard_map/ppermute | solution.py:355
  49.2 1.6 %collective-permute-start.9 = (bf16[256,512]{1,0:T(8,128)(2,1)S(1)}, bf16[256,512]{1,0:T(8,128)(2,1)S(1)}, u32[]{:S(2)}, u32[]{:S(2)}) collective-permute-start(bf16[256,512]{1,0:T(8,128)(2,1)S(1)} %collective-permute-done.8.refs_0_), channel_id=1, source_target_pairs={{0,8},{1,9},{2,10},{3,11},{4,12},{5,13},{6,14},{7,15},{8,0},{9,1},... | collective-permute-start | bytes 786440 | tf_op jit(solution)/shard_map/ppermute | solution.py:355
  49.2 1.9 %collective-permute-start.12 = (bf16[256,512]{1,0:T(8,128)(2,1)S(1)}, bf16[256,512]{1,0:T(8,128)(2,1)S(1)}, u32[]{:S(2)}, u32[]{:S(2)}) collective-permute-start(bf16[256,512]{1,0:T(8,128)(2,1)S(1)} %collective-permute-done.10.refs_2_), channel_id=1, source_target_pairs={{0,8},{1,9},{2,10},{3,11},{4,12},{5,13},{6,14},{7,15},{8,0},{9,1},... | collective-permute-start | bytes 786440 | tf_op jit(solution)/shard_map/ppermute | solution.py:355
  49.7 18.8 %copy-start.5 = (f32[1024]{0:T(1024)S(1)}, f32[1024]{0:T(1024)}, u32[]{:S(2)}) copy-start(f32[1024]{0:T(1024)} %param.15) | copy-start | bytes 12292
  49.7 25.9 %slice-start = ((s8[6291456]{0:T(1024)(128)(4,1)}), s8[4194304]{0:T(1024)(128)(4,1)S(1)}, s32[]{:S(2)}) async-start(s8[6291456]{0:T(1024)(128)(4,1)} %bitcast.16), calls=%async_computation | async-start | bytes 8388608
  50.8 24.8 %slice-start.1 = ((s8[6291456]{0:T(1024)(128)(4,1)}), s8[2097152]{0:T(1024)(128)(4,1)S(1)}, s32[]{:S(2)}) async-start(s8[6291456]{0:T(1024)(128)(4,1)} %bitcast.16), calls=%async_computation.1 | async-start | bytes 4194304
  52.2 41.5 %copy-start = (bf16[1,1536,1024]{2,1,0:T(8,128)(2,1)S(1)}, bf16[1,1536,1024]{2,1,0:T(8,128)(2,1)}, u32[]{:S(2)}) copy-start(bf16[1,1536,1024]{2,1,0:T(8,128)(2,1)} %param.19) | copy-start | bytes 9437188
  53.6 14.9 %collective-permute-start.14 = (bf16[128,1024]{1,0:T(8,128)(2,1)S(1)}, bf16[128,1024]{1,0:T(8,128)(2,1)S(1)}, u32[]{:S(2)}, u32[]{:S(2)}) collective-permute-start(bf16[128,1024]{1,0:T(8,128)(2,1)S(1)} %get-tuple-element.71), channel_id=1, source_target_pairs={{0,4},{1,5},{2,6},{3,7},{4,0},{5,1},{6,2},{7,3},{8,12},{9,13},{10,... | collective-permute-start | bytes 786440 | tf_op jit(solution)/shard_map/ppermute | solution.py:355
  68.6 5.0 %collective-permute-start.17 = (bf16[32,1024]{1,0:T(8,128)(2,1)S(1)}, bf16[32,1024]{1,0:T(8,128)(2,1)S(1)}, u32[]{:S(2)}, u32[]{:S(2)}) collective-permute-start(bf16[32,1024]{1,0:T(8,128)(2,1)S(1)} %get-tuple-element.78), channel_id=1, source_target_pairs={{0,1},{1,0},{2,3},{3,2},{4,5},{5,4},{6,7},{7,6},{8,9},{9,8},{10,11... | collective-permute-start | bytes 196616 | tf_op jit(solution)/shard_map/ppermute | solution.py:355
  69.2 4.4 %collective-permute-start.18 = (bf16[32,1024]{1,0:T(8,128)(2,1)S(1)}, bf16[32,1024]{1,0:T(8,128)(2,1)S(1)}, u32[]{:S(2)}, u32[]{:S(2)}) collective-permute-start(bf16[32,1024]{1,0:T(8,128)(2,1)S(1)} %get-tuple-element.79), channel_id=1, source_target_pairs={{0,2},{1,3},{2,0},{3,1},{4,6},{5,7},{6,4},{7,5},{8,10},{9,11},{10,... | collective-permute-start | bytes 196616 | tf_op jit(solution)/shard_map/ppermute | solution.py:355
  69.2 6.4 %collective-permute-start.19 = (bf16[32,1024]{1,0:T(8,128)(2,1)S(1)}, bf16[32,1024]{1,0:T(8,128)(2,1)S(1)}, u32[]{:S(2)}, u32[]{:S(2)}) collective-permute-start(bf16[32,1024]{1,0:T(8,128)(2,1)S(1)} %get-tuple-element.80), channel_id=1, source_target_pairs={{0,3},{1,2},{2,1},{3,0},{4,7},{5,6},{6,5},{7,4},{8,11},{9,10},{10,... | collective-permute-start | bytes 196616 | tf_op jit(solution)/shard_map/ppermute | solution.py:355
  72.2 20.2 %collective-permute-start.15 = (bf16[208,1024]{1,0:T(8,128)(2,1)S(1)}, bf16[208,1024]{1,0:T(8,128)(2,1)S(1)}, u32[]{:S(2)}, u32[]{:S(2)}) collective-permute-start(bf16[208,1024]{1,0:T(8,128)(2,1)S(1)} %get-tuple-element.72), channel_id=1, source_target_pairs={{0,4},{1,5},{2,6},{3,7},{4,0},{5,1},{6,2},{7,3},{8,12},{9,13},{10,... | collective-permute-start | bytes 1277960 | tf_op jit(solution)/shard_map/ppermute | solution.py:355
  76.9 1.5 %collective-permute-start.20 = (bf16[32,3200]{1,0:T(8,128)(2,1)S(1)}, bf16[32,3200]{1,0:T(8,128)(2,1)S(1)}, u32[]{:S(2)}, u32[]{:S(2)}) collective-permute-start(bf16[32,3200]{1,0:T(8,128)(2,1)S(1)} %get-tuple-element.82), channel_id=1, source_target_pairs={{0,8},{1,9},{2,10},{3,11},{4,12},{5,13},{6,14},{7,15},{8,0},{9,1},... | collective-permute-start | bytes 614408 | tf_op jit(solution)/shard_map/ppermute | solution.py:355
  76.9 1.7 %collective-permute-start.21 = (bf16[32,3200]{1,0:T(8,128)(2,1)S(1)}, bf16[32,3200]{1,0:T(8,128)(2,1)S(1)}, u32[]{:S(2)}, u32[]{:S(2)}) collective-permute-start(bf16[32,3200]{1,0:T(8,128)(2,1)S(1)} %get-tuple-element.83), channel_id=1, source_target_pairs={{0,8},{1,9},{2,10},{3,11},{4,12},{5,13},{6,14},{7,15},{8,0},{9,1},... | collective-permute-start | bytes 614408 | tf_op jit(solution)/shard_map/ppermute | solution.py:355
  78.7 5.8 %collective-permute-start.22 = (bf16[16,3200]{1,0:T(8,128)(2,1)S(1)}, bf16[16,3200]{1,0:T(8,128)(2,1)S(1)}, u32[]{:S(2)}, u32[]{:S(2)}) collective-permute-start(bf16[16,3200]{1,0:T(8,128)(2,1)S(1)} %get-tuple-element.85), channel_id=1, source_target_pairs={{0,16},{1,17},{2,18},{3,19},{4,20},{5,21},{6,22},{7,23},{8,24},{9,... | collective-permute-start | bytes 307208 | tf_op jit(solution)/shard_map/ppermute | solution.py:355
  79.8 6.2 %collective-permute-start.23 = (bf16[16,3200]{1,0:T(8,128)(2,1)S(1)}, bf16[16,3200]{1,0:T(8,128)(2,1)S(1)}, u32[]{:S(2)}, u32[]{:S(2)}) collective-permute-start(bf16[16,3200]{1,0:T(8,128)(2,1)S(1)} %get-tuple-element.86), channel_id=1, source_target_pairs={{0,16},{1,17},{2,18},{3,19},{4,20},{5,21},{6,22},{7,23},{8,24},{9,... | collective-permute-start | bytes 307208 | tf_op jit(solution)/shard_map/ppermute | solution.py:355
  86.1 6.2 %collective-permute-start.25 = (bf16[32,1536]{1,0:T(8,128)(2,1)S(1)}, bf16[32,1536]{1,0:T(8,128)(2,1)S(1)}, u32[]{:S(2)}, u32[]{:S(2)}) collective-permute-start(bf16[32,1536]{1,0:T(8,128)(2,1)S(1)} %shard_map.111.refs_0_), channel_id=1, source_target_pairs={{0,16},{1,17},{2,18},{3,19},{4,20},{5,21},{6,22},{7,23},{8,24},{9,... | collective-permute-start | bytes 294920 | tf_op jit(solution)/shard_map/ppermute | solution.py:355
  87.2 5.1 %collective-permute-start.24 = (bf16[32,1536]{1,0:T(8,128)(2,1)S(1)}, bf16[32,1536]{1,0:T(8,128)(2,1)S(1)}, u32[]{:S(2)}, u32[]{:S(2)}) collective-permute-start(bf16[32,1536]{1,0:T(8,128)(2,1)S(1)} %shard_map.111.refs_0_), channel_id=1, source_target_pairs={{0,8},{1,9},{2,10},{3,11},{4,12},{5,13},{6,14},{7,15},{8,0},{9,1},... | collective-permute-start | bytes 294920 | tf_op jit(solution)/shard_map/ppermute | solution.py:355
  92.3 1.3 %collective-permute-start.26 = (bf16[32,1536]{1,0:T(8,128)(2,1)S(1)}, bf16[32,1536]{1,0:T(8,128)(2,1)S(1)}, u32[]{:S(2)}, u32[]{:S(2)}) collective-permute-start(bf16[32,1536]{1,0:T(8,128)(2,1)S(1)} %collective-permute-done.25.refs_2_), channel_id=1, source_target_pairs={{0,8},{1,9},{2,10},{3,11},{4,12},{5,13},{6,14},{7,15},{8,0},{9,1},... | collective-permute-start | bytes 294920 | tf_op jit(solution)/shard_map/ppermute | solution.py:355
  92.3 7.8 %collective-permute-start.16 = (bf16[48,1024]{1,0:T(8,128)(2,1)S(1)}, bf16[48,1024]{1,0:T(8,128)(2,1)S(1)}, u32[]{:S(2)}, u32[]{:S(2)}) collective-permute-start(bf16[48,1024]{1,0:T(8,128)(2,1)S(1)} %get-tuple-element.74), channel_id=1, source_target_pairs={{0,4},{1,5},{2,6},{3,7},{4,0},{5,1},{6,2},{7,3},{8,12},{9,13},{10,... | collective-permute-start | bytes 294920 | tf_op jit(solution)/shard_map/ppermute | solution.py:355
  94.3 5.8 %collective-permute-start.27 = (bf16[32,1024]{1,0:T(8,128)(2,1)S(1)}, bf16[32,1024]{1,0:T(8,128)(2,1)S(1)}, u32[]{:S(2)}, u32[]{:S(2)}) collective-permute-start(bf16[32,1024]{1,0:T(8,128)(2,1)S(1)} %get-tuple-element.90), channel_id=1, source_target_pairs={{0,1},{1,0},{2,3},{3,2},{4,5},{5,4},{6,7},{7,6},{8,9},{9,8},{10,11... | collective-permute-start | bytes 196616 | tf_op jit(solution)/shard_map/ppermute | solution.py:355
  95.0 6.6 %collective-permute-start.28 = (bf16[32,1024]{1,0:T(8,128)(2,1)S(1)}, bf16[32,1024]{1,0:T(8,128)(2,1)S(1)}, u32[]{:S(2)}, u32[]{:S(2)}) collective-permute-start(bf16[32,1024]{1,0:T(8,128)(2,1)S(1)} %get-tuple-element.91), channel_id=1, source_target_pairs={{0,2},{1,3},{2,0},{3,1},{4,6},{5,7},{6,4},{7,5},{8,10},{9,11},{10,... | collective-permute-start | bytes 196616 | tf_op jit(solution)/shard_map/ppermute | solution.py:355
  96.1 6.6 %collective-permute-start.29 = (bf16[32,1024]{1,0:T(8,128)(2,1)S(1)}, bf16[32,1024]{1,0:T(8,128)(2,1)S(1)}, u32[]{:S(2)}, u32[]{:S(2)}) collective-permute-start(bf16[32,1024]{1,0:T(8,128)(2,1)S(1)} %get-tuple-element.92), channel_id=1, source_target_pairs={{0,3},{1,2},{2,1},{3,0},{4,7},{5,6},{6,5},{7,4},{8,11},{9,10},{10,... | collective-permute-start | bytes 196616 | tf_op jit(solution)/shard_map/ppermute | solution.py:355
  102.7 8.3 %collective-permute-start.30 = (bf16[64,1024]{1,0:T(8,128)(2,1)S(1)}, bf16[64,1024]{1,0:T(8,128)(2,1)S(1)}, u32[]{:S(2)}, u32[]{:S(2)}) collective-permute-start(bf16[64,1024]{1,0:T(8,128)(2,1)S(1)} %shard_map.113), channel_id=1, source_target_pairs={{0,4},{1,5},{2,6},{3,7},{4,0},{5,1},{6,2},{7,3},{8,12},{9,13},{10,... | collective-permute-start | bytes 393224 | tf_op jit(solution)/shard_map/ppermute | solution.py:355

commit v12 on v11

--- a/solution.py
+++ b/solution.py
@@ -1,4 +1,5 @@
 import functools
+import math
 
 import jax
 import jax.numpy as jnp
@@ -13,6 +14,7 @@
 HEAD_SIZE = 128
 GROUP_EXTENT = QUERY_HEADS // KEY_VALUE_HEADS
 NEG_FILL = -1e30
+EXPONENT = HEAD_SIZE ** (-0.5) * math.log2(math.e)
 BF16 = jnp.bfloat16
 F32 = jnp.float32
 VMEM = pl.BlockSpec(memory_space=pltpu.VMEM)
@@ -70,15 +72,23 @@
         c.wait()
 
 
+def far_first(C):
+    return [*range(2, C), 1, 0]
+
+
+def hops(E):
+    return [*reversed(range(E // 2))]
+
+
 def pack_kernel(C, qw, q_ref, new_ref, past_ref, *refs):
     outs, sems = refs[:C], refs[C]
     c = lax.axis_index("ctx")
     _, lo = own_hi_lo()
     kv = new_ref.shape[1]
     pairs = []
-    for s in reversed(range(C)):
+    for i, s in enumerate(far_first(C)):
         target = jnp.bitwise_xor(c, s)
-        out = outs[s]
+        out = outs[i]
         for t in range(2):
             shard = lax.div(target, PAIR) * 2 * PAIR + lax.rem(target, PAIR)
             shard = shard + PAIR * jnp.bitwise_xor(lo, t)
@@ -92,15 +102,14 @@
 def attend_kernel(C, t, *refs):
     msgs, out, kv_s, q_s = refs[:C], refs[C], refs[-2], refs[-1]
     if t == 1:
-        refs[C + 1][...] = msgs[0][...]
+        refs[C + 1][...] = msgs[-1][...]
     c = lax.axis_index("ctx")
     tok, qw = msgs[0].shape[0], out.shape[1]
     rows = C * tok
     _, lo = own_hi_lo()
     shard = lax.div(c, PAIR) * 2 * PAIR + lax.rem(c, PAIR) + PAIR * jnp.bitwise_xor(lo, t)
     head = lax.div(shard * (qw // HEAD_SIZE), GROUP_EXTENT)
-    for s in range(C):
-        msg = msgs[s]
+    for msg, s in zip(msgs, far_first(C)):
         at = aligned(jnp.bitwise_xor(c, s) * tok, tok)
         q_s[pl.ds(at, tok), :] = msg[:, t * qw : (t + 1) * qw]
         for i, to in ((0, rows + at), (1, at)):
@@ -109,20 +118,22 @@
                 cols = pl.ds(aligned(first + head * HEAD_SIZE, 128), HEAD_SIZE)
                 kv_s[pl.ds(to, tok), part * HEAD_SIZE : (part + 1) * HEAD_SIZE] = msg[:, cols]
     block = 128
+    visible = lax.broadcasted_iota(jnp.int32, (block, block), 1) <= lax.broadcasted_iota(
+        jnp.int32, (block, block), 0
+    )
     for b in range(rows // block):
         seen = rows + (b + 1) * block
         k = kv_s[:seen, :HEAD_SIZE]
         v = kv_s[:seen, HEAD_SIZE:]
-        row = lax.broadcasted_iota(jnp.int32, (block, seen), 0) + (rows + b * block)
-        visible = lax.broadcasted_iota(jnp.int32, (block, seen), 1) <= row
         at = slice(b * block, (b + 1) * block)
         for h in range(qw // HEAD_SIZE):
             q = q_s[at, h * HEAD_SIZE : (h + 1) * HEAD_SIZE]
             scores = lax.dot_general(q, k, (((1,), (1,)), ((), ())), preferred_element_type=F32)
-            scores = jnp.where(visible, scores * HEAD_SIZE ** (-0.5), NEG_FILL)
-            weights = jnp.exp(scores - jnp.max(scores, axis=1, keepdims=True))
-            total = jnp.sum(weights, axis=1, keepdims=True)
-            numerator = dot(weights.astype(BF16), v)
+            parts = (scores[:, : seen - block], jnp.where(visible, scores[:, seen - block :], NEG_FILL))
+            top = jnp.maximum(*[jnp.max(x, axis=1, keepdims=True) for x in parts])
+            parts = [jnp.exp2((x - top) * EXPONENT) for x in parts]
+            total = sum(jnp.sum(x, axis=1, keepdims=True) for x in parts)
+            numerator = dot(jnp.concatenate([x.astype(BF16) for x in parts], axis=1), v)
             out[at, h * HEAD_SIZE : (h + 1) * HEAD_SIZE] = (numerator / total).astype(BF16)
 
 
@@ -168,24 +179,31 @@
         stacked[jnp.bitwise_xor(turn, s)] = atts[s][...]
     last[...] = stacked[C - 1]
     half = acc.shape[1] // 2
+    pieces = list(ws)
+    shards = [pieces.pop(0) if d < 2 or d % 2 == 0 else (pieces.pop(0), pieces.pop(0)) for d in range(C - 1)]
     for j in range(2):
         at = slice(j * half, (j + 1) * half)
         total = res[:, at].astype(F32) if with_residual else None
-        for d in range(C - 1):
-            term = dot(stacked[d], ws[d][:, at])
-            total = term if total is None else total + term
+        for d, w in enumerate(shards):
+            if not isinstance(w, tuple):
+                term = dot(stacked[d], w[:, at])
+                total = term if total is None else total + term
         acc[:, at] = total
+    for d, w in enumerate(shards):
+        if isinstance(w, tuple):
+            cut = w[0].shape[1]
+            acc[:, :cut] += dot(stacked[d], w[0][...])
+            acc[:, cut:] += dot(stacked[d], w[1][...])
 
 
 def last_kernel(E, cap, *refs):
-    accs, lasts, w_ref, places = refs[:2], refs[2:4], refs[4], refs[5:7]
-    own_ref, first_ref, second_ref, keep_ref, send_ref = refs[7:]
+    accs, lasts, ws, places = refs[:2], refs[2:4], refs[4:6], refs[6:8]
+    own_ref, first_ref, second_ref, keep_ref, send_ref = refs[8:]
     few = first_ref.shape[0]
-    half = own_ref.shape[1] // 2
-    for j in range(2):
-        cols = slice(j * half, (j + 1) * half)
+    cut = ws[0].shape[1]
+    for j, cols in enumerate((slice(0, cut), slice(cut, own_ref.shape[1]))):
         for t in (1, 0):
-            total = accs[t][:, cols] + dot(lasts[t][...], w_ref[:, cols])
+            total = accs[t][:, cols] + dot(lasts[t][...], ws[j][...])
             rounded = total.astype(BF16)
             if t == 0:
                 own_ref[:, cols] = total
@@ -214,10 +232,10 @@
     e = lax.axis_index("exp")
     own_rows = E * cap // C
     wide = w_ref.shape[1]
-    for d in range(E // 2):
+    for x, d in zip(xs, hops(E)):
         for t in range(2):
             at = aligned(jnp.bitwise_xor(e, spread(d) ^ (PAIR * t)) * cap, cap)
-            x_s[pl.ds(at, cap), :] = xs[d][t * cap : (t + 1) * cap, :]
+            x_s[pl.ds(at, cap), :] = x[t * cap : (t + 1) * cap, :]
     plain = x_s[...].astype(F32) / gain_ref[...]
     square = jnp.sum(plain * plain, axis=1, keepdims=True)
     lane = lax.broadcasted_iota(jnp.int32, (E * cap, 128), 1)
@@ -299,8 +317,8 @@
             outs[d][t * cap : (t + 1) * cap, :] = part_s[pl.ds(at, cap), :]
 
 
-def forward_kernel(cap, *refs):
-    for d, x in enumerate(refs[:-1]):
+def forward_kernel(E, cap, *refs):
+    for x, d in zip(refs[:-1], hops(E)):
         refs[-1][d * cap : (d + 1) * cap, :] = x[cap:, :]
 
 
@@ -311,19 +329,24 @@
 
 
 def combine_kernel(E, cap, mixed, place_ref, gate_ref, *refs):
-    xs, far, out, x_s = refs[: E // 2], refs[E // 2], refs[E // 2 + 1], refs[E // 2 + 2]
-    for d in range(E // 2):
+    xs, (far, out, x_s, out_s, sems) = refs[: E // 2], refs[E // 2 :]
+    for x, d in zip(xs, hops(E)):
         at = spread(d) * cap
-        x_s[at : at + cap, :] = xs[d][:cap, :]
+        x_s[at : at + cap, :] = x[:cap, :]
         at = (spread(d) ^ PAIR) * cap
         x_s[at : at + cap, :] = far[d * cap : (d + 1) * cap, :]
-    half = mixed.shape[1] // 2
-    for j in range(2):
-        cols = slice(j * half, (j + 1) * half)
+    count, _, width = out_s.shape
+    copies = []
+    for j in range(count):
+        cols = slice(j * width, (j + 1) * width)
         collected = lax.dot_general(
             place_ref[...], x_s[:, cols], (((0,), (0,)), ((), ())), preferred_element_type=F32
         )
-        out[:, cols] = (mixed[:, cols] + gate_ref[:, :1] * collected).astype(BF16)
+        out_s[j] = (mixed[:, cols] + gate_ref[:, :1] * collected).astype(BF16)
+        copies.append(pltpu.make_async_copy(out_s.at[j], out.at[:, cols], sems.at[j]))
+        copies[-1].start()
+    for c in copies:
+        c.wait()
 
 
 def body(
@@ -372,7 +395,7 @@
         in_hbm(cached_keys_values.reshape(tok, kv)),
     )
     res = residual.reshape(rows, width)
-    got = [msgs[0]] + [permute(msgs[s], ctx=s) for s in range(1, C)]
+    got = [permute(x, ctx=s) if s else x for s, x in zip(far_first(C), msgs)]
     shards = {0: out_weight, 1: permute(out_weight, exp=1)}
     for d in range(2, C, 2):
         shards[d] = permute(out_weight, exp=spread(d))
@@ -390,9 +413,14 @@
 
     other, own_msg = attend(1, got)
     theirs = permute(other, exp=PAIR)
-    (mine,) = attend(0, [own_msg, after(got[1], other)] + got[2:])
+    (mine,) = attend(0, [after(got[0], other), *got[1:-1], own_msg])
+    cut = width - max(width // 4, 128)
+    near = after(shards[1], theirs)[:, cut:]
     for d in range(2, C, 2):
-        shards[d + 1] = permute(after(shards[d], other), exp=1)
+        shards[d + 1] = (
+            permute(after(shards[d], other)[:, :cut], exp=1),
+            permute(near, exp=spread(d)),
+        )
     tokens_last = lambda x: jnp.transpose(x.reshape(C, tok, x.shape[3]), (0, 2, 1))
     place, gate, *staged = call(
         functools.partial(route_kernel, E, cap),
@@ -415,7 +443,7 @@
         return [atts[s] for s in range(C)]
 
     def project(atts, *extra):
-        operands = [*extra, *atts, *[shards[d] for d in range(C - 1)]]
+        operands = [*extra, *atts, shards[0], shards[1], *[w for d in range(2, C - 1) for w in (shards[d] if d % 2 else [shards[d]])]]
         return call(
             functools.partial(project_kernel, C, bool(extra)),
             [sds((rows, width), F32), sds((rows, qw), BF16)],
@@ -429,7 +457,8 @@
     other_place = permute(after(place, theirs), exp=PAIR)
     mine_all = gather(mine)
     acc, last = project(mine_all, res)
-    theirs_all = gather(after(theirs, place, shards[1]), lambda: (other_place,))
+    quarter = [shards[d][1] for d in range(3, C, 2)]
+    theirs_all = gather(after(theirs, place, shards[1]), lambda: (other_place, *quarter))
     acc_far, last_far = project(theirs_all)
     gain = norm_gain.reshape(1, width)
     few = rows * 13 // 16
@@ -442,17 +471,14 @@
             sds((slots, width), F32),
             sds((slots, width), BF16),
         ],
-        7,
+        8,
         cost=(0, 2**14),
-    )(acc, acc_far, last, last_far, shards[C - 1], place, other_place)
+    )(acc, acc_far, last, last_far, *shards[C - 1], place, other_place)
     received = permute(send, exp=PAIR)
     outgoing = call(
         outgoing_kernel, [sds((2 * cap, width), BF16)] * (E // 2), 3, cost=(0, 2**20)
     )(keep, received, gain)
-    incoming = {0: outgoing[0]}
-    for d in reversed(range(1, E // 2)):
-        incoming[d] = permute(outgoing[d], exp=spread(d))
-    incoming = [incoming[d] for d in range(E // 2)]
+    incoming = [permute(outgoing[d], exp=spread(d)) for d in hops(E)[:-1]] + [outgoing[0]]
     first = permute(after(first, received), exp=PAIR)
     second = permute(after(second, first), exp=PAIR)
 
@@ -498,18 +524,23 @@
         scratch=[pltpu.VMEM((slots, hidden), BF16), pltpu.VMEM((slots, width), BF16)],
         cost=(2 * slots * width * hidden, 2 * width * hidden),
     )(acts[0], *[acts[s] for s in range(1, C)], w_down.reshape(hidden, width))
-    returned = [expert_out[0]]
-    returned += [permute(expert_out[d], exp=spread(d)) for d in reversed(range(1, E // 2))][::-1]
-    returned[0] = after(returned[0], second)
+    returned = [permute(expert_out[d], exp=spread(d)) for d in hops(E)[:-1]]
+    returned.append(after(expert_out[0], second))
     far = call(
-        functools.partial(forward_kernel, cap), sds((slots // 2, width), BF16), E // 2, cost=(0, 2**19)
+        functools.partial(forward_kernel, E, cap), sds((slots // 2, width), BF16), E // 2, cost=(0, 2**19)
     )(*returned)
     mixed = call(mix_kernel, sds((rows, width), F32), 3, cost=(0, 2**14))(own, first, second)
+    columns = min(4, width // 128)
     result = call(
         functools.partial(combine_kernel, E, cap),
         sds((rows, width), BF16),
         4 + E // 2,
-        scratch=[pltpu.VMEM((slots, width), BF16)],
+        scratch=[
+            pltpu.VMEM((slots, width), BF16),
+            pltpu.VMEM((columns, rows, width // columns), BF16),
+            pltpu.SemaphoreType.DMA((columns,)),
+        ],
+        out_specs=HBM,
         cost=(0, 2 * 2**20),
     )(mixed, place, gate, *returned, permute(far, exp=PAIR))
     return result.reshape(C, 1, tok, width)

time: 113 us -> 112 us (level)
  waiting for transfers between devices: 68 us -> 61.4 us
  starting transfers between devices: 26.8 us -> 33.1 us
    ppermute x31 -> x32, waiting for transfers between devices: 68 us -> 61.4 us  [permute(): return lax.ppermute(x, ('ctx', 'exp'), pairs)]
    ppermute x31 -> x32, starting transfers between devices: 26.8 us -> 33.1 us  [permute(): return lax.ppermute(x, ('ctx', 'exp'), pairs)]
  transfers between devices with their start and end apart: 31 -> 32, of which waited for: 19 -> 20; matrix products, arithmetic and copies ran while one was open for 0% -> 0% of each run, Pallas kernels for 10% -> 10%
where the time goes in v12:
time: 112 us
  waiting for transfers between devices  61.4 us (55%)
  starting transfers between devices  33.1 us (30%)
  Pallas kernels  13.5 us (12%)
  local copies, waits for them, and re-layouts  3.83 us (3%)
    ppermute x32, waiting for transfers between devices, permute(): return lax.ppermute(x, ('ctx', 'exp'), pairs)  61.4 us
    ppermute x32, starting transfers between devices, permute(): return lax.ppermute(x, ('ctx', 'exp'), pairs)  33.1 us
    pallas_call x2, Pallas kernels, attend(): call(functools.partial(attend_kernel, C, t), [sds((rows, qw), BF16)] + [s...  4.63 us
    unnamed x16, local copies, waits for them, and re-layouts  3.73 us
  transfers between devices with their start and end apart: 32, of which 20 were waited for; matrix products, arithmetic and copies ran while one was open for 0% of the time, Pallas kernels for 10%

profile of v12, /device:TPU:0, one launch (start us, length us, event | category | flops | bytes accessed | tf_op | source)
XLA Modules:
  0.0 112.1 jit_solution(10134664374207463354)
XLA Ops:
  0.0 3.0 %collective-permute-start.3 = (bf16[512,1024]{1,0:T(8,128)(2,1)}, bf16[512,1024]{1,0:T(8,128)(2,1)S(1)}, u32[]{:S(2)}, u32[]{:S(2)}) collective-permute-start(bf16[512,1024]{1,0:T(8,128)(2,1)} %refs_0_.1), channel_id=1, source_target_pairs={{0,2},{1,3},{2,0},{3,1},{4,6},{5,7},{6,4},{7,5},{8,10},{9,11},{10,... | collective-permute-start | bytes 3145736 | tf_op jit(solution)/shard_map/ppermute | solution.py:378
  3.0 1.5 %collective-permute-start.7 = (bf16[512,1024]{1,0:T(8,128)(2,1)}, bf16[512,1024]{1,0:T(8,128)(2,1)S(1)}, u32[]{:S(2)}, u32[]{:S(2)}) collective-permute-start(bf16[512,1024]{1,0:T(8,128)(2,1)} %refs_0_.1), channel_id=1, source_target_pairs={{0,1},{1,0},{2,3},{3,2},{4,5},{5,4},{6,7},{7,6},{8,9},{9,8},{10,11... | collective-permute-start | bytes 3145736 | tf_op jit(solution)/shard_map/ppermute | solution.py:378
  4.5 1.4 %shard_map.100 = (bf16[64,2048]{1,0:T(8,128)(2,1)S(1)}, bf16[64,2048]{1,0:T(8,128)(2,1)S(1)}, bf16[64,2048]{1,0:T(8,128)(2,1)S(1)}, bf16[64,2048]{1,0:T(8,128)(2,1)S(1)}) custom-call(bf16[64,4096]{1,0:T(8,128)(2,1)} %bitcast.25, bf16[64,512]{1,0:T(8,128)(2,1)} %bitcast.26, bf16[64,512]{1,0:T(8,128)(2,1)} %bitcast.27), custom_call_target="tpu_custom_call" | custom-call | bytes 1048576 | tf_op jit(solution)/shard_map/pallas_call | solution.py:384
  6.0 1.6 %collective-permute-start = (bf16[64,2048]{1,0:T(8,128)(2,1)S(1)}, bf16[64,2048]{1,0:T(8,128)(2,1)S(1)}, u32[]{:S(2)}, u32[]{:S(2)}) collective-permute-start(bf16[64,2048]{1,0:T(8,128)(2,1)S(1)} %get-tuple-element.50), channel_id=1, source_target_pairs={{0,16},{1,17},{2,18},{3,19},{4,20},{5,21},{6,22},{7,23},{8,24},{9,... | collective-permute-start | bytes 786440 | tf_op jit(solution)/shard_map/ppermute | solution.py:378
  7.6 0.6 collective-permute-start.2
  8.2 7.1 %collective-permute-done.refs_0_ = bf16[64,2048]{1,0:T(8,128)(2,1)S(1)} collective-permute-done((bf16[64,2048]{1,0:T(8,128)(2,1)S(1)}, bf16[64,2048]{1,0:T(8,128)(2,1)S(1)}, u32[]{:S(2)}, u32[]{:S(2)}) %collective-permute-start) | collective-permute-done | bytes 262176 | tf_op jit(solution)/shard_map/ppermute | solution.py:378
  15.3 2.9 %collective-permute-done.1.refs_1_ = bf16[64,2048]{1,0:T(8,128)(2,1)S(1)} collective-permute-done((bf16[64,2048]{1,0:T(8,128)(2,1)S(1)}, bf16[64,2048]{1,0:T(8,128)(2,1)S(1)}, u32[]{:S(2)}, u32[]{:S(2)}) %collective-permute-start.1) | collective-permute-done | bytes 262176 | tf_op jit(solution)/shard_map/ppermute | solution.py:378
  18.2 2.3 %shard_map.101 = (bf16[256,512]{1,0:T(8,128)(2,1)S(1)}, bf16[64,2048]{1,0:T(8,128)(2,1)S(1)}) custom-call(bf16[64,2048]{1,0:T(8,128)(2,1)S(1)} %collective-permute-done.refs_0_, bf16[64,2048]{1,0:T(8,128)(2,1)S(1)} %collective-permute-done.1.refs_1_, bf16[64,2048]{1,0:T(8,128)(2,1)S(1)} %collective-permute-done.2.refs_2_, ...), custom_call_target="tpu_custom_call" | custom-call | bytes 16384 | tf_op jit(solution)/shard_map/pallas_call | solution.py:405
  20.5 2.7 %collective-permute-start.8 = (bf16[256,512]{1,0:T(8,128)(2,1)S(1)}, bf16[256,512]{1,0:T(8,128)(2,1)S(1)}, u32[]{:S(2)}, u32[]{:S(2)}) collective-permute-start(bf16[256,512]{1,0:T(8,128)(2,1)S(1)} %get-tuple-element.54), channel_id=1, source_target_pairs={{0,4},{1,5},{2,6},{3,7},{4,0},{5,1},{6,2},{7,3},{8,12},{9,13},{10,... | collective-permute-start | bytes 786440 | tf_op jit(solution)/shard_map/ppermute | solution.py:378
  23.2 6.8 %collective-permute-done.3.refs_7_.refs_6_ = bf16[512,1024]{1,0:T(8,128)(2,1)S(1)} collective-permute-done((bf16[512,1024]{1,0:T(8,128)(2,1)}, bf16[512,1024]{1,0:T(8,128)(2,1)S(1)}, u32[]{:S(2)}, u32[]{:S(2)}) %collective-permute-start.3) | collective-permute-done | bytes 1048608 | tf_op jit(solution)/shard_map/ppermute | solution.py:378
  30.1 2.7 %collective-permute-start.14 = (bf16[512,768]{1,0:T(8,128)(2,1)S(1)}, bf16[512,768]{1,0:T(8,128)(2,1)S(1)}, u32[]{:S(2)}, u32[]{:S(2)}) collective-permute-start(bf16[512,768]{1,0:T(8,128)(2,1)S(1)} %slice.7), channel_id=1, source_target_pairs={{0,1},{1,0},{2,3},{3,2},{4,5},{5,4},{6,7},{7,6},{8,9},{9,8},{10,11... | collective-permute-start | bytes 2359304 | tf_op jit(solution)/shard_map/ppermute | solution.py:378
  32.8 2.3 %shard_map.102.refs_1_ = bf16[256,512]{1,0:T(8,128)(2,1)S(1)} custom-call(bf16[64,2048]{1,0:T(8,128)(2,1)S(1)} %collective-permute-done.refs_0_, bf16[64,2048]{1,0:T(8,128)(2,1)S(1)} %collective-permute-done.1.refs_1_, bf16[64,2048]{1,0:T(8,128)(2,1)S(1)} %collective-permute-done.2.refs_2_, bf16[64,2048]{1,0:T(8,128)(2,1)S(1)} %get-tuple-element.56.refs_3_), custom_call_target="tpu_custom_call" | custom-call | bytes 16384 | tf_op jit(solution)/shard_map/pallas_call | solution.py:405
  35.1 2.4 %collective-permute-start.5 = (bf16[256,512]{1,0:T(8,128)(2,1)S(1)}, bf16[256,512]{1,0:T(8,128)(2,1)S(1)}, u32[]{:S(2)}, u32[]{:S(2)}) collective-permute-start(bf16[256,512]{1,0:T(8,128)(2,1)S(1)} %shard_map.102.refs_1_), channel_id=1, source_target_pairs={{0,16},{1,17},{2,18},{3,19},{4,20},{5,21},{6,22},{7,23},{8,24},{9,... | collective-permute-start | bytes 786440 | tf_op jit(solution)/shard_map/ppermute | solution.py:378
  37.4 1.2 %copy-done.1 = bf16[512,1024]{1,0:T(8,128)(2,1)S(1)} copy-done((bf16[512,1024]{1,0:T(8,128)(2,1)S(1)}, bf16[512,1024]{1,0:T(8,128)(2,1)}, u32[]{:S(2)}) %copy-start.1) | copy-done | bytes 1048600
  38.7 1.0 copy-done.2
  39.7 0.7 copy-done.3
  40.4 0.7 copy-done.4
  41.7 3.0 %collective-permute-start.11 = (bf16[128,256]{1,0:T(8,128)(2,1)S(1)}, bf16[128,256]{1,0:T(8,128)(2,1)S(1)}, u32[]{:S(2)}, u32[]{:S(2)}) collective-permute-start(bf16[128,256]{1,0:T(8,128)(2,1)S(1)} %get-tuple-element.64.refs_6_.place_ref), channel_id=1, source_target_pairs={{0,4},{1,5},{2,6},{3,7},{4,0},{5,1},{6,2},{7,3},{8,12},{9,13},{10,... | collective-permute-start | bytes 196616 | tf_op jit(solution)/shard_map/ppermute | solution.py:378
  44.7 2.8 %collective-permute-done.11.refs_7_ = bf16[128,256]{1,0:T(8,128)(2,1)S(1)} collective-permute-done((bf16[128,256]{1,0:T(8,128)(2,1)S(1)}, bf16[128,256]{1,0:T(8,128)(2,1)S(1)}, u32[]{:S(2)}, u32[]{:S(2)}) %collective-permute-start.11) | collective-permute-done | bytes 65568 | tf_op jit(solution)/shard_map/ppermute | solution.py:378
  47.5 0.7 collective-permute-done.10.refs_2_
  48.2 1.5 %collective-permute-done.12.refs_5_ = bf16[512,256]{1,0:T(8,128)(2,1)S(1)} collective-permute-done((bf16[512,256]{1,0:T(8,128)(2,1)S(1)}, bf16[512,256]{1,0:T(8,128)(2,1)S(1)}, u32[]{:S(2)}, u32[]{:S(2)}) %collective-permute-start.12) | collective-permute-done | bytes 262176 | tf_op jit(solution)/shard_map/ppermute | solution.py:378
  49.7 1.1 shard_map.104
  51.2 1.1 shard_map.105
  52.3 1.6 %shard_map.106 = (f32[256,1024]{1,0:T(8,128)S(1)}, bf16[208,1024]{1,0:T(8,128)(2,1)S(1)}, bf16[48,1024]{1,0:T(8,128)(2,1)S(1)}, f32[128,1024]{1,0:T(8,128)S(1)}, bf16[128,1024]{1,0:T(8,128)(2,1)S(1)}) custom-call(f32[256,1024]{1,0:T(8,128)S(1)} %get-tuple-element.61.refs_0_, f32[256,1024]{1,0:T(8,128)S(1)} %get-tuple-element.67.refs_1_, ...), custom_call_target="tpu_custom_call" | custom-call | bytes 16384 | tf_op jit(solution)/shard_map/pallas_call | solution.py:465
  53.9 2.4 %collective-permute-start.15 = (bf16[128,1024]{1,0:T(8,128)(2,1)S(1)}, bf16[128,1024]{1,0:T(8,128)(2,1)S(1)}, u32[]{:S(2)}, u32[]{:S(2)}) collective-permute-start(bf16[128,1024]{1,0:T(8,128)(2,1)S(1)} %get-tuple-element.73), channel_id=1, source_target_pairs={{0,4},{1,5},{2,6},{3,7},{4,0},{5,1},{6,2},{7,3},{8,12},{9,13},{10,... | collective-permute-start | bytes 786440 | tf_op jit(solution)/shard_map/ppermute | solution.py:378
  56.3 12.6 %collective-permute-done.15.got_ref = bf16[128,1024]{1,0:T(8,128)(2,1)S(1)} collective-permute-done((bf16[128,1024]{1,0:T(8,128)(2,1)S(1)}, bf16[128,1024]{1,0:T(8,128)(2,1)S(1)}, u32[]{:S(2)}, u32[]{:S(2)}) %collective-permute-start.15) | collective-permute-done | bytes 262176 | tf_op jit(solution)/shard_map/ppermute | solution.py:378
  69.0 1.8 %collective-permute-start.19 = (bf16[32,1024]{1,0:T(8,128)(2,1)S(1)}, bf16[32,1024]{1,0:T(8,128)(2,1)S(1)}, u32[]{:S(2)}, u32[]{:S(2)}) collective-permute-start(bf16[32,1024]{1,0:T(8,128)(2,1)S(1)} %get-tuple-element.80), channel_id=1, source_target_pairs={{0,2},{1,3},{2,0},{3,1},{4,6},{5,7},{6,4},{7,5},{8,10},{9,11},{10,... | collective-permute-start | bytes 196616 | tf_op jit(solution)/shard_map/ppermute | solution.py:378
  70.8 1.7 %collective-permute-start.20 = (bf16[32,1024]{1,0:T(8,128)(2,1)S(1)}, bf16[32,1024]{1,0:T(8,128)(2,1)S(1)}, u32[]{:S(2)}, u32[]{:S(2)}) collective-permute-start(bf16[32,1024]{1,0:T(8,128)(2,1)S(1)} %get-tuple-element.81), channel_id=1, source_target_pairs={{0,1},{1,0},{2,3},{3,2},{4,5},{5,4},{6,7},{7,6},{8,9},{9,8},{10,11... | collective-permute-start | bytes 196616 | tf_op jit(solution)/shard_map/ppermute | solution.py:378
  72.5 1.0 collective-permute-start.16
  73.5 0.7 collective-permute-done.18.refs_0_
  74.2 0.9 collective-permute-done.20.refs_2_
  75.1 1.3 %shard_map.109 = (f32[64,3200]{1,0:T(8,128)S(1)}, bf16[32,3200]{1,0:T(8,128)(2,1)S(1)}, bf16[32,3200]{1,0:T(8,128)(2,1)S(1)}) custom-call(bf16[32,1024]{1,0:T(8,128)(2,1)S(1)} %collective-permute-done.18.refs_0_, bf16[32,1024]{1,0:T(8,128)(2,1)S(1)} %collective-permute-done.19.refs_1_, bf16[32,1024]{1,0:T(8,128)(2,1)S(1)} %collective-permute-done.20.refs_2_, ...), custom_call_target="tpu_custom_call" | custom-call | bytes 1024 | tf_op jit(solution)/shard_map/pallas_call | solution.py:490
  76.3 0.5 collective-permute-start.22
  76.8 0.9 collective-permute-done.21.refs_0_
  78.2 1.8 %collective-permute-start.23 = (bf16[16,3200]{1,0:T(8,128)(2,1)S(1)}, bf16[16,3200]{1,0:T(8,128)(2,1)S(1)}, u32[]{:S(2)}, u32[]{:S(2)}) collective-permute-start(bf16[16,3200]{1,0:T(8,128)(2,1)S(1)} %get-tuple-element.87), channel_id=1, source_target_pairs={{0,16},{1,17},{2,18},{3,19},{4,20},{5,21},{6,22},{7,23},{8,24},{9,... | collective-permute-start | bytes 307208 | tf_op jit(solution)/shard_map/ppermute | solution.py:378
  80.2 3.7 %collective-permute-done.23.refs_0_ = bf16[16,3200]{1,0:T(8,128)(2,1)S(1)} collective-permute-done((bf16[16,3200]{1,0:T(8,128)(2,1)S(1)}, bf16[16,3200]{1,0:T(8,128)(2,1)S(1)}, u32[]{:S(2)}, u32[]{:S(2)}) %collective-permute-start.23) | collective-permute-done | bytes 102432 | tf_op jit(solution)/shard_map/ppermute | solution.py:378
  83.9 1.5 %collective-permute-done.24.refs_1_ = bf16[16,3200]{1,0:T(8,128)(2,1)S(1)} collective-permute-done((bf16[16,3200]{1,0:T(8,128)(2,1)S(1)}, bf16[16,3200]{1,0:T(8,128)(2,1)S(1)}, u32[]{:S(2)}, u32[]{:S(2)}) %collective-permute-start.24) | collective-permute-done | bytes 102432 | tf_op jit(solution)/shard_map/ppermute | solution.py:378
  85.6 1.8 %collective-permute-start.26 = (bf16[32,1536]{1,0:T(8,128)(2,1)S(1)}, bf16[32,1536]{1,0:T(8,128)(2,1)S(1)}, u32[]{:S(2)}, u32[]{:S(2)}) collective-permute-start(bf16[32,1536]{1,0:T(8,128)(2,1)S(1)} %shard_map.111.refs_0_), channel_id=1, source_target_pairs={{0,16},{1,17},{2,18},{3,19},{4,20},{5,21},{6,22},{7,23},{8,24},{9,... | collective-permute-start | bytes 294920 | tf_op jit(solution)/shard_map/ppermute | solution.py:378
  87.4 5.2 %collective-permute-done.16.first = bf16[208,1024]{1,0:T(8,128)(2,1)S(1)} collective-permute-done((bf16[208,1024]{1,0:T(8,128)(2,1)S(1)}, bf16[208,1024]{1,0:T(8,128)(2,1)S(1)}, u32[]{:S(2)}, u32[]{:S(2)}) %collective-permute-start.16) | collective-permute-done | bytes 426016 | tf_op jit(solution)/shard_map/ppermute | solution.py:378
  92.6 1.3 %collective-permute-done.27.refs_3_ = bf16[32,1536]{1,0:T(8,128)(2,1)S(1)} collective-permute-done((bf16[32,1536]{1,0:T(8,128)(2,1)S(1)}, bf16[32,1536]{1,0:T(8,128)(2,1)S(1)}, u32[]{:S(2)}, u32[]{:S(2)}) %collective-permute-start.27) | collective-permute-done | bytes 98336 | tf_op jit(solution)/shard_map/ppermute | solution.py:378
  93.9 0.7 shard_map.112
  94.5 1.7 %collective-permute-start.28 = (bf16[32,1024]{1,0:T(8,128)(2,1)S(1)}, bf16[32,1024]{1,0:T(8,128)(2,1)S(1)}, u32[]{:S(2)}, u32[]{:S(2)}) collective-permute-start(bf16[32,1024]{1,0:T(8,128)(2,1)S(1)} %get-tuple-element.90), channel_id=1, source_target_pairs={{0,3},{1,2},{2,1},{3,0},{4,7},{5,6},{6,5},{7,4},{8,11},{9,10},{10,... | collective-permute-start | bytes 196616 | tf_op jit(solution)/shard_map/ppermute | solution.py:378
  96.5 1.6 %collective-permute-start.30 = (bf16[32,1024]{1,0:T(8,128)(2,1)S(1)}, bf16[32,1024]{1,0:T(8,128)(2,1)S(1)}, u32[]{:S(2)}, u32[]{:S(2)}) collective-permute-start(bf16[32,1024]{1,0:T(8,128)(2,1)S(1)} %get-tuple-element.92), channel_id=1, source_target_pairs={{0,1},{1,0},{2,3},{3,2},{4,5},{5,4},{6,7},{7,6},{8,9},{9,8},{10,11... | collective-permute-start | bytes 196616 | tf_op jit(solution)/shard_map/ppermute | solution.py:378
  98.1 2.6 %collective-permute-done.17.second = bf16[48,1024]{1,0:T(8,128)(2,1)S(1)} collective-permute-done((bf16[48,1024]{1,0:T(8,128)(2,1)S(1)}, bf16[48,1024]{1,0:T(8,128)(2,1)S(1)}, u32[]{:S(2)}, u32[]{:S(2)}) %collective-permute-start.17) | collective-permute-done | bytes 98336 | tf_op jit(solution)/shard_map/ppermute | solution.py:378
  100.7 1.3 %collective-permute-done.28.refs_0_ = bf16[32,1024]{1,0:T(8,128)(2,1)S(1)} collective-permute-done((bf16[32,1024]{1,0:T(8,128)(2,1)S(1)}, bf16[32,1024]{1,0:T(8,128)(2,1)S(1)}, u32[]{:S(2)}, u32[]{:S(2)}) %collective-permute-start.28) | collective-permute-done | bytes 65568 | tf_op jit(solution)/shard_map/ppermute | solution.py:378
  102.3 0.6 collective-permute-start.31
  102.9 8.1 %collective-permute-done.31.refs_4_ = bf16[64,1024]{1,0:T(8,128)(2,1)S(1)} collective-permute-done((bf16[64,1024]{1,0:T(8,128)(2,1)S(1)}, bf16[64,1024]{1,0:T(8,128)(2,1)S(1)}, u32[]{:S(2)}, u32[]{:S(2)}) %collective-permute-start.31) | collective-permute-done | bytes 131104 | tf_op jit(solution)/shard_map/ppermute | solution.py:378
  111.0 1.1 shard_map.114
  (50 shorter events, 2.6 us)
Async XLA Ops:
  0.0 30.0 %collective-permute-start.3 = (bf16[512,1024]{1,0:T(8,128)(2,1)}, bf16[512,1024]{1,0:T(8,128)(2,1)S(1)}, u32[]{:S(2)}, u32[]{:S(2)}) collective-permute-start(bf16[512,1024]{1,0:T(8,128)(2,1)} %refs_0_.1), channel_id=1, source_target_pairs={{0,2},{1,3},{2,0},{3,1},{4,6},{5,7},{6,4},{7,5},{8,10},{9,11},{10,... | collective-permute-start | bytes 3145736 | tf_op jit(solution)/shard_map/ppermute | solution.py:378
  3.0 38.4 %collective-permute-start.7 = (bf16[512,1024]{1,0:T(8,128)(2,1)}, bf16[512,1024]{1,0:T(8,128)(2,1)S(1)}, u32[]{:S(2)}, u32[]{:S(2)}) collective-permute-start(bf16[512,1024]{1,0:T(8,128)(2,1)} %refs_0_.1), channel_id=1, source_target_pairs={{0,1},{1,0},{2,3},{3,2},{4,5},{5,4},{6,7},{7,6},{8,9},{9,8},{10,11... | collective-permute-start | bytes 3145736 | tf_op jit(solution)/shard_map/ppermute | solution.py:378
  6.0 9.3 %collective-permute-start = (bf16[64,2048]{1,0:T(8,128)(2,1)S(1)}, bf16[64,2048]{1,0:T(8,128)(2,1)S(1)}, u32[]{:S(2)}, u32[]{:S(2)}) collective-permute-start(bf16[64,2048]{1,0:T(8,128)(2,1)S(1)} %get-tuple-element.50), channel_id=1, source_target_pairs={{0,16},{1,17},{2,18},{3,19},{4,20},{5,21},{6,22},{7,23},{8,24},{9,... | collective-permute-start | bytes 786440 | tf_op jit(solution)/shard_map/ppermute | solution.py:378
  7.6 10.6 %collective-permute-start.1 = (bf16[64,2048]{1,0:T(8,128)(2,1)S(1)}, bf16[64,2048]{1,0:T(8,128)(2,1)S(1)}, u32[]{:S(2)}, u32[]{:S(2)}) collective-permute-start(bf16[64,2048]{1,0:T(8,128)(2,1)S(1)} %get-tuple-element.51), channel_id=1, source_target_pairs={{0,24},{1,25},{2,26},{3,27},{4,28},{5,29},{6,30},{7,31},{8,16},{9,... | collective-permute-start | bytes 786440 | tf_op jit(solution)/shard_map/ppermute | solution.py:378
  7.6 10.6 %collective-permute-start.2 = (bf16[64,2048]{1,0:T(8,128)(2,1)S(1)}, bf16[64,2048]{1,0:T(8,128)(2,1)S(1)}, u32[]{:S(2)}, u32[]{:S(2)}) collective-permute-start(bf16[64,2048]{1,0:T(8,128)(2,1)S(1)} %get-tuple-element.52), channel_id=1, source_target_pairs={{0,8},{1,9},{2,10},{3,11},{4,12},{5,13},{6,14},{7,15},{8,0},{9,1},... | collective-permute-start | bytes 786440 | tf_op jit(solution)/shard_map/ppermute | solution.py:378
  20.5 20.9 %collective-permute-start.8 = (bf16[256,512]{1,0:T(8,128)(2,1)S(1)}, bf16[256,512]{1,0:T(8,128)(2,1)S(1)}, u32[]{:S(2)}, u32[]{:S(2)}) collective-permute-start(bf16[256,512]{1,0:T(8,128)(2,1)S(1)} %get-tuple-element.54), channel_id=1, source_target_pairs={{0,4},{1,5},{2,6},{3,7},{4,0},{5,1},{6,2},{7,3},{8,12},{9,13},{10,... | collective-permute-start | bytes 786440 | tf_op jit(solution)/shard_map/ppermute | solution.py:378
  30.1 22.2 %collective-permute-start.14 = (bf16[512,768]{1,0:T(8,128)(2,1)S(1)}, bf16[512,768]{1,0:T(8,128)(2,1)S(1)}, u32[]{:S(2)}, u32[]{:S(2)}) collective-permute-start(bf16[512,768]{1,0:T(8,128)(2,1)S(1)} %slice.7), channel_id=1, source_target_pairs={{0,1},{1,0},{2,3},{3,2},{4,5},{5,4},{6,7},{7,6},{8,9},{9,8},{10,11... | collective-permute-start | bytes 2359304 | tf_op jit(solution)/shard_map/ppermute | solution.py:378
  35.1 9.6 %collective-permute-start.5 = (bf16[256,512]{1,0:T(8,128)(2,1)S(1)}, bf16[256,512]{1,0:T(8,128)(2,1)S(1)}, u32[]{:S(2)}, u32[]{:S(2)}) collective-permute-start(bf16[256,512]{1,0:T(8,128)(2,1)S(1)} %shard_map.102.refs_1_), channel_id=1, source_target_pairs={{0,16},{1,17},{2,18},{3,19},{4,20},{5,21},{6,22},{7,23},{8,24},{9,... | collective-permute-start | bytes 786440 | tf_op jit(solution)/shard_map/ppermute | solution.py:378
  37.4 1.2 %copy-start.1 = (bf16[512,1024]{1,0:T(8,128)(2,1)S(1)}, bf16[512,1024]{1,0:T(8,128)(2,1)}, u32[]{:S(2)}) copy-start(bf16[512,1024]{1,0:T(8,128)(2,1)} %refs_0_.1) | copy-start | bytes 3145732
  38.7 1.0 copy-start.2
  39.7 0.7 copy-start.3
  40.4 0.7 copy-start.4
  41.5 6.7 %collective-permute-start.10 = (bf16[256,512]{1,0:T(8,128)(2,1)S(1)}, bf16[256,512]{1,0:T(8,128)(2,1)S(1)}, u32[]{:S(2)}, u32[]{:S(2)}) collective-permute-start(bf16[256,512]{1,0:T(8,128)(2,1)S(1)} %collective-permute-done.8.refs_0_), channel_id=1, source_target_pairs={{0,16},{1,17},{2,18},{3,19},{4,20},{5,21},{6,22},{7,23},{8,24},{9,... | collective-permute-start | bytes 786440 | tf_op jit(solution)/shard_map/ppermute | solution.py:378
  41.6 8.1 %collective-permute-start.12 = (bf16[512,256]{1,0:T(8,128)(2,1)S(1)}, bf16[512,256]{1,0:T(8,128)(2,1)S(1)}, u32[]{:S(2)}, u32[]{:S(2)}) collective-permute-start(bf16[512,256]{1,0:T(8,128)(2,1)S(1)} %slice.6), channel_id=1, source_target_pairs={{0,2},{1,3},{2,0},{3,1},{4,6},{5,7},{6,4},{7,5},{8,10},{9,11},{10,... | collective-permute-start | bytes 786440 | tf_op jit(solution)/shard_map/ppermute | solution.py:378
  41.7 5.8 %collective-permute-start.11 = (bf16[128,256]{1,0:T(8,128)(2,1)S(1)}, bf16[128,256]{1,0:T(8,128)(2,1)S(1)}, u32[]{:S(2)}, u32[]{:S(2)}) collective-permute-start(bf16[128,256]{1,0:T(8,128)(2,1)S(1)} %get-tuple-element.64.refs_6_.place_ref), channel_id=1, source_target_pairs={{0,4},{1,5},{2,6},{3,7},{4,0},{5,1},{6,2},{7,3},{8,12},{9,13},{10,... | collective-permute-start | bytes 196616 | tf_op jit(solution)/shard_map/ppermute | solution.py:378
  44.7 5.0 %collective-permute-start.4 = (bf16[256,512]{1,0:T(8,128)(2,1)S(1)}, bf16[256,512]{1,0:T(8,128)(2,1)S(1)}, u32[]{:S(2)}, u32[]{:S(2)}) collective-permute-start(bf16[256,512]{1,0:T(8,128)(2,1)S(1)} %shard_map.102.refs_1_), channel_id=1, source_target_pairs={{0,8},{1,9},{2,10},{3,11},{4,12},{5,13},{6,14},{7,15},{8,0},{9,1},... | collective-permute-start | bytes 786440 | tf_op jit(solution)/shard_map/ppermute | solution.py:378
  47.5 2.2 %collective-permute-start.6 = (bf16[256,512]{1,0:T(8,128)(2,1)S(1)}, bf16[256,512]{1,0:T(8,128)(2,1)S(1)}, u32[]{:S(2)}, u32[]{:S(2)}) collective-permute-start(bf16[256,512]{1,0:T(8,128)(2,1)S(1)} %collective-permute-done.5.refs_3_), channel_id=1, source_target_pairs={{0,8},{1,9},{2,10},{3,11},{4,12},{5,13},{6,14},{7,15},{8,0},{9,1},... | collective-permute-start | bytes 786440 | tf_op jit(solution)/shard_map/ppermute | solution.py:378
  48.2 2.6 %collective-permute-start.9 = (bf16[256,512]{1,0:T(8,128)(2,1)S(1)}, bf16[256,512]{1,0:T(8,128)(2,1)S(1)}, u32[]{:S(2)}, u32[]{:S(2)}) collective-permute-start(bf16[256,512]{1,0:T(8,128)(2,1)S(1)} %collective-permute-done.8.refs_0_), channel_id=1, source_target_pairs={{0,8},{1,9},{2,10},{3,11},{4,12},{5,13},{6,14},{7,15},{8,0},{9,1},... | collective-permute-start | bytes 786440 | tf_op jit(solution)/shard_map/ppermute | solution.py:378
  49.7 1.5 %collective-permute-start.13 = (bf16[256,512]{1,0:T(8,128)(2,1)S(1)}, bf16[256,512]{1,0:T(8,128)(2,1)S(1)}, u32[]{:S(2)}, u32[]{:S(2)}) collective-permute-start(bf16[256,512]{1,0:T(8,128)(2,1)S(1)} %collective-permute-done.10.refs_2_), channel_id=1, source_target_pairs={{0,8},{1,9},{2,10},{3,11},{4,12},{5,13},{6,14},{7,15},{8,0},{9,1},... | collective-permute-start | bytes 786440 | tf_op jit(solution)/shard_map/ppermute | solution.py:378
  49.7 19.2 %copy-start.5 = (f32[1024]{0:T(1024)S(1)}, f32[1024]{0:T(1024)}, u32[]{:S(2)}) copy-start(f32[1024]{0:T(1024)} %param.15) | copy-start | bytes 12292
  49.7 25.3 %slice-start = ((s8[6291456]{0:T(1024)(128)(4,1)}), s8[4194304]{0:T(1024)(128)(4,1)S(1)}, s32[]{:S(2)}) async-start(s8[6291456]{0:T(1024)(128)(4,1)} %bitcast.16), calls=%async_computation | async-start | bytes 8388608
  50.8 24.2 %slice-start.1 = ((s8[6291456]{0:T(1024)(128)(4,1)}), s8[2097152]{0:T(1024)(128)(4,1)S(1)}, s32[]{:S(2)}) async-start(s8[6291456]{0:T(1024)(128)(4,1)} %bitcast.16), calls=%async_computation.1 | async-start | bytes 4194304
  52.3 41.6 %copy-start = (bf16[1,1536,1024]{2,1,0:T(8,128)(2,1)S(1)}, bf16[1,1536,1024]{2,1,0:T(8,128)(2,1)}, u32[]{:S(2)}) copy-start(bf16[1,1536,1024]{2,1,0:T(8,128)(2,1)} %param.19) | copy-start | bytes 9437188
  53.9 14.9 %collective-permute-start.15 = (bf16[128,1024]{1,0:T(8,128)(2,1)S(1)}, bf16[128,1024]{1,0:T(8,128)(2,1)S(1)}, u32[]{:S(2)}, u32[]{:S(2)}) collective-permute-start(bf16[128,1024]{1,0:T(8,128)(2,1)S(1)} %get-tuple-element.73), channel_id=1, source_target_pairs={{0,4},{1,5},{2,6},{3,7},{4,0},{5,1},{6,2},{7,3},{8,12},{9,13},{10,... | collective-permute-start | bytes 786440 | tf_op jit(solution)/shard_map/ppermute | solution.py:378
  68.9 5.2 %collective-permute-start.18 = (bf16[32,1024]{1,0:T(8,128)(2,1)S(1)}, bf16[32,1024]{1,0:T(8,128)(2,1)S(1)}, u32[]{:S(2)}, u32[]{:S(2)}) collective-permute-start(bf16[32,1024]{1,0:T(8,128)(2,1)S(1)} %get-tuple-element.79), channel_id=1, source_target_pairs={{0,3},{1,2},{2,1},{3,0},{4,7},{5,6},{6,5},{7,4},{8,11},{9,10},{10,... | collective-permute-start | bytes 196616 | tf_op jit(solution)/shard_map/ppermute | solution.py:378
  69.0 5.2 %collective-permute-start.19 = (bf16[32,1024]{1,0:T(8,128)(2,1)S(1)}, bf16[32,1024]{1,0:T(8,128)(2,1)S(1)}, u32[]{:S(2)}, u32[]{:S(2)}) collective-permute-start(bf16[32,1024]{1,0:T(8,128)(2,1)S(1)} %get-tuple-element.80), channel_id=1, source_target_pairs={{0,2},{1,3},{2,0},{3,1},{4,6},{5,7},{6,4},{7,5},{8,10},{9,11},{10,... | collective-permute-start | bytes 196616 | tf_op jit(solution)/shard_map/ppermute | solution.py:378
  70.8 4.3 %collective-permute-start.20 = (bf16[32,1024]{1,0:T(8,128)(2,1)S(1)}, bf16[32,1024]{1,0:T(8,128)(2,1)S(1)}, u32[]{:S(2)}, u32[]{:S(2)}) collective-permute-start(bf16[32,1024]{1,0:T(8,128)(2,1)S(1)} %get-tuple-element.81), channel_id=1, source_target_pairs={{0,1},{1,0},{2,3},{3,2},{4,5},{5,4},{6,7},{7,6},{8,9},{9,8},{10,11... | collective-permute-start | bytes 196616 | tf_op jit(solution)/shard_map/ppermute | solution.py:378
  72.5 20.1 %collective-permute-start.16 = (bf16[208,1024]{1,0:T(8,128)(2,1)S(1)}, bf16[208,1024]{1,0:T(8,128)(2,1)S(1)}, u32[]{:S(2)}, u32[]{:S(2)}) collective-permute-start(bf16[208,1024]{1,0:T(8,128)(2,1)S(1)} %get-tuple-element.74), channel_id=1, source_target_pairs={{0,4},{1,5},{2,6},{3,7},{4,0},{5,1},{6,2},{7,3},{8,12},{9,13},{10,... | collective-permute-start | bytes 1277960 | tf_op jit(solution)/shard_map/ppermute | solution.py:378
  76.3 1.5 %collective-permute-start.21 = (bf16[32,3200]{1,0:T(8,128)(2,1)S(1)}, bf16[32,3200]{1,0:T(8,128)(2,1)S(1)}, u32[]{:S(2)}, u32[]{:S(2)}) collective-permute-start(bf16[32,3200]{1,0:T(8,128)(2,1)S(1)} %get-tuple-element.84), channel_id=1, source_target_pairs={{0,8},{1,9},{2,10},{3,11},{4,12},{5,13},{6,14},{7,15},{8,0},{9,1},... | collective-permute-start | bytes 614408 | tf_op jit(solution)/shard_map/ppermute | solution.py:378
  76.3 1.7 %collective-permute-start.22 = (bf16[32,3200]{1,0:T(8,128)(2,1)S(1)}, bf16[32,3200]{1,0:T(8,128)(2,1)S(1)}, u32[]{:S(2)}, u32[]{:S(2)}) collective-permute-start(bf16[32,3200]{1,0:T(8,128)(2,1)S(1)} %get-tuple-element.85), channel_id=1, source_target_pairs={{0,8},{1,9},{2,10},{3,11},{4,12},{5,13},{6,14},{7,15},{8,0},{9,1},... | collective-permute-start | bytes 614408 | tf_op jit(solution)/shard_map/ppermute | solution.py:378
  78.2 5.8 %collective-permute-start.23 = (bf16[16,3200]{1,0:T(8,128)(2,1)S(1)}, bf16[16,3200]{1,0:T(8,128)(2,1)S(1)}, u32[]{:S(2)}, u32[]{:S(2)}) collective-permute-start(bf16[16,3200]{1,0:T(8,128)(2,1)S(1)} %get-tuple-element.87), channel_id=1, source_target_pairs={{0,16},{1,17},{2,18},{3,19},{4,20},{5,21},{6,22},{7,23},{8,24},{9,... | collective-permute-start | bytes 307208 | tf_op jit(solution)/shard_map/ppermute | solution.py:378
  80.0 5.5 %collective-permute-start.24 = (bf16[16,3200]{1,0:T(8,128)(2,1)S(1)}, bf16[16,3200]{1,0:T(8,128)(2,1)S(1)}, u32[]{:S(2)}, u32[]{:S(2)}) collective-permute-start(bf16[16,3200]{1,0:T(8,128)(2,1)S(1)} %get-tuple-element.88), channel_id=1, source_target_pairs={{0,16},{1,17},{2,18},{3,19},{4,20},{5,21},{6,22},{7,23},{8,24},{9,... | collective-permute-start | bytes 307208 | tf_op jit(solution)/shard_map/ppermute | solution.py:378
  85.6 7.0 %collective-permute-start.26 = (bf16[32,1536]{1,0:T(8,128)(2,1)S(1)}, bf16[32,1536]{1,0:T(8,128)(2,1)S(1)}, u32[]{:S(2)}, u32[]{:S(2)}) collective-permute-start(bf16[32,1536]{1,0:T(8,128)(2,1)S(1)} %shard_map.111.refs_0_), channel_id=1, source_target_pairs={{0,16},{1,17},{2,18},{3,19},{4,20},{5,21},{6,22},{7,23},{8,24},{9,... | collective-permute-start | bytes 294920 | tf_op jit(solution)/shard_map/ppermute | solution.py:378
  87.4 5.2 %collective-permute-start.25 = (bf16[32,1536]{1,0:T(8,128)(2,1)S(1)}, bf16[32,1536]{1,0:T(8,128)(2,1)S(1)}, u32[]{:S(2)}, u32[]{:S(2)}) collective-permute-start(bf16[32,1536]{1,0:T(8,128)(2,1)S(1)} %shard_map.111.refs_0_), channel_id=1, source_target_pairs={{0,8},{1,9},{2,10},{3,11},{4,12},{5,13},{6,14},{7,15},{8,0},{9,1},... | collective-permute-start | bytes 294920 | tf_op jit(solution)/shard_map/ppermute | solution.py:378
  92.6 1.3 %collective-permute-start.27 = (bf16[32,1536]{1,0:T(8,128)(2,1)S(1)}, bf16[32,1536]{1,0:T(8,128)(2,1)S(1)}, u32[]{:S(2)}, u32[]{:S(2)}) collective-permute-start(bf16[32,1536]{1,0:T(8,128)(2,1)S(1)} %collective-permute-done.26.refs_2_), channel_id=1, source_target_pairs={{0,8},{1,9},{2,10},{3,11},{4,12},{5,13},{6,14},{7,15},{8,0},{9,1},... | collective-permute-start | bytes 294920 | tf_op jit(solution)/shard_map/ppermute | solution.py:378
  92.6 8.1 %collective-permute-start.17 = (bf16[48,1024]{1,0:T(8,128)(2,1)S(1)}, bf16[48,1024]{1,0:T(8,128)(2,1)S(1)}, u32[]{:S(2)}, u32[]{:S(2)}) collective-permute-start(bf16[48,1024]{1,0:T(8,128)(2,1)S(1)} %get-tuple-element.76), channel_id=1, source_target_pairs={{0,4},{1,5},{2,6},{3,7},{4,0},{5,1},{6,2},{7,3},{8,12},{9,13},{10,... | collective-permute-start | bytes 294920 | tf_op jit(solution)/shard_map/ppermute | solution.py:378
  94.5 7.5 %collective-permute-start.28 = (bf16[32,1024]{1,0:T(8,128)(2,1)S(1)}, bf16[32,1024]{1,0:T(8,128)(2,1)S(1)}, u32[]{:S(2)}, u32[]{:S(2)}) collective-permute-start(bf16[32,1024]{1,0:T(8,128)(2,1)S(1)} %get-tuple-element.90), channel_id=1, source_target_pairs={{0,3},{1,2},{2,1},{3,0},{4,7},{5,6},{6,5},{7,4},{8,11},{9,10},{10,... | collective-permute-start | bytes 196616 | tf_op jit(solution)/shard_map/ppermute | solution.py:378
  96.3 6.0 %collective-permute-start.29 = (bf16[32,1024]{1,0:T(8,128)(2,1)S(1)}, bf16[32,1024]{1,0:T(8,128)(2,1)S(1)}, u32[]{:S(2)}, u32[]{:S(2)}) collective-permute-start(bf16[32,1024]{1,0:T(8,128)(2,1)S(1)} %get-tuple-element.91), channel_id=1, source_target_pairs={{0,2},{1,3},{2,0},{3,1},{4,6},{5,7},{6,4},{7,5},{8,10},{9,11},{10,... | collective-permute-start | bytes 196616 | tf_op jit(solution)/shard_map/ppermute | solution.py:378
  96.5 5.7 %collective-permute-start.30 = (bf16[32,1024]{1,0:T(8,128)(2,1)S(1)}, bf16[32,1024]{1,0:T(8,128)(2,1)S(1)}, u32[]{:S(2)}, u32[]{:S(2)}) collective-permute-start(bf16[32,1024]{1,0:T(8,128)(2,1)S(1)} %get-tuple-element.92), channel_id=1, source_target_pairs={{0,1},{1,0},{2,3},{3,2},{4,5},{5,4},{6,7},{7,6},{8,9},{9,8},{10,11... | collective-permute-start | bytes 196616 | tf_op jit(solution)/shard_map/ppermute | solution.py:378
  102.3 8.8 %collective-permute-start.31 = (bf16[64,1024]{1,0:T(8,128)(2,1)S(1)}, bf16[64,1024]{1,0:T(8,128)(2,1)S(1)}, u32[]{:S(2)}, u32[]{:S(2)}) collective-permute-start(bf16[64,1024]{1,0:T(8,128)(2,1)S(1)} %shard_map.113), channel_id=1, source_target_pairs={{0,4},{1,5},{2,6},{3,7},{4,0},{5,1},{6,2},{7,3},{8,12},{9,13},{10,... | collective-permute-start | bytes 393224 | tf_op jit(solution)/shard_map/ppermute | solution.py:378

commit v13 on v12

--- a/solution.py
+++ b/solution.py
@@ -78,6 +78,15 @@
 
 def hops(E):
     return [*reversed(range(E // 2))]
+
+
+def all_hops(E):
+    far = [b for b in range(E) if b & PAIR]
+    near = [b for b in reversed(range(1, E)) if not b & PAIR]
+    order = []
+    for i, b in enumerate(far):
+        order += [b, *near[i : i + 1]]
+    return [*order, 0]
 
 
 def pack_kernel(C, qw, q_ref, new_ref, past_ref, *refs):
@@ -137,36 +146,37 @@
             out[at, h * HEAD_SIZE : (h + 1) * HEAD_SIZE] = (numerator / total).astype(BF16)
 
 
-def route_kernel(E, cap, routes_ref, gates_ref, *refs):
-    place_ref, gate_ref, line_s, gate_s = refs[2], refs[3], refs[-2], refs[-1]
-    for src, dst in zip(refs[:2], refs[4:6]):
+def route_kernel(E, cap, routes_ref, other_ref, gates_ref, *refs):
+    line_s, gate_s = refs[-2:]
+    for src, dst in zip(refs[:2], refs[5:7]):
         dst[...] = src[...]
-    e = lax.axis_index("exp")
     blocks, _, tok = routes_ref.shape
     rows = blocks * tok
-    for i in range(blocks):
-        routes = routes_ref[i]
-        resident = routes < E
-        target = jnp.sum(jnp.where(resident, routes + 1, 0), axis=0, keepdims=True) - 1
-        gate = jnp.sum(jnp.where(resident, gates_ref[i], 0.0), axis=0, keepdims=True)
-        line_s[:, i * tok : (i + 1) * tok] = jnp.broadcast_to(target, (8, tok))
-        gate_s[:, i * tok : (i + 1) * tok] = jnp.broadcast_to(gate, (128, tok))
-    target = line_s[:1, :]
-    gate_ref[...] = gate_s[...].T
-    has = target >= 0
-    experts = lax.broadcasted_iota(jnp.int32, (E, rows), 0)
-    one_hot = jnp.where(target == experts, 1.0, 0.0)
     earlier = jnp.where(
         lax.broadcasted_iota(jnp.int32, (rows, rows), 0)
         < lax.broadcasted_iota(jnp.int32, (rows, rows), 1),
         1.0,
         0.0,
     ).astype(BF16)
-    rank = jnp.sum(dot(one_hot.astype(BF16), earlier) * one_hot, axis=0, keepdims=True)
-    slot = jnp.bitwise_xor(target, e) * cap + rank.astype(jnp.int32)
-    slot = jnp.where(has, slot, -1)
-    places = lax.broadcasted_iota(jnp.int32, (E * cap, rows), 0)
-    place_ref[...] = jnp.where(slot == places, 1.0, 0.0).astype(BF16)
+    for t, ref in enumerate((routes_ref, other_ref)):
+        for i in range(blocks):
+            routes = ref[i]
+            resident = routes < E
+            target = jnp.sum(jnp.where(resident, routes + 1, 0), axis=0, keepdims=True) - 1
+            line_s[:, i * tok : (i + 1) * tok] = jnp.broadcast_to(target, (8, tok))
+            if t == 0:
+                gate = jnp.sum(jnp.where(resident, gates_ref[i], 0.0), axis=0, keepdims=True)
+                gate_s[:, i * tok : (i + 1) * tok] = jnp.broadcast_to(gate, (128, tok))
+        target = line_s[:1, :]
+        experts = lax.broadcasted_iota(jnp.int32, (E, rows), 0)
+        one_hot = jnp.where(target == experts, 1.0, 0.0)
+        rank = jnp.sum(dot(one_hot.astype(BF16), earlier) * one_hot, axis=0, keepdims=True)
+        own = jnp.bitwise_xor(lax.axis_index("exp"), PAIR * t)
+        slot = jnp.bitwise_xor(target, own) * cap + rank.astype(jnp.int32)
+        slot = jnp.where(target >= 0, slot, -1)
+        places = lax.broadcasted_iota(jnp.int32, (E * cap, rows), 0)
+        refs[2 + t][...] = jnp.where(slot == places, 1.0, 0.0).astype(BF16)
+    refs[4][...] = gate_s[...].T
 
 
 def project_kernel(C, with_residual, *refs):
@@ -198,7 +208,7 @@
 
 def last_kernel(E, cap, *refs):
     accs, lasts, ws, places = refs[:2], refs[2:4], refs[4:6], refs[6:8]
-    own_ref, first_ref, second_ref, keep_ref, send_ref = refs[8:]
+    own_ref, first_ref, second_ref, *outs = refs[8:]
     few = first_ref.shape[0]
     cut = ws[0].shape[1]
     for j, cols in enumerate((slice(0, cut), slice(cut, own_ref.shape[1]))):
@@ -210,36 +220,26 @@
             else:
                 first_ref[:, cols] = rounded[:few]
                 second_ref[:, cols] = rounded[few:]
-            picked = dot(places[t][...], rounded)
-            for d in range(E // 2):
-                near, far = spread(d) ^ (PAIR * t), spread(d) ^ PAIR ^ (PAIR * t)
-                at = (2 * d + t) * cap
-                keep_ref[at : at + cap, cols] = picked[near * cap : (near + 1) * cap]
-                at = (2 * d + 1 - t) * cap
-                send_ref[at : at + cap, cols] = picked[far * cap : (far + 1) * cap].astype(BF16)
-
-
-def outgoing_kernel(keep_ref, got_ref, gain_ref, *outs):
-    scaled = ((keep_ref[...] + got_ref[...].astype(F32)) * gain_ref[...]).astype(BF16)
-    count = outs[0].shape[0]
-    for d, out in enumerate(outs):
-        out[...] = scaled[d * count : (d + 1) * count]
+            picked = dot(places[t][...], rounded).astype(BF16)
+            for out, b in zip(outs, all_hops(E)):
+                at = (b ^ (PAIR * t)) * cap
+                out[t * cap : (t + 1) * cap, cols] = picked[at : at + cap]
 
 
 def gate_up_kernel(C, E, cap, order, *refs):
-    xs, gain_ref, w_ref, keep_ref, *sends, x_s, part_s = refs[: E // 2], *refs[E // 2 :]
+    xs, gain_ref, w_ref, keep_ref, *sends, x_s, part_s = refs[:E], *refs[E:]
     c = lax.axis_index("ctx")
     e = lax.axis_index("exp")
     own_rows = E * cap // C
     wide = w_ref.shape[1]
-    for x, d in zip(xs, hops(E)):
-        for t in range(2):
-            at = aligned(jnp.bitwise_xor(e, spread(d) ^ (PAIR * t)) * cap, cap)
-            x_s[pl.ds(at, cap), :] = x[t * cap : (t + 1) * cap, :]
-    plain = x_s[...].astype(F32) / gain_ref[...]
-    square = jnp.sum(plain * plain, axis=1, keepdims=True)
-    lane = lax.broadcasted_iota(jnp.int32, (E * cap, 128), 1)
-    part_s[:, wide:] = jnp.where(lane == 0, square, 0.0)
+    came = dict(zip(all_hops(E), xs))
+    for b in range(E):
+        at = aligned(jnp.bitwise_xor(e, b) * cap, cap)
+        total = came[b][:cap, :].astype(F32) + came[b ^ PAIR][cap:, :].astype(F32)
+        x_s[pl.ds(at, cap), :] = (total * gain_ref[...]).astype(BF16)
+        square = jnp.sum(total * total, axis=1, keepdims=True)
+        lane = lax.broadcasted_iota(jnp.int32, (cap, 128), 1)
+        part_s[pl.ds(at, cap), wide:] = jnp.where(lane == 0, square, 0.0)
     step = 512
     for j in range(wide // step):
         at = slice(j * step, (j + 1) * step)
@@ -411,26 +411,29 @@
             limit=16,
         )(*msgs)
 
-    other, own_msg = attend(1, got)
+    tokens_last = lambda x: jnp.transpose(x.reshape(C, tok, x.shape[3]), (0, 2, 1))
+    own_routes = tokens_last(routes)
+    other_routes = permute(after(own_routes, got[-2]), exp=PAIR)
+    other, own_msg = attend(1, [after(got[0], other_routes), *got[1:]])
     theirs = permute(other, exp=PAIR)
     (mine,) = attend(0, [after(got[0], other), *got[1:-1], own_msg])
     cut = width - max(width // 4, 128)
     near = after(shards[1], theirs)[:, cut:]
     for d in range(2, C, 2):
         shards[d + 1] = (
-            permute(after(shards[d], other)[:, :cut], exp=1),
+            permute(after(shards[d], mine)[:, :cut], exp=1),
             permute(near, exp=spread(d)),
         )
-    tokens_last = lambda x: jnp.transpose(x.reshape(C, tok, x.shape[3]), (0, 2, 1))
-    place, gate, *staged = call(
+    place, other_place, gate, *staged = call(
         functools.partial(route_kernel, E, cap),
-        [sds((slots, rows), BF16), sds((rows, 128), F32)]
+        [sds((slots, rows), BF16)] * 2
+        + [sds((rows, 128), F32)]
         + [sds((qw, width), BF16), sds((rows, width), BF16)],
-        4,
+        5,
         scratch=[pltpu.VMEM((8, rows), jnp.int32), pltpu.VMEM((128, rows), F32)],
         cost=(0, 2**14),
         limit=16,
-    )(tokens_last(after(routes, mine, *step)), tokens_last(after(gates, mine)), out_weight, res)
+    )(after(own_routes, mine, *step), other_routes, tokens_last(gates), out_weight, res)
     shards[0], res = staged
 
     def gather(x, before=lambda: ()):
@@ -454,32 +457,26 @@
             cost=(0, 2**14),
         )(*operands)
 
-    other_place = permute(after(place, theirs), exp=PAIR)
     mine_all = gather(mine)
     acc, last = project(mine_all, res)
     quarter = [shards[d][1] for d in range(3, C, 2)]
-    theirs_all = gather(after(theirs, place, shards[1]), lambda: (other_place, *quarter))
+    theirs_all = gather(after(theirs, place, shards[1]), lambda: quarter)
     acc_far, last_far = project(theirs_all)
     gain = norm_gain.reshape(1, width)
     few = rows * 13 // 16
-    own, first, second, keep, send = call(
+    own, first, second, *outgoing = call(
         functools.partial(last_kernel, E, cap),
         [
             sds((rows, width), F32),
             sds((few, width), BF16),
             sds((rows - few, width), BF16),
-            sds((slots, width), F32),
-            sds((slots, width), BF16),
-        ],
+        ]
+        + [sds((2 * cap, width), BF16)] * E,
         8,
         cost=(0, 2**14),
     )(acc, acc_far, last, last_far, *shards[C - 1], place, other_place)
-    received = permute(send, exp=PAIR)
-    outgoing = call(
-        outgoing_kernel, [sds((2 * cap, width), BF16)] * (E // 2), 3, cost=(0, 2**20)
-    )(keep, received, gain)
-    incoming = [permute(outgoing[d], exp=spread(d)) for d in hops(E)[:-1]] + [outgoing[0]]
-    first = permute(after(first, received), exp=PAIR)
+    incoming = [permute(x, exp=b) if b else x for x, b in zip(outgoing, all_hops(E))]
+    first = permute(after(first, incoming[all_hops(E).index(1)]), exp=PAIR)
     second = permute(after(second, first), exp=PAIR)
 
     order = [0]
@@ -490,7 +487,7 @@
     keep, *sends = call(
         functools.partial(gate_up_kernel, C, E, cap, order),
         [sds((slots // 2, wide + 128), F32)] + [sds((slots // 4, wide + 128), BF16)] * 2,
-        E // 2 + 2,
+        E + 2,
         scratch=[pltpu.VMEM((slots, width), BF16), pltpu.VMEM((slots, wide + 128), F32)],
         cost=(0, 2**10),
     )(*incoming, gain, w_gate_up.reshape(width, wide))

time: 112 us -> 115 us (1.027)
  starting transfers between devices: 33.1 us -> 45.8 us
  waiting for transfers between devices: 61.4 us -> 51.6 us
    ppermute x32 -> x35, starting transfers between devices: 33.1 us -> 45.8 us  [permute(): return lax.ppermute(x, ('ctx', 'exp'), pairs)]
    ppermute x32 -> x35, waiting for transfers between devices: 61.4 us -> 51.6 us  [permute(): return lax.ppermute(x, ('ctx', 'exp'), pairs)]
  transfers between devices with their start and end apart: 32 -> 35, of which waited for: 20 -> 19; matrix products, arithmetic and copies ran while one was open for 0% -> 0% of each run, Pallas kernels for 10% -> 9%
where the time goes in v13:
time: 115 us
  waiting for transfers between devices  51.6 us (45%)
  starting transfers between devices  45.8 us (40%)
  Pallas kernels  13.5 us (12%)
  local copies, waits for them, and re-layouts  3.83 us (3%)
    ppermute x35, waiting for transfers between devices, permute(): return lax.ppermute(x, ('ctx', 'exp'), pairs)  51.6 us
    ppermute x35, starting transfers between devices, permute(): return lax.ppermute(x, ('ctx', 'exp'), pairs)  45.8 us
    pallas_call x2, Pallas kernels, attend(): call(functools.partial(attend_kernel, C, t), [sds((rows, qw), BF16)] + [s...  4.63 us
    unnamed x16, local copies, waits for them, and re-layouts  3.73 us
  transfers between devices with their start and end apart: 35, of which 19 were waited for; matrix products, arithmetic and copies ran while one was open for 0% of the time, Pallas kernels for 9%

profile of v13, /device:TPU:0, one launch (start us, length us, event | category | flops | bytes accessed | tf_op | source)
XLA Modules:
  0.0 115.0 jit_solution(5586499419048793796)
XLA Ops:
  0.0 3.0 %collective-permute-start.4 = (bf16[512,1024]{1,0:T(8,128)(2,1)}, bf16[512,1024]{1,0:T(8,128)(2,1)S(1)}, u32[]{:S(2)}, u32[]{:S(2)}) collective-permute-start(bf16[512,1024]{1,0:T(8,128)(2,1)} %refs_0_.1), channel_id=1, source_target_pairs={{0,2},{1,3},{2,0},{3,1},{4,6},{5,7},{6,4},{7,5},{8,10},{9,11},{10,... | collective-permute-start | bytes 3145736 | tf_op jit(solution)/shard_map/ppermute | solution.py:378
  3.0 1.5 %collective-permute-start.8 = (bf16[512,1024]{1,0:T(8,128)(2,1)}, bf16[512,1024]{1,0:T(8,128)(2,1)S(1)}, u32[]{:S(2)}, u32[]{:S(2)}) collective-permute-start(bf16[512,1024]{1,0:T(8,128)(2,1)} %refs_0_.1), channel_id=1, source_target_pairs={{0,1},{1,0},{2,3},{3,2},{4,5},{5,4},{6,7},{7,6},{8,9},{9,8},{10,11... | collective-permute-start | bytes 3145736 | tf_op jit(solution)/shard_map/ppermute | solution.py:378
  4.5 1.4 %shard_map.100 = (bf16[64,2048]{1,0:T(8,128)(2,1)S(1)}, bf16[64,2048]{1,0:T(8,128)(2,1)S(1)}, bf16[64,2048]{1,0:T(8,128)(2,1)S(1)}, bf16[64,2048]{1,0:T(8,128)(2,1)S(1)}) custom-call(bf16[64,4096]{1,0:T(8,128)(2,1)} %bitcast.25, bf16[64,512]{1,0:T(8,128)(2,1)} %bitcast.26, bf16[64,512]{1,0:T(8,128)(2,1)} %bitcast.27), custom_call_target="tpu_custom_call" | custom-call | bytes 1048576 | tf_op jit(solution)/shard_map/pallas_call | solution.py:384
  6.0 1.6 %collective-permute-start = (bf16[64,2048]{1,0:T(8,128)(2,1)S(1)}, bf16[64,2048]{1,0:T(8,128)(2,1)S(1)}, u32[]{:S(2)}, u32[]{:S(2)}) collective-permute-start(bf16[64,2048]{1,0:T(8,128)(2,1)S(1)} %get-tuple-element.53), channel_id=1, source_target_pairs={{0,16},{1,17},{2,18},{3,19},{4,20},{5,21},{6,22},{7,23},{8,24},{9,... | collective-permute-start | bytes 786440 | tf_op jit(solution)/shard_map/ppermute | solution.py:378
  7.9 2.6 %collective-permute-start.2 = (s32[4,8,64]{2,1,0:T(8,128)}, s32[4,8,64]{2,1,0:T(8,128)S(1)}, u32[]{:S(2)}, u32[]{:S(2)}) collective-permute-start(s32[4,8,64]{2,1,0:T(8,128)} %bitcast.21), channel_id=1, source_target_pairs={{0,4},{1,5},{2,6},{3,7},{4,0},{5,1},{6,2},{7,3},{8,12},{9,13},{10,... | collective-permute-start | bytes 24584 | tf_op jit(solution)/shard_map/ppermute | solution.py:378
  10.5 4.7 %collective-permute-done.refs_0_ = bf16[64,2048]{1,0:T(8,128)(2,1)S(1)} collective-permute-done((bf16[64,2048]{1,0:T(8,128)(2,1)S(1)}, bf16[64,2048]{1,0:T(8,128)(2,1)S(1)}, u32[]{:S(2)}, u32[]{:S(2)}) %collective-permute-start) | collective-permute-done | bytes 262176 | tf_op jit(solution)/shard_map/ppermute | solution.py:378
  15.2 10.8 %collective-permute-done.2.other_ref = s32[4,8,64]{2,1,0:T(8,128)S(1)} collective-permute-done((s32[4,8,64]{2,1,0:T(8,128)}, s32[4,8,64]{2,1,0:T(8,128)S(1)}, u32[]{:S(2)}, u32[]{:S(2)}) %collective-permute-start.2) | collective-permute-done | bytes 8224 | tf_op jit(solution)/shard_map/ppermute | solution.py:378
  26.0 2.3 %shard_map.101 = (bf16[256,512]{1,0:T(8,128)(2,1)S(1)}, bf16[64,2048]{1,0:T(8,128)(2,1)S(1)}) custom-call(bf16[64,2048]{1,0:T(8,128)(2,1)S(1)} %collective-permute-done.refs_0_, bf16[64,2048]{1,0:T(8,128)(2,1)S(1)} %collective-permute-done.3.refs_1_, bf16[64,2048]{1,0:T(8,128)(2,1)S(1)} %collective-permute-done.1.refs_2_, ...), custom_call_target="tpu_custom_call" | custom-call | bytes 16384 | tf_op jit(solution)/shard_map/pallas_call | solution.py:405
  28.3 3.4 %collective-permute-start.9 = (bf16[256,512]{1,0:T(8,128)(2,1)S(1)}, bf16[256,512]{1,0:T(8,128)(2,1)S(1)}, u32[]{:S(2)}, u32[]{:S(2)}) collective-permute-start(bf16[256,512]{1,0:T(8,128)(2,1)S(1)} %get-tuple-element.59), channel_id=1, source_target_pairs={{0,4},{1,5},{2,6},{3,7},{4,0},{5,1},{6,2},{7,3},{8,12},{9,13},{10,... | collective-permute-start | bytes 786440 | tf_op jit(solution)/shard_map/ppermute | solution.py:378
  31.8 2.3 %shard_map.102.refs_1_ = bf16[256,512]{1,0:T(8,128)(2,1)S(1)} custom-call(bf16[64,2048]{1,0:T(8,128)(2,1)S(1)} %collective-permute-done.refs_0_, bf16[64,2048]{1,0:T(8,128)(2,1)S(1)} %collective-permute-done.3.refs_1_, bf16[64,2048]{1,0:T(8,128)(2,1)S(1)} %collective-permute-done.1.refs_2_, bf16[64,2048]{1,0:T(8,128)(2,1)S(1)} %get-tuple-element.61.refs_3_), custom_call_target="tpu_custom_call" | custom-call | bytes 16384 | tf_op jit(solution)/shard_map/pallas_call | solution.py:405
  34.2 1.6 %collective-permute-start.14 = (bf16[512,768]{1,0:T(8,128)(2,1)S(1)}, bf16[512,768]{1,0:T(8,128)(2,1)S(1)}, u32[]{:S(2)}, u32[]{:S(2)}) collective-permute-start(bf16[512,768]{1,0:T(8,128)(2,1)S(1)} %slice.7), channel_id=1, source_target_pairs={{0,1},{1,0},{2,3},{3,2},{4,5},{5,4},{6,7},{7,6},{8,9},{9,8},{10,11... | collective-permute-start | bytes 2359304 | tf_op jit(solution)/shard_map/ppermute | solution.py:378
  35.7 1.5 %collective-permute-start.6 = (bf16[256,512]{1,0:T(8,128)(2,1)S(1)}, bf16[256,512]{1,0:T(8,128)(2,1)S(1)}, u32[]{:S(2)}, u32[]{:S(2)}) collective-permute-start(bf16[256,512]{1,0:T(8,128)(2,1)S(1)} %shard_map.102.refs_1_), channel_id=1, source_target_pairs={{0,16},{1,17},{2,18},{3,19},{4,20},{5,21},{6,22},{7,23},{8,24},{9,... | collective-permute-start | bytes 786440 | tf_op jit(solution)/shard_map/ppermute | solution.py:378
  37.3 1.2 %copy-done.1 = bf16[512,1024]{1,0:T(8,128)(2,1)S(1)} copy-done((bf16[512,1024]{1,0:T(8,128)(2,1)S(1)}, bf16[512,1024]{1,0:T(8,128)(2,1)}, u32[]{:S(2)}) %copy-start.1) | copy-done | bytes 1048600
  38.5 1.0 copy-done.2
  39.5 0.7 copy-done.3
  40.2 0.7 copy-done.4
  41.3 1.3 %collective-permute-done.9.refs_0_ = bf16[256,512]{1,0:T(8,128)(2,1)S(1)} collective-permute-done((bf16[256,512]{1,0:T(8,128)(2,1)S(1)}, bf16[256,512]{1,0:T(8,128)(2,1)S(1)}, u32[]{:S(2)}, u32[]{:S(2)}) %collective-permute-start.9) | collective-permute-done | bytes 262176 | tf_op jit(solution)/shard_map/ppermute | solution.py:378
  42.5 1.5 %collective-permute-start.11 = (bf16[256,512]{1,0:T(8,128)(2,1)S(1)}, bf16[256,512]{1,0:T(8,128)(2,1)S(1)}, u32[]{:S(2)}, u32[]{:S(2)}) collective-permute-start(bf16[256,512]{1,0:T(8,128)(2,1)S(1)} %collective-permute-done.9.refs_0_), channel_id=1, source_target_pairs={{0,16},{1,17},{2,18},{3,19},{4,20},{5,21},{6,22},{7,23},{8,24},{9,... | collective-permute-start | bytes 786440 | tf_op jit(solution)/shard_map/ppermute | solution.py:378
  44.8 4.2 %collective-permute-done.11.refs_2_ = bf16[256,512]{1,0:T(8,128)(2,1)S(1)} collective-permute-done((bf16[256,512]{1,0:T(8,128)(2,1)S(1)}, bf16[256,512]{1,0:T(8,128)(2,1)S(1)}, u32[]{:S(2)}, u32[]{:S(2)}) %collective-permute-start.11) | collective-permute-done | bytes 262176 | tf_op jit(solution)/shard_map/ppermute | solution.py:378
  48.9 1.6 %collective-permute-done.12.refs_5_ = bf16[512,256]{1,0:T(8,128)(2,1)S(1)} collective-permute-done((bf16[512,256]{1,0:T(8,128)(2,1)S(1)}, bf16[512,256]{1,0:T(8,128)(2,1)S(1)}, u32[]{:S(2)}, u32[]{:S(2)}) %collective-permute-start.12) | collective-permute-done | bytes 262176 | tf_op jit(solution)/shard_map/ppermute | solution.py:378
  50.6 1.1 shard_map.104
  52.1 1.1 shard_map.105
  53.2 1.6 %shard_map.106 = (f32[256,1024]{1,0:T(8,128)S(1)}, bf16[208,1024]{1,0:T(8,128)(2,1)S(1)}, bf16[48,1024]{1,0:T(8,128)(2,1)S(1)}, bf16[32,1024]{1,0:T(8,128)(2,1)S...) custom-call(f32[256,1024]{1,0:T(8,128)S(1)} %get-tuple-element.65.re, ...), custom_call_target="tpu_custom_call" | custom-call | bytes 16384 | tf_op jit(solution)/shard_map/pallas_call | solution.py:467
  54.8 1.5 %collective-permute-start.15 = (bf16[32,1024]{1,0:T(8,128)(2,1)S(1)}, bf16[32,1024]{1,0:T(8,128)(2,1)S(1)}, u32[]{:S(2)}, u32[]{:S(2)}) collective-permute-start(bf16[32,1024]{1,0:T(8,128)(2,1)S(1)} %get-tuple-element.77), channel_id=1, source_target_pairs={{0,1},{1,0},{2,3},{3,2},{4,5},{5,4},{6,7},{7,6},{8,9},{9,8},{10,11... | collective-permute-start | bytes 196616 | tf_op jit(solution)/shard_map/ppermute | solution.py:378
  56.4 1.7 %collective-permute-start.18 = (bf16[32,1024]{1,0:T(8,128)(2,1)S(1)}, bf16[32,1024]{1,0:T(8,128)(2,1)S(1)}, u32[]{:S(2)}, u32[]{:S(2)}) collective-permute-start(bf16[32,1024]{1,0:T(8,128)(2,1)S(1)} %get-tuple-element.82), channel_id=1, source_target_pairs={{0,4},{1,5},{2,6},{3,7},{4,0},{5,1},{6,2},{7,3},{8,12},{9,13},{10,... | collective-permute-start | bytes 196616 | tf_op jit(solution)/shard_map/ppermute | solution.py:378
  58.1 1.7 %collective-permute-start.19 = (bf16[32,1024]{1,0:T(8,128)(2,1)S(1)}, bf16[32,1024]{1,0:T(8,128)(2,1)S(1)}, u32[]{:S(2)}, u32[]{:S(2)}) collective-permute-start(bf16[32,1024]{1,0:T(8,128)(2,1)S(1)} %get-tuple-element.83), channel_id=1, source_target_pairs={{0,3},{1,2},{2,1},{3,0},{4,7},{5,6},{6,5},{7,4},{8,11},{9,10},{10,... | collective-permute-start | bytes 196616 | tf_op jit(solution)/shard_map/ppermute | solution.py:378
  59.8 0.9 collective-permute-start.20
  60.7 1.5 %collective-permute-start.21 = (bf16[32,1024]{1,0:T(8,128)(2,1)S(1)}, bf16[32,1024]{1,0:T(8,128)(2,1)S(1)}, u32[]{:S(2)}, u32[]{:S(2)}) collective-permute-start(bf16[32,1024]{1,0:T(8,128)(2,1)S(1)} %get-tuple-element.85), channel_id=1, source_target_pairs={{0,2},{1,3},{2,0},{3,1},{4,6},{5,7},{6,4},{7,5},{8,10},{9,11},{10,... | collective-permute-start | bytes 196616 | tf_op jit(solution)/shard_map/ppermute | solution.py:378
  62.2 2.9 %collective-permute-start.22 = (bf16[32,1024]{1,0:T(8,128)(2,1)S(1)}, bf16[32,1024]{1,0:T(8,128)(2,1)S(1)}, u32[]{:S(2)}, u32[]{:S(2)}) collective-permute-start(bf16[32,1024]{1,0:T(8,128)(2,1)S(1)} %get-tuple-element.86), channel_id=1, source_target_pairs={{0,6},{1,7},{2,4},{3,5},{4,2},{5,3},{6,0},{7,1},{8,14},{9,15},{10,... | collective-permute-start | bytes 196616 | tf_op jit(solution)/shard_map/ppermute | solution.py:378
  65.1 1.3 %collective-permute-start.23 = (bf16[32,1024]{1,0:T(8,128)(2,1)S(1)}, bf16[32,1024]{1,0:T(8,128)(2,1)S(1)}, u32[]{:S(2)}, u32[]{:S(2)}) collective-permute-start(bf16[32,1024]{1,0:T(8,128)(2,1)S(1)} %get-tuple-element.87), channel_id=1, source_target_pairs={{0,7},{1,6},{2,5},{3,4},{4,3},{5,2},{6,1},{7,0},{8,15},{9,14},{10,... | collective-permute-start | bytes 196616 | tf_op jit(solution)/shard_map/ppermute | solution.py:378
  66.4 2.2 %collective-permute-done.20.refs_2_ = bf16[32,1024]{1,0:T(8,128)(2,1)S(1)} collective-permute-done((bf16[32,1024]{1,0:T(8,128)(2,1)S(1)}, bf16[32,1024]{1,0:T(8,128)(2,1)S(1)}, u32[]{:S(2)}, u32[]{:S(2)}) %collective-permute-start.20) | collective-permute-done | bytes 65568 | tf_op jit(solution)/shard_map/ppermute | solution.py:378
  68.8 4.1 %collective-permute-done.23.refs_6_ = bf16[32,1024]{1,0:T(8,128)(2,1)S(1)} collective-permute-done((bf16[32,1024]{1,0:T(8,128)(2,1)S(1)}, bf16[32,1024]{1,0:T(8,128)(2,1)S(1)}, u32[]{:S(2)}, u32[]{:S(2)}) %collective-permute-start.23) | collective-permute-done | bytes 65568 | tf_op jit(solution)/shard_map/ppermute | solution.py:378
  72.9 1.3 %shard_map.108 = (f32[64,3200]{1,0:T(8,128)S(1)}, bf16[32,3200]{1,0:T(8,128)(2,1)S(1)}, bf16[32,3200]{1,0:T(8,128)(2,1)S(1)}) custom-call(bf16[32,1024]{1,0:T(8,128)(2,1)S(1)} %collective-permute-done.18.refs_0_, bf16[32,1024]{1,0:T(8,128)(2,1)S(1)} %collective-permute-done.19.refs_1_, bf16[32,1024]{1,0:T(8,128)(2,1)S(1)} %collective-permute-done.20.refs_2_, ...), custom_call_target="tpu_custom_call" | custom-call | bytes 1024 | tf_op jit(solution)/shard_map/pallas_call | solution.py:487
  74.7 0.9 collective-permute-done.24.refs_0_
  76.7 1.5 %collective-permute-start.27 = (bf16[16,3200]{1,0:T(8,128)(2,1)S(1)}, bf16[16,3200]{1,0:T(8,128)(2,1)S(1)}, u32[]{:S(2)}, u32[]{:S(2)}) collective-permute-start(bf16[16,3200]{1,0:T(8,128)(2,1)S(1)} %get-tuple-element.94), channel_id=1, source_target_pairs={{0,16},{1,17},{2,18},{3,19},{4,20},{5,21},{6,22},{7,23},{8,24},{9,... | collective-permute-start | bytes 307208 | tf_op jit(solution)/shard_map/ppermute | solution.py:378
  78.2 3.7 %collective-permute-done.26.refs_0_ = bf16[16,3200]{1,0:T(8,128)(2,1)S(1)} collective-permute-done((bf16[16,3200]{1,0:T(8,128)(2,1)S(1)}, bf16[16,3200]{1,0:T(8,128)(2,1)S(1)}, u32[]{:S(2)}, u32[]{:S(2)}) %collective-permute-start.26) | collective-permute-done | bytes 102432 | tf_op jit(solution)/shard_map/ppermute | solution.py:378
  81.8 1.5 %collective-permute-done.27.refs_1_ = bf16[16,3200]{1,0:T(8,128)(2,1)S(1)} collective-permute-done((bf16[16,3200]{1,0:T(8,128)(2,1)S(1)}, bf16[16,3200]{1,0:T(8,128)(2,1)S(1)}, u32[]{:S(2)}, u32[]{:S(2)}) %collective-permute-start.27) | collective-permute-done | bytes 102432 | tf_op jit(solution)/shard_map/ppermute | solution.py:378
  83.5 0.6 collective-permute-start.29
  84.1 4.1 %collective-permute-done.29.refs_2_ = bf16[32,1536]{1,0:T(8,128)(2,1)S(1)} collective-permute-done((bf16[32,1536]{1,0:T(8,128)(2,1)S(1)}, bf16[32,1536]{1,0:T(8,128)(2,1)S(1)}, u32[]{:S(2)}, u32[]{:S(2)}) %collective-permute-start.29) | collective-permute-done | bytes 98336 | tf_op jit(solution)/shard_map/ppermute | solution.py:378
  88.2 1.8 %collective-permute-done.16.first = bf16[208,1024]{1,0:T(8,128)(2,1)S(1)} collective-permute-done((bf16[208,1024]{1,0:T(8,128)(2,1)S(1)}, bf16[208,1024]{1,0:T(8,128)(2,1)S(1)}, u32[]{:S(2)}, u32[]{:S(2)}) %collective-permute-start.16) | collective-permute-done | bytes 426016 | tf_op jit(solution)/shard_map/ppermute | solution.py:378
  89.9 7.6 %collective-permute-start.17 = (bf16[48,1024]{1,0:T(8,128)(2,1)S(1)}, bf16[48,1024]{1,0:T(8,128)(2,1)S(1)}, u32[]{:S(2)}, u32[]{:S(2)}) collective-permute-start(bf16[48,1024]{1,0:T(8,128)(2,1)S(1)} %get-tuple-element.80), channel_id=1, source_target_pairs={{0,4},{1,5},{2,6},{3,7},{4,0},{5,1},{6,2},{7,3},{8,12},{9,13},{10,... | collective-permute-start | bytes 294920 | tf_op jit(solution)/shard_map/ppermute | solution.py:378
  97.5 0.7 shard_map.111
  98.2 2.5 %collective-permute-start.31 = (bf16[32,1024]{1,0:T(8,128)(2,1)S(1)}, bf16[32,1024]{1,0:T(8,128)(2,1)S(1)}, u32[]{:S(2)}, u32[]{:S(2)}) collective-permute-start(bf16[32,1024]{1,0:T(8,128)(2,1)S(1)} %get-tuple-element.96), channel_id=1, source_target_pairs={{0,3},{1,2},{2,1},{3,0},{4,7},{5,6},{6,5},{7,4},{8,11},{9,10},{10,... | collective-permute-start | bytes 196616 | tf_op jit(solution)/shard_map/ppermute | solution.py:378
  101.8 2.0 %collective-permute-done.31.refs_0_ = bf16[32,1024]{1,0:T(8,128)(2,1)S(1)} collective-permute-done((bf16[32,1024]{1,0:T(8,128)(2,1)S(1)}, bf16[32,1024]{1,0:T(8,128)(2,1)S(1)}, u32[]{:S(2)}, u32[]{:S(2)}) %collective-permute-start.31) | collective-permute-done | bytes 65568 | tf_op jit(solution)/shard_map/ppermute | solution.py:378
  103.8 1.3 %collective-permute-done.32.refs_1_ = bf16[32,1024]{1,0:T(8,128)(2,1)S(1)} collective-permute-done((bf16[32,1024]{1,0:T(8,128)(2,1)S(1)}, bf16[32,1024]{1,0:T(8,128)(2,1)S(1)}, u32[]{:S(2)}, u32[]{:S(2)}) %collective-permute-start.32) | collective-permute-done | bytes 65568 | tf_op jit(solution)/shard_map/ppermute | solution.py:378
  105.4 2.1 %collective-permute-start.34 = (bf16[64,1024]{1,0:T(8,128)(2,1)S(1)}, bf16[64,1024]{1,0:T(8,128)(2,1)S(1)}, u32[]{:S(2)}, u32[]{:S(2)}) collective-permute-start(bf16[64,1024]{1,0:T(8,128)(2,1)S(1)} %shard_map.112), channel_id=1, source_target_pairs={{0,4},{1,5},{2,6},{3,7},{4,0},{5,1},{6,2},{7,3},{8,12},{9,13},{10,... | collective-permute-start | bytes 393224 | tf_op jit(solution)/shard_map/ppermute | solution.py:378
  107.7 6.3 %collective-permute-done.34.refs_4_ = bf16[64,1024]{1,0:T(8,128)(2,1)S(1)} collective-permute-done((bf16[64,1024]{1,0:T(8,128)(2,1)S(1)}, bf16[64,1024]{1,0:T(8,128)(2,1)S(1)}, u32[]{:S(2)}, u32[]{:S(2)}) %collective-permute-start.34) | collective-permute-done | bytes 131104 | tf_op jit(solution)/shard_map/ppermute | solution.py:378
  113.9 1.1 shard_map.113
  (55 shorter events, 5.2 us)
Async XLA Ops:
  0.0 34.1 %collective-permute-start.4 = (bf16[512,1024]{1,0:T(8,128)(2,1)}, bf16[512,1024]{1,0:T(8,128)(2,1)S(1)}, u32[]{:S(2)}, u32[]{:S(2)}) collective-permute-start(bf16[512,1024]{1,0:T(8,128)(2,1)} %refs_0_.1), channel_id=1, source_target_pairs={{0,2},{1,3},{2,0},{3,1},{4,6},{5,7},{6,4},{7,5},{8,10},{9,11},{10,... | collective-permute-start | bytes 3145736 | tf_op jit(solution)/shard_map/ppermute | solution.py:378
  3.0 39.5 %collective-permute-start.8 = (bf16[512,1024]{1,0:T(8,128)(2,1)}, bf16[512,1024]{1,0:T(8,128)(2,1)S(1)}, u32[]{:S(2)}, u32[]{:S(2)}) collective-permute-start(bf16[512,1024]{1,0:T(8,128)(2,1)} %refs_0_.1), channel_id=1, source_target_pairs={{0,1},{1,0},{2,3},{3,2},{4,5},{5,4},{6,7},{7,6},{8,9},{9,8},{10,11... | collective-permute-start | bytes 3145736 | tf_op jit(solution)/shard_map/ppermute | solution.py:378
  6.0 1.9 %collective-permute-start.1 = (bf16[64,2048]{1,0:T(8,128)(2,1)S(1)}, bf16[64,2048]{1,0:T(8,128)(2,1)S(1)}, u32[]{:S(2)}, u32[]{:S(2)}) collective-permute-start(bf16[64,2048]{1,0:T(8,128)(2,1)S(1)} %get-tuple-element.54), channel_id=1, source_target_pairs={{0,8},{1,9},{2,10},{3,11},{4,12},{5,13},{6,14},{7,15},{8,0},{9,1},... | collective-permute-start | bytes 786440 | tf_op jit(solution)/shard_map/ppermute | solution.py:378
  6.0 9.2 %collective-permute-start = (bf16[64,2048]{1,0:T(8,128)(2,1)S(1)}, bf16[64,2048]{1,0:T(8,128)(2,1)S(1)}, u32[]{:S(2)}, u32[]{:S(2)}) collective-permute-start(bf16[64,2048]{1,0:T(8,128)(2,1)S(1)} %get-tuple-element.53), channel_id=1, source_target_pairs={{0,16},{1,17},{2,18},{3,19},{4,20},{5,21},{6,22},{7,23},{8,24},{9,... | collective-permute-start | bytes 786440 | tf_op jit(solution)/shard_map/ppermute | solution.py:378
  7.6 18.4 %collective-permute-start.3 = (bf16[64,2048]{1,0:T(8,128)(2,1)S(1)}, bf16[64,2048]{1,0:T(8,128)(2,1)S(1)}, u32[]{:S(2)}, u32[]{:S(2)}) collective-permute-start(bf16[64,2048]{1,0:T(8,128)(2,1)S(1)} %get-tuple-element.57), channel_id=1, source_target_pairs={{0,24},{1,25},{2,26},{3,27},{4,28},{5,29},{6,30},{7,31},{8,16},{9,... | collective-permute-start | bytes 786440 | tf_op jit(solution)/shard_map/ppermute | solution.py:378
  7.9 18.1 %collective-permute-start.2 = (s32[4,8,64]{2,1,0:T(8,128)}, s32[4,8,64]{2,1,0:T(8,128)S(1)}, u32[]{:S(2)}, u32[]{:S(2)}) collective-permute-start(s32[4,8,64]{2,1,0:T(8,128)} %bitcast.21), channel_id=1, source_target_pairs={{0,4},{1,5},{2,6},{3,7},{4,0},{5,1},{6,2},{7,3},{8,12},{9,13},{10,... | collective-permute-start | bytes 24584 | tf_op jit(solution)/shard_map/ppermute | solution.py:378
  28.3 14.2 %collective-permute-start.9 = (bf16[256,512]{1,0:T(8,128)(2,1)S(1)}, bf16[256,512]{1,0:T(8,128)(2,1)S(1)}, u32[]{:S(2)}, u32[]{:S(2)}) collective-permute-start(bf16[256,512]{1,0:T(8,128)(2,1)S(1)} %get-tuple-element.59), channel_id=1, source_target_pairs={{0,4},{1,5},{2,6},{3,7},{4,0},{5,1},{6,2},{7,3},{8,12},{9,13},{10,... | collective-permute-start | bytes 786440 | tf_op jit(solution)/shard_map/ppermute | solution.py:378
  34.2 19.0 %collective-permute-start.14 = (bf16[512,768]{1,0:T(8,128)(2,1)S(1)}, bf16[512,768]{1,0:T(8,128)(2,1)S(1)}, u32[]{:S(2)}, u32[]{:S(2)}) collective-permute-start(bf16[512,768]{1,0:T(8,128)(2,1)S(1)} %slice.7), channel_id=1, source_target_pairs={{0,1},{1,0},{2,3},{3,2},{4,5},{5,4},{6,7},{7,6},{8,9},{9,8},{10,11... | collective-permute-start | bytes 2359304 | tf_op jit(solution)/shard_map/ppermute | solution.py:378
  35.7 8.5 %collective-permute-start.6 = (bf16[256,512]{1,0:T(8,128)(2,1)S(1)}, bf16[256,512]{1,0:T(8,128)(2,1)S(1)}, u32[]{:S(2)}, u32[]{:S(2)}) collective-permute-start(bf16[256,512]{1,0:T(8,128)(2,1)S(1)} %shard_map.102.refs_1_), channel_id=1, source_target_pairs={{0,16},{1,17},{2,18},{3,19},{4,20},{5,21},{6,22},{7,23},{8,24},{9,... | collective-permute-start | bytes 786440 | tf_op jit(solution)/shard_map/ppermute | solution.py:378
  37.3 1.2 %copy-start.1 = (bf16[512,1024]{1,0:T(8,128)(2,1)S(1)}, bf16[512,1024]{1,0:T(8,128)(2,1)}, u32[]{:S(2)}) copy-start(bf16[512,1024]{1,0:T(8,128)(2,1)} %refs_0_.1) | copy-start | bytes 3145732
  38.5 1.0 copy-start.2
  39.5 0.7 copy-start.3
  40.2 0.7 copy-start.4
  42.5 6.4 %collective-permute-start.11 = (bf16[256,512]{1,0:T(8,128)(2,1)S(1)}, bf16[256,512]{1,0:T(8,128)(2,1)S(1)}, u32[]{:S(2)}, u32[]{:S(2)}) collective-permute-start(bf16[256,512]{1,0:T(8,128)(2,1)S(1)} %collective-permute-done.9.refs_0_), channel_id=1, source_target_pairs={{0,16},{1,17},{2,18},{3,19},{4,20},{5,21},{6,22},{7,23},{8,24},{9,... | collective-permute-start | bytes 786440 | tf_op jit(solution)/shard_map/ppermute | solution.py:378
  44.1 6.4 %collective-permute-start.12 = (bf16[512,256]{1,0:T(8,128)(2,1)S(1)}, bf16[512,256]{1,0:T(8,128)(2,1)S(1)}, u32[]{:S(2)}, u32[]{:S(2)}) collective-permute-start(bf16[512,256]{1,0:T(8,128)(2,1)S(1)} %slice.6), channel_id=1, source_target_pairs={{0,2},{1,3},{2,0},{3,1},{4,6},{5,7},{6,4},{7,5},{8,10},{9,11},{10,... | collective-permute-start | bytes 786440 | tf_op jit(solution)/shard_map/ppermute | solution.py:378
  44.2 6.4 %collective-permute-start.5 = (bf16[256,512]{1,0:T(8,128)(2,1)S(1)}, bf16[256,512]{1,0:T(8,128)(2,1)S(1)}, u32[]{:S(2)}, u32[]{:S(2)}) collective-permute-start(bf16[256,512]{1,0:T(8,128)(2,1)S(1)} %shard_map.102.refs_1_), channel_id=1, source_target_pairs={{0,8},{1,9},{2,10},{3,11},{4,12},{5,13},{6,14},{7,15},{8,0},{9,1},... | collective-permute-start | bytes 786440 | tf_op jit(solution)/shard_map/ppermute | solution.py:378
  44.3 6.3 %collective-permute-start.7 = (bf16[256,512]{1,0:T(8,128)(2,1)S(1)}, bf16[256,512]{1,0:T(8,128)(2,1)S(1)}, u32[]{:S(2)}, u32[]{:S(2)}) collective-permute-start(bf16[256,512]{1,0:T(8,128)(2,1)S(1)} %collective-permute-done.6.refs_3_), channel_id=1, source_target_pairs={{0,8},{1,9},{2,10},{3,11},{4,12},{5,13},{6,14},{7,15},{8,0},{9,1},... | collective-permute-start | bytes 786440 | tf_op jit(solution)/shard_map/ppermute | solution.py:378
  48.9 2.8 %collective-permute-start.10 = (bf16[256,512]{1,0:T(8,128)(2,1)S(1)}, bf16[256,512]{1,0:T(8,128)(2,1)S(1)}, u32[]{:S(2)}, u32[]{:S(2)}) collective-permute-start(bf16[256,512]{1,0:T(8,128)(2,1)S(1)} %collective-permute-done.9.refs_0_), channel_id=1, source_target_pairs={{0,8},{1,9},{2,10},{3,11},{4,12},{5,13},{6,14},{7,15},{8,0},{9,1},... | collective-permute-start | bytes 786440 | tf_op jit(solution)/shard_map/ppermute | solution.py:378
  50.5 1.5 %collective-permute-start.13 = (bf16[256,512]{1,0:T(8,128)(2,1)S(1)}, bf16[256,512]{1,0:T(8,128)(2,1)S(1)}, u32[]{:S(2)}, u32[]{:S(2)}) collective-permute-start(bf16[256,512]{1,0:T(8,128)(2,1)S(1)} %collective-permute-done.11.refs_2_), channel_id=1, source_target_pairs={{0,8},{1,9},{2,10},{3,11},{4,12},{5,13},{6,14},{7,15},{8,0},{9,1},... | collective-permute-start | bytes 786440 | tf_op jit(solution)/shard_map/ppermute | solution.py:378
  50.6 22.4 %slice-start = ((s8[6291456]{0:T(1024)(128)(4,1)}), s8[4194304]{0:T(1024)(128)(4,1)S(1)}, s32[]{:S(2)}) async-start(s8[6291456]{0:T(1024)(128)(4,1)} %bitcast.16), calls=%async_computation | async-start | bytes 8388608
  50.6 22.3 %copy-start.5 = (f32[1024]{0:T(1024)S(1)}, f32[1024]{0:T(1024)}, u32[]{:S(2)}) copy-start(f32[1024]{0:T(1024)} %param.15) | copy-start | bytes 12292
  51.7 21.3 %slice-start.1 = ((s8[6291456]{0:T(1024)(128)(4,1)}), s8[2097152]{0:T(1024)(128)(4,1)S(1)}, s32[]{:S(2)}) async-start(s8[6291456]{0:T(1024)(128)(4,1)} %bitcast.16), calls=%async_computation.1 | async-start | bytes 4194304
  53.2 44.4 %copy-start = (bf16[1,1536,1024]{2,1,0:T(8,128)(2,1)S(1)}, bf16[1,1536,1024]{2,1,0:T(8,128)(2,1)}, u32[]{:S(2)}) copy-start(bf16[1,1536,1024]{2,1,0:T(8,128)(2,1)} %param.19) | copy-start | bytes 9437188
  54.8 7.4 %collective-permute-start.15 = (bf16[32,1024]{1,0:T(8,128)(2,1)S(1)}, bf16[32,1024]{1,0:T(8,128)(2,1)S(1)}, u32[]{:S(2)}, u32[]{:S(2)}) collective-permute-start(bf16[32,1024]{1,0:T(8,128)(2,1)S(1)} %get-tuple-element.77), channel_id=1, source_target_pairs={{0,1},{1,0},{2,3},{3,2},{4,5},{5,4},{6,7},{7,6},{8,9},{9,8},{10,11... | collective-permute-start | bytes 196616 | tf_op jit(solution)/shard_map/ppermute | solution.py:378
  56.4 8.8 %collective-permute-start.18 = (bf16[32,1024]{1,0:T(8,128)(2,1)S(1)}, bf16[32,1024]{1,0:T(8,128)(2,1)S(1)}, u32[]{:S(2)}, u32[]{:S(2)}) collective-permute-start(bf16[32,1024]{1,0:T(8,128)(2,1)S(1)} %get-tuple-element.82), channel_id=1, source_target_pairs={{0,4},{1,5},{2,6},{3,7},{4,0},{5,1},{6,2},{7,3},{8,12},{9,13},{10,... | collective-permute-start | bytes 196616 | tf_op jit(solution)/shard_map/ppermute | solution.py:378
  58.1 8.3 %collective-permute-start.19 = (bf16[32,1024]{1,0:T(8,128)(2,1)S(1)}, bf16[32,1024]{1,0:T(8,128)(2,1)S(1)}, u32[]{:S(2)}, u32[]{:S(2)}) collective-permute-start(bf16[32,1024]{1,0:T(8,128)(2,1)S(1)} %get-tuple-element.83), channel_id=1, source_target_pairs={{0,3},{1,2},{2,1},{3,0},{4,7},{5,6},{6,5},{7,4},{8,11},{9,10},{10,... | collective-permute-start | bytes 196616 | tf_op jit(solution)/shard_map/ppermute | solution.py:378
  59.8 8.8 %collective-permute-start.20 = (bf16[32,1024]{1,0:T(8,128)(2,1)S(1)}, bf16[32,1024]{1,0:T(8,128)(2,1)S(1)}, u32[]{:S(2)}, u32[]{:S(2)}) collective-permute-start(bf16[32,1024]{1,0:T(8,128)(2,1)S(1)} %get-tuple-element.84), channel_id=1, source_target_pairs={{0,5},{1,4},{2,7},{3,6},{4,1},{5,0},{6,3},{7,2},{8,13},{9,12},{10,... | collective-permute-start | bytes 196616 | tf_op jit(solution)/shard_map/ppermute | solution.py:378
  60.7 7.9 %collective-permute-start.21 = (bf16[32,1024]{1,0:T(8,128)(2,1)S(1)}, bf16[32,1024]{1,0:T(8,128)(2,1)S(1)}, u32[]{:S(2)}, u32[]{:S(2)}) collective-permute-start(bf16[32,1024]{1,0:T(8,128)(2,1)S(1)} %get-tuple-element.85), channel_id=1, source_target_pairs={{0,2},{1,3},{2,0},{3,1},{4,6},{5,7},{6,4},{7,5},{8,10},{9,11},{10,... | collective-permute-start | bytes 196616 | tf_op jit(solution)/shard_map/ppermute | solution.py:378
  62.2 6.6 %collective-permute-start.22 = (bf16[32,1024]{1,0:T(8,128)(2,1)S(1)}, bf16[32,1024]{1,0:T(8,128)(2,1)S(1)}, u32[]{:S(2)}, u32[]{:S(2)}) collective-permute-start(bf16[32,1024]{1,0:T(8,128)(2,1)S(1)} %get-tuple-element.86), channel_id=1, source_target_pairs={{0,6},{1,7},{2,4},{3,5},{4,2},{5,3},{6,0},{7,1},{8,14},{9,15},{10,... | collective-permute-start | bytes 196616 | tf_op jit(solution)/shard_map/ppermute | solution.py:378
  65.1 7.8 %collective-permute-start.23 = (bf16[32,1024]{1,0:T(8,128)(2,1)S(1)}, bf16[32,1024]{1,0:T(8,128)(2,1)S(1)}, u32[]{:S(2)}, u32[]{:S(2)}) collective-permute-start(bf16[32,1024]{1,0:T(8,128)(2,1)S(1)} %get-tuple-element.87), channel_id=1, source_target_pairs={{0,7},{1,6},{2,5},{3,4},{4,3},{5,2},{6,1},{7,0},{8,15},{9,14},{10,... | collective-permute-start | bytes 196616 | tf_op jit(solution)/shard_map/ppermute | solution.py:378
  66.4 23.5 %collective-permute-start.16 = (bf16[208,1024]{1,0:T(8,128)(2,1)S(1)}, bf16[208,1024]{1,0:T(8,128)(2,1)S(1)}, u32[]{:S(2)}, u32[]{:S(2)}) collective-permute-start(bf16[208,1024]{1,0:T(8,128)(2,1)S(1)} %get-tuple-element.78), channel_id=1, source_target_pairs={{0,4},{1,5},{2,6},{3,7},{4,0},{5,1},{6,2},{7,3},{8,12},{9,13},{10,... | collective-permute-start | bytes 1277960 | tf_op jit(solution)/shard_map/ppermute | solution.py:378
  74.2 1.5 %collective-permute-start.24 = (bf16[32,3200]{1,0:T(8,128)(2,1)S(1)}, bf16[32,3200]{1,0:T(8,128)(2,1)S(1)}, u32[]{:S(2)}, u32[]{:S(2)}) collective-permute-start(bf16[32,3200]{1,0:T(8,128)(2,1)S(1)} %get-tuple-element.90), channel_id=1, source_target_pairs={{0,8},{1,9},{2,10},{3,11},{4,12},{5,13},{6,14},{7,15},{8,0},{9,1},... | collective-permute-start | bytes 614408 | tf_op jit(solution)/shard_map/ppermute | solution.py:378
  74.2 1.7 %collective-permute-start.25 = (bf16[32,3200]{1,0:T(8,128)(2,1)S(1)}, bf16[32,3200]{1,0:T(8,128)(2,1)S(1)}, u32[]{:S(2)}, u32[]{:S(2)}) collective-permute-start(bf16[32,3200]{1,0:T(8,128)(2,1)S(1)} %get-tuple-element.91), channel_id=1, source_target_pairs={{0,8},{1,9},{2,10},{3,11},{4,12},{5,13},{6,14},{7,15},{8,0},{9,1},... | collective-permute-start | bytes 614408 | tf_op jit(solution)/shard_map/ppermute | solution.py:378
  76.1 5.8 %collective-permute-start.26 = (bf16[16,3200]{1,0:T(8,128)(2,1)S(1)}, bf16[16,3200]{1,0:T(8,128)(2,1)S(1)}, u32[]{:S(2)}, u32[]{:S(2)}) collective-permute-start(bf16[16,3200]{1,0:T(8,128)(2,1)S(1)} %get-tuple-element.93), channel_id=1, source_target_pairs={{0,16},{1,17},{2,18},{3,19},{4,20},{5,21},{6,22},{7,23},{8,24},{9,... | collective-permute-start | bytes 307208 | tf_op jit(solution)/shard_map/ppermute | solution.py:378
  76.7 6.7 %collective-permute-start.27 = (bf16[16,3200]{1,0:T(8,128)(2,1)S(1)}, bf16[16,3200]{1,0:T(8,128)(2,1)S(1)}, u32[]{:S(2)}, u32[]{:S(2)}) collective-permute-start(bf16[16,3200]{1,0:T(8,128)(2,1)S(1)} %get-tuple-element.94), channel_id=1, source_target_pairs={{0,16},{1,17},{2,18},{3,19},{4,20},{5,21},{6,22},{7,23},{8,24},{9,... | collective-permute-start | bytes 307208 | tf_op jit(solution)/shard_map/ppermute | solution.py:378
  83.5 4.7 %collective-permute-start.29 = (bf16[32,1536]{1,0:T(8,128)(2,1)S(1)}, bf16[32,1536]{1,0:T(8,128)(2,1)S(1)}, u32[]{:S(2)}, u32[]{:S(2)}) collective-permute-start(bf16[32,1536]{1,0:T(8,128)(2,1)S(1)} %shard_map.110.refs_0_), channel_id=1, source_target_pairs={{0,16},{1,17},{2,18},{3,19},{4,20},{5,21},{6,22},{7,23},{8,24},{9,... | collective-permute-start | bytes 294920 | tf_op jit(solution)/shard_map/ppermute | solution.py:378
  84.1 13.4 %collective-permute-start.28 = (bf16[32,1536]{1,0:T(8,128)(2,1)S(1)}, bf16[32,1536]{1,0:T(8,128)(2,1)S(1)}, u32[]{:S(2)}, u32[]{:S(2)}) collective-permute-start(bf16[32,1536]{1,0:T(8,128)(2,1)S(1)} %shard_map.110.refs_0_), channel_id=1, source_target_pairs={{0,8},{1,9},{2,10},{3,11},{4,12},{5,13},{6,14},{7,15},{8,0},{9,1},... | collective-permute-start | bytes 294920 | tf_op jit(solution)/shard_map/ppermute | solution.py:378
  89.9 7.6 %collective-permute-start.30 = (bf16[32,1536]{1,0:T(8,128)(2,1)S(1)}, bf16[32,1536]{1,0:T(8,128)(2,1)S(1)}, u32[]{:S(2)}, u32[]{:S(2)}) collective-permute-start(bf16[32,1536]{1,0:T(8,128)(2,1)S(1)} %collective-permute-done.29.refs_2_), channel_id=1, source_target_pairs={{0,8},{1,9},{2,10},{3,11},{4,12},{5,13},{6,14},{7,15},{8,0},{9,1},... | collective-permute-start | bytes 294920 | tf_op jit(solution)/shard_map/ppermute | solution.py:378
  89.9 11.8 %collective-permute-start.17 = (bf16[48,1024]{1,0:T(8,128)(2,1)S(1)}, bf16[48,1024]{1,0:T(8,128)(2,1)S(1)}, u32[]{:S(2)}, u32[]{:S(2)}) collective-permute-start(bf16[48,1024]{1,0:T(8,128)(2,1)S(1)} %get-tuple-element.80), channel_id=1, source_target_pairs={{0,4},{1,5},{2,6},{3,7},{4,0},{5,1},{6,2},{7,3},{8,12},{9,13},{10,... | collective-permute-start | bytes 294920 | tf_op jit(solution)/shard_map/ppermute | solution.py:378
  98.2 5.6 %collective-permute-start.31 = (bf16[32,1024]{1,0:T(8,128)(2,1)S(1)}, bf16[32,1024]{1,0:T(8,128)(2,1)S(1)}, u32[]{:S(2)}, u32[]{:S(2)}) collective-permute-start(bf16[32,1024]{1,0:T(8,128)(2,1)S(1)} %get-tuple-element.96), channel_id=1, source_target_pairs={{0,3},{1,2},{2,1},{3,0},{4,7},{5,6},{6,5},{7,4},{8,11},{9,10},{10,... | collective-permute-start | bytes 196616 | tf_op jit(solution)/shard_map/ppermute | solution.py:378
  100.7 4.3 %collective-permute-start.32 = (bf16[32,1024]{1,0:T(8,128)(2,1)S(1)}, bf16[32,1024]{1,0:T(8,128)(2,1)S(1)}, u32[]{:S(2)}, u32[]{:S(2)}) collective-permute-start(bf16[32,1024]{1,0:T(8,128)(2,1)S(1)} %get-tuple-element.97), channel_id=1, source_target_pairs={{0,2},{1,3},{2,0},{3,1},{4,6},{5,7},{6,4},{7,5},{8,10},{9,11},{10,... | collective-permute-start | bytes 196616 | tf_op jit(solution)/shard_map/ppermute | solution.py:378
  101.2 4.3 %collective-permute-start.33 = (bf16[32,1024]{1,0:T(8,128)(2,1)S(1)}, bf16[32,1024]{1,0:T(8,128)(2,1)S(1)}, u32[]{:S(2)}, u32[]{:S(2)}) collective-permute-start(bf16[32,1024]{1,0:T(8,128)(2,1)S(1)} %get-tuple-element.98), channel_id=1, source_target_pairs={{0,1},{1,0},{2,3},{3,2},{4,5},{5,4},{6,7},{7,6},{8,9},{9,8},{10,11... | collective-permute-start | bytes 196616 | tf_op jit(solution)/shard_map/ppermute | solution.py:378
  105.4 8.5 %collective-permute-start.34 = (bf16[64,1024]{1,0:T(8,128)(2,1)S(1)}, bf16[64,1024]{1,0:T(8,128)(2,1)S(1)}, u32[]{:S(2)}, u32[]{:S(2)}) collective-permute-start(bf16[64,1024]{1,0:T(8,128)(2,1)S(1)} %shard_map.112), channel_id=1, source_target_pairs={{0,4},{1,5},{2,6},{3,7},{4,0},{5,1},{6,2},{7,3},{8,12},{9,13},{10,... | collective-permute-start | bytes 393224 | tf_op jit(solution)/shard_map/ppermute | solution.py:378

commit v14 on v13

--- a/solution.py
+++ b/solution.py
@@ -413,8 +413,8 @@
 
     tokens_last = lambda x: jnp.transpose(x.reshape(C, tok, x.shape[3]), (0, 2, 1))
     own_routes = tokens_last(routes)
-    other_routes = permute(after(own_routes, got[-2]), exp=PAIR)
-    other, own_msg = attend(1, [after(got[0], other_routes), *got[1:]])
+    other_routes = permute(after(own_routes, *got), exp=PAIR)
+    other, own_msg = attend(1, got)
     theirs = permute(other, exp=PAIR)
     (mine,) = attend(0, [after(got[0], other), *got[1:-1], own_msg])
     cut = width - max(width // 4, 128)
@@ -463,7 +463,7 @@
     theirs_all = gather(after(theirs, place, shards[1]), lambda: quarter)
     acc_far, last_far = project(theirs_all)
     gain = norm_gain.reshape(1, width)
-    few = rows * 13 // 16
+    few = rows * 5 // 8
     own, first, second, *outgoing = call(
         functools.partial(last_kernel, E, cap),
         [
@@ -476,7 +476,7 @@
         cost=(0, 2**14),
     )(acc, acc_far, last, last_far, *shards[C - 1], place, other_place)
     incoming = [permute(x, exp=b) if b else x for x, b in zip(outgoing, all_hops(E))]
-    first = permute(after(first, incoming[all_hops(E).index(1)]), exp=PAIR)
+    first = permute(after(first, *incoming), exp=PAIR)
     second = permute(after(second, first), exp=PAIR)
 
     order = [0]

time: 115 us -> 111 us (0.965)
  starting transfers between devices: 45.8 us -> 36.9 us
  waiting for transfers between devices: 51.6 us -> 56.3 us
    ppermute x35, starting transfers between devices: 45.8 us -> 36.9 us  [permute(): return lax.ppermute(x, ('ctx', 'exp'), pairs)]
    ppermute x35, waiting for transfers between devices: 51.6 us -> 56.3 us  [permute(): return lax.ppermute(x, ('ctx', 'exp'), pairs)]
where the time goes in v14:
time: 111 us
  waiting for transfers between devices  56.3 us (51%)
  starting transfers between devices  36.9 us (33%)
  Pallas kernels  13.5 us (12%)
  local copies, waits for them, and re-layouts  3.83 us (3%)
    ppermute x35, waiting for transfers between devices, permute(): return lax.ppermute(x, ('ctx', 'exp'), pairs)  56.3 us
    ppermute x35, starting transfers between devices, permute(): return lax.ppermute(x, ('ctx', 'exp'), pairs)  36.9 us
    pallas_call x2, Pallas kernels, attend(): call(functools.partial(attend_kernel, C, t), [sds((rows, qw), BF16)] + [s...  4.63 us
    unnamed x16, local copies, waits for them, and re-layouts  3.73 us
  transfers between devices with their start and end apart: 35, of which 19 were waited for; matrix products, arithmetic and copies ran while one was open for 0% of the time, Pallas kernels for 9%

profile of v14, /device:TPU:0, one launch (start us, length us, event | category | flops | bytes accessed | tf_op | source)
XLA Modules:
  0.0 110.7 jit_solution(6159666243138886516)
XLA Ops:
  0.0 3.0 %collective-permute-start.3 = (bf16[512,1024]{1,0:T(8,128)(2,1)}, bf16[512,1024]{1,0:T(8,128)(2,1)S(1)}, u32[]{:S(2)}, u32[]{:S(2)}) collective-permute-start(bf16[512,1024]{1,0:T(8,128)(2,1)} %refs_0_.1), channel_id=1, source_target_pairs={{0,2},{1,3},{2,0},{3,1},{4,6},{5,7},{6,4},{7,5},{8,10},{9,11},{10,... | collective-permute-start | bytes 3145736 | tf_op jit(solution)/shard_map/ppermute | solution.py:378
  3.0 1.5 %collective-permute-start.8 = (bf16[512,1024]{1,0:T(8,128)(2,1)}, bf16[512,1024]{1,0:T(8,128)(2,1)S(1)}, u32[]{:S(2)}, u32[]{:S(2)}) collective-permute-start(bf16[512,1024]{1,0:T(8,128)(2,1)} %refs_0_.1), channel_id=1, source_target_pairs={{0,1},{1,0},{2,3},{3,2},{4,5},{5,4},{6,7},{7,6},{8,9},{9,8},{10,11... | collective-permute-start | bytes 3145736 | tf_op jit(solution)/shard_map/ppermute | solution.py:378
  4.5 1.4 %shard_map.100 = (bf16[64,2048]{1,0:T(8,128)(2,1)S(1)}, bf16[64,2048]{1,0:T(8,128)(2,1)S(1)}, bf16[64,2048]{1,0:T(8,128)(2,1)S(1)}, bf16[64,2048]{1,0:T(8,128)(2,1)S(1)}) custom-call(bf16[64,4096]{1,0:T(8,128)(2,1)} %bitcast.25, bf16[64,512]{1,0:T(8,128)(2,1)} %bitcast.26, bf16[64,512]{1,0:T(8,128)(2,1)} %bitcast.27), custom_call_target="tpu_custom_call" | custom-call | bytes 1048576 | tf_op jit(solution)/shard_map/pallas_call | solution.py:384
  6.0 1.6 %collective-permute-start = (bf16[64,2048]{1,0:T(8,128)(2,1)S(1)}, bf16[64,2048]{1,0:T(8,128)(2,1)S(1)}, u32[]{:S(2)}, u32[]{:S(2)}) collective-permute-start(bf16[64,2048]{1,0:T(8,128)(2,1)S(1)} %get-tuple-element.52), channel_id=1, source_target_pairs={{0,16},{1,17},{2,18},{3,19},{4,20},{5,21},{6,22},{7,23},{8,24},{9,... | collective-permute-start | bytes 786440 | tf_op jit(solution)/shard_map/ppermute | solution.py:378
  8.2 7.1 %collective-permute-done.refs_0_ = bf16[64,2048]{1,0:T(8,128)(2,1)S(1)} collective-permute-done((bf16[64,2048]{1,0:T(8,128)(2,1)S(1)}, bf16[64,2048]{1,0:T(8,128)(2,1)S(1)}, u32[]{:S(2)}, u32[]{:S(2)}) %collective-permute-start) | collective-permute-done | bytes 262176 | tf_op jit(solution)/shard_map/ppermute | solution.py:378
  15.3 2.9 %collective-permute-done.1.refs_1_ = bf16[64,2048]{1,0:T(8,128)(2,1)S(1)} collective-permute-done((bf16[64,2048]{1,0:T(8,128)(2,1)S(1)}, bf16[64,2048]{1,0:T(8,128)(2,1)S(1)}, u32[]{:S(2)}, u32[]{:S(2)}) %collective-permute-start.1) | collective-permute-done | bytes 262176 | tf_op jit(solution)/shard_map/ppermute | solution.py:378
  18.2 2.3 %shard_map.101 = (bf16[256,512]{1,0:T(8,128)(2,1)S(1)}, bf16[64,2048]{1,0:T(8,128)(2,1)S(1)}) custom-call(bf16[64,2048]{1,0:T(8,128)(2,1)S(1)} %collective-permute-done.refs_0_, bf16[64,2048]{1,0:T(8,128)(2,1)S(1)} %collective-permute-done.1.refs_1_, bf16[64,2048]{1,0:T(8,128)(2,1)S(1)} %collective-permute-done.2.refs_2_, ...), custom_call_target="tpu_custom_call" | custom-call | bytes 16384 | tf_op jit(solution)/shard_map/pallas_call | solution.py:405
  20.5 2.7 %collective-permute-start.9 = (bf16[256,512]{1,0:T(8,128)(2,1)S(1)}, bf16[256,512]{1,0:T(8,128)(2,1)S(1)}, u32[]{:S(2)}, u32[]{:S(2)}) collective-permute-start(bf16[256,512]{1,0:T(8,128)(2,1)S(1)} %get-tuple-element.56), channel_id=1, source_target_pairs={{0,4},{1,5},{2,6},{3,7},{4,0},{5,1},{6,2},{7,3},{8,12},{9,13},{10,... | collective-permute-start | bytes 786440 | tf_op jit(solution)/shard_map/ppermute | solution.py:378
  23.2 2.3 %shard_map.102.refs_1_ = bf16[256,512]{1,0:T(8,128)(2,1)S(1)} custom-call(bf16[64,2048]{1,0:T(8,128)(2,1)S(1)} %collective-permute-done.refs_0_, bf16[64,2048]{1,0:T(8,128)(2,1)S(1)} %collective-permute-done.1.refs_1_, bf16[64,2048]{1,0:T(8,128)(2,1)S(1)} %collective-permute-done.2.refs_2_, bf16[64,2048]{1,0:T(8,128)(2,1)S(1)} %get-tuple-element.58.refs_3_), custom_call_target="tpu_custom_call" | custom-call | bytes 16384 | tf_op jit(solution)/shard_map/pallas_call | solution.py:405
  25.5 4.5 %collective-permute-done.3.refs_7_.refs_6_ = bf16[512,1024]{1,0:T(8,128)(2,1)S(1)} collective-permute-done((bf16[512,1024]{1,0:T(8,128)(2,1)}, bf16[512,1024]{1,0:T(8,128)(2,1)S(1)}, u32[]{:S(2)}, u32[]{:S(2)}) %collective-permute-start.3) | collective-permute-done | bytes 1048608 | tf_op jit(solution)/shard_map/ppermute | solution.py:378
  30.1 2.7 %collective-permute-start.14 = (bf16[512,768]{1,0:T(8,128)(2,1)S(1)}, bf16[512,768]{1,0:T(8,128)(2,1)S(1)}, u32[]{:S(2)}, u32[]{:S(2)}) collective-permute-start(bf16[512,768]{1,0:T(8,128)(2,1)S(1)} %slice.7), channel_id=1, source_target_pairs={{0,1},{1,0},{2,3},{3,2},{4,5},{5,4},{6,7},{7,6},{8,9},{9,8},{10,11... | collective-permute-start | bytes 2359304 | tf_op jit(solution)/shard_map/ppermute | solution.py:378
  32.8 0.7 collective-permute-start.4
  33.4 2.3 %collective-permute-start.6 = (bf16[256,512]{1,0:T(8,128)(2,1)S(1)}, bf16[256,512]{1,0:T(8,128)(2,1)S(1)}, u32[]{:S(2)}, u32[]{:S(2)}) collective-permute-start(bf16[256,512]{1,0:T(8,128)(2,1)S(1)} %shard_map.102.refs_1_), channel_id=1, source_target_pairs={{0,16},{1,17},{2,18},{3,19},{4,20},{5,21},{6,22},{7,23},{8,24},{9,... | collective-permute-start | bytes 786440 | tf_op jit(solution)/shard_map/ppermute | solution.py:378
  35.7 1.9 %collective-permute-done.4.other_ref = s32[4,8,64]{2,1,0:T(8,128)S(1)} collective-permute-done((s32[4,8,64]{2,1,0:T(8,128)}, s32[4,8,64]{2,1,0:T(8,128)S(1)}, u32[]{:S(2)}, u32[]{:S(2)}) %collective-permute-start.4) | collective-permute-done | bytes 8224 | tf_op jit(solution)/shard_map/ppermute | solution.py:378
  37.6 1.2 %copy-done.1 = bf16[512,1024]{1,0:T(8,128)(2,1)S(1)} copy-done((bf16[512,1024]{1,0:T(8,128)(2,1)S(1)}, bf16[512,1024]{1,0:T(8,128)(2,1)}, u32[]{:S(2)}) %copy-start.1) | copy-done | bytes 1048600
  38.8 1.0 copy-done.2
  39.9 0.7 copy-done.3
  40.6 0.7 copy-done.4
  41.6 2.4 %collective-permute-start.11 = (bf16[256,512]{1,0:T(8,128)(2,1)S(1)}, bf16[256,512]{1,0:T(8,128)(2,1)S(1)}, u32[]{:S(2)}, u32[]{:S(2)}) collective-permute-start(bf16[256,512]{1,0:T(8,128)(2,1)S(1)} %collective-permute-done.9.refs_0_), channel_id=1, source_target_pairs={{0,16},{1,17},{2,18},{3,19},{4,20},{5,21},{6,22},{7,23},{8,24},{9,... | collective-permute-start | bytes 786440 | tf_op jit(solution)/shard_map/ppermute | solution.py:378
  44.8 4.1 %collective-permute-done.11.refs_2_ = bf16[256,512]{1,0:T(8,128)(2,1)S(1)} collective-permute-done((bf16[256,512]{1,0:T(8,128)(2,1)S(1)}, bf16[256,512]{1,0:T(8,128)(2,1)S(1)}, u32[]{:S(2)}, u32[]{:S(2)}) %collective-permute-start.11) | collective-permute-done | bytes 262176 | tf_op jit(solution)/shard_map/ppermute | solution.py:378
  48.8 1.7 %collective-permute-done.12.refs_5_ = bf16[512,256]{1,0:T(8,128)(2,1)S(1)} collective-permute-done((bf16[512,256]{1,0:T(8,128)(2,1)S(1)}, bf16[512,256]{1,0:T(8,128)(2,1)S(1)}, u32[]{:S(2)}, u32[]{:S(2)}) %collective-permute-start.12) | collective-permute-done | bytes 262176 | tf_op jit(solution)/shard_map/ppermute | solution.py:378
  50.5 1.1 shard_map.104
  52.0 1.1 shard_map.105
  53.1 1.6 %shard_map.106 = (f32[256,1024]{1,0:T(8,128)S(1)}, bf16[160,1024]{1,0:T(8,128)(2,1)S(1)}, bf16[96,1024]{1,0:T(8,128)(2,1)S(1)}, bf16[32,1024]{1,0:T(8,128)(2,1)S...) custom-call(f32[256,1024]{1,0:T(8,128)S(1)} %get-tuple-element.63.re, ...), custom_call_target="tpu_custom_call" | custom-call | bytes 16384 | tf_op jit(solution)/shard_map/pallas_call | solution.py:467
  54.8 1.1 collective-permute-start.15
  55.9 1.5 %collective-permute-start.16 = (bf16[32,1024]{1,0:T(8,128)(2,1)S(1)}, bf16[32,1024]{1,0:T(8,128)(2,1)S(1)}, u32[]{:S(2)}, u32[]{:S(2)}) collective-permute-start(bf16[32,1024]{1,0:T(8,128)(2,1)S(1)} %get-tuple-element.76), channel_id=1, source_target_pairs={{0,3},{1,2},{2,1},{3,0},{4,7},{5,6},{6,5},{7,4},{8,11},{9,10},{10,... | collective-permute-start | bytes 196616 | tf_op jit(solution)/shard_map/ppermute | solution.py:378
  57.4 1.5 %collective-permute-start.17 = (bf16[32,1024]{1,0:T(8,128)(2,1)S(1)}, bf16[32,1024]{1,0:T(8,128)(2,1)S(1)}, u32[]{:S(2)}, u32[]{:S(2)}) collective-permute-start(bf16[32,1024]{1,0:T(8,128)(2,1)S(1)} %get-tuple-element.77), channel_id=1, source_target_pairs={{0,5},{1,4},{2,7},{3,6},{4,1},{5,0},{6,3},{7,2},{8,13},{9,12},{10,... | collective-permute-start | bytes 196616 | tf_op jit(solution)/shard_map/ppermute | solution.py:378
  58.8 1.8 %collective-permute-start.18 = (bf16[32,1024]{1,0:T(8,128)(2,1)S(1)}, bf16[32,1024]{1,0:T(8,128)(2,1)S(1)}, u32[]{:S(2)}, u32[]{:S(2)}) collective-permute-start(bf16[32,1024]{1,0:T(8,128)(2,1)S(1)} %get-tuple-element.78), channel_id=1, source_target_pairs={{0,2},{1,3},{2,0},{3,1},{4,6},{5,7},{6,4},{7,5},{8,10},{9,11},{10,... | collective-permute-start | bytes 196616 | tf_op jit(solution)/shard_map/ppermute | solution.py:378
  60.7 2.5 %collective-permute-start.19 = (bf16[32,1024]{1,0:T(8,128)(2,1)S(1)}, bf16[32,1024]{1,0:T(8,128)(2,1)S(1)}, u32[]{:S(2)}, u32[]{:S(2)}) collective-permute-start(bf16[32,1024]{1,0:T(8,128)(2,1)S(1)} %get-tuple-element.79), channel_id=1, source_target_pairs={{0,6},{1,7},{2,4},{3,5},{4,2},{5,3},{6,0},{7,1},{8,14},{9,15},{10,... | collective-permute-start | bytes 196616 | tf_op jit(solution)/shard_map/ppermute | solution.py:378
  63.2 2.7 %collective-permute-start.21 = (bf16[32,1024]{1,0:T(8,128)(2,1)S(1)}, bf16[32,1024]{1,0:T(8,128)(2,1)S(1)}, u32[]{:S(2)}, u32[]{:S(2)}) collective-permute-start(bf16[32,1024]{1,0:T(8,128)(2,1)S(1)} %get-tuple-element.81), channel_id=1, source_target_pairs={{0,7},{1,6},{2,5},{3,4},{4,3},{5,2},{6,1},{7,0},{8,15},{9,14},{10,... | collective-permute-start | bytes 196616 | tf_op jit(solution)/shard_map/ppermute | solution.py:378
  66.0 0.9 collective-permute-done.19.refs_4_
  67.4 2.8 %collective-permute-done.21.refs_6_ = bf16[32,1024]{1,0:T(8,128)(2,1)S(1)} collective-permute-done((bf16[32,1024]{1,0:T(8,128)(2,1)S(1)}, bf16[32,1024]{1,0:T(8,128)(2,1)S(1)}, u32[]{:S(2)}, u32[]{:S(2)}) %collective-permute-start.21) | collective-permute-done | bytes 65568 | tf_op jit(solution)/shard_map/ppermute | solution.py:378
  70.2 1.3 %shard_map.108 = (f32[64,3200]{1,0:T(8,128)S(1)}, bf16[32,3200]{1,0:T(8,128)(2,1)S(1)}, bf16[32,3200]{1,0:T(8,128)(2,1)S(1)}) custom-call(bf16[32,1024]{1,0:T(8,128)(2,1)S(1)} %collective-permute-done.15.refs_0_, bf16[32,1024]{1,0:T(8,128)(2,1)S(1)} %collective-permute-done.16.refs_1_, bf16[32,1024]{1,0:T(8,128)(2,1)S(1)} %collective-permute-done.17.refs_2_, ...), custom_call_target="tpu_custom_call" | custom-call | bytes 1024 | tf_op jit(solution)/shard_map/pallas_call | solution.py:487
  72.0 0.9 collective-permute-done.24.refs_0_
  73.4 0.9 collective-permute-start.26
  74.2 1.2 %collective-permute-start.27 = (bf16[16,3200]{1,0:T(8,128)(2,1)S(1)}, bf16[16,3200]{1,0:T(8,128)(2,1)S(1)}, u32[]{:S(2)}, u32[]{:S(2)}) collective-permute-start(bf16[16,3200]{1,0:T(8,128)(2,1)S(1)} %get-tuple-element.92), channel_id=1, source_target_pairs={{0,16},{1,17},{2,18},{3,19},{4,20},{5,21},{6,22},{7,23},{8,24},{9,... | collective-permute-start | bytes 307208 | tf_op jit(solution)/shard_map/ppermute | solution.py:378
  75.4 3.7 %collective-permute-done.26.refs_0_ = bf16[16,3200]{1,0:T(8,128)(2,1)S(1)} collective-permute-done((bf16[16,3200]{1,0:T(8,128)(2,1)S(1)}, bf16[16,3200]{1,0:T(8,128)(2,1)S(1)}, u32[]{:S(2)}, u32[]{:S(2)}) %collective-permute-start.26) | collective-permute-done | bytes 102432 | tf_op jit(solution)/shard_map/ppermute | solution.py:378
  79.1 1.5 %collective-permute-done.27.refs_1_ = bf16[16,3200]{1,0:T(8,128)(2,1)S(1)} collective-permute-done((bf16[16,3200]{1,0:T(8,128)(2,1)S(1)}, bf16[16,3200]{1,0:T(8,128)(2,1)S(1)}, u32[]{:S(2)}, u32[]{:S(2)}) %collective-permute-start.27) | collective-permute-done | bytes 102432 | tf_op jit(solution)/shard_map/ppermute | solution.py:378
  80.8 0.9 collective-permute-start.29
  81.6 7.6 %collective-permute-done.22.first = bf16[160,1024]{1,0:T(8,128)(2,1)S(1)} collective-permute-done((bf16[160,1024]{1,0:T(8,128)(2,1)S(1)}, bf16[160,1024]{1,0:T(8,128)(2,1)S(1)}, u32[]{:S(2)}, u32[]{:S(2)}) %collective-permute-start.22) | collective-permute-done | bytes 327712 | tf_op jit(solution)/shard_map/ppermute | solution.py:378
  89.3 1.3 %collective-permute-done.30.refs_3_ = bf16[32,1536]{1,0:T(8,128)(2,1)S(1)} collective-permute-done((bf16[32,1536]{1,0:T(8,128)(2,1)S(1)}, bf16[32,1536]{1,0:T(8,128)(2,1)S(1)}, u32[]{:S(2)}, u32[]{:S(2)}) %collective-permute-start.30) | collective-permute-done | bytes 98336 | tf_op jit(solution)/shard_map/ppermute | solution.py:378
  90.6 0.7 shard_map.111
  91.2 2.3 %collective-permute-start.31 = (bf16[32,1024]{1,0:T(8,128)(2,1)S(1)}, bf16[32,1024]{1,0:T(8,128)(2,1)S(1)}, u32[]{:S(2)}, u32[]{:S(2)}) collective-permute-start(bf16[32,1024]{1,0:T(8,128)(2,1)S(1)} %get-tuple-element.94), channel_id=1, source_target_pairs={{0,3},{1,2},{2,1},{3,0},{4,7},{5,6},{6,5},{7,4},{8,11},{9,10},{10,... | collective-permute-start | bytes 196616 | tf_op jit(solution)/shard_map/ppermute | solution.py:378
  93.8 1.0 collective-permute-start.33
  94.8 5.9 %collective-permute-done.23.second = bf16[96,1024]{1,0:T(8,128)(2,1)S(1)} collective-permute-done((bf16[96,1024]{1,0:T(8,128)(2,1)S(1)}, bf16[96,1024]{1,0:T(8,128)(2,1)S(1)}, u32[]{:S(2)}, u32[]{:S(2)}) %collective-permute-start.23) | collective-permute-done | bytes 196640 | tf_op jit(solution)/shard_map/ppermute | solution.py:378
  100.7 0.9 collective-permute-done.32.refs_1_
  102.2 7.4 %collective-permute-done.34.refs_4_ = bf16[64,1024]{1,0:T(8,128)(2,1)S(1)} collective-permute-done((bf16[64,1024]{1,0:T(8,128)(2,1)S(1)}, bf16[64,1024]{1,0:T(8,128)(2,1)S(1)}, u32[]{:S(2)}, u32[]{:S(2)}) %collective-permute-start.34) | collective-permute-done | bytes 131104 | tf_op jit(solution)/shard_map/ppermute | solution.py:378
  109.6 1.1 shard_map.113
  (55 shorter events, 4.8 us)
Async XLA Ops:
  0.0 30.0 %collective-permute-start.3 = (bf16[512,1024]{1,0:T(8,128)(2,1)}, bf16[512,1024]{1,0:T(8,128)(2,1)S(1)}, u32[]{:S(2)}, u32[]{:S(2)}) collective-permute-start(bf16[512,1024]{1,0:T(8,128)(2,1)} %refs_0_.1), channel_id=1, source_target_pairs={{0,2},{1,3},{2,0},{3,1},{4,6},{5,7},{6,4},{7,5},{8,10},{9,11},{10,... | collective-permute-start | bytes 3145736 | tf_op jit(solution)/shard_map/ppermute | solution.py:378
  3.0 38.6 %collective-permute-start.8 = (bf16[512,1024]{1,0:T(8,128)(2,1)}, bf16[512,1024]{1,0:T(8,128)(2,1)S(1)}, u32[]{:S(2)}, u32[]{:S(2)}) collective-permute-start(bf16[512,1024]{1,0:T(8,128)(2,1)} %refs_0_.1), channel_id=1, source_target_pairs={{0,1},{1,0},{2,3},{3,2},{4,5},{5,4},{6,7},{7,6},{8,9},{9,8},{10,11... | collective-permute-start | bytes 3145736 | tf_op jit(solution)/shard_map/ppermute | solution.py:378
  6.0 9.3 %collective-permute-start = (bf16[64,2048]{1,0:T(8,128)(2,1)S(1)}, bf16[64,2048]{1,0:T(8,128)(2,1)S(1)}, u32[]{:S(2)}, u32[]{:S(2)}) collective-permute-start(bf16[64,2048]{1,0:T(8,128)(2,1)S(1)} %get-tuple-element.52), channel_id=1, source_target_pairs={{0,16},{1,17},{2,18},{3,19},{4,20},{5,21},{6,22},{7,23},{8,24},{9,... | collective-permute-start | bytes 786440 | tf_op jit(solution)/shard_map/ppermute | solution.py:378
  7.6 10.6 %collective-permute-start.1 = (bf16[64,2048]{1,0:T(8,128)(2,1)S(1)}, bf16[64,2048]{1,0:T(8,128)(2,1)S(1)}, u32[]{:S(2)}, u32[]{:S(2)}) collective-permute-start(bf16[64,2048]{1,0:T(8,128)(2,1)S(1)} %get-tuple-element.53), channel_id=1, source_target_pairs={{0,24},{1,25},{2,26},{3,27},{4,28},{5,29},{6,30},{7,31},{8,16},{9,... | collective-permute-start | bytes 786440 | tf_op jit(solution)/shard_map/ppermute | solution.py:378
  7.6 10.6 %collective-permute-start.2 = (bf16[64,2048]{1,0:T(8,128)(2,1)S(1)}, bf16[64,2048]{1,0:T(8,128)(2,1)S(1)}, u32[]{:S(2)}, u32[]{:S(2)}) collective-permute-start(bf16[64,2048]{1,0:T(8,128)(2,1)S(1)} %get-tuple-element.54), channel_id=1, source_target_pairs={{0,8},{1,9},{2,10},{3,11},{4,12},{5,13},{6,14},{7,15},{8,0},{9,1},... | collective-permute-start | bytes 786440 | tf_op jit(solution)/shard_map/ppermute | solution.py:378
  20.5 21.1 %collective-permute-start.9 = (bf16[256,512]{1,0:T(8,128)(2,1)S(1)}, bf16[256,512]{1,0:T(8,128)(2,1)S(1)}, u32[]{:S(2)}, u32[]{:S(2)}) collective-permute-start(bf16[256,512]{1,0:T(8,128)(2,1)S(1)} %get-tuple-element.56), channel_id=1, source_target_pairs={{0,4},{1,5},{2,6},{3,7},{4,0},{5,1},{6,2},{7,3},{8,12},{9,13},{10,... | collective-permute-start | bytes 786440 | tf_op jit(solution)/shard_map/ppermute | solution.py:378
  30.1 23.0 %collective-permute-start.14 = (bf16[512,768]{1,0:T(8,128)(2,1)S(1)}, bf16[512,768]{1,0:T(8,128)(2,1)S(1)}, u32[]{:S(2)}, u32[]{:S(2)}) collective-permute-start(bf16[512,768]{1,0:T(8,128)(2,1)S(1)} %slice.7), channel_id=1, source_target_pairs={{0,1},{1,0},{2,3},{3,2},{4,5},{5,4},{6,7},{7,6},{8,9},{9,8},{10,11... | collective-permute-start | bytes 2359304 | tf_op jit(solution)/shard_map/ppermute | solution.py:378
  32.8 4.8 %collective-permute-start.4 = (s32[4,8,64]{2,1,0:T(8,128)}, s32[4,8,64]{2,1,0:T(8,128)S(1)}, u32[]{:S(2)}, u32[]{:S(2)}) collective-permute-start(s32[4,8,64]{2,1,0:T(8,128)} %bitcast.21), channel_id=1, source_target_pairs={{0,4},{1,5},{2,6},{3,7},{4,0},{5,1},{6,2},{7,3},{8,12},{9,13},{10,... | collective-permute-start | bytes 24584 | tf_op jit(solution)/shard_map/ppermute | solution.py:378
  33.4 10.8 %collective-permute-start.6 = (bf16[256,512]{1,0:T(8,128)(2,1)S(1)}, bf16[256,512]{1,0:T(8,128)(2,1)S(1)}, u32[]{:S(2)}, u32[]{:S(2)}) collective-permute-start(bf16[256,512]{1,0:T(8,128)(2,1)S(1)} %shard_map.102.refs_1_), channel_id=1, source_target_pairs={{0,16},{1,17},{2,18},{3,19},{4,20},{5,21},{6,22},{7,23},{8,24},{9,... | collective-permute-start | bytes 786440 | tf_op jit(solution)/shard_map/ppermute | solution.py:378
  37.6 1.2 %copy-start.1 = (bf16[512,1024]{1,0:T(8,128)(2,1)S(1)}, bf16[512,1024]{1,0:T(8,128)(2,1)}, u32[]{:S(2)}) copy-start(bf16[512,1024]{1,0:T(8,128)(2,1)} %refs_0_.1) | copy-start | bytes 3145732
  38.8 1.0 copy-start.2
  39.9 0.7 copy-start.3
  40.6 0.7 copy-start.4
  41.6 7.2 %collective-permute-start.11 = (bf16[256,512]{1,0:T(8,128)(2,1)S(1)}, bf16[256,512]{1,0:T(8,128)(2,1)S(1)}, u32[]{:S(2)}, u32[]{:S(2)}) collective-permute-start(bf16[256,512]{1,0:T(8,128)(2,1)S(1)} %collective-permute-done.9.refs_0_), channel_id=1, source_target_pairs={{0,16},{1,17},{2,18},{3,19},{4,20},{5,21},{6,22},{7,23},{8,24},{9,... | collective-permute-start | bytes 786440 | tf_op jit(solution)/shard_map/ppermute | solution.py:378
  44.1 6.4 %collective-permute-start.12 = (bf16[512,256]{1,0:T(8,128)(2,1)S(1)}, bf16[512,256]{1,0:T(8,128)(2,1)S(1)}, u32[]{:S(2)}, u32[]{:S(2)}) collective-permute-start(bf16[512,256]{1,0:T(8,128)(2,1)S(1)} %slice.6), channel_id=1, source_target_pairs={{0,2},{1,3},{2,0},{3,1},{4,6},{5,7},{6,4},{7,5},{8,10},{9,11},{10,... | collective-permute-start | bytes 786440 | tf_op jit(solution)/shard_map/ppermute | solution.py:378
  44.2 6.3 %collective-permute-start.5 = (bf16[256,512]{1,0:T(8,128)(2,1)S(1)}, bf16[256,512]{1,0:T(8,128)(2,1)S(1)}, u32[]{:S(2)}, u32[]{:S(2)}) collective-permute-start(bf16[256,512]{1,0:T(8,128)(2,1)S(1)} %shard_map.102.refs_1_), channel_id=1, source_target_pairs={{0,8},{1,9},{2,10},{3,11},{4,12},{5,13},{6,14},{7,15},{8,0},{9,1},... | collective-permute-start | bytes 786440 | tf_op jit(solution)/shard_map/ppermute | solution.py:378
  44.3 6.3 %collective-permute-start.7 = (bf16[256,512]{1,0:T(8,128)(2,1)S(1)}, bf16[256,512]{1,0:T(8,128)(2,1)S(1)}, u32[]{:S(2)}, u32[]{:S(2)}) collective-permute-start(bf16[256,512]{1,0:T(8,128)(2,1)S(1)} %collective-permute-done.6.refs_3_), channel_id=1, source_target_pairs={{0,8},{1,9},{2,10},{3,11},{4,12},{5,13},{6,14},{7,15},{8,0},{9,1},... | collective-permute-start | bytes 786440 | tf_op jit(solution)/shard_map/ppermute | solution.py:378
  48.8 2.8 %collective-permute-start.10 = (bf16[256,512]{1,0:T(8,128)(2,1)S(1)}, bf16[256,512]{1,0:T(8,128)(2,1)S(1)}, u32[]{:S(2)}, u32[]{:S(2)}) collective-permute-start(bf16[256,512]{1,0:T(8,128)(2,1)S(1)} %collective-permute-done.9.refs_0_), channel_id=1, source_target_pairs={{0,8},{1,9},{2,10},{3,11},{4,12},{5,13},{6,14},{7,15},{8,0},{9,1},... | collective-permute-start | bytes 786440 | tf_op jit(solution)/shard_map/ppermute | solution.py:378
  50.5 1.5 %collective-permute-start.13 = (bf16[256,512]{1,0:T(8,128)(2,1)S(1)}, bf16[256,512]{1,0:T(8,128)(2,1)S(1)}, u32[]{:S(2)}, u32[]{:S(2)}) collective-permute-start(bf16[256,512]{1,0:T(8,128)(2,1)S(1)} %collective-permute-done.11.refs_2_), channel_id=1, source_target_pairs={{0,8},{1,9},{2,10},{3,11},{4,12},{5,13},{6,14},{7,15},{8,0},{9,1},... | collective-permute-start | bytes 786440 | tf_op jit(solution)/shard_map/ppermute | solution.py:378
  50.5 19.7 %slice-start = ((s8[6291456]{0:T(1024)(128)(4,1)}), s8[4194304]{0:T(1024)(128)(4,1)S(1)}, s32[]{:S(2)}) async-start(s8[6291456]{0:T(1024)(128)(4,1)} %bitcast.16), calls=%async_computation | async-start | bytes 8388608
  50.5 19.7 %copy-start.5 = (f32[1024]{0:T(1024)S(1)}, f32[1024]{0:T(1024)}, u32[]{:S(2)}) copy-start(f32[1024]{0:T(1024)} %param.15) | copy-start | bytes 12292
  51.6 18.6 %slice-start.1 = ((s8[6291456]{0:T(1024)(128)(4,1)}), s8[2097152]{0:T(1024)(128)(4,1)S(1)}, s32[]{:S(2)}) async-start(s8[6291456]{0:T(1024)(128)(4,1)} %bitcast.16), calls=%async_computation.1 | async-start | bytes 4194304
  53.1 37.4 %copy-start = (bf16[1,1536,1024]{2,1,0:T(8,128)(2,1)S(1)}, bf16[1,1536,1024]{2,1,0:T(8,128)(2,1)}, u32[]{:S(2)}) copy-start(bf16[1,1536,1024]{2,1,0:T(8,128)(2,1)} %param.19) | copy-start | bytes 9437188
  54.8 8.4 %collective-permute-start.15 = (bf16[32,1024]{1,0:T(8,128)(2,1)S(1)}, bf16[32,1024]{1,0:T(8,128)(2,1)S(1)}, u32[]{:S(2)}, u32[]{:S(2)}) collective-permute-start(bf16[32,1024]{1,0:T(8,128)(2,1)S(1)} %get-tuple-element.75), channel_id=1, source_target_pairs={{0,4},{1,5},{2,6},{3,7},{4,0},{5,1},{6,2},{7,3},{8,12},{9,13},{10,... | collective-permute-start | bytes 196616 | tf_op jit(solution)/shard_map/ppermute | solution.py:378
  55.9 7.4 %collective-permute-start.16 = (bf16[32,1024]{1,0:T(8,128)(2,1)S(1)}, bf16[32,1024]{1,0:T(8,128)(2,1)S(1)}, u32[]{:S(2)}, u32[]{:S(2)}) collective-permute-start(bf16[32,1024]{1,0:T(8,128)(2,1)S(1)} %get-tuple-element.76), channel_id=1, source_target_pairs={{0,3},{1,2},{2,1},{3,0},{4,7},{5,6},{6,5},{7,4},{8,11},{9,10},{10,... | collective-permute-start | bytes 196616 | tf_op jit(solution)/shard_map/ppermute | solution.py:378
  57.4 8.6 %collective-permute-start.17 = (bf16[32,1024]{1,0:T(8,128)(2,1)S(1)}, bf16[32,1024]{1,0:T(8,128)(2,1)S(1)}, u32[]{:S(2)}, u32[]{:S(2)}) collective-permute-start(bf16[32,1024]{1,0:T(8,128)(2,1)S(1)} %get-tuple-element.77), channel_id=1, source_target_pairs={{0,5},{1,4},{2,7},{3,6},{4,1},{5,0},{6,3},{7,2},{8,13},{9,12},{10,... | collective-permute-start | bytes 196616 | tf_op jit(solution)/shard_map/ppermute | solution.py:378
  58.8 7.1 %collective-permute-start.18 = (bf16[32,1024]{1,0:T(8,128)(2,1)S(1)}, bf16[32,1024]{1,0:T(8,128)(2,1)S(1)}, u32[]{:S(2)}, u32[]{:S(2)}) collective-permute-start(bf16[32,1024]{1,0:T(8,128)(2,1)S(1)} %get-tuple-element.78), channel_id=1, source_target_pairs={{0,2},{1,3},{2,0},{3,1},{4,6},{5,7},{6,4},{7,5},{8,10},{9,11},{10,... | collective-permute-start | bytes 196616 | tf_op jit(solution)/shard_map/ppermute | solution.py:378
  60.7 6.2 %collective-permute-start.19 = (bf16[32,1024]{1,0:T(8,128)(2,1)S(1)}, bf16[32,1024]{1,0:T(8,128)(2,1)S(1)}, u32[]{:S(2)}, u32[]{:S(2)}) collective-permute-start(bf16[32,1024]{1,0:T(8,128)(2,1)S(1)} %get-tuple-element.79), channel_id=1, source_target_pairs={{0,6},{1,7},{2,4},{3,5},{4,2},{5,3},{6,0},{7,1},{8,14},{9,15},{10,... | collective-permute-start | bytes 196616 | tf_op jit(solution)/shard_map/ppermute | solution.py:378
  63.2 4.3 %collective-permute-start.20 = (bf16[32,1024]{1,0:T(8,128)(2,1)S(1)}, bf16[32,1024]{1,0:T(8,128)(2,1)S(1)}, u32[]{:S(2)}, u32[]{:S(2)}) collective-permute-start(bf16[32,1024]{1,0:T(8,128)(2,1)S(1)} %get-tuple-element.80), channel_id=1, source_target_pairs={{0,1},{1,0},{2,3},{3,2},{4,5},{5,4},{6,7},{7,6},{8,9},{9,8},{10,11... | collective-permute-start | bytes 196616 | tf_op jit(solution)/shard_map/ppermute | solution.py:378
  63.2 7.0 %collective-permute-start.21 = (bf16[32,1024]{1,0:T(8,128)(2,1)S(1)}, bf16[32,1024]{1,0:T(8,128)(2,1)S(1)}, u32[]{:S(2)}, u32[]{:S(2)}) collective-permute-start(bf16[32,1024]{1,0:T(8,128)(2,1)S(1)} %get-tuple-element.81), channel_id=1, source_target_pairs={{0,7},{1,6},{2,5},{3,4},{4,3},{5,2},{6,1},{7,0},{8,15},{9,14},{10,... | collective-permute-start | bytes 196616 | tf_op jit(solution)/shard_map/ppermute | solution.py:378
  71.5 1.5 %collective-permute-start.24 = (bf16[32,3200]{1,0:T(8,128)(2,1)S(1)}, bf16[32,3200]{1,0:T(8,128)(2,1)S(1)}, u32[]{:S(2)}, u32[]{:S(2)}) collective-permute-start(bf16[32,3200]{1,0:T(8,128)(2,1)S(1)} %get-tuple-element.88), channel_id=1, source_target_pairs={{0,8},{1,9},{2,10},{3,11},{4,12},{5,13},{6,14},{7,15},{8,0},{9,1},... | collective-permute-start | bytes 614408 | tf_op jit(solution)/shard_map/ppermute | solution.py:378
  71.5 1.7 %collective-permute-start.25 = (bf16[32,3200]{1,0:T(8,128)(2,1)S(1)}, bf16[32,3200]{1,0:T(8,128)(2,1)S(1)}, u32[]{:S(2)}, u32[]{:S(2)}) collective-permute-start(bf16[32,3200]{1,0:T(8,128)(2,1)S(1)} %get-tuple-element.89), channel_id=1, source_target_pairs={{0,8},{1,9},{2,10},{3,11},{4,12},{5,13},{6,14},{7,15},{8,0},{9,1},... | collective-permute-start | bytes 614408 | tf_op jit(solution)/shard_map/ppermute | solution.py:378
  72.0 17.2 %collective-permute-start.22 = (bf16[160,1024]{1,0:T(8,128)(2,1)S(1)}, bf16[160,1024]{1,0:T(8,128)(2,1)S(1)}, u32[]{:S(2)}, u32[]{:S(2)}) collective-permute-start(bf16[160,1024]{1,0:T(8,128)(2,1)S(1)} %get-tuple-element.83), channel_id=1, source_target_pairs={{0,4},{1,5},{2,6},{3,7},{4,0},{5,1},{6,2},{7,3},{8,12},{9,13},{10,... | collective-permute-start | bytes 983048 | tf_op jit(solution)/shard_map/ppermute | solution.py:378
  73.4 5.8 %collective-permute-start.26 = (bf16[16,3200]{1,0:T(8,128)(2,1)S(1)}, bf16[16,3200]{1,0:T(8,128)(2,1)S(1)}, u32[]{:S(2)}, u32[]{:S(2)}) collective-permute-start(bf16[16,3200]{1,0:T(8,128)(2,1)S(1)} %get-tuple-element.91), channel_id=1, source_target_pairs={{0,16},{1,17},{2,18},{3,19},{4,20},{5,21},{6,22},{7,23},{8,24},{9,... | collective-permute-start | bytes 307208 | tf_op jit(solution)/shard_map/ppermute | solution.py:378
  74.2 6.4 %collective-permute-start.27 = (bf16[16,3200]{1,0:T(8,128)(2,1)S(1)}, bf16[16,3200]{1,0:T(8,128)(2,1)S(1)}, u32[]{:S(2)}, u32[]{:S(2)}) collective-permute-start(bf16[16,3200]{1,0:T(8,128)(2,1)S(1)} %get-tuple-element.92), channel_id=1, source_target_pairs={{0,16},{1,17},{2,18},{3,19},{4,20},{5,21},{6,22},{7,23},{8,24},{9,... | collective-permute-start | bytes 307208 | tf_op jit(solution)/shard_map/ppermute | solution.py:378
  80.8 8.5 %collective-permute-start.29 = (bf16[32,1536]{1,0:T(8,128)(2,1)S(1)}, bf16[32,1536]{1,0:T(8,128)(2,1)S(1)}, u32[]{:S(2)}, u32[]{:S(2)}) collective-permute-start(bf16[32,1536]{1,0:T(8,128)(2,1)S(1)} %shard_map.110.refs_0_), channel_id=1, source_target_pairs={{0,16},{1,17},{2,18},{3,19},{4,20},{5,21},{6,22},{7,23},{8,24},{9,... | collective-permute-start | bytes 294920 | tf_op jit(solution)/shard_map/ppermute | solution.py:378
  81.6 7.6 %collective-permute-start.28 = (bf16[32,1536]{1,0:T(8,128)(2,1)S(1)}, bf16[32,1536]{1,0:T(8,128)(2,1)S(1)}, u32[]{:S(2)}, u32[]{:S(2)}) collective-permute-start(bf16[32,1536]{1,0:T(8,128)(2,1)S(1)} %shard_map.110.refs_0_), channel_id=1, source_target_pairs={{0,8},{1,9},{2,10},{3,11},{4,12},{5,13},{6,14},{7,15},{8,0},{9,1},... | collective-permute-start | bytes 294920 | tf_op jit(solution)/shard_map/ppermute | solution.py:378
  89.3 1.3 %collective-permute-start.30 = (bf16[32,1536]{1,0:T(8,128)(2,1)S(1)}, bf16[32,1536]{1,0:T(8,128)(2,1)S(1)}, u32[]{:S(2)}, u32[]{:S(2)}) collective-permute-start(bf16[32,1536]{1,0:T(8,128)(2,1)S(1)} %collective-permute-done.29.refs_2_), channel_id=1, source_target_pairs={{0,8},{1,9},{2,10},{3,11},{4,12},{5,13},{6,14},{7,15},{8,0},{9,1},... | collective-permute-start | bytes 294920 | tf_op jit(solution)/shard_map/ppermute | solution.py:378
  89.3 11.4 %collective-permute-start.23 = (bf16[96,1024]{1,0:T(8,128)(2,1)S(1)}, bf16[96,1024]{1,0:T(8,128)(2,1)S(1)}, u32[]{:S(2)}, u32[]{:S(2)}) collective-permute-start(bf16[96,1024]{1,0:T(8,128)(2,1)S(1)} %get-tuple-element.85), channel_id=1, source_target_pairs={{0,4},{1,5},{2,6},{3,7},{4,0},{5,1},{6,2},{7,3},{8,12},{9,13},{10,... | collective-permute-start | bytes 589832 | tf_op jit(solution)/shard_map/ppermute | solution.py:378
  91.2 9.5 %collective-permute-start.31 = (bf16[32,1024]{1,0:T(8,128)(2,1)S(1)}, bf16[32,1024]{1,0:T(8,128)(2,1)S(1)}, u32[]{:S(2)}, u32[]{:S(2)}) collective-permute-start(bf16[32,1024]{1,0:T(8,128)(2,1)S(1)} %get-tuple-element.94), channel_id=1, source_target_pairs={{0,3},{1,2},{2,1},{3,0},{4,7},{5,6},{6,5},{7,4},{8,11},{9,10},{10,... | collective-permute-start | bytes 196616 | tf_op jit(solution)/shard_map/ppermute | solution.py:378
  93.5 8.0 %collective-permute-start.32 = (bf16[32,1024]{1,0:T(8,128)(2,1)S(1)}, bf16[32,1024]{1,0:T(8,128)(2,1)S(1)}, u32[]{:S(2)}, u32[]{:S(2)}) collective-permute-start(bf16[32,1024]{1,0:T(8,128)(2,1)S(1)} %get-tuple-element.95), channel_id=1, source_target_pairs={{0,2},{1,3},{2,0},{3,1},{4,6},{5,7},{6,4},{7,5},{8,10},{9,11},{10,... | collective-permute-start | bytes 196616 | tf_op jit(solution)/shard_map/ppermute | solution.py:378
  93.8 7.8 %collective-permute-start.33 = (bf16[32,1024]{1,0:T(8,128)(2,1)S(1)}, bf16[32,1024]{1,0:T(8,128)(2,1)S(1)}, u32[]{:S(2)}, u32[]{:S(2)}) collective-permute-start(bf16[32,1024]{1,0:T(8,128)(2,1)S(1)} %get-tuple-element.96), channel_id=1, source_target_pairs={{0,1},{1,0},{2,3},{3,2},{4,5},{5,4},{6,7},{7,6},{8,9},{9,8},{10,11... | collective-permute-start | bytes 196616 | tf_op jit(solution)/shard_map/ppermute | solution.py:378
  101.6 8.0 %collective-permute-start.34 = (bf16[64,1024]{1,0:T(8,128)(2,1)S(1)}, bf16[64,1024]{1,0:T(8,128)(2,1)S(1)}, u32[]{:S(2)}, u32[]{:S(2)}) collective-permute-start(bf16[64,1024]{1,0:T(8,128)(2,1)S(1)} %shard_map.112), channel_id=1, source_target_pairs={{0,4},{1,5},{2,6},{3,7},{4,0},{5,1},{6,2},{7,3},{8,12},{9,13},{10,... | collective-permute-start | bytes 393224 | tf_op jit(solution)/shard_map/ppermute | solution.py:378

commit v15 on v14

--- a/solution.py
+++ b/solution.py
@@ -74,10 +74,6 @@
 
 def far_first(C):
     return [*range(2, C), 1, 0]
-
-
-def hops(E):
-    return [*reversed(range(E // 2))]
 
 
 def all_hops(E):
@@ -146,10 +142,7 @@
             out[at, h * HEAD_SIZE : (h + 1) * HEAD_SIZE] = (numerator / total).astype(BF16)
 
 
-def route_kernel(E, cap, routes_ref, other_ref, gates_ref, *refs):
-    line_s, gate_s = refs[-2:]
-    for src, dst in zip(refs[:2], refs[5:7]):
-        dst[...] = src[...]
+def place_tokens(E, cap, t, routes_ref, place_ref, line_s):
     blocks, _, tok = routes_ref.shape
     rows = blocks * tok
     earlier = jnp.where(
@@ -158,25 +151,31 @@
         1.0,
         0.0,
     ).astype(BF16)
-    for t, ref in enumerate((routes_ref, other_ref)):
-        for i in range(blocks):
-            routes = ref[i]
-            resident = routes < E
-            target = jnp.sum(jnp.where(resident, routes + 1, 0), axis=0, keepdims=True) - 1
-            line_s[:, i * tok : (i + 1) * tok] = jnp.broadcast_to(target, (8, tok))
-            if t == 0:
-                gate = jnp.sum(jnp.where(resident, gates_ref[i], 0.0), axis=0, keepdims=True)
-                gate_s[:, i * tok : (i + 1) * tok] = jnp.broadcast_to(gate, (128, tok))
-        target = line_s[:1, :]
-        experts = lax.broadcasted_iota(jnp.int32, (E, rows), 0)
-        one_hot = jnp.where(target == experts, 1.0, 0.0)
-        rank = jnp.sum(dot(one_hot.astype(BF16), earlier) * one_hot, axis=0, keepdims=True)
-        own = jnp.bitwise_xor(lax.axis_index("exp"), PAIR * t)
-        slot = jnp.bitwise_xor(target, own) * cap + rank.astype(jnp.int32)
-        slot = jnp.where(target >= 0, slot, -1)
-        places = lax.broadcasted_iota(jnp.int32, (E * cap, rows), 0)
-        refs[2 + t][...] = jnp.where(slot == places, 1.0, 0.0).astype(BF16)
-    refs[4][...] = gate_s[...].T
+    for i in range(blocks):
+        routes = routes_ref[i]
+        target = jnp.sum(jnp.where(routes < E, routes + 1, 0), axis=0, keepdims=True) - 1
+        line_s[:, i * tok : (i + 1) * tok] = jnp.broadcast_to(target, (8, tok))
+    target = line_s[:1, :]
+    experts = lax.broadcasted_iota(jnp.int32, (E, rows), 0)
+    one_hot = jnp.where(target == experts, 1.0, 0.0)
+    rank = jnp.sum(dot(one_hot.astype(BF16), earlier) * one_hot, axis=0, keepdims=True)
+    own = jnp.bitwise_xor(lax.axis_index("exp"), PAIR * t)
+    slot = jnp.bitwise_xor(target, own) * cap + rank.astype(jnp.int32)
+    slot = jnp.where(target >= 0, slot, -1)
+    places = lax.broadcasted_iota(jnp.int32, (E * cap, rows), 0)
+    place_ref[...] = jnp.where(slot == places, 1.0, 0.0).astype(BF16)
+
+
+def route_kernel(E, cap, routes_ref, gates_ref, *refs):
+    place_ref, gate_ref, line_s, gate_s = refs[2], refs[3], refs[-2], refs[-1]
+    for src, dst in zip(refs[:2], refs[4:6]):
+        dst[...] = src[...]
+    place_tokens(E, cap, 0, routes_ref, place_ref, line_s)
+    blocks, _, tok = routes_ref.shape
+    for i in range(blocks):
+        gate = jnp.sum(jnp.where(routes_ref[i] < E, gates_ref[i], 0.0), axis=0, keepdims=True)
+        gate_s[:, i * tok : (i + 1) * tok] = jnp.broadcast_to(gate, (128, tok))
+    gate_ref[...] = gate_s[...].T
 
 
 def project_kernel(C, with_residual, *refs):
@@ -303,7 +302,7 @@
 
 
 def down_kernel(C, E, cap, *refs):
-    acts, w_ref, outs, x_s, part_s = refs[:C], refs[C], refs[C + 1 : C + 1 + E // 2], refs[-2], refs[-1]
+    acts, w_ref, outs, x_s, part_s = refs[:C], refs[C], refs[C + 1 : C + 1 + E], refs[-2], refs[-1]
     c = lax.axis_index("ctx")
     e = lax.axis_index("exp")
     own_rows = E * cap // C
@@ -311,15 +310,9 @@
         at = aligned(jnp.bitwise_xor(c, s) * own_rows, own_rows)
         x_s[pl.ds(at, own_rows), :] = acts[s][...]
     part_s[...] = dot(x_s[...], w_ref[...]).astype(BF16)
-    for d in range(E // 2):
-        for t in range(2):
-            at = aligned(jnp.bitwise_xor(e, spread(d) ^ (PAIR * t)) * cap, cap)
-            outs[d][t * cap : (t + 1) * cap, :] = part_s[pl.ds(at, cap), :]
-
-
-def forward_kernel(E, cap, *refs):
-    for x, d in zip(refs[:-1], hops(E)):
-        refs[-1][d * cap : (d + 1) * cap, :] = x[cap:, :]
+    for out, b in zip(outs, all_hops(E)):
+        at = aligned(jnp.bitwise_xor(e, b) * cap, cap)
+        out[...] = part_s[pl.ds(at, cap), :]
 
 
 def mix_kernel(own, first, second, out):
@@ -329,12 +322,9 @@
 
 
 def combine_kernel(E, cap, mixed, place_ref, gate_ref, *refs):
-    xs, (far, out, x_s, out_s, sems) = refs[: E // 2], refs[E // 2 :]
-    for x, d in zip(xs, hops(E)):
-        at = spread(d) * cap
-        x_s[at : at + cap, :] = x[:cap, :]
-        at = (spread(d) ^ PAIR) * cap
-        x_s[at : at + cap, :] = far[d * cap : (d + 1) * cap, :]
+    xs, (out, x_s, out_s, sems) = refs[:E], refs[E:]
+    for x, b in zip(xs, all_hops(E)):
+        x_s[b * cap : (b + 1) * cap, :] = x[...]
     count, _, width = out_s.shape
     copies = []
     for j in range(count):
@@ -417,23 +407,23 @@
     other, own_msg = attend(1, got)
     theirs = permute(other, exp=PAIR)
     (mine,) = attend(0, [after(got[0], other), *got[1:-1], own_msg])
-    cut = width - max(width // 4, 128)
-    near = after(shards[1], theirs)[:, cut:]
-    for d in range(2, C, 2):
-        shards[d + 1] = (
-            permute(after(shards[d], mine)[:, :cut], exp=1),
-            permute(near, exp=spread(d)),
-        )
-    place, other_place, gate, *staged = call(
+    place, gate, *staged = call(
         functools.partial(route_kernel, E, cap),
-        [sds((slots, rows), BF16)] * 2
-        + [sds((rows, 128), F32)]
+        [sds((slots, rows), BF16), sds((rows, 128), F32)]
         + [sds((qw, width), BF16), sds((rows, width), BF16)],
-        5,
+        4,
         scratch=[pltpu.VMEM((8, rows), jnp.int32), pltpu.VMEM((128, rows), F32)],
         cost=(0, 2**14),
         limit=16,
-    )(after(own_routes, mine, *step), other_routes, tokens_last(gates), out_weight, res)
+    )(after(own_routes, mine), tokens_last(gates), out_weight, res)
+    other_place = call(
+        functools.partial(place_tokens, E, cap, 1),
+        sds((slots, rows), BF16),
+        1,
+        scratch=[pltpu.VMEM((8, rows), jnp.int32)],
+        cost=(0, 2**14),
+        limit=16,
+    )(other_routes)
     shards[0], res = staged
 
     def gather(x, before=lambda: ()):
@@ -458,12 +448,19 @@
         )(*operands)
 
     mine_all = gather(mine)
+    cut = width - max(width * 3 // 8, 128)
+    near = after(shards[1], place)[:, cut:]
+    for d in range(2, C, 2):
+        shards[d + 1] = (
+            permute(after(shards[d], place, *mine_all[2::2])[:, :cut], exp=1),
+            permute(near, exp=spread(d)),
+        )
     acc, last = project(mine_all, res)
     quarter = [shards[d][1] for d in range(3, C, 2)]
     theirs_all = gather(after(theirs, place, shards[1]), lambda: quarter)
     acc_far, last_far = project(theirs_all)
     gain = norm_gain.reshape(1, width)
-    few = rows * 5 // 8
+    few = rows // 2
     own, first, second, *outgoing = call(
         functools.partial(last_kernel, E, cap),
         [
@@ -516,22 +513,18 @@
         bit //= 2
     expert_out = call(
         functools.partial(down_kernel, C, E, cap),
-        [sds((2 * cap, width), BF16)] * (E // 2),
+        [sds((cap, width), BF16)] * E,
         C + 1,
         scratch=[pltpu.VMEM((slots, hidden), BF16), pltpu.VMEM((slots, width), BF16)],
         cost=(2 * slots * width * hidden, 2 * width * hidden),
     )(acts[0], *[acts[s] for s in range(1, C)], w_down.reshape(hidden, width))
-    returned = [permute(expert_out[d], exp=spread(d)) for d in hops(E)[:-1]]
-    returned.append(after(expert_out[0], second))
-    far = call(
-        functools.partial(forward_kernel, E, cap), sds((slots // 2, width), BF16), E // 2, cost=(0, 2**19)
-    )(*returned)
+    returned = [permute(x, exp=b) if b else x for x, b in zip(expert_out, all_hops(E))]
     mixed = call(mix_kernel, sds((rows, width), F32), 3, cost=(0, 2**14))(own, first, second)
     columns = min(4, width // 128)
     result = call(
         functools.partial(combine_kernel, E, cap),
         sds((rows, width), BF16),
-        4 + E // 2,
+        3 + E,
         scratch=[
             pltpu.VMEM((slots, width), BF16),
             pltpu.VMEM((columns, rows, width // columns), BF16),
@@ -539,7 +532,7 @@
         ],
         out_specs=HBM,
         cost=(0, 2 * 2**20),
-    )(mixed, place, gate, *returned, permute(far, exp=PAIR))
+    )(mixed, place, gate, *returned)
     return result.reshape(C, 1, tok, width)
 
 

time: 111 us -> 111 us (level)
  waiting for transfers between devices: 56.3 us -> 51.7 us
  starting transfers between devices: 36.9 us -> 41.3 us
    ppermute x35 -> x38, waiting for transfers between devices: 56.3 us -> 51.7 us  [permute(): return lax.ppermute(x, ('ctx', 'exp'), pairs)]
    ppermute x35 -> x38, starting transfers between devices: 36.9 us -> 41.3 us  [permute(): return lax.ppermute(x, ('ctx', 'exp'), pairs)]
  transfers between devices with their start and end apart: 35 -> 38, of which waited for: 19 -> 19; matrix products, arithmetic and copies ran while one was open for 0% -> 0% of each run, Pallas kernels for 9% -> 9%
where the time goes in v15:
time: 111 us
  waiting for transfers between devices  51.7 us (47%)
  starting transfers between devices  41.3 us (37%)
  Pallas kernels  13.7 us (12%)
  local copies, waits for them, and re-layouts  3.83 us (3%)
    ppermute x38, waiting for transfers between devices, permute(): return lax.ppermute(x, ('ctx', 'exp'), pairs)  51.7 us
    ppermute x38, starting transfers between devices, permute(): return lax.ppermute(x, ('ctx', 'exp'), pairs)  41.3 us
    pallas_call x2, Pallas kernels, attend(): call(functools.partial(attend_kernel, C, t), [sds((rows, qw), BF16)] + [s...  4.65 us
    unnamed x16, local copies, waits for them, and re-layouts  3.72 us
  transfers between devices with their start and end apart: 38, of which 19 were waited for; matrix products, arithmetic and copies ran while one was open for 0% of the time, Pallas kernels for 9%

profile of v15, /device:TPU:0, one launch (start us, length us, event | category | flops | bytes accessed | tf_op | source)
XLA Modules:
  0.0 110.7 jit_solution(7884070723547636493)
XLA Ops:
  0.0 2.9 %collective-permute-start.6 = (bf16[512,1024]{1,0:T(8,128)(2,1)}, bf16[512,1024]{1,0:T(8,128)(2,1)S(1)}, u32[]{:S(2)}, u32[]{:S(2)}) collective-permute-start(bf16[512,1024]{1,0:T(8,128)(2,1)} %refs_0_.1), channel_id=1, source_target_pairs={{0,1},{1,0},{2,3},{3,2},{4,5},{5,4},{6,7},{7,6},{8,9},{9,8},{10,11... | collective-permute-start | bytes 3145736 | tf_op jit(solution)/shard_map/ppermute | solution.py:368
  2.9 1.6 %collective-permute-start.7 = (bf16[512,1024]{1,0:T(8,128)(2,1)}, bf16[512,1024]{1,0:T(8,128)(2,1)S(1)}, u32[]{:S(2)}, u32[]{:S(2)}) collective-permute-start(bf16[512,1024]{1,0:T(8,128)(2,1)} %refs_0_.1), channel_id=1, source_target_pairs={{0,2},{1,3},{2,0},{3,1},{4,6},{5,7},{6,4},{7,5},{8,10},{9,11},{10,... | collective-permute-start | bytes 3145736 | tf_op jit(solution)/shard_map/ppermute | solution.py:368
  4.5 1.4 %shard_map.100 = (bf16[64,2048]{1,0:T(8,128)(2,1)S(1)}, bf16[64,2048]{1,0:T(8,128)(2,1)S(1)}, bf16[64,2048]{1,0:T(8,128)(2,1)S(1)}, bf16[64,2048]{1,0:T(8,128)(2,1)S(1)}) custom-call(bf16[64,4096]{1,0:T(8,128)(2,1)} %bitcast.25, bf16[64,512]{1,0:T(8,128)(2,1)} %bitcast.26, bf16[64,512]{1,0:T(8,128)(2,1)} %bitcast.27), custom_call_target="tpu_custom_call" | custom-call | bytes 1048576 | tf_op jit(solution)/shard_map/pallas_call | solution.py:374
  6.0 1.6 %collective-permute-start = (bf16[64,2048]{1,0:T(8,128)(2,1)S(1)}, bf16[64,2048]{1,0:T(8,128)(2,1)S(1)}, u32[]{:S(2)}, u32[]{:S(2)}) collective-permute-start(bf16[64,2048]{1,0:T(8,128)(2,1)S(1)} %get-tuple-element.54), channel_id=1, source_target_pairs={{0,16},{1,17},{2,18},{3,19},{4,20},{5,21},{6,22},{7,23},{8,24},{9,... | collective-permute-start | bytes 786440 | tf_op jit(solution)/shard_map/ppermute | solution.py:368
  8.2 7.1 %collective-permute-done.refs_0_ = bf16[64,2048]{1,0:T(8,128)(2,1)S(1)} collective-permute-done((bf16[64,2048]{1,0:T(8,128)(2,1)S(1)}, bf16[64,2048]{1,0:T(8,128)(2,1)S(1)}, u32[]{:S(2)}, u32[]{:S(2)}) %collective-permute-start) | collective-permute-done | bytes 262176 | tf_op jit(solution)/shard_map/ppermute | solution.py:368
  15.3 2.9 %collective-permute-done.1.refs_1_ = bf16[64,2048]{1,0:T(8,128)(2,1)S(1)} collective-permute-done((bf16[64,2048]{1,0:T(8,128)(2,1)S(1)}, bf16[64,2048]{1,0:T(8,128)(2,1)S(1)}, u32[]{:S(2)}, u32[]{:S(2)}) %collective-permute-start.1) | collective-permute-done | bytes 262176 | tf_op jit(solution)/shard_map/ppermute | solution.py:368
  18.2 2.3 %shard_map.101 = (bf16[256,512]{1,0:T(8,128)(2,1)S(1)}, bf16[64,2048]{1,0:T(8,128)(2,1)S(1)}) custom-call(bf16[64,2048]{1,0:T(8,128)(2,1)S(1)} %collective-permute-done.refs_0_, bf16[64,2048]{1,0:T(8,128)(2,1)S(1)} %collective-permute-done.1.refs_1_, bf16[64,2048]{1,0:T(8,128)(2,1)S(1)} %collective-permute-done.2.refs_2_, ...), custom_call_target="tpu_custom_call" | custom-call | bytes 16384 | tf_op jit(solution)/shard_map/pallas_call | solution.py:395
  20.5 2.3 %shard_map.102.refs_1_ = bf16[256,512]{1,0:T(8,128)(2,1)S(1)} custom-call(bf16[64,2048]{1,0:T(8,128)(2,1)S(1)} %collective-permute-done.refs_0_, bf16[64,2048]{1,0:T(8,128)(2,1)S(1)} %collective-permute-done.1.refs_1_, bf16[64,2048]{1,0:T(8,128)(2,1)S(1)} %collective-permute-done.2.refs_2_, bf16[64,2048]{1,0:T(8,128)(2,1)S(1)} %get-tuple-element.60.refs_3_), custom_call_target="tpu_custom_call" | custom-call | bytes 16384 | tf_op jit(solution)/shard_map/pallas_call | solution.py:395
  22.8 0.8 collective-permute-start.4
  23.6 2.6 %collective-permute-start.8 = (bf16[256,512]{1,0:T(8,128)(2,1)S(1)}, bf16[256,512]{1,0:T(8,128)(2,1)S(1)}, u32[]{:S(2)}, u32[]{:S(2)}) collective-permute-start(bf16[256,512]{1,0:T(8,128)(2,1)S(1)} %get-tuple-element.58), channel_id=1, source_target_pairs={{0,4},{1,5},{2,6},{3,7},{4,0},{5,1},{6,2},{7,3},{8,12},{9,13},{10,... | collective-permute-start | bytes 786440 | tf_op jit(solution)/shard_map/ppermute | solution.py:368
  26.2 1.2 %copy-done.1 = bf16[512,1024]{1,0:T(8,128)(2,1)S(1)} copy-done((bf16[512,1024]{1,0:T(8,128)(2,1)S(1)}, bf16[512,1024]{1,0:T(8,128)(2,1)}, u32[]{:S(2)}) %copy-start.1) | copy-done | bytes 1048600
  27.4 1.0 copy-done.2
  28.5 0.7 copy-done.3
  29.2 0.7 copy-done.4
  30.8 1.2 %collective-permute-done.4.refs_3_ = bf16[256,512]{1,0:T(8,128)(2,1)S(1)} collective-permute-done((bf16[256,512]{1,0:T(8,128)(2,1)S(1)}, bf16[256,512]{1,0:T(8,128)(2,1)S(1)}, u32[]{:S(2)}, u32[]{:S(2)}) %collective-permute-start.4) | collective-permute-done | bytes 262176 | tf_op jit(solution)/shard_map/ppermute | solution.py:368
  32.6 6.2 %collective-permute-done.8.refs_0_ = bf16[256,512]{1,0:T(8,128)(2,1)S(1)} collective-permute-done((bf16[256,512]{1,0:T(8,128)(2,1)S(1)}, bf16[256,512]{1,0:T(8,128)(2,1)S(1)}, u32[]{:S(2)}, u32[]{:S(2)}) %collective-permute-start.8) | collective-permute-done | bytes 262176 | tf_op jit(solution)/shard_map/ppermute | solution.py:368
  38.9 1.7 %collective-permute-start.10 = (bf16[256,512]{1,0:T(8,128)(2,1)S(1)}, bf16[256,512]{1,0:T(8,128)(2,1)S(1)}, u32[]{:S(2)}, u32[]{:S(2)}) collective-permute-start(bf16[256,512]{1,0:T(8,128)(2,1)S(1)} %collective-permute-done.8.refs_0_), channel_id=1, source_target_pairs={{0,16},{1,17},{2,18},{3,19},{4,20},{5,21},{6,22},{7,23},{8,24},{9,... | collective-permute-start | bytes 786440 | tf_op jit(solution)/shard_map/ppermute | solution.py:368
  40.6 6.9 %collective-permute-done.10.refs_2_ = bf16[256,512]{1,0:T(8,128)(2,1)S(1)} collective-permute-done((bf16[256,512]{1,0:T(8,128)(2,1)S(1)}, bf16[256,512]{1,0:T(8,128)(2,1)S(1)}, u32[]{:S(2)}, u32[]{:S(2)}) %collective-permute-start.10) | collective-permute-done | bytes 262176 | tf_op jit(solution)/shard_map/ppermute | solution.py:368
  48.3 0.7 collective-permute-done.5.refs_4_
  49.0 1.1 shard_map.104
  50.1 1.1 shard_map.105
  51.2 1.5 %shard_map.107 = (f32[256,1024]{1,0:T(8,128)S(1)}, bf16[128,1024]{1,0:T(8,128)(2,1)S(1)}, bf16[128,1024]{1,0:T(8,128)(2,1)S(1)}, bf16[32,1024]{1,0:T(8,128)(2,1)...) custom-call(f32[256,1024]{1,0:T(8,128)S(1)} %get-tuple-element.64.re, ...), custom_call_target="tpu_custom_call" | custom-call | bytes 16384 | tf_op jit(solution)/shard_map/pallas_call | solution.py:464
  53.1 2.7 %collective-permute-start.16 = (bf16[32,1024]{1,0:T(8,128)(2,1)S(1)}, bf16[32,1024]{1,0:T(8,128)(2,1)S(1)}, u32[]{:S(2)}, u32[]{:S(2)}) collective-permute-start(bf16[32,1024]{1,0:T(8,128)(2,1)S(1)} %get-tuple-element.77), channel_id=1, source_target_pairs={{0,3},{1,2},{2,1},{3,0},{4,7},{5,6},{6,5},{7,4},{8,11},{9,10},{10,... | collective-permute-start | bytes 196616 | tf_op jit(solution)/shard_map/ppermute | solution.py:368
  55.9 1.0 collective-permute-start.17
  56.9 1.8 %collective-permute-start.18 = (bf16[32,1024]{1,0:T(8,128)(2,1)S(1)}, bf16[32,1024]{1,0:T(8,128)(2,1)S(1)}, u32[]{:S(2)}, u32[]{:S(2)}) collective-permute-start(bf16[32,1024]{1,0:T(8,128)(2,1)S(1)} %get-tuple-element.79), channel_id=1, source_target_pairs={{0,2},{1,3},{2,0},{3,1},{4,6},{5,7},{6,4},{7,5},{8,10},{9,11},{10,... | collective-permute-start | bytes 196616 | tf_op jit(solution)/shard_map/ppermute | solution.py:368
  58.6 2.5 %collective-permute-start.19 = (bf16[32,1024]{1,0:T(8,128)(2,1)S(1)}, bf16[32,1024]{1,0:T(8,128)(2,1)S(1)}, u32[]{:S(2)}, u32[]{:S(2)}) collective-permute-start(bf16[32,1024]{1,0:T(8,128)(2,1)S(1)} %get-tuple-element.80), channel_id=1, source_target_pairs={{0,6},{1,7},{2,4},{3,5},{4,2},{5,3},{6,0},{7,1},{8,14},{9,15},{10,... | collective-permute-start | bytes 196616 | tf_op jit(solution)/shard_map/ppermute | solution.py:368
  61.7 2.2 %collective-permute-start.21 = (bf16[32,1024]{1,0:T(8,128)(2,1)S(1)}, bf16[32,1024]{1,0:T(8,128)(2,1)S(1)}, u32[]{:S(2)}, u32[]{:S(2)}) collective-permute-start(bf16[32,1024]{1,0:T(8,128)(2,1)S(1)} %get-tuple-element.82), channel_id=1, source_target_pairs={{0,7},{1,6},{2,5},{3,4},{4,3},{5,2},{6,1},{7,0},{8,15},{9,14},{10,... | collective-permute-start | bytes 196616 | tf_op jit(solution)/shard_map/ppermute | solution.py:368
  63.9 0.9 collective-permute-done.19.refs_4_
  65.5 3.2 %collective-permute-done.21.refs_6_ = bf16[32,1024]{1,0:T(8,128)(2,1)S(1)} collective-permute-done((bf16[32,1024]{1,0:T(8,128)(2,1)S(1)}, bf16[32,1024]{1,0:T(8,128)(2,1)S(1)}, u32[]{:S(2)}, u32[]{:S(2)}) %collective-permute-start.21) | collective-permute-done | bytes 65568 | tf_op jit(solution)/shard_map/ppermute | solution.py:368
  68.7 1.3 %shard_map.109 = (f32[64,3200]{1,0:T(8,128)S(1)}, bf16[32,3200]{1,0:T(8,128)(2,1)S(1)}, bf16[32,3200]{1,0:T(8,128)(2,1)S(1)}) custom-call(bf16[32,1024]{1,0:T(8,128)(2,1)S(1)} %collective-permute-done.15.refs_0_, bf16[32,1024]{1,0:T(8,128)(2,1)S(1)} %collective-permute-done.16.refs_1_, bf16[32,1024]{1,0:T(8,128)(2,1)S(1)} %collective-permute-done.17.refs_2_, ...), custom_call_target="tpu_custom_call" | custom-call | bytes 1024 | tf_op jit(solution)/shard_map/pallas_call | solution.py:484
  70.5 0.9 collective-permute-done.24.refs_0_
  71.8 1.2 %collective-permute-start.26 = (bf16[16,3200]{1,0:T(8,128)(2,1)S(1)}, bf16[16,3200]{1,0:T(8,128)(2,1)S(1)}, u32[]{:S(2)}, u32[]{:S(2)}) collective-permute-start(bf16[16,3200]{1,0:T(8,128)(2,1)S(1)} %get-tuple-element.92), channel_id=1, source_target_pairs={{0,16},{1,17},{2,18},{3,19},{4,20},{5,21},{6,22},{7,23},{8,24},{9,... | collective-permute-start | bytes 307208 | tf_op jit(solution)/shard_map/ppermute | solution.py:368
  73.1 0.9 collective-permute-start.27
  73.9 3.7 %collective-permute-done.26.refs_0_ = bf16[16,3200]{1,0:T(8,128)(2,1)S(1)} collective-permute-done((bf16[16,3200]{1,0:T(8,128)(2,1)S(1)}, bf16[16,3200]{1,0:T(8,128)(2,1)S(1)}, u32[]{:S(2)}, u32[]{:S(2)}) %collective-permute-start.26) | collective-permute-done | bytes 102432 | tf_op jit(solution)/shard_map/ppermute | solution.py:368
  77.6 1.5 %collective-permute-done.27.refs_1_ = bf16[16,3200]{1,0:T(8,128)(2,1)S(1)} collective-permute-done((bf16[16,3200]{1,0:T(8,128)(2,1)S(1)}, bf16[16,3200]{1,0:T(8,128)(2,1)S(1)}, u32[]{:S(2)}, u32[]{:S(2)}) %collective-permute-start.27) | collective-permute-done | bytes 102432 | tf_op jit(solution)/shard_map/ppermute | solution.py:368
  79.3 1.2 %collective-permute-start.29 = (bf16[32,1536]{1,0:T(8,128)(2,1)S(1)}, bf16[32,1536]{1,0:T(8,128)(2,1)S(1)}, u32[]{:S(2)}, u32[]{:S(2)}) collective-permute-start(bf16[32,1536]{1,0:T(8,128)(2,1)S(1)} %shard_map.111.refs_0_), channel_id=1, source_target_pairs={{0,16},{1,17},{2,18},{3,19},{4,20},{5,21},{6,22},{7,23},{8,24},{9,... | collective-permute-start | bytes 294920 | tf_op jit(solution)/shard_map/ppermute | solution.py:368
  80.5 3.5 %collective-permute-done.22.first = bf16[128,1024]{1,0:T(8,128)(2,1)S(1)} collective-permute-done((bf16[128,1024]{1,0:T(8,128)(2,1)S(1)}, bf16[128,1024]{1,0:T(8,128)(2,1)S(1)}, u32[]{:S(2)}, u32[]{:S(2)}) %collective-permute-start.22) | collective-permute-done | bytes 262176 | tf_op jit(solution)/shard_map/ppermute | solution.py:368
  84.6 0.8 collective-permute-done.28.refs_1_
  85.5 0.7 shard_map.112
  86.2 3.0 %collective-permute-start.31 = (bf16[16,1024]{1,0:T(8,128)(2,1)S(1)}, bf16[16,1024]{1,0:T(8,128)(2,1)S(1)}, u32[]{:S(2)}, u32[]{:S(2)}) collective-permute-start(bf16[16,1024]{1,0:T(8,128)(2,1)S(1)} %get-tuple-element.95), channel_id=1, source_target_pairs={{0,4},{1,5},{2,6},{3,7},{4,0},{5,1},{6,2},{7,3},{8,12},{9,13},{10,... | collective-permute-start | bytes 98312 | tf_op jit(solution)/shard_map/ppermute | solution.py:368
  89.2 1.1 collective-permute-start.32
  90.3 2.8 %collective-permute-start.33 = (bf16[16,1024]{1,0:T(8,128)(2,1)S(1)}, bf16[16,1024]{1,0:T(8,128)(2,1)S(1)}, u32[]{:S(2)}, u32[]{:S(2)}) collective-permute-start(bf16[16,1024]{1,0:T(8,128)(2,1)S(1)} %get-tuple-element.97), channel_id=1, source_target_pairs={{0,5},{1,4},{2,7},{3,6},{4,1},{5,0},{6,3},{7,2},{8,13},{9,12},{10,... | collective-permute-start | bytes 98312 | tf_op jit(solution)/shard_map/ppermute | solution.py:368
  93.1 7.0 %collective-permute-done.23.second = bf16[128,1024]{1,0:T(8,128)(2,1)S(1)} collective-permute-done((bf16[128,1024]{1,0:T(8,128)(2,1)S(1)}, bf16[128,1024]{1,0:T(8,128)(2,1)S(1)}, u32[]{:S(2)}, u32[]{:S(2)}) %collective-permute-start.23) | collective-permute-done | bytes 262176 | tf_op jit(solution)/shard_map/ppermute | solution.py:368
  100.1 1.4 %collective-permute-start.35 = (bf16[16,1024]{1,0:T(8,128)(2,1)S(1)}, bf16[16,1024]{1,0:T(8,128)(2,1)S(1)}, u32[]{:S(2)}, u32[]{:S(2)}) collective-permute-start(bf16[16,1024]{1,0:T(8,128)(2,1)S(1)} %get-tuple-element.99), channel_id=1, source_target_pairs={{0,6},{1,7},{2,4},{3,5},{4,2},{5,3},{6,0},{7,1},{8,14},{9,15},{10,... | collective-permute-start | bytes 98312 | tf_op jit(solution)/shard_map/ppermute | solution.py:368
  101.5 1.4 %collective-permute-start.36 = (bf16[16,1024]{1,0:T(8,128)(2,1)S(1)}, bf16[16,1024]{1,0:T(8,128)(2,1)S(1)}, u32[]{:S(2)}, u32[]{:S(2)}) collective-permute-start(bf16[16,1024]{1,0:T(8,128)(2,1)S(1)} %get-tuple-element.100), channel_id=1, source_target_pairs={{0,1},{1,0},{2,3},{3,2},{4,5},{5,4},{6,7},{7,6},{8,9},{9,8},{10,11... | collective-permute-start | bytes 98312 | tf_op jit(solution)/shard_map/ppermute | solution.py:368
  103.0 2.5 %collective-permute-start.37 = (bf16[16,1024]{1,0:T(8,128)(2,1)S(1)}, bf16[16,1024]{1,0:T(8,128)(2,1)S(1)}, u32[]{:S(2)}, u32[]{:S(2)}) collective-permute-start(bf16[16,1024]{1,0:T(8,128)(2,1)S(1)} %get-tuple-element.101), channel_id=1, source_target_pairs={{0,7},{1,6},{2,5},{3,4},{4,3},{5,2},{6,1},{7,0},{8,15},{9,14},{10,... | collective-permute-start | bytes 98312 | tf_op jit(solution)/shard_map/ppermute | solution.py:368
  105.9 3.7 %collective-permute-done.37.refs_6_ = bf16[16,1024]{1,0:T(8,128)(2,1)S(1)} collective-permute-done((bf16[16,1024]{1,0:T(8,128)(2,1)S(1)}, bf16[16,1024]{1,0:T(8,128)(2,1)S(1)}, u32[]{:S(2)}, u32[]{:S(2)}) %collective-permute-start.37) | collective-permute-done | bytes 32800 | tf_op jit(solution)/shard_map/ppermute | solution.py:368
  109.6 1.1 shard_map.113
  (61 shorter events, 6.8 us)
Async XLA Ops:
  0.0 30.2 %collective-permute-start.6 = (bf16[512,1024]{1,0:T(8,128)(2,1)}, bf16[512,1024]{1,0:T(8,128)(2,1)S(1)}, u32[]{:S(2)}, u32[]{:S(2)}) collective-permute-start(bf16[512,1024]{1,0:T(8,128)(2,1)} %refs_0_.1), channel_id=1, source_target_pairs={{0,1},{1,0},{2,3},{3,2},{4,5},{5,4},{6,7},{7,6},{8,9},{9,8},{10,11... | collective-permute-start | bytes 3145736 | tf_op jit(solution)/shard_map/ppermute | solution.py:368
  2.9 29.0 %collective-permute-start.7 = (bf16[512,1024]{1,0:T(8,128)(2,1)}, bf16[512,1024]{1,0:T(8,128)(2,1)S(1)}, u32[]{:S(2)}, u32[]{:S(2)}) collective-permute-start(bf16[512,1024]{1,0:T(8,128)(2,1)} %refs_0_.1), channel_id=1, source_target_pairs={{0,2},{1,3},{2,0},{3,1},{4,6},{5,7},{6,4},{7,5},{8,10},{9,11},{10,... | collective-permute-start | bytes 3145736 | tf_op jit(solution)/shard_map/ppermute | solution.py:368
  6.0 9.3 %collective-permute-start = (bf16[64,2048]{1,0:T(8,128)(2,1)S(1)}, bf16[64,2048]{1,0:T(8,128)(2,1)S(1)}, u32[]{:S(2)}, u32[]{:S(2)}) collective-permute-start(bf16[64,2048]{1,0:T(8,128)(2,1)S(1)} %get-tuple-element.54), channel_id=1, source_target_pairs={{0,16},{1,17},{2,18},{3,19},{4,20},{5,21},{6,22},{7,23},{8,24},{9,... | collective-permute-start | bytes 786440 | tf_op jit(solution)/shard_map/ppermute | solution.py:368
  7.6 10.6 %collective-permute-start.1 = (bf16[64,2048]{1,0:T(8,128)(2,1)S(1)}, bf16[64,2048]{1,0:T(8,128)(2,1)S(1)}, u32[]{:S(2)}, u32[]{:S(2)}) collective-permute-start(bf16[64,2048]{1,0:T(8,128)(2,1)S(1)} %get-tuple-element.55), channel_id=1, source_target_pairs={{0,24},{1,25},{2,26},{3,27},{4,28},{5,29},{6,30},{7,31},{8,16},{9,... | collective-permute-start | bytes 786440 | tf_op jit(solution)/shard_map/ppermute | solution.py:368
  7.6 10.6 %collective-permute-start.2 = (bf16[64,2048]{1,0:T(8,128)(2,1)S(1)}, bf16[64,2048]{1,0:T(8,128)(2,1)S(1)}, u32[]{:S(2)}, u32[]{:S(2)}) collective-permute-start(bf16[64,2048]{1,0:T(8,128)(2,1)S(1)} %get-tuple-element.56), channel_id=1, source_target_pairs={{0,8},{1,9},{2,10},{3,11},{4,12},{5,13},{6,14},{7,15},{8,0},{9,1},... | collective-permute-start | bytes 786440 | tf_op jit(solution)/shard_map/ppermute | solution.py:368
  22.8 9.1 %collective-permute-start.4 = (bf16[256,512]{1,0:T(8,128)(2,1)S(1)}, bf16[256,512]{1,0:T(8,128)(2,1)S(1)}, u32[]{:S(2)}, u32[]{:S(2)}) collective-permute-start(bf16[256,512]{1,0:T(8,128)(2,1)S(1)} %shard_map.102.refs_1_), channel_id=1, source_target_pairs={{0,16},{1,17},{2,18},{3,19},{4,20},{5,21},{6,22},{7,23},{8,24},{9,... | collective-permute-start | bytes 786440 | tf_op jit(solution)/shard_map/ppermute | solution.py:368
  23.6 15.2 %collective-permute-start.8 = (bf16[256,512]{1,0:T(8,128)(2,1)S(1)}, bf16[256,512]{1,0:T(8,128)(2,1)S(1)}, u32[]{:S(2)}, u32[]{:S(2)}) collective-permute-start(bf16[256,512]{1,0:T(8,128)(2,1)S(1)} %get-tuple-element.58), channel_id=1, source_target_pairs={{0,4},{1,5},{2,6},{3,7},{4,0},{5,1},{6,2},{7,3},{8,12},{9,13},{10,... | collective-permute-start | bytes 786440 | tf_op jit(solution)/shard_map/ppermute | solution.py:368
  26.2 1.2 %copy-start.1 = (bf16[512,1024]{1,0:T(8,128)(2,1)S(1)}, bf16[512,1024]{1,0:T(8,128)(2,1)}, u32[]{:S(2)}) copy-start(bf16[512,1024]{1,0:T(8,128)(2,1)} %refs_0_.1) | copy-start | bytes 3145732
  27.4 1.0 copy-start.2
  28.5 0.7 copy-start.3
  29.2 0.7 copy-start.4
  30.3 17.2 %collective-permute-start.11 = (bf16[512,384]{1,0:T(8,128)(2,1)S(1)}, bf16[512,384]{1,0:T(8,128)(2,1)S(1)}, u32[]{:S(2)}, u32[]{:S(2)}) collective-permute-start(bf16[512,384]{1,0:T(8,128)(2,1)S(1)} %slice.6), channel_id=1, source_target_pairs={{0,2},{1,3},{2,0},{3,1},{4,6},{5,7},{6,4},{7,5},{8,10},{9,11},{10,... | collective-permute-start | bytes 1179656 | tf_op jit(solution)/shard_map/ppermute | solution.py:368
  32.0 19.1 %collective-permute-start.13 = (bf16[512,640]{1,0:T(8,128)(2,1)S(1)}, bf16[512,640]{1,0:T(8,128)(2,1)S(1)}, u32[]{:S(2)}, u32[]{:S(2)}) collective-permute-start(bf16[512,640]{1,0:T(8,128)(2,1)S(1)} %slice.7), channel_id=1, source_target_pairs={{0,1},{1,0},{2,3},{3,2},{4,5},{5,4},{6,7},{7,6},{8,9},{9,8},{10,11... | collective-permute-start | bytes 1966088 | tf_op jit(solution)/shard_map/ppermute | solution.py:368
  38.9 8.6 %collective-permute-start.10 = (bf16[256,512]{1,0:T(8,128)(2,1)S(1)}, bf16[256,512]{1,0:T(8,128)(2,1)S(1)}, u32[]{:S(2)}, u32[]{:S(2)}) collective-permute-start(bf16[256,512]{1,0:T(8,128)(2,1)S(1)} %collective-permute-done.8.refs_0_), channel_id=1, source_target_pairs={{0,16},{1,17},{2,18},{3,19},{4,20},{5,21},{6,22},{7,23},{8,24},{9,... | collective-permute-start | bytes 786440 | tf_op jit(solution)/shard_map/ppermute | solution.py:368
  40.6 7.4 %collective-permute-start.14 = (s32[4,8,64]{2,1,0:T(8,128)S(1)}, s32[4,8,64]{2,1,0:T(8,128)S(1)}, u32[]{:S(2)}, u32[]{:S(2)}) collective-permute-start(s32[4,8,64]{2,1,0:T(8,128)S(1)} %bitcast.23), channel_id=1, source_target_pairs={{0,4},{1,5},{2,6},{3,7},{4,0},{5,1},{6,2},{7,3},{8,12},{9,13},{10,... | collective-permute-start | bytes 24584 | tf_op jit(solution)/shard_map/ppermute | solution.py:368
  40.6 7.7 %collective-permute-start.3 = (bf16[256,512]{1,0:T(8,128)(2,1)S(1)}, bf16[256,512]{1,0:T(8,128)(2,1)S(1)}, u32[]{:S(2)}, u32[]{:S(2)}) collective-permute-start(bf16[256,512]{1,0:T(8,128)(2,1)S(1)} %shard_map.102.refs_1_), channel_id=1, source_target_pairs={{0,8},{1,9},{2,10},{3,11},{4,12},{5,13},{6,14},{7,15},{8,0},{9,1},... | collective-permute-start | bytes 786440 | tf_op jit(solution)/shard_map/ppermute | solution.py:368
  47.5 1.5 %collective-permute-start.5 = (bf16[256,512]{1,0:T(8,128)(2,1)S(1)}, bf16[256,512]{1,0:T(8,128)(2,1)S(1)}, u32[]{:S(2)}, u32[]{:S(2)}) collective-permute-start(bf16[256,512]{1,0:T(8,128)(2,1)S(1)} %collective-permute-done.4.refs_3_), channel_id=1, source_target_pairs={{0,8},{1,9},{2,10},{3,11},{4,12},{5,13},{6,14},{7,15},{8,0},{9,1},... | collective-permute-start | bytes 786440 | tf_op jit(solution)/shard_map/ppermute | solution.py:368
  47.5 2.6 %collective-permute-start.9 = (bf16[256,512]{1,0:T(8,128)(2,1)S(1)}, bf16[256,512]{1,0:T(8,128)(2,1)S(1)}, u32[]{:S(2)}, u32[]{:S(2)}) collective-permute-start(bf16[256,512]{1,0:T(8,128)(2,1)S(1)} %collective-permute-done.8.refs_0_), channel_id=1, source_target_pairs={{0,8},{1,9},{2,10},{3,11},{4,12},{5,13},{6,14},{7,15},{8,0},{9,1},... | collective-permute-start | bytes 786440 | tf_op jit(solution)/shard_map/ppermute | solution.py:368
  48.0 2.1 %collective-permute-start.12 = (bf16[256,512]{1,0:T(8,128)(2,1)S(1)}, bf16[256,512]{1,0:T(8,128)(2,1)S(1)}, u32[]{:S(2)}, u32[]{:S(2)}) collective-permute-start(bf16[256,512]{1,0:T(8,128)(2,1)S(1)} %collective-permute-done.10.refs_2_), channel_id=1, source_target_pairs={{0,8},{1,9},{2,10},{3,11},{4,12},{5,13},{6,14},{7,15},{8,0},{9,1},... | collective-permute-start | bytes 786440 | tf_op jit(solution)/shard_map/ppermute | solution.py:368
  49.0 19.7 %slice-start = ((s8[6291456]{0:T(1024)(128)(4,1)}), s8[4194304]{0:T(1024)(128)(4,1)S(1)}, s32[]{:S(2)}) async-start(s8[6291456]{0:T(1024)(128)(4,1)} %bitcast.16), calls=%async_computation | async-start | bytes 8388608
  49.0 19.7 %copy-start.5 = (f32[1024]{0:T(1024)S(1)}, f32[1024]{0:T(1024)}, u32[]{:S(2)}) copy-start(f32[1024]{0:T(1024)} %param.15) | copy-start | bytes 12292
  50.1 18.6 %slice-start.1 = ((s8[6291456]{0:T(1024)(128)(4,1)}), s8[2097152]{0:T(1024)(128)(4,1)S(1)}, s32[]{:S(2)}) async-start(s8[6291456]{0:T(1024)(128)(4,1)} %bitcast.16), calls=%async_computation.1 | async-start | bytes 4194304
  51.2 34.3 %copy-start = (bf16[1,1536,1024]{2,1,0:T(8,128)(2,1)S(1)}, bf16[1,1536,1024]{2,1,0:T(8,128)(2,1)}, u32[]{:S(2)}) copy-start(bf16[1,1536,1024]{2,1,0:T(8,128)(2,1)} %param.19) | copy-start | bytes 9437188
  52.7 8.5 %collective-permute-start.15 = (bf16[32,1024]{1,0:T(8,128)(2,1)S(1)}, bf16[32,1024]{1,0:T(8,128)(2,1)S(1)}, u32[]{:S(2)}, u32[]{:S(2)}) collective-permute-start(bf16[32,1024]{1,0:T(8,128)(2,1)S(1)} %get-tuple-element.76), channel_id=1, source_target_pairs={{0,4},{1,5},{2,6},{3,7},{4,0},{5,1},{6,2},{7,3},{8,12},{9,13},{10,... | collective-permute-start | bytes 196616 | tf_op jit(solution)/shard_map/ppermute | solution.py:368
  53.1 8.6 %collective-permute-start.16 = (bf16[32,1024]{1,0:T(8,128)(2,1)S(1)}, bf16[32,1024]{1,0:T(8,128)(2,1)S(1)}, u32[]{:S(2)}, u32[]{:S(2)}) collective-permute-start(bf16[32,1024]{1,0:T(8,128)(2,1)S(1)} %get-tuple-element.77), channel_id=1, source_target_pairs={{0,3},{1,2},{2,1},{3,0},{4,7},{5,6},{6,5},{7,4},{8,11},{9,10},{10,... | collective-permute-start | bytes 196616 | tf_op jit(solution)/shard_map/ppermute | solution.py:368
  55.9 8.1 %collective-permute-start.17 = (bf16[32,1024]{1,0:T(8,128)(2,1)S(1)}, bf16[32,1024]{1,0:T(8,128)(2,1)S(1)}, u32[]{:S(2)}, u32[]{:S(2)}) collective-permute-start(bf16[32,1024]{1,0:T(8,128)(2,1)S(1)} %get-tuple-element.78), channel_id=1, source_target_pairs={{0,5},{1,4},{2,7},{3,6},{4,1},{5,0},{6,3},{7,2},{8,13},{9,12},{10,... | collective-permute-start | bytes 196616 | tf_op jit(solution)/shard_map/ppermute | solution.py:368
  56.9 7.1 %collective-permute-start.18 = (bf16[32,1024]{1,0:T(8,128)(2,1)S(1)}, bf16[32,1024]{1,0:T(8,128)(2,1)S(1)}, u32[]{:S(2)}, u32[]{:S(2)}) collective-permute-start(bf16[32,1024]{1,0:T(8,128)(2,1)S(1)} %get-tuple-element.79), channel_id=1, source_target_pairs={{0,2},{1,3},{2,0},{3,1},{4,6},{5,7},{6,4},{7,5},{8,10},{9,11},{10,... | collective-permute-start | bytes 196616 | tf_op jit(solution)/shard_map/ppermute | solution.py:368
  58.6 6.2 %collective-permute-start.19 = (bf16[32,1024]{1,0:T(8,128)(2,1)S(1)}, bf16[32,1024]{1,0:T(8,128)(2,1)S(1)}, u32[]{:S(2)}, u32[]{:S(2)}) collective-permute-start(bf16[32,1024]{1,0:T(8,128)(2,1)S(1)} %get-tuple-element.80), channel_id=1, source_target_pairs={{0,6},{1,7},{2,4},{3,5},{4,2},{5,3},{6,0},{7,1},{8,14},{9,15},{10,... | collective-permute-start | bytes 196616 | tf_op jit(solution)/shard_map/ppermute | solution.py:368
  61.2 4.3 %collective-permute-start.20 = (bf16[32,1024]{1,0:T(8,128)(2,1)S(1)}, bf16[32,1024]{1,0:T(8,128)(2,1)S(1)}, u32[]{:S(2)}, u32[]{:S(2)}) collective-permute-start(bf16[32,1024]{1,0:T(8,128)(2,1)S(1)} %get-tuple-element.81), channel_id=1, source_target_pairs={{0,1},{1,0},{2,3},{3,2},{4,5},{5,4},{6,7},{7,6},{8,9},{9,8},{10,11... | collective-permute-start | bytes 196616 | tf_op jit(solution)/shard_map/ppermute | solution.py:368
  61.7 7.0 %collective-permute-start.21 = (bf16[32,1024]{1,0:T(8,128)(2,1)S(1)}, bf16[32,1024]{1,0:T(8,128)(2,1)S(1)}, u32[]{:S(2)}, u32[]{:S(2)}) collective-permute-start(bf16[32,1024]{1,0:T(8,128)(2,1)S(1)} %get-tuple-element.82), channel_id=1, source_target_pairs={{0,7},{1,6},{2,5},{3,4},{4,3},{5,2},{6,1},{7,0},{8,15},{9,14},{10,... | collective-permute-start | bytes 196616 | tf_op jit(solution)/shard_map/ppermute | solution.py:368
  70.0 1.5 %collective-permute-start.24 = (bf16[32,3200]{1,0:T(8,128)(2,1)S(1)}, bf16[32,3200]{1,0:T(8,128)(2,1)S(1)}, u32[]{:S(2)}, u32[]{:S(2)}) collective-permute-start(bf16[32,3200]{1,0:T(8,128)(2,1)S(1)} %get-tuple-element.89), channel_id=1, source_target_pairs={{0,8},{1,9},{2,10},{3,11},{4,12},{5,13},{6,14},{7,15},{8,0},{9,1},... | collective-permute-start | bytes 614408 | tf_op jit(solution)/shard_map/ppermute | solution.py:368
  70.0 1.7 %collective-permute-start.25 = (bf16[32,3200]{1,0:T(8,128)(2,1)S(1)}, bf16[32,3200]{1,0:T(8,128)(2,1)S(1)}, u32[]{:S(2)}, u32[]{:S(2)}) collective-permute-start(bf16[32,3200]{1,0:T(8,128)(2,1)S(1)} %get-tuple-element.90), channel_id=1, source_target_pairs={{0,8},{1,9},{2,10},{3,11},{4,12},{5,13},{6,14},{7,15},{8,0},{9,1},... | collective-permute-start | bytes 614408 | tf_op jit(solution)/shard_map/ppermute | solution.py:368
  70.5 13.5 %collective-permute-start.22 = (bf16[128,1024]{1,0:T(8,128)(2,1)S(1)}, bf16[128,1024]{1,0:T(8,128)(2,1)S(1)}, u32[]{:S(2)}, u32[]{:S(2)}) collective-permute-start(bf16[128,1024]{1,0:T(8,128)(2,1)S(1)} %get-tuple-element.84), channel_id=1, source_target_pairs={{0,4},{1,5},{2,6},{3,7},{4,0},{5,1},{6,2},{7,3},{8,12},{9,13},{10,... | collective-permute-start | bytes 786440 | tf_op jit(solution)/shard_map/ppermute | solution.py:368
  71.8 5.8 %collective-permute-start.26 = (bf16[16,3200]{1,0:T(8,128)(2,1)S(1)}, bf16[16,3200]{1,0:T(8,128)(2,1)S(1)}, u32[]{:S(2)}, u32[]{:S(2)}) collective-permute-start(bf16[16,3200]{1,0:T(8,128)(2,1)S(1)} %get-tuple-element.92), channel_id=1, source_target_pairs={{0,16},{1,17},{2,18},{3,19},{4,20},{5,21},{6,22},{7,23},{8,24},{9,... | collective-permute-start | bytes 307208 | tf_op jit(solution)/shard_map/ppermute | solution.py:368
  73.1 6.0 %collective-permute-start.27 = (bf16[16,3200]{1,0:T(8,128)(2,1)S(1)}, bf16[16,3200]{1,0:T(8,128)(2,1)S(1)}, u32[]{:S(2)}, u32[]{:S(2)}) collective-permute-start(bf16[16,3200]{1,0:T(8,128)(2,1)S(1)} %get-tuple-element.93), channel_id=1, source_target_pairs={{0,16},{1,17},{2,18},{3,19},{4,20},{5,21},{6,22},{7,23},{8,24},{9,... | collective-permute-start | bytes 307208 | tf_op jit(solution)/shard_map/ppermute | solution.py:368
  79.3 4.8 %collective-permute-start.29 = (bf16[32,1536]{1,0:T(8,128)(2,1)S(1)}, bf16[32,1536]{1,0:T(8,128)(2,1)S(1)}, u32[]{:S(2)}, u32[]{:S(2)}) collective-permute-start(bf16[32,1536]{1,0:T(8,128)(2,1)S(1)} %shard_map.111.refs_0_), channel_id=1, source_target_pairs={{0,16},{1,17},{2,18},{3,19},{4,20},{5,21},{6,22},{7,23},{8,24},{9,... | collective-permute-start | bytes 294920 | tf_op jit(solution)/shard_map/ppermute | solution.py:368
  84.0 16.1 %collective-permute-start.23 = (bf16[128,1024]{1,0:T(8,128)(2,1)S(1)}, bf16[128,1024]{1,0:T(8,128)(2,1)S(1)}, u32[]{:S(2)}, u32[]{:S(2)}) collective-permute-start(bf16[128,1024]{1,0:T(8,128)(2,1)S(1)} %get-tuple-element.86), channel_id=1, source_target_pairs={{0,4},{1,5},{2,6},{3,7},{4,0},{5,1},{6,2},{7,3},{8,12},{9,13},{10,... | collective-permute-start | bytes 786440 | tf_op jit(solution)/shard_map/ppermute | solution.py:368
  84.0 1.3 %collective-permute-start.28 = (bf16[32,1536]{1,0:T(8,128)(2,1)S(1)}, bf16[32,1536]{1,0:T(8,128)(2,1)S(1)}, u32[]{:S(2)}, u32[]{:S(2)}) collective-permute-start(bf16[32,1536]{1,0:T(8,128)(2,1)S(1)} %shard_map.111.refs_0_), channel_id=1, source_target_pairs={{0,8},{1,9},{2,10},{3,11},{4,12},{5,13},{6,14},{7,15},{8,0},{9,1},... | collective-permute-start | bytes 294920 | tf_op jit(solution)/shard_map/ppermute | solution.py:368
  84.1 1.4 %collective-permute-start.30 = (bf16[32,1536]{1,0:T(8,128)(2,1)S(1)}, bf16[32,1536]{1,0:T(8,128)(2,1)S(1)}, u32[]{:S(2)}, u32[]{:S(2)}) collective-permute-start(bf16[32,1536]{1,0:T(8,128)(2,1)S(1)} %collective-permute-done.29.refs_2_), channel_id=1, source_target_pairs={{0,8},{1,9},{2,10},{3,11},{4,12},{5,13},{6,14},{7,15},{8,0},{9,1},... | collective-permute-start | bytes 294920 | tf_op jit(solution)/shard_map/ppermute | solution.py:368
  86.2 15.3 %collective-permute-start.31 = (bf16[16,1024]{1,0:T(8,128)(2,1)S(1)}, bf16[16,1024]{1,0:T(8,128)(2,1)S(1)}, u32[]{:S(2)}, u32[]{:S(2)}) collective-permute-start(bf16[16,1024]{1,0:T(8,128)(2,1)S(1)} %get-tuple-element.95), channel_id=1, source_target_pairs={{0,4},{1,5},{2,6},{3,7},{4,0},{5,1},{6,2},{7,3},{8,12},{9,13},{10,... | collective-permute-start | bytes 98312 | tf_op jit(solution)/shard_map/ppermute | solution.py:368
  89.2 13.8 %collective-permute-start.32 = (bf16[16,1024]{1,0:T(8,128)(2,1)S(1)}, bf16[16,1024]{1,0:T(8,128)(2,1)S(1)}, u32[]{:S(2)}, u32[]{:S(2)}) collective-permute-start(bf16[16,1024]{1,0:T(8,128)(2,1)S(1)} %get-tuple-element.96), channel_id=1, source_target_pairs={{0,3},{1,2},{2,1},{3,0},{4,7},{5,6},{6,5},{7,4},{8,11},{9,10},{10,... | collective-permute-start | bytes 98312 | tf_op jit(solution)/shard_map/ppermute | solution.py:368
  90.3 15.3 %collective-permute-start.33 = (bf16[16,1024]{1,0:T(8,128)(2,1)S(1)}, bf16[16,1024]{1,0:T(8,128)(2,1)S(1)}, u32[]{:S(2)}, u32[]{:S(2)}) collective-permute-start(bf16[16,1024]{1,0:T(8,128)(2,1)S(1)} %get-tuple-element.97), channel_id=1, source_target_pairs={{0,5},{1,4},{2,7},{3,6},{4,1},{5,0},{6,3},{7,2},{8,13},{9,12},{10,... | collective-permute-start | bytes 98312 | tf_op jit(solution)/shard_map/ppermute | solution.py:368
  93.1 12.5 %collective-permute-start.34 = (bf16[16,1024]{1,0:T(8,128)(2,1)S(1)}, bf16[16,1024]{1,0:T(8,128)(2,1)S(1)}, u32[]{:S(2)}, u32[]{:S(2)}) collective-permute-start(bf16[16,1024]{1,0:T(8,128)(2,1)S(1)} %get-tuple-element.98), channel_id=1, source_target_pairs={{0,2},{1,3},{2,0},{3,1},{4,6},{5,7},{6,4},{7,5},{8,10},{9,11},{10,... | collective-permute-start | bytes 98312 | tf_op jit(solution)/shard_map/ppermute | solution.py:368
  100.1 5.7 %collective-permute-start.35 = (bf16[16,1024]{1,0:T(8,128)(2,1)S(1)}, bf16[16,1024]{1,0:T(8,128)(2,1)S(1)}, u32[]{:S(2)}, u32[]{:S(2)}) collective-permute-start(bf16[16,1024]{1,0:T(8,128)(2,1)S(1)} %get-tuple-element.99), channel_id=1, source_target_pairs={{0,6},{1,7},{2,4},{3,5},{4,2},{5,3},{6,0},{7,1},{8,14},{9,15},{10,... | collective-permute-start | bytes 98312 | tf_op jit(solution)/shard_map/ppermute | solution.py:368
  101.5 4.3 %collective-permute-start.36 = (bf16[16,1024]{1,0:T(8,128)(2,1)S(1)}, bf16[16,1024]{1,0:T(8,128)(2,1)S(1)}, u32[]{:S(2)}, u32[]{:S(2)}) collective-permute-start(bf16[16,1024]{1,0:T(8,128)(2,1)S(1)} %get-tuple-element.100), channel_id=1, source_target_pairs={{0,1},{1,0},{2,3},{3,2},{4,5},{5,4},{6,7},{7,6},{8,9},{9,8},{10,11... | collective-permute-start | bytes 98312 | tf_op jit(solution)/shard_map/ppermute | solution.py:368
  103.0 6.6 %collective-permute-start.37 = (bf16[16,1024]{1,0:T(8,128)(2,1)S(1)}, bf16[16,1024]{1,0:T(8,128)(2,1)S(1)}, u32[]{:S(2)}, u32[]{:S(2)}) collective-permute-start(bf16[16,1024]{1,0:T(8,128)(2,1)S(1)} %get-tuple-element.101), channel_id=1, source_target_pairs={{0,7},{1,6},{2,5},{3,4},{4,3},{5,2},{6,1},{7,0},{8,15},{9,14},{10,... | collective-permute-start | bytes 98312 | tf_op jit(solution)/shard_map/ppermute | solution.py:368

commit v16 on v15

--- a/solution.py
+++ b/solution.py
@@ -77,12 +77,7 @@
 
 
 def all_hops(E):
-    far = [b for b in range(E) if b & PAIR]
-    near = [b for b in reversed(range(1, E)) if not b & PAIR]
-    order = []
-    for i, b in enumerate(far):
-        order += [b, *near[i : i + 1]]
-    return [*order, 0]
+    return [b for b in range(E) if b & PAIR] + [b for b in reversed(range(E)) if not b & PAIR]
 
 
 def pack_kernel(C, qw, q_ref, new_ref, past_ref, *refs):
@@ -207,8 +202,7 @@
 
 def last_kernel(E, cap, *refs):
     accs, lasts, ws, places = refs[:2], refs[2:4], refs[4:6], refs[6:8]
-    own_ref, first_ref, second_ref, *outs = refs[8:]
-    few = first_ref.shape[0]
+    own_ref, full_ref, *outs = refs[8:]
     cut = ws[0].shape[1]
     for j, cols in enumerate((slice(0, cut), slice(cut, own_ref.shape[1]))):
         for t in (1, 0):
@@ -217,8 +211,7 @@
             if t == 0:
                 own_ref[:, cols] = total
             else:
-                first_ref[:, cols] = rounded[:few]
-                second_ref[:, cols] = rounded[few:]
+                full_ref[:, cols] = rounded
             picked = dot(places[t][...], rounded).astype(BF16)
             for out, b in zip(outs, all_hops(E)):
                 at = (b ^ (PAIR * t)) * cap
@@ -315,10 +308,8 @@
         out[...] = part_s[pl.ds(at, cap), :]
 
 
-def mix_kernel(own, first, second, out):
-    few = first.shape[0]
-    out[:few, :] = own[:few, :] + first[...].astype(F32)
-    out[few:, :] = own[few:, :] + second[...].astype(F32)
+def mix_kernel(own, got, out):
+    out[...] = own[...] + got[...].astype(F32)
 
 
 def combine_kernel(E, cap, mixed, place_ref, gate_ref, *refs):
@@ -460,21 +451,18 @@
     theirs_all = gather(after(theirs, place, shards[1]), lambda: quarter)
     acc_far, last_far = project(theirs_all)
     gain = norm_gain.reshape(1, width)
-    few = rows // 2
-    own, first, second, *outgoing = call(
+    own, full, *outgoing = call(
         functools.partial(last_kernel, E, cap),
         [
             sds((rows, width), F32),
-            sds((few, width), BF16),
-            sds((rows - few, width), BF16),
+            sds((rows, width), BF16),
         ]
         + [sds((2 * cap, width), BF16)] * E,
         8,
         cost=(0, 2**14),
     )(acc, acc_far, last, last_far, *shards[C - 1], place, other_place)
     incoming = [permute(x, exp=b) if b else x for x, b in zip(outgoing, all_hops(E))]
-    first = permute(after(first, *incoming), exp=PAIR)
-    second = permute(after(second, first), exp=PAIR)
+    arrived = permute(after(full, *incoming), exp=PAIR)
 
     order = [0]
     bit = C // 2
@@ -505,7 +493,7 @@
         cost=(0, 2**10),
     )(keep, *[permute(x, ctx=bit) for x in sends])
     acts = {0: activated}
-    acts[bit] = after(permute(activated, ctx=bit), first)
+    acts[bit] = permute(activated, ctx=bit)
     bit //= 2
     while bit:
         for r in list(acts):
@@ -519,7 +507,7 @@
         cost=(2 * slots * width * hidden, 2 * width * hidden),
     )(acts[0], *[acts[s] for s in range(1, C)], w_down.reshape(hidden, width))
     returned = [permute(x, exp=b) if b else x for x, b in zip(expert_out, all_hops(E))]
-    mixed = call(mix_kernel, sds((rows, width), F32), 3, cost=(0, 2**14))(own, first, second)
+    mixed = call(mix_kernel, sds((rows, width), F32), 2, cost=(0, 2**14))(own, arrived)
     columns = min(4, width // 128)
     result = call(
         functools.partial(combine_kernel, E, cap),

time: 111 us -> 108 us (0.973)
  starting transfers between devices: 41.3 us -> 38 us
    ppermute x38 -> x37, starting transfers between devices: 41.3 us -> 38 us  [permute(): return lax.ppermute(x, ('ctx', 'exp'), pairs)]
    ppermute x38 -> x37, waiting for transfers between devices: 51.7 us -> 51.4 us  [permute(): return lax.ppermute(x, ('ctx', 'exp'), pairs)]
  transfers between devices with their start and end apart: 38 -> 37, of which waited for: 19 -> 21; matrix products, arithmetic and copies ran while one was open for 0% -> 0% of each run, Pallas kernels for 9% -> 9%
where the time goes in v16:
time: 108 us; the launch traced here: 107 us
  waiting for transfers between devices  51.4 us (48%)
  starting transfers between devices  38 us (35%)
  Pallas kernels  13.7 us (13%)
  local copies, waits for them, and re-layouts  3.83 us (4%)
    ppermute x37, waiting for transfers between devices, permute(): return lax.ppermute(x, ('ctx', 'exp'), pairs)  51.4 us
    ppermute x37, starting transfers between devices, permute(): return lax.ppermute(x, ('ctx', 'exp'), pairs)  38 us
    pallas_call x2, Pallas kernels, attend(): call(functools.partial(attend_kernel, C, t), [sds((rows, qw), BF16)] + [s...  4.65 us
    unnamed x16, local copies, waits for them, and re-layouts  3.72 us
  transfers between devices with their start and end apart: 37, of which 21 were waited for; matrix products, arithmetic and copies ran while one was open for 0% of the time, Pallas kernels for 9%

profile of v16, /device:TPU:0, one launch (start us, length us, event | category | flops | bytes accessed | tf_op | source)
XLA Modules:
  0.0 107.1 jit_solution(17626944672656425102)
XLA Ops:
  0.0 2.9 %collective-permute-start.6 = (bf16[512,1024]{1,0:T(8,128)(2,1)}, bf16[512,1024]{1,0:T(8,128)(2,1)S(1)}, u32[]{:S(2)}, u32[]{:S(2)}) collective-permute-start(bf16[512,1024]{1,0:T(8,128)(2,1)} %refs_0_.1), channel_id=1, source_target_pairs={{0,1},{1,0},{2,3},{3,2},{4,5},{5,4},{6,7},{7,6},{8,9},{9,8},{10,11... | collective-permute-start | bytes 3145736 | tf_op jit(solution)/shard_map/ppermute | solution.py:359
  2.9 1.6 %collective-permute-start.7 = (bf16[512,1024]{1,0:T(8,128)(2,1)}, bf16[512,1024]{1,0:T(8,128)(2,1)S(1)}, u32[]{:S(2)}, u32[]{:S(2)}) collective-permute-start(bf16[512,1024]{1,0:T(8,128)(2,1)} %refs_0_.1), channel_id=1, source_target_pairs={{0,2},{1,3},{2,0},{3,1},{4,6},{5,7},{6,4},{7,5},{8,10},{9,11},{10,... | collective-permute-start | bytes 3145736 | tf_op jit(solution)/shard_map/ppermute | solution.py:359
  4.5 1.4 %shard_map.100 = (bf16[64,2048]{1,0:T(8,128)(2,1)S(1)}, bf16[64,2048]{1,0:T(8,128)(2,1)S(1)}, bf16[64,2048]{1,0:T(8,128)(2,1)S(1)}, bf16[64,2048]{1,0:T(8,128)(2,1)S(1)}) custom-call(bf16[64,4096]{1,0:T(8,128)(2,1)} %bitcast.25, bf16[64,512]{1,0:T(8,128)(2,1)} %bitcast.26, bf16[64,512]{1,0:T(8,128)(2,1)} %bitcast.27), custom_call_target="tpu_custom_call" | custom-call | bytes 1048576 | tf_op jit(solution)/shard_map/pallas_call | solution.py:365
  6.0 1.6 %collective-permute-start = (bf16[64,2048]{1,0:T(8,128)(2,1)S(1)}, bf16[64,2048]{1,0:T(8,128)(2,1)S(1)}, u32[]{:S(2)}, u32[]{:S(2)}) collective-permute-start(bf16[64,2048]{1,0:T(8,128)(2,1)S(1)} %get-tuple-element.51), channel_id=1, source_target_pairs={{0,16},{1,17},{2,18},{3,19},{4,20},{5,21},{6,22},{7,23},{8,24},{9,... | collective-permute-start | bytes 786440 | tf_op jit(solution)/shard_map/ppermute | solution.py:359
  8.2 7.1 %collective-permute-done.refs_0_ = bf16[64,2048]{1,0:T(8,128)(2,1)S(1)} collective-permute-done((bf16[64,2048]{1,0:T(8,128)(2,1)S(1)}, bf16[64,2048]{1,0:T(8,128)(2,1)S(1)}, u32[]{:S(2)}, u32[]{:S(2)}) %collective-permute-start) | collective-permute-done | bytes 262176 | tf_op jit(solution)/shard_map/ppermute | solution.py:359
  15.3 2.9 %collective-permute-done.1.refs_1_ = bf16[64,2048]{1,0:T(8,128)(2,1)S(1)} collective-permute-done((bf16[64,2048]{1,0:T(8,128)(2,1)S(1)}, bf16[64,2048]{1,0:T(8,128)(2,1)S(1)}, u32[]{:S(2)}, u32[]{:S(2)}) %collective-permute-start.1) | collective-permute-done | bytes 262176 | tf_op jit(solution)/shard_map/ppermute | solution.py:359
  18.2 2.3 %shard_map.101 = (bf16[256,512]{1,0:T(8,128)(2,1)S(1)}, bf16[64,2048]{1,0:T(8,128)(2,1)S(1)}) custom-call(bf16[64,2048]{1,0:T(8,128)(2,1)S(1)} %collective-permute-done.refs_0_, bf16[64,2048]{1,0:T(8,128)(2,1)S(1)} %collective-permute-done.1.refs_1_, bf16[64,2048]{1,0:T(8,128)(2,1)S(1)} %collective-permute-done.2.refs_2_, ...), custom_call_target="tpu_custom_call" | custom-call | bytes 16384 | tf_op jit(solution)/shard_map/pallas_call | solution.py:386
  20.5 2.3 %shard_map.102.refs_1_ = bf16[256,512]{1,0:T(8,128)(2,1)S(1)} custom-call(bf16[64,2048]{1,0:T(8,128)(2,1)S(1)} %collective-permute-done.refs_0_, bf16[64,2048]{1,0:T(8,128)(2,1)S(1)} %collective-permute-done.1.refs_1_, bf16[64,2048]{1,0:T(8,128)(2,1)S(1)} %collective-permute-done.2.refs_2_, bf16[64,2048]{1,0:T(8,128)(2,1)S(1)} %get-tuple-element.57.refs_3_), custom_call_target="tpu_custom_call" | custom-call | bytes 16384 | tf_op jit(solution)/shard_map/pallas_call | solution.py:386
  22.8 0.8 collective-permute-start.4
  23.6 2.6 %collective-permute-start.8 = (bf16[256,512]{1,0:T(8,128)(2,1)S(1)}, bf16[256,512]{1,0:T(8,128)(2,1)S(1)}, u32[]{:S(2)}, u32[]{:S(2)}) collective-permute-start(bf16[256,512]{1,0:T(8,128)(2,1)S(1)} %get-tuple-element.55), channel_id=1, source_target_pairs={{0,4},{1,5},{2,6},{3,7},{4,0},{5,1},{6,2},{7,3},{8,12},{9,13},{10,... | collective-permute-start | bytes 786440 | tf_op jit(solution)/shard_map/ppermute | solution.py:359
  26.2 1.2 %copy-done.1 = bf16[512,1024]{1,0:T(8,128)(2,1)S(1)} copy-done((bf16[512,1024]{1,0:T(8,128)(2,1)S(1)}, bf16[512,1024]{1,0:T(8,128)(2,1)}, u32[]{:S(2)}) %copy-start.1) | copy-done | bytes 1048600
  27.4 1.0 copy-done.2
  28.5 0.7 copy-done.3
  29.2 0.7 copy-done.4
  30.8 1.2 %collective-permute-done.4.refs_3_ = bf16[256,512]{1,0:T(8,128)(2,1)S(1)} collective-permute-done((bf16[256,512]{1,0:T(8,128)(2,1)S(1)}, bf16[256,512]{1,0:T(8,128)(2,1)S(1)}, u32[]{:S(2)}, u32[]{:S(2)}) %collective-permute-start.4) | collective-permute-done | bytes 262176 | tf_op jit(solution)/shard_map/ppermute | solution.py:359
  32.6 6.2 %collective-permute-done.8.refs_0_ = bf16[256,512]{1,0:T(8,128)(2,1)S(1)} collective-permute-done((bf16[256,512]{1,0:T(8,128)(2,1)S(1)}, bf16[256,512]{1,0:T(8,128)(2,1)S(1)}, u32[]{:S(2)}, u32[]{:S(2)}) %collective-permute-start.8) | collective-permute-done | bytes 262176 | tf_op jit(solution)/shard_map/ppermute | solution.py:359
  38.9 1.7 %collective-permute-start.10 = (bf16[256,512]{1,0:T(8,128)(2,1)S(1)}, bf16[256,512]{1,0:T(8,128)(2,1)S(1)}, u32[]{:S(2)}, u32[]{:S(2)}) collective-permute-start(bf16[256,512]{1,0:T(8,128)(2,1)S(1)} %collective-permute-done.8.refs_0_), channel_id=1, source_target_pairs={{0,16},{1,17},{2,18},{3,19},{4,20},{5,21},{6,22},{7,23},{8,24},{9,... | collective-permute-start | bytes 786440 | tf_op jit(solution)/shard_map/ppermute | solution.py:359
  40.6 6.9 %collective-permute-done.10.refs_2_ = bf16[256,512]{1,0:T(8,128)(2,1)S(1)} collective-permute-done((bf16[256,512]{1,0:T(8,128)(2,1)S(1)}, bf16[256,512]{1,0:T(8,128)(2,1)S(1)}, u32[]{:S(2)}, u32[]{:S(2)}) %collective-permute-start.10) | collective-permute-done | bytes 262176 | tf_op jit(solution)/shard_map/ppermute | solution.py:359
  49.0 1.1 %shard_map.104 = (f32[256,1024]{1,0:T(8,128)S(1)}, bf16[256,512]{1,0:T(8,128)(2,1)S(1)}) custom-call(bf16[256,1024]{1,0:T(8,128)(2,1)S(1)} %get-tuple-element.59.refs_0_, bf16[256,512]{1,0:T(8,128)(2,1)S(1)} %shard_map.102.refs_1_, bf16[256,512]{1,0:T(8,128)(2,1)S(1)} %collective-permute-done.3.refs_2_, bf16[256,512]{1,0:T(8,128)(2,1)S(1)} %collective-permute-done.4.refs_3_, ...), custom_call_target="tpu_custom_call" | custom-call | bytes 16384 | tf_op jit(solution)/shard_map/pallas_call | solution.py:431
  50.1 1.1 shard_map.105
  51.2 1.5 %shard_map.107 = (f32[256,1024]{1,0:T(8,128)S(1)}, bf16[256,1024]{1,0:T(8,128)(2,1)S(1)}, bf16[32,1024]{1,0:T(8,128)(2,1)S(1)}, bf16[32,1024]{1,0:T(8,128)(2,1)S...) custom-call(f32[256,1024]{1,0:T(8,128)S(1)} %get-tuple-element.61.re, ...), custom_call_target="tpu_custom_call" | custom-call | bytes 16384 | tf_op jit(solution)/shard_map/pallas_call | solution.py:454
  53.1 2.5 %collective-permute-start.16 = (bf16[32,1024]{1,0:T(8,128)(2,1)S(1)}, bf16[32,1024]{1,0:T(8,128)(2,1)S(1)}, u32[]{:S(2)}, u32[]{:S(2)}) collective-permute-start(bf16[32,1024]{1,0:T(8,128)(2,1)S(1)} %get-tuple-element.74), channel_id=1, source_target_pairs={{0,5},{1,4},{2,7},{3,6},{4,1},{5,0},{6,3},{7,2},{8,13},{9,12},{10,... | collective-permute-start | bytes 196616 | tf_op jit(solution)/shard_map/ppermute | solution.py:359
  55.7 2.5 %collective-permute-start.17 = (bf16[32,1024]{1,0:T(8,128)(2,1)S(1)}, bf16[32,1024]{1,0:T(8,128)(2,1)S(1)}, u32[]{:S(2)}, u32[]{:S(2)}) collective-permute-start(bf16[32,1024]{1,0:T(8,128)(2,1)S(1)} %get-tuple-element.75), channel_id=1, source_target_pairs={{0,6},{1,7},{2,4},{3,5},{4,2},{5,3},{6,0},{7,1},{8,14},{9,15},{10,... | collective-permute-start | bytes 196616 | tf_op jit(solution)/shard_map/ppermute | solution.py:359
  58.2 2.2 %collective-permute-start.18 = (bf16[32,1024]{1,0:T(8,128)(2,1)S(1)}, bf16[32,1024]{1,0:T(8,128)(2,1)S(1)}, u32[]{:S(2)}, u32[]{:S(2)}) collective-permute-start(bf16[32,1024]{1,0:T(8,128)(2,1)S(1)} %get-tuple-element.76), channel_id=1, source_target_pairs={{0,7},{1,6},{2,5},{3,4},{4,3},{5,2},{6,1},{7,0},{8,15},{9,14},{10,... | collective-permute-start | bytes 196616 | tf_op jit(solution)/shard_map/ppermute | solution.py:359
  60.4 1.6 %collective-permute-done.15.refs_0_ = bf16[32,1024]{1,0:T(8,128)(2,1)S(1)} collective-permute-done((bf16[32,1024]{1,0:T(8,128)(2,1)S(1)}, bf16[32,1024]{1,0:T(8,128)(2,1)S(1)}, u32[]{:S(2)}, u32[]{:S(2)}) %collective-permute-start.15) | collective-permute-done | bytes 65568 | tf_op jit(solution)/shard_map/ppermute | solution.py:359
  62.4 1.7 %collective-permute-done.16.refs_1_ = bf16[32,1024]{1,0:T(8,128)(2,1)S(1)} collective-permute-done((bf16[32,1024]{1,0:T(8,128)(2,1)S(1)}, bf16[32,1024]{1,0:T(8,128)(2,1)S(1)}, u32[]{:S(2)}, u32[]{:S(2)}) %collective-permute-start.16) | collective-permute-done | bytes 65568 | tf_op jit(solution)/shard_map/ppermute | solution.py:359
  64.1 1.5 %collective-permute-start.21 = (bf16[32,1024]{1,0:T(8,128)(2,1)S(1)}, bf16[32,1024]{1,0:T(8,128)(2,1)S(1)}, u32[]{:S(2)}, u32[]{:S(2)}) collective-permute-start(bf16[32,1024]{1,0:T(8,128)(2,1)S(1)} %get-tuple-element.79), channel_id=1, source_target_pairs={{0,1},{1,0},{2,3},{3,2},{4,5},{5,4},{6,7},{7,6},{8,9},{9,8},{10,11... | collective-permute-start | bytes 196616 | tf_op jit(solution)/shard_map/ppermute | solution.py:359
  65.6 1.1 %collective-permute-done.19.refs_4_ = bf16[32,1024]{1,0:T(8,128)(2,1)S(1)} collective-permute-done((bf16[32,1024]{1,0:T(8,128)(2,1)S(1)}, bf16[32,1024]{1,0:T(8,128)(2,1)S(1)}, u32[]{:S(2)}, u32[]{:S(2)}) %collective-permute-start.19) | collective-permute-done | bytes 65568 | tf_op jit(solution)/shard_map/ppermute | solution.py:359
  66.7 0.8 collective-permute-done.20.refs_5_
  67.6 0.8 collective-permute-done.21.refs_6_
  68.4 1.3 %shard_map.109 = (f32[64,3200]{1,0:T(8,128)S(1)}, bf16[32,3200]{1,0:T(8,128)(2,1)S(1)}, bf16[32,3200]{1,0:T(8,128)(2,1)S(1)}) custom-call(bf16[32,1024]{1,0:T(8,128)(2,1)S(1)} %collective-permute-done.15.refs_0_, bf16[32,1024]{1,0:T(8,128)(2,1)S(1)} %collective-permute-done.16.refs_1_, bf16[32,1024]{1,0:T(8,128)(2,1)S(1)} %collective-permute-done.17.refs_2_, ...), custom_call_target="tpu_custom_call" | custom-call | bytes 1024 | tf_op jit(solution)/shard_map/pallas_call | solution.py:472
  71.5 1.2 %collective-permute-start.25 = (bf16[16,3200]{1,0:T(8,128)(2,1)S(1)}, bf16[16,3200]{1,0:T(8,128)(2,1)S(1)}, u32[]{:S(2)}, u32[]{:S(2)}) collective-permute-start(bf16[16,3200]{1,0:T(8,128)(2,1)S(1)} %get-tuple-element.87), channel_id=1, source_target_pairs={{0,16},{1,17},{2,18},{3,19},{4,20},{5,21},{6,22},{7,23},{8,24},{9,... | collective-permute-start | bytes 307208 | tf_op jit(solution)/shard_map/ppermute | solution.py:359
  72.8 0.9 collective-permute-start.26
  73.6 3.7 %collective-permute-done.25.refs_0_ = bf16[16,3200]{1,0:T(8,128)(2,1)S(1)} collective-permute-done((bf16[16,3200]{1,0:T(8,128)(2,1)S(1)}, bf16[16,3200]{1,0:T(8,128)(2,1)S(1)}, u32[]{:S(2)}, u32[]{:S(2)}) %collective-permute-start.25) | collective-permute-done | bytes 102432 | tf_op jit(solution)/shard_map/ppermute | solution.py:359
  77.3 1.5 %collective-permute-done.26.refs_1_ = bf16[16,3200]{1,0:T(8,128)(2,1)S(1)} collective-permute-done((bf16[16,3200]{1,0:T(8,128)(2,1)S(1)}, bf16[16,3200]{1,0:T(8,128)(2,1)S(1)}, u32[]{:S(2)}, u32[]{:S(2)}) %collective-permute-start.26) | collective-permute-done | bytes 102432 | tf_op jit(solution)/shard_map/ppermute | solution.py:359
  79.0 1.2 %collective-permute-start.28 = (bf16[32,1536]{1,0:T(8,128)(2,1)S(1)}, bf16[32,1536]{1,0:T(8,128)(2,1)S(1)}, u32[]{:S(2)}, u32[]{:S(2)}) collective-permute-start(bf16[32,1536]{1,0:T(8,128)(2,1)S(1)} %shard_map.111.refs_0_), channel_id=1, source_target_pairs={{0,16},{1,17},{2,18},{3,19},{4,20},{5,21},{6,22},{7,23},{8,24},{9,... | collective-permute-start | bytes 294920 | tf_op jit(solution)/shard_map/ppermute | solution.py:359
  80.2 3.5 %collective-permute-done.28.refs_2_ = bf16[32,1536]{1,0:T(8,128)(2,1)S(1)} collective-permute-done((bf16[32,1536]{1,0:T(8,128)(2,1)S(1)}, bf16[32,1536]{1,0:T(8,128)(2,1)S(1)}, u32[]{:S(2)}, u32[]{:S(2)}) %collective-permute-start.28) | collective-permute-done | bytes 98336 | tf_op jit(solution)/shard_map/ppermute | solution.py:359
  83.6 1.3 %collective-permute-done.29.refs_3_ = bf16[32,1536]{1,0:T(8,128)(2,1)S(1)} collective-permute-done((bf16[32,1536]{1,0:T(8,128)(2,1)S(1)}, bf16[32,1536]{1,0:T(8,128)(2,1)S(1)}, u32[]{:S(2)}, u32[]{:S(2)}) %collective-permute-start.29) | collective-permute-done | bytes 98336 | tf_op jit(solution)/shard_map/ppermute | solution.py:359
  85.6 1.3 %collective-permute-start.30 = (bf16[16,1024]{1,0:T(8,128)(2,1)S(1)}, bf16[16,1024]{1,0:T(8,128)(2,1)S(1)}, u32[]{:S(2)}, u32[]{:S(2)}) collective-permute-start(bf16[16,1024]{1,0:T(8,128)(2,1)S(1)} %get-tuple-element.89), channel_id=1, source_target_pairs={{0,4},{1,5},{2,6},{3,7},{4,0},{5,1},{6,2},{7,3},{8,12},{9,13},{10,... | collective-permute-start | bytes 98312 | tf_op jit(solution)/shard_map/ppermute | solution.py:359
  87.0 2.6 %collective-permute-start.31 = (bf16[16,1024]{1,0:T(8,128)(2,1)S(1)}, bf16[16,1024]{1,0:T(8,128)(2,1)S(1)}, u32[]{:S(2)}, u32[]{:S(2)}) collective-permute-start(bf16[16,1024]{1,0:T(8,128)(2,1)S(1)} %get-tuple-element.90), channel_id=1, source_target_pairs={{0,5},{1,4},{2,7},{3,6},{4,1},{5,0},{6,3},{7,2},{8,13},{9,12},{10,... | collective-permute-start | bytes 98312 | tf_op jit(solution)/shard_map/ppermute | solution.py:359
  89.6 2.7 %collective-permute-start.32 = (bf16[16,1024]{1,0:T(8,128)(2,1)S(1)}, bf16[16,1024]{1,0:T(8,128)(2,1)S(1)}, u32[]{:S(2)}, u32[]{:S(2)}) collective-permute-start(bf16[16,1024]{1,0:T(8,128)(2,1)S(1)} %get-tuple-element.91), channel_id=1, source_target_pairs={{0,6},{1,7},{2,4},{3,5},{4,2},{5,3},{6,0},{7,1},{8,14},{9,15},{10,... | collective-permute-start | bytes 98312 | tf_op jit(solution)/shard_map/ppermute | solution.py:359
  92.2 1.1 %collective-permute-start.33 = (bf16[16,1024]{1,0:T(8,128)(2,1)S(1)}, bf16[16,1024]{1,0:T(8,128)(2,1)S(1)}, u32[]{:S(2)}, u32[]{:S(2)}) collective-permute-start(bf16[16,1024]{1,0:T(8,128)(2,1)S(1)} %get-tuple-element.92), channel_id=1, source_target_pairs={{0,7},{1,6},{2,5},{3,4},{4,3},{5,2},{6,1},{7,0},{8,15},{9,14},{10,... | collective-permute-start | bytes 98312 | tf_op jit(solution)/shard_map/ppermute | solution.py:359
  93.3 6.2 %collective-permute-done.22.got = bf16[256,1024]{1,0:T(8,128)(2,1)S(1)} collective-permute-done((bf16[256,1024]{1,0:T(8,128)(2,1)S(1)}, bf16[256,1024]{1,0:T(8,128)(2,1)S(1)}, u32[]{:S(2)}, u32[]{:S(2)}) %collective-permute-start.22) | collective-permute-done | bytes 524320 | tf_op jit(solution)/shard_map/ppermute | solution.py:359
  100.2 1.9 %collective-permute-start.35 = (bf16[16,1024]{1,0:T(8,128)(2,1)S(1)}, bf16[16,1024]{1,0:T(8,128)(2,1)S(1)}, u32[]{:S(2)}, u32[]{:S(2)}) collective-permute-start(bf16[16,1024]{1,0:T(8,128)(2,1)S(1)} %get-tuple-element.94), channel_id=1, source_target_pairs={{0,2},{1,3},{2,0},{3,1},{4,6},{5,7},{6,4},{7,5},{8,10},{9,11},{10,... | collective-permute-start | bytes 98312 | tf_op jit(solution)/shard_map/ppermute | solution.py:359
  102.2 0.8 collective-permute-start.36
  103.2 1.2 %collective-permute-done.34.refs_4_ = bf16[16,1024]{1,0:T(8,128)(2,1)S(1)} collective-permute-done((bf16[16,1024]{1,0:T(8,128)(2,1)S(1)}, bf16[16,1024]{1,0:T(8,128)(2,1)S(1)}, u32[]{:S(2)}, u32[]{:S(2)}) %collective-permute-start.34) | collective-permute-done | bytes 32800 | tf_op jit(solution)/shard_map/ppermute | solution.py:359
  104.4 1.7 %collective-permute-done.36.refs_6_ = bf16[16,1024]{1,0:T(8,128)(2,1)S(1)} collective-permute-done((bf16[16,1024]{1,0:T(8,128)(2,1)S(1)}, bf16[16,1024]{1,0:T(8,128)(2,1)S(1)}, u32[]{:S(2)}, u32[]{:S(2)}) %collective-permute-start.36) | collective-permute-done | bytes 32800 | tf_op jit(solution)/shard_map/ppermute | solution.py:359
  106.1 1.1 %shard_map.113 = bf16[256,1024]{1,0:T(8,128)(2,1)} custom-call(f32[256,1024]{1,0:T(8,128)S(1)} %shard_map.108.mixed, bf16[128,256]{1,0:T(8,128)(2,1)S(1)} %get-tuple-element.62.refs_6_.place_ref, f32[256,128]{1,0:T(8,128)S(1)} %get-tuple-element.82.gate_ref, bf16[16,1024]{1,0:T(8,128)(2,1)S(1)} %collective-permute-done.30.refs_0_, ...), custom_call_target="tpu_custom_call" | custom-call | bytes 2097152 | tf_op jit(solution)/shard_map/pallas_call | solution.py:512
  (59 shorter events, 8.1 us)
Async XLA Ops:
  0.0 30.2 %collective-permute-start.6 = (bf16[512,1024]{1,0:T(8,128)(2,1)}, bf16[512,1024]{1,0:T(8,128)(2,1)S(1)}, u32[]{:S(2)}, u32[]{:S(2)}) collective-permute-start(bf16[512,1024]{1,0:T(8,128)(2,1)} %refs_0_.1), channel_id=1, source_target_pairs={{0,1},{1,0},{2,3},{3,2},{4,5},{5,4},{6,7},{7,6},{8,9},{9,8},{10,11... | collective-permute-start | bytes 3145736 | tf_op jit(solution)/shard_map/ppermute | solution.py:359
  2.9 29.0 %collective-permute-start.7 = (bf16[512,1024]{1,0:T(8,128)(2,1)}, bf16[512,1024]{1,0:T(8,128)(2,1)S(1)}, u32[]{:S(2)}, u32[]{:S(2)}) collective-permute-start(bf16[512,1024]{1,0:T(8,128)(2,1)} %refs_0_.1), channel_id=1, source_target_pairs={{0,2},{1,3},{2,0},{3,1},{4,6},{5,7},{6,4},{7,5},{8,10},{9,11},{10,... | collective-permute-start | bytes 3145736 | tf_op jit(solution)/shard_map/ppermute | solution.py:359
  6.0 9.3 %collective-permute-start = (bf16[64,2048]{1,0:T(8,128)(2,1)S(1)}, bf16[64,2048]{1,0:T(8,128)(2,1)S(1)}, u32[]{:S(2)}, u32[]{:S(2)}) collective-permute-start(bf16[64,2048]{1,0:T(8,128)(2,1)S(1)} %get-tuple-element.51), channel_id=1, source_target_pairs={{0,16},{1,17},{2,18},{3,19},{4,20},{5,21},{6,22},{7,23},{8,24},{9,... | collective-permute-start | bytes 786440 | tf_op jit(solution)/shard_map/ppermute | solution.py:359
  7.6 10.6 %collective-permute-start.1 = (bf16[64,2048]{1,0:T(8,128)(2,1)S(1)}, bf16[64,2048]{1,0:T(8,128)(2,1)S(1)}, u32[]{:S(2)}, u32[]{:S(2)}) collective-permute-start(bf16[64,2048]{1,0:T(8,128)(2,1)S(1)} %get-tuple-element.52), channel_id=1, source_target_pairs={{0,24},{1,25},{2,26},{3,27},{4,28},{5,29},{6,30},{7,31},{8,16},{9,... | collective-permute-start | bytes 786440 | tf_op jit(solution)/shard_map/ppermute | solution.py:359
  7.6 10.6 %collective-permute-start.2 = (bf16[64,2048]{1,0:T(8,128)(2,1)S(1)}, bf16[64,2048]{1,0:T(8,128)(2,1)S(1)}, u32[]{:S(2)}, u32[]{:S(2)}) collective-permute-start(bf16[64,2048]{1,0:T(8,128)(2,1)S(1)} %get-tuple-element.53), channel_id=1, source_target_pairs={{0,8},{1,9},{2,10},{3,11},{4,12},{5,13},{6,14},{7,15},{8,0},{9,1},... | collective-permute-start | bytes 786440 | tf_op jit(solution)/shard_map/ppermute | solution.py:359
  22.8 9.1 %collective-permute-start.4 = (bf16[256,512]{1,0:T(8,128)(2,1)S(1)}, bf16[256,512]{1,0:T(8,128)(2,1)S(1)}, u32[]{:S(2)}, u32[]{:S(2)}) collective-permute-start(bf16[256,512]{1,0:T(8,128)(2,1)S(1)} %shard_map.102.refs_1_), channel_id=1, source_target_pairs={{0,16},{1,17},{2,18},{3,19},{4,20},{5,21},{6,22},{7,23},{8,24},{9,... | collective-permute-start | bytes 786440 | tf_op jit(solution)/shard_map/ppermute | solution.py:359
  23.6 15.2 %collective-permute-start.8 = (bf16[256,512]{1,0:T(8,128)(2,1)S(1)}, bf16[256,512]{1,0:T(8,128)(2,1)S(1)}, u32[]{:S(2)}, u32[]{:S(2)}) collective-permute-start(bf16[256,512]{1,0:T(8,128)(2,1)S(1)} %get-tuple-element.55), channel_id=1, source_target_pairs={{0,4},{1,5},{2,6},{3,7},{4,0},{5,1},{6,2},{7,3},{8,12},{9,13},{10,... | collective-permute-start | bytes 786440 | tf_op jit(solution)/shard_map/ppermute | solution.py:359
  26.2 1.2 %copy-start.1 = (bf16[512,1024]{1,0:T(8,128)(2,1)S(1)}, bf16[512,1024]{1,0:T(8,128)(2,1)}, u32[]{:S(2)}) copy-start(bf16[512,1024]{1,0:T(8,128)(2,1)} %refs_0_.1) | copy-start | bytes 3145732
  27.4 1.0 copy-start.2
  28.5 0.7 copy-start.3
  29.2 0.7 copy-start.4
  30.3 17.2 %collective-permute-start.11 = (bf16[512,384]{1,0:T(8,128)(2,1)S(1)}, bf16[512,384]{1,0:T(8,128)(2,1)S(1)}, u32[]{:S(2)}, u32[]{:S(2)}) collective-permute-start(bf16[512,384]{1,0:T(8,128)(2,1)S(1)} %slice.6), channel_id=1, source_target_pairs={{0,2},{1,3},{2,0},{3,1},{4,6},{5,7},{6,4},{7,5},{8,10},{9,11},{10,... | collective-permute-start | bytes 1179656 | tf_op jit(solution)/shard_map/ppermute | solution.py:359
  32.0 19.1 %collective-permute-start.13 = (bf16[512,640]{1,0:T(8,128)(2,1)S(1)}, bf16[512,640]{1,0:T(8,128)(2,1)S(1)}, u32[]{:S(2)}, u32[]{:S(2)}) collective-permute-start(bf16[512,640]{1,0:T(8,128)(2,1)S(1)} %slice.7), channel_id=1, source_target_pairs={{0,1},{1,0},{2,3},{3,2},{4,5},{5,4},{6,7},{7,6},{8,9},{9,8},{10,11... | collective-permute-start | bytes 1966088 | tf_op jit(solution)/shard_map/ppermute | solution.py:359
  38.9 8.6 %collective-permute-start.10 = (bf16[256,512]{1,0:T(8,128)(2,1)S(1)}, bf16[256,512]{1,0:T(8,128)(2,1)S(1)}, u32[]{:S(2)}, u32[]{:S(2)}) collective-permute-start(bf16[256,512]{1,0:T(8,128)(2,1)S(1)} %collective-permute-done.8.refs_0_), channel_id=1, source_target_pairs={{0,16},{1,17},{2,18},{3,19},{4,20},{5,21},{6,22},{7,23},{8,24},{9,... | collective-permute-start | bytes 786440 | tf_op jit(solution)/shard_map/ppermute | solution.py:359
  40.6 7.4 %collective-permute-start.14 = (s32[4,8,64]{2,1,0:T(8,128)S(1)}, s32[4,8,64]{2,1,0:T(8,128)S(1)}, u32[]{:S(2)}, u32[]{:S(2)}) collective-permute-start(s32[4,8,64]{2,1,0:T(8,128)S(1)} %bitcast.23), channel_id=1, source_target_pairs={{0,4},{1,5},{2,6},{3,7},{4,0},{5,1},{6,2},{7,3},{8,12},{9,13},{10,... | collective-permute-start | bytes 24584 | tf_op jit(solution)/shard_map/ppermute | solution.py:359
  40.6 7.7 %collective-permute-start.3 = (bf16[256,512]{1,0:T(8,128)(2,1)S(1)}, bf16[256,512]{1,0:T(8,128)(2,1)S(1)}, u32[]{:S(2)}, u32[]{:S(2)}) collective-permute-start(bf16[256,512]{1,0:T(8,128)(2,1)S(1)} %shard_map.102.refs_1_), channel_id=1, source_target_pairs={{0,8},{1,9},{2,10},{3,11},{4,12},{5,13},{6,14},{7,15},{8,0},{9,1},... | collective-permute-start | bytes 786440 | tf_op jit(solution)/shard_map/ppermute | solution.py:359
  47.5 1.5 %collective-permute-start.5 = (bf16[256,512]{1,0:T(8,128)(2,1)S(1)}, bf16[256,512]{1,0:T(8,128)(2,1)S(1)}, u32[]{:S(2)}, u32[]{:S(2)}) collective-permute-start(bf16[256,512]{1,0:T(8,128)(2,1)S(1)} %collective-permute-done.4.refs_3_), channel_id=1, source_target_pairs={{0,8},{1,9},{2,10},{3,11},{4,12},{5,13},{6,14},{7,15},{8,0},{9,1},... | collective-permute-start | bytes 786440 | tf_op jit(solution)/shard_map/ppermute | solution.py:359
  47.5 2.6 %collective-permute-start.9 = (bf16[256,512]{1,0:T(8,128)(2,1)S(1)}, bf16[256,512]{1,0:T(8,128)(2,1)S(1)}, u32[]{:S(2)}, u32[]{:S(2)}) collective-permute-start(bf16[256,512]{1,0:T(8,128)(2,1)S(1)} %collective-permute-done.8.refs_0_), channel_id=1, source_target_pairs={{0,8},{1,9},{2,10},{3,11},{4,12},{5,13},{6,14},{7,15},{8,0},{9,1},... | collective-permute-start | bytes 786440 | tf_op jit(solution)/shard_map/ppermute | solution.py:359
  48.0 2.1 %collective-permute-start.12 = (bf16[256,512]{1,0:T(8,128)(2,1)S(1)}, bf16[256,512]{1,0:T(8,128)(2,1)S(1)}, u32[]{:S(2)}, u32[]{:S(2)}) collective-permute-start(bf16[256,512]{1,0:T(8,128)(2,1)S(1)} %collective-permute-done.10.refs_2_), channel_id=1, source_target_pairs={{0,8},{1,9},{2,10},{3,11},{4,12},{5,13},{6,14},{7,15},{8,0},{9,1},... | collective-permute-start | bytes 786440 | tf_op jit(solution)/shard_map/ppermute | solution.py:359
  49.0 19.4 %slice-start = ((s8[6291456]{0:T(1024)(128)(4,1)}), s8[4194304]{0:T(1024)(128)(4,1)S(1)}, s32[]{:S(2)}) async-start(s8[6291456]{0:T(1024)(128)(4,1)} %bitcast.16), calls=%async_computation | async-start | bytes 8388608
  49.0 19.4 %copy-start.5 = (f32[1024]{0:T(1024)S(1)}, f32[1024]{0:T(1024)}, u32[]{:S(2)}) copy-start(f32[1024]{0:T(1024)} %param.15) | copy-start | bytes 12292
  50.1 18.3 %slice-start.1 = ((s8[6291456]{0:T(1024)(128)(4,1)}), s8[2097152]{0:T(1024)(128)(4,1)S(1)}, s32[]{:S(2)}) async-start(s8[6291456]{0:T(1024)(128)(4,1)} %bitcast.16), calls=%async_computation.1 | async-start | bytes 4194304
  51.2 33.7 %copy-start = (bf16[1,1536,1024]{2,1,0:T(8,128)(2,1)S(1)}, bf16[1,1536,1024]{2,1,0:T(8,128)(2,1)}, u32[]{:S(2)}) copy-start(bf16[1,1536,1024]{2,1,0:T(8,128)(2,1)} %param.19) | copy-start | bytes 9437188
  52.7 9.3 %collective-permute-start.15 = (bf16[32,1024]{1,0:T(8,128)(2,1)S(1)}, bf16[32,1024]{1,0:T(8,128)(2,1)S(1)}, u32[]{:S(2)}, u32[]{:S(2)}) collective-permute-start(bf16[32,1024]{1,0:T(8,128)(2,1)S(1)} %get-tuple-element.73), channel_id=1, source_target_pairs={{0,4},{1,5},{2,6},{3,7},{4,0},{5,1},{6,2},{7,3},{8,12},{9,13},{10,... | collective-permute-start | bytes 196616 | tf_op jit(solution)/shard_map/ppermute | solution.py:359
  53.1 11.0 %collective-permute-start.16 = (bf16[32,1024]{1,0:T(8,128)(2,1)S(1)}, bf16[32,1024]{1,0:T(8,128)(2,1)S(1)}, u32[]{:S(2)}, u32[]{:S(2)}) collective-permute-start(bf16[32,1024]{1,0:T(8,128)(2,1)S(1)} %get-tuple-element.74), channel_id=1, source_target_pairs={{0,5},{1,4},{2,7},{3,6},{4,1},{5,0},{6,3},{7,2},{8,13},{9,12},{10,... | collective-permute-start | bytes 196616 | tf_op jit(solution)/shard_map/ppermute | solution.py:359
  55.7 9.9 %collective-permute-start.17 = (bf16[32,1024]{1,0:T(8,128)(2,1)S(1)}, bf16[32,1024]{1,0:T(8,128)(2,1)S(1)}, u32[]{:S(2)}, u32[]{:S(2)}) collective-permute-start(bf16[32,1024]{1,0:T(8,128)(2,1)S(1)} %get-tuple-element.75), channel_id=1, source_target_pairs={{0,6},{1,7},{2,4},{3,5},{4,2},{5,3},{6,0},{7,1},{8,14},{9,15},{10,... | collective-permute-start | bytes 196616 | tf_op jit(solution)/shard_map/ppermute | solution.py:359
  58.2 7.4 %collective-permute-start.18 = (bf16[32,1024]{1,0:T(8,128)(2,1)S(1)}, bf16[32,1024]{1,0:T(8,128)(2,1)S(1)}, u32[]{:S(2)}, u32[]{:S(2)}) collective-permute-start(bf16[32,1024]{1,0:T(8,128)(2,1)S(1)} %get-tuple-element.76), channel_id=1, source_target_pairs={{0,7},{1,6},{2,5},{3,4},{4,3},{5,2},{6,1},{7,0},{8,15},{9,14},{10,... | collective-permute-start | bytes 196616 | tf_op jit(solution)/shard_map/ppermute | solution.py:359
  60.4 6.3 %collective-permute-start.19 = (bf16[32,1024]{1,0:T(8,128)(2,1)S(1)}, bf16[32,1024]{1,0:T(8,128)(2,1)S(1)}, u32[]{:S(2)}, u32[]{:S(2)}) collective-permute-start(bf16[32,1024]{1,0:T(8,128)(2,1)S(1)} %get-tuple-element.77), channel_id=1, source_target_pairs={{0,3},{1,2},{2,1},{3,0},{4,7},{5,6},{6,5},{7,4},{8,11},{9,10},{10,... | collective-permute-start | bytes 196616 | tf_op jit(solution)/shard_map/ppermute | solution.py:359
  62.0 5.5 %collective-permute-start.20 = (bf16[32,1024]{1,0:T(8,128)(2,1)S(1)}, bf16[32,1024]{1,0:T(8,128)(2,1)S(1)}, u32[]{:S(2)}, u32[]{:S(2)}) collective-permute-start(bf16[32,1024]{1,0:T(8,128)(2,1)S(1)} %get-tuple-element.78), channel_id=1, source_target_pairs={{0,2},{1,3},{2,0},{3,1},{4,6},{5,7},{6,4},{7,5},{8,10},{9,11},{10,... | collective-permute-start | bytes 196616 | tf_op jit(solution)/shard_map/ppermute | solution.py:359
  64.1 4.3 %collective-permute-start.21 = (bf16[32,1024]{1,0:T(8,128)(2,1)S(1)}, bf16[32,1024]{1,0:T(8,128)(2,1)S(1)}, u32[]{:S(2)}, u32[]{:S(2)}) collective-permute-start(bf16[32,1024]{1,0:T(8,128)(2,1)S(1)} %get-tuple-element.79), channel_id=1, source_target_pairs={{0,1},{1,0},{2,3},{3,2},{4,5},{5,4},{6,7},{7,6},{8,9},{9,8},{10,11... | collective-permute-start | bytes 196616 | tf_op jit(solution)/shard_map/ppermute | solution.py:359
  69.7 1.5 %collective-permute-start.23 = (bf16[32,3200]{1,0:T(8,128)(2,1)S(1)}, bf16[32,3200]{1,0:T(8,128)(2,1)S(1)}, u32[]{:S(2)}, u32[]{:S(2)}) collective-permute-start(bf16[32,3200]{1,0:T(8,128)(2,1)S(1)} %get-tuple-element.84), channel_id=1, source_target_pairs={{0,8},{1,9},{2,10},{3,11},{4,12},{5,13},{6,14},{7,15},{8,0},{9,1},... | collective-permute-start | bytes 614408 | tf_op jit(solution)/shard_map/ppermute | solution.py:359
  69.7 1.7 %collective-permute-start.24 = (bf16[32,3200]{1,0:T(8,128)(2,1)S(1)}, bf16[32,3200]{1,0:T(8,128)(2,1)S(1)}, u32[]{:S(2)}, u32[]{:S(2)}) collective-permute-start(bf16[32,3200]{1,0:T(8,128)(2,1)S(1)} %get-tuple-element.85), channel_id=1, source_target_pairs={{0,8},{1,9},{2,10},{3,11},{4,12},{5,13},{6,14},{7,15},{8,0},{9,1},... | collective-permute-start | bytes 614408 | tf_op jit(solution)/shard_map/ppermute | solution.py:359
  70.2 29.3 %collective-permute-start.22 = (bf16[256,1024]{1,0:T(8,128)(2,1)S(1)}, bf16[256,1024]{1,0:T(8,128)(2,1)S(1)}, u32[]{:S(2)}, u32[]{:S(2)}) collective-permute-start(bf16[256,1024]{1,0:T(8,128)(2,1)S(1)} %get-tuple-element.81), channel_id=1, source_target_pairs={{0,4},{1,5},{2,6},{3,7},{4,0},{5,1},{6,2},{7,3},{8,12},{9,13},{10,... | collective-permute-start | bytes 1572872 | tf_op jit(solution)/shard_map/ppermute | solution.py:359
  71.5 5.8 %collective-permute-start.25 = (bf16[16,3200]{1,0:T(8,128)(2,1)S(1)}, bf16[16,3200]{1,0:T(8,128)(2,1)S(1)}, u32[]{:S(2)}, u32[]{:S(2)}) collective-permute-start(bf16[16,3200]{1,0:T(8,128)(2,1)S(1)} %get-tuple-element.87), channel_id=1, source_target_pairs={{0,16},{1,17},{2,18},{3,19},{4,20},{5,21},{6,22},{7,23},{8,24},{9,... | collective-permute-start | bytes 307208 | tf_op jit(solution)/shard_map/ppermute | solution.py:359
  72.8 6.0 %collective-permute-start.26 = (bf16[16,3200]{1,0:T(8,128)(2,1)S(1)}, bf16[16,3200]{1,0:T(8,128)(2,1)S(1)}, u32[]{:S(2)}, u32[]{:S(2)}) collective-permute-start(bf16[16,3200]{1,0:T(8,128)(2,1)S(1)} %get-tuple-element.88), channel_id=1, source_target_pairs={{0,16},{1,17},{2,18},{3,19},{4,20},{5,21},{6,22},{7,23},{8,24},{9,... | collective-permute-start | bytes 307208 | tf_op jit(solution)/shard_map/ppermute | solution.py:359
  79.0 4.7 %collective-permute-start.28 = (bf16[32,1536]{1,0:T(8,128)(2,1)S(1)}, bf16[32,1536]{1,0:T(8,128)(2,1)S(1)}, u32[]{:S(2)}, u32[]{:S(2)}) collective-permute-start(bf16[32,1536]{1,0:T(8,128)(2,1)S(1)} %shard_map.111.refs_0_), channel_id=1, source_target_pairs={{0,16},{1,17},{2,18},{3,19},{4,20},{5,21},{6,22},{7,23},{8,24},{9,... | collective-permute-start | bytes 294920 | tf_op jit(solution)/shard_map/ppermute | solution.py:359
  80.2 3.5 %collective-permute-start.27 = (bf16[32,1536]{1,0:T(8,128)(2,1)S(1)}, bf16[32,1536]{1,0:T(8,128)(2,1)S(1)}, u32[]{:S(2)}, u32[]{:S(2)}) collective-permute-start(bf16[32,1536]{1,0:T(8,128)(2,1)S(1)} %shard_map.111.refs_0_), channel_id=1, source_target_pairs={{0,8},{1,9},{2,10},{3,11},{4,12},{5,13},{6,14},{7,15},{8,0},{9,1},... | collective-permute-start | bytes 294920 | tf_op jit(solution)/shard_map/ppermute | solution.py:359
  83.6 1.3 %collective-permute-start.29 = (bf16[32,1536]{1,0:T(8,128)(2,1)S(1)}, bf16[32,1536]{1,0:T(8,128)(2,1)S(1)}, u32[]{:S(2)}, u32[]{:S(2)}) collective-permute-start(bf16[32,1536]{1,0:T(8,128)(2,1)S(1)} %collective-permute-done.28.refs_2_), channel_id=1, source_target_pairs={{0,8},{1,9},{2,10},{3,11},{4,12},{5,13},{6,14},{7,15},{8,0},{9,1},... | collective-permute-start | bytes 294920 | tf_op jit(solution)/shard_map/ppermute | solution.py:359
  85.6 14.6 %collective-permute-start.30 = (bf16[16,1024]{1,0:T(8,128)(2,1)S(1)}, bf16[16,1024]{1,0:T(8,128)(2,1)S(1)}, u32[]{:S(2)}, u32[]{:S(2)}) collective-permute-start(bf16[16,1024]{1,0:T(8,128)(2,1)S(1)} %get-tuple-element.89), channel_id=1, source_target_pairs={{0,4},{1,5},{2,6},{3,7},{4,0},{5,1},{6,2},{7,3},{8,12},{9,13},{10,... | collective-permute-start | bytes 98312 | tf_op jit(solution)/shard_map/ppermute | solution.py:359
  87.0 15.2 %collective-permute-start.31 = (bf16[16,1024]{1,0:T(8,128)(2,1)S(1)}, bf16[16,1024]{1,0:T(8,128)(2,1)S(1)}, u32[]{:S(2)}, u32[]{:S(2)}) collective-permute-start(bf16[16,1024]{1,0:T(8,128)(2,1)S(1)} %get-tuple-element.90), channel_id=1, source_target_pairs={{0,5},{1,4},{2,7},{3,6},{4,1},{5,0},{6,3},{7,2},{8,13},{9,12},{10,... | collective-permute-start | bytes 98312 | tf_op jit(solution)/shard_map/ppermute | solution.py:359
  89.6 13.6 %collective-permute-start.32 = (bf16[16,1024]{1,0:T(8,128)(2,1)S(1)}, bf16[16,1024]{1,0:T(8,128)(2,1)S(1)}, u32[]{:S(2)}, u32[]{:S(2)}) collective-permute-start(bf16[16,1024]{1,0:T(8,128)(2,1)S(1)} %get-tuple-element.91), channel_id=1, source_target_pairs={{0,6},{1,7},{2,4},{3,5},{4,2},{5,3},{6,0},{7,1},{8,14},{9,15},{10,... | collective-permute-start | bytes 98312 | tf_op jit(solution)/shard_map/ppermute | solution.py:359
  92.2 10.9 %collective-permute-start.33 = (bf16[16,1024]{1,0:T(8,128)(2,1)S(1)}, bf16[16,1024]{1,0:T(8,128)(2,1)S(1)}, u32[]{:S(2)}, u32[]{:S(2)}) collective-permute-start(bf16[16,1024]{1,0:T(8,128)(2,1)S(1)} %get-tuple-element.92), channel_id=1, source_target_pairs={{0,7},{1,6},{2,5},{3,4},{4,3},{5,2},{6,1},{7,0},{8,15},{9,14},{10,... | collective-permute-start | bytes 98312 | tf_op jit(solution)/shard_map/ppermute | solution.py:359
  99.5 4.8 %collective-permute-start.34 = (bf16[16,1024]{1,0:T(8,128)(2,1)S(1)}, bf16[16,1024]{1,0:T(8,128)(2,1)S(1)}, u32[]{:S(2)}, u32[]{:S(2)}) collective-permute-start(bf16[16,1024]{1,0:T(8,128)(2,1)S(1)} %get-tuple-element.93), channel_id=1, source_target_pairs={{0,3},{1,2},{2,1},{3,0},{4,7},{5,6},{6,5},{7,4},{8,11},{9,10},{10,... | collective-permute-start | bytes 98312 | tf_op jit(solution)/shard_map/ppermute | solution.py:359
  100.2 4.2 %collective-permute-start.35 = (bf16[16,1024]{1,0:T(8,128)(2,1)S(1)}, bf16[16,1024]{1,0:T(8,128)(2,1)S(1)}, u32[]{:S(2)}, u32[]{:S(2)}) collective-permute-start(bf16[16,1024]{1,0:T(8,128)(2,1)S(1)} %get-tuple-element.94), channel_id=1, source_target_pairs={{0,2},{1,3},{2,0},{3,1},{4,6},{5,7},{6,4},{7,5},{8,10},{9,11},{10,... | collective-permute-start | bytes 98312 | tf_op jit(solution)/shard_map/ppermute | solution.py:359
  102.2 3.9 %collective-permute-start.36 = (bf16[16,1024]{1,0:T(8,128)(2,1)S(1)}, bf16[16,1024]{1,0:T(8,128)(2,1)S(1)}, u32[]{:S(2)}, u32[]{:S(2)}) collective-permute-start(bf16[16,1024]{1,0:T(8,128)(2,1)S(1)} %get-tuple-element.95), channel_id=1, source_target_pairs={{0,1},{1,0},{2,3},{3,2},{4,5},{5,4},{6,7},{7,6},{8,9},{9,8},{10,11... | collective-permute-start | bytes 98312 | tf_op jit(solution)/shard_map/ppermute | solution.py:359

commit v17 on v16

--- a/solution.py
+++ b/solution.py
@@ -448,7 +448,7 @@
         )
     acc, last = project(mine_all, res)
     quarter = [shards[d][1] for d in range(3, C, 2)]
-    theirs_all = gather(after(theirs, place, shards[1]), lambda: quarter)
+    theirs_all = gather(after(theirs, place, shards[1]), lambda: (acc, other_place, *quarter))
     acc_far, last_far = project(theirs_all)
     gain = norm_gain.reshape(1, width)
     own, full, *outgoing = call(

time: 108 us -> 110 us (1.019)
  starting transfers between devices: 38 us -> 39.8 us
    ppermute x37, starting transfers between devices: 38 us -> 39.8 us  [permute(): return lax.ppermute(x, ('ctx', 'exp'), pairs)]
where the time goes in v17:
time: 110 us; the launch traced here: 109 us
  waiting for transfers between devices  52 us (47%)
  starting transfers between devices  39.8 us (36%)
  Pallas kernels  13.7 us (12%)
  local copies, waits for them, and re-layouts  3.83 us (3%)
    ppermute x37, waiting for transfers between devices, permute(): return lax.ppermute(x, ('ctx', 'exp'), pairs)  52 us
    ppermute x37, starting transfers between devices, permute(): return lax.ppermute(x, ('ctx', 'exp'), pairs)  39.8 us
    pallas_call x2, Pallas kernels, attend(): call(functools.partial(attend_kernel, C, t), [sds((rows, qw), BF16)] + [s...  4.65 us
    unnamed x16, local copies, waits for them, and re-layouts  3.72 us
  transfers between devices with their start and end apart: 37, of which 21 were waited for; matrix products, arithmetic and copies ran while one was open for 0% of the time, Pallas kernels for 9%

profile of v17, /device:TPU:0, one launch (start us, length us, event | category | flops | bytes accessed | tf_op | source)
XLA Modules:
  0.0 109.5 jit_solution(5976181041287419988)
XLA Ops:
  0.0 2.9 %collective-permute-start.6 = (bf16[512,1024]{1,0:T(8,128)(2,1)}, bf16[512,1024]{1,0:T(8,128)(2,1)S(1)}, u32[]{:S(2)}, u32[]{:S(2)}) collective-permute-start(bf16[512,1024]{1,0:T(8,128)(2,1)} %refs_0_.1), channel_id=1, source_target_pairs={{0,1},{1,0},{2,3},{3,2},{4,5},{5,4},{6,7},{7,6},{8,9},{9,8},{10,11... | collective-permute-start | bytes 3145736 | tf_op jit(solution)/shard_map/ppermute | solution.py:359
  2.9 1.6 %collective-permute-start.7 = (bf16[512,1024]{1,0:T(8,128)(2,1)}, bf16[512,1024]{1,0:T(8,128)(2,1)S(1)}, u32[]{:S(2)}, u32[]{:S(2)}) collective-permute-start(bf16[512,1024]{1,0:T(8,128)(2,1)} %refs_0_.1), channel_id=1, source_target_pairs={{0,2},{1,3},{2,0},{3,1},{4,6},{5,7},{6,4},{7,5},{8,10},{9,11},{10,... | collective-permute-start | bytes 3145736 | tf_op jit(solution)/shard_map/ppermute | solution.py:359
  4.5 1.4 %shard_map.100 = (bf16[64,2048]{1,0:T(8,128)(2,1)S(1)}, bf16[64,2048]{1,0:T(8,128)(2,1)S(1)}, bf16[64,2048]{1,0:T(8,128)(2,1)S(1)}, bf16[64,2048]{1,0:T(8,128)(2,1)S(1)}) custom-call(bf16[64,4096]{1,0:T(8,128)(2,1)} %bitcast.25, bf16[64,512]{1,0:T(8,128)(2,1)} %bitcast.26, bf16[64,512]{1,0:T(8,128)(2,1)} %bitcast.27), custom_call_target="tpu_custom_call" | custom-call | bytes 1048576 | tf_op jit(solution)/shard_map/pallas_call | solution.py:365
  6.0 1.6 %collective-permute-start = (bf16[64,2048]{1,0:T(8,128)(2,1)S(1)}, bf16[64,2048]{1,0:T(8,128)(2,1)S(1)}, u32[]{:S(2)}, u32[]{:S(2)}) collective-permute-start(bf16[64,2048]{1,0:T(8,128)(2,1)S(1)} %get-tuple-element.51), channel_id=1, source_target_pairs={{0,16},{1,17},{2,18},{3,19},{4,20},{5,21},{6,22},{7,23},{8,24},{9,... | collective-permute-start | bytes 786440 | tf_op jit(solution)/shard_map/ppermute | solution.py:359
  8.2 7.1 %collective-permute-done.refs_0_ = bf16[64,2048]{1,0:T(8,128)(2,1)S(1)} collective-permute-done((bf16[64,2048]{1,0:T(8,128)(2,1)S(1)}, bf16[64,2048]{1,0:T(8,128)(2,1)S(1)}, u32[]{:S(2)}, u32[]{:S(2)}) %collective-permute-start) | collective-permute-done | bytes 262176 | tf_op jit(solution)/shard_map/ppermute | solution.py:359
  15.3 2.9 %collective-permute-done.1.refs_1_ = bf16[64,2048]{1,0:T(8,128)(2,1)S(1)} collective-permute-done((bf16[64,2048]{1,0:T(8,128)(2,1)S(1)}, bf16[64,2048]{1,0:T(8,128)(2,1)S(1)}, u32[]{:S(2)}, u32[]{:S(2)}) %collective-permute-start.1) | collective-permute-done | bytes 262176 | tf_op jit(solution)/shard_map/ppermute | solution.py:359
  18.2 2.3 %shard_map.101 = (bf16[256,512]{1,0:T(8,128)(2,1)S(1)}, bf16[64,2048]{1,0:T(8,128)(2,1)S(1)}) custom-call(bf16[64,2048]{1,0:T(8,128)(2,1)S(1)} %collective-permute-done.refs_0_, bf16[64,2048]{1,0:T(8,128)(2,1)S(1)} %collective-permute-done.1.refs_1_, bf16[64,2048]{1,0:T(8,128)(2,1)S(1)} %collective-permute-done.2.refs_2_, ...), custom_call_target="tpu_custom_call" | custom-call | bytes 16384 | tf_op jit(solution)/shard_map/pallas_call | solution.py:386
  20.5 2.3 %shard_map.102.refs_1_ = bf16[256,512]{1,0:T(8,128)(2,1)S(1)} custom-call(bf16[64,2048]{1,0:T(8,128)(2,1)S(1)} %collective-permute-done.refs_0_, bf16[64,2048]{1,0:T(8,128)(2,1)S(1)} %collective-permute-done.1.refs_1_, bf16[64,2048]{1,0:T(8,128)(2,1)S(1)} %collective-permute-done.2.refs_2_, bf16[64,2048]{1,0:T(8,128)(2,1)S(1)} %get-tuple-element.57.refs_3_), custom_call_target="tpu_custom_call" | custom-call | bytes 16384 | tf_op jit(solution)/shard_map/pallas_call | solution.py:386
  23.6 2.6 %collective-permute-start.8 = (bf16[256,512]{1,0:T(8,128)(2,1)S(1)}, bf16[256,512]{1,0:T(8,128)(2,1)S(1)}, u32[]{:S(2)}, u32[]{:S(2)}) collective-permute-start(bf16[256,512]{1,0:T(8,128)(2,1)S(1)} %get-tuple-element.55), channel_id=1, source_target_pairs={{0,4},{1,5},{2,6},{3,7},{4,0},{5,1},{6,2},{7,3},{8,12},{9,13},{10,... | collective-permute-start | bytes 786440 | tf_op jit(solution)/shard_map/ppermute | solution.py:359
  26.2 1.2 %copy-done.1 = bf16[512,1024]{1,0:T(8,128)(2,1)S(1)} copy-done((bf16[512,1024]{1,0:T(8,128)(2,1)S(1)}, bf16[512,1024]{1,0:T(8,128)(2,1)}, u32[]{:S(2)}) %copy-start.1) | copy-done | bytes 1048600
  27.4 1.0 copy-done.2
  30.8 1.2 %collective-permute-done.4.refs_3_ = bf16[256,512]{1,0:T(8,128)(2,1)S(1)} collective-permute-done((bf16[256,512]{1,0:T(8,128)(2,1)S(1)}, bf16[256,512]{1,0:T(8,128)(2,1)S(1)}, u32[]{:S(2)}, u32[]{:S(2)}) %collective-permute-start.4) | collective-permute-done | bytes 262176 | tf_op jit(solution)/shard_map/ppermute | solution.py:359
  32.6 2.6 %collective-permute-start.11 = (s32[4,8,64]{2,1,0:T(8,128)S(1)}, s32[4,8,64]{2,1,0:T(8,128)S(1)}, u32[]{:S(2)}, u32[]{:S(2)}) collective-permute-start(s32[4,8,64]{2,1,0:T(8,128)S(1)} %bitcast.23), channel_id=1, source_target_pairs={{0,4},{1,5},{2,6},{3,7},{4,0},{5,1},{6,2},{7,3},{8,12},{9,13},{10,... | collective-permute-start | bytes 24584 | tf_op jit(solution)/shard_map/ppermute | solution.py:359
  35.3 3.6 %collective-permute-done.8.refs_0_ = bf16[256,512]{1,0:T(8,128)(2,1)S(1)} collective-permute-done((bf16[256,512]{1,0:T(8,128)(2,1)S(1)}, bf16[256,512]{1,0:T(8,128)(2,1)S(1)}, u32[]{:S(2)}, u32[]{:S(2)}) %collective-permute-start.8) | collective-permute-done | bytes 262176 | tf_op jit(solution)/shard_map/ppermute | solution.py:359
  39.4 1.7 %collective-permute-done.11.routes_ref = s32[4,8,64]{2,1,0:T(8,128)S(1)} collective-permute-done((s32[4,8,64]{2,1,0:T(8,128)S(1)}, s32[4,8,64]{2,1,0:T(8,128)S(1)}, u32[]{:S(2)}, u32[]{:S(2)}) %collective-permute-start.11) | collective-permute-done | bytes 8224 | tf_op jit(solution)/shard_map/ppermute | solution.py:359
  41.1 1.7 %collective-permute-start.10 = (bf16[256,512]{1,0:T(8,128)(2,1)S(1)}, bf16[256,512]{1,0:T(8,128)(2,1)S(1)}, u32[]{:S(2)}, u32[]{:S(2)}) collective-permute-start(bf16[256,512]{1,0:T(8,128)(2,1)S(1)} %collective-permute-done.8.refs_0_), channel_id=1, source_target_pairs={{0,16},{1,17},{2,18},{3,19},{4,20},{5,21},{6,22},{7,23},{8,24},{9,... | collective-permute-start | bytes 786440 | tf_op jit(solution)/shard_map/ppermute | solution.py:359
  43.2 1.1 shard_map.104
  44.3 5.7 %collective-permute-done.10.refs_2_ = bf16[256,512]{1,0:T(8,128)(2,1)S(1)} collective-permute-done((bf16[256,512]{1,0:T(8,128)(2,1)S(1)}, bf16[256,512]{1,0:T(8,128)(2,1)S(1)}, u32[]{:S(2)}, u32[]{:S(2)}) %collective-permute-start.10) | collective-permute-done | bytes 262176 | tf_op jit(solution)/shard_map/ppermute | solution.py:359
  50.1 1.5 %collective-permute-done.13.refs_3_ = bf16[256,512]{1,0:T(8,128)(2,1)S(1)} collective-permute-done((bf16[256,512]{1,0:T(8,128)(2,1)S(1)}, bf16[256,512]{1,0:T(8,128)(2,1)S(1)}, u32[]{:S(2)}, u32[]{:S(2)}) %collective-permute-start.13) | collective-permute-done | bytes 262176 | tf_op jit(solution)/shard_map/ppermute | solution.py:359
  51.6 1.1 shard_map.106
  52.7 1.5 %shard_map.107 = (f32[256,1024]{1,0:T(8,128)S(1)}, bf16[256,1024]{1,0:T(8,128)(2,1)S(1)}, bf16[32,1024]{1,0:T(8,128)(2,1)S(1)}, bf16[32,1024]{1,0:T(8,128)(2,1)S...) custom-call(f32[256,1024]{1,0:T(8,128)S(1)} %get-tuple-element.61.re, ...), custom_call_target="tpu_custom_call" | custom-call | bytes 16384 | tf_op jit(solution)/shard_map/pallas_call | solution.py:454
  54.2 3.2 %collective-permute-start.15 = (bf16[32,1024]{1,0:T(8,128)(2,1)S(1)}, bf16[32,1024]{1,0:T(8,128)(2,1)S(1)}, u32[]{:S(2)}, u32[]{:S(2)}) collective-permute-start(bf16[32,1024]{1,0:T(8,128)(2,1)S(1)} %get-tuple-element.73), channel_id=1, source_target_pairs={{0,4},{1,5},{2,6},{3,7},{4,0},{5,1},{6,2},{7,3},{8,12},{9,13},{10,... | collective-permute-start | bytes 196616 | tf_op jit(solution)/shard_map/ppermute | solution.py:359
  57.4 0.9 collective-permute-start.17
  58.3 3.9 %collective-permute-start.18 = (bf16[32,1024]{1,0:T(8,128)(2,1)S(1)}, bf16[32,1024]{1,0:T(8,128)(2,1)S(1)}, u32[]{:S(2)}, u32[]{:S(2)}) collective-permute-start(bf16[32,1024]{1,0:T(8,128)(2,1)S(1)} %get-tuple-element.76), channel_id=1, source_target_pairs={{0,7},{1,6},{2,5},{3,4},{4,3},{5,2},{6,1},{7,0},{8,15},{9,14},{10,... | collective-permute-start | bytes 196616 | tf_op jit(solution)/shard_map/ppermute | solution.py:359
  62.2 3.8 %collective-permute-done.15.refs_0_ = bf16[32,1024]{1,0:T(8,128)(2,1)S(1)} collective-permute-done((bf16[32,1024]{1,0:T(8,128)(2,1)S(1)}, bf16[32,1024]{1,0:T(8,128)(2,1)S(1)}, u32[]{:S(2)}, u32[]{:S(2)}) %collective-permute-start.15) | collective-permute-done | bytes 65568 | tf_op jit(solution)/shard_map/ppermute | solution.py:359
  65.9 1.3 %collective-permute-done.16.refs_1_ = bf16[32,1024]{1,0:T(8,128)(2,1)S(1)} collective-permute-done((bf16[32,1024]{1,0:T(8,128)(2,1)S(1)}, bf16[32,1024]{1,0:T(8,128)(2,1)S(1)}, u32[]{:S(2)}, u32[]{:S(2)}) %collective-permute-start.16) | collective-permute-done | bytes 65568 | tf_op jit(solution)/shard_map/ppermute | solution.py:359
  67.2 1.5 %collective-permute-start.21 = (bf16[32,1024]{1,0:T(8,128)(2,1)S(1)}, bf16[32,1024]{1,0:T(8,128)(2,1)S(1)}, u32[]{:S(2)}, u32[]{:S(2)}) collective-permute-start(bf16[32,1024]{1,0:T(8,128)(2,1)S(1)} %get-tuple-element.79), channel_id=1, source_target_pairs={{0,1},{1,0},{2,3},{3,2},{4,5},{5,4},{6,7},{7,6},{8,9},{9,8},{10,11... | collective-permute-start | bytes 196616 | tf_op jit(solution)/shard_map/ppermute | solution.py:359
  68.8 1.4 %collective-permute-done.20.refs_5_ = bf16[32,1024]{1,0:T(8,128)(2,1)S(1)} collective-permute-done((bf16[32,1024]{1,0:T(8,128)(2,1)S(1)}, bf16[32,1024]{1,0:T(8,128)(2,1)S(1)}, u32[]{:S(2)}, u32[]{:S(2)}) %collective-permute-start.20) | collective-permute-done | bytes 65568 | tf_op jit(solution)/shard_map/ppermute | solution.py:359
  70.2 1.3 %collective-permute-done.21.refs_6_ = bf16[32,1024]{1,0:T(8,128)(2,1)S(1)} collective-permute-done((bf16[32,1024]{1,0:T(8,128)(2,1)S(1)}, bf16[32,1024]{1,0:T(8,128)(2,1)S(1)}, u32[]{:S(2)}, u32[]{:S(2)}) %collective-permute-start.21) | collective-permute-done | bytes 65568 | tf_op jit(solution)/shard_map/ppermute | solution.py:359
  71.5 1.3 %shard_map.109 = (f32[64,3200]{1,0:T(8,128)S(1)}, bf16[32,3200]{1,0:T(8,128)(2,1)S(1)}, bf16[32,3200]{1,0:T(8,128)(2,1)S(1)}) custom-call(bf16[32,1024]{1,0:T(8,128)(2,1)S(1)} %collective-permute-done.15.refs_0_, bf16[32,1024]{1,0:T(8,128)(2,1)S(1)} %collective-permute-done.16.refs_1_, bf16[32,1024]{1,0:T(8,128)(2,1)S(1)} %collective-permute-done.17.refs_2_, ...), custom_call_target="tpu_custom_call" | custom-call | bytes 1024 | tf_op jit(solution)/shard_map/pallas_call | solution.py:472
  73.4 0.9 collective-permute-done.23.refs_0_
  74.7 0.9 collective-permute-start.25
  75.6 1.2 %collective-permute-start.26 = (bf16[16,3200]{1,0:T(8,128)(2,1)S(1)}, bf16[16,3200]{1,0:T(8,128)(2,1)S(1)}, u32[]{:S(2)}, u32[]{:S(2)}) collective-permute-start(bf16[16,3200]{1,0:T(8,128)(2,1)S(1)} %get-tuple-element.88), channel_id=1, source_target_pairs={{0,16},{1,17},{2,18},{3,19},{4,20},{5,21},{6,22},{7,23},{8,24},{9,... | collective-permute-start | bytes 307208 | tf_op jit(solution)/shard_map/ppermute | solution.py:359
  76.8 3.7 %collective-permute-done.25.refs_0_ = bf16[16,3200]{1,0:T(8,128)(2,1)S(1)} collective-permute-done((bf16[16,3200]{1,0:T(8,128)(2,1)S(1)}, bf16[16,3200]{1,0:T(8,128)(2,1)S(1)}, u32[]{:S(2)}, u32[]{:S(2)}) %collective-permute-start.25) | collective-permute-done | bytes 102432 | tf_op jit(solution)/shard_map/ppermute | solution.py:359
  80.4 1.5 %collective-permute-done.26.refs_1_ = bf16[16,3200]{1,0:T(8,128)(2,1)S(1)} collective-permute-done((bf16[16,3200]{1,0:T(8,128)(2,1)S(1)}, bf16[16,3200]{1,0:T(8,128)(2,1)S(1)}, u32[]{:S(2)}, u32[]{:S(2)}) %collective-permute-start.26) | collective-permute-done | bytes 102432 | tf_op jit(solution)/shard_map/ppermute | solution.py:359
  82.1 0.9 collective-permute-start.28
  83.0 3.8 %collective-permute-done.28.refs_2_ = bf16[32,1536]{1,0:T(8,128)(2,1)S(1)} collective-permute-done((bf16[32,1536]{1,0:T(8,128)(2,1)S(1)}, bf16[32,1536]{1,0:T(8,128)(2,1)S(1)}, u32[]{:S(2)}, u32[]{:S(2)}) %collective-permute-start.28) | collective-permute-done | bytes 98336 | tf_op jit(solution)/shard_map/ppermute | solution.py:359
  86.8 1.3 %collective-permute-done.29.refs_3_ = bf16[32,1536]{1,0:T(8,128)(2,1)S(1)} collective-permute-done((bf16[32,1536]{1,0:T(8,128)(2,1)S(1)}, bf16[32,1536]{1,0:T(8,128)(2,1)S(1)}, u32[]{:S(2)}, u32[]{:S(2)}) %collective-permute-start.29) | collective-permute-done | bytes 98336 | tf_op jit(solution)/shard_map/ppermute | solution.py:359
  88.7 1.3 %collective-permute-start.30 = (bf16[16,1024]{1,0:T(8,128)(2,1)S(1)}, bf16[16,1024]{1,0:T(8,128)(2,1)S(1)}, u32[]{:S(2)}, u32[]{:S(2)}) collective-permute-start(bf16[16,1024]{1,0:T(8,128)(2,1)S(1)} %get-tuple-element.89), channel_id=1, source_target_pairs={{0,4},{1,5},{2,6},{3,7},{4,0},{5,1},{6,2},{7,3},{8,12},{9,13},{10,... | collective-permute-start | bytes 98312 | tf_op jit(solution)/shard_map/ppermute | solution.py:359
  90.1 2.6 %collective-permute-start.31 = (bf16[16,1024]{1,0:T(8,128)(2,1)S(1)}, bf16[16,1024]{1,0:T(8,128)(2,1)S(1)}, u32[]{:S(2)}, u32[]{:S(2)}) collective-permute-start(bf16[16,1024]{1,0:T(8,128)(2,1)S(1)} %get-tuple-element.90), channel_id=1, source_target_pairs={{0,5},{1,4},{2,7},{3,6},{4,1},{5,0},{6,3},{7,2},{8,13},{9,12},{10,... | collective-permute-start | bytes 98312 | tf_op jit(solution)/shard_map/ppermute | solution.py:359
  92.7 1.8 %collective-permute-start.32 = (bf16[16,1024]{1,0:T(8,128)(2,1)S(1)}, bf16[16,1024]{1,0:T(8,128)(2,1)S(1)}, u32[]{:S(2)}, u32[]{:S(2)}) collective-permute-start(bf16[16,1024]{1,0:T(8,128)(2,1)S(1)} %get-tuple-element.91), channel_id=1, source_target_pairs={{0,6},{1,7},{2,4},{3,5},{4,2},{5,3},{6,0},{7,1},{8,14},{9,15},{10,... | collective-permute-start | bytes 98312 | tf_op jit(solution)/shard_map/ppermute | solution.py:359
  94.5 2.0 %collective-permute-start.33 = (bf16[16,1024]{1,0:T(8,128)(2,1)S(1)}, bf16[16,1024]{1,0:T(8,128)(2,1)S(1)}, u32[]{:S(2)}, u32[]{:S(2)}) collective-permute-start(bf16[16,1024]{1,0:T(8,128)(2,1)S(1)} %get-tuple-element.92), channel_id=1, source_target_pairs={{0,7},{1,6},{2,5},{3,4},{4,3},{5,2},{6,1},{7,0},{8,15},{9,14},{10,... | collective-permute-start | bytes 98312 | tf_op jit(solution)/shard_map/ppermute | solution.py:359
  96.5 6.0 %collective-permute-done.22.got = bf16[256,1024]{1,0:T(8,128)(2,1)S(1)} collective-permute-done((bf16[256,1024]{1,0:T(8,128)(2,1)S(1)}, bf16[256,1024]{1,0:T(8,128)(2,1)S(1)}, u32[]{:S(2)}, u32[]{:S(2)}) %collective-permute-start.22) | collective-permute-done | bytes 524320 | tf_op jit(solution)/shard_map/ppermute | solution.py:359
  103.1 1.3 %collective-permute-start.35 = (bf16[16,1024]{1,0:T(8,128)(2,1)S(1)}, bf16[16,1024]{1,0:T(8,128)(2,1)S(1)}, u32[]{:S(2)}, u32[]{:S(2)}) collective-permute-start(bf16[16,1024]{1,0:T(8,128)(2,1)S(1)} %get-tuple-element.94), channel_id=1, source_target_pairs={{0,2},{1,3},{2,0},{3,1},{4,6},{5,7},{6,4},{7,5},{8,10},{9,11},{10,... | collective-permute-start | bytes 98312 | tf_op jit(solution)/shard_map/ppermute | solution.py:359
  104.5 1.5 %collective-permute-start.36 = (bf16[16,1024]{1,0:T(8,128)(2,1)S(1)}, bf16[16,1024]{1,0:T(8,128)(2,1)S(1)}, u32[]{:S(2)}, u32[]{:S(2)}) collective-permute-start(bf16[16,1024]{1,0:T(8,128)(2,1)S(1)} %get-tuple-element.95), channel_id=1, source_target_pairs={{0,1},{1,0},{2,3},{3,2},{4,5},{5,4},{6,7},{7,6},{8,9},{9,8},{10,11... | collective-permute-start | bytes 98312 | tf_op jit(solution)/shard_map/ppermute | solution.py:359
  106.1 1.2 %collective-permute-done.34.refs_4_ = bf16[16,1024]{1,0:T(8,128)(2,1)S(1)} collective-permute-done((bf16[16,1024]{1,0:T(8,128)(2,1)S(1)}, bf16[16,1024]{1,0:T(8,128)(2,1)S(1)}, u32[]{:S(2)}, u32[]{:S(2)}) %collective-permute-start.34) | collective-permute-done | bytes 32800 | tf_op jit(solution)/shard_map/ppermute | solution.py:359
  107.3 1.1 %collective-permute-done.36.refs_6_ = bf16[16,1024]{1,0:T(8,128)(2,1)S(1)} collective-permute-done((bf16[16,1024]{1,0:T(8,128)(2,1)S(1)}, bf16[16,1024]{1,0:T(8,128)(2,1)S(1)}, u32[]{:S(2)}, u32[]{:S(2)}) %collective-permute-start.36) | collective-permute-done | bytes 32800 | tf_op jit(solution)/shard_map/ppermute | solution.py:359
  108.4 1.1 shard_map.113
  (59 shorter events, 8.0 us)
Async XLA Ops:
  0.0 30.2 %collective-permute-start.6 = (bf16[512,1024]{1,0:T(8,128)(2,1)}, bf16[512,1024]{1,0:T(8,128)(2,1)S(1)}, u32[]{:S(2)}, u32[]{:S(2)}) collective-permute-start(bf16[512,1024]{1,0:T(8,128)(2,1)} %refs_0_.1), channel_id=1, source_target_pairs={{0,1},{1,0},{2,3},{3,2},{4,5},{5,4},{6,7},{7,6},{8,9},{9,8},{10,11... | collective-permute-start | bytes 3145736 | tf_op jit(solution)/shard_map/ppermute | solution.py:359
  2.9 29.0 %collective-permute-start.7 = (bf16[512,1024]{1,0:T(8,128)(2,1)}, bf16[512,1024]{1,0:T(8,128)(2,1)S(1)}, u32[]{:S(2)}, u32[]{:S(2)}) collective-permute-start(bf16[512,1024]{1,0:T(8,128)(2,1)} %refs_0_.1), channel_id=1, source_target_pairs={{0,2},{1,3},{2,0},{3,1},{4,6},{5,7},{6,4},{7,5},{8,10},{9,11},{10,... | collective-permute-start | bytes 3145736 | tf_op jit(solution)/shard_map/ppermute | solution.py:359
  6.0 9.3 %collective-permute-start = (bf16[64,2048]{1,0:T(8,128)(2,1)S(1)}, bf16[64,2048]{1,0:T(8,128)(2,1)S(1)}, u32[]{:S(2)}, u32[]{:S(2)}) collective-permute-start(bf16[64,2048]{1,0:T(8,128)(2,1)S(1)} %get-tuple-element.51), channel_id=1, source_target_pairs={{0,16},{1,17},{2,18},{3,19},{4,20},{5,21},{6,22},{7,23},{8,24},{9,... | collective-permute-start | bytes 786440 | tf_op jit(solution)/shard_map/ppermute | solution.py:359
  7.6 10.6 %collective-permute-start.1 = (bf16[64,2048]{1,0:T(8,128)(2,1)S(1)}, bf16[64,2048]{1,0:T(8,128)(2,1)S(1)}, u32[]{:S(2)}, u32[]{:S(2)}) collective-permute-start(bf16[64,2048]{1,0:T(8,128)(2,1)S(1)} %get-tuple-element.52), channel_id=1, source_target_pairs={{0,24},{1,25},{2,26},{3,27},{4,28},{5,29},{6,30},{7,31},{8,16},{9,... | collective-permute-start | bytes 786440 | tf_op jit(solution)/shard_map/ppermute | solution.py:359
  7.6 10.6 %collective-permute-start.2 = (bf16[64,2048]{1,0:T(8,128)(2,1)S(1)}, bf16[64,2048]{1,0:T(8,128)(2,1)S(1)}, u32[]{:S(2)}, u32[]{:S(2)}) collective-permute-start(bf16[64,2048]{1,0:T(8,128)(2,1)S(1)} %get-tuple-element.53), channel_id=1, source_target_pairs={{0,8},{1,9},{2,10},{3,11},{4,12},{5,13},{6,14},{7,15},{8,0},{9,1},... | collective-permute-start | bytes 786440 | tf_op jit(solution)/shard_map/ppermute | solution.py:359
  22.8 9.1 %collective-permute-start.4 = (bf16[256,512]{1,0:T(8,128)(2,1)S(1)}, bf16[256,512]{1,0:T(8,128)(2,1)S(1)}, u32[]{:S(2)}, u32[]{:S(2)}) collective-permute-start(bf16[256,512]{1,0:T(8,128)(2,1)S(1)} %shard_map.102.refs_1_), channel_id=1, source_target_pairs={{0,16},{1,17},{2,18},{3,19},{4,20},{5,21},{6,22},{7,23},{8,24},{9,... | collective-permute-start | bytes 786440 | tf_op jit(solution)/shard_map/ppermute | solution.py:359
  23.6 15.2 %collective-permute-start.8 = (bf16[256,512]{1,0:T(8,128)(2,1)S(1)}, bf16[256,512]{1,0:T(8,128)(2,1)S(1)}, u32[]{:S(2)}, u32[]{:S(2)}) collective-permute-start(bf16[256,512]{1,0:T(8,128)(2,1)S(1)} %get-tuple-element.55), channel_id=1, source_target_pairs={{0,4},{1,5},{2,6},{3,7},{4,0},{5,1},{6,2},{7,3},{8,12},{9,13},{10,... | collective-permute-start | bytes 786440 | tf_op jit(solution)/shard_map/ppermute | solution.py:359
  26.2 1.2 %copy-start.1 = (bf16[512,1024]{1,0:T(8,128)(2,1)S(1)}, bf16[512,1024]{1,0:T(8,128)(2,1)}, u32[]{:S(2)}) copy-start(bf16[512,1024]{1,0:T(8,128)(2,1)} %refs_0_.1) | copy-start | bytes 3145732
  27.4 1.0 copy-start.2
  28.5 0.7 copy-start.3
  29.2 0.7 copy-start.4
  30.3 19.8 %collective-permute-start.12 = (bf16[512,384]{1,0:T(8,128)(2,1)S(1)}, bf16[512,384]{1,0:T(8,128)(2,1)S(1)}, u32[]{:S(2)}, u32[]{:S(2)}) collective-permute-start(bf16[512,384]{1,0:T(8,128)(2,1)S(1)} %slice.6), channel_id=1, source_target_pairs={{0,2},{1,3},{2,0},{3,1},{4,6},{5,7},{6,4},{7,5},{8,10},{9,11},{10,... | collective-permute-start | bytes 1179656 | tf_op jit(solution)/shard_map/ppermute | solution.py:359
  32.0 20.6 %collective-permute-start.14 = (bf16[512,640]{1,0:T(8,128)(2,1)S(1)}, bf16[512,640]{1,0:T(8,128)(2,1)S(1)}, u32[]{:S(2)}, u32[]{:S(2)}) collective-permute-start(bf16[512,640]{1,0:T(8,128)(2,1)S(1)} %slice.7), channel_id=1, source_target_pairs={{0,1},{1,0},{2,3},{3,2},{4,5},{5,4},{6,7},{7,6},{8,9},{9,8},{10,11... | collective-permute-start | bytes 1966088 | tf_op jit(solution)/shard_map/ppermute | solution.py:359
  32.6 8.5 %collective-permute-start.11 = (s32[4,8,64]{2,1,0:T(8,128)S(1)}, s32[4,8,64]{2,1,0:T(8,128)S(1)}, u32[]{:S(2)}, u32[]{:S(2)}) collective-permute-start(s32[4,8,64]{2,1,0:T(8,128)S(1)} %bitcast.23), channel_id=1, source_target_pairs={{0,4},{1,5},{2,6},{3,7},{4,0},{5,1},{6,2},{7,3},{8,12},{9,13},{10,... | collective-permute-start | bytes 24584 | tf_op jit(solution)/shard_map/ppermute | solution.py:359
  35.3 7.9 %collective-permute-start.3 = (bf16[256,512]{1,0:T(8,128)(2,1)S(1)}, bf16[256,512]{1,0:T(8,128)(2,1)S(1)}, u32[]{:S(2)}, u32[]{:S(2)}) collective-permute-start(bf16[256,512]{1,0:T(8,128)(2,1)S(1)} %shard_map.102.refs_1_), channel_id=1, source_target_pairs={{0,8},{1,9},{2,10},{3,11},{4,12},{5,13},{6,14},{7,15},{8,0},{9,1},... | collective-permute-start | bytes 786440 | tf_op jit(solution)/shard_map/ppermute | solution.py:359
  38.9 4.3 %collective-permute-start.5 = (bf16[256,512]{1,0:T(8,128)(2,1)S(1)}, bf16[256,512]{1,0:T(8,128)(2,1)S(1)}, u32[]{:S(2)}, u32[]{:S(2)}) collective-permute-start(bf16[256,512]{1,0:T(8,128)(2,1)S(1)} %collective-permute-done.4.refs_3_), channel_id=1, source_target_pairs={{0,8},{1,9},{2,10},{3,11},{4,12},{5,13},{6,14},{7,15},{8,0},{9,1},... | collective-permute-start | bytes 786440 | tf_op jit(solution)/shard_map/ppermute | solution.py:359
  41.1 8.9 %collective-permute-start.10 = (bf16[256,512]{1,0:T(8,128)(2,1)S(1)}, bf16[256,512]{1,0:T(8,128)(2,1)S(1)}, u32[]{:S(2)}, u32[]{:S(2)}) collective-permute-start(bf16[256,512]{1,0:T(8,128)(2,1)S(1)} %collective-permute-done.8.refs_0_), channel_id=1, source_target_pairs={{0,16},{1,17},{2,18},{3,19},{4,20},{5,21},{6,22},{7,23},{8,24},{9,... | collective-permute-start | bytes 786440 | tf_op jit(solution)/shard_map/ppermute | solution.py:359
  43.1 6.9 %collective-permute-start.9 = (bf16[256,512]{1,0:T(8,128)(2,1)S(1)}, bf16[256,512]{1,0:T(8,128)(2,1)S(1)}, u32[]{:S(2)}, u32[]{:S(2)}) collective-permute-start(bf16[256,512]{1,0:T(8,128)(2,1)S(1)} %collective-permute-done.8.refs_0_), channel_id=1, source_target_pairs={{0,8},{1,9},{2,10},{3,11},{4,12},{5,13},{6,14},{7,15},{8,0},{9,1},... | collective-permute-start | bytes 786440 | tf_op jit(solution)/shard_map/ppermute | solution.py:359
  43.2 28.3 %slice-start = ((s8[6291456]{0:T(1024)(128)(4,1)}), s8[4194304]{0:T(1024)(128)(4,1)S(1)}, s32[]{:S(2)}) async-start(s8[6291456]{0:T(1024)(128)(4,1)} %bitcast.16), calls=%async_computation | async-start | bytes 8388608
  43.2 28.3 %copy-start.5 = (f32[1024]{0:T(1024)S(1)}, f32[1024]{0:T(1024)}, u32[]{:S(2)}) copy-start(f32[1024]{0:T(1024)} %param.15) | copy-start | bytes 12292
  50.1 21.5 %slice-start.1 = ((s8[6291456]{0:T(1024)(128)(4,1)}), s8[2097152]{0:T(1024)(128)(4,1)S(1)}, s32[]{:S(2)}) async-start(s8[6291456]{0:T(1024)(128)(4,1)} %bitcast.16), calls=%async_computation.1 | async-start | bytes 4194304
  50.1 1.5 %collective-permute-start.13 = (bf16[256,512]{1,0:T(8,128)(2,1)S(1)}, bf16[256,512]{1,0:T(8,128)(2,1)S(1)}, u32[]{:S(2)}, u32[]{:S(2)}) collective-permute-start(bf16[256,512]{1,0:T(8,128)(2,1)S(1)} %collective-permute-done.10.refs_2_), channel_id=1, source_target_pairs={{0,8},{1,9},{2,10},{3,11},{4,12},{5,13},{6,14},{7,15},{8,0},{9,1},... | collective-permute-start | bytes 786440 | tf_op jit(solution)/shard_map/ppermute | solution.py:359
  52.7 35.4 %copy-start = (bf16[1,1536,1024]{2,1,0:T(8,128)(2,1)S(1)}, bf16[1,1536,1024]{2,1,0:T(8,128)(2,1)}, u32[]{:S(2)}) copy-start(bf16[1,1536,1024]{2,1,0:T(8,128)(2,1)} %param.19) | copy-start | bytes 9437188
  54.2 11.7 %collective-permute-start.15 = (bf16[32,1024]{1,0:T(8,128)(2,1)S(1)}, bf16[32,1024]{1,0:T(8,128)(2,1)S(1)}, u32[]{:S(2)}, u32[]{:S(2)}) collective-permute-start(bf16[32,1024]{1,0:T(8,128)(2,1)S(1)} %get-tuple-element.73), channel_id=1, source_target_pairs={{0,4},{1,5},{2,6},{3,7},{4,0},{5,1},{6,2},{7,3},{8,12},{9,13},{10,... | collective-permute-start | bytes 196616 | tf_op jit(solution)/shard_map/ppermute | solution.py:359
  57.4 9.9 %collective-permute-start.16 = (bf16[32,1024]{1,0:T(8,128)(2,1)S(1)}, bf16[32,1024]{1,0:T(8,128)(2,1)S(1)}, u32[]{:S(2)}, u32[]{:S(2)}) collective-permute-start(bf16[32,1024]{1,0:T(8,128)(2,1)S(1)} %get-tuple-element.74), channel_id=1, source_target_pairs={{0,5},{1,4},{2,7},{3,6},{4,1},{5,0},{6,3},{7,2},{8,13},{9,12},{10,... | collective-permute-start | bytes 196616 | tf_op jit(solution)/shard_map/ppermute | solution.py:359
  57.4 11.4 %collective-permute-start.17 = (bf16[32,1024]{1,0:T(8,128)(2,1)S(1)}, bf16[32,1024]{1,0:T(8,128)(2,1)S(1)}, u32[]{:S(2)}, u32[]{:S(2)}) collective-permute-start(bf16[32,1024]{1,0:T(8,128)(2,1)S(1)} %get-tuple-element.75), channel_id=1, source_target_pairs={{0,6},{1,7},{2,4},{3,5},{4,2},{5,3},{6,0},{7,1},{8,14},{9,15},{10,... | collective-permute-start | bytes 196616 | tf_op jit(solution)/shard_map/ppermute | solution.py:359
  58.3 10.5 %collective-permute-start.18 = (bf16[32,1024]{1,0:T(8,128)(2,1)S(1)}, bf16[32,1024]{1,0:T(8,128)(2,1)S(1)}, u32[]{:S(2)}, u32[]{:S(2)}) collective-permute-start(bf16[32,1024]{1,0:T(8,128)(2,1)S(1)} %get-tuple-element.76), channel_id=1, source_target_pairs={{0,7},{1,6},{2,5},{3,4},{4,3},{5,2},{6,1},{7,0},{8,15},{9,14},{10,... | collective-permute-start | bytes 196616 | tf_op jit(solution)/shard_map/ppermute | solution.py:359
  62.2 6.6 %collective-permute-start.19 = (bf16[32,1024]{1,0:T(8,128)(2,1)S(1)}, bf16[32,1024]{1,0:T(8,128)(2,1)S(1)}, u32[]{:S(2)}, u32[]{:S(2)}) collective-permute-start(bf16[32,1024]{1,0:T(8,128)(2,1)S(1)} %get-tuple-element.77), channel_id=1, source_target_pairs={{0,3},{1,2},{2,1},{3,0},{4,7},{5,6},{6,5},{7,4},{8,11},{9,10},{10,... | collective-permute-start | bytes 196616 | tf_op jit(solution)/shard_map/ppermute | solution.py:359
  65.9 4.3 %collective-permute-start.20 = (bf16[32,1024]{1,0:T(8,128)(2,1)S(1)}, bf16[32,1024]{1,0:T(8,128)(2,1)S(1)}, u32[]{:S(2)}, u32[]{:S(2)}) collective-permute-start(bf16[32,1024]{1,0:T(8,128)(2,1)S(1)} %get-tuple-element.78), channel_id=1, source_target_pairs={{0,2},{1,3},{2,0},{3,1},{4,6},{5,7},{6,4},{7,5},{8,10},{9,11},{10,... | collective-permute-start | bytes 196616 | tf_op jit(solution)/shard_map/ppermute | solution.py:359
  67.2 4.3 %collective-permute-start.21 = (bf16[32,1024]{1,0:T(8,128)(2,1)S(1)}, bf16[32,1024]{1,0:T(8,128)(2,1)S(1)}, u32[]{:S(2)}, u32[]{:S(2)}) collective-permute-start(bf16[32,1024]{1,0:T(8,128)(2,1)S(1)} %get-tuple-element.79), channel_id=1, source_target_pairs={{0,1},{1,0},{2,3},{3,2},{4,5},{5,4},{6,7},{7,6},{8,9},{9,8},{10,11... | collective-permute-start | bytes 196616 | tf_op jit(solution)/shard_map/ppermute | solution.py:359
  72.8 1.5 %collective-permute-start.23 = (bf16[32,3200]{1,0:T(8,128)(2,1)S(1)}, bf16[32,3200]{1,0:T(8,128)(2,1)S(1)}, u32[]{:S(2)}, u32[]{:S(2)}) collective-permute-start(bf16[32,3200]{1,0:T(8,128)(2,1)S(1)} %get-tuple-element.84), channel_id=1, source_target_pairs={{0,8},{1,9},{2,10},{3,11},{4,12},{5,13},{6,14},{7,15},{8,0},{9,1},... | collective-permute-start | bytes 614408 | tf_op jit(solution)/shard_map/ppermute | solution.py:359
  72.8 1.7 %collective-permute-start.24 = (bf16[32,3200]{1,0:T(8,128)(2,1)S(1)}, bf16[32,3200]{1,0:T(8,128)(2,1)S(1)}, u32[]{:S(2)}, u32[]{:S(2)}) collective-permute-start(bf16[32,3200]{1,0:T(8,128)(2,1)S(1)} %get-tuple-element.85), channel_id=1, source_target_pairs={{0,8},{1,9},{2,10},{3,11},{4,12},{5,13},{6,14},{7,15},{8,0},{9,1},... | collective-permute-start | bytes 614408 | tf_op jit(solution)/shard_map/ppermute | solution.py:359
  73.3 29.1 %collective-permute-start.22 = (bf16[256,1024]{1,0:T(8,128)(2,1)S(1)}, bf16[256,1024]{1,0:T(8,128)(2,1)S(1)}, u32[]{:S(2)}, u32[]{:S(2)}) collective-permute-start(bf16[256,1024]{1,0:T(8,128)(2,1)S(1)} %get-tuple-element.81), channel_id=1, source_target_pairs={{0,4},{1,5},{2,6},{3,7},{4,0},{5,1},{6,2},{7,3},{8,12},{9,13},{10,... | collective-permute-start | bytes 1572872 | tf_op jit(solution)/shard_map/ppermute | solution.py:359
  74.7 5.8 %collective-permute-start.25 = (bf16[16,3200]{1,0:T(8,128)(2,1)S(1)}, bf16[16,3200]{1,0:T(8,128)(2,1)S(1)}, u32[]{:S(2)}, u32[]{:S(2)}) collective-permute-start(bf16[16,3200]{1,0:T(8,128)(2,1)S(1)} %get-tuple-element.87), channel_id=1, source_target_pairs={{0,16},{1,17},{2,18},{3,19},{4,20},{5,21},{6,22},{7,23},{8,24},{9,... | collective-permute-start | bytes 307208 | tf_op jit(solution)/shard_map/ppermute | solution.py:359
  75.6 6.3 %collective-permute-start.26 = (bf16[16,3200]{1,0:T(8,128)(2,1)S(1)}, bf16[16,3200]{1,0:T(8,128)(2,1)S(1)}, u32[]{:S(2)}, u32[]{:S(2)}) collective-permute-start(bf16[16,3200]{1,0:T(8,128)(2,1)S(1)} %get-tuple-element.88), channel_id=1, source_target_pairs={{0,16},{1,17},{2,18},{3,19},{4,20},{5,21},{6,22},{7,23},{8,24},{9,... | collective-permute-start | bytes 307208 | tf_op jit(solution)/shard_map/ppermute | solution.py:359
  82.1 4.7 %collective-permute-start.28 = (bf16[32,1536]{1,0:T(8,128)(2,1)S(1)}, bf16[32,1536]{1,0:T(8,128)(2,1)S(1)}, u32[]{:S(2)}, u32[]{:S(2)}) collective-permute-start(bf16[32,1536]{1,0:T(8,128)(2,1)S(1)} %shard_map.111.refs_0_), channel_id=1, source_target_pairs={{0,16},{1,17},{2,18},{3,19},{4,20},{5,21},{6,22},{7,23},{8,24},{9,... | collective-permute-start | bytes 294920 | tf_op jit(solution)/shard_map/ppermute | solution.py:359
  83.0 3.8 %collective-permute-start.27 = (bf16[32,1536]{1,0:T(8,128)(2,1)S(1)}, bf16[32,1536]{1,0:T(8,128)(2,1)S(1)}, u32[]{:S(2)}, u32[]{:S(2)}) collective-permute-start(bf16[32,1536]{1,0:T(8,128)(2,1)S(1)} %shard_map.111.refs_0_), channel_id=1, source_target_pairs={{0,8},{1,9},{2,10},{3,11},{4,12},{5,13},{6,14},{7,15},{8,0},{9,1},... | collective-permute-start | bytes 294920 | tf_op jit(solution)/shard_map/ppermute | solution.py:359
  86.8 1.3 %collective-permute-start.29 = (bf16[32,1536]{1,0:T(8,128)(2,1)S(1)}, bf16[32,1536]{1,0:T(8,128)(2,1)S(1)}, u32[]{:S(2)}, u32[]{:S(2)}) collective-permute-start(bf16[32,1536]{1,0:T(8,128)(2,1)S(1)} %collective-permute-done.28.refs_2_), channel_id=1, source_target_pairs={{0,8},{1,9},{2,10},{3,11},{4,12},{5,13},{6,14},{7,15},{8,0},{9,1},... | collective-permute-start | bytes 294920 | tf_op jit(solution)/shard_map/ppermute | solution.py:359
  88.7 14.4 %collective-permute-start.30 = (bf16[16,1024]{1,0:T(8,128)(2,1)S(1)}, bf16[16,1024]{1,0:T(8,128)(2,1)S(1)}, u32[]{:S(2)}, u32[]{:S(2)}) collective-permute-start(bf16[16,1024]{1,0:T(8,128)(2,1)S(1)} %get-tuple-element.89), channel_id=1, source_target_pairs={{0,4},{1,5},{2,6},{3,7},{4,0},{5,1},{6,2},{7,3},{8,12},{9,13},{10,... | collective-permute-start | bytes 98312 | tf_op jit(solution)/shard_map/ppermute | solution.py:359
  90.1 14.4 %collective-permute-start.31 = (bf16[16,1024]{1,0:T(8,128)(2,1)S(1)}, bf16[16,1024]{1,0:T(8,128)(2,1)S(1)}, u32[]{:S(2)}, u32[]{:S(2)}) collective-permute-start(bf16[16,1024]{1,0:T(8,128)(2,1)S(1)} %get-tuple-element.90), channel_id=1, source_target_pairs={{0,5},{1,4},{2,7},{3,6},{4,1},{5,0},{6,3},{7,2},{8,13},{9,12},{10,... | collective-permute-start | bytes 98312 | tf_op jit(solution)/shard_map/ppermute | solution.py:359
  92.7 13.4 %collective-permute-start.32 = (bf16[16,1024]{1,0:T(8,128)(2,1)S(1)}, bf16[16,1024]{1,0:T(8,128)(2,1)S(1)}, u32[]{:S(2)}, u32[]{:S(2)}) collective-permute-start(bf16[16,1024]{1,0:T(8,128)(2,1)S(1)} %get-tuple-element.91), channel_id=1, source_target_pairs={{0,6},{1,7},{2,4},{3,5},{4,2},{5,3},{6,0},{7,1},{8,14},{9,15},{10,... | collective-permute-start | bytes 98312 | tf_op jit(solution)/shard_map/ppermute | solution.py:359
  94.5 11.6 %collective-permute-start.33 = (bf16[16,1024]{1,0:T(8,128)(2,1)S(1)}, bf16[16,1024]{1,0:T(8,128)(2,1)S(1)}, u32[]{:S(2)}, u32[]{:S(2)}) collective-permute-start(bf16[16,1024]{1,0:T(8,128)(2,1)S(1)} %get-tuple-element.92), channel_id=1, source_target_pairs={{0,7},{1,6},{2,5},{3,4},{4,3},{5,2},{6,1},{7,0},{8,15},{9,14},{10,... | collective-permute-start | bytes 98312 | tf_op jit(solution)/shard_map/ppermute | solution.py:359
  102.4 4.8 %collective-permute-start.34 = (bf16[16,1024]{1,0:T(8,128)(2,1)S(1)}, bf16[16,1024]{1,0:T(8,128)(2,1)S(1)}, u32[]{:S(2)}, u32[]{:S(2)}) collective-permute-start(bf16[16,1024]{1,0:T(8,128)(2,1)S(1)} %get-tuple-element.93), channel_id=1, source_target_pairs={{0,3},{1,2},{2,1},{3,0},{4,7},{5,6},{6,5},{7,4},{8,11},{9,10},{10,... | collective-permute-start | bytes 98312 | tf_op jit(solution)/shard_map/ppermute | solution.py:359
  103.1 4.1 %collective-permute-start.35 = (bf16[16,1024]{1,0:T(8,128)(2,1)S(1)}, bf16[16,1024]{1,0:T(8,128)(2,1)S(1)}, u32[]{:S(2)}, u32[]{:S(2)}) collective-permute-start(bf16[16,1024]{1,0:T(8,128)(2,1)S(1)} %get-tuple-element.94), channel_id=1, source_target_pairs={{0,2},{1,3},{2,0},{3,1},{4,6},{5,7},{6,4},{7,5},{8,10},{9,11},{10,... | collective-permute-start | bytes 98312 | tf_op jit(solution)/shard_map/ppermute | solution.py:359
  104.5 3.9 %collective-permute-start.36 = (bf16[16,1024]{1,0:T(8,128)(2,1)S(1)}, bf16[16,1024]{1,0:T(8,128)(2,1)S(1)}, u32[]{:S(2)}, u32[]{:S(2)}) collective-permute-start(bf16[16,1024]{1,0:T(8,128)(2,1)S(1)} %get-tuple-element.95), channel_id=1, source_target_pairs={{0,1},{1,0},{2,3},{3,2},{4,5},{5,4},{6,7},{7,6},{8,9},{9,8},{10,11... | collective-permute-start | bytes 98312 | tf_op jit(solution)/shard_map/ppermute | solution.py:359

commit v18 on v16

--- a/solution.py
+++ b/solution.py
@@ -471,7 +471,7 @@
         bit //= 2
     keep, *sends = call(
         functools.partial(gate_up_kernel, C, E, cap, order),
-        [sds((slots // 2, wide + 128), F32)] + [sds((slots // 4, wide + 128), BF16)] * 2,
+        [sds((slots // 2, wide + 128), F32)] + [sds((slots // 8, wide + 128), BF16)] * 4,
         E + 2,
         scratch=[pltpu.VMEM((slots, width), BF16), pltpu.VMEM((slots, wide + 128), F32)],
         cost=(0, 2**10),

time: 108 us -> 105 us (0.972)
  waiting for transfers between devices: 51.4 us -> 48.6 us
    ppermute x37 -> x39, waiting for transfers between devices: 51.4 us -> 48.6 us  [permute(): return lax.ppermute(x, ('ctx', 'exp'), pairs)]
    ppermute x37 -> x39, starting transfers between devices: 38 us -> 38.3 us  [permute(): return lax.ppermute(x, ('ctx', 'exp'), pairs)]
  transfers between devices with their start and end apart: 37 -> 39, of which waited for: 21 -> 23; matrix products, arithmetic and copies ran while one was open for 0% -> 0% of each run, Pallas kernels for 9% -> 11%
where the time goes in v18:
time: 105 us
  waiting for transfers between devices  48.6 us (46%)
  starting transfers between devices  38.3 us (36%)
  Pallas kernels  13.7 us (13%)
  local copies, waits for them, and re-layouts  3.83 us (4%)
    ppermute x39, waiting for transfers between devices, permute(): return lax.ppermute(x, ('ctx', 'exp'), pairs)  48.6 us
    ppermute x39, starting transfers between devices, permute(): return lax.ppermute(x, ('ctx', 'exp'), pairs)  38.3 us
    pallas_call x2, Pallas kernels, attend(): call(functools.partial(attend_kernel, C, t), [sds((rows, qw), BF16)] + [s...  4.65 us
    unnamed x16, local copies, waits for them, and re-layouts  3.72 us
    pallas_call x2, Pallas kernels, project(): call(functools.partial(project_kernel, C, bool(extra)), [sds((rows, width...  2.14 us
  transfers between devices with their start and end apart: 39, of which 23 were waited for; matrix products, arithmetic and copies ran while one was open for 0% of the time, Pallas kernels for 11%

profile of v18, /device:TPU:0, one launch (start us, length us, event | category | flops | bytes accessed | tf_op | source)
XLA Modules:
  0.0 104.6 jit_solution(15110408246400441123)
XLA Ops:
  0.0 2.9 %collective-permute-start.6 = (bf16[512,1024]{1,0:T(8,128)(2,1)}, bf16[512,1024]{1,0:T(8,128)(2,1)S(1)}, u32[]{:S(2)}, u32[]{:S(2)}) collective-permute-start(bf16[512,1024]{1,0:T(8,128)(2,1)} %refs_0_.1), channel_id=1, source_target_pairs={{0,1},{1,0},{2,3},{3,2},{4,5},{5,4},{6,7},{7,6},{8,9},{9,8},{10,11... | collective-permute-start | bytes 3145736 | tf_op jit(solution)/shard_map/ppermute | solution.py:359
  2.9 1.6 %collective-permute-start.7 = (bf16[512,1024]{1,0:T(8,128)(2,1)}, bf16[512,1024]{1,0:T(8,128)(2,1)S(1)}, u32[]{:S(2)}, u32[]{:S(2)}) collective-permute-start(bf16[512,1024]{1,0:T(8,128)(2,1)} %refs_0_.1), channel_id=1, source_target_pairs={{0,2},{1,3},{2,0},{3,1},{4,6},{5,7},{6,4},{7,5},{8,10},{9,11},{10,... | collective-permute-start | bytes 3145736 | tf_op jit(solution)/shard_map/ppermute | solution.py:359
  4.5 1.4 %shard_map.100 = (bf16[64,2048]{1,0:T(8,128)(2,1)S(1)}, bf16[64,2048]{1,0:T(8,128)(2,1)S(1)}, bf16[64,2048]{1,0:T(8,128)(2,1)S(1)}, bf16[64,2048]{1,0:T(8,128)(2,1)S(1)}) custom-call(bf16[64,4096]{1,0:T(8,128)(2,1)} %bitcast.25, bf16[64,512]{1,0:T(8,128)(2,1)} %bitcast.26, bf16[64,512]{1,0:T(8,128)(2,1)} %bitcast.27), custom_call_target="tpu_custom_call" | custom-call | bytes 1048576 | tf_op jit(solution)/shard_map/pallas_call | solution.py:365
  6.0 1.6 %collective-permute-start = (bf16[64,2048]{1,0:T(8,128)(2,1)S(1)}, bf16[64,2048]{1,0:T(8,128)(2,1)S(1)}, u32[]{:S(2)}, u32[]{:S(2)}) collective-permute-start(bf16[64,2048]{1,0:T(8,128)(2,1)S(1)} %get-tuple-element.53), channel_id=1, source_target_pairs={{0,16},{1,17},{2,18},{3,19},{4,20},{5,21},{6,22},{7,23},{8,24},{9,... | collective-permute-start | bytes 786440 | tf_op jit(solution)/shard_map/ppermute | solution.py:359
  8.2 7.1 %collective-permute-done.refs_0_ = bf16[64,2048]{1,0:T(8,128)(2,1)S(1)} collective-permute-done((bf16[64,2048]{1,0:T(8,128)(2,1)S(1)}, bf16[64,2048]{1,0:T(8,128)(2,1)S(1)}, u32[]{:S(2)}, u32[]{:S(2)}) %collective-permute-start) | collective-permute-done | bytes 262176 | tf_op jit(solution)/shard_map/ppermute | solution.py:359
  15.3 2.9 %collective-permute-done.1.refs_1_ = bf16[64,2048]{1,0:T(8,128)(2,1)S(1)} collective-permute-done((bf16[64,2048]{1,0:T(8,128)(2,1)S(1)}, bf16[64,2048]{1,0:T(8,128)(2,1)S(1)}, u32[]{:S(2)}, u32[]{:S(2)}) %collective-permute-start.1) | collective-permute-done | bytes 262176 | tf_op jit(solution)/shard_map/ppermute | solution.py:359
  18.2 2.3 %shard_map.101 = (bf16[256,512]{1,0:T(8,128)(2,1)S(1)}, bf16[64,2048]{1,0:T(8,128)(2,1)S(1)}) custom-call(bf16[64,2048]{1,0:T(8,128)(2,1)S(1)} %collective-permute-done.refs_0_, bf16[64,2048]{1,0:T(8,128)(2,1)S(1)} %collective-permute-done.1.refs_1_, bf16[64,2048]{1,0:T(8,128)(2,1)S(1)} %collective-permute-done.2.refs_2_, ...), custom_call_target="tpu_custom_call" | custom-call | bytes 16384 | tf_op jit(solution)/shard_map/pallas_call | solution.py:386
  20.5 2.3 %shard_map.102.refs_1_ = bf16[256,512]{1,0:T(8,128)(2,1)S(1)} custom-call(bf16[64,2048]{1,0:T(8,128)(2,1)S(1)} %collective-permute-done.refs_0_, bf16[64,2048]{1,0:T(8,128)(2,1)S(1)} %collective-permute-done.1.refs_1_, bf16[64,2048]{1,0:T(8,128)(2,1)S(1)} %collective-permute-done.2.refs_2_, bf16[64,2048]{1,0:T(8,128)(2,1)S(1)} %get-tuple-element.59.refs_3_), custom_call_target="tpu_custom_call" | custom-call | bytes 16384 | tf_op jit(solution)/shard_map/pallas_call | solution.py:386
  22.8 0.8 collective-permute-start.4
  23.6 2.6 %collective-permute-start.8 = (bf16[256,512]{1,0:T(8,128)(2,1)S(1)}, bf16[256,512]{1,0:T(8,128)(2,1)S(1)}, u32[]{:S(2)}, u32[]{:S(2)}) collective-permute-start(bf16[256,512]{1,0:T(8,128)(2,1)S(1)} %get-tuple-element.57), channel_id=1, source_target_pairs={{0,4},{1,5},{2,6},{3,7},{4,0},{5,1},{6,2},{7,3},{8,12},{9,13},{10,... | collective-permute-start | bytes 786440 | tf_op jit(solution)/shard_map/ppermute | solution.py:359
  26.2 1.2 %copy-done.1 = bf16[512,1024]{1,0:T(8,128)(2,1)S(1)} copy-done((bf16[512,1024]{1,0:T(8,128)(2,1)S(1)}, bf16[512,1024]{1,0:T(8,128)(2,1)}, u32[]{:S(2)}) %copy-start.1) | copy-done | bytes 1048600
  27.4 1.0 copy-done.2
  28.5 0.7 copy-done.3
  30.8 1.2 %collective-permute-done.4.refs_3_ = bf16[256,512]{1,0:T(8,128)(2,1)S(1)} collective-permute-done((bf16[256,512]{1,0:T(8,128)(2,1)S(1)}, bf16[256,512]{1,0:T(8,128)(2,1)S(1)}, u32[]{:S(2)}, u32[]{:S(2)}) %collective-permute-start.4) | collective-permute-done | bytes 262176 | tf_op jit(solution)/shard_map/ppermute | solution.py:359
  32.6 6.2 %collective-permute-done.8.refs_0_ = bf16[256,512]{1,0:T(8,128)(2,1)S(1)} collective-permute-done((bf16[256,512]{1,0:T(8,128)(2,1)S(1)}, bf16[256,512]{1,0:T(8,128)(2,1)S(1)}, u32[]{:S(2)}, u32[]{:S(2)}) %collective-permute-start.8) | collective-permute-done | bytes 262176 | tf_op jit(solution)/shard_map/ppermute | solution.py:359
  38.9 1.7 %collective-permute-start.10 = (bf16[256,512]{1,0:T(8,128)(2,1)S(1)}, bf16[256,512]{1,0:T(8,128)(2,1)S(1)}, u32[]{:S(2)}, u32[]{:S(2)}) collective-permute-start(bf16[256,512]{1,0:T(8,128)(2,1)S(1)} %collective-permute-done.8.refs_0_), channel_id=1, source_target_pairs={{0,16},{1,17},{2,18},{3,19},{4,20},{5,21},{6,22},{7,23},{8,24},{9,... | collective-permute-start | bytes 786440 | tf_op jit(solution)/shard_map/ppermute | solution.py:359
  40.6 6.9 %collective-permute-done.10.refs_2_ = bf16[256,512]{1,0:T(8,128)(2,1)S(1)} collective-permute-done((bf16[256,512]{1,0:T(8,128)(2,1)S(1)}, bf16[256,512]{1,0:T(8,128)(2,1)S(1)}, u32[]{:S(2)}, u32[]{:S(2)}) %collective-permute-start.10) | collective-permute-done | bytes 262176 | tf_op jit(solution)/shard_map/ppermute | solution.py:359
  49.0 1.1 %shard_map.104 = (f32[256,1024]{1,0:T(8,128)S(1)}, bf16[256,512]{1,0:T(8,128)(2,1)S(1)}) custom-call(bf16[256,1024]{1,0:T(8,128)(2,1)S(1)} %get-tuple-element.61.refs_0_, bf16[256,512]{1,0:T(8,128)(2,1)S(1)} %shard_map.102.refs_1_, bf16[256,512]{1,0:T(8,128)(2,1)S(1)} %collective-permute-done.3.refs_2_, bf16[256,512]{1,0:T(8,128)(2,1)S(1)} %collective-permute-done.4.refs_3_, ...), custom_call_target="tpu_custom_call" | custom-call | bytes 16384 | tf_op jit(solution)/shard_map/pallas_call | solution.py:431
  50.1 1.1 %shard_map.105 = (f32[256,1024]{1,0:T(8,128)S(1)}, bf16[256,512]{1,0:T(8,128)(2,1)S(1)}) custom-call(bf16[256,512]{1,0:T(8,128)(2,1)S(1)} %collective-permute-done.8.refs_0_, bf16[256,512]{1,0:T(8,128)(2,1)S(1)} %collective-permute-done.9.refs_1_, bf16[256,512]{1,0:T(8,128)(2,1)S(1)} %collective-permute-done.10.refs_2_, ...), custom_call_target="tpu_custom_call" | custom-call | bytes 16384 | tf_op jit(solution)/shard_map/pallas_call | solution.py:431
  51.2 1.5 %shard_map.107 = (f32[256,1024]{1,0:T(8,128)S(1)}, bf16[256,1024]{1,0:T(8,128)(2,1)S(1)}, bf16[32,1024]{1,0:T(8,128)(2,1)S(1)}, bf16[32,1024]{1,0:T(8,128)(2,1)S...) custom-call(f32[256,1024]{1,0:T(8,128)S(1)} %get-tuple-element.63.re, ...), custom_call_target="tpu_custom_call" | custom-call | bytes 16384 | tf_op jit(solution)/shard_map/pallas_call | solution.py:454
  53.1 2.5 %collective-permute-start.16 = (bf16[32,1024]{1,0:T(8,128)(2,1)S(1)}, bf16[32,1024]{1,0:T(8,128)(2,1)S(1)}, u32[]{:S(2)}, u32[]{:S(2)}) collective-permute-start(bf16[32,1024]{1,0:T(8,128)(2,1)S(1)} %get-tuple-element.76), channel_id=1, source_target_pairs={{0,5},{1,4},{2,7},{3,6},{4,1},{5,0},{6,3},{7,2},{8,13},{9,12},{10,... | collective-permute-start | bytes 196616 | tf_op jit(solution)/shard_map/ppermute | solution.py:359
  55.7 2.5 %collective-permute-start.17 = (bf16[32,1024]{1,0:T(8,128)(2,1)S(1)}, bf16[32,1024]{1,0:T(8,128)(2,1)S(1)}, u32[]{:S(2)}, u32[]{:S(2)}) collective-permute-start(bf16[32,1024]{1,0:T(8,128)(2,1)S(1)} %get-tuple-element.77), channel_id=1, source_target_pairs={{0,6},{1,7},{2,4},{3,5},{4,2},{5,3},{6,0},{7,1},{8,14},{9,15},{10,... | collective-permute-start | bytes 196616 | tf_op jit(solution)/shard_map/ppermute | solution.py:359
  58.2 2.2 %collective-permute-start.18 = (bf16[32,1024]{1,0:T(8,128)(2,1)S(1)}, bf16[32,1024]{1,0:T(8,128)(2,1)S(1)}, u32[]{:S(2)}, u32[]{:S(2)}) collective-permute-start(bf16[32,1024]{1,0:T(8,128)(2,1)S(1)} %get-tuple-element.78), channel_id=1, source_target_pairs={{0,7},{1,6},{2,5},{3,4},{4,3},{5,2},{6,1},{7,0},{8,15},{9,14},{10,... | collective-permute-start | bytes 196616 | tf_op jit(solution)/shard_map/ppermute | solution.py:359
  60.4 1.6 %collective-permute-done.15.refs_0_ = bf16[32,1024]{1,0:T(8,128)(2,1)S(1)} collective-permute-done((bf16[32,1024]{1,0:T(8,128)(2,1)S(1)}, bf16[32,1024]{1,0:T(8,128)(2,1)S(1)}, u32[]{:S(2)}, u32[]{:S(2)}) %collective-permute-start.15) | collective-permute-done | bytes 65568 | tf_op jit(solution)/shard_map/ppermute | solution.py:359
  62.4 1.7 %collective-permute-done.16.refs_1_ = bf16[32,1024]{1,0:T(8,128)(2,1)S(1)} collective-permute-done((bf16[32,1024]{1,0:T(8,128)(2,1)S(1)}, bf16[32,1024]{1,0:T(8,128)(2,1)S(1)}, u32[]{:S(2)}, u32[]{:S(2)}) %collective-permute-start.16) | collective-permute-done | bytes 65568 | tf_op jit(solution)/shard_map/ppermute | solution.py:359
  64.1 1.5 %collective-permute-start.21 = (bf16[32,1024]{1,0:T(8,128)(2,1)S(1)}, bf16[32,1024]{1,0:T(8,128)(2,1)S(1)}, u32[]{:S(2)}, u32[]{:S(2)}) collective-permute-start(bf16[32,1024]{1,0:T(8,128)(2,1)S(1)} %get-tuple-element.81), channel_id=1, source_target_pairs={{0,1},{1,0},{2,3},{3,2},{4,5},{5,4},{6,7},{7,6},{8,9},{9,8},{10,11... | collective-permute-start | bytes 196616 | tf_op jit(solution)/shard_map/ppermute | solution.py:359
  65.6 1.1 %collective-permute-done.19.refs_4_ = bf16[32,1024]{1,0:T(8,128)(2,1)S(1)} collective-permute-done((bf16[32,1024]{1,0:T(8,128)(2,1)S(1)}, bf16[32,1024]{1,0:T(8,128)(2,1)S(1)}, u32[]{:S(2)}, u32[]{:S(2)}) %collective-permute-start.19) | collective-permute-done | bytes 65568 | tf_op jit(solution)/shard_map/ppermute | solution.py:359
  66.7 0.8 collective-permute-done.20.refs_5_
  67.6 0.8 collective-permute-done.21.refs_6_
  68.9 1.3 %shard_map.109 = (f32[64,3200]{1,0:T(8,128)S(1)}, bf16[16,3200]{1,0:T(8,128)(2,1)S(1)}, bf16[16,3200]{1,0:T(8,128)(2,1)S(1)}, bf16[16,3200]{1,0:T(8,128)(2,1)S(1)}, bf16[16,3200]{1,0:T(8,128)(2,1)S(1)}) custom-call(bf16[32,1024]{1,0:T(8,128)(2,1)S(1)} %collective-permute-done.15.refs_0_, bf16[32,1024]{1,0:T(8,128)(2,1)S(1)} %collective-permute-done.16.refs_1_, ...), custom_call_target="tpu_custom_call" | custom-call | bytes 1024 | tf_op jit(solution)/shard_map/pallas_call | solution.py:472
  72.3 1.2 %collective-permute-start.27 = (bf16[16,3200]{1,0:T(8,128)(2,1)S(1)}, bf16[16,3200]{1,0:T(8,128)(2,1)S(1)}, u32[]{:S(2)}, u32[]{:S(2)}) collective-permute-start(bf16[16,3200]{1,0:T(8,128)(2,1)S(1)} %get-tuple-element.91), channel_id=1, source_target_pairs={{0,16},{1,17},{2,18},{3,19},{4,20},{5,21},{6,22},{7,23},{8,24},{9,... | collective-permute-start | bytes 307208 | tf_op jit(solution)/shard_map/ppermute | solution.py:359
  73.5 0.9 collective-permute-start.28
  74.4 3.7 %collective-permute-done.27.refs_0_ = bf16[16,3200]{1,0:T(8,128)(2,1)S(1)} collective-permute-done((bf16[16,3200]{1,0:T(8,128)(2,1)S(1)}, bf16[16,3200]{1,0:T(8,128)(2,1)S(1)}, u32[]{:S(2)}, u32[]{:S(2)}) %collective-permute-start.27) | collective-permute-done | bytes 102432 | tf_op jit(solution)/shard_map/ppermute | solution.py:359
  78.0 1.6 %collective-permute-done.28.refs_1_ = bf16[16,3200]{1,0:T(8,128)(2,1)S(1)} collective-permute-done((bf16[16,3200]{1,0:T(8,128)(2,1)S(1)}, bf16[16,3200]{1,0:T(8,128)(2,1)S(1)}, u32[]{:S(2)}, u32[]{:S(2)}) %collective-permute-start.28) | collective-permute-done | bytes 102432 | tf_op jit(solution)/shard_map/ppermute | solution.py:359
  79.8 1.2 %collective-permute-start.30 = (bf16[32,1536]{1,0:T(8,128)(2,1)S(1)}, bf16[32,1536]{1,0:T(8,128)(2,1)S(1)}, u32[]{:S(2)}, u32[]{:S(2)}) collective-permute-start(bf16[32,1536]{1,0:T(8,128)(2,1)S(1)} %shard_map.111.refs_0_), channel_id=1, source_target_pairs={{0,16},{1,17},{2,18},{3,19},{4,20},{5,21},{6,22},{7,23},{8,24},{9,... | collective-permute-start | bytes 294920 | tf_op jit(solution)/shard_map/ppermute | solution.py:359
  81.1 3.5 %collective-permute-done.30.refs_2_ = bf16[32,1536]{1,0:T(8,128)(2,1)S(1)} collective-permute-done((bf16[32,1536]{1,0:T(8,128)(2,1)S(1)}, bf16[32,1536]{1,0:T(8,128)(2,1)S(1)}, u32[]{:S(2)}, u32[]{:S(2)}) %collective-permute-start.30) | collective-permute-done | bytes 98336 | tf_op jit(solution)/shard_map/ppermute | solution.py:359
  84.5 1.3 %collective-permute-done.31.refs_3_ = bf16[32,1536]{1,0:T(8,128)(2,1)S(1)} collective-permute-done((bf16[32,1536]{1,0:T(8,128)(2,1)S(1)}, bf16[32,1536]{1,0:T(8,128)(2,1)S(1)}, u32[]{:S(2)}, u32[]{:S(2)}) %collective-permute-start.31) | collective-permute-done | bytes 98336 | tf_op jit(solution)/shard_map/ppermute | solution.py:359
  86.5 2.5 %collective-permute-start.32 = (bf16[16,1024]{1,0:T(8,128)(2,1)S(1)}, bf16[16,1024]{1,0:T(8,128)(2,1)S(1)}, u32[]{:S(2)}, u32[]{:S(2)}) collective-permute-start(bf16[16,1024]{1,0:T(8,128)(2,1)S(1)} %get-tuple-element.93), channel_id=1, source_target_pairs={{0,4},{1,5},{2,6},{3,7},{4,0},{5,1},{6,2},{7,3},{8,12},{9,13},{10,... | collective-permute-start | bytes 98312 | tf_op jit(solution)/shard_map/ppermute | solution.py:359
  89.0 1.5 %collective-permute-start.33 = (bf16[16,1024]{1,0:T(8,128)(2,1)S(1)}, bf16[16,1024]{1,0:T(8,128)(2,1)S(1)}, u32[]{:S(2)}, u32[]{:S(2)}) collective-permute-start(bf16[16,1024]{1,0:T(8,128)(2,1)S(1)} %get-tuple-element.94), channel_id=1, source_target_pairs={{0,5},{1,4},{2,7},{3,6},{4,1},{5,0},{6,3},{7,2},{8,13},{9,12},{10,... | collective-permute-start | bytes 98312 | tf_op jit(solution)/shard_map/ppermute | solution.py:359
  90.5 2.1 %collective-permute-start.34 = (bf16[16,1024]{1,0:T(8,128)(2,1)S(1)}, bf16[16,1024]{1,0:T(8,128)(2,1)S(1)}, u32[]{:S(2)}, u32[]{:S(2)}) collective-permute-start(bf16[16,1024]{1,0:T(8,128)(2,1)S(1)} %get-tuple-element.95), channel_id=1, source_target_pairs={{0,6},{1,7},{2,4},{3,5},{4,2},{5,3},{6,0},{7,1},{8,14},{9,15},{10,... | collective-permute-start | bytes 98312 | tf_op jit(solution)/shard_map/ppermute | solution.py:359
  92.7 1.5 %collective-permute-start.35 = (bf16[16,1024]{1,0:T(8,128)(2,1)S(1)}, bf16[16,1024]{1,0:T(8,128)(2,1)S(1)}, u32[]{:S(2)}, u32[]{:S(2)}) collective-permute-start(bf16[16,1024]{1,0:T(8,128)(2,1)S(1)} %get-tuple-element.96), channel_id=1, source_target_pairs={{0,7},{1,6},{2,5},{3,4},{4,3},{5,2},{6,1},{7,0},{8,15},{9,14},{10,... | collective-permute-start | bytes 98312 | tf_op jit(solution)/shard_map/ppermute | solution.py:359
  94.2 3.5 %collective-permute-done.32.refs_0_ = bf16[16,1024]{1,0:T(8,128)(2,1)S(1)} collective-permute-done((bf16[16,1024]{1,0:T(8,128)(2,1)S(1)}, bf16[16,1024]{1,0:T(8,128)(2,1)S(1)}, u32[]{:S(2)}, u32[]{:S(2)}) %collective-permute-start.32) | collective-permute-done | bytes 32800 | tf_op jit(solution)/shard_map/ppermute | solution.py:359
  97.8 0.9 collective-permute-done.33.refs_1_
  98.6 1.0 collective-permute-start.37
  99.6 1.6 %collective-permute-start.38 = (bf16[16,1024]{1,0:T(8,128)(2,1)S(1)}, bf16[16,1024]{1,0:T(8,128)(2,1)S(1)}, u32[]{:S(2)}, u32[]{:S(2)}) collective-permute-start(bf16[16,1024]{1,0:T(8,128)(2,1)S(1)} %get-tuple-element.99), channel_id=1, source_target_pairs={{0,1},{1,0},{2,3},{3,2},{4,5},{5,4},{6,7},{7,6},{8,9},{9,8},{10,11... | collective-permute-start | bytes 98312 | tf_op jit(solution)/shard_map/ppermute | solution.py:359
  101.4 1.2 %collective-permute-done.36.refs_4_ = bf16[16,1024]{1,0:T(8,128)(2,1)S(1)} collective-permute-done((bf16[16,1024]{1,0:T(8,128)(2,1)S(1)}, bf16[16,1024]{1,0:T(8,128)(2,1)S(1)}, u32[]{:S(2)}, u32[]{:S(2)}) %collective-permute-start.36) | collective-permute-done | bytes 32800 | tf_op jit(solution)/shard_map/ppermute | solution.py:359
  102.6 1.0 collective-permute-done.38.refs_6_
  103.5 1.1 %shard_map.113 = bf16[256,1024]{1,0:T(8,128)(2,1)} custom-call(f32[256,1024]{1,0:T(8,128)S(1)} %shard_map.108.mixed, bf16[128,256]{1,0:T(8,128)(2,1)S(1)} %get-tuple-element.64.refs_6_.place_ref, f32[256,128]{1,0:T(8,128)S(1)} %get-tuple-element.84.gate_ref, bf16[16,1024]{1,0:T(8,128)(2,1)S(1)} %collective-permute-done.32.refs_0_, ...), custom_call_target="tpu_custom_call" | custom-call | bytes 2097152 | tf_op jit(solution)/shard_map/pallas_call | solution.py:512
  (63 shorter events, 8.8 us)
Async XLA Ops:
  0.0 30.2 %collective-permute-start.6 = (bf16[512,1024]{1,0:T(8,128)(2,1)}, bf16[512,1024]{1,0:T(8,128)(2,1)S(1)}, u32[]{:S(2)}, u32[]{:S(2)}) collective-permute-start(bf16[512,1024]{1,0:T(8,128)(2,1)} %refs_0_.1), channel_id=1, source_target_pairs={{0,1},{1,0},{2,3},{3,2},{4,5},{5,4},{6,7},{7,6},{8,9},{9,8},{10,11... | collective-permute-start | bytes 3145736 | tf_op jit(solution)/shard_map/ppermute | solution.py:359
  2.9 29.0 %collective-permute-start.7 = (bf16[512,1024]{1,0:T(8,128)(2,1)}, bf16[512,1024]{1,0:T(8,128)(2,1)S(1)}, u32[]{:S(2)}, u32[]{:S(2)}) collective-permute-start(bf16[512,1024]{1,0:T(8,128)(2,1)} %refs_0_.1), channel_id=1, source_target_pairs={{0,2},{1,3},{2,0},{3,1},{4,6},{5,7},{6,4},{7,5},{8,10},{9,11},{10,... | collective-permute-start | bytes 3145736 | tf_op jit(solution)/shard_map/ppermute | solution.py:359
  6.0 9.3 %collective-permute-start = (bf16[64,2048]{1,0:T(8,128)(2,1)S(1)}, bf16[64,2048]{1,0:T(8,128)(2,1)S(1)}, u32[]{:S(2)}, u32[]{:S(2)}) collective-permute-start(bf16[64,2048]{1,0:T(8,128)(2,1)S(1)} %get-tuple-element.53), channel_id=1, source_target_pairs={{0,16},{1,17},{2,18},{3,19},{4,20},{5,21},{6,22},{7,23},{8,24},{9,... | collective-permute-start | bytes 786440 | tf_op jit(solution)/shard_map/ppermute | solution.py:359
  7.6 10.6 %collective-permute-start.1 = (bf16[64,2048]{1,0:T(8,128)(2,1)S(1)}, bf16[64,2048]{1,0:T(8,128)(2,1)S(1)}, u32[]{:S(2)}, u32[]{:S(2)}) collective-permute-start(bf16[64,2048]{1,0:T(8,128)(2,1)S(1)} %get-tuple-element.54), channel_id=1, source_target_pairs={{0,24},{1,25},{2,26},{3,27},{4,28},{5,29},{6,30},{7,31},{8,16},{9,... | collective-permute-start | bytes 786440 | tf_op jit(solution)/shard_map/ppermute | solution.py:359
  7.6 10.6 %collective-permute-start.2 = (bf16[64,2048]{1,0:T(8,128)(2,1)S(1)}, bf16[64,2048]{1,0:T(8,128)(2,1)S(1)}, u32[]{:S(2)}, u32[]{:S(2)}) collective-permute-start(bf16[64,2048]{1,0:T(8,128)(2,1)S(1)} %get-tuple-element.55), channel_id=1, source_target_pairs={{0,8},{1,9},{2,10},{3,11},{4,12},{5,13},{6,14},{7,15},{8,0},{9,1},... | collective-permute-start | bytes 786440 | tf_op jit(solution)/shard_map/ppermute | solution.py:359
  22.8 9.1 %collective-permute-start.4 = (bf16[256,512]{1,0:T(8,128)(2,1)S(1)}, bf16[256,512]{1,0:T(8,128)(2,1)S(1)}, u32[]{:S(2)}, u32[]{:S(2)}) collective-permute-start(bf16[256,512]{1,0:T(8,128)(2,1)S(1)} %shard_map.102.refs_1_), channel_id=1, source_target_pairs={{0,16},{1,17},{2,18},{3,19},{4,20},{5,21},{6,22},{7,23},{8,24},{9,... | collective-permute-start | bytes 786440 | tf_op jit(solution)/shard_map/ppermute | solution.py:359
  23.6 15.2 %collective-permute-start.8 = (bf16[256,512]{1,0:T(8,128)(2,1)S(1)}, bf16[256,512]{1,0:T(8,128)(2,1)S(1)}, u32[]{:S(2)}, u32[]{:S(2)}) collective-permute-start(bf16[256,512]{1,0:T(8,128)(2,1)S(1)} %get-tuple-element.57), channel_id=1, source_target_pairs={{0,4},{1,5},{2,6},{3,7},{4,0},{5,1},{6,2},{7,3},{8,12},{9,13},{10,... | collective-permute-start | bytes 786440 | tf_op jit(solution)/shard_map/ppermute | solution.py:359
  26.2 1.2 %copy-start.1 = (bf16[512,1024]{1,0:T(8,128)(2,1)S(1)}, bf16[512,1024]{1,0:T(8,128)(2,1)}, u32[]{:S(2)}) copy-start(bf16[512,1024]{1,0:T(8,128)(2,1)} %refs_0_.1) | copy-start | bytes 3145732
  27.4 1.0 copy-start.2
  28.5 0.7 copy-start.3
  29.2 0.7 copy-start.4
  30.3 17.2 %collective-permute-start.11 = (bf16[512,384]{1,0:T(8,128)(2,1)S(1)}, bf16[512,384]{1,0:T(8,128)(2,1)S(1)}, u32[]{:S(2)}, u32[]{:S(2)}) collective-permute-start(bf16[512,384]{1,0:T(8,128)(2,1)S(1)} %slice.6), channel_id=1, source_target_pairs={{0,2},{1,3},{2,0},{3,1},{4,6},{5,7},{6,4},{7,5},{8,10},{9,11},{10,... | collective-permute-start | bytes 1179656 | tf_op jit(solution)/shard_map/ppermute | solution.py:359
  32.0 19.1 %collective-permute-start.13 = (bf16[512,640]{1,0:T(8,128)(2,1)S(1)}, bf16[512,640]{1,0:T(8,128)(2,1)S(1)}, u32[]{:S(2)}, u32[]{:S(2)}) collective-permute-start(bf16[512,640]{1,0:T(8,128)(2,1)S(1)} %slice.7), channel_id=1, source_target_pairs={{0,1},{1,0},{2,3},{3,2},{4,5},{5,4},{6,7},{7,6},{8,9},{9,8},{10,11... | collective-permute-start | bytes 1966088 | tf_op jit(solution)/shard_map/ppermute | solution.py:359
  38.9 8.6 %collective-permute-start.10 = (bf16[256,512]{1,0:T(8,128)(2,1)S(1)}, bf16[256,512]{1,0:T(8,128)(2,1)S(1)}, u32[]{:S(2)}, u32[]{:S(2)}) collective-permute-start(bf16[256,512]{1,0:T(8,128)(2,1)S(1)} %collective-permute-done.8.refs_0_), channel_id=1, source_target_pairs={{0,16},{1,17},{2,18},{3,19},{4,20},{5,21},{6,22},{7,23},{8,24},{9,... | collective-permute-start | bytes 786440 | tf_op jit(solution)/shard_map/ppermute | solution.py:359
  40.6 7.4 %collective-permute-start.14 = (s32[4,8,64]{2,1,0:T(8,128)S(1)}, s32[4,8,64]{2,1,0:T(8,128)S(1)}, u32[]{:S(2)}, u32[]{:S(2)}) collective-permute-start(s32[4,8,64]{2,1,0:T(8,128)S(1)} %bitcast.23), channel_id=1, source_target_pairs={{0,4},{1,5},{2,6},{3,7},{4,0},{5,1},{6,2},{7,3},{8,12},{9,13},{10,... | collective-permute-start | bytes 24584 | tf_op jit(solution)/shard_map/ppermute | solution.py:359
  40.6 7.7 %collective-permute-start.3 = (bf16[256,512]{1,0:T(8,128)(2,1)S(1)}, bf16[256,512]{1,0:T(8,128)(2,1)S(1)}, u32[]{:S(2)}, u32[]{:S(2)}) collective-permute-start(bf16[256,512]{1,0:T(8,128)(2,1)S(1)} %shard_map.102.refs_1_), channel_id=1, source_target_pairs={{0,8},{1,9},{2,10},{3,11},{4,12},{5,13},{6,14},{7,15},{8,0},{9,1},... | collective-permute-start | bytes 786440 | tf_op jit(solution)/shard_map/ppermute | solution.py:359
  47.5 1.5 %collective-permute-start.5 = (bf16[256,512]{1,0:T(8,128)(2,1)S(1)}, bf16[256,512]{1,0:T(8,128)(2,1)S(1)}, u32[]{:S(2)}, u32[]{:S(2)}) collective-permute-start(bf16[256,512]{1,0:T(8,128)(2,1)S(1)} %collective-permute-done.4.refs_3_), channel_id=1, source_target_pairs={{0,8},{1,9},{2,10},{3,11},{4,12},{5,13},{6,14},{7,15},{8,0},{9,1},... | collective-permute-start | bytes 786440 | tf_op jit(solution)/shard_map/ppermute | solution.py:359
  47.5 2.6 %collective-permute-start.9 = (bf16[256,512]{1,0:T(8,128)(2,1)S(1)}, bf16[256,512]{1,0:T(8,128)(2,1)S(1)}, u32[]{:S(2)}, u32[]{:S(2)}) collective-permute-start(bf16[256,512]{1,0:T(8,128)(2,1)S(1)} %collective-permute-done.8.refs_0_), channel_id=1, source_target_pairs={{0,8},{1,9},{2,10},{3,11},{4,12},{5,13},{6,14},{7,15},{8,0},{9,1},... | collective-permute-start | bytes 786440 | tf_op jit(solution)/shard_map/ppermute | solution.py:359
  48.0 2.1 %collective-permute-start.12 = (bf16[256,512]{1,0:T(8,128)(2,1)S(1)}, bf16[256,512]{1,0:T(8,128)(2,1)S(1)}, u32[]{:S(2)}, u32[]{:S(2)}) collective-permute-start(bf16[256,512]{1,0:T(8,128)(2,1)S(1)} %collective-permute-done.10.refs_2_), channel_id=1, source_target_pairs={{0,8},{1,9},{2,10},{3,11},{4,12},{5,13},{6,14},{7,15},{8,0},{9,1},... | collective-permute-start | bytes 786440 | tf_op jit(solution)/shard_map/ppermute | solution.py:359
  49.0 19.9 %slice-start = ((s8[6291456]{0:T(1024)(128)(4,1)}), s8[4194304]{0:T(1024)(128)(4,1)S(1)}, s32[]{:S(2)}) async-start(s8[6291456]{0:T(1024)(128)(4,1)} %bitcast.16), calls=%async_computation | async-start | bytes 8388608
  49.0 19.9 %copy-start.5 = (f32[1024]{0:T(1024)S(1)}, f32[1024]{0:T(1024)}, u32[]{:S(2)}) copy-start(f32[1024]{0:T(1024)} %param.15) | copy-start | bytes 12292
  50.1 18.8 %slice-start.1 = ((s8[6291456]{0:T(1024)(128)(4,1)}), s8[2097152]{0:T(1024)(128)(4,1)S(1)}, s32[]{:S(2)}) async-start(s8[6291456]{0:T(1024)(128)(4,1)} %bitcast.16), calls=%async_computation.1 | async-start | bytes 4194304
  51.2 34.6 %copy-start = (bf16[1,1536,1024]{2,1,0:T(8,128)(2,1)S(1)}, bf16[1,1536,1024]{2,1,0:T(8,128)(2,1)}, u32[]{:S(2)}) copy-start(bf16[1,1536,1024]{2,1,0:T(8,128)(2,1)} %param.19) | copy-start | bytes 9437188
  52.7 9.3 %collective-permute-start.15 = (bf16[32,1024]{1,0:T(8,128)(2,1)S(1)}, bf16[32,1024]{1,0:T(8,128)(2,1)S(1)}, u32[]{:S(2)}, u32[]{:S(2)}) collective-permute-start(bf16[32,1024]{1,0:T(8,128)(2,1)S(1)} %get-tuple-element.75), channel_id=1, source_target_pairs={{0,4},{1,5},{2,6},{3,7},{4,0},{5,1},{6,2},{7,3},{8,12},{9,13},{10,... | collective-permute-start | bytes 196616 | tf_op jit(solution)/shard_map/ppermute | solution.py:359
  53.1 11.0 %collective-permute-start.16 = (bf16[32,1024]{1,0:T(8,128)(2,1)S(1)}, bf16[32,1024]{1,0:T(8,128)(2,1)S(1)}, u32[]{:S(2)}, u32[]{:S(2)}) collective-permute-start(bf16[32,1024]{1,0:T(8,128)(2,1)S(1)} %get-tuple-element.76), channel_id=1, source_target_pairs={{0,5},{1,4},{2,7},{3,6},{4,1},{5,0},{6,3},{7,2},{8,13},{9,12},{10,... | collective-permute-start | bytes 196616 | tf_op jit(solution)/shard_map/ppermute | solution.py:359
  55.7 9.9 %collective-permute-start.17 = (bf16[32,1024]{1,0:T(8,128)(2,1)S(1)}, bf16[32,1024]{1,0:T(8,128)(2,1)S(1)}, u32[]{:S(2)}, u32[]{:S(2)}) collective-permute-start(bf16[32,1024]{1,0:T(8,128)(2,1)S(1)} %get-tuple-element.77), channel_id=1, source_target_pairs={{0,6},{1,7},{2,4},{3,5},{4,2},{5,3},{6,0},{7,1},{8,14},{9,15},{10,... | collective-permute-start | bytes 196616 | tf_op jit(solution)/shard_map/ppermute | solution.py:359
  58.2 7.4 %collective-permute-start.18 = (bf16[32,1024]{1,0:T(8,128)(2,1)S(1)}, bf16[32,1024]{1,0:T(8,128)(2,1)S(1)}, u32[]{:S(2)}, u32[]{:S(2)}) collective-permute-start(bf16[32,1024]{1,0:T(8,128)(2,1)S(1)} %get-tuple-element.78), channel_id=1, source_target_pairs={{0,7},{1,6},{2,5},{3,4},{4,3},{5,2},{6,1},{7,0},{8,15},{9,14},{10,... | collective-permute-start | bytes 196616 | tf_op jit(solution)/shard_map/ppermute | solution.py:359
  60.4 6.3 %collective-permute-start.19 = (bf16[32,1024]{1,0:T(8,128)(2,1)S(1)}, bf16[32,1024]{1,0:T(8,128)(2,1)S(1)}, u32[]{:S(2)}, u32[]{:S(2)}) collective-permute-start(bf16[32,1024]{1,0:T(8,128)(2,1)S(1)} %get-tuple-element.79), channel_id=1, source_target_pairs={{0,3},{1,2},{2,1},{3,0},{4,7},{5,6},{6,5},{7,4},{8,11},{9,10},{10,... | collective-permute-start | bytes 196616 | tf_op jit(solution)/shard_map/ppermute | solution.py:359
  62.0 5.5 %collective-permute-start.20 = (bf16[32,1024]{1,0:T(8,128)(2,1)S(1)}, bf16[32,1024]{1,0:T(8,128)(2,1)S(1)}, u32[]{:S(2)}, u32[]{:S(2)}) collective-permute-start(bf16[32,1024]{1,0:T(8,128)(2,1)S(1)} %get-tuple-element.80), channel_id=1, source_target_pairs={{0,2},{1,3},{2,0},{3,1},{4,6},{5,7},{6,4},{7,5},{8,10},{9,11},{10,... | collective-permute-start | bytes 196616 | tf_op jit(solution)/shard_map/ppermute | solution.py:359
  64.1 4.3 %collective-permute-start.21 = (bf16[32,1024]{1,0:T(8,128)(2,1)S(1)}, bf16[32,1024]{1,0:T(8,128)(2,1)S(1)}, u32[]{:S(2)}, u32[]{:S(2)}) collective-permute-start(bf16[32,1024]{1,0:T(8,128)(2,1)S(1)} %get-tuple-element.81), channel_id=1, source_target_pairs={{0,1},{1,0},{2,3},{3,2},{4,5},{5,4},{6,7},{7,6},{8,9},{9,8},{10,11... | collective-permute-start | bytes 196616 | tf_op jit(solution)/shard_map/ppermute | solution.py:359
  68.4 31.2 %collective-permute-start.22 = (bf16[256,1024]{1,0:T(8,128)(2,1)S(1)}, bf16[256,1024]{1,0:T(8,128)(2,1)S(1)}, u32[]{:S(2)}, u32[]{:S(2)}) collective-permute-start(bf16[256,1024]{1,0:T(8,128)(2,1)S(1)} %get-tuple-element.83), channel_id=1, source_target_pairs={{0,4},{1,5},{2,6},{3,7},{4,0},{5,1},{6,2},{7,3},{8,12},{9,13},{10,... | collective-permute-start | bytes 1572872 | tf_op jit(solution)/shard_map/ppermute | solution.py:359
  70.2 1.3 %collective-permute-start.23 = (bf16[16,3200]{1,0:T(8,128)(2,1)S(1)}, bf16[16,3200]{1,0:T(8,128)(2,1)S(1)}, u32[]{:S(2)}, u32[]{:S(2)}) collective-permute-start(bf16[16,3200]{1,0:T(8,128)(2,1)S(1)} %get-tuple-element.86), channel_id=1, source_target_pairs={{0,8},{1,9},{2,10},{3,11},{4,12},{5,13},{6,14},{7,15},{8,0},{9,1},... | collective-permute-start | bytes 307208 | tf_op jit(solution)/shard_map/ppermute | solution.py:359
  70.2 1.4 %collective-permute-start.24 = (bf16[16,3200]{1,0:T(8,128)(2,1)S(1)}, bf16[16,3200]{1,0:T(8,128)(2,1)S(1)}, u32[]{:S(2)}, u32[]{:S(2)}) collective-permute-start(bf16[16,3200]{1,0:T(8,128)(2,1)S(1)} %get-tuple-element.87), channel_id=1, source_target_pairs={{0,8},{1,9},{2,10},{3,11},{4,12},{5,13},{6,14},{7,15},{8,0},{9,1},... | collective-permute-start | bytes 307208 | tf_op jit(solution)/shard_map/ppermute | solution.py:359
  70.7 1.3 %collective-permute-start.25 = (bf16[16,3200]{1,0:T(8,128)(2,1)S(1)}, bf16[16,3200]{1,0:T(8,128)(2,1)S(1)}, u32[]{:S(2)}, u32[]{:S(2)}) collective-permute-start(bf16[16,3200]{1,0:T(8,128)(2,1)S(1)} %get-tuple-element.88), channel_id=1, source_target_pairs={{0,8},{1,9},{2,10},{3,11},{4,12},{5,13},{6,14},{7,15},{8,0},{9,1},... | collective-permute-start | bytes 307208 | tf_op jit(solution)/shard_map/ppermute | solution.py:359
  70.8 1.4 %collective-permute-start.26 = (bf16[16,3200]{1,0:T(8,128)(2,1)S(1)}, bf16[16,3200]{1,0:T(8,128)(2,1)S(1)}, u32[]{:S(2)}, u32[]{:S(2)}) collective-permute-start(bf16[16,3200]{1,0:T(8,128)(2,1)S(1)} %get-tuple-element.89), channel_id=1, source_target_pairs={{0,8},{1,9},{2,10},{3,11},{4,12},{5,13},{6,14},{7,15},{8,0},{9,1},... | collective-permute-start | bytes 307208 | tf_op jit(solution)/shard_map/ppermute | solution.py:359
  72.3 5.8 %collective-permute-start.27 = (bf16[16,3200]{1,0:T(8,128)(2,1)S(1)}, bf16[16,3200]{1,0:T(8,128)(2,1)S(1)}, u32[]{:S(2)}, u32[]{:S(2)}) collective-permute-start(bf16[16,3200]{1,0:T(8,128)(2,1)S(1)} %get-tuple-element.91), channel_id=1, source_target_pairs={{0,16},{1,17},{2,18},{3,19},{4,20},{5,21},{6,22},{7,23},{8,24},{9,... | collective-permute-start | bytes 307208 | tf_op jit(solution)/shard_map/ppermute | solution.py:359
  73.5 6.2 %collective-permute-start.28 = (bf16[16,3200]{1,0:T(8,128)(2,1)S(1)}, bf16[16,3200]{1,0:T(8,128)(2,1)S(1)}, u32[]{:S(2)}, u32[]{:S(2)}) collective-permute-start(bf16[16,3200]{1,0:T(8,128)(2,1)S(1)} %get-tuple-element.92), channel_id=1, source_target_pairs={{0,16},{1,17},{2,18},{3,19},{4,20},{5,21},{6,22},{7,23},{8,24},{9,... | collective-permute-start | bytes 307208 | tf_op jit(solution)/shard_map/ppermute | solution.py:359
  79.8 4.7 %collective-permute-start.30 = (bf16[32,1536]{1,0:T(8,128)(2,1)S(1)}, bf16[32,1536]{1,0:T(8,128)(2,1)S(1)}, u32[]{:S(2)}, u32[]{:S(2)}) collective-permute-start(bf16[32,1536]{1,0:T(8,128)(2,1)S(1)} %shard_map.111.refs_0_), channel_id=1, source_target_pairs={{0,16},{1,17},{2,18},{3,19},{4,20},{5,21},{6,22},{7,23},{8,24},{9,... | collective-permute-start | bytes 294920 | tf_op jit(solution)/shard_map/ppermute | solution.py:359
  81.0 3.5 %collective-permute-start.29 = (bf16[32,1536]{1,0:T(8,128)(2,1)S(1)}, bf16[32,1536]{1,0:T(8,128)(2,1)S(1)}, u32[]{:S(2)}, u32[]{:S(2)}) collective-permute-start(bf16[32,1536]{1,0:T(8,128)(2,1)S(1)} %shard_map.111.refs_0_), channel_id=1, source_target_pairs={{0,8},{1,9},{2,10},{3,11},{4,12},{5,13},{6,14},{7,15},{8,0},{9,1},... | collective-permute-start | bytes 294920 | tf_op jit(solution)/shard_map/ppermute | solution.py:359
  84.5 1.3 %collective-permute-start.31 = (bf16[32,1536]{1,0:T(8,128)(2,1)S(1)}, bf16[32,1536]{1,0:T(8,128)(2,1)S(1)}, u32[]{:S(2)}, u32[]{:S(2)}) collective-permute-start(bf16[32,1536]{1,0:T(8,128)(2,1)S(1)} %collective-permute-done.30.refs_2_), channel_id=1, source_target_pairs={{0,8},{1,9},{2,10},{3,11},{4,12},{5,13},{6,14},{7,15},{8,0},{9,1},... | collective-permute-start | bytes 294920 | tf_op jit(solution)/shard_map/ppermute | solution.py:359
  86.5 11.3 %collective-permute-start.32 = (bf16[16,1024]{1,0:T(8,128)(2,1)S(1)}, bf16[16,1024]{1,0:T(8,128)(2,1)S(1)}, u32[]{:S(2)}, u32[]{:S(2)}) collective-permute-start(bf16[16,1024]{1,0:T(8,128)(2,1)S(1)} %get-tuple-element.93), channel_id=1, source_target_pairs={{0,4},{1,5},{2,6},{3,7},{4,0},{5,1},{6,2},{7,3},{8,12},{9,13},{10,... | collective-permute-start | bytes 98312 | tf_op jit(solution)/shard_map/ppermute | solution.py:359
  89.0 9.7 %collective-permute-start.33 = (bf16[16,1024]{1,0:T(8,128)(2,1)S(1)}, bf16[16,1024]{1,0:T(8,128)(2,1)S(1)}, u32[]{:S(2)}, u32[]{:S(2)}) collective-permute-start(bf16[16,1024]{1,0:T(8,128)(2,1)S(1)} %get-tuple-element.94), channel_id=1, source_target_pairs={{0,5},{1,4},{2,7},{3,6},{4,1},{5,0},{6,3},{7,2},{8,13},{9,12},{10,... | collective-permute-start | bytes 98312 | tf_op jit(solution)/shard_map/ppermute | solution.py:359
  90.5 10.9 %collective-permute-start.34 = (bf16[16,1024]{1,0:T(8,128)(2,1)S(1)}, bf16[16,1024]{1,0:T(8,128)(2,1)S(1)}, u32[]{:S(2)}, u32[]{:S(2)}) collective-permute-start(bf16[16,1024]{1,0:T(8,128)(2,1)S(1)} %get-tuple-element.95), channel_id=1, source_target_pairs={{0,6},{1,7},{2,4},{3,5},{4,2},{5,3},{6,0},{7,1},{8,14},{9,15},{10,... | collective-permute-start | bytes 98312 | tf_op jit(solution)/shard_map/ppermute | solution.py:359
  92.7 8.7 %collective-permute-start.35 = (bf16[16,1024]{1,0:T(8,128)(2,1)S(1)}, bf16[16,1024]{1,0:T(8,128)(2,1)S(1)}, u32[]{:S(2)}, u32[]{:S(2)}) collective-permute-start(bf16[16,1024]{1,0:T(8,128)(2,1)S(1)} %get-tuple-element.96), channel_id=1, source_target_pairs={{0,7},{1,6},{2,5},{3,4},{4,3},{5,2},{6,1},{7,0},{8,15},{9,14},{10,... | collective-permute-start | bytes 98312 | tf_op jit(solution)/shard_map/ppermute | solution.py:359
  97.8 4.8 %collective-permute-start.36 = (bf16[16,1024]{1,0:T(8,128)(2,1)S(1)}, bf16[16,1024]{1,0:T(8,128)(2,1)S(1)}, u32[]{:S(2)}, u32[]{:S(2)}) collective-permute-start(bf16[16,1024]{1,0:T(8,128)(2,1)S(1)} %get-tuple-element.97), channel_id=1, source_target_pairs={{0,3},{1,2},{2,1},{3,0},{4,7},{5,6},{6,5},{7,4},{8,11},{9,10},{10,... | collective-permute-start | bytes 98312 | tf_op jit(solution)/shard_map/ppermute | solution.py:359
  98.6 3.9 %collective-permute-start.37 = (bf16[16,1024]{1,0:T(8,128)(2,1)S(1)}, bf16[16,1024]{1,0:T(8,128)(2,1)S(1)}, u32[]{:S(2)}, u32[]{:S(2)}) collective-permute-start(bf16[16,1024]{1,0:T(8,128)(2,1)S(1)} %get-tuple-element.98), channel_id=1, source_target_pairs={{0,2},{1,3},{2,0},{3,1},{4,6},{5,7},{6,4},{7,5},{8,10},{9,11},{10,... | collective-permute-start | bytes 98312 | tf_op jit(solution)/shard_map/ppermute | solution.py:359
  99.6 3.9 %collective-permute-start.38 = (bf16[16,1024]{1,0:T(8,128)(2,1)S(1)}, bf16[16,1024]{1,0:T(8,128)(2,1)S(1)}, u32[]{:S(2)}, u32[]{:S(2)}) collective-permute-start(bf16[16,1024]{1,0:T(8,128)(2,1)S(1)} %get-tuple-element.99), channel_id=1, source_target_pairs={{0,1},{1,0},{2,3},{3,2},{4,5},{5,4},{6,7},{7,6},{8,9},{9,8},{10,11... | collective-permute-start | bytes 98312 | tf_op jit(solution)/shard_map/ppermute | solution.py:359

commit v19 on v18

--- a/solution.py
+++ b/solution.py
@@ -443,7 +443,7 @@
     near = after(shards[1], place)[:, cut:]
     for d in range(2, C, 2):
         shards[d + 1] = (
-            permute(after(shards[d], place, *mine_all[2::2])[:, :cut], exp=1),
+            permute(after(shards[d], place)[:, :cut], exp=1),
             permute(near, exp=spread(d)),
         )
     acc, last = project(mine_all, res)
@@ -462,7 +462,7 @@
         cost=(0, 2**14),
     )(acc, acc_far, last, last_far, *shards[C - 1], place, other_place)
     incoming = [permute(x, exp=b) if b else x for x, b in zip(outgoing, all_hops(E))]
-    arrived = permute(after(full, *incoming), exp=PAIR)
+    arrived = permute(after(full, *incoming[: E // 2]), exp=PAIR)
 
     order = [0]
     bit = C // 2

time: 105 us -> 102 us (0.971)
  waiting for transfers between devices: 48.6 us -> 38.4 us
  starting transfers between devices: 38.3 us -> 45.7 us
    ppermute x39, waiting for transfers between devices: 48.6 us -> 38.4 us  [permute(): return lax.ppermute(x, ('ctx', 'exp'), pairs)]
    ppermute x39, starting transfers between devices: 38.3 us -> 45.7 us  [permute(): return lax.ppermute(x, ('ctx', 'exp'), pairs)]
  transfers between devices with their start and end apart: 39 -> 39, of which waited for: 23 -> 22; matrix products, arithmetic and copies ran while one was open for 0% -> 0% of each run, Pallas kernels for 11% -> 11%
where the time goes in v19:
time: 102 us
  starting transfers between devices  45.7 us (45%)
  waiting for transfers between devices  38.4 us (38%)
  Pallas kernels  13.6 us (13%)
  local copies, waits for them, and re-layouts  3.82 us (4%)
    ppermute x39, starting transfers between devices, permute(): return lax.ppermute(x, ('ctx', 'exp'), pairs)  45.7 us
    ppermute x39, waiting for transfers between devices, permute(): return lax.ppermute(x, ('ctx', 'exp'), pairs)  38.4 us
    pallas_call x2, Pallas kernels, attend(): call(functools.partial(attend_kernel, C, t), [sds((rows, qw), BF16)] + [s...  4.63 us
    unnamed x16, local copies, waits for them, and re-layouts  3.72 us
    pallas_call x2, Pallas kernels, project(): call(functools.partial(project_kernel, C, bool(extra)), [sds((rows, width...  2.12 us
  transfers between devices with their start and end apart: 39, of which 22 were waited for; matrix products, arithmetic and copies ran while one was open for 0% of the time, Pallas kernels for 11%

profile of v19, /device:TPU:0, one launch (start us, length us, event | category | flops | bytes accessed | tf_op | source)
XLA Modules:
  0.0 101.7 jit_solution(9949913969974595313)
XLA Ops:
  0.0 2.9 %collective-permute-start.6 = (bf16[512,1024]{1,0:T(8,128)(2,1)}, bf16[512,1024]{1,0:T(8,128)(2,1)S(1)}, u32[]{:S(2)}, u32[]{:S(2)}) collective-permute-start(bf16[512,1024]{1,0:T(8,128)(2,1)} %refs_0_.1), channel_id=1, source_target_pairs={{0,1},{1,0},{2,3},{3,2},{4,5},{5,4},{6,7},{7,6},{8,9},{9,8},{10,11... | collective-permute-start | bytes 3145736 | tf_op jit(solution)/shard_map/ppermute | solution.py:359
  2.9 1.6 %collective-permute-start.7 = (bf16[512,1024]{1,0:T(8,128)(2,1)}, bf16[512,1024]{1,0:T(8,128)(2,1)S(1)}, u32[]{:S(2)}, u32[]{:S(2)}) collective-permute-start(bf16[512,1024]{1,0:T(8,128)(2,1)} %refs_0_.1), channel_id=1, source_target_pairs={{0,2},{1,3},{2,0},{3,1},{4,6},{5,7},{6,4},{7,5},{8,10},{9,11},{10,... | collective-permute-start | bytes 3145736 | tf_op jit(solution)/shard_map/ppermute | solution.py:359
  4.5 1.4 %shard_map.100 = (bf16[64,2048]{1,0:T(8,128)(2,1)S(1)}, bf16[64,2048]{1,0:T(8,128)(2,1)S(1)}, bf16[64,2048]{1,0:T(8,128)(2,1)S(1)}, bf16[64,2048]{1,0:T(8,128)(2,1)S(1)}) custom-call(bf16[64,4096]{1,0:T(8,128)(2,1)} %bitcast.25, bf16[64,512]{1,0:T(8,128)(2,1)} %bitcast.26, bf16[64,512]{1,0:T(8,128)(2,1)} %bitcast.27), custom_call_target="tpu_custom_call" | custom-call | bytes 1048576 | tf_op jit(solution)/shard_map/pallas_call | solution.py:365
  6.0 1.6 %collective-permute-start = (bf16[64,2048]{1,0:T(8,128)(2,1)S(1)}, bf16[64,2048]{1,0:T(8,128)(2,1)S(1)}, u32[]{:S(2)}, u32[]{:S(2)}) collective-permute-start(bf16[64,2048]{1,0:T(8,128)(2,1)S(1)} %get-tuple-element.53), channel_id=1, source_target_pairs={{0,16},{1,17},{2,18},{3,19},{4,20},{5,21},{6,22},{7,23},{8,24},{9,... | collective-permute-start | bytes 786440 | tf_op jit(solution)/shard_map/ppermute | solution.py:359
  8.2 7.1 %collective-permute-done.refs_0_ = bf16[64,2048]{1,0:T(8,128)(2,1)S(1)} collective-permute-done((bf16[64,2048]{1,0:T(8,128)(2,1)S(1)}, bf16[64,2048]{1,0:T(8,128)(2,1)S(1)}, u32[]{:S(2)}, u32[]{:S(2)}) %collective-permute-start) | collective-permute-done | bytes 262176 | tf_op jit(solution)/shard_map/ppermute | solution.py:359
  15.3 2.9 %collective-permute-done.1.refs_1_ = bf16[64,2048]{1,0:T(8,128)(2,1)S(1)} collective-permute-done((bf16[64,2048]{1,0:T(8,128)(2,1)S(1)}, bf16[64,2048]{1,0:T(8,128)(2,1)S(1)}, u32[]{:S(2)}, u32[]{:S(2)}) %collective-permute-start.1) | collective-permute-done | bytes 262176 | tf_op jit(solution)/shard_map/ppermute | solution.py:359
  18.2 2.3 %shard_map.101 = (bf16[256,512]{1,0:T(8,128)(2,1)S(1)}, bf16[64,2048]{1,0:T(8,128)(2,1)S(1)}) custom-call(bf16[64,2048]{1,0:T(8,128)(2,1)S(1)} %collective-permute-done.refs_0_, bf16[64,2048]{1,0:T(8,128)(2,1)S(1)} %collective-permute-done.1.refs_1_, bf16[64,2048]{1,0:T(8,128)(2,1)S(1)} %collective-permute-done.2.refs_2_, ...), custom_call_target="tpu_custom_call" | custom-call | bytes 16384 | tf_op jit(solution)/shard_map/pallas_call | solution.py:386
  20.5 2.7 %collective-permute-start.8 = (bf16[256,512]{1,0:T(8,128)(2,1)S(1)}, bf16[256,512]{1,0:T(8,128)(2,1)S(1)}, u32[]{:S(2)}, u32[]{:S(2)}) collective-permute-start(bf16[256,512]{1,0:T(8,128)(2,1)S(1)} %get-tuple-element.57), channel_id=1, source_target_pairs={{0,4},{1,5},{2,6},{3,7},{4,0},{5,1},{6,2},{7,3},{8,12},{9,13},{10,... | collective-permute-start | bytes 786440 | tf_op jit(solution)/shard_map/ppermute | solution.py:359
  23.2 2.3 %shard_map.102.refs_1_ = bf16[256,512]{1,0:T(8,128)(2,1)S(1)} custom-call(bf16[64,2048]{1,0:T(8,128)(2,1)S(1)} %collective-permute-done.refs_0_, bf16[64,2048]{1,0:T(8,128)(2,1)S(1)} %collective-permute-done.1.refs_1_, bf16[64,2048]{1,0:T(8,128)(2,1)S(1)} %collective-permute-done.2.refs_2_, bf16[64,2048]{1,0:T(8,128)(2,1)S(1)} %get-tuple-element.59.refs_3_), custom_call_target="tpu_custom_call" | custom-call | bytes 16384 | tf_op jit(solution)/shard_map/pallas_call | solution.py:386
  25.5 1.2 %copy-done.1 = bf16[512,1024]{1,0:T(8,128)(2,1)S(1)} copy-done((bf16[512,1024]{1,0:T(8,128)(2,1)S(1)}, bf16[512,1024]{1,0:T(8,128)(2,1)}, u32[]{:S(2)}) %copy-start.1) | copy-done | bytes 1048600
  26.7 1.0 %copy-done.2 = bf16[4,1,64,1024]{3,2,1,0:T(8,128)(2,1)S(1)} copy-done((bf16[4,1,64,1024]{3,2,1,0:T(8,128)(2,1)S(1)}, bf16[4,1,64,1024]{3,2,1,0:T(8,128)(2,1)}, u32[]{:S(2)}) %copy-start.2) | copy-done | bytes 524312
  27.7 0.7 copy-done.3
  28.5 0.7 copy-done.4
  30.1 2.5 %collective-permute-done.7.refs_7_.refs_6_ = bf16[512,1024]{1,0:T(8,128)(2,1)S(1)} collective-permute-done((bf16[512,1024]{1,0:T(8,128)(2,1)}, bf16[512,1024]{1,0:T(8,128)(2,1)S(1)}, u32[]{:S(2)}, u32[]{:S(2)}) %collective-permute-start.7) | collective-permute-done | bytes 1048608 | tf_op jit(solution)/shard_map/ppermute | solution.py:359
  33.1 2.8 %collective-permute-start.4 = (bf16[256,512]{1,0:T(8,128)(2,1)S(1)}, bf16[256,512]{1,0:T(8,128)(2,1)S(1)}, u32[]{:S(2)}, u32[]{:S(2)}) collective-permute-start(bf16[256,512]{1,0:T(8,128)(2,1)S(1)} %shard_map.102.refs_1_), channel_id=1, source_target_pairs={{0,16},{1,17},{2,18},{3,19},{4,20},{5,21},{6,22},{7,23},{8,24},{9,... | collective-permute-start | bytes 786440 | tf_op jit(solution)/shard_map/ppermute | solution.py:359
  35.9 2.9 %collective-permute-start.14 = (s32[4,8,64]{2,1,0:T(8,128)S(1)}, s32[4,8,64]{2,1,0:T(8,128)S(1)}, u32[]{:S(2)}, u32[]{:S(2)}) collective-permute-start(s32[4,8,64]{2,1,0:T(8,128)S(1)} %bitcast.23), channel_id=1, source_target_pairs={{0,4},{1,5},{2,6},{3,7},{4,0},{5,1},{6,2},{7,3},{8,12},{9,13},{10,... | collective-permute-start | bytes 24584 | tf_op jit(solution)/shard_map/ppermute | solution.py:359
  38.9 3.8 %collective-permute-done.4.refs_3_ = bf16[256,512]{1,0:T(8,128)(2,1)S(1)} collective-permute-done((bf16[256,512]{1,0:T(8,128)(2,1)S(1)}, bf16[256,512]{1,0:T(8,128)(2,1)S(1)}, u32[]{:S(2)}, u32[]{:S(2)}) %collective-permute-start.4) | collective-permute-done | bytes 262176 | tf_op jit(solution)/shard_map/ppermute | solution.py:359
  42.7 3.4 %collective-permute-done.10.refs_2_ = bf16[256,512]{1,0:T(8,128)(2,1)S(1)} collective-permute-done((bf16[256,512]{1,0:T(8,128)(2,1)S(1)}, bf16[256,512]{1,0:T(8,128)(2,1)S(1)}, u32[]{:S(2)}, u32[]{:S(2)}) %collective-permute-start.10) | collective-permute-done | bytes 262176 | tf_op jit(solution)/shard_map/ppermute | solution.py:359
  46.9 0.7 collective-permute-done.5.refs_4_
  47.6 1.1 %shard_map.104 = (f32[256,1024]{1,0:T(8,128)S(1)}, bf16[256,512]{1,0:T(8,128)(2,1)S(1)}) custom-call(bf16[256,1024]{1,0:T(8,128)(2,1)S(1)} %get-tuple-element.61.refs_0_, bf16[256,512]{1,0:T(8,128)(2,1)S(1)} %shard_map.102.refs_1_, bf16[256,512]{1,0:T(8,128)(2,1)S(1)} %collective-permute-done.3.refs_2_, bf16[256,512]{1,0:T(8,128)(2,1)S(1)} %collective-permute-done.4.refs_3_, ...), custom_call_target="tpu_custom_call" | custom-call | bytes 16384 | tf_op jit(solution)/shard_map/pallas_call | solution.py:431
  48.7 1.1 %shard_map.105 = (f32[256,1024]{1,0:T(8,128)S(1)}, bf16[256,512]{1,0:T(8,128)(2,1)S(1)}) custom-call(bf16[256,512]{1,0:T(8,128)(2,1)S(1)} %collective-permute-done.8.refs_0_, bf16[256,512]{1,0:T(8,128)(2,1)S(1)} %collective-permute-done.9.refs_1_, bf16[256,512]{1,0:T(8,128)(2,1)S(1)} %collective-permute-done.10.refs_2_, ...), custom_call_target="tpu_custom_call" | custom-call | bytes 16384 | tf_op jit(solution)/shard_map/pallas_call | solution.py:431
  49.8 1.5 %shard_map.107 = (f32[256,1024]{1,0:T(8,128)S(1)}, bf16[256,1024]{1,0:T(8,128)(2,1)S(1)}, bf16[32,1024]{1,0:T(8,128)(2,1)S(1)}, bf16[32,1024]{1,0:T(8,128)(2,1)S...) custom-call(f32[256,1024]{1,0:T(8,128)S(1)} %get-tuple-element.63.re, ...), custom_call_target="tpu_custom_call" | custom-call | bytes 16384 | tf_op jit(solution)/shard_map/pallas_call | solution.py:454
  51.3 0.7 collective-permute-start.15
  52.0 3.2 %collective-permute-start.16 = (bf16[32,1024]{1,0:T(8,128)(2,1)S(1)}, bf16[32,1024]{1,0:T(8,128)(2,1)S(1)}, u32[]{:S(2)}, u32[]{:S(2)}) collective-permute-start(bf16[32,1024]{1,0:T(8,128)(2,1)S(1)} %get-tuple-element.76), channel_id=1, source_target_pairs={{0,5},{1,4},{2,7},{3,6},{4,1},{5,0},{6,3},{7,2},{8,13},{9,12},{10,... | collective-permute-start | bytes 196616 | tf_op jit(solution)/shard_map/ppermute | solution.py:359
  55.2 2.8 %collective-permute-start.17 = (bf16[32,1024]{1,0:T(8,128)(2,1)S(1)}, bf16[32,1024]{1,0:T(8,128)(2,1)S(1)}, u32[]{:S(2)}, u32[]{:S(2)}) collective-permute-start(bf16[32,1024]{1,0:T(8,128)(2,1)S(1)} %get-tuple-element.77), channel_id=1, source_target_pairs={{0,6},{1,7},{2,4},{3,5},{4,2},{5,3},{6,0},{7,1},{8,14},{9,15},{10,... | collective-permute-start | bytes 196616 | tf_op jit(solution)/shard_map/ppermute | solution.py:359
  58.0 1.0 collective-permute-start.18
  59.0 3.0 %collective-permute-start.21 = (bf16[32,1024]{1,0:T(8,128)(2,1)S(1)}, bf16[32,1024]{1,0:T(8,128)(2,1)S(1)}, u32[]{:S(2)}, u32[]{:S(2)}) collective-permute-start(bf16[32,1024]{1,0:T(8,128)(2,1)S(1)} %get-tuple-element.82), channel_id=1, source_target_pairs={{0,2},{1,3},{2,0},{3,1},{4,6},{5,7},{6,4},{7,5},{8,10},{9,11},{10,... | collective-permute-start | bytes 196616 | tf_op jit(solution)/shard_map/ppermute | solution.py:359
  62.0 2.0 %collective-permute-done.16.refs_1_ = bf16[32,1024]{1,0:T(8,128)(2,1)S(1)} collective-permute-done((bf16[32,1024]{1,0:T(8,128)(2,1)S(1)}, bf16[32,1024]{1,0:T(8,128)(2,1)S(1)}, u32[]{:S(2)}, u32[]{:S(2)}) %collective-permute-start.16) | collective-permute-done | bytes 65568 | tf_op jit(solution)/shard_map/ppermute | solution.py:359
  63.9 1.2 %collective-permute-done.18.refs_3_ = bf16[32,1024]{1,0:T(8,128)(2,1)S(1)} collective-permute-done((bf16[32,1024]{1,0:T(8,128)(2,1)S(1)}, bf16[32,1024]{1,0:T(8,128)(2,1)S(1)}, u32[]{:S(2)}, u32[]{:S(2)}) %collective-permute-start.18) | collective-permute-done | bytes 65568 | tf_op jit(solution)/shard_map/ppermute | solution.py:359
  65.1 2.9 %collective-permute-start.19 = (bf16[256,1024]{1,0:T(8,128)(2,1)S(1)}, bf16[256,1024]{1,0:T(8,128)(2,1)S(1)}, u32[]{:S(2)}, u32[]{:S(2)}) collective-permute-start(bf16[256,1024]{1,0:T(8,128)(2,1)S(1)} %get-tuple-element.79), channel_id=1, source_target_pairs={{0,4},{1,5},{2,6},{3,7},{4,0},{5,1},{6,2},{7,3},{8,12},{9,13},{10,... | collective-permute-start | bytes 1572872 | tf_op jit(solution)/shard_map/ppermute | solution.py:359
  68.2 1.3 %shard_map.109 = (f32[64,3200]{1,0:T(8,128)S(1)}, bf16[16,3200]{1,0:T(8,128)(2,1)S(1)}, bf16[16,3200]{1,0:T(8,128)(2,1)S(1)}, bf16[16,3200]{1,0:T(8,128)(2,1)S(1)}, bf16[16,3200]{1,0:T(8,128)(2,1)S(1)}) custom-call(bf16[32,1024]{1,0:T(8,128)(2,1)S(1)} %collective-permute-done.15.refs_0_, bf16[32,1024]{1,0:T(8,128)(2,1)S(1)} %collective-permute-done.16.refs_1_, ...), custom_call_target="tpu_custom_call" | custom-call | bytes 1024 | tf_op jit(solution)/shard_map/pallas_call | solution.py:472
  71.6 1.7 %collective-permute-start.27 = (bf16[16,3200]{1,0:T(8,128)(2,1)S(1)}, bf16[16,3200]{1,0:T(8,128)(2,1)S(1)}, u32[]{:S(2)}, u32[]{:S(2)}) collective-permute-start(bf16[16,3200]{1,0:T(8,128)(2,1)S(1)} %get-tuple-element.91), channel_id=1, source_target_pairs={{0,16},{1,17},{2,18},{3,19},{4,20},{5,21},{6,22},{7,23},{8,24},{9,... | collective-permute-start | bytes 307208 | tf_op jit(solution)/shard_map/ppermute | solution.py:359
  73.7 3.7 %collective-permute-done.27.refs_0_ = bf16[16,3200]{1,0:T(8,128)(2,1)S(1)} collective-permute-done((bf16[16,3200]{1,0:T(8,128)(2,1)S(1)}, bf16[16,3200]{1,0:T(8,128)(2,1)S(1)}, u32[]{:S(2)}, u32[]{:S(2)}) %collective-permute-start.27) | collective-permute-done | bytes 102432 | tf_op jit(solution)/shard_map/ppermute | solution.py:359
  77.4 1.6 %collective-permute-done.28.refs_1_ = bf16[16,3200]{1,0:T(8,128)(2,1)S(1)} collective-permute-done((bf16[16,3200]{1,0:T(8,128)(2,1)S(1)}, bf16[16,3200]{1,0:T(8,128)(2,1)S(1)}, u32[]{:S(2)}, u32[]{:S(2)}) %collective-permute-start.28) | collective-permute-done | bytes 102432 | tf_op jit(solution)/shard_map/ppermute | solution.py:359
  79.1 1.7 %collective-permute-start.30 = (bf16[32,1536]{1,0:T(8,128)(2,1)S(1)}, bf16[32,1536]{1,0:T(8,128)(2,1)S(1)}, u32[]{:S(2)}, u32[]{:S(2)}) collective-permute-start(bf16[32,1536]{1,0:T(8,128)(2,1)S(1)} %shard_map.111.refs_0_), channel_id=1, source_target_pairs={{0,16},{1,17},{2,18},{3,19},{4,20},{5,21},{6,22},{7,23},{8,24},{9,... | collective-permute-start | bytes 294920 | tf_op jit(solution)/shard_map/ppermute | solution.py:359
  80.8 3.0 %collective-permute-done.30.refs_2_ = bf16[32,1536]{1,0:T(8,128)(2,1)S(1)} collective-permute-done((bf16[32,1536]{1,0:T(8,128)(2,1)S(1)}, bf16[32,1536]{1,0:T(8,128)(2,1)S(1)}, u32[]{:S(2)}, u32[]{:S(2)}) %collective-permute-start.30) | collective-permute-done | bytes 98336 | tf_op jit(solution)/shard_map/ppermute | solution.py:359
  83.8 1.3 %collective-permute-done.31.refs_3_ = bf16[32,1536]{1,0:T(8,128)(2,1)S(1)} collective-permute-done((bf16[32,1536]{1,0:T(8,128)(2,1)S(1)}, bf16[32,1536]{1,0:T(8,128)(2,1)S(1)}, u32[]{:S(2)}, u32[]{:S(2)}) %collective-permute-start.31) | collective-permute-done | bytes 98336 | tf_op jit(solution)/shard_map/ppermute | solution.py:359
  85.1 0.7 shard_map.112
  85.8 0.8 collective-permute-start.32
  86.6 2.9 %collective-permute-start.33 = (bf16[16,1024]{1,0:T(8,128)(2,1)S(1)}, bf16[16,1024]{1,0:T(8,128)(2,1)S(1)}, u32[]{:S(2)}, u32[]{:S(2)}) collective-permute-start(bf16[16,1024]{1,0:T(8,128)(2,1)S(1)} %get-tuple-element.94), channel_id=1, source_target_pairs={{0,5},{1,4},{2,7},{3,6},{4,1},{5,0},{6,3},{7,2},{8,13},{9,12},{10,... | collective-permute-start | bytes 98312 | tf_op jit(solution)/shard_map/ppermute | solution.py:359
  89.5 2.8 %collective-permute-start.34 = (bf16[16,1024]{1,0:T(8,128)(2,1)S(1)}, bf16[16,1024]{1,0:T(8,128)(2,1)S(1)}, u32[]{:S(2)}, u32[]{:S(2)}) collective-permute-start(bf16[16,1024]{1,0:T(8,128)(2,1)S(1)} %get-tuple-element.95), channel_id=1, source_target_pairs={{0,6},{1,7},{2,4},{3,5},{4,2},{5,3},{6,0},{7,1},{8,14},{9,15},{10,... | collective-permute-start | bytes 98312 | tf_op jit(solution)/shard_map/ppermute | solution.py:359
  92.4 1.1 %collective-permute-start.35 = (bf16[16,1024]{1,0:T(8,128)(2,1)S(1)}, bf16[16,1024]{1,0:T(8,128)(2,1)S(1)}, u32[]{:S(2)}, u32[]{:S(2)}) collective-permute-start(bf16[16,1024]{1,0:T(8,128)(2,1)S(1)} %get-tuple-element.96), channel_id=1, source_target_pairs={{0,7},{1,6},{2,5},{3,4},{4,3},{5,2},{6,1},{7,0},{8,15},{9,14},{10,... | collective-permute-start | bytes 98312 | tf_op jit(solution)/shard_map/ppermute | solution.py:359
  93.5 1.0 collective-permute-done.32.refs_0_
  95.1 1.6 %collective-permute-start.37 = (bf16[16,1024]{1,0:T(8,128)(2,1)S(1)}, bf16[16,1024]{1,0:T(8,128)(2,1)S(1)}, u32[]{:S(2)}, u32[]{:S(2)}) collective-permute-start(bf16[16,1024]{1,0:T(8,128)(2,1)S(1)} %get-tuple-element.98), channel_id=1, source_target_pairs={{0,2},{1,3},{2,0},{3,1},{4,6},{5,7},{6,4},{7,5},{8,10},{9,11},{10,... | collective-permute-start | bytes 98312 | tf_op jit(solution)/shard_map/ppermute | solution.py:359
  96.7 1.3 %collective-permute-start.38 = (bf16[16,1024]{1,0:T(8,128)(2,1)S(1)}, bf16[16,1024]{1,0:T(8,128)(2,1)S(1)}, u32[]{:S(2)}, u32[]{:S(2)}) collective-permute-start(bf16[16,1024]{1,0:T(8,128)(2,1)S(1)} %get-tuple-element.99), channel_id=1, source_target_pairs={{0,1},{1,0},{2,3},{3,2},{4,5},{5,4},{6,7},{7,6},{8,9},{9,8},{10,11... | collective-permute-start | bytes 98312 | tf_op jit(solution)/shard_map/ppermute | solution.py:359
  98.1 0.8 collective-permute-done.35.refs_3_
  99.3 1.3 %collective-permute-done.38.refs_6_ = bf16[16,1024]{1,0:T(8,128)(2,1)S(1)} collective-permute-done((bf16[16,1024]{1,0:T(8,128)(2,1)S(1)}, bf16[16,1024]{1,0:T(8,128)(2,1)S(1)}, u32[]{:S(2)}, u32[]{:S(2)}) %collective-permute-start.38) | collective-permute-done | bytes 32800 | tf_op jit(solution)/shard_map/ppermute | solution.py:359
  100.6 1.1 %shard_map.113 = bf16[256,1024]{1,0:T(8,128)(2,1)} custom-call(f32[256,1024]{1,0:T(8,128)S(1)} %shard_map.108.mixed, bf16[128,256]{1,0:T(8,128)(2,1)S(1)} %get-tuple-element.64.refs_6_.place_ref, f32[256,128]{1,0:T(8,128)S(1)} %get-tuple-element.80.gate_ref, bf16[16,1024]{1,0:T(8,128)(2,1)S(1)} %collective-permute-done.32.refs_0_, ...), custom_call_target="tpu_custom_call" | custom-call | bytes 2097152 | tf_op jit(solution)/shard_map/pallas_call | solution.py:512
  (63 shorter events, 6.9 us)
Async XLA Ops:
  0.0 29.5 %collective-permute-start.6 = (bf16[512,1024]{1,0:T(8,128)(2,1)}, bf16[512,1024]{1,0:T(8,128)(2,1)S(1)}, u32[]{:S(2)}, u32[]{:S(2)}) collective-permute-start(bf16[512,1024]{1,0:T(8,128)(2,1)} %refs_0_.1), channel_id=1, source_target_pairs={{0,1},{1,0},{2,3},{3,2},{4,5},{5,4},{6,7},{7,6},{8,9},{9,8},{10,11... | collective-permute-start | bytes 3145736 | tf_op jit(solution)/shard_map/ppermute | solution.py:359
  2.9 29.7 %collective-permute-start.7 = (bf16[512,1024]{1,0:T(8,128)(2,1)}, bf16[512,1024]{1,0:T(8,128)(2,1)S(1)}, u32[]{:S(2)}, u32[]{:S(2)}) collective-permute-start(bf16[512,1024]{1,0:T(8,128)(2,1)} %refs_0_.1), channel_id=1, source_target_pairs={{0,2},{1,3},{2,0},{3,1},{4,6},{5,7},{6,4},{7,5},{8,10},{9,11},{10,... | collective-permute-start | bytes 3145736 | tf_op jit(solution)/shard_map/ppermute | solution.py:359
  6.0 9.3 %collective-permute-start = (bf16[64,2048]{1,0:T(8,128)(2,1)S(1)}, bf16[64,2048]{1,0:T(8,128)(2,1)S(1)}, u32[]{:S(2)}, u32[]{:S(2)}) collective-permute-start(bf16[64,2048]{1,0:T(8,128)(2,1)S(1)} %get-tuple-element.53), channel_id=1, source_target_pairs={{0,16},{1,17},{2,18},{3,19},{4,20},{5,21},{6,22},{7,23},{8,24},{9,... | collective-permute-start | bytes 786440 | tf_op jit(solution)/shard_map/ppermute | solution.py:359
  7.6 10.6 %collective-permute-start.1 = (bf16[64,2048]{1,0:T(8,128)(2,1)S(1)}, bf16[64,2048]{1,0:T(8,128)(2,1)S(1)}, u32[]{:S(2)}, u32[]{:S(2)}) collective-permute-start(bf16[64,2048]{1,0:T(8,128)(2,1)S(1)} %get-tuple-element.54), channel_id=1, source_target_pairs={{0,24},{1,25},{2,26},{3,27},{4,28},{5,29},{6,30},{7,31},{8,16},{9,... | collective-permute-start | bytes 786440 | tf_op jit(solution)/shard_map/ppermute | solution.py:359
  7.6 10.6 %collective-permute-start.2 = (bf16[64,2048]{1,0:T(8,128)(2,1)S(1)}, bf16[64,2048]{1,0:T(8,128)(2,1)S(1)}, u32[]{:S(2)}, u32[]{:S(2)}) collective-permute-start(bf16[64,2048]{1,0:T(8,128)(2,1)S(1)} %get-tuple-element.55), channel_id=1, source_target_pairs={{0,8},{1,9},{2,10},{3,11},{4,12},{5,13},{6,14},{7,15},{8,0},{9,1},... | collective-permute-start | bytes 786440 | tf_op jit(solution)/shard_map/ppermute | solution.py:359
  20.5 15.4 %collective-permute-start.8 = (bf16[256,512]{1,0:T(8,128)(2,1)S(1)}, bf16[256,512]{1,0:T(8,128)(2,1)S(1)}, u32[]{:S(2)}, u32[]{:S(2)}) collective-permute-start(bf16[256,512]{1,0:T(8,128)(2,1)S(1)} %get-tuple-element.57), channel_id=1, source_target_pairs={{0,4},{1,5},{2,6},{3,7},{4,0},{5,1},{6,2},{7,3},{8,12},{9,13},{10,... | collective-permute-start | bytes 786440 | tf_op jit(solution)/shard_map/ppermute | solution.py:359
  25.5 1.2 %copy-start.1 = (bf16[512,1024]{1,0:T(8,128)(2,1)S(1)}, bf16[512,1024]{1,0:T(8,128)(2,1)}, u32[]{:S(2)}) copy-start(bf16[512,1024]{1,0:T(8,128)(2,1)} %refs_0_.1) | copy-start | bytes 3145732
  26.7 1.0 %copy-start.2 = (bf16[4,1,64,1024]{3,2,1,0:T(8,128)(2,1)S(1)}, bf16[4,1,64,1024]{3,2,1,0:T(8,128)(2,1)}, u32[]{:S(2)}) copy-start(bf16[4,1,64,1024]{3,2,1,0:T(8,128)(2,1)} %param.13) | copy-start | bytes 1572868
  27.7 0.7 copy-start.3
  28.5 0.7 copy-start.4
  29.5 16.5 %collective-permute-start.11 = (bf16[512,384]{1,0:T(8,128)(2,1)S(1)}, bf16[512,384]{1,0:T(8,128)(2,1)S(1)}, u32[]{:S(2)}, u32[]{:S(2)}) collective-permute-start(bf16[512,384]{1,0:T(8,128)(2,1)S(1)} %slice.6), channel_id=1, source_target_pairs={{0,2},{1,3},{2,0},{3,1},{4,6},{5,7},{6,4},{7,5},{8,10},{9,11},{10,... | collective-permute-start | bytes 1179656 | tf_op jit(solution)/shard_map/ppermute | solution.py:359
  32.7 17.1 %collective-permute-start.13 = (bf16[512,640]{1,0:T(8,128)(2,1)S(1)}, bf16[512,640]{1,0:T(8,128)(2,1)S(1)}, u32[]{:S(2)}, u32[]{:S(2)}) collective-permute-start(bf16[512,640]{1,0:T(8,128)(2,1)S(1)} %slice.7), channel_id=1, source_target_pairs={{0,1},{1,0},{2,3},{3,2},{4,5},{5,4},{6,7},{7,6},{8,9},{9,8},{10,11... | collective-permute-start | bytes 1966088 | tf_op jit(solution)/shard_map/ppermute | solution.py:359
  33.1 9.5 %collective-permute-start.4 = (bf16[256,512]{1,0:T(8,128)(2,1)S(1)}, bf16[256,512]{1,0:T(8,128)(2,1)S(1)}, u32[]{:S(2)}, u32[]{:S(2)}) collective-permute-start(bf16[256,512]{1,0:T(8,128)(2,1)S(1)} %shard_map.102.refs_1_), channel_id=1, source_target_pairs={{0,16},{1,17},{2,18},{3,19},{4,20},{5,21},{6,22},{7,23},{8,24},{9,... | collective-permute-start | bytes 786440 | tf_op jit(solution)/shard_map/ppermute | solution.py:359
  35.9 10.1 %collective-permute-start.10 = (bf16[256,512]{1,0:T(8,128)(2,1)S(1)}, bf16[256,512]{1,0:T(8,128)(2,1)S(1)}, u32[]{:S(2)}, u32[]{:S(2)}) collective-permute-start(bf16[256,512]{1,0:T(8,128)(2,1)S(1)} %collective-permute-done.8.refs_0_), channel_id=1, source_target_pairs={{0,16},{1,17},{2,18},{3,19},{4,20},{5,21},{6,22},{7,23},{8,24},{9,... | collective-permute-start | bytes 786440 | tf_op jit(solution)/shard_map/ppermute | solution.py:359
  35.9 10.6 %collective-permute-start.14 = (s32[4,8,64]{2,1,0:T(8,128)S(1)}, s32[4,8,64]{2,1,0:T(8,128)S(1)}, u32[]{:S(2)}, u32[]{:S(2)}) collective-permute-start(s32[4,8,64]{2,1,0:T(8,128)S(1)} %bitcast.23), channel_id=1, source_target_pairs={{0,4},{1,5},{2,6},{3,7},{4,0},{5,1},{6,2},{7,3},{8,12},{9,13},{10,... | collective-permute-start | bytes 24584 | tf_op jit(solution)/shard_map/ppermute | solution.py:359
  42.7 4.2 %collective-permute-start.3 = (bf16[256,512]{1,0:T(8,128)(2,1)S(1)}, bf16[256,512]{1,0:T(8,128)(2,1)S(1)}, u32[]{:S(2)}, u32[]{:S(2)}) collective-permute-start(bf16[256,512]{1,0:T(8,128)(2,1)S(1)} %shard_map.102.refs_1_), channel_id=1, source_target_pairs={{0,8},{1,9},{2,10},{3,11},{4,12},{5,13},{6,14},{7,15},{8,0},{9,1},... | collective-permute-start | bytes 786440 | tf_op jit(solution)/shard_map/ppermute | solution.py:359
  46.0 1.5 %collective-permute-start.5 = (bf16[256,512]{1,0:T(8,128)(2,1)S(1)}, bf16[256,512]{1,0:T(8,128)(2,1)S(1)}, u32[]{:S(2)}, u32[]{:S(2)}) collective-permute-start(bf16[256,512]{1,0:T(8,128)(2,1)S(1)} %collective-permute-done.4.refs_3_), channel_id=1, source_target_pairs={{0,8},{1,9},{2,10},{3,11},{4,12},{5,13},{6,14},{7,15},{8,0},{9,1},... | collective-permute-start | bytes 786440 | tf_op jit(solution)/shard_map/ppermute | solution.py:359
  46.0 2.6 %collective-permute-start.9 = (bf16[256,512]{1,0:T(8,128)(2,1)S(1)}, bf16[256,512]{1,0:T(8,128)(2,1)S(1)}, u32[]{:S(2)}, u32[]{:S(2)}) collective-permute-start(bf16[256,512]{1,0:T(8,128)(2,1)S(1)} %collective-permute-done.8.refs_0_), channel_id=1, source_target_pairs={{0,8},{1,9},{2,10},{3,11},{4,12},{5,13},{6,14},{7,15},{8,0},{9,1},... | collective-permute-start | bytes 786440 | tf_op jit(solution)/shard_map/ppermute | solution.py:359
  46.5 2.1 %collective-permute-start.12 = (bf16[256,512]{1,0:T(8,128)(2,1)S(1)}, bf16[256,512]{1,0:T(8,128)(2,1)S(1)}, u32[]{:S(2)}, u32[]{:S(2)}) collective-permute-start(bf16[256,512]{1,0:T(8,128)(2,1)S(1)} %collective-permute-done.10.refs_2_), channel_id=1, source_target_pairs={{0,8},{1,9},{2,10},{3,11},{4,12},{5,13},{6,14},{7,15},{8,0},{9,1},... | collective-permute-start | bytes 786440 | tf_op jit(solution)/shard_map/ppermute | solution.py:359
  47.6 20.6 %slice-start = ((s8[6291456]{0:T(1024)(128)(4,1)}), s8[4194304]{0:T(1024)(128)(4,1)S(1)}, s32[]{:S(2)}) async-start(s8[6291456]{0:T(1024)(128)(4,1)} %bitcast.16), calls=%async_computation | async-start | bytes 8388608
  47.6 20.6 %copy-start.5 = (f32[1024]{0:T(1024)S(1)}, f32[1024]{0:T(1024)}, u32[]{:S(2)}) copy-start(f32[1024]{0:T(1024)} %param.15) | copy-start | bytes 12292
  48.6 19.6 %slice-start.1 = ((s8[6291456]{0:T(1024)(128)(4,1)}), s8[2097152]{0:T(1024)(128)(4,1)S(1)}, s32[]{:S(2)}) async-start(s8[6291456]{0:T(1024)(128)(4,1)} %bitcast.16), calls=%async_computation.1 | async-start | bytes 4194304
  49.8 35.4 %copy-start = (bf16[1,1536,1024]{2,1,0:T(8,128)(2,1)S(1)}, bf16[1,1536,1024]{2,1,0:T(8,128)(2,1)}, u32[]{:S(2)}) copy-start(bf16[1,1536,1024]{2,1,0:T(8,128)(2,1)} %param.19) | copy-start | bytes 9437188
  51.3 7.7 %collective-permute-start.15 = (bf16[32,1024]{1,0:T(8,128)(2,1)S(1)}, bf16[32,1024]{1,0:T(8,128)(2,1)S(1)}, u32[]{:S(2)}, u32[]{:S(2)}) collective-permute-start(bf16[32,1024]{1,0:T(8,128)(2,1)S(1)} %get-tuple-element.75), channel_id=1, source_target_pairs={{0,4},{1,5},{2,6},{3,7},{4,0},{5,1},{6,2},{7,3},{8,12},{9,13},{10,... | collective-permute-start | bytes 196616 | tf_op jit(solution)/shard_map/ppermute | solution.py:359
  52.0 11.9 %collective-permute-start.16 = (bf16[32,1024]{1,0:T(8,128)(2,1)S(1)}, bf16[32,1024]{1,0:T(8,128)(2,1)S(1)}, u32[]{:S(2)}, u32[]{:S(2)}) collective-permute-start(bf16[32,1024]{1,0:T(8,128)(2,1)S(1)} %get-tuple-element.76), channel_id=1, source_target_pairs={{0,5},{1,4},{2,7},{3,6},{4,1},{5,0},{6,3},{7,2},{8,13},{9,12},{10,... | collective-permute-start | bytes 196616 | tf_op jit(solution)/shard_map/ppermute | solution.py:359
  55.2 8.7 %collective-permute-start.17 = (bf16[32,1024]{1,0:T(8,128)(2,1)S(1)}, bf16[32,1024]{1,0:T(8,128)(2,1)S(1)}, u32[]{:S(2)}, u32[]{:S(2)}) collective-permute-start(bf16[32,1024]{1,0:T(8,128)(2,1)S(1)} %get-tuple-element.77), channel_id=1, source_target_pairs={{0,6},{1,7},{2,4},{3,5},{4,2},{5,3},{6,0},{7,1},{8,14},{9,15},{10,... | collective-permute-start | bytes 196616 | tf_op jit(solution)/shard_map/ppermute | solution.py:359
  58.0 7.1 %collective-permute-start.18 = (bf16[32,1024]{1,0:T(8,128)(2,1)S(1)}, bf16[32,1024]{1,0:T(8,128)(2,1)S(1)}, u32[]{:S(2)}, u32[]{:S(2)}) collective-permute-start(bf16[32,1024]{1,0:T(8,128)(2,1)S(1)} %get-tuple-element.78), channel_id=1, source_target_pairs={{0,7},{1,6},{2,5},{3,4},{4,3},{5,2},{6,1},{7,0},{8,15},{9,14},{10,... | collective-permute-start | bytes 196616 | tf_op jit(solution)/shard_map/ppermute | solution.py:359
  59.0 9.0 %collective-permute-start.20 = (bf16[32,1024]{1,0:T(8,128)(2,1)S(1)}, bf16[32,1024]{1,0:T(8,128)(2,1)S(1)}, u32[]{:S(2)}, u32[]{:S(2)}) collective-permute-start(bf16[32,1024]{1,0:T(8,128)(2,1)S(1)} %get-tuple-element.81), channel_id=1, source_target_pairs={{0,3},{1,2},{2,1},{3,0},{4,7},{5,6},{6,5},{7,4},{8,11},{9,10},{10,... | collective-permute-start | bytes 196616 | tf_op jit(solution)/shard_map/ppermute | solution.py:359
  59.0 9.0 %collective-permute-start.21 = (bf16[32,1024]{1,0:T(8,128)(2,1)S(1)}, bf16[32,1024]{1,0:T(8,128)(2,1)S(1)}, u32[]{:S(2)}, u32[]{:S(2)}) collective-permute-start(bf16[32,1024]{1,0:T(8,128)(2,1)S(1)} %get-tuple-element.82), channel_id=1, source_target_pairs={{0,2},{1,3},{2,0},{3,1},{4,6},{5,7},{6,4},{7,5},{8,10},{9,11},{10,... | collective-permute-start | bytes 196616 | tf_op jit(solution)/shard_map/ppermute | solution.py:359
  63.9 4.3 %collective-permute-start.22 = (bf16[32,1024]{1,0:T(8,128)(2,1)S(1)}, bf16[32,1024]{1,0:T(8,128)(2,1)S(1)}, u32[]{:S(2)}, u32[]{:S(2)}) collective-permute-start(bf16[32,1024]{1,0:T(8,128)(2,1)S(1)} %get-tuple-element.83), channel_id=1, source_target_pairs={{0,1},{1,0},{2,3},{3,2},{4,5},{5,4},{6,7},{7,6},{8,9},{9,8},{10,11... | collective-permute-start | bytes 196616 | tf_op jit(solution)/shard_map/ppermute | solution.py:359
  65.1 31.6 %collective-permute-start.19 = (bf16[256,1024]{1,0:T(8,128)(2,1)S(1)}, bf16[256,1024]{1,0:T(8,128)(2,1)S(1)}, u32[]{:S(2)}, u32[]{:S(2)}) collective-permute-start(bf16[256,1024]{1,0:T(8,128)(2,1)S(1)} %get-tuple-element.79), channel_id=1, source_target_pairs={{0,4},{1,5},{2,6},{3,7},{4,0},{5,1},{6,2},{7,3},{8,12},{9,13},{10,... | collective-permute-start | bytes 1572872 | tf_op jit(solution)/shard_map/ppermute | solution.py:359
  69.5 1.3 %collective-permute-start.23 = (bf16[16,3200]{1,0:T(8,128)(2,1)S(1)}, bf16[16,3200]{1,0:T(8,128)(2,1)S(1)}, u32[]{:S(2)}, u32[]{:S(2)}) collective-permute-start(bf16[16,3200]{1,0:T(8,128)(2,1)S(1)} %get-tuple-element.86), channel_id=1, source_target_pairs={{0,8},{1,9},{2,10},{3,11},{4,12},{5,13},{6,14},{7,15},{8,0},{9,1},... | collective-permute-start | bytes 307208 | tf_op jit(solution)/shard_map/ppermute | solution.py:359
  69.5 1.4 %collective-permute-start.24 = (bf16[16,3200]{1,0:T(8,128)(2,1)S(1)}, bf16[16,3200]{1,0:T(8,128)(2,1)S(1)}, u32[]{:S(2)}, u32[]{:S(2)}) collective-permute-start(bf16[16,3200]{1,0:T(8,128)(2,1)S(1)} %get-tuple-element.87), channel_id=1, source_target_pairs={{0,8},{1,9},{2,10},{3,11},{4,12},{5,13},{6,14},{7,15},{8,0},{9,1},... | collective-permute-start | bytes 307208 | tf_op jit(solution)/shard_map/ppermute | solution.py:359
  70.0 1.3 %collective-permute-start.25 = (bf16[16,3200]{1,0:T(8,128)(2,1)S(1)}, bf16[16,3200]{1,0:T(8,128)(2,1)S(1)}, u32[]{:S(2)}, u32[]{:S(2)}) collective-permute-start(bf16[16,3200]{1,0:T(8,128)(2,1)S(1)} %get-tuple-element.88), channel_id=1, source_target_pairs={{0,8},{1,9},{2,10},{3,11},{4,12},{5,13},{6,14},{7,15},{8,0},{9,1},... | collective-permute-start | bytes 307208 | tf_op jit(solution)/shard_map/ppermute | solution.py:359
  70.1 1.4 %collective-permute-start.26 = (bf16[16,3200]{1,0:T(8,128)(2,1)S(1)}, bf16[16,3200]{1,0:T(8,128)(2,1)S(1)}, u32[]{:S(2)}, u32[]{:S(2)}) collective-permute-start(bf16[16,3200]{1,0:T(8,128)(2,1)S(1)} %get-tuple-element.89), channel_id=1, source_target_pairs={{0,8},{1,9},{2,10},{3,11},{4,12},{5,13},{6,14},{7,15},{8,0},{9,1},... | collective-permute-start | bytes 307208 | tf_op jit(solution)/shard_map/ppermute | solution.py:359
  71.6 5.8 %collective-permute-start.27 = (bf16[16,3200]{1,0:T(8,128)(2,1)S(1)}, bf16[16,3200]{1,0:T(8,128)(2,1)S(1)}, u32[]{:S(2)}, u32[]{:S(2)}) collective-permute-start(bf16[16,3200]{1,0:T(8,128)(2,1)S(1)} %get-tuple-element.91), channel_id=1, source_target_pairs={{0,16},{1,17},{2,18},{3,19},{4,20},{5,21},{6,22},{7,23},{8,24},{9,... | collective-permute-start | bytes 307208 | tf_op jit(solution)/shard_map/ppermute | solution.py:359
  73.3 5.7 %collective-permute-start.28 = (bf16[16,3200]{1,0:T(8,128)(2,1)S(1)}, bf16[16,3200]{1,0:T(8,128)(2,1)S(1)}, u32[]{:S(2)}, u32[]{:S(2)}) collective-permute-start(bf16[16,3200]{1,0:T(8,128)(2,1)S(1)} %get-tuple-element.92), channel_id=1, source_target_pairs={{0,16},{1,17},{2,18},{3,19},{4,20},{5,21},{6,22},{7,23},{8,24},{9,... | collective-permute-start | bytes 307208 | tf_op jit(solution)/shard_map/ppermute | solution.py:359
  79.1 4.7 %collective-permute-start.30 = (bf16[32,1536]{1,0:T(8,128)(2,1)S(1)}, bf16[32,1536]{1,0:T(8,128)(2,1)S(1)}, u32[]{:S(2)}, u32[]{:S(2)}) collective-permute-start(bf16[32,1536]{1,0:T(8,128)(2,1)S(1)} %shard_map.111.refs_0_), channel_id=1, source_target_pairs={{0,16},{1,17},{2,18},{3,19},{4,20},{5,21},{6,22},{7,23},{8,24},{9,... | collective-permute-start | bytes 294920 | tf_op jit(solution)/shard_map/ppermute | solution.py:359
  80.8 3.0 %collective-permute-start.29 = (bf16[32,1536]{1,0:T(8,128)(2,1)S(1)}, bf16[32,1536]{1,0:T(8,128)(2,1)S(1)}, u32[]{:S(2)}, u32[]{:S(2)}) collective-permute-start(bf16[32,1536]{1,0:T(8,128)(2,1)S(1)} %shard_map.111.refs_0_), channel_id=1, source_target_pairs={{0,8},{1,9},{2,10},{3,11},{4,12},{5,13},{6,14},{7,15},{8,0},{9,1},... | collective-permute-start | bytes 294920 | tf_op jit(solution)/shard_map/ppermute | solution.py:359
  83.8 1.3 %collective-permute-start.31 = (bf16[32,1536]{1,0:T(8,128)(2,1)S(1)}, bf16[32,1536]{1,0:T(8,128)(2,1)S(1)}, u32[]{:S(2)}, u32[]{:S(2)}) collective-permute-start(bf16[32,1536]{1,0:T(8,128)(2,1)S(1)} %collective-permute-done.30.refs_2_), channel_id=1, source_target_pairs={{0,8},{1,9},{2,10},{3,11},{4,12},{5,13},{6,14},{7,15},{8,0},{9,1},... | collective-permute-start | bytes 294920 | tf_op jit(solution)/shard_map/ppermute | solution.py:359
  85.8 8.7 %collective-permute-start.32 = (bf16[16,1024]{1,0:T(8,128)(2,1)S(1)}, bf16[16,1024]{1,0:T(8,128)(2,1)S(1)}, u32[]{:S(2)}, u32[]{:S(2)}) collective-permute-start(bf16[16,1024]{1,0:T(8,128)(2,1)S(1)} %get-tuple-element.93), channel_id=1, source_target_pairs={{0,4},{1,5},{2,6},{3,7},{4,0},{5,1},{6,2},{7,3},{8,12},{9,13},{10,... | collective-permute-start | bytes 98312 | tf_op jit(solution)/shard_map/ppermute | solution.py:359
  86.6 8.5 %collective-permute-start.33 = (bf16[16,1024]{1,0:T(8,128)(2,1)S(1)}, bf16[16,1024]{1,0:T(8,128)(2,1)S(1)}, u32[]{:S(2)}, u32[]{:S(2)}) collective-permute-start(bf16[16,1024]{1,0:T(8,128)(2,1)S(1)} %get-tuple-element.94), channel_id=1, source_target_pairs={{0,5},{1,4},{2,7},{3,6},{4,1},{5,0},{6,3},{7,2},{8,13},{9,12},{10,... | collective-permute-start | bytes 98312 | tf_op jit(solution)/shard_map/ppermute | solution.py:359
  89.5 8.6 %collective-permute-start.34 = (bf16[16,1024]{1,0:T(8,128)(2,1)S(1)}, bf16[16,1024]{1,0:T(8,128)(2,1)S(1)}, u32[]{:S(2)}, u32[]{:S(2)}) collective-permute-start(bf16[16,1024]{1,0:T(8,128)(2,1)S(1)} %get-tuple-element.95), channel_id=1, source_target_pairs={{0,6},{1,7},{2,4},{3,5},{4,2},{5,3},{6,0},{7,1},{8,14},{9,15},{10,... | collective-permute-start | bytes 98312 | tf_op jit(solution)/shard_map/ppermute | solution.py:359
  92.4 6.6 %collective-permute-start.35 = (bf16[16,1024]{1,0:T(8,128)(2,1)S(1)}, bf16[16,1024]{1,0:T(8,128)(2,1)S(1)}, u32[]{:S(2)}, u32[]{:S(2)}) collective-permute-start(bf16[16,1024]{1,0:T(8,128)(2,1)S(1)} %get-tuple-element.96), channel_id=1, source_target_pairs={{0,7},{1,6},{2,5},{3,4},{4,3},{5,2},{6,1},{7,0},{8,15},{9,14},{10,... | collective-permute-start | bytes 98312 | tf_op jit(solution)/shard_map/ppermute | solution.py:359
  94.5 4.8 %collective-permute-start.36 = (bf16[16,1024]{1,0:T(8,128)(2,1)S(1)}, bf16[16,1024]{1,0:T(8,128)(2,1)S(1)}, u32[]{:S(2)}, u32[]{:S(2)}) collective-permute-start(bf16[16,1024]{1,0:T(8,128)(2,1)S(1)} %get-tuple-element.97), channel_id=1, source_target_pairs={{0,3},{1,2},{2,1},{3,0},{4,7},{5,6},{6,5},{7,4},{8,11},{9,10},{10,... | collective-permute-start | bytes 98312 | tf_op jit(solution)/shard_map/ppermute | solution.py:359
  95.1 4.2 %collective-permute-start.37 = (bf16[16,1024]{1,0:T(8,128)(2,1)S(1)}, bf16[16,1024]{1,0:T(8,128)(2,1)S(1)}, u32[]{:S(2)}, u32[]{:S(2)}) collective-permute-start(bf16[16,1024]{1,0:T(8,128)(2,1)S(1)} %get-tuple-element.98), channel_id=1, source_target_pairs={{0,2},{1,3},{2,0},{3,1},{4,6},{5,7},{6,4},{7,5},{8,10},{9,11},{10,... | collective-permute-start | bytes 98312 | tf_op jit(solution)/shard_map/ppermute | solution.py:359
  96.7 3.9 %collective-permute-start.38 = (bf16[16,1024]{1,0:T(8,128)(2,1)S(1)}, bf16[16,1024]{1,0:T(8,128)(2,1)S(1)}, u32[]{:S(2)}, u32[]{:S(2)}) collective-permute-start(bf16[16,1024]{1,0:T(8,128)(2,1)S(1)} %get-tuple-element.99), channel_id=1, source_target_pairs={{0,1},{1,0},{2,3},{3,2},{4,5},{5,4},{6,7},{7,6},{8,9},{9,8},{10,11... | collective-permute-start | bytes 98312 | tf_op jit(solution)/shard_map/ppermute | solution.py:359

commit v20 on v19

--- a/solution.py
+++ b/solution.py
@@ -406,7 +406,7 @@
         scratch=[pltpu.VMEM((8, rows), jnp.int32), pltpu.VMEM((128, rows), F32)],
         cost=(0, 2**14),
         limit=16,
-    )(after(own_routes, mine), tokens_last(gates), out_weight, res)
+    )(after(own_routes, other), tokens_last(gates), out_weight, res)
     other_place = call(
         functools.partial(place_tokens, E, cap, 1),
         sds((slots, rows), BF16),
@@ -443,7 +443,7 @@
     near = after(shards[1], place)[:, cut:]
     for d in range(2, C, 2):
         shards[d + 1] = (
-            permute(after(shards[d], place)[:, :cut], exp=1),
+            permute(after(shards[d], place, mine)[:, :cut], exp=1),
             permute(near, exp=spread(d)),
         )
     acc, last = project(mine_all, res)

time: 102 us -> 102 us (level)
  starting transfers between devices: 45.7 us -> 42.5 us
  waiting for transfers between devices: 38.4 us -> 41.4 us
    ppermute x39, starting transfers between devices: 45.7 us -> 42.5 us  [permute(): return lax.ppermute(x, ('ctx', 'exp'), pairs)]
    ppermute x39, waiting for transfers between devices: 38.4 us -> 41.4 us  [permute(): return lax.ppermute(x, ('ctx', 'exp'), pairs)]
  transfers between devices with their start and end apart: 39 -> 39, of which waited for: 22 -> 21; matrix products, arithmetic and copies ran while one was open for 0% -> 0% of each run, Pallas kernels for 11% -> 11%
where the time goes in v20:
time: 102 us
  starting transfers between devices  42.5 us (42%)
  waiting for transfers between devices  41.4 us (41%)
  Pallas kernels  13.6 us (13%)
  local copies, waits for them, and re-layouts  3.83 us (4%)
    ppermute x39, starting transfers between devices, permute(): return lax.ppermute(x, ('ctx', 'exp'), pairs)  42.5 us
    ppermute x39, waiting for transfers between devices, permute(): return lax.ppermute(x, ('ctx', 'exp'), pairs)  41.4 us
    pallas_call x2, Pallas kernels, attend(): call(functools.partial(attend_kernel, C, t), [sds((rows, qw), BF16)] + [s...  4.63 us
    unnamed x16, local copies, waits for them, and re-layouts  3.72 us
    pallas_call x2, Pallas kernels, project(): call(functools.partial(project_kernel, C, bool(extra)), [sds((rows, width...  2.13 us
  transfers between devices with their start and end apart: 39, of which 21 were waited for; matrix products, arithmetic and copies ran while one was open for 0% of the time, Pallas kernels for 11%

profile of v20, /device:TPU:0, one launch (start us, length us, event | category | flops | bytes accessed | tf_op | source)
XLA Modules:
  0.0 101.6 jit_solution(7089566166505193593)
XLA Ops:
  0.0 2.9 %collective-permute-start.6 = (bf16[512,1024]{1,0:T(8,128)(2,1)}, bf16[512,1024]{1,0:T(8,128)(2,1)S(1)}, u32[]{:S(2)}, u32[]{:S(2)}) collective-permute-start(bf16[512,1024]{1,0:T(8,128)(2,1)} %refs_0_.1), channel_id=1, source_target_pairs={{0,1},{1,0},{2,3},{3,2},{4,5},{5,4},{6,7},{7,6},{8,9},{9,8},{10,11... | collective-permute-start | bytes 3145736 | tf_op jit(solution)/shard_map/ppermute | solution.py:359
  2.9 1.6 %collective-permute-start.7 = (bf16[512,1024]{1,0:T(8,128)(2,1)}, bf16[512,1024]{1,0:T(8,128)(2,1)S(1)}, u32[]{:S(2)}, u32[]{:S(2)}) collective-permute-start(bf16[512,1024]{1,0:T(8,128)(2,1)} %refs_0_.1), channel_id=1, source_target_pairs={{0,2},{1,3},{2,0},{3,1},{4,6},{5,7},{6,4},{7,5},{8,10},{9,11},{10,... | collective-permute-start | bytes 3145736 | tf_op jit(solution)/shard_map/ppermute | solution.py:359
  4.5 1.4 %shard_map.100 = (bf16[64,2048]{1,0:T(8,128)(2,1)S(1)}, bf16[64,2048]{1,0:T(8,128)(2,1)S(1)}, bf16[64,2048]{1,0:T(8,128)(2,1)S(1)}, bf16[64,2048]{1,0:T(8,128)(2,1)S(1)}) custom-call(bf16[64,4096]{1,0:T(8,128)(2,1)} %bitcast.25, bf16[64,512]{1,0:T(8,128)(2,1)} %bitcast.26, bf16[64,512]{1,0:T(8,128)(2,1)} %bitcast.27), custom_call_target="tpu_custom_call" | custom-call | bytes 1048576 | tf_op jit(solution)/shard_map/pallas_call | solution.py:365
  6.0 1.6 %collective-permute-start = (bf16[64,2048]{1,0:T(8,128)(2,1)S(1)}, bf16[64,2048]{1,0:T(8,128)(2,1)S(1)}, u32[]{:S(2)}, u32[]{:S(2)}) collective-permute-start(bf16[64,2048]{1,0:T(8,128)(2,1)S(1)} %get-tuple-element.53), channel_id=1, source_target_pairs={{0,16},{1,17},{2,18},{3,19},{4,20},{5,21},{6,22},{7,23},{8,24},{9,... | collective-permute-start | bytes 786440 | tf_op jit(solution)/shard_map/ppermute | solution.py:359
  7.6 0.6 collective-permute-start.2
  8.2 7.1 %collective-permute-done.refs_0_ = bf16[64,2048]{1,0:T(8,128)(2,1)S(1)} collective-permute-done((bf16[64,2048]{1,0:T(8,128)(2,1)S(1)}, bf16[64,2048]{1,0:T(8,128)(2,1)S(1)}, u32[]{:S(2)}, u32[]{:S(2)}) %collective-permute-start) | collective-permute-done | bytes 262176 | tf_op jit(solution)/shard_map/ppermute | solution.py:359
  15.3 2.9 %collective-permute-done.1.refs_1_ = bf16[64,2048]{1,0:T(8,128)(2,1)S(1)} collective-permute-done((bf16[64,2048]{1,0:T(8,128)(2,1)S(1)}, bf16[64,2048]{1,0:T(8,128)(2,1)S(1)}, u32[]{:S(2)}, u32[]{:S(2)}) %collective-permute-start.1) | collective-permute-done | bytes 262176 | tf_op jit(solution)/shard_map/ppermute | solution.py:359
  18.2 2.3 %shard_map.101 = (bf16[256,512]{1,0:T(8,128)(2,1)S(1)}, bf16[64,2048]{1,0:T(8,128)(2,1)S(1)}) custom-call(bf16[64,2048]{1,0:T(8,128)(2,1)S(1)} %collective-permute-done.refs_0_, bf16[64,2048]{1,0:T(8,128)(2,1)S(1)} %collective-permute-done.1.refs_1_, bf16[64,2048]{1,0:T(8,128)(2,1)S(1)} %collective-permute-done.2.refs_2_, ...), custom_call_target="tpu_custom_call" | custom-call | bytes 16384 | tf_op jit(solution)/shard_map/pallas_call | solution.py:386
  20.5 2.7 %collective-permute-start.8 = (bf16[256,512]{1,0:T(8,128)(2,1)S(1)}, bf16[256,512]{1,0:T(8,128)(2,1)S(1)}, u32[]{:S(2)}, u32[]{:S(2)}) collective-permute-start(bf16[256,512]{1,0:T(8,128)(2,1)S(1)} %get-tuple-element.57), channel_id=1, source_target_pairs={{0,4},{1,5},{2,6},{3,7},{4,0},{5,1},{6,2},{7,3},{8,12},{9,13},{10,... | collective-permute-start | bytes 786440 | tf_op jit(solution)/shard_map/ppermute | solution.py:359
  23.2 1.2 %copy-done.1 = bf16[512,1024]{1,0:T(8,128)(2,1)S(1)} copy-done((bf16[512,1024]{1,0:T(8,128)(2,1)S(1)}, bf16[512,1024]{1,0:T(8,128)(2,1)}, u32[]{:S(2)}) %copy-start.1) | copy-done | bytes 1048600
  24.4 1.0 %copy-done.2 = bf16[4,1,64,1024]{3,2,1,0:T(8,128)(2,1)S(1)} copy-done((bf16[4,1,64,1024]{3,2,1,0:T(8,128)(2,1)S(1)}, bf16[4,1,64,1024]{3,2,1,0:T(8,128)(2,1)}, u32[]{:S(2)}) %copy-start.2) | copy-done | bytes 524312
  25.4 0.7 copy-done.3
  26.1 0.7 copy-done.4
  27.2 1.0 %collective-permute-start.11 = (bf16[512,384]{1,0:T(8,128)(2,1)S(1)}, bf16[512,384]{1,0:T(8,128)(2,1)S(1)}, u32[]{:S(2)}, u32[]{:S(2)}) collective-permute-start(bf16[512,384]{1,0:T(8,128)(2,1)S(1)} %slice.6), channel_id=1, source_target_pairs={{0,2},{1,3},{2,0},{3,1},{4,6},{5,7},{6,4},{7,5},{8,10},{9,11},{10,... | collective-permute-start | bytes 1179656 | tf_op jit(solution)/shard_map/ppermute | solution.py:359
  28.2 2.3 %shard_map.103.refs_1_ = bf16[256,512]{1,0:T(8,128)(2,1)S(1)} custom-call(bf16[64,2048]{1,0:T(8,128)(2,1)S(1)} %collective-permute-done.refs_0_, bf16[64,2048]{1,0:T(8,128)(2,1)S(1)} %collective-permute-done.1.refs_1_, bf16[64,2048]{1,0:T(8,128)(2,1)S(1)} %collective-permute-done.2.refs_2_, bf16[64,2048]{1,0:T(8,128)(2,1)S(1)} %get-tuple-element.61.refs_3_), custom_call_target="tpu_custom_call" | custom-call | bytes 16384 | tf_op jit(solution)/shard_map/pallas_call | solution.py:386
  30.6 3.5 %collective-permute-done.7.refs_7_.refs_6_ = bf16[512,1024]{1,0:T(8,128)(2,1)S(1)} collective-permute-done((bf16[512,1024]{1,0:T(8,128)(2,1)}, bf16[512,1024]{1,0:T(8,128)(2,1)S(1)}, u32[]{:S(2)}, u32[]{:S(2)}) %collective-permute-start.7) | collective-permute-done | bytes 1048608 | tf_op jit(solution)/shard_map/ppermute | solution.py:359
  34.3 2.8 %collective-permute-start.4 = (bf16[256,512]{1,0:T(8,128)(2,1)S(1)}, bf16[256,512]{1,0:T(8,128)(2,1)S(1)}, u32[]{:S(2)}, u32[]{:S(2)}) collective-permute-start(bf16[256,512]{1,0:T(8,128)(2,1)S(1)} %shard_map.103.refs_1_), channel_id=1, source_target_pairs={{0,16},{1,17},{2,18},{3,19},{4,20},{5,21},{6,22},{7,23},{8,24},{9,... | collective-permute-start | bytes 786440 | tf_op jit(solution)/shard_map/ppermute | solution.py:359
  37.1 1.8 %collective-permute-start.14 = (s32[4,8,64]{2,1,0:T(8,128)S(1)}, s32[4,8,64]{2,1,0:T(8,128)S(1)}, u32[]{:S(2)}, u32[]{:S(2)}) collective-permute-start(s32[4,8,64]{2,1,0:T(8,128)S(1)} %bitcast.23), channel_id=1, source_target_pairs={{0,4},{1,5},{2,6},{3,7},{4,0},{5,1},{6,2},{7,3},{8,12},{9,13},{10,... | collective-permute-start | bytes 24584 | tf_op jit(solution)/shard_map/ppermute | solution.py:359
  38.9 4.9 %collective-permute-done.4.refs_3_ = bf16[256,512]{1,0:T(8,128)(2,1)S(1)} collective-permute-done((bf16[256,512]{1,0:T(8,128)(2,1)S(1)}, bf16[256,512]{1,0:T(8,128)(2,1)S(1)}, u32[]{:S(2)}, u32[]{:S(2)}) %collective-permute-start.4) | collective-permute-done | bytes 262176 | tf_op jit(solution)/shard_map/ppermute | solution.py:359
  43.8 2.8 %collective-permute-done.10.refs_2_ = bf16[256,512]{1,0:T(8,128)(2,1)S(1)} collective-permute-done((bf16[256,512]{1,0:T(8,128)(2,1)S(1)}, bf16[256,512]{1,0:T(8,128)(2,1)S(1)}, u32[]{:S(2)}, u32[]{:S(2)}) %collective-permute-start.10) | collective-permute-done | bytes 262176 | tf_op jit(solution)/shard_map/ppermute | solution.py:359
  47.5 0.7 collective-permute-done.5.refs_4_
  48.2 1.1 %shard_map.104 = (f32[256,1024]{1,0:T(8,128)S(1)}, bf16[256,512]{1,0:T(8,128)(2,1)S(1)}) custom-call(bf16[256,1024]{1,0:T(8,128)(2,1)S(1)} %get-tuple-element.59.refs_0_, bf16[256,512]{1,0:T(8,128)(2,1)S(1)} %shard_map.103.refs_1_, bf16[256,512]{1,0:T(8,128)(2,1)S(1)} %collective-permute-done.3.refs_2_, bf16[256,512]{1,0:T(8,128)(2,1)S(1)} %collective-permute-done.4.refs_3_, ...), custom_call_target="tpu_custom_call" | custom-call | bytes 16384 | tf_op jit(solution)/shard_map/pallas_call | solution.py:431
  49.3 1.1 %shard_map.105 = (f32[256,1024]{1,0:T(8,128)S(1)}, bf16[256,512]{1,0:T(8,128)(2,1)S(1)}) custom-call(bf16[256,512]{1,0:T(8,128)(2,1)S(1)} %collective-permute-done.8.refs_0_, bf16[256,512]{1,0:T(8,128)(2,1)S(1)} %collective-permute-done.9.refs_1_, bf16[256,512]{1,0:T(8,128)(2,1)S(1)} %collective-permute-done.10.refs_2_, ...), custom_call_target="tpu_custom_call" | custom-call | bytes 16384 | tf_op jit(solution)/shard_map/pallas_call | solution.py:431
  50.4 1.5 %shard_map.107 = (f32[256,1024]{1,0:T(8,128)S(1)}, bf16[256,1024]{1,0:T(8,128)(2,1)S(1)}, bf16[32,1024]{1,0:T(8,128)(2,1)S(1)}, bf16[32,1024]{1,0:T(8,128)(2,1)S...) custom-call(f32[256,1024]{1,0:T(8,128)S(1)} %get-tuple-element.63.re, ...), custom_call_target="tpu_custom_call" | custom-call | bytes 16384 | tf_op jit(solution)/shard_map/pallas_call | solution.py:454
  52.3 2.9 %collective-permute-start.16 = (bf16[32,1024]{1,0:T(8,128)(2,1)S(1)}, bf16[32,1024]{1,0:T(8,128)(2,1)S(1)}, u32[]{:S(2)}, u32[]{:S(2)}) collective-permute-start(bf16[32,1024]{1,0:T(8,128)(2,1)S(1)} %get-tuple-element.76), channel_id=1, source_target_pairs={{0,5},{1,4},{2,7},{3,6},{4,1},{5,0},{6,3},{7,2},{8,13},{9,12},{10,... | collective-permute-start | bytes 196616 | tf_op jit(solution)/shard_map/ppermute | solution.py:359
  55.2 2.8 %collective-permute-start.17 = (bf16[32,1024]{1,0:T(8,128)(2,1)S(1)}, bf16[32,1024]{1,0:T(8,128)(2,1)S(1)}, u32[]{:S(2)}, u32[]{:S(2)}) collective-permute-start(bf16[32,1024]{1,0:T(8,128)(2,1)S(1)} %get-tuple-element.77), channel_id=1, source_target_pairs={{0,6},{1,7},{2,4},{3,5},{4,2},{5,3},{6,0},{7,1},{8,14},{9,15},{10,... | collective-permute-start | bytes 196616 | tf_op jit(solution)/shard_map/ppermute | solution.py:359
  58.0 1.6 %collective-permute-start.18 = (bf16[32,1024]{1,0:T(8,128)(2,1)S(1)}, bf16[32,1024]{1,0:T(8,128)(2,1)S(1)}, u32[]{:S(2)}, u32[]{:S(2)}) collective-permute-start(bf16[32,1024]{1,0:T(8,128)(2,1)S(1)} %get-tuple-element.78), channel_id=1, source_target_pairs={{0,7},{1,6},{2,5},{3,4},{4,3},{5,2},{6,1},{7,0},{8,15},{9,14},{10,... | collective-permute-start | bytes 196616 | tf_op jit(solution)/shard_map/ppermute | solution.py:359
  59.6 2.2 %collective-permute-done.15.refs_0_ = bf16[32,1024]{1,0:T(8,128)(2,1)S(1)} collective-permute-done((bf16[32,1024]{1,0:T(8,128)(2,1)S(1)}, bf16[32,1024]{1,0:T(8,128)(2,1)S(1)}, u32[]{:S(2)}, u32[]{:S(2)}) %collective-permute-start.15) | collective-permute-done | bytes 65568 | tf_op jit(solution)/shard_map/ppermute | solution.py:359
  62.0 2.0 %collective-permute-done.16.refs_1_ = bf16[32,1024]{1,0:T(8,128)(2,1)S(1)} collective-permute-done((bf16[32,1024]{1,0:T(8,128)(2,1)S(1)}, bf16[32,1024]{1,0:T(8,128)(2,1)S(1)}, u32[]{:S(2)}, u32[]{:S(2)}) %collective-permute-start.16) | collective-permute-done | bytes 65568 | tf_op jit(solution)/shard_map/ppermute | solution.py:359
  63.9 1.5 %collective-permute-start.22 = (bf16[32,1024]{1,0:T(8,128)(2,1)S(1)}, bf16[32,1024]{1,0:T(8,128)(2,1)S(1)}, u32[]{:S(2)}, u32[]{:S(2)}) collective-permute-start(bf16[32,1024]{1,0:T(8,128)(2,1)S(1)} %get-tuple-element.83), channel_id=1, source_target_pairs={{0,1},{1,0},{2,3},{3,2},{4,5},{5,4},{6,7},{7,6},{8,9},{9,8},{10,11... | collective-permute-start | bytes 196616 | tf_op jit(solution)/shard_map/ppermute | solution.py:359
  65.4 2.6 %collective-permute-start.19 = (bf16[256,1024]{1,0:T(8,128)(2,1)S(1)}, bf16[256,1024]{1,0:T(8,128)(2,1)S(1)}, u32[]{:S(2)}, u32[]{:S(2)}) collective-permute-start(bf16[256,1024]{1,0:T(8,128)(2,1)S(1)} %get-tuple-element.79), channel_id=1, source_target_pairs={{0,4},{1,5},{2,6},{3,7},{4,0},{5,1},{6,2},{7,3},{8,12},{9,13},{10,... | collective-permute-start | bytes 1572872 | tf_op jit(solution)/shard_map/ppermute | solution.py:359
  68.2 1.3 %shard_map.109 = (f32[64,3200]{1,0:T(8,128)S(1)}, bf16[16,3200]{1,0:T(8,128)(2,1)S(1)}, bf16[16,3200]{1,0:T(8,128)(2,1)S(1)}, bf16[16,3200]{1,0:T(8,128)(2,1)S(1)}, bf16[16,3200]{1,0:T(8,128)(2,1)S(1)}) custom-call(bf16[32,1024]{1,0:T(8,128)(2,1)S(1)} %collective-permute-done.15.refs_0_, bf16[32,1024]{1,0:T(8,128)(2,1)S(1)} %collective-permute-done.16.refs_1_, ...), custom_call_target="tpu_custom_call" | custom-call | bytes 1024 | tf_op jit(solution)/shard_map/pallas_call | solution.py:472
  71.6 1.7 %collective-permute-start.27 = (bf16[16,3200]{1,0:T(8,128)(2,1)S(1)}, bf16[16,3200]{1,0:T(8,128)(2,1)S(1)}, u32[]{:S(2)}, u32[]{:S(2)}) collective-permute-start(bf16[16,3200]{1,0:T(8,128)(2,1)S(1)} %get-tuple-element.91), channel_id=1, source_target_pairs={{0,16},{1,17},{2,18},{3,19},{4,20},{5,21},{6,22},{7,23},{8,24},{9,... | collective-permute-start | bytes 307208 | tf_op jit(solution)/shard_map/ppermute | solution.py:359
  73.7 3.7 %collective-permute-done.27.refs_0_ = bf16[16,3200]{1,0:T(8,128)(2,1)S(1)} collective-permute-done((bf16[16,3200]{1,0:T(8,128)(2,1)S(1)}, bf16[16,3200]{1,0:T(8,128)(2,1)S(1)}, u32[]{:S(2)}, u32[]{:S(2)}) %collective-permute-start.27) | collective-permute-done | bytes 102432 | tf_op jit(solution)/shard_map/ppermute | solution.py:359
  77.3 1.6 %collective-permute-done.28.refs_1_ = bf16[16,3200]{1,0:T(8,128)(2,1)S(1)} collective-permute-done((bf16[16,3200]{1,0:T(8,128)(2,1)S(1)}, bf16[16,3200]{1,0:T(8,128)(2,1)S(1)}, u32[]{:S(2)}, u32[]{:S(2)}) %collective-permute-start.28) | collective-permute-done | bytes 102432 | tf_op jit(solution)/shard_map/ppermute | solution.py:359
  79.1 1.7 %collective-permute-start.30 = (bf16[32,1536]{1,0:T(8,128)(2,1)S(1)}, bf16[32,1536]{1,0:T(8,128)(2,1)S(1)}, u32[]{:S(2)}, u32[]{:S(2)}) collective-permute-start(bf16[32,1536]{1,0:T(8,128)(2,1)S(1)} %shard_map.111.refs_0_), channel_id=1, source_target_pairs={{0,16},{1,17},{2,18},{3,19},{4,20},{5,21},{6,22},{7,23},{8,24},{9,... | collective-permute-start | bytes 294920 | tf_op jit(solution)/shard_map/ppermute | solution.py:359
  80.8 3.0 %collective-permute-done.30.refs_2_ = bf16[32,1536]{1,0:T(8,128)(2,1)S(1)} collective-permute-done((bf16[32,1536]{1,0:T(8,128)(2,1)S(1)}, bf16[32,1536]{1,0:T(8,128)(2,1)S(1)}, u32[]{:S(2)}, u32[]{:S(2)}) %collective-permute-start.30) | collective-permute-done | bytes 98336 | tf_op jit(solution)/shard_map/ppermute | solution.py:359
  83.8 1.3 %collective-permute-done.31.refs_3_ = bf16[32,1536]{1,0:T(8,128)(2,1)S(1)} collective-permute-done((bf16[32,1536]{1,0:T(8,128)(2,1)S(1)}, bf16[32,1536]{1,0:T(8,128)(2,1)S(1)}, u32[]{:S(2)}, u32[]{:S(2)}) %collective-permute-start.31) | collective-permute-done | bytes 98336 | tf_op jit(solution)/shard_map/ppermute | solution.py:359
  85.1 0.7 shard_map.112
  85.8 0.5 collective-permute-start.32
  86.3 3.4 %collective-permute-start.33 = (bf16[16,1024]{1,0:T(8,128)(2,1)S(1)}, bf16[16,1024]{1,0:T(8,128)(2,1)S(1)}, u32[]{:S(2)}, u32[]{:S(2)}) collective-permute-start(bf16[16,1024]{1,0:T(8,128)(2,1)S(1)} %get-tuple-element.94), channel_id=1, source_target_pairs={{0,5},{1,4},{2,7},{3,6},{4,1},{5,0},{6,3},{7,2},{8,13},{9,12},{10,... | collective-permute-start | bytes 98312 | tf_op jit(solution)/shard_map/ppermute | solution.py:359
  89.7 2.7 %collective-permute-start.34 = (bf16[16,1024]{1,0:T(8,128)(2,1)S(1)}, bf16[16,1024]{1,0:T(8,128)(2,1)S(1)}, u32[]{:S(2)}, u32[]{:S(2)}) collective-permute-start(bf16[16,1024]{1,0:T(8,128)(2,1)S(1)} %get-tuple-element.95), channel_id=1, source_target_pairs={{0,6},{1,7},{2,4},{3,5},{4,2},{5,3},{6,0},{7,1},{8,14},{9,15},{10,... | collective-permute-start | bytes 98312 | tf_op jit(solution)/shard_map/ppermute | solution.py:359
  92.4 1.1 %collective-permute-start.35 = (bf16[16,1024]{1,0:T(8,128)(2,1)S(1)}, bf16[16,1024]{1,0:T(8,128)(2,1)S(1)}, u32[]{:S(2)}, u32[]{:S(2)}) collective-permute-start(bf16[16,1024]{1,0:T(8,128)(2,1)S(1)} %get-tuple-element.96), channel_id=1, source_target_pairs={{0,7},{1,6},{2,5},{3,4},{4,3},{5,2},{6,1},{7,0},{8,15},{9,14},{10,... | collective-permute-start | bytes 98312 | tf_op jit(solution)/shard_map/ppermute | solution.py:359
  93.9 1.2 %collective-permute-done.33.refs_1_ = bf16[16,1024]{1,0:T(8,128)(2,1)S(1)} collective-permute-done((bf16[16,1024]{1,0:T(8,128)(2,1)S(1)}, bf16[16,1024]{1,0:T(8,128)(2,1)S(1)}, u32[]{:S(2)}, u32[]{:S(2)}) %collective-permute-start.33) | collective-permute-done | bytes 32800 | tf_op jit(solution)/shard_map/ppermute | solution.py:359
  95.1 1.4 %collective-permute-start.37 = (bf16[16,1024]{1,0:T(8,128)(2,1)S(1)}, bf16[16,1024]{1,0:T(8,128)(2,1)S(1)}, u32[]{:S(2)}, u32[]{:S(2)}) collective-permute-start(bf16[16,1024]{1,0:T(8,128)(2,1)S(1)} %get-tuple-element.98), channel_id=1, source_target_pairs={{0,2},{1,3},{2,0},{3,1},{4,6},{5,7},{6,4},{7,5},{8,10},{9,11},{10,... | collective-permute-start | bytes 98312 | tf_op jit(solution)/shard_map/ppermute | solution.py:359
  97.2 1.8 %collective-permute-done.35.refs_3_ = bf16[16,1024]{1,0:T(8,128)(2,1)S(1)} collective-permute-done((bf16[16,1024]{1,0:T(8,128)(2,1)S(1)}, bf16[16,1024]{1,0:T(8,128)(2,1)S(1)}, u32[]{:S(2)}, u32[]{:S(2)}) %collective-permute-start.35) | collective-permute-done | bytes 32800 | tf_op jit(solution)/shard_map/ppermute | solution.py:359
  99.1 1.4 %collective-permute-done.38.refs_6_ = bf16[16,1024]{1,0:T(8,128)(2,1)S(1)} collective-permute-done((bf16[16,1024]{1,0:T(8,128)(2,1)S(1)}, bf16[16,1024]{1,0:T(8,128)(2,1)S(1)}, u32[]{:S(2)}, u32[]{:S(2)}) %collective-permute-start.38) | collective-permute-done | bytes 32800 | tf_op jit(solution)/shard_map/ppermute | solution.py:359
  100.5 1.1 %shard_map.113 = bf16[256,1024]{1,0:T(8,128)(2,1)} custom-call(f32[256,1024]{1,0:T(8,128)S(1)} %shard_map.108.mixed, bf16[128,256]{1,0:T(8,128)(2,1)S(1)} %get-tuple-element.64.refs_6_.place_ref, f32[256,128]{1,0:T(8,128)S(1)} %get-tuple-element.80.gate_ref, bf16[16,1024]{1,0:T(8,128)(2,1)S(1)} %collective-permute-done.32.refs_0_, ...), custom_call_target="tpu_custom_call" | custom-call | bytes 2097152 | tf_op jit(solution)/shard_map/pallas_call | solution.py:512
  (63 shorter events, 5.9 us)
Async XLA Ops:
  0.0 27.2 %collective-permute-start.6 = (bf16[512,1024]{1,0:T(8,128)(2,1)}, bf16[512,1024]{1,0:T(8,128)(2,1)S(1)}, u32[]{:S(2)}, u32[]{:S(2)}) collective-permute-start(bf16[512,1024]{1,0:T(8,128)(2,1)} %refs_0_.1), channel_id=1, source_target_pairs={{0,1},{1,0},{2,3},{3,2},{4,5},{5,4},{6,7},{7,6},{8,9},{9,8},{10,11... | collective-permute-start | bytes 3145736 | tf_op jit(solution)/shard_map/ppermute | solution.py:359
  2.9 31.1 %collective-permute-start.7 = (bf16[512,1024]{1,0:T(8,128)(2,1)}, bf16[512,1024]{1,0:T(8,128)(2,1)S(1)}, u32[]{:S(2)}, u32[]{:S(2)}) collective-permute-start(bf16[512,1024]{1,0:T(8,128)(2,1)} %refs_0_.1), channel_id=1, source_target_pairs={{0,2},{1,3},{2,0},{3,1},{4,6},{5,7},{6,4},{7,5},{8,10},{9,11},{10,... | collective-permute-start | bytes 3145736 | tf_op jit(solution)/shard_map/ppermute | solution.py:359
  6.0 9.3 %collective-permute-start = (bf16[64,2048]{1,0:T(8,128)(2,1)S(1)}, bf16[64,2048]{1,0:T(8,128)(2,1)S(1)}, u32[]{:S(2)}, u32[]{:S(2)}) collective-permute-start(bf16[64,2048]{1,0:T(8,128)(2,1)S(1)} %get-tuple-element.53), channel_id=1, source_target_pairs={{0,16},{1,17},{2,18},{3,19},{4,20},{5,21},{6,22},{7,23},{8,24},{9,... | collective-permute-start | bytes 786440 | tf_op jit(solution)/shard_map/ppermute | solution.py:359
  7.6 10.6 %collective-permute-start.1 = (bf16[64,2048]{1,0:T(8,128)(2,1)S(1)}, bf16[64,2048]{1,0:T(8,128)(2,1)S(1)}, u32[]{:S(2)}, u32[]{:S(2)}) collective-permute-start(bf16[64,2048]{1,0:T(8,128)(2,1)S(1)} %get-tuple-element.54), channel_id=1, source_target_pairs={{0,24},{1,25},{2,26},{3,27},{4,28},{5,29},{6,30},{7,31},{8,16},{9,... | collective-permute-start | bytes 786440 | tf_op jit(solution)/shard_map/ppermute | solution.py:359
  7.6 10.6 %collective-permute-start.2 = (bf16[64,2048]{1,0:T(8,128)(2,1)S(1)}, bf16[64,2048]{1,0:T(8,128)(2,1)S(1)}, u32[]{:S(2)}, u32[]{:S(2)}) collective-permute-start(bf16[64,2048]{1,0:T(8,128)(2,1)S(1)} %get-tuple-element.55), channel_id=1, source_target_pairs={{0,8},{1,9},{2,10},{3,11},{4,12},{5,13},{6,14},{7,15},{8,0},{9,1},... | collective-permute-start | bytes 786440 | tf_op jit(solution)/shard_map/ppermute | solution.py:359
  20.5 16.5 %collective-permute-start.8 = (bf16[256,512]{1,0:T(8,128)(2,1)S(1)}, bf16[256,512]{1,0:T(8,128)(2,1)S(1)}, u32[]{:S(2)}, u32[]{:S(2)}) collective-permute-start(bf16[256,512]{1,0:T(8,128)(2,1)S(1)} %get-tuple-element.57), channel_id=1, source_target_pairs={{0,4},{1,5},{2,6},{3,7},{4,0},{5,1},{6,2},{7,3},{8,12},{9,13},{10,... | collective-permute-start | bytes 786440 | tf_op jit(solution)/shard_map/ppermute | solution.py:359
  23.2 1.2 %copy-start.1 = (bf16[512,1024]{1,0:T(8,128)(2,1)S(1)}, bf16[512,1024]{1,0:T(8,128)(2,1)}, u32[]{:S(2)}) copy-start(bf16[512,1024]{1,0:T(8,128)(2,1)} %refs_0_.1) | copy-start | bytes 3145732
  24.4 1.0 %copy-start.2 = (bf16[4,1,64,1024]{3,2,1,0:T(8,128)(2,1)S(1)}, bf16[4,1,64,1024]{3,2,1,0:T(8,128)(2,1)}, u32[]{:S(2)}) copy-start(bf16[4,1,64,1024]{3,2,1,0:T(8,128)(2,1)} %param.13) | copy-start | bytes 1572868
  25.4 0.7 copy-start.3
  26.1 0.7 copy-start.4
  27.2 19.4 %collective-permute-start.11 = (bf16[512,384]{1,0:T(8,128)(2,1)S(1)}, bf16[512,384]{1,0:T(8,128)(2,1)S(1)}, u32[]{:S(2)}, u32[]{:S(2)}) collective-permute-start(bf16[512,384]{1,0:T(8,128)(2,1)S(1)} %slice.6), channel_id=1, source_target_pairs={{0,2},{1,3},{2,0},{3,1},{4,6},{5,7},{6,4},{7,5},{8,10},{9,11},{10,... | collective-permute-start | bytes 1179656 | tf_op jit(solution)/shard_map/ppermute | solution.py:359
  34.1 16.2 %collective-permute-start.13 = (bf16[512,640]{1,0:T(8,128)(2,1)S(1)}, bf16[512,640]{1,0:T(8,128)(2,1)S(1)}, u32[]{:S(2)}, u32[]{:S(2)}) collective-permute-start(bf16[512,640]{1,0:T(8,128)(2,1)S(1)} %slice.7), channel_id=1, source_target_pairs={{0,1},{1,0},{2,3},{3,2},{4,5},{5,4},{6,7},{7,6},{8,9},{9,8},{10,11... | collective-permute-start | bytes 1966088 | tf_op jit(solution)/shard_map/ppermute | solution.py:359
  34.3 9.5 %collective-permute-start.4 = (bf16[256,512]{1,0:T(8,128)(2,1)S(1)}, bf16[256,512]{1,0:T(8,128)(2,1)S(1)}, u32[]{:S(2)}, u32[]{:S(2)}) collective-permute-start(bf16[256,512]{1,0:T(8,128)(2,1)S(1)} %shard_map.103.refs_1_), channel_id=1, source_target_pairs={{0,16},{1,17},{2,18},{3,19},{4,20},{5,21},{6,22},{7,23},{8,24},{9,... | collective-permute-start | bytes 786440 | tf_op jit(solution)/shard_map/ppermute | solution.py:359
  37.0 9.6 %collective-permute-start.10 = (bf16[256,512]{1,0:T(8,128)(2,1)S(1)}, bf16[256,512]{1,0:T(8,128)(2,1)S(1)}, u32[]{:S(2)}, u32[]{:S(2)}) collective-permute-start(bf16[256,512]{1,0:T(8,128)(2,1)S(1)} %collective-permute-done.8.refs_0_), channel_id=1, source_target_pairs={{0,16},{1,17},{2,18},{3,19},{4,20},{5,21},{6,22},{7,23},{8,24},{9,... | collective-permute-start | bytes 786440 | tf_op jit(solution)/shard_map/ppermute | solution.py:359
  37.1 10.1 %collective-permute-start.14 = (s32[4,8,64]{2,1,0:T(8,128)S(1)}, s32[4,8,64]{2,1,0:T(8,128)S(1)}, u32[]{:S(2)}, u32[]{:S(2)}) collective-permute-start(s32[4,8,64]{2,1,0:T(8,128)S(1)} %bitcast.23), channel_id=1, source_target_pairs={{0,4},{1,5},{2,6},{3,7},{4,0},{5,1},{6,2},{7,3},{8,12},{9,13},{10,... | collective-permute-start | bytes 24584 | tf_op jit(solution)/shard_map/ppermute | solution.py:359
  43.8 3.6 %collective-permute-start.3 = (bf16[256,512]{1,0:T(8,128)(2,1)S(1)}, bf16[256,512]{1,0:T(8,128)(2,1)S(1)}, u32[]{:S(2)}, u32[]{:S(2)}) collective-permute-start(bf16[256,512]{1,0:T(8,128)(2,1)S(1)} %shard_map.103.refs_1_), channel_id=1, source_target_pairs={{0,8},{1,9},{2,10},{3,11},{4,12},{5,13},{6,14},{7,15},{8,0},{9,1},... | collective-permute-start | bytes 786440 | tf_op jit(solution)/shard_map/ppermute | solution.py:359
  46.6 1.5 %collective-permute-start.5 = (bf16[256,512]{1,0:T(8,128)(2,1)S(1)}, bf16[256,512]{1,0:T(8,128)(2,1)S(1)}, u32[]{:S(2)}, u32[]{:S(2)}) collective-permute-start(bf16[256,512]{1,0:T(8,128)(2,1)S(1)} %collective-permute-done.4.refs_3_), channel_id=1, source_target_pairs={{0,8},{1,9},{2,10},{3,11},{4,12},{5,13},{6,14},{7,15},{8,0},{9,1},... | collective-permute-start | bytes 786440 | tf_op jit(solution)/shard_map/ppermute | solution.py:359
  46.6 2.6 %collective-permute-start.9 = (bf16[256,512]{1,0:T(8,128)(2,1)S(1)}, bf16[256,512]{1,0:T(8,128)(2,1)S(1)}, u32[]{:S(2)}, u32[]{:S(2)}) collective-permute-start(bf16[256,512]{1,0:T(8,128)(2,1)S(1)} %collective-permute-done.8.refs_0_), channel_id=1, source_target_pairs={{0,8},{1,9},{2,10},{3,11},{4,12},{5,13},{6,14},{7,15},{8,0},{9,1},... | collective-permute-start | bytes 786440 | tf_op jit(solution)/shard_map/ppermute | solution.py:359
  47.1 2.1 %collective-permute-start.12 = (bf16[256,512]{1,0:T(8,128)(2,1)S(1)}, bf16[256,512]{1,0:T(8,128)(2,1)S(1)}, u32[]{:S(2)}, u32[]{:S(2)}) collective-permute-start(bf16[256,512]{1,0:T(8,128)(2,1)S(1)} %collective-permute-done.10.refs_2_), channel_id=1, source_target_pairs={{0,8},{1,9},{2,10},{3,11},{4,12},{5,13},{6,14},{7,15},{8,0},{9,1},... | collective-permute-start | bytes 786440 | tf_op jit(solution)/shard_map/ppermute | solution.py:359
  48.2 20.0 %slice-start = ((s8[6291456]{0:T(1024)(128)(4,1)}), s8[4194304]{0:T(1024)(128)(4,1)S(1)}, s32[]{:S(2)}) async-start(s8[6291456]{0:T(1024)(128)(4,1)} %bitcast.16), calls=%async_computation | async-start | bytes 8388608
  48.2 20.0 %copy-start.5 = (f32[1024]{0:T(1024)S(1)}, f32[1024]{0:T(1024)}, u32[]{:S(2)}) copy-start(f32[1024]{0:T(1024)} %param.15) | copy-start | bytes 12292
  49.2 19.0 %slice-start.1 = ((s8[6291456]{0:T(1024)(128)(4,1)}), s8[2097152]{0:T(1024)(128)(4,1)S(1)}, s32[]{:S(2)}) async-start(s8[6291456]{0:T(1024)(128)(4,1)} %bitcast.16), calls=%async_computation.1 | async-start | bytes 4194304
  50.4 34.8 %copy-start = (bf16[1,1536,1024]{2,1,0:T(8,128)(2,1)S(1)}, bf16[1,1536,1024]{2,1,0:T(8,128)(2,1)}, u32[]{:S(2)}) copy-start(bf16[1,1536,1024]{2,1,0:T(8,128)(2,1)} %param.19) | copy-start | bytes 9437188
  51.9 10.0 %collective-permute-start.15 = (bf16[32,1024]{1,0:T(8,128)(2,1)S(1)}, bf16[32,1024]{1,0:T(8,128)(2,1)S(1)}, u32[]{:S(2)}, u32[]{:S(2)}) collective-permute-start(bf16[32,1024]{1,0:T(8,128)(2,1)S(1)} %get-tuple-element.75), channel_id=1, source_target_pairs={{0,4},{1,5},{2,6},{3,7},{4,0},{5,1},{6,2},{7,3},{8,12},{9,13},{10,... | collective-permute-start | bytes 196616 | tf_op jit(solution)/shard_map/ppermute | solution.py:359
  52.3 11.6 %collective-permute-start.16 = (bf16[32,1024]{1,0:T(8,128)(2,1)S(1)}, bf16[32,1024]{1,0:T(8,128)(2,1)S(1)}, u32[]{:S(2)}, u32[]{:S(2)}) collective-permute-start(bf16[32,1024]{1,0:T(8,128)(2,1)S(1)} %get-tuple-element.76), channel_id=1, source_target_pairs={{0,5},{1,4},{2,7},{3,6},{4,1},{5,0},{6,3},{7,2},{8,13},{9,12},{10,... | collective-permute-start | bytes 196616 | tf_op jit(solution)/shard_map/ppermute | solution.py:359
  55.2 10.2 %collective-permute-start.17 = (bf16[32,1024]{1,0:T(8,128)(2,1)S(1)}, bf16[32,1024]{1,0:T(8,128)(2,1)S(1)}, u32[]{:S(2)}, u32[]{:S(2)}) collective-permute-start(bf16[32,1024]{1,0:T(8,128)(2,1)S(1)} %get-tuple-element.77), channel_id=1, source_target_pairs={{0,6},{1,7},{2,4},{3,5},{4,2},{5,3},{6,0},{7,1},{8,14},{9,15},{10,... | collective-permute-start | bytes 196616 | tf_op jit(solution)/shard_map/ppermute | solution.py:359
  58.0 7.4 %collective-permute-start.18 = (bf16[32,1024]{1,0:T(8,128)(2,1)S(1)}, bf16[32,1024]{1,0:T(8,128)(2,1)S(1)}, u32[]{:S(2)}, u32[]{:S(2)}) collective-permute-start(bf16[32,1024]{1,0:T(8,128)(2,1)S(1)} %get-tuple-element.78), channel_id=1, source_target_pairs={{0,7},{1,6},{2,5},{3,4},{4,3},{5,2},{6,1},{7,0},{8,15},{9,14},{10,... | collective-permute-start | bytes 196616 | tf_op jit(solution)/shard_map/ppermute | solution.py:359
  59.6 8.4 %collective-permute-start.20 = (bf16[32,1024]{1,0:T(8,128)(2,1)S(1)}, bf16[32,1024]{1,0:T(8,128)(2,1)S(1)}, u32[]{:S(2)}, u32[]{:S(2)}) collective-permute-start(bf16[32,1024]{1,0:T(8,128)(2,1)S(1)} %get-tuple-element.81), channel_id=1, source_target_pairs={{0,3},{1,2},{2,1},{3,0},{4,7},{5,6},{6,5},{7,4},{8,11},{9,10},{10,... | collective-permute-start | bytes 196616 | tf_op jit(solution)/shard_map/ppermute | solution.py:359
  61.8 6.2 %collective-permute-start.21 = (bf16[32,1024]{1,0:T(8,128)(2,1)S(1)}, bf16[32,1024]{1,0:T(8,128)(2,1)S(1)}, u32[]{:S(2)}, u32[]{:S(2)}) collective-permute-start(bf16[32,1024]{1,0:T(8,128)(2,1)S(1)} %get-tuple-element.82), channel_id=1, source_target_pairs={{0,2},{1,3},{2,0},{3,1},{4,6},{5,7},{6,4},{7,5},{8,10},{9,11},{10,... | collective-permute-start | bytes 196616 | tf_op jit(solution)/shard_map/ppermute | solution.py:359
  63.9 4.3 %collective-permute-start.22 = (bf16[32,1024]{1,0:T(8,128)(2,1)S(1)}, bf16[32,1024]{1,0:T(8,128)(2,1)S(1)}, u32[]{:S(2)}, u32[]{:S(2)}) collective-permute-start(bf16[32,1024]{1,0:T(8,128)(2,1)S(1)} %get-tuple-element.83), channel_id=1, source_target_pairs={{0,1},{1,0},{2,3},{3,2},{4,5},{5,4},{6,7},{7,6},{8,9},{9,8},{10,11... | collective-permute-start | bytes 196616 | tf_op jit(solution)/shard_map/ppermute | solution.py:359
  65.4 31.2 %collective-permute-start.19 = (bf16[256,1024]{1,0:T(8,128)(2,1)S(1)}, bf16[256,1024]{1,0:T(8,128)(2,1)S(1)}, u32[]{:S(2)}, u32[]{:S(2)}) collective-permute-start(bf16[256,1024]{1,0:T(8,128)(2,1)S(1)} %get-tuple-element.79), channel_id=1, source_target_pairs={{0,4},{1,5},{2,6},{3,7},{4,0},{5,1},{6,2},{7,3},{8,12},{9,13},{10,... | collective-permute-start | bytes 1572872 | tf_op jit(solution)/shard_map/ppermute | solution.py:359
  69.5 1.3 %collective-permute-start.23 = (bf16[16,3200]{1,0:T(8,128)(2,1)S(1)}, bf16[16,3200]{1,0:T(8,128)(2,1)S(1)}, u32[]{:S(2)}, u32[]{:S(2)}) collective-permute-start(bf16[16,3200]{1,0:T(8,128)(2,1)S(1)} %get-tuple-element.86), channel_id=1, source_target_pairs={{0,8},{1,9},{2,10},{3,11},{4,12},{5,13},{6,14},{7,15},{8,0},{9,1},... | collective-permute-start | bytes 307208 | tf_op jit(solution)/shard_map/ppermute | solution.py:359
  69.5 1.4 %collective-permute-start.24 = (bf16[16,3200]{1,0:T(8,128)(2,1)S(1)}, bf16[16,3200]{1,0:T(8,128)(2,1)S(1)}, u32[]{:S(2)}, u32[]{:S(2)}) collective-permute-start(bf16[16,3200]{1,0:T(8,128)(2,1)S(1)} %get-tuple-element.87), channel_id=1, source_target_pairs={{0,8},{1,9},{2,10},{3,11},{4,12},{5,13},{6,14},{7,15},{8,0},{9,1},... | collective-permute-start | bytes 307208 | tf_op jit(solution)/shard_map/ppermute | solution.py:359
  70.0 1.3 %collective-permute-start.25 = (bf16[16,3200]{1,0:T(8,128)(2,1)S(1)}, bf16[16,3200]{1,0:T(8,128)(2,1)S(1)}, u32[]{:S(2)}, u32[]{:S(2)}) collective-permute-start(bf16[16,3200]{1,0:T(8,128)(2,1)S(1)} %get-tuple-element.88), channel_id=1, source_target_pairs={{0,8},{1,9},{2,10},{3,11},{4,12},{5,13},{6,14},{7,15},{8,0},{9,1},... | collective-permute-start | bytes 307208 | tf_op jit(solution)/shard_map/ppermute | solution.py:359
  70.1 1.4 %collective-permute-start.26 = (bf16[16,3200]{1,0:T(8,128)(2,1)S(1)}, bf16[16,3200]{1,0:T(8,128)(2,1)S(1)}, u32[]{:S(2)}, u32[]{:S(2)}) collective-permute-start(bf16[16,3200]{1,0:T(8,128)(2,1)S(1)} %get-tuple-element.89), channel_id=1, source_target_pairs={{0,8},{1,9},{2,10},{3,11},{4,12},{5,13},{6,14},{7,15},{8,0},{9,1},... | collective-permute-start | bytes 307208 | tf_op jit(solution)/shard_map/ppermute | solution.py:359
  71.6 5.8 %collective-permute-start.27 = (bf16[16,3200]{1,0:T(8,128)(2,1)S(1)}, bf16[16,3200]{1,0:T(8,128)(2,1)S(1)}, u32[]{:S(2)}, u32[]{:S(2)}) collective-permute-start(bf16[16,3200]{1,0:T(8,128)(2,1)S(1)} %get-tuple-element.91), channel_id=1, source_target_pairs={{0,16},{1,17},{2,18},{3,19},{4,20},{5,21},{6,22},{7,23},{8,24},{9,... | collective-permute-start | bytes 307208 | tf_op jit(solution)/shard_map/ppermute | solution.py:359
  73.3 5.7 %collective-permute-start.28 = (bf16[16,3200]{1,0:T(8,128)(2,1)S(1)}, bf16[16,3200]{1,0:T(8,128)(2,1)S(1)}, u32[]{:S(2)}, u32[]{:S(2)}) collective-permute-start(bf16[16,3200]{1,0:T(8,128)(2,1)S(1)} %get-tuple-element.92), channel_id=1, source_target_pairs={{0,16},{1,17},{2,18},{3,19},{4,20},{5,21},{6,22},{7,23},{8,24},{9,... | collective-permute-start | bytes 307208 | tf_op jit(solution)/shard_map/ppermute | solution.py:359
  79.1 4.7 %collective-permute-start.30 = (bf16[32,1536]{1,0:T(8,128)(2,1)S(1)}, bf16[32,1536]{1,0:T(8,128)(2,1)S(1)}, u32[]{:S(2)}, u32[]{:S(2)}) collective-permute-start(bf16[32,1536]{1,0:T(8,128)(2,1)S(1)} %shard_map.111.refs_0_), channel_id=1, source_target_pairs={{0,16},{1,17},{2,18},{3,19},{4,20},{5,21},{6,22},{7,23},{8,24},{9,... | collective-permute-start | bytes 294920 | tf_op jit(solution)/shard_map/ppermute | solution.py:359
  80.8 3.0 %collective-permute-start.29 = (bf16[32,1536]{1,0:T(8,128)(2,1)S(1)}, bf16[32,1536]{1,0:T(8,128)(2,1)S(1)}, u32[]{:S(2)}, u32[]{:S(2)}) collective-permute-start(bf16[32,1536]{1,0:T(8,128)(2,1)S(1)} %shard_map.111.refs_0_), channel_id=1, source_target_pairs={{0,8},{1,9},{2,10},{3,11},{4,12},{5,13},{6,14},{7,15},{8,0},{9,1},... | collective-permute-start | bytes 294920 | tf_op jit(solution)/shard_map/ppermute | solution.py:359
  83.8 1.3 %collective-permute-start.31 = (bf16[32,1536]{1,0:T(8,128)(2,1)S(1)}, bf16[32,1536]{1,0:T(8,128)(2,1)S(1)}, u32[]{:S(2)}, u32[]{:S(2)}) collective-permute-start(bf16[32,1536]{1,0:T(8,128)(2,1)S(1)} %collective-permute-done.30.refs_2_), channel_id=1, source_target_pairs={{0,8},{1,9},{2,10},{3,11},{4,12},{5,13},{6,14},{7,15},{8,0},{9,1},... | collective-permute-start | bytes 294920 | tf_op jit(solution)/shard_map/ppermute | solution.py:359
  85.8 7.7 %collective-permute-start.32 = (bf16[16,1024]{1,0:T(8,128)(2,1)S(1)}, bf16[16,1024]{1,0:T(8,128)(2,1)S(1)}, u32[]{:S(2)}, u32[]{:S(2)}) collective-permute-start(bf16[16,1024]{1,0:T(8,128)(2,1)S(1)} %get-tuple-element.93), channel_id=1, source_target_pairs={{0,4},{1,5},{2,6},{3,7},{4,0},{5,1},{6,2},{7,3},{8,12},{9,13},{10,... | collective-permute-start | bytes 98312 | tf_op jit(solution)/shard_map/ppermute | solution.py:359
  86.3 8.8 %collective-permute-start.33 = (bf16[16,1024]{1,0:T(8,128)(2,1)S(1)}, bf16[16,1024]{1,0:T(8,128)(2,1)S(1)}, u32[]{:S(2)}, u32[]{:S(2)}) collective-permute-start(bf16[16,1024]{1,0:T(8,128)(2,1)S(1)} %get-tuple-element.94), channel_id=1, source_target_pairs={{0,5},{1,4},{2,7},{3,6},{4,1},{5,0},{6,3},{7,2},{8,13},{9,12},{10,... | collective-permute-start | bytes 98312 | tf_op jit(solution)/shard_map/ppermute | solution.py:359
  89.7 7.5 %collective-permute-start.34 = (bf16[16,1024]{1,0:T(8,128)(2,1)S(1)}, bf16[16,1024]{1,0:T(8,128)(2,1)S(1)}, u32[]{:S(2)}, u32[]{:S(2)}) collective-permute-start(bf16[16,1024]{1,0:T(8,128)(2,1)S(1)} %get-tuple-element.95), channel_id=1, source_target_pairs={{0,6},{1,7},{2,4},{3,5},{4,2},{5,3},{6,0},{7,1},{8,14},{9,15},{10,... | collective-permute-start | bytes 98312 | tf_op jit(solution)/shard_map/ppermute | solution.py:359
  92.4 6.6 %collective-permute-start.35 = (bf16[16,1024]{1,0:T(8,128)(2,1)S(1)}, bf16[16,1024]{1,0:T(8,128)(2,1)S(1)}, u32[]{:S(2)}, u32[]{:S(2)}) collective-permute-start(bf16[16,1024]{1,0:T(8,128)(2,1)S(1)} %get-tuple-element.96), channel_id=1, source_target_pairs={{0,7},{1,6},{2,5},{3,4},{4,3},{5,2},{6,1},{7,0},{8,15},{9,14},{10,... | collective-permute-start | bytes 98312 | tf_op jit(solution)/shard_map/ppermute | solution.py:359
  93.5 5.5 %collective-permute-start.36 = (bf16[16,1024]{1,0:T(8,128)(2,1)S(1)}, bf16[16,1024]{1,0:T(8,128)(2,1)S(1)}, u32[]{:S(2)}, u32[]{:S(2)}) collective-permute-start(bf16[16,1024]{1,0:T(8,128)(2,1)S(1)} %get-tuple-element.97), channel_id=1, source_target_pairs={{0,3},{1,2},{2,1},{3,0},{4,7},{5,6},{6,5},{7,4},{8,11},{9,10},{10,... | collective-permute-start | bytes 98312 | tf_op jit(solution)/shard_map/ppermute | solution.py:359
  95.1 3.9 %collective-permute-start.37 = (bf16[16,1024]{1,0:T(8,128)(2,1)S(1)}, bf16[16,1024]{1,0:T(8,128)(2,1)S(1)}, u32[]{:S(2)}, u32[]{:S(2)}) collective-permute-start(bf16[16,1024]{1,0:T(8,128)(2,1)S(1)} %get-tuple-element.98), channel_id=1, source_target_pairs={{0,2},{1,3},{2,0},{3,1},{4,6},{5,7},{6,4},{7,5},{8,10},{9,11},{10,... | collective-permute-start | bytes 98312 | tf_op jit(solution)/shard_map/ppermute | solution.py:359
  96.6 3.9 %collective-permute-start.38 = (bf16[16,1024]{1,0:T(8,128)(2,1)S(1)}, bf16[16,1024]{1,0:T(8,128)(2,1)S(1)}, u32[]{:S(2)}, u32[]{:S(2)}) collective-permute-start(bf16[16,1024]{1,0:T(8,128)(2,1)S(1)} %get-tuple-element.99), channel_id=1, source_target_pairs={{0,1},{1,0},{2,3},{3,2},{4,5},{5,4},{6,7},{7,6},{8,9},{9,8},{10,11... | collective-permute-start | bytes 98312 | tf_op jit(solution)/shard_map/ppermute | solution.py:359

commit v21 on v19

--- a/solution.py
+++ b/solution.py
@@ -439,7 +439,7 @@
         )(*operands)
 
     mine_all = gather(mine)
-    cut = width - max(width * 3 // 8, 128)
+    cut = width - max(width // 4, 128)
     near = after(shards[1], place)[:, cut:]
     for d in range(2, C, 2):
         shards[d + 1] = (

time: 102 us -> 101 us (level)
  waiting for transfers between devices: 38.4 us -> 36.7 us
    ppermute x39, waiting for transfers between devices: 38.4 us -> 36.7 us  [permute(): return lax.ppermute(x, ('ctx', 'exp'), pairs)]
  transfers between devices with their start and end apart: 39 -> 39, of which waited for: 22 -> 23; matrix products, arithmetic and copies ran while one was open for 0% -> 0% of each run, Pallas kernels for 11% -> 11%
where the time goes in v21:
time: 101 us
  starting transfers between devices  46.3 us (46%)
  waiting for transfers between devices  36.7 us (36%)
  Pallas kernels  13.8 us (14%)
  local copies, waits for them, and re-layouts  3.82 us (4%)
    ppermute x39, starting transfers between devices, permute(): return lax.ppermute(x, ('ctx', 'exp'), pairs)  46.3 us
    ppermute x39, waiting for transfers between devices, permute(): return lax.ppermute(x, ('ctx', 'exp'), pairs)  36.7 us
    pallas_call x2, Pallas kernels, attend(): call(functools.partial(attend_kernel, C, t), [sds((rows, qw), BF16)] + [s...  4.63 us
    unnamed x16, local copies, waits for them, and re-layouts  3.72 us
    pallas_call x2, Pallas kernels, project(): call(functools.partial(project_kernel, C, bool(extra)), [sds((rows, width...  2.14 us
  transfers between devices with their start and end apart: 39, of which 23 were waited for; matrix products, arithmetic and copies ran while one was open for 0% of the time, Pallas kernels for 11%

profile of v21, /device:TPU:0, one launch (start us, length us, event | category | flops | bytes accessed | tf_op | source)
XLA Modules:
  0.0 100.9 jit_solution(12174210240787807239)
XLA Ops:
  0.0 3.0 %collective-permute-start.7 = (bf16[512,1024]{1,0:T(8,128)(2,1)}, bf16[512,1024]{1,0:T(8,128)(2,1)S(1)}, u32[]{:S(2)}, u32[]{:S(2)}) collective-permute-start(bf16[512,1024]{1,0:T(8,128)(2,1)} %refs_0_.1), channel_id=1, source_target_pairs={{0,2},{1,3},{2,0},{3,1},{4,6},{5,7},{6,4},{7,5},{8,10},{9,11},{10,... | collective-permute-start | bytes 3145736 | tf_op jit(solution)/shard_map/ppermute | solution.py:359
  3.0 1.5 %collective-permute-start.6 = (bf16[512,1024]{1,0:T(8,128)(2,1)}, bf16[512,1024]{1,0:T(8,128)(2,1)S(1)}, u32[]{:S(2)}, u32[]{:S(2)}) collective-permute-start(bf16[512,1024]{1,0:T(8,128)(2,1)} %refs_0_.1), channel_id=1, source_target_pairs={{0,1},{1,0},{2,3},{3,2},{4,5},{5,4},{6,7},{7,6},{8,9},{9,8},{10,11... | collective-permute-start | bytes 3145736 | tf_op jit(solution)/shard_map/ppermute | solution.py:359
  4.5 1.4 %shard_map.100 = (bf16[64,2048]{1,0:T(8,128)(2,1)S(1)}, bf16[64,2048]{1,0:T(8,128)(2,1)S(1)}, bf16[64,2048]{1,0:T(8,128)(2,1)S(1)}, bf16[64,2048]{1,0:T(8,128)(2,1)S(1)}) custom-call(bf16[64,4096]{1,0:T(8,128)(2,1)} %bitcast.25, bf16[64,512]{1,0:T(8,128)(2,1)} %bitcast.26, bf16[64,512]{1,0:T(8,128)(2,1)} %bitcast.27), custom_call_target="tpu_custom_call" | custom-call | bytes 1048576 | tf_op jit(solution)/shard_map/pallas_call | solution.py:365
  6.0 1.6 %collective-permute-start = (bf16[64,2048]{1,0:T(8,128)(2,1)S(1)}, bf16[64,2048]{1,0:T(8,128)(2,1)S(1)}, u32[]{:S(2)}, u32[]{:S(2)}) collective-permute-start(bf16[64,2048]{1,0:T(8,128)(2,1)S(1)} %get-tuple-element.53), channel_id=1, source_target_pairs={{0,16},{1,17},{2,18},{3,19},{4,20},{5,21},{6,22},{7,23},{8,24},{9,... | collective-permute-start | bytes 786440 | tf_op jit(solution)/shard_map/ppermute | solution.py:359
  8.2 7.1 %collective-permute-done.refs_0_ = bf16[64,2048]{1,0:T(8,128)(2,1)S(1)} collective-permute-done((bf16[64,2048]{1,0:T(8,128)(2,1)S(1)}, bf16[64,2048]{1,0:T(8,128)(2,1)S(1)}, u32[]{:S(2)}, u32[]{:S(2)}) %collective-permute-start) | collective-permute-done | bytes 262176 | tf_op jit(solution)/shard_map/ppermute | solution.py:359
  15.3 2.9 %collective-permute-done.1.refs_1_ = bf16[64,2048]{1,0:T(8,128)(2,1)S(1)} collective-permute-done((bf16[64,2048]{1,0:T(8,128)(2,1)S(1)}, bf16[64,2048]{1,0:T(8,128)(2,1)S(1)}, u32[]{:S(2)}, u32[]{:S(2)}) %collective-permute-start.1) | collective-permute-done | bytes 262176 | tf_op jit(solution)/shard_map/ppermute | solution.py:359
  18.2 2.3 %shard_map.101 = (bf16[256,512]{1,0:T(8,128)(2,1)S(1)}, bf16[64,2048]{1,0:T(8,128)(2,1)S(1)}) custom-call(bf16[64,2048]{1,0:T(8,128)(2,1)S(1)} %collective-permute-done.refs_0_, bf16[64,2048]{1,0:T(8,128)(2,1)S(1)} %collective-permute-done.1.refs_1_, bf16[64,2048]{1,0:T(8,128)(2,1)S(1)} %collective-permute-done.2.refs_2_, ...), custom_call_target="tpu_custom_call" | custom-call | bytes 16384 | tf_op jit(solution)/shard_map/pallas_call | solution.py:386
  20.5 2.7 %collective-permute-start.8 = (bf16[256,512]{1,0:T(8,128)(2,1)S(1)}, bf16[256,512]{1,0:T(8,128)(2,1)S(1)}, u32[]{:S(2)}, u32[]{:S(2)}) collective-permute-start(bf16[256,512]{1,0:T(8,128)(2,1)S(1)} %get-tuple-element.57), channel_id=1, source_target_pairs={{0,4},{1,5},{2,6},{3,7},{4,0},{5,1},{6,2},{7,3},{8,12},{9,13},{10,... | collective-permute-start | bytes 786440 | tf_op jit(solution)/shard_map/ppermute | solution.py:359
  23.2 2.3 %shard_map.102.refs_1_ = bf16[256,512]{1,0:T(8,128)(2,1)S(1)} custom-call(bf16[64,2048]{1,0:T(8,128)(2,1)S(1)} %collective-permute-done.refs_0_, bf16[64,2048]{1,0:T(8,128)(2,1)S(1)} %collective-permute-done.1.refs_1_, bf16[64,2048]{1,0:T(8,128)(2,1)S(1)} %collective-permute-done.2.refs_2_, bf16[64,2048]{1,0:T(8,128)(2,1)S(1)} %get-tuple-element.59.refs_3_), custom_call_target="tpu_custom_call" | custom-call | bytes 16384 | tf_op jit(solution)/shard_map/pallas_call | solution.py:386
  25.5 1.2 %copy-done.1 = bf16[512,1024]{1,0:T(8,128)(2,1)S(1)} copy-done((bf16[512,1024]{1,0:T(8,128)(2,1)S(1)}, bf16[512,1024]{1,0:T(8,128)(2,1)}, u32[]{:S(2)}) %copy-start.1) | copy-done | bytes 1048600
  26.7 1.0 %copy-done.2 = bf16[4,1,64,1024]{3,2,1,0:T(8,128)(2,1)S(1)} copy-done((bf16[4,1,64,1024]{3,2,1,0:T(8,128)(2,1)S(1)}, bf16[4,1,64,1024]{3,2,1,0:T(8,128)(2,1)}, u32[]{:S(2)}) %copy-start.2) | copy-done | bytes 524312
  27.7 0.7 copy-done.3
  30.1 2.7 %collective-permute-start.13 = (bf16[512,768]{1,0:T(8,128)(2,1)S(1)}, bf16[512,768]{1,0:T(8,128)(2,1)S(1)}, u32[]{:S(2)}, u32[]{:S(2)}) collective-permute-start(bf16[512,768]{1,0:T(8,128)(2,1)S(1)} %slice.7), channel_id=1, source_target_pairs={{0,1},{1,0},{2,3},{3,2},{4,5},{5,4},{6,7},{7,6},{8,9},{9,8},{10,11... | collective-permute-start | bytes 2359304 | tf_op jit(solution)/shard_map/ppermute | solution.py:359
  32.8 2.3 %collective-permute-start.4 = (bf16[256,512]{1,0:T(8,128)(2,1)S(1)}, bf16[256,512]{1,0:T(8,128)(2,1)S(1)}, u32[]{:S(2)}, u32[]{:S(2)}) collective-permute-start(bf16[256,512]{1,0:T(8,128)(2,1)S(1)} %shard_map.102.refs_1_), channel_id=1, source_target_pairs={{0,16},{1,17},{2,18},{3,19},{4,20},{5,21},{6,22},{7,23},{8,24},{9,... | collective-permute-start | bytes 786440 | tf_op jit(solution)/shard_map/ppermute | solution.py:359
  35.1 1.1 %collective-permute-done.8.refs_0_ = bf16[256,512]{1,0:T(8,128)(2,1)S(1)} collective-permute-done((bf16[256,512]{1,0:T(8,128)(2,1)S(1)}, bf16[256,512]{1,0:T(8,128)(2,1)S(1)}, u32[]{:S(2)}, u32[]{:S(2)}) %collective-permute-start.8) | collective-permute-done | bytes 262176 | tf_op jit(solution)/shard_map/ppermute | solution.py:359
  36.5 2.9 %collective-permute-start.14 = (s32[4,8,64]{2,1,0:T(8,128)S(1)}, s32[4,8,64]{2,1,0:T(8,128)S(1)}, u32[]{:S(2)}, u32[]{:S(2)}) collective-permute-start(s32[4,8,64]{2,1,0:T(8,128)S(1)} %bitcast.23), channel_id=1, source_target_pairs={{0,4},{1,5},{2,6},{3,7},{4,0},{5,1},{6,2},{7,3},{8,12},{9,13},{10,... | collective-permute-start | bytes 24584 | tf_op jit(solution)/shard_map/ppermute | solution.py:359
  39.4 2.5 %collective-permute-done.4.refs_3_ = bf16[256,512]{1,0:T(8,128)(2,1)S(1)} collective-permute-done((bf16[256,512]{1,0:T(8,128)(2,1)S(1)}, bf16[256,512]{1,0:T(8,128)(2,1)S(1)}, u32[]{:S(2)}, u32[]{:S(2)}) %collective-permute-start.4) | collective-permute-done | bytes 262176 | tf_op jit(solution)/shard_map/ppermute | solution.py:359
  41.8 3.2 %collective-permute-done.11.refs_5_ = bf16[512,256]{1,0:T(8,128)(2,1)S(1)} collective-permute-done((bf16[512,256]{1,0:T(8,128)(2,1)S(1)}, bf16[512,256]{1,0:T(8,128)(2,1)S(1)}, u32[]{:S(2)}, u32[]{:S(2)}) %collective-permute-start.11) | collective-permute-done | bytes 262176 | tf_op jit(solution)/shard_map/ppermute | solution.py:359
  45.0 0.8 collective-permute-done.10.refs_2_
  46.6 1.1 %shard_map.104 = (f32[256,1024]{1,0:T(8,128)S(1)}, bf16[256,512]{1,0:T(8,128)(2,1)S(1)}) custom-call(bf16[256,1024]{1,0:T(8,128)(2,1)S(1)} %get-tuple-element.61.refs_0_, bf16[256,512]{1,0:T(8,128)(2,1)S(1)} %shard_map.102.refs_1_, bf16[256,512]{1,0:T(8,128)(2,1)S(1)} %collective-permute-done.3.refs_2_, bf16[256,512]{1,0:T(8,128)(2,1)S(1)} %collective-permute-done.4.refs_3_, ...), custom_call_target="tpu_custom_call" | custom-call | bytes 16384 | tf_op jit(solution)/shard_map/pallas_call | solution.py:431
  47.8 1.1 %shard_map.105 = (f32[256,1024]{1,0:T(8,128)S(1)}, bf16[256,512]{1,0:T(8,128)(2,1)S(1)}) custom-call(bf16[256,512]{1,0:T(8,128)(2,1)S(1)} %collective-permute-done.8.refs_0_, bf16[256,512]{1,0:T(8,128)(2,1)S(1)} %collective-permute-done.9.refs_1_, bf16[256,512]{1,0:T(8,128)(2,1)S(1)} %collective-permute-done.10.refs_2_, ...), custom_call_target="tpu_custom_call" | custom-call | bytes 16384 | tf_op jit(solution)/shard_map/pallas_call | solution.py:431
  48.8 1.1 %collective-permute-done.13.refs_4_ = bf16[512,768]{1,0:T(8,128)(2,1)S(1)} collective-permute-done((bf16[512,768]{1,0:T(8,128)(2,1)S(1)}, bf16[512,768]{1,0:T(8,128)(2,1)S(1)}, u32[]{:S(2)}, u32[]{:S(2)}) %collective-permute-start.13) | collective-permute-done | bytes 786464 | tf_op jit(solution)/shard_map/ppermute | solution.py:359
  49.9 1.6 %shard_map.107 = (f32[256,1024]{1,0:T(8,128)S(1)}, bf16[256,1024]{1,0:T(8,128)(2,1)S(1)}, bf16[32,1024]{1,0:T(8,128)(2,1)S(1)}, bf16[32,1024]{1,0:T(8,128)(2,1)S...) custom-call(f32[256,1024]{1,0:T(8,128)S(1)} %get-tuple-element.63.re, ...), custom_call_target="tpu_custom_call" | custom-call | bytes 16384 | tf_op jit(solution)/shard_map/pallas_call | solution.py:454
  52.1 3.1 %collective-permute-start.16 = (bf16[32,1024]{1,0:T(8,128)(2,1)S(1)}, bf16[32,1024]{1,0:T(8,128)(2,1)S(1)}, u32[]{:S(2)}, u32[]{:S(2)}) collective-permute-start(bf16[32,1024]{1,0:T(8,128)(2,1)S(1)} %get-tuple-element.76), channel_id=1, source_target_pairs={{0,5},{1,4},{2,7},{3,6},{4,1},{5,0},{6,3},{7,2},{8,13},{9,12},{10,... | collective-permute-start | bytes 196616 | tf_op jit(solution)/shard_map/ppermute | solution.py:359
  55.2 2.5 %collective-permute-start.17 = (bf16[32,1024]{1,0:T(8,128)(2,1)S(1)}, bf16[32,1024]{1,0:T(8,128)(2,1)S(1)}, u32[]{:S(2)}, u32[]{:S(2)}) collective-permute-start(bf16[32,1024]{1,0:T(8,128)(2,1)S(1)} %get-tuple-element.77), channel_id=1, source_target_pairs={{0,6},{1,7},{2,4},{3,5},{4,2},{5,3},{6,0},{7,1},{8,14},{9,15},{10,... | collective-permute-start | bytes 196616 | tf_op jit(solution)/shard_map/ppermute | solution.py:359
  57.7 1.5 %collective-permute-start.18 = (bf16[32,1024]{1,0:T(8,128)(2,1)S(1)}, bf16[32,1024]{1,0:T(8,128)(2,1)S(1)}, u32[]{:S(2)}, u32[]{:S(2)}) collective-permute-start(bf16[32,1024]{1,0:T(8,128)(2,1)S(1)} %get-tuple-element.78), channel_id=1, source_target_pairs={{0,7},{1,6},{2,5},{3,4},{4,3},{5,2},{6,1},{7,0},{8,15},{9,14},{10,... | collective-permute-start | bytes 196616 | tf_op jit(solution)/shard_map/ppermute | solution.py:359
  59.2 1.1 %collective-permute-done.15.refs_0_ = bf16[32,1024]{1,0:T(8,128)(2,1)S(1)} collective-permute-done((bf16[32,1024]{1,0:T(8,128)(2,1)S(1)}, bf16[32,1024]{1,0:T(8,128)(2,1)S(1)}, u32[]{:S(2)}, u32[]{:S(2)}) %collective-permute-start.15) | collective-permute-done | bytes 65568 | tf_op jit(solution)/shard_map/ppermute | solution.py:359
  60.3 1.7 %collective-permute-start.21 = (bf16[32,1024]{1,0:T(8,128)(2,1)S(1)}, bf16[32,1024]{1,0:T(8,128)(2,1)S(1)}, u32[]{:S(2)}, u32[]{:S(2)}) collective-permute-start(bf16[32,1024]{1,0:T(8,128)(2,1)S(1)} %get-tuple-element.82), channel_id=1, source_target_pairs={{0,2},{1,3},{2,0},{3,1},{4,6},{5,7},{6,4},{7,5},{8,10},{9,11},{10,... | collective-permute-start | bytes 196616 | tf_op jit(solution)/shard_map/ppermute | solution.py:359
  62.0 1.4 %collective-permute-done.16.refs_1_ = bf16[32,1024]{1,0:T(8,128)(2,1)S(1)} collective-permute-done((bf16[32,1024]{1,0:T(8,128)(2,1)S(1)}, bf16[32,1024]{1,0:T(8,128)(2,1)S(1)}, u32[]{:S(2)}, u32[]{:S(2)}) %collective-permute-start.16) | collective-permute-done | bytes 65568 | tf_op jit(solution)/shard_map/ppermute | solution.py:359
  63.4 1.4 %collective-permute-start.22 = (bf16[32,1024]{1,0:T(8,128)(2,1)S(1)}, bf16[32,1024]{1,0:T(8,128)(2,1)S(1)}, u32[]{:S(2)}, u32[]{:S(2)}) collective-permute-start(bf16[32,1024]{1,0:T(8,128)(2,1)S(1)} %get-tuple-element.83), channel_id=1, source_target_pairs={{0,1},{1,0},{2,3},{3,2},{4,5},{5,4},{6,7},{7,6},{8,9},{9,8},{10,11... | collective-permute-start | bytes 196616 | tf_op jit(solution)/shard_map/ppermute | solution.py:359
  64.8 2.4 %collective-permute-start.19 = (bf16[256,1024]{1,0:T(8,128)(2,1)S(1)}, bf16[256,1024]{1,0:T(8,128)(2,1)S(1)}, u32[]{:S(2)}, u32[]{:S(2)}) collective-permute-start(bf16[256,1024]{1,0:T(8,128)(2,1)S(1)} %get-tuple-element.79), channel_id=1, source_target_pairs={{0,4},{1,5},{2,6},{3,7},{4,0},{5,1},{6,2},{7,3},{8,12},{9,13},{10,... | collective-permute-start | bytes 1572872 | tf_op jit(solution)/shard_map/ppermute | solution.py:359
  67.7 1.3 %shard_map.109 = (f32[64,3200]{1,0:T(8,128)S(1)}, bf16[16,3200]{1,0:T(8,128)(2,1)S(1)}, bf16[16,3200]{1,0:T(8,128)(2,1)S(1)}, bf16[16,3200]{1,0:T(8,128)(2,1)S(1)}, bf16[16,3200]{1,0:T(8,128)(2,1)S(1)}) custom-call(bf16[32,1024]{1,0:T(8,128)(2,1)S(1)} %collective-permute-done.15.refs_0_, bf16[32,1024]{1,0:T(8,128)(2,1)S(1)} %collective-permute-done.16.refs_1_, ...), custom_call_target="tpu_custom_call" | custom-call | bytes 1024 | tf_op jit(solution)/shard_map/pallas_call | solution.py:472
  71.0 2.0 %collective-permute-start.27 = (bf16[16,3200]{1,0:T(8,128)(2,1)S(1)}, bf16[16,3200]{1,0:T(8,128)(2,1)S(1)}, u32[]{:S(2)}, u32[]{:S(2)}) collective-permute-start(bf16[16,3200]{1,0:T(8,128)(2,1)S(1)} %get-tuple-element.91), channel_id=1, source_target_pairs={{0,16},{1,17},{2,18},{3,19},{4,20},{5,21},{6,22},{7,23},{8,24},{9,... | collective-permute-start | bytes 307208 | tf_op jit(solution)/shard_map/ppermute | solution.py:359
  73.1 3.7 %collective-permute-done.27.refs_0_ = bf16[16,3200]{1,0:T(8,128)(2,1)S(1)} collective-permute-done((bf16[16,3200]{1,0:T(8,128)(2,1)S(1)}, bf16[16,3200]{1,0:T(8,128)(2,1)S(1)}, u32[]{:S(2)}, u32[]{:S(2)}) %collective-permute-start.27) | collective-permute-done | bytes 102432 | tf_op jit(solution)/shard_map/ppermute | solution.py:359
  76.8 1.8 %collective-permute-done.28.refs_1_ = bf16[16,3200]{1,0:T(8,128)(2,1)S(1)} collective-permute-done((bf16[16,3200]{1,0:T(8,128)(2,1)S(1)}, bf16[16,3200]{1,0:T(8,128)(2,1)S(1)}, u32[]{:S(2)}, u32[]{:S(2)}) %collective-permute-start.28) | collective-permute-done | bytes 102432 | tf_op jit(solution)/shard_map/ppermute | solution.py:359
  78.8 1.8 %collective-permute-start.30 = (bf16[32,1536]{1,0:T(8,128)(2,1)S(1)}, bf16[32,1536]{1,0:T(8,128)(2,1)S(1)}, u32[]{:S(2)}, u32[]{:S(2)}) collective-permute-start(bf16[32,1536]{1,0:T(8,128)(2,1)S(1)} %shard_map.111.refs_0_), channel_id=1, source_target_pairs={{0,16},{1,17},{2,18},{3,19},{4,20},{5,21},{6,22},{7,23},{8,24},{9,... | collective-permute-start | bytes 294920 | tf_op jit(solution)/shard_map/ppermute | solution.py:359
  80.6 2.9 %collective-permute-done.30.refs_2_ = bf16[32,1536]{1,0:T(8,128)(2,1)S(1)} collective-permute-done((bf16[32,1536]{1,0:T(8,128)(2,1)S(1)}, bf16[32,1536]{1,0:T(8,128)(2,1)S(1)}, u32[]{:S(2)}, u32[]{:S(2)}) %collective-permute-start.30) | collective-permute-done | bytes 98336 | tf_op jit(solution)/shard_map/ppermute | solution.py:359
  83.4 1.3 %collective-permute-done.31.refs_3_ = bf16[32,1536]{1,0:T(8,128)(2,1)S(1)} collective-permute-done((bf16[32,1536]{1,0:T(8,128)(2,1)S(1)}, bf16[32,1536]{1,0:T(8,128)(2,1)S(1)}, u32[]{:S(2)}, u32[]{:S(2)}) %collective-permute-start.31) | collective-permute-done | bytes 98336 | tf_op jit(solution)/shard_map/ppermute | solution.py:359
  85.4 0.8 collective-permute-start.32
  86.2 2.9 %collective-permute-start.33 = (bf16[16,1024]{1,0:T(8,128)(2,1)S(1)}, bf16[16,1024]{1,0:T(8,128)(2,1)S(1)}, u32[]{:S(2)}, u32[]{:S(2)}) collective-permute-start(bf16[16,1024]{1,0:T(8,128)(2,1)S(1)} %get-tuple-element.94), channel_id=1, source_target_pairs={{0,5},{1,4},{2,7},{3,6},{4,1},{5,0},{6,3},{7,2},{8,13},{9,12},{10,... | collective-permute-start | bytes 98312 | tf_op jit(solution)/shard_map/ppermute | solution.py:359
  89.1 2.3 %collective-permute-start.34 = (bf16[16,1024]{1,0:T(8,128)(2,1)S(1)}, bf16[16,1024]{1,0:T(8,128)(2,1)S(1)}, u32[]{:S(2)}, u32[]{:S(2)}) collective-permute-start(bf16[16,1024]{1,0:T(8,128)(2,1)S(1)} %get-tuple-element.95), channel_id=1, source_target_pairs={{0,6},{1,7},{2,4},{3,5},{4,2},{5,3},{6,0},{7,1},{8,14},{9,15},{10,... | collective-permute-start | bytes 98312 | tf_op jit(solution)/shard_map/ppermute | solution.py:359
  91.5 1.7 %collective-permute-start.35 = (bf16[16,1024]{1,0:T(8,128)(2,1)S(1)}, bf16[16,1024]{1,0:T(8,128)(2,1)S(1)}, u32[]{:S(2)}, u32[]{:S(2)}) collective-permute-start(bf16[16,1024]{1,0:T(8,128)(2,1)S(1)} %get-tuple-element.96), channel_id=1, source_target_pairs={{0,7},{1,6},{2,5},{3,4},{4,3},{5,2},{6,1},{7,0},{8,15},{9,14},{10,... | collective-permute-start | bytes 98312 | tf_op jit(solution)/shard_map/ppermute | solution.py:359
  93.1 1.0 collective-permute-done.33.refs_1_
  94.1 1.8 %collective-permute-start.37 = (bf16[16,1024]{1,0:T(8,128)(2,1)S(1)}, bf16[16,1024]{1,0:T(8,128)(2,1)S(1)}, u32[]{:S(2)}, u32[]{:S(2)}) collective-permute-start(bf16[16,1024]{1,0:T(8,128)(2,1)S(1)} %get-tuple-element.98), channel_id=1, source_target_pairs={{0,2},{1,3},{2,0},{3,1},{4,6},{5,7},{6,4},{7,5},{8,10},{9,11},{10,... | collective-permute-start | bytes 98312 | tf_op jit(solution)/shard_map/ppermute | solution.py:359
  95.9 0.8 collective-permute-start.38
  96.8 1.4 %collective-permute-done.35.refs_3_ = bf16[16,1024]{1,0:T(8,128)(2,1)S(1)} collective-permute-done((bf16[16,1024]{1,0:T(8,128)(2,1)S(1)}, bf16[16,1024]{1,0:T(8,128)(2,1)S(1)}, u32[]{:S(2)}, u32[]{:S(2)}) %collective-permute-start.35) | collective-permute-done | bytes 32800 | tf_op jit(solution)/shard_map/ppermute | solution.py:359
  98.3 1.5 %collective-permute-done.38.refs_6_ = bf16[16,1024]{1,0:T(8,128)(2,1)S(1)} collective-permute-done((bf16[16,1024]{1,0:T(8,128)(2,1)S(1)}, bf16[16,1024]{1,0:T(8,128)(2,1)S(1)}, u32[]{:S(2)}, u32[]{:S(2)}) %collective-permute-start.38) | collective-permute-done | bytes 32800 | tf_op jit(solution)/shard_map/ppermute | solution.py:359
  99.8 1.1 %shard_map.113 = bf16[256,1024]{1,0:T(8,128)(2,1)} custom-call(f32[256,1024]{1,0:T(8,128)S(1)} %shard_map.108.mixed, bf16[128,256]{1,0:T(8,128)(2,1)S(1)} %get-tuple-element.64.refs_6_.place_ref, f32[256,128]{1,0:T(8,128)S(1)} %get-tuple-element.80.gate_ref, bf16[16,1024]{1,0:T(8,128)(2,1)S(1)} %collective-permute-done.32.refs_0_, ...), custom_call_target="tpu_custom_call" | custom-call | bytes 2097152 | tf_op jit(solution)/shard_map/pallas_call | solution.py:512
  (63 shorter events, 7.6 us)
Async XLA Ops:
  0.0 30.0 %collective-permute-start.7 = (bf16[512,1024]{1,0:T(8,128)(2,1)}, bf16[512,1024]{1,0:T(8,128)(2,1)S(1)}, u32[]{:S(2)}, u32[]{:S(2)}) collective-permute-start(bf16[512,1024]{1,0:T(8,128)(2,1)} %refs_0_.1), channel_id=1, source_target_pairs={{0,2},{1,3},{2,0},{3,1},{4,6},{5,7},{6,4},{7,5},{8,10},{9,11},{10,... | collective-permute-start | bytes 3145736 | tf_op jit(solution)/shard_map/ppermute | solution.py:359
  3.0 32.0 %collective-permute-start.6 = (bf16[512,1024]{1,0:T(8,128)(2,1)}, bf16[512,1024]{1,0:T(8,128)(2,1)S(1)}, u32[]{:S(2)}, u32[]{:S(2)}) collective-permute-start(bf16[512,1024]{1,0:T(8,128)(2,1)} %refs_0_.1), channel_id=1, source_target_pairs={{0,1},{1,0},{2,3},{3,2},{4,5},{5,4},{6,7},{7,6},{8,9},{9,8},{10,11... | collective-permute-start | bytes 3145736 | tf_op jit(solution)/shard_map/ppermute | solution.py:359
  6.0 9.3 %collective-permute-start = (bf16[64,2048]{1,0:T(8,128)(2,1)S(1)}, bf16[64,2048]{1,0:T(8,128)(2,1)S(1)}, u32[]{:S(2)}, u32[]{:S(2)}) collective-permute-start(bf16[64,2048]{1,0:T(8,128)(2,1)S(1)} %get-tuple-element.53), channel_id=1, source_target_pairs={{0,16},{1,17},{2,18},{3,19},{4,20},{5,21},{6,22},{7,23},{8,24},{9,... | collective-permute-start | bytes 786440 | tf_op jit(solution)/shard_map/ppermute | solution.py:359
  7.6 10.6 %collective-permute-start.1 = (bf16[64,2048]{1,0:T(8,128)(2,1)S(1)}, bf16[64,2048]{1,0:T(8,128)(2,1)S(1)}, u32[]{:S(2)}, u32[]{:S(2)}) collective-permute-start(bf16[64,2048]{1,0:T(8,128)(2,1)S(1)} %get-tuple-element.54), channel_id=1, source_target_pairs={{0,24},{1,25},{2,26},{3,27},{4,28},{5,29},{6,30},{7,31},{8,16},{9,... | collective-permute-start | bytes 786440 | tf_op jit(solution)/shard_map/ppermute | solution.py:359
  7.6 10.6 %collective-permute-start.2 = (bf16[64,2048]{1,0:T(8,128)(2,1)S(1)}, bf16[64,2048]{1,0:T(8,128)(2,1)S(1)}, u32[]{:S(2)}, u32[]{:S(2)}) collective-permute-start(bf16[64,2048]{1,0:T(8,128)(2,1)S(1)} %get-tuple-element.55), channel_id=1, source_target_pairs={{0,8},{1,9},{2,10},{3,11},{4,12},{5,13},{6,14},{7,15},{8,0},{9,1},... | collective-permute-start | bytes 786440 | tf_op jit(solution)/shard_map/ppermute | solution.py:359
  20.5 15.7 %collective-permute-start.8 = (bf16[256,512]{1,0:T(8,128)(2,1)S(1)}, bf16[256,512]{1,0:T(8,128)(2,1)S(1)}, u32[]{:S(2)}, u32[]{:S(2)}) collective-permute-start(bf16[256,512]{1,0:T(8,128)(2,1)S(1)} %get-tuple-element.57), channel_id=1, source_target_pairs={{0,4},{1,5},{2,6},{3,7},{4,0},{5,1},{6,2},{7,3},{8,12},{9,13},{10,... | collective-permute-start | bytes 786440 | tf_op jit(solution)/shard_map/ppermute | solution.py:359
  25.5 1.2 %copy-start.1 = (bf16[512,1024]{1,0:T(8,128)(2,1)S(1)}, bf16[512,1024]{1,0:T(8,128)(2,1)}, u32[]{:S(2)}) copy-start(bf16[512,1024]{1,0:T(8,128)(2,1)} %refs_0_.1) | copy-start | bytes 3145732
  26.7 1.0 %copy-start.2 = (bf16[4,1,64,1024]{3,2,1,0:T(8,128)(2,1)S(1)}, bf16[4,1,64,1024]{3,2,1,0:T(8,128)(2,1)}, u32[]{:S(2)}) copy-start(bf16[4,1,64,1024]{3,2,1,0:T(8,128)(2,1)} %param.13) | copy-start | bytes 1572868
  27.7 0.7 copy-start.3
  28.5 0.7 copy-start.4
  30.1 19.8 %collective-permute-start.13 = (bf16[512,768]{1,0:T(8,128)(2,1)S(1)}, bf16[512,768]{1,0:T(8,128)(2,1)S(1)}, u32[]{:S(2)}, u32[]{:S(2)}) collective-permute-start(bf16[512,768]{1,0:T(8,128)(2,1)S(1)} %slice.7), channel_id=1, source_target_pairs={{0,1},{1,0},{2,3},{3,2},{4,5},{5,4},{6,7},{7,6},{8,9},{9,8},{10,11... | collective-permute-start | bytes 2359304 | tf_op jit(solution)/shard_map/ppermute | solution.py:359
  32.8 9.1 %collective-permute-start.4 = (bf16[256,512]{1,0:T(8,128)(2,1)S(1)}, bf16[256,512]{1,0:T(8,128)(2,1)S(1)}, u32[]{:S(2)}, u32[]{:S(2)}) collective-permute-start(bf16[256,512]{1,0:T(8,128)(2,1)S(1)} %shard_map.102.refs_1_), channel_id=1, source_target_pairs={{0,16},{1,17},{2,18},{3,19},{4,20},{5,21},{6,22},{7,23},{8,24},{9,... | collective-permute-start | bytes 786440 | tf_op jit(solution)/shard_map/ppermute | solution.py:359
  36.2 8.7 %collective-permute-start.11 = (bf16[512,256]{1,0:T(8,128)(2,1)S(1)}, bf16[512,256]{1,0:T(8,128)(2,1)S(1)}, u32[]{:S(2)}, u32[]{:S(2)}) collective-permute-start(bf16[512,256]{1,0:T(8,128)(2,1)S(1)} %slice.6), channel_id=1, source_target_pairs={{0,2},{1,3},{2,0},{3,1},{4,6},{5,7},{6,4},{7,5},{8,10},{9,11},{10,... | collective-permute-start | bytes 786440 | tf_op jit(solution)/shard_map/ppermute | solution.py:359
  36.3 9.5 %collective-permute-start.10 = (bf16[256,512]{1,0:T(8,128)(2,1)S(1)}, bf16[256,512]{1,0:T(8,128)(2,1)S(1)}, u32[]{:S(2)}, u32[]{:S(2)}) collective-permute-start(bf16[256,512]{1,0:T(8,128)(2,1)S(1)} %collective-permute-done.8.refs_0_), channel_id=1, source_target_pairs={{0,16},{1,17},{2,18},{3,19},{4,20},{5,21},{6,22},{7,23},{8,24},{9,... | collective-permute-start | bytes 786440 | tf_op jit(solution)/shard_map/ppermute | solution.py:359
  36.5 9.4 %collective-permute-start.14 = (s32[4,8,64]{2,1,0:T(8,128)S(1)}, s32[4,8,64]{2,1,0:T(8,128)S(1)}, u32[]{:S(2)}, u32[]{:S(2)}) collective-permute-start(s32[4,8,64]{2,1,0:T(8,128)S(1)} %bitcast.23), channel_id=1, source_target_pairs={{0,4},{1,5},{2,6},{3,7},{4,0},{5,1},{6,2},{7,3},{8,12},{9,13},{10,... | collective-permute-start | bytes 24584 | tf_op jit(solution)/shard_map/ppermute | solution.py:359
  41.8 4.8 %collective-permute-start.3 = (bf16[256,512]{1,0:T(8,128)(2,1)S(1)}, bf16[256,512]{1,0:T(8,128)(2,1)S(1)}, u32[]{:S(2)}, u32[]{:S(2)}) collective-permute-start(bf16[256,512]{1,0:T(8,128)(2,1)S(1)} %shard_map.102.refs_1_), channel_id=1, source_target_pairs={{0,8},{1,9},{2,10},{3,11},{4,12},{5,13},{6,14},{7,15},{8,0},{9,1},... | collective-permute-start | bytes 786440 | tf_op jit(solution)/shard_map/ppermute | solution.py:359
  45.0 1.6 %collective-permute-start.5 = (bf16[256,512]{1,0:T(8,128)(2,1)S(1)}, bf16[256,512]{1,0:T(8,128)(2,1)S(1)}, u32[]{:S(2)}, u32[]{:S(2)}) collective-permute-start(bf16[256,512]{1,0:T(8,128)(2,1)S(1)} %collective-permute-done.4.refs_3_), channel_id=1, source_target_pairs={{0,8},{1,9},{2,10},{3,11},{4,12},{5,13},{6,14},{7,15},{8,0},{9,1},... | collective-permute-start | bytes 786440 | tf_op jit(solution)/shard_map/ppermute | solution.py:359
  45.8 1.9 %collective-permute-start.9 = (bf16[256,512]{1,0:T(8,128)(2,1)S(1)}, bf16[256,512]{1,0:T(8,128)(2,1)S(1)}, u32[]{:S(2)}, u32[]{:S(2)}) collective-permute-start(bf16[256,512]{1,0:T(8,128)(2,1)S(1)} %collective-permute-done.8.refs_0_), channel_id=1, source_target_pairs={{0,8},{1,9},{2,10},{3,11},{4,12},{5,13},{6,14},{7,15},{8,0},{9,1},... | collective-permute-start | bytes 786440 | tf_op jit(solution)/shard_map/ppermute | solution.py:359
  45.8 1.9 %collective-permute-start.12 = (bf16[256,512]{1,0:T(8,128)(2,1)S(1)}, bf16[256,512]{1,0:T(8,128)(2,1)S(1)}, u32[]{:S(2)}, u32[]{:S(2)}) collective-permute-start(bf16[256,512]{1,0:T(8,128)(2,1)S(1)} %collective-permute-done.10.refs_2_), channel_id=1, source_target_pairs={{0,8},{1,9},{2,10},{3,11},{4,12},{5,13},{6,14},{7,15},{8,0},{9,1},... | collective-permute-start | bytes 786440 | tf_op jit(solution)/shard_map/ppermute | solution.py:359
  46.6 21.0 %slice-start = ((s8[6291456]{0:T(1024)(128)(4,1)}), s8[4194304]{0:T(1024)(128)(4,1)S(1)}, s32[]{:S(2)}) async-start(s8[6291456]{0:T(1024)(128)(4,1)} %bitcast.16), calls=%async_computation | async-start | bytes 8388608
  46.6 21.0 %copy-start.5 = (f32[1024]{0:T(1024)S(1)}, f32[1024]{0:T(1024)}, u32[]{:S(2)}) copy-start(f32[1024]{0:T(1024)} %param.15) | copy-start | bytes 12292
  47.7 19.9 %slice-start.1 = ((s8[6291456]{0:T(1024)(128)(4,1)}), s8[2097152]{0:T(1024)(128)(4,1)S(1)}, s32[]{:S(2)}) async-start(s8[6291456]{0:T(1024)(128)(4,1)} %bitcast.16), calls=%async_computation.1 | async-start | bytes 4194304
  49.9 34.9 %copy-start = (bf16[1,1536,1024]{2,1,0:T(8,128)(2,1)S(1)}, bf16[1,1536,1024]{2,1,0:T(8,128)(2,1)}, u32[]{:S(2)}) copy-start(bf16[1,1536,1024]{2,1,0:T(8,128)(2,1)} %param.19) | copy-start | bytes 9437188
  51.5 8.8 %collective-permute-start.15 = (bf16[32,1024]{1,0:T(8,128)(2,1)S(1)}, bf16[32,1024]{1,0:T(8,128)(2,1)S(1)}, u32[]{:S(2)}, u32[]{:S(2)}) collective-permute-start(bf16[32,1024]{1,0:T(8,128)(2,1)S(1)} %get-tuple-element.75), channel_id=1, source_target_pairs={{0,4},{1,5},{2,6},{3,7},{4,0},{5,1},{6,2},{7,3},{8,12},{9,13},{10,... | collective-permute-start | bytes 196616 | tf_op jit(solution)/shard_map/ppermute | solution.py:359
  52.1 11.3 %collective-permute-start.16 = (bf16[32,1024]{1,0:T(8,128)(2,1)S(1)}, bf16[32,1024]{1,0:T(8,128)(2,1)S(1)}, u32[]{:S(2)}, u32[]{:S(2)}) collective-permute-start(bf16[32,1024]{1,0:T(8,128)(2,1)S(1)} %get-tuple-element.76), channel_id=1, source_target_pairs={{0,5},{1,4},{2,7},{3,6},{4,1},{5,0},{6,3},{7,2},{8,13},{9,12},{10,... | collective-permute-start | bytes 196616 | tf_op jit(solution)/shard_map/ppermute | solution.py:359
  55.2 9.6 %collective-permute-start.17 = (bf16[32,1024]{1,0:T(8,128)(2,1)S(1)}, bf16[32,1024]{1,0:T(8,128)(2,1)S(1)}, u32[]{:S(2)}, u32[]{:S(2)}) collective-permute-start(bf16[32,1024]{1,0:T(8,128)(2,1)S(1)} %get-tuple-element.77), channel_id=1, source_target_pairs={{0,6},{1,7},{2,4},{3,5},{4,2},{5,3},{6,0},{7,1},{8,14},{9,15},{10,... | collective-permute-start | bytes 196616 | tf_op jit(solution)/shard_map/ppermute | solution.py:359
  57.7 7.1 %collective-permute-start.18 = (bf16[32,1024]{1,0:T(8,128)(2,1)S(1)}, bf16[32,1024]{1,0:T(8,128)(2,1)S(1)}, u32[]{:S(2)}, u32[]{:S(2)}) collective-permute-start(bf16[32,1024]{1,0:T(8,128)(2,1)S(1)} %get-tuple-element.78), channel_id=1, source_target_pairs={{0,7},{1,6},{2,5},{3,4},{4,3},{5,2},{6,1},{7,0},{8,15},{9,14},{10,... | collective-permute-start | bytes 196616 | tf_op jit(solution)/shard_map/ppermute | solution.py:359
  59.2 8.0 %collective-permute-start.20 = (bf16[32,1024]{1,0:T(8,128)(2,1)S(1)}, bf16[32,1024]{1,0:T(8,128)(2,1)S(1)}, u32[]{:S(2)}, u32[]{:S(2)}) collective-permute-start(bf16[32,1024]{1,0:T(8,128)(2,1)S(1)} %get-tuple-element.81), channel_id=1, source_target_pairs={{0,3},{1,2},{2,1},{3,0},{4,7},{5,6},{6,5},{7,4},{8,11},{9,10},{10,... | collective-permute-start | bytes 196616 | tf_op jit(solution)/shard_map/ppermute | solution.py:359
  60.3 6.9 %collective-permute-start.21 = (bf16[32,1024]{1,0:T(8,128)(2,1)S(1)}, bf16[32,1024]{1,0:T(8,128)(2,1)S(1)}, u32[]{:S(2)}, u32[]{:S(2)}) collective-permute-start(bf16[32,1024]{1,0:T(8,128)(2,1)S(1)} %get-tuple-element.82), channel_id=1, source_target_pairs={{0,2},{1,3},{2,0},{3,1},{4,6},{5,7},{6,4},{7,5},{8,10},{9,11},{10,... | collective-permute-start | bytes 196616 | tf_op jit(solution)/shard_map/ppermute | solution.py:359
  63.4 4.3 %collective-permute-start.22 = (bf16[32,1024]{1,0:T(8,128)(2,1)S(1)}, bf16[32,1024]{1,0:T(8,128)(2,1)S(1)}, u32[]{:S(2)}, u32[]{:S(2)}) collective-permute-start(bf16[32,1024]{1,0:T(8,128)(2,1)S(1)} %get-tuple-element.83), channel_id=1, source_target_pairs={{0,1},{1,0},{2,3},{3,2},{4,5},{5,4},{6,7},{7,6},{8,9},{9,8},{10,11... | collective-permute-start | bytes 196616 | tf_op jit(solution)/shard_map/ppermute | solution.py:359
  64.8 31.0 %collective-permute-start.19 = (bf16[256,1024]{1,0:T(8,128)(2,1)S(1)}, bf16[256,1024]{1,0:T(8,128)(2,1)S(1)}, u32[]{:S(2)}, u32[]{:S(2)}) collective-permute-start(bf16[256,1024]{1,0:T(8,128)(2,1)S(1)} %get-tuple-element.79), channel_id=1, source_target_pairs={{0,4},{1,5},{2,6},{3,7},{4,0},{5,1},{6,2},{7,3},{8,12},{9,13},{10,... | collective-permute-start | bytes 1572872 | tf_op jit(solution)/shard_map/ppermute | solution.py:359
  68.9 1.3 %collective-permute-start.23 = (bf16[16,3200]{1,0:T(8,128)(2,1)S(1)}, bf16[16,3200]{1,0:T(8,128)(2,1)S(1)}, u32[]{:S(2)}, u32[]{:S(2)}) collective-permute-start(bf16[16,3200]{1,0:T(8,128)(2,1)S(1)} %get-tuple-element.86), channel_id=1, source_target_pairs={{0,8},{1,9},{2,10},{3,11},{4,12},{5,13},{6,14},{7,15},{8,0},{9,1},... | collective-permute-start | bytes 307208 | tf_op jit(solution)/shard_map/ppermute | solution.py:359
  69.0 1.4 %collective-permute-start.24 = (bf16[16,3200]{1,0:T(8,128)(2,1)S(1)}, bf16[16,3200]{1,0:T(8,128)(2,1)S(1)}, u32[]{:S(2)}, u32[]{:S(2)}) collective-permute-start(bf16[16,3200]{1,0:T(8,128)(2,1)S(1)} %get-tuple-element.87), channel_id=1, source_target_pairs={{0,8},{1,9},{2,10},{3,11},{4,12},{5,13},{6,14},{7,15},{8,0},{9,1},... | collective-permute-start | bytes 307208 | tf_op jit(solution)/shard_map/ppermute | solution.py:359
  69.5 1.3 %collective-permute-start.25 = (bf16[16,3200]{1,0:T(8,128)(2,1)S(1)}, bf16[16,3200]{1,0:T(8,128)(2,1)S(1)}, u32[]{:S(2)}, u32[]{:S(2)}) collective-permute-start(bf16[16,3200]{1,0:T(8,128)(2,1)S(1)} %get-tuple-element.88), channel_id=1, source_target_pairs={{0,8},{1,9},{2,10},{3,11},{4,12},{5,13},{6,14},{7,15},{8,0},{9,1},... | collective-permute-start | bytes 307208 | tf_op jit(solution)/shard_map/ppermute | solution.py:359
  69.5 1.4 %collective-permute-start.26 = (bf16[16,3200]{1,0:T(8,128)(2,1)S(1)}, bf16[16,3200]{1,0:T(8,128)(2,1)S(1)}, u32[]{:S(2)}, u32[]{:S(2)}) collective-permute-start(bf16[16,3200]{1,0:T(8,128)(2,1)S(1)} %get-tuple-element.89), channel_id=1, source_target_pairs={{0,8},{1,9},{2,10},{3,11},{4,12},{5,13},{6,14},{7,15},{8,0},{9,1},... | collective-permute-start | bytes 307208 | tf_op jit(solution)/shard_map/ppermute | solution.py:359
  71.0 5.8 %collective-permute-start.27 = (bf16[16,3200]{1,0:T(8,128)(2,1)S(1)}, bf16[16,3200]{1,0:T(8,128)(2,1)S(1)}, u32[]{:S(2)}, u32[]{:S(2)}) collective-permute-start(bf16[16,3200]{1,0:T(8,128)(2,1)S(1)} %get-tuple-element.91), channel_id=1, source_target_pairs={{0,16},{1,17},{2,18},{3,19},{4,20},{5,21},{6,22},{7,23},{8,24},{9,... | collective-permute-start | bytes 307208 | tf_op jit(solution)/shard_map/ppermute | solution.py:359
  73.0 5.6 %collective-permute-start.28 = (bf16[16,3200]{1,0:T(8,128)(2,1)S(1)}, bf16[16,3200]{1,0:T(8,128)(2,1)S(1)}, u32[]{:S(2)}, u32[]{:S(2)}) collective-permute-start(bf16[16,3200]{1,0:T(8,128)(2,1)S(1)} %get-tuple-element.92), channel_id=1, source_target_pairs={{0,16},{1,17},{2,18},{3,19},{4,20},{5,21},{6,22},{7,23},{8,24},{9,... | collective-permute-start | bytes 307208 | tf_op jit(solution)/shard_map/ppermute | solution.py:359
  78.8 4.7 %collective-permute-start.30 = (bf16[32,1536]{1,0:T(8,128)(2,1)S(1)}, bf16[32,1536]{1,0:T(8,128)(2,1)S(1)}, u32[]{:S(2)}, u32[]{:S(2)}) collective-permute-start(bf16[32,1536]{1,0:T(8,128)(2,1)S(1)} %shard_map.111.refs_0_), channel_id=1, source_target_pairs={{0,16},{1,17},{2,18},{3,19},{4,20},{5,21},{6,22},{7,23},{8,24},{9,... | collective-permute-start | bytes 294920 | tf_op jit(solution)/shard_map/ppermute | solution.py:359
  80.6 2.9 %collective-permute-start.29 = (bf16[32,1536]{1,0:T(8,128)(2,1)S(1)}, bf16[32,1536]{1,0:T(8,128)(2,1)S(1)}, u32[]{:S(2)}, u32[]{:S(2)}) collective-permute-start(bf16[32,1536]{1,0:T(8,128)(2,1)S(1)} %shard_map.111.refs_0_), channel_id=1, source_target_pairs={{0,8},{1,9},{2,10},{3,11},{4,12},{5,13},{6,14},{7,15},{8,0},{9,1},... | collective-permute-start | bytes 294920 | tf_op jit(solution)/shard_map/ppermute | solution.py:359
  83.4 1.3 %collective-permute-start.31 = (bf16[32,1536]{1,0:T(8,128)(2,1)S(1)}, bf16[32,1536]{1,0:T(8,128)(2,1)S(1)}, u32[]{:S(2)}, u32[]{:S(2)}) collective-permute-start(bf16[32,1536]{1,0:T(8,128)(2,1)S(1)} %collective-permute-done.30.refs_2_), channel_id=1, source_target_pairs={{0,8},{1,9},{2,10},{3,11},{4,12},{5,13},{6,14},{7,15},{8,0},{9,1},... | collective-permute-start | bytes 294920 | tf_op jit(solution)/shard_map/ppermute | solution.py:359
  85.4 7.7 %collective-permute-start.32 = (bf16[16,1024]{1,0:T(8,128)(2,1)S(1)}, bf16[16,1024]{1,0:T(8,128)(2,1)S(1)}, u32[]{:S(2)}, u32[]{:S(2)}) collective-permute-start(bf16[16,1024]{1,0:T(8,128)(2,1)S(1)} %get-tuple-element.93), channel_id=1, source_target_pairs={{0,4},{1,5},{2,6},{3,7},{4,0},{5,1},{6,2},{7,3},{8,12},{9,13},{10,... | collective-permute-start | bytes 98312 | tf_op jit(solution)/shard_map/ppermute | solution.py:359
  86.2 7.9 %collective-permute-start.33 = (bf16[16,1024]{1,0:T(8,128)(2,1)S(1)}, bf16[16,1024]{1,0:T(8,128)(2,1)S(1)}, u32[]{:S(2)}, u32[]{:S(2)}) collective-permute-start(bf16[16,1024]{1,0:T(8,128)(2,1)S(1)} %get-tuple-element.94), channel_id=1, source_target_pairs={{0,5},{1,4},{2,7},{3,6},{4,1},{5,0},{6,3},{7,2},{8,13},{9,12},{10,... | collective-permute-start | bytes 98312 | tf_op jit(solution)/shard_map/ppermute | solution.py:359
  89.1 7.7 %collective-permute-start.34 = (bf16[16,1024]{1,0:T(8,128)(2,1)S(1)}, bf16[16,1024]{1,0:T(8,128)(2,1)S(1)}, u32[]{:S(2)}, u32[]{:S(2)}) collective-permute-start(bf16[16,1024]{1,0:T(8,128)(2,1)S(1)} %get-tuple-element.95), channel_id=1, source_target_pairs={{0,6},{1,7},{2,4},{3,5},{4,2},{5,3},{6,0},{7,1},{8,14},{9,15},{10,... | collective-permute-start | bytes 98312 | tf_op jit(solution)/shard_map/ppermute | solution.py:359
  91.5 6.7 %collective-permute-start.35 = (bf16[16,1024]{1,0:T(8,128)(2,1)S(1)}, bf16[16,1024]{1,0:T(8,128)(2,1)S(1)}, u32[]{:S(2)}, u32[]{:S(2)}) collective-permute-start(bf16[16,1024]{1,0:T(8,128)(2,1)S(1)} %get-tuple-element.96), channel_id=1, source_target_pairs={{0,7},{1,6},{2,5},{3,4},{4,3},{5,2},{6,1},{7,0},{8,15},{9,14},{10,... | collective-permute-start | bytes 98312 | tf_op jit(solution)/shard_map/ppermute | solution.py:359
  93.1 5.2 %collective-permute-start.36 = (bf16[16,1024]{1,0:T(8,128)(2,1)S(1)}, bf16[16,1024]{1,0:T(8,128)(2,1)S(1)}, u32[]{:S(2)}, u32[]{:S(2)}) collective-permute-start(bf16[16,1024]{1,0:T(8,128)(2,1)S(1)} %get-tuple-element.97), channel_id=1, source_target_pairs={{0,3},{1,2},{2,1},{3,0},{4,7},{5,6},{6,5},{7,4},{8,11},{9,10},{10,... | collective-permute-start | bytes 98312 | tf_op jit(solution)/shard_map/ppermute | solution.py:359
  94.1 4.2 %collective-permute-start.37 = (bf16[16,1024]{1,0:T(8,128)(2,1)S(1)}, bf16[16,1024]{1,0:T(8,128)(2,1)S(1)}, u32[]{:S(2)}, u32[]{:S(2)}) collective-permute-start(bf16[16,1024]{1,0:T(8,128)(2,1)S(1)} %get-tuple-element.98), channel_id=1, source_target_pairs={{0,2},{1,3},{2,0},{3,1},{4,6},{5,7},{6,4},{7,5},{8,10},{9,11},{10,... | collective-permute-start | bytes 98312 | tf_op jit(solution)/shard_map/ppermute | solution.py:359
  95.9 3.9 %collective-permute-start.38 = (bf16[16,1024]{1,0:T(8,128)(2,1)S(1)}, bf16[16,1024]{1,0:T(8,128)(2,1)S(1)}, u32[]{:S(2)}, u32[]{:S(2)}) collective-permute-start(bf16[16,1024]{1,0:T(8,128)(2,1)S(1)} %get-tuple-element.99), channel_id=1, source_target_pairs={{0,1},{1,0},{2,3},{3,2},{4,5},{5,4},{6,7},{7,6},{8,9},{9,8},{10,11... | collective-permute-start | bytes 98312 | tf_op jit(solution)/shard_map/ppermute | solution.py:359

commit v22 on v21

--- a/solution.py
+++ b/solution.py
@@ -462,7 +462,7 @@
         cost=(0, 2**14),
     )(acc, acc_far, last, last_far, *shards[C - 1], place, other_place)
     incoming = [permute(x, exp=b) if b else x for x, b in zip(outgoing, all_hops(E))]
-    arrived = permute(after(full, *incoming[: E // 2]), exp=PAIR)
+    arrived = permute(after(full, *incoming[: E // 2 - 1]), exp=PAIR)
 
     order = [0]
     bit = C // 2

time: 101 us -> 110 us (1.089)
  starting transfers between devices: 46.3 us -> 53.9 us
    ppermute x39, starting transfers between devices: 46.3 us -> 53.9 us  [permute(): return lax.ppermute(x, ('ctx', 'exp'), pairs)]
  transfers between devices with their start and end apart: 39 -> 39, of which waited for: 23 -> 23; matrix products, arithmetic and copies ran while one was open for 0% -> 0% of each run, Pallas kernels for 11% -> 10%
where the time goes in v22:
time: 110 us; the launch traced here: 109 us
  starting transfers between devices  53.9 us (49%)
  waiting for transfers between devices  37.5 us (34%)
  Pallas kernels  13.8 us (13%)
  local copies, waits for them, and re-layouts  3.82 us (3%)
    ppermute x39, starting transfers between devices, permute(): return lax.ppermute(x, ('ctx', 'exp'), pairs)  53.9 us
    ppermute x39, waiting for transfers between devices, permute(): return lax.ppermute(x, ('ctx', 'exp'), pairs)  37.5 us
    pallas_call x2, Pallas kernels, attend(): call(functools.partial(attend_kernel, C, t), [sds((rows, qw), BF16)] + [s...  4.63 us
    unnamed x16, local copies, waits for them, and re-layouts  3.72 us
  transfers between devices with their start and end apart: 39, of which 23 were waited for; matrix products, arithmetic and copies ran while one was open for 0% of the time, Pallas kernels for 10%

profile of v22, /device:TPU:0, one launch (start us, length us, event | category | flops | bytes accessed | tf_op | source)
XLA Modules:
  0.0 109.2 jit_solution(321946412762070360)
XLA Ops:
  0.0 3.0 %collective-permute-start.7 = (bf16[512,1024]{1,0:T(8,128)(2,1)}, bf16[512,1024]{1,0:T(8,128)(2,1)S(1)}, u32[]{:S(2)}, u32[]{:S(2)}) collective-permute-start(bf16[512,1024]{1,0:T(8,128)(2,1)} %refs_0_.1), channel_id=1, source_target_pairs={{0,2},{1,3},{2,0},{3,1},{4,6},{5,7},{6,4},{7,5},{8,10},{9,11},{10,... | collective-permute-start | bytes 3145736 | tf_op jit(solution)/shard_map/ppermute | solution.py:359
  3.0 1.5 %collective-permute-start.6 = (bf16[512,1024]{1,0:T(8,128)(2,1)}, bf16[512,1024]{1,0:T(8,128)(2,1)S(1)}, u32[]{:S(2)}, u32[]{:S(2)}) collective-permute-start(bf16[512,1024]{1,0:T(8,128)(2,1)} %refs_0_.1), channel_id=1, source_target_pairs={{0,1},{1,0},{2,3},{3,2},{4,5},{5,4},{6,7},{7,6},{8,9},{9,8},{10,11... | collective-permute-start | bytes 3145736 | tf_op jit(solution)/shard_map/ppermute | solution.py:359
  4.5 1.4 %shard_map.100 = (bf16[64,2048]{1,0:T(8,128)(2,1)S(1)}, bf16[64,2048]{1,0:T(8,128)(2,1)S(1)}, bf16[64,2048]{1,0:T(8,128)(2,1)S(1)}, bf16[64,2048]{1,0:T(8,128)(2,1)S(1)}) custom-call(bf16[64,4096]{1,0:T(8,128)(2,1)} %bitcast.25, bf16[64,512]{1,0:T(8,128)(2,1)} %bitcast.26, bf16[64,512]{1,0:T(8,128)(2,1)} %bitcast.27), custom_call_target="tpu_custom_call" | custom-call | bytes 1048576 | tf_op jit(solution)/shard_map/pallas_call | solution.py:365
  6.0 1.6 %collective-permute-start = (bf16[64,2048]{1,0:T(8,128)(2,1)S(1)}, bf16[64,2048]{1,0:T(8,128)(2,1)S(1)}, u32[]{:S(2)}, u32[]{:S(2)}) collective-permute-start(bf16[64,2048]{1,0:T(8,128)(2,1)S(1)} %get-tuple-element.53), channel_id=1, source_target_pairs={{0,16},{1,17},{2,18},{3,19},{4,20},{5,21},{6,22},{7,23},{8,24},{9,... | collective-permute-start | bytes 786440 | tf_op jit(solution)/shard_map/ppermute | solution.py:359
  8.2 7.1 %collective-permute-done.refs_0_ = bf16[64,2048]{1,0:T(8,128)(2,1)S(1)} collective-permute-done((bf16[64,2048]{1,0:T(8,128)(2,1)S(1)}, bf16[64,2048]{1,0:T(8,128)(2,1)S(1)}, u32[]{:S(2)}, u32[]{:S(2)}) %collective-permute-start) | collective-permute-done | bytes 262176 | tf_op jit(solution)/shard_map/ppermute | solution.py:359
  15.3 2.9 %collective-permute-done.1.refs_1_ = bf16[64,2048]{1,0:T(8,128)(2,1)S(1)} collective-permute-done((bf16[64,2048]{1,0:T(8,128)(2,1)S(1)}, bf16[64,2048]{1,0:T(8,128)(2,1)S(1)}, u32[]{:S(2)}, u32[]{:S(2)}) %collective-permute-start.1) | collective-permute-done | bytes 262176 | tf_op jit(solution)/shard_map/ppermute | solution.py:359
  18.2 2.3 %shard_map.101 = (bf16[256,512]{1,0:T(8,128)(2,1)S(1)}, bf16[64,2048]{1,0:T(8,128)(2,1)S(1)}) custom-call(bf16[64,2048]{1,0:T(8,128)(2,1)S(1)} %collective-permute-done.refs_0_, bf16[64,2048]{1,0:T(8,128)(2,1)S(1)} %collective-permute-done.1.refs_1_, bf16[64,2048]{1,0:T(8,128)(2,1)S(1)} %collective-permute-done.2.refs_2_, ...), custom_call_target="tpu_custom_call" | custom-call | bytes 16384 | tf_op jit(solution)/shard_map/pallas_call | solution.py:386
  20.5 2.7 %collective-permute-start.8 = (bf16[256,512]{1,0:T(8,128)(2,1)S(1)}, bf16[256,512]{1,0:T(8,128)(2,1)S(1)}, u32[]{:S(2)}, u32[]{:S(2)}) collective-permute-start(bf16[256,512]{1,0:T(8,128)(2,1)S(1)} %get-tuple-element.57), channel_id=1, source_target_pairs={{0,4},{1,5},{2,6},{3,7},{4,0},{5,1},{6,2},{7,3},{8,12},{9,13},{10,... | collective-permute-start | bytes 786440 | tf_op jit(solution)/shard_map/ppermute | solution.py:359
  23.2 2.3 %shard_map.102.refs_1_ = bf16[256,512]{1,0:T(8,128)(2,1)S(1)} custom-call(bf16[64,2048]{1,0:T(8,128)(2,1)S(1)} %collective-permute-done.refs_0_, bf16[64,2048]{1,0:T(8,128)(2,1)S(1)} %collective-permute-done.1.refs_1_, bf16[64,2048]{1,0:T(8,128)(2,1)S(1)} %collective-permute-done.2.refs_2_, bf16[64,2048]{1,0:T(8,128)(2,1)S(1)} %get-tuple-element.59.refs_3_), custom_call_target="tpu_custom_call" | custom-call | bytes 16384 | tf_op jit(solution)/shard_map/pallas_call | solution.py:386
  25.5 1.2 %copy-done.1 = bf16[512,1024]{1,0:T(8,128)(2,1)S(1)} copy-done((bf16[512,1024]{1,0:T(8,128)(2,1)S(1)}, bf16[512,1024]{1,0:T(8,128)(2,1)}, u32[]{:S(2)}) %copy-start.1) | copy-done | bytes 1048600
  26.7 1.0 copy-done.2
  27.7 0.7 copy-done.3
  30.1 2.7 %collective-permute-start.13 = (bf16[512,768]{1,0:T(8,128)(2,1)S(1)}, bf16[512,768]{1,0:T(8,128)(2,1)S(1)}, u32[]{:S(2)}, u32[]{:S(2)}) collective-permute-start(bf16[512,768]{1,0:T(8,128)(2,1)S(1)} %slice.7), channel_id=1, source_target_pairs={{0,1},{1,0},{2,3},{3,2},{4,5},{5,4},{6,7},{7,6},{8,9},{9,8},{10,11... | collective-permute-start | bytes 2359304 | tf_op jit(solution)/shard_map/ppermute | solution.py:359
  32.8 2.3 %collective-permute-start.4 = (bf16[256,512]{1,0:T(8,128)(2,1)S(1)}, bf16[256,512]{1,0:T(8,128)(2,1)S(1)}, u32[]{:S(2)}, u32[]{:S(2)}) collective-permute-start(bf16[256,512]{1,0:T(8,128)(2,1)S(1)} %shard_map.102.refs_1_), channel_id=1, source_target_pairs={{0,16},{1,17},{2,18},{3,19},{4,20},{5,21},{6,22},{7,23},{8,24},{9,... | collective-permute-start | bytes 786440 | tf_op jit(solution)/shard_map/ppermute | solution.py:359
  35.1 1.1 %collective-permute-done.8.refs_0_ = bf16[256,512]{1,0:T(8,128)(2,1)S(1)} collective-permute-done((bf16[256,512]{1,0:T(8,128)(2,1)S(1)}, bf16[256,512]{1,0:T(8,128)(2,1)S(1)}, u32[]{:S(2)}, u32[]{:S(2)}) %collective-permute-start.8) | collective-permute-done | bytes 262176 | tf_op jit(solution)/shard_map/ppermute | solution.py:359
  36.5 2.9 %collective-permute-start.14 = (s32[4,8,64]{2,1,0:T(8,128)S(1)}, s32[4,8,64]{2,1,0:T(8,128)S(1)}, u32[]{:S(2)}, u32[]{:S(2)}) collective-permute-start(s32[4,8,64]{2,1,0:T(8,128)S(1)} %bitcast.23), channel_id=1, source_target_pairs={{0,4},{1,5},{2,6},{3,7},{4,0},{5,1},{6,2},{7,3},{8,12},{9,13},{10,... | collective-permute-start | bytes 24584 | tf_op jit(solution)/shard_map/ppermute | solution.py:359
  39.4 2.5 %collective-permute-done.4.refs_3_ = bf16[256,512]{1,0:T(8,128)(2,1)S(1)} collective-permute-done((bf16[256,512]{1,0:T(8,128)(2,1)S(1)}, bf16[256,512]{1,0:T(8,128)(2,1)S(1)}, u32[]{:S(2)}, u32[]{:S(2)}) %collective-permute-start.4) | collective-permute-done | bytes 262176 | tf_op jit(solution)/shard_map/ppermute | solution.py:359
  41.8 3.2 %collective-permute-done.11.refs_5_ = bf16[512,256]{1,0:T(8,128)(2,1)S(1)} collective-permute-done((bf16[512,256]{1,0:T(8,128)(2,1)S(1)}, bf16[512,256]{1,0:T(8,128)(2,1)S(1)}, u32[]{:S(2)}, u32[]{:S(2)}) %collective-permute-start.11) | collective-permute-done | bytes 262176 | tf_op jit(solution)/shard_map/ppermute | solution.py:359
  45.0 0.8 collective-permute-done.10.refs_2_
  46.6 1.1 shard_map.104
  47.8 1.1 shard_map.105
  48.8 1.1 collective-permute-done.13.refs_4_
  49.9 1.6 %shard_map.107 = (f32[256,1024]{1,0:T(8,128)S(1)}, bf16[256,1024]{1,0:T(8,128)(2,1)S(1)}, bf16[32,1024]{1,0:T(8,128)(2,1)S(1)}, bf16[32,1024]{1,0:T(8,128)(2,1)S...) custom-call(f32[256,1024]{1,0:T(8,128)S(1)} %get-tuple-element.63.re, ...), custom_call_target="tpu_custom_call" | custom-call | bytes 16384 | tf_op jit(solution)/shard_map/pallas_call | solution.py:454
  52.1 3.1 %collective-permute-start.16 = (bf16[32,1024]{1,0:T(8,128)(2,1)S(1)}, bf16[32,1024]{1,0:T(8,128)(2,1)S(1)}, u32[]{:S(2)}, u32[]{:S(2)}) collective-permute-start(bf16[32,1024]{1,0:T(8,128)(2,1)S(1)} %get-tuple-element.76), channel_id=1, source_target_pairs={{0,5},{1,4},{2,7},{3,6},{4,1},{5,0},{6,3},{7,2},{8,13},{9,12},{10,... | collective-permute-start | bytes 196616 | tf_op jit(solution)/shard_map/ppermute | solution.py:359
  55.2 2.5 %collective-permute-start.17 = (bf16[32,1024]{1,0:T(8,128)(2,1)S(1)}, bf16[32,1024]{1,0:T(8,128)(2,1)S(1)}, u32[]{:S(2)}, u32[]{:S(2)}) collective-permute-start(bf16[32,1024]{1,0:T(8,128)(2,1)S(1)} %get-tuple-element.77), channel_id=1, source_target_pairs={{0,6},{1,7},{2,4},{3,5},{4,2},{5,3},{6,0},{7,1},{8,14},{9,15},{10,... | collective-permute-start | bytes 196616 | tf_op jit(solution)/shard_map/ppermute | solution.py:359
  57.7 1.5 %collective-permute-start.19 = (bf16[32,1024]{1,0:T(8,128)(2,1)S(1)}, bf16[32,1024]{1,0:T(8,128)(2,1)S(1)}, u32[]{:S(2)}, u32[]{:S(2)}) collective-permute-start(bf16[32,1024]{1,0:T(8,128)(2,1)S(1)} %get-tuple-element.80), channel_id=1, source_target_pairs={{0,7},{1,6},{2,5},{3,4},{4,3},{5,2},{6,1},{7,0},{8,15},{9,14},{10,... | collective-permute-start | bytes 196616 | tf_op jit(solution)/shard_map/ppermute | solution.py:359
  59.2 1.1 collective-permute-done.15.refs_0_
  60.3 1.7 %collective-permute-start.21 = (bf16[32,1024]{1,0:T(8,128)(2,1)S(1)}, bf16[32,1024]{1,0:T(8,128)(2,1)S(1)}, u32[]{:S(2)}, u32[]{:S(2)}) collective-permute-start(bf16[32,1024]{1,0:T(8,128)(2,1)S(1)} %get-tuple-element.82), channel_id=1, source_target_pairs={{0,2},{1,3},{2,0},{3,1},{4,6},{5,7},{6,4},{7,5},{8,10},{9,11},{10,... | collective-permute-start | bytes 196616 | tf_op jit(solution)/shard_map/ppermute | solution.py:359
  62.0 1.4 %collective-permute-done.16.refs_1_ = bf16[32,1024]{1,0:T(8,128)(2,1)S(1)} collective-permute-done((bf16[32,1024]{1,0:T(8,128)(2,1)S(1)}, bf16[32,1024]{1,0:T(8,128)(2,1)S(1)}, u32[]{:S(2)}, u32[]{:S(2)}) %collective-permute-start.16) | collective-permute-done | bytes 65568 | tf_op jit(solution)/shard_map/ppermute | solution.py:359
  63.4 1.4 %collective-permute-start.22 = (bf16[32,1024]{1,0:T(8,128)(2,1)S(1)}, bf16[32,1024]{1,0:T(8,128)(2,1)S(1)}, u32[]{:S(2)}, u32[]{:S(2)}) collective-permute-start(bf16[32,1024]{1,0:T(8,128)(2,1)S(1)} %get-tuple-element.83), channel_id=1, source_target_pairs={{0,1},{1,0},{2,3},{3,2},{4,5},{5,4},{6,7},{7,6},{8,9},{9,8},{10,11... | collective-permute-start | bytes 196616 | tf_op jit(solution)/shard_map/ppermute | solution.py:359
  64.8 0.9 collective-permute-start.18
  65.8 1.9 %collective-permute-done.22.refs_6_ = bf16[32,1024]{1,0:T(8,128)(2,1)S(1)} collective-permute-done((bf16[32,1024]{1,0:T(8,128)(2,1)S(1)}, bf16[32,1024]{1,0:T(8,128)(2,1)S(1)}, u32[]{:S(2)}, u32[]{:S(2)}) %collective-permute-start.22) | collective-permute-done | bytes 65568 | tf_op jit(solution)/shard_map/ppermute | solution.py:359
  67.7 1.3 %shard_map.109 = (f32[64,3200]{1,0:T(8,128)S(1)}, bf16[16,3200]{1,0:T(8,128)(2,1)S(1)}, bf16[16,3200]{1,0:T(8,128)(2,1)S(1)}, bf16[16,3200]{1,0:T(8,128)(2,1)S(1)}, bf16[16,3200]{1,0:T(8,128)(2,1)S(1)}) custom-call(bf16[32,1024]{1,0:T(8,128)(2,1)S(1)} %collective-permute-done.15.refs_0_, bf16[32,1024]{1,0:T(8,128)(2,1)S(1)} %collective-permute-done.16.refs_1_, ...), custom_call_target="tpu_custom_call" | custom-call | bytes 1024 | tf_op jit(solution)/shard_map/pallas_call | solution.py:472
  71.0 2.3 %collective-permute-start.27 = (bf16[16,3200]{1,0:T(8,128)(2,1)S(1)}, bf16[16,3200]{1,0:T(8,128)(2,1)S(1)}, u32[]{:S(2)}, u32[]{:S(2)}) collective-permute-start(bf16[16,3200]{1,0:T(8,128)(2,1)S(1)} %get-tuple-element.91), channel_id=1, source_target_pairs={{0,16},{1,17},{2,18},{3,19},{4,20},{5,21},{6,22},{7,23},{8,24},{9,... | collective-permute-start | bytes 307208 | tf_op jit(solution)/shard_map/ppermute | solution.py:359
  73.4 3.6 %collective-permute-done.27.refs_0_ = bf16[16,3200]{1,0:T(8,128)(2,1)S(1)} collective-permute-done((bf16[16,3200]{1,0:T(8,128)(2,1)S(1)}, bf16[16,3200]{1,0:T(8,128)(2,1)S(1)}, u32[]{:S(2)}, u32[]{:S(2)}) %collective-permute-start.27) | collective-permute-done | bytes 102432 | tf_op jit(solution)/shard_map/ppermute | solution.py:359
  77.0 1.9 %collective-permute-done.28.refs_1_ = bf16[16,3200]{1,0:T(8,128)(2,1)S(1)} collective-permute-done((bf16[16,3200]{1,0:T(8,128)(2,1)S(1)}, bf16[16,3200]{1,0:T(8,128)(2,1)S(1)}, u32[]{:S(2)}, u32[]{:S(2)}) %collective-permute-start.28) | collective-permute-done | bytes 102432 | tf_op jit(solution)/shard_map/ppermute | solution.py:359
  79.1 1.8 %collective-permute-start.30 = (bf16[32,1536]{1,0:T(8,128)(2,1)S(1)}, bf16[32,1536]{1,0:T(8,128)(2,1)S(1)}, u32[]{:S(2)}, u32[]{:S(2)}) collective-permute-start(bf16[32,1536]{1,0:T(8,128)(2,1)S(1)} %shard_map.111.refs_0_), channel_id=1, source_target_pairs={{0,16},{1,17},{2,18},{3,19},{4,20},{5,21},{6,22},{7,23},{8,24},{9,... | collective-permute-start | bytes 294920 | tf_op jit(solution)/shard_map/ppermute | solution.py:359
  80.9 2.9 %collective-permute-done.30.refs_2_ = bf16[32,1536]{1,0:T(8,128)(2,1)S(1)} collective-permute-done((bf16[32,1536]{1,0:T(8,128)(2,1)S(1)}, bf16[32,1536]{1,0:T(8,128)(2,1)S(1)}, u32[]{:S(2)}, u32[]{:S(2)}) %collective-permute-start.30) | collective-permute-done | bytes 98336 | tf_op jit(solution)/shard_map/ppermute | solution.py:359
  83.8 1.3 %collective-permute-done.31.refs_3_ = bf16[32,1536]{1,0:T(8,128)(2,1)S(1)} collective-permute-done((bf16[32,1536]{1,0:T(8,128)(2,1)S(1)}, bf16[32,1536]{1,0:T(8,128)(2,1)S(1)}, u32[]{:S(2)}, u32[]{:S(2)}) %collective-permute-start.31) | collective-permute-done | bytes 98336 | tf_op jit(solution)/shard_map/ppermute | solution.py:359
  85.7 10.5 %collective-permute-start.32 = (bf16[16,1024]{1,0:T(8,128)(2,1)S(1)}, bf16[16,1024]{1,0:T(8,128)(2,1)S(1)}, u32[]{:S(2)}, u32[]{:S(2)}) collective-permute-start(bf16[16,1024]{1,0:T(8,128)(2,1)S(1)} %get-tuple-element.93), channel_id=1, source_target_pairs={{0,4},{1,5},{2,6},{3,7},{4,0},{5,1},{6,2},{7,3},{8,12},{9,13},{10,... | collective-permute-start | bytes 98312 | tf_op jit(solution)/shard_map/ppermute | solution.py:359
  96.2 1.2 %collective-permute-start.33 = (bf16[16,1024]{1,0:T(8,128)(2,1)S(1)}, bf16[16,1024]{1,0:T(8,128)(2,1)S(1)}, u32[]{:S(2)}, u32[]{:S(2)}) collective-permute-start(bf16[16,1024]{1,0:T(8,128)(2,1)S(1)} %get-tuple-element.94), channel_id=1, source_target_pairs={{0,5},{1,4},{2,7},{3,6},{4,1},{5,0},{6,3},{7,2},{8,13},{9,12},{10,... | collective-permute-start | bytes 98312 | tf_op jit(solution)/shard_map/ppermute | solution.py:359
  97.4 1.9 %collective-permute-start.34 = (bf16[16,1024]{1,0:T(8,128)(2,1)S(1)}, bf16[16,1024]{1,0:T(8,128)(2,1)S(1)}, u32[]{:S(2)}, u32[]{:S(2)}) collective-permute-start(bf16[16,1024]{1,0:T(8,128)(2,1)S(1)} %get-tuple-element.95), channel_id=1, source_target_pairs={{0,6},{1,7},{2,4},{3,5},{4,2},{5,3},{6,0},{7,1},{8,14},{9,15},{10,... | collective-permute-start | bytes 98312 | tf_op jit(solution)/shard_map/ppermute | solution.py:359
  99.3 1.9 %collective-permute-start.35 = (bf16[16,1024]{1,0:T(8,128)(2,1)S(1)}, bf16[16,1024]{1,0:T(8,128)(2,1)S(1)}, u32[]{:S(2)}, u32[]{:S(2)}) collective-permute-start(bf16[16,1024]{1,0:T(8,128)(2,1)S(1)} %get-tuple-element.96), channel_id=1, source_target_pairs={{0,7},{1,6},{2,5},{3,4},{4,3},{5,2},{6,1},{7,0},{8,15},{9,14},{10,... | collective-permute-start | bytes 98312 | tf_op jit(solution)/shard_map/ppermute | solution.py:359
  101.2 1.5 %collective-permute-start.36 = (bf16[16,1024]{1,0:T(8,128)(2,1)S(1)}, bf16[16,1024]{1,0:T(8,128)(2,1)S(1)}, u32[]{:S(2)}, u32[]{:S(2)}) collective-permute-start(bf16[16,1024]{1,0:T(8,128)(2,1)S(1)} %get-tuple-element.97), channel_id=1, source_target_pairs={{0,3},{1,2},{2,1},{3,0},{4,7},{5,6},{6,5},{7,4},{8,11},{9,10},{10,... | collective-permute-start | bytes 98312 | tf_op jit(solution)/shard_map/ppermute | solution.py:359
  102.7 1.5 %collective-permute-start.37 = (bf16[16,1024]{1,0:T(8,128)(2,1)S(1)}, bf16[16,1024]{1,0:T(8,128)(2,1)S(1)}, u32[]{:S(2)}, u32[]{:S(2)}) collective-permute-start(bf16[16,1024]{1,0:T(8,128)(2,1)S(1)} %get-tuple-element.98), channel_id=1, source_target_pairs={{0,2},{1,3},{2,0},{3,1},{4,6},{5,7},{6,4},{7,5},{8,10},{9,11},{10,... | collective-permute-start | bytes 98312 | tf_op jit(solution)/shard_map/ppermute | solution.py:359
  104.8 1.2 %collective-permute-done.35.refs_3_ = bf16[16,1024]{1,0:T(8,128)(2,1)S(1)} collective-permute-done((bf16[16,1024]{1,0:T(8,128)(2,1)S(1)}, bf16[16,1024]{1,0:T(8,128)(2,1)S(1)}, u32[]{:S(2)}, u32[]{:S(2)}) %collective-permute-start.35) | collective-permute-done | bytes 32800 | tf_op jit(solution)/shard_map/ppermute | solution.py:359
  106.6 1.5 %collective-permute-done.38.refs_6_ = bf16[16,1024]{1,0:T(8,128)(2,1)S(1)} collective-permute-done((bf16[16,1024]{1,0:T(8,128)(2,1)S(1)}, bf16[16,1024]{1,0:T(8,128)(2,1)S(1)}, u32[]{:S(2)}, u32[]{:S(2)}) %collective-permute-start.38) | collective-permute-done | bytes 32800 | tf_op jit(solution)/shard_map/ppermute | solution.py:359
  108.1 1.1 shard_map.113
  (63 shorter events, 8.1 us)
Async XLA Ops:
  0.0 30.0 %collective-permute-start.7 = (bf16[512,1024]{1,0:T(8,128)(2,1)}, bf16[512,1024]{1,0:T(8,128)(2,1)S(1)}, u32[]{:S(2)}, u32[]{:S(2)}) collective-permute-start(bf16[512,1024]{1,0:T(8,128)(2,1)} %refs_0_.1), channel_id=1, source_target_pairs={{0,2},{1,3},{2,0},{3,1},{4,6},{5,7},{6,4},{7,5},{8,10},{9,11},{10,... | collective-permute-start | bytes 3145736 | tf_op jit(solution)/shard_map/ppermute | solution.py:359
  3.0 32.0 %collective-permute-start.6 = (bf16[512,1024]{1,0:T(8,128)(2,1)}, bf16[512,1024]{1,0:T(8,128)(2,1)S(1)}, u32[]{:S(2)}, u32[]{:S(2)}) collective-permute-start(bf16[512,1024]{1,0:T(8,128)(2,1)} %refs_0_.1), channel_id=1, source_target_pairs={{0,1},{1,0},{2,3},{3,2},{4,5},{5,4},{6,7},{7,6},{8,9},{9,8},{10,11... | collective-permute-start | bytes 3145736 | tf_op jit(solution)/shard_map/ppermute | solution.py:359
  6.0 9.3 %collective-permute-start = (bf16[64,2048]{1,0:T(8,128)(2,1)S(1)}, bf16[64,2048]{1,0:T(8,128)(2,1)S(1)}, u32[]{:S(2)}, u32[]{:S(2)}) collective-permute-start(bf16[64,2048]{1,0:T(8,128)(2,1)S(1)} %get-tuple-element.53), channel_id=1, source_target_pairs={{0,16},{1,17},{2,18},{3,19},{4,20},{5,21},{6,22},{7,23},{8,24},{9,... | collective-permute-start | bytes 786440 | tf_op jit(solution)/shard_map/ppermute | solution.py:359
  7.6 10.6 %collective-permute-start.1 = (bf16[64,2048]{1,0:T(8,128)(2,1)S(1)}, bf16[64,2048]{1,0:T(8,128)(2,1)S(1)}, u32[]{:S(2)}, u32[]{:S(2)}) collective-permute-start(bf16[64,2048]{1,0:T(8,128)(2,1)S(1)} %get-tuple-element.54), channel_id=1, source_target_pairs={{0,24},{1,25},{2,26},{3,27},{4,28},{5,29},{6,30},{7,31},{8,16},{9,... | collective-permute-start | bytes 786440 | tf_op jit(solution)/shard_map/ppermute | solution.py:359
  7.6 10.6 %collective-permute-start.2 = (bf16[64,2048]{1,0:T(8,128)(2,1)S(1)}, bf16[64,2048]{1,0:T(8,128)(2,1)S(1)}, u32[]{:S(2)}, u32[]{:S(2)}) collective-permute-start(bf16[64,2048]{1,0:T(8,128)(2,1)S(1)} %get-tuple-element.55), channel_id=1, source_target_pairs={{0,8},{1,9},{2,10},{3,11},{4,12},{5,13},{6,14},{7,15},{8,0},{9,1},... | collective-permute-start | bytes 786440 | tf_op jit(solution)/shard_map/ppermute | solution.py:359
  20.5 15.7 %collective-permute-start.8 = (bf16[256,512]{1,0:T(8,128)(2,1)S(1)}, bf16[256,512]{1,0:T(8,128)(2,1)S(1)}, u32[]{:S(2)}, u32[]{:S(2)}) collective-permute-start(bf16[256,512]{1,0:T(8,128)(2,1)S(1)} %get-tuple-element.57), channel_id=1, source_target_pairs={{0,4},{1,5},{2,6},{3,7},{4,0},{5,1},{6,2},{7,3},{8,12},{9,13},{10,... | collective-permute-start | bytes 786440 | tf_op jit(solution)/shard_map/ppermute | solution.py:359
  25.5 1.2 %copy-start.1 = (bf16[512,1024]{1,0:T(8,128)(2,1)S(1)}, bf16[512,1024]{1,0:T(8,128)(2,1)}, u32[]{:S(2)}) copy-start(bf16[512,1024]{1,0:T(8,128)(2,1)} %refs_0_.1) | copy-start | bytes 3145732
  26.7 1.0 copy-start.2
  27.7 0.7 copy-start.3
  28.5 0.7 copy-start.4
  30.1 19.8 %collective-permute-start.13 = (bf16[512,768]{1,0:T(8,128)(2,1)S(1)}, bf16[512,768]{1,0:T(8,128)(2,1)S(1)}, u32[]{:S(2)}, u32[]{:S(2)}) collective-permute-start(bf16[512,768]{1,0:T(8,128)(2,1)S(1)} %slice.7), channel_id=1, source_target_pairs={{0,1},{1,0},{2,3},{3,2},{4,5},{5,4},{6,7},{7,6},{8,9},{9,8},{10,11... | collective-permute-start | bytes 2359304 | tf_op jit(solution)/shard_map/ppermute | solution.py:359
  32.8 9.1 %collective-permute-start.4 = (bf16[256,512]{1,0:T(8,128)(2,1)S(1)}, bf16[256,512]{1,0:T(8,128)(2,1)S(1)}, u32[]{:S(2)}, u32[]{:S(2)}) collective-permute-start(bf16[256,512]{1,0:T(8,128)(2,1)S(1)} %shard_map.102.refs_1_), channel_id=1, source_target_pairs={{0,16},{1,17},{2,18},{3,19},{4,20},{5,21},{6,22},{7,23},{8,24},{9,... | collective-permute-start | bytes 786440 | tf_op jit(solution)/shard_map/ppermute | solution.py:359
  36.2 8.7 %collective-permute-start.11 = (bf16[512,256]{1,0:T(8,128)(2,1)S(1)}, bf16[512,256]{1,0:T(8,128)(2,1)S(1)}, u32[]{:S(2)}, u32[]{:S(2)}) collective-permute-start(bf16[512,256]{1,0:T(8,128)(2,1)S(1)} %slice.6), channel_id=1, source_target_pairs={{0,2},{1,3},{2,0},{3,1},{4,6},{5,7},{6,4},{7,5},{8,10},{9,11},{10,... | collective-permute-start | bytes 786440 | tf_op jit(solution)/shard_map/ppermute | solution.py:359
  36.3 9.5 %collective-permute-start.10 = (bf16[256,512]{1,0:T(8,128)(2,1)S(1)}, bf16[256,512]{1,0:T(8,128)(2,1)S(1)}, u32[]{:S(2)}, u32[]{:S(2)}) collective-permute-start(bf16[256,512]{1,0:T(8,128)(2,1)S(1)} %collective-permute-done.8.refs_0_), channel_id=1, source_target_pairs={{0,16},{1,17},{2,18},{3,19},{4,20},{5,21},{6,22},{7,23},{8,24},{9,... | collective-permute-start | bytes 786440 | tf_op jit(solution)/shard_map/ppermute | solution.py:359
  36.5 9.4 %collective-permute-start.14 = (s32[4,8,64]{2,1,0:T(8,128)S(1)}, s32[4,8,64]{2,1,0:T(8,128)S(1)}, u32[]{:S(2)}, u32[]{:S(2)}) collective-permute-start(s32[4,8,64]{2,1,0:T(8,128)S(1)} %bitcast.23), channel_id=1, source_target_pairs={{0,4},{1,5},{2,6},{3,7},{4,0},{5,1},{6,2},{7,3},{8,12},{9,13},{10,... | collective-permute-start | bytes 24584 | tf_op jit(solution)/shard_map/ppermute | solution.py:359
  41.8 4.8 %collective-permute-start.3 = (bf16[256,512]{1,0:T(8,128)(2,1)S(1)}, bf16[256,512]{1,0:T(8,128)(2,1)S(1)}, u32[]{:S(2)}, u32[]{:S(2)}) collective-permute-start(bf16[256,512]{1,0:T(8,128)(2,1)S(1)} %shard_map.102.refs_1_), channel_id=1, source_target_pairs={{0,8},{1,9},{2,10},{3,11},{4,12},{5,13},{6,14},{7,15},{8,0},{9,1},... | collective-permute-start | bytes 786440 | tf_op jit(solution)/shard_map/ppermute | solution.py:359
  45.0 1.6 %collective-permute-start.5 = (bf16[256,512]{1,0:T(8,128)(2,1)S(1)}, bf16[256,512]{1,0:T(8,128)(2,1)S(1)}, u32[]{:S(2)}, u32[]{:S(2)}) collective-permute-start(bf16[256,512]{1,0:T(8,128)(2,1)S(1)} %collective-permute-done.4.refs_3_), channel_id=1, source_target_pairs={{0,8},{1,9},{2,10},{3,11},{4,12},{5,13},{6,14},{7,15},{8,0},{9,1},... | collective-permute-start | bytes 786440 | tf_op jit(solution)/shard_map/ppermute | solution.py:359
  45.8 1.9 %collective-permute-start.9 = (bf16[256,512]{1,0:T(8,128)(2,1)S(1)}, bf16[256,512]{1,0:T(8,128)(2,1)S(1)}, u32[]{:S(2)}, u32[]{:S(2)}) collective-permute-start(bf16[256,512]{1,0:T(8,128)(2,1)S(1)} %collective-permute-done.8.refs_0_), channel_id=1, source_target_pairs={{0,8},{1,9},{2,10},{3,11},{4,12},{5,13},{6,14},{7,15},{8,0},{9,1},... | collective-permute-start | bytes 786440 | tf_op jit(solution)/shard_map/ppermute | solution.py:359
  45.8 1.9 %collective-permute-start.12 = (bf16[256,512]{1,0:T(8,128)(2,1)S(1)}, bf16[256,512]{1,0:T(8,128)(2,1)S(1)}, u32[]{:S(2)}, u32[]{:S(2)}) collective-permute-start(bf16[256,512]{1,0:T(8,128)(2,1)S(1)} %collective-permute-done.10.refs_2_), channel_id=1, source_target_pairs={{0,8},{1,9},{2,10},{3,11},{4,12},{5,13},{6,14},{7,15},{8,0},{9,1},... | collective-permute-start | bytes 786440 | tf_op jit(solution)/shard_map/ppermute | solution.py:359
  46.6 21.0 %slice-start = ((s8[6291456]{0:T(1024)(128)(4,1)}), s8[4194304]{0:T(1024)(128)(4,1)S(1)}, s32[]{:S(2)}) async-start(s8[6291456]{0:T(1024)(128)(4,1)} %bitcast.16), calls=%async_computation | async-start | bytes 8388608
  46.6 21.0 %copy-start.5 = (f32[1024]{0:T(1024)S(1)}, f32[1024]{0:T(1024)}, u32[]{:S(2)}) copy-start(f32[1024]{0:T(1024)} %param.15) | copy-start | bytes 12292
  47.7 19.9 %slice-start.1 = ((s8[6291456]{0:T(1024)(128)(4,1)}), s8[2097152]{0:T(1024)(128)(4,1)S(1)}, s32[]{:S(2)}) async-start(s8[6291456]{0:T(1024)(128)(4,1)} %bitcast.16), calls=%async_computation.1 | async-start | bytes 4194304
  49.9 35.2 %copy-start = (bf16[1,1536,1024]{2,1,0:T(8,128)(2,1)S(1)}, bf16[1,1536,1024]{2,1,0:T(8,128)(2,1)}, u32[]{:S(2)}) copy-start(bf16[1,1536,1024]{2,1,0:T(8,128)(2,1)} %param.19) | copy-start | bytes 9437188
  51.5 8.8 %collective-permute-start.15 = (bf16[32,1024]{1,0:T(8,128)(2,1)S(1)}, bf16[32,1024]{1,0:T(8,128)(2,1)S(1)}, u32[]{:S(2)}, u32[]{:S(2)}) collective-permute-start(bf16[32,1024]{1,0:T(8,128)(2,1)S(1)} %get-tuple-element.75), channel_id=1, source_target_pairs={{0,4},{1,5},{2,6},{3,7},{4,0},{5,1},{6,2},{7,3},{8,12},{9,13},{10,... | collective-permute-start | bytes 196616 | tf_op jit(solution)/shard_map/ppermute | solution.py:359
  52.1 11.3 %collective-permute-start.16 = (bf16[32,1024]{1,0:T(8,128)(2,1)S(1)}, bf16[32,1024]{1,0:T(8,128)(2,1)S(1)}, u32[]{:S(2)}, u32[]{:S(2)}) collective-permute-start(bf16[32,1024]{1,0:T(8,128)(2,1)S(1)} %get-tuple-element.76), channel_id=1, source_target_pairs={{0,5},{1,4},{2,7},{3,6},{4,1},{5,0},{6,3},{7,2},{8,13},{9,12},{10,... | collective-permute-start | bytes 196616 | tf_op jit(solution)/shard_map/ppermute | solution.py:359
  55.2 9.6 %collective-permute-start.17 = (bf16[32,1024]{1,0:T(8,128)(2,1)S(1)}, bf16[32,1024]{1,0:T(8,128)(2,1)S(1)}, u32[]{:S(2)}, u32[]{:S(2)}) collective-permute-start(bf16[32,1024]{1,0:T(8,128)(2,1)S(1)} %get-tuple-element.77), channel_id=1, source_target_pairs={{0,6},{1,7},{2,4},{3,5},{4,2},{5,3},{6,0},{7,1},{8,14},{9,15},{10,... | collective-permute-start | bytes 196616 | tf_op jit(solution)/shard_map/ppermute | solution.py:359
  57.7 8.1 %collective-permute-start.19 = (bf16[32,1024]{1,0:T(8,128)(2,1)S(1)}, bf16[32,1024]{1,0:T(8,128)(2,1)S(1)}, u32[]{:S(2)}, u32[]{:S(2)}) collective-permute-start(bf16[32,1024]{1,0:T(8,128)(2,1)S(1)} %get-tuple-element.80), channel_id=1, source_target_pairs={{0,7},{1,6},{2,5},{3,4},{4,3},{5,2},{6,1},{7,0},{8,15},{9,14},{10,... | collective-permute-start | bytes 196616 | tf_op jit(solution)/shard_map/ppermute | solution.py:359
  59.2 6.5 %collective-permute-start.20 = (bf16[32,1024]{1,0:T(8,128)(2,1)S(1)}, bf16[32,1024]{1,0:T(8,128)(2,1)S(1)}, u32[]{:S(2)}, u32[]{:S(2)}) collective-permute-start(bf16[32,1024]{1,0:T(8,128)(2,1)S(1)} %get-tuple-element.81), channel_id=1, source_target_pairs={{0,3},{1,2},{2,1},{3,0},{4,7},{5,6},{6,5},{7,4},{8,11},{9,10},{10,... | collective-permute-start | bytes 196616 | tf_op jit(solution)/shard_map/ppermute | solution.py:359
  60.3 5.5 %collective-permute-start.21 = (bf16[32,1024]{1,0:T(8,128)(2,1)S(1)}, bf16[32,1024]{1,0:T(8,128)(2,1)S(1)}, u32[]{:S(2)}, u32[]{:S(2)}) collective-permute-start(bf16[32,1024]{1,0:T(8,128)(2,1)S(1)} %get-tuple-element.82), channel_id=1, source_target_pairs={{0,2},{1,3},{2,0},{3,1},{4,6},{5,7},{6,4},{7,5},{8,10},{9,11},{10,... | collective-permute-start | bytes 196616 | tf_op jit(solution)/shard_map/ppermute | solution.py:359
  63.4 4.3 %collective-permute-start.22 = (bf16[32,1024]{1,0:T(8,128)(2,1)S(1)}, bf16[32,1024]{1,0:T(8,128)(2,1)S(1)}, u32[]{:S(2)}, u32[]{:S(2)}) collective-permute-start(bf16[32,1024]{1,0:T(8,128)(2,1)S(1)} %get-tuple-element.83), channel_id=1, source_target_pairs={{0,1},{1,0},{2,3},{3,2},{4,5},{5,4},{6,7},{7,6},{8,9},{9,8},{10,11... | collective-permute-start | bytes 196616 | tf_op jit(solution)/shard_map/ppermute | solution.py:359
  64.8 39.4 %collective-permute-start.18 = (bf16[256,1024]{1,0:T(8,128)(2,1)S(1)}, bf16[256,1024]{1,0:T(8,128)(2,1)S(1)}, u32[]{:S(2)}, u32[]{:S(2)}) collective-permute-start(bf16[256,1024]{1,0:T(8,128)(2,1)S(1)} %get-tuple-element.78), channel_id=1, source_target_pairs={{0,4},{1,5},{2,6},{3,7},{4,0},{5,1},{6,2},{7,3},{8,12},{9,13},{10,... | collective-permute-start | bytes 1572872 | tf_op jit(solution)/shard_map/ppermute | solution.py:359
  68.9 1.3 %collective-permute-start.23 = (bf16[16,3200]{1,0:T(8,128)(2,1)S(1)}, bf16[16,3200]{1,0:T(8,128)(2,1)S(1)}, u32[]{:S(2)}, u32[]{:S(2)}) collective-permute-start(bf16[16,3200]{1,0:T(8,128)(2,1)S(1)} %get-tuple-element.86), channel_id=1, source_target_pairs={{0,8},{1,9},{2,10},{3,11},{4,12},{5,13},{6,14},{7,15},{8,0},{9,1},... | collective-permute-start | bytes 307208 | tf_op jit(solution)/shard_map/ppermute | solution.py:359
  69.0 1.4 %collective-permute-start.24 = (bf16[16,3200]{1,0:T(8,128)(2,1)S(1)}, bf16[16,3200]{1,0:T(8,128)(2,1)S(1)}, u32[]{:S(2)}, u32[]{:S(2)}) collective-permute-start(bf16[16,3200]{1,0:T(8,128)(2,1)S(1)} %get-tuple-element.87), channel_id=1, source_target_pairs={{0,8},{1,9},{2,10},{3,11},{4,12},{5,13},{6,14},{7,15},{8,0},{9,1},... | collective-permute-start | bytes 307208 | tf_op jit(solution)/shard_map/ppermute | solution.py:359
  69.5 1.3 %collective-permute-start.25 = (bf16[16,3200]{1,0:T(8,128)(2,1)S(1)}, bf16[16,3200]{1,0:T(8,128)(2,1)S(1)}, u32[]{:S(2)}, u32[]{:S(2)}) collective-permute-start(bf16[16,3200]{1,0:T(8,128)(2,1)S(1)} %get-tuple-element.88), channel_id=1, source_target_pairs={{0,8},{1,9},{2,10},{3,11},{4,12},{5,13},{6,14},{7,15},{8,0},{9,1},... | collective-permute-start | bytes 307208 | tf_op jit(solution)/shard_map/ppermute | solution.py:359
  69.5 1.4 %collective-permute-start.26 = (bf16[16,3200]{1,0:T(8,128)(2,1)S(1)}, bf16[16,3200]{1,0:T(8,128)(2,1)S(1)}, u32[]{:S(2)}, u32[]{:S(2)}) collective-permute-start(bf16[16,3200]{1,0:T(8,128)(2,1)S(1)} %get-tuple-element.89), channel_id=1, source_target_pairs={{0,8},{1,9},{2,10},{3,11},{4,12},{5,13},{6,14},{7,15},{8,0},{9,1},... | collective-permute-start | bytes 307208 | tf_op jit(solution)/shard_map/ppermute | solution.py:359
  71.0 6.0 %collective-permute-start.27 = (bf16[16,3200]{1,0:T(8,128)(2,1)S(1)}, bf16[16,3200]{1,0:T(8,128)(2,1)S(1)}, u32[]{:S(2)}, u32[]{:S(2)}) collective-permute-start(bf16[16,3200]{1,0:T(8,128)(2,1)S(1)} %get-tuple-element.91), channel_id=1, source_target_pairs={{0,16},{1,17},{2,18},{3,19},{4,20},{5,21},{6,22},{7,23},{8,24},{9,... | collective-permute-start | bytes 307208 | tf_op jit(solution)/shard_map/ppermute | solution.py:359
  73.3 5.6 %collective-permute-start.28 = (bf16[16,3200]{1,0:T(8,128)(2,1)S(1)}, bf16[16,3200]{1,0:T(8,128)(2,1)S(1)}, u32[]{:S(2)}, u32[]{:S(2)}) collective-permute-start(bf16[16,3200]{1,0:T(8,128)(2,1)S(1)} %get-tuple-element.92), channel_id=1, source_target_pairs={{0,16},{1,17},{2,18},{3,19},{4,20},{5,21},{6,22},{7,23},{8,24},{9,... | collective-permute-start | bytes 307208 | tf_op jit(solution)/shard_map/ppermute | solution.py:359
  79.1 4.7 %collective-permute-start.30 = (bf16[32,1536]{1,0:T(8,128)(2,1)S(1)}, bf16[32,1536]{1,0:T(8,128)(2,1)S(1)}, u32[]{:S(2)}, u32[]{:S(2)}) collective-permute-start(bf16[32,1536]{1,0:T(8,128)(2,1)S(1)} %shard_map.111.refs_0_), channel_id=1, source_target_pairs={{0,16},{1,17},{2,18},{3,19},{4,20},{5,21},{6,22},{7,23},{8,24},{9,... | collective-permute-start | bytes 294920 | tf_op jit(solution)/shard_map/ppermute | solution.py:359
  80.9 2.9 %collective-permute-start.29 = (bf16[32,1536]{1,0:T(8,128)(2,1)S(1)}, bf16[32,1536]{1,0:T(8,128)(2,1)S(1)}, u32[]{:S(2)}, u32[]{:S(2)}) collective-permute-start(bf16[32,1536]{1,0:T(8,128)(2,1)S(1)} %shard_map.111.refs_0_), channel_id=1, source_target_pairs={{0,8},{1,9},{2,10},{3,11},{4,12},{5,13},{6,14},{7,15},{8,0},{9,1},... | collective-permute-start | bytes 294920 | tf_op jit(solution)/shard_map/ppermute | solution.py:359
  83.7 1.3 %collective-permute-start.31 = (bf16[32,1536]{1,0:T(8,128)(2,1)S(1)}, bf16[32,1536]{1,0:T(8,128)(2,1)S(1)}, u32[]{:S(2)}, u32[]{:S(2)}) collective-permute-start(bf16[32,1536]{1,0:T(8,128)(2,1)S(1)} %collective-permute-done.30.refs_2_), channel_id=1, source_target_pairs={{0,8},{1,9},{2,10},{3,11},{4,12},{5,13},{6,14},{7,15},{8,0},{9,1},... | collective-permute-start | bytes 294920 | tf_op jit(solution)/shard_map/ppermute | solution.py:359
  85.7 15.4 %collective-permute-start.32 = (bf16[16,1024]{1,0:T(8,128)(2,1)S(1)}, bf16[16,1024]{1,0:T(8,128)(2,1)S(1)}, u32[]{:S(2)}, u32[]{:S(2)}) collective-permute-start(bf16[16,1024]{1,0:T(8,128)(2,1)S(1)} %get-tuple-element.93), channel_id=1, source_target_pairs={{0,4},{1,5},{2,6},{3,7},{4,0},{5,1},{6,2},{7,3},{8,12},{9,13},{10,... | collective-permute-start | bytes 98312 | tf_op jit(solution)/shard_map/ppermute | solution.py:359
  96.2 6.5 %collective-permute-start.33 = (bf16[16,1024]{1,0:T(8,128)(2,1)S(1)}, bf16[16,1024]{1,0:T(8,128)(2,1)S(1)}, u32[]{:S(2)}, u32[]{:S(2)}) collective-permute-start(bf16[16,1024]{1,0:T(8,128)(2,1)S(1)} %get-tuple-element.94), channel_id=1, source_target_pairs={{0,5},{1,4},{2,7},{3,6},{4,1},{5,0},{6,3},{7,2},{8,13},{9,12},{10,... | collective-permute-start | bytes 98312 | tf_op jit(solution)/shard_map/ppermute | solution.py:359
  97.4 7.4 %collective-permute-start.34 = (bf16[16,1024]{1,0:T(8,128)(2,1)S(1)}, bf16[16,1024]{1,0:T(8,128)(2,1)S(1)}, u32[]{:S(2)}, u32[]{:S(2)}) collective-permute-start(bf16[16,1024]{1,0:T(8,128)(2,1)S(1)} %get-tuple-element.95), channel_id=1, source_target_pairs={{0,6},{1,7},{2,4},{3,5},{4,2},{5,3},{6,0},{7,1},{8,14},{9,15},{10,... | collective-permute-start | bytes 98312 | tf_op jit(solution)/shard_map/ppermute | solution.py:359
  99.3 6.7 %collective-permute-start.35 = (bf16[16,1024]{1,0:T(8,128)(2,1)S(1)}, bf16[16,1024]{1,0:T(8,128)(2,1)S(1)}, u32[]{:S(2)}, u32[]{:S(2)}) collective-permute-start(bf16[16,1024]{1,0:T(8,128)(2,1)S(1)} %get-tuple-element.96), channel_id=1, source_target_pairs={{0,7},{1,6},{2,5},{3,4},{4,3},{5,2},{6,1},{7,0},{8,15},{9,14},{10,... | collective-permute-start | bytes 98312 | tf_op jit(solution)/shard_map/ppermute | solution.py:359
  101.2 5.2 %collective-permute-start.36 = (bf16[16,1024]{1,0:T(8,128)(2,1)S(1)}, bf16[16,1024]{1,0:T(8,128)(2,1)S(1)}, u32[]{:S(2)}, u32[]{:S(2)}) collective-permute-start(bf16[16,1024]{1,0:T(8,128)(2,1)S(1)} %get-tuple-element.97), channel_id=1, source_target_pairs={{0,3},{1,2},{2,1},{3,0},{4,7},{5,6},{6,5},{7,4},{8,11},{9,10},{10,... | collective-permute-start | bytes 98312 | tf_op jit(solution)/shard_map/ppermute | solution.py:359
  102.7 3.9 %collective-permute-start.37 = (bf16[16,1024]{1,0:T(8,128)(2,1)S(1)}, bf16[16,1024]{1,0:T(8,128)(2,1)S(1)}, u32[]{:S(2)}, u32[]{:S(2)}) collective-permute-start(bf16[16,1024]{1,0:T(8,128)(2,1)S(1)} %get-tuple-element.98), channel_id=1, source_target_pairs={{0,2},{1,3},{2,0},{3,1},{4,6},{5,7},{6,4},{7,5},{8,10},{9,11},{10,... | collective-permute-start | bytes 98312 | tf_op jit(solution)/shard_map/ppermute | solution.py:359
  104.2 3.9 %collective-permute-start.38 = (bf16[16,1024]{1,0:T(8,128)(2,1)S(1)}, bf16[16,1024]{1,0:T(8,128)(2,1)S(1)}, u32[]{:S(2)}, u32[]{:S(2)}) collective-permute-start(bf16[16,1024]{1,0:T(8,128)(2,1)S(1)} %get-tuple-element.99), channel_id=1, source_target_pairs={{0,1},{1,0},{2,3},{3,2},{4,5},{5,4},{6,7},{7,6},{8,9},{9,8},{10,11... | collective-permute-start | bytes 98312 | tf_op jit(solution)/shard_map/ppermute | solution.py:359
